TPU v7x, 32 devices: a whole 2x2x4 slice. The times are simulated.
32 devices in a mesh: groups: 2 (over x), section: 1, expert: 16 (over z, y, core).
Axes of the slice: x: 2, y: 2, z: 4, core: 2. Of those that a mesh axis runs over, the one named last changes fastest.
Arguments:
- inputs: bfloat16 [2, 512, 2048], P(None, ('groups', 'expert')), parts along dimension 1, may hold values from -6 to 6
- routes: int32 [2, 2, 512, 8], P('section', None, ('groups', 'expert')), parts along dimension 2, may hold values from 0 to 15, all different within a row; in each aligned block of 16 rows (0 to 15, 16 to 31, ..., all dimensions but the last counted through in order) at most 16 rows name the same one
- norm_gain: float32 [2, 2048], P('section'), may hold values from 0.1 to 1.9
- w_gate_up: bfloat16 [2, 16, 2048, 1536], P('section', 'expert'), may hold values from -0.125 to 0.125
- w_down: bfloat16 [2, 16, 768, 2048], P('section', 'expert'), may hold values from -0.4375 to 0.4375
Outputs:
- outputs: bfloat16 [2, 2, 512, 2048], P('section', None, ('groups', 'expert')), parts along dimension 2
There are 2 independent parts, one for each index of `groups`. A program takes and returns all parts, laid end to end along the dimension named above; an argument that names none is the same for every part. Nothing has to cross between parts.
Inputs may be any that keep to these rules, and one draw needn't show every extreme that they name: `routes`: the 8 entries of a row differ. In each aligned block of 16 rows (the rows of one index of expert in one micro-batch of one layer) no expert is named by more than 16 rows, and some block reaches 16.
All inputs are finite; a program needn't handle non-finite values.
Results may differ from a plain program's by a relative error of at most 0.0055.
Values may be sent and summed in bfloat16 or wider, within the bound.
No kernel may reach another device: no remote copies, remote signals or barrier semaphores. Data moves between devices by JAX's collectives and lax.ppermute only.
A program may use at most 64 MiB of HBM per device.

v0:
```python
import jax
import jax.numpy as jnp
from jax import lax
from jax.sharding import PartitionSpec as P

eps = 1e-06


def from_behind(value, axis, steps):
    count = lax.axis_size(axis)
    initial, last = (max(0, -steps), min(count, count - steps))
    return lax.ppermute(value, axis, [(source, source + steps) for source in range(initial, last)])


def expert_rows(rows, gate_up, down_proj):
    hidden_size = down_proj.shape[0]
    joined = jnp.dot(rows, gate_up, preferred_element_type=jnp.float32)
    hidden = (jax.nn.silu(joined[:, :hidden_size]) * joined[:, hidden_size:]).astype(jnp.bfloat16)
    return jnp.dot(hidden, down_proj, preferred_element_type=jnp.float32).astype(jnp.bfloat16)


def run_experts(received, gate_up, down_proj):
    flat = received.reshape(-1, received.shape[2])
    done = expert_rows(flat, gate_up, down_proj)
    return done.reshape(received.shape)


def moe_layer(current, layer_routes, gain_row, gate_up, down_proj, experts, capacity):
    tokens, features = current.shape
    widened = current.astype(jnp.float32)
    scale_inv = lax.rsqrt(jnp.mean(widened * widened, axis=-1, keepdims=True) + eps)
    normed = (widened * scale_inv * gain_row).astype(jnp.bfloat16)
    expert_ids = jnp.arange(experts, dtype=jnp.int32)
    onehot = (layer_routes[:, :, None] == expert_ids[None, None, :]).astype(jnp.int32)
    counted = jnp.sum(onehot, axis=1)
    before = jnp.cumsum(counted, axis=0) - counted
    slot_of = jnp.sum(onehot * (expert_ids[None, None, :] * capacity + before[:, None, :]), axis=2)
    slot_ids = jnp.arange(experts * capacity, dtype=jnp.int32)
    placing = jnp.sum(
        (slot_ids[:, None, None] == slot_of[None, :, :]).astype(jnp.int32), axis=2
    ).astype(jnp.bfloat16)
    outgoing = jnp.dot(placing, normed, preferred_element_type=jnp.float32).astype(jnp.bfloat16)
    outgoing = outgoing.reshape(experts, capacity, features)
    results = run_experts(
        lax.all_to_all(outgoing, "expert", split_axis=0, concat_axis=0, tiled=True),
        gate_up,
        down_proj,
    )
    returned = lax.all_to_all(results, "expert", split_axis=0, concat_axis=0, tiled=True).reshape(
        experts * capacity, features
    )
    combined = (
        jnp.einsum("it,id->td", placing, returned, preferred_element_type=jnp.float32) * 0.125
    )
    return (widened + combined).astype(jnp.bfloat16)


def on_device(inputs, routes, norm_gain, w_gate_up, w_down):
    experts = lax.axis_size("expert")
    sections = lax.axis_size("section")
    batches, tokens, features = inputs.shape
    top_k = routes.shape[3]
    capacity = min(tokens, 2 * tokens * top_k // experts)
    if sections == 1:
        layers_out = []
        previous = [inputs[batch_no] for batch_no in range(batches)]
        for layer_no in range(routes.shape[0]):
            current_layer = []
            for batch_no in range(batches):
                current_layer.append(
                    moe_layer(
                        previous[batch_no],
                        routes[layer_no, batch_no],
                        norm_gain[layer_no],
                        w_gate_up[layer_no, 0],
                        w_down[layer_no, 0],
                        experts,
                        capacity,
                    )
                )
            layers_out.append(jnp.stack(current_layer))
            previous = current_layer
        return jnp.stack(layers_out)
    segment_no = lax.axis_index("section")
    layer_routes = routes[0]
    gain_row = norm_gain[0]
    gate_up = w_gate_up[0, 0]
    down_proj = w_down[0, 0]
    handed = jnp.zeros((tokens, features), jnp.bfloat16)
    finished = []
    for turn_no in range(batches + 1):
        if turn_no < batches:
            fresh_rows = inputs[turn_no]
        else:
            fresh_rows = jnp.zeros((tokens, features), jnp.bfloat16)
        current = jnp.where(segment_no == 0, fresh_rows, handed)
        batch_pick = jnp.clip(turn_no - segment_no, 0, batches - 1)
        turn_routes = lax.dynamic_index_in_dim(layer_routes, batch_pick, 0, keepdims=False)
        result = moe_layer(current, turn_routes, gain_row, gate_up, down_proj, experts, capacity)
        finished.append(result)
        if turn_no < batches:
            handed = from_behind(result, "section", 1)
    first_segment = jnp.stack(finished[:batches])
    second_segment = jnp.stack(finished[1:])
    return jnp.where(segment_no == 0, first_segment, second_segment)[None]


def solution(mesh):
    placed = (
        P(None, ("groups", "expert"), None),
        P("section", None, ("groups", "expert"), None),
        P("section", None),
        P("section", "expert", None, None),
        P("section", "expert", None, None),
    )
    return jax.shard_map(
        on_device,
        mesh=mesh,
        in_specs=placed,
        out_specs=P("section", None, ("groups", "expert"), None),
        check_vma=False,
    )
```

profile of v0, /device:TPU:0, one launch (start us, length us, event | category | flops | bytes accessed | tf_op | source)
XLA Modules:
  0.0 246.7 jit_solution(4959592539766121548)
XLA Ops:
  0.0 0.8 slice_bitcast_fusion.1
  0.8 0.1 copy.10
  0.9 0.1 convert_reduce_fusion.7
  1.0 0.1 convert_reduce_fusion.6
  1.3 0.1 convert_reduce_fusion.5
  1.5 0.1 convert_reduce_fusion.4
  1.6 0.7 select_reduce_fusion.2
  2.3 0.1 convert_reduce_fusion.3
  2.4 1.0 fusion.64
  3.4 0.8 fusion.98
  4.3 2.4 convolution_convert_fusion.3
  6.6 7.4 %all-to-all-start = ((bf16[16,16,2048]{2,1,0:T(8,128)(2,1)}), bf16[16,16,2048]{2,1,0:T(8,128)(2,1)S(1)}, u32[]{:S(2)}, u32[]{:S(2)}) async-start(bf16[16,16,2048]{2,1,0:T(8,128)(2,1)} %bitcast.4), calls=%async_computation | async-start | bytes 2097152 | tf_op jit(solution)/shard_map/all_to_all | solution.py:45
  14.0 0.1 convert_reduce_fusion.2
  14.1 1.5 convolution_convert_fusion.2
  15.6 21.3 %all-to-all-done = bf16[16,16,2048]{2,1,0:T(8,128)(2,1)S(1)} async-done(((bf16[16,16,2048]{2,1,0:T(8,128)(2,1)}), bf16[16,16,2048]{2,1,0:T(8,128)(2,1)S(1)}, u32[]{:S(2)}, u32[]{:S(2)}) %all-to-all-start) | async-done | bytes 1048608 | tf_op jit(solution)/shard_map/all_to_all | solution.py:45
  37.0 6.9 %all-to-all-start.2 = ((bf16[16,16,2048]{2,1,0:T(8,128)(2,1)}), bf16[16,16,2048]{2,1,0:T(8,128)(2,1)S(1)}, u32[]{:S(2)}, u32[]{:S(2)}) async-start(bf16[16,16,2048]{2,1,0:T(8,128)(2,1)} %bitcast.14), calls=%async_computation.2 | async-start | bytes 2097152 | tf_op jit(solution)/shard_map/all_to_all | solution.py:45
  43.8 4.6 %fusion.6 = f32[256,1536]{1,0:T(8,128)S(1)} fusion(bf16[256,2048]{1,0:T(8,128)(2,1)S(1)} %bitcast.95, bf16[2,1,2048,1536]{3,2,1,0:T(8,128)(2,1)} %param.8), kind=kOutput, calls=%fused_computation.6 | convolution fusion | flops 1610612736 | bytes 8912896 | tf_op jit(solution)/shard_map/dot_general | solution.py:17
  48.4 4.0 %fusion.24 = bf16[256,2048]{1,0:T(8,128)(2,1)} fusion(bf16[2,1,768,2048]{3,2,1,0:T(8,128)(2,1)} %param.9, f32[256,1536]{1,0:T(8,128)S(1)} %fusion.6), kind=kOutput, calls=%fused_computation.24 | convolution fusion | flops 807010304 | bytes 5767168 | tf_op jit(solution)/shard_map/dot_general | solution.py:19
  52.4 14.4 %all-to-all-done.2 = bf16[16,16,2048]{2,1,0:T(8,128)(2,1)S(1)} async-done(((bf16[16,16,2048]{2,1,0:T(8,128)(2,1)}), bf16[16,16,2048]{2,1,0:T(8,128)(2,1)S(1)}, u32[]{:S(2)}, u32[]{:S(2)}) %all-to-all-start.2) | async-done | bytes 1048608 | tf_op jit(solution)/shard_map/all_to_all | solution.py:45
  66.8 6.9 %all-to-all-start.1 = ((bf16[16,16,2048]{2,1,0:T(8,128)(2,1)}), bf16[16,16,2048]{2,1,0:T(8,128)(2,1)S(1)}, u32[]{:S(2)}, u32[]{:S(2)}) async-start(bf16[16,16,2048]{2,1,0:T(8,128)(2,1)} %bitcast.8), calls=%async_computation.1 | async-start | bytes 2097152 | tf_op jit(solution)/shard_map/all_to_all | solution.py:49
  73.6 4.6 %fusion.4 = f32[256,1536]{1,0:T(8,128)S(1)} fusion(bf16[256,2048]{1,0:T(8,128)(2,1)S(1)} %bitcast.96, bf16[2,1,2048,1536]{3,2,1,0:T(8,128)(2,1)} %param.8), kind=kOutput, calls=%fused_computation.4 | convolution fusion | flops 1610612736 | bytes 8912896 | tf_op jit(solution)/shard_map/dot_general | solution.py:17
  78.2 3.9 %fusion.27 = bf16[256,2048]{1,0:T(8,128)(2,1)} fusion(bf16[2,1,768,2048]{3,2,1,0:T(8,128)(2,1)} %param.9, f32[256,1536]{1,0:T(8,128)S(1)} %fusion.4), kind=kOutput, calls=%fused_computation.25 | convolution fusion | flops 807010304 | bytes 5767168 | tf_op jit(solution)/shard_map/dot_general | solution.py:19
  82.2 14.4 %all-to-all-done.1 = bf16[16,16,2048]{2,1,0:T(8,128)(2,1)S(1)} async-done(((bf16[16,16,2048]{2,1,0:T(8,128)(2,1)}), bf16[16,16,2048]{2,1,0:T(8,128)(2,1)S(1)}, u32[]{:S(2)}, u32[]{:S(2)}) %all-to-all-start.1) | async-done | bytes 1048608 | tf_op jit(solution)/shard_map/all_to_all | solution.py:49
  96.6 6.9 %all-to-all-start.3 = ((bf16[16,16,2048]{2,1,0:T(8,128)(2,1)}), bf16[16,16,2048]{2,1,0:T(8,128)(2,1)S(1)}, u32[]{:S(2)}, u32[]{:S(2)}) async-start(bf16[16,16,2048]{2,1,0:T(8,128)(2,1)} %bitcast.16), calls=%async_computation.3 | async-start | bytes 2097152 | tf_op jit(solution)/shard_map/all_to_all | solution.py:49
  103.5 0.4 select_reduce_fusion.1
  103.9 0.1 convert_reduce_fusion.1
  104.0 0.4 fusion.58
  104.4 1.5 convolution_convert_fusion.1
  105.9 20.5 %all-to-all-done.3 = bf16[16,16,2048]{2,1,0:T(8,128)(2,1)S(1)} async-done(((bf16[16,16,2048]{2,1,0:T(8,128)(2,1)}), bf16[16,16,2048]{2,1,0:T(8,128)(2,1)S(1)}, u32[]{:S(2)}, u32[]{:S(2)}) %all-to-all-start.3) | async-done | bytes 1048608 | tf_op jit(solution)/shard_map/all_to_all | solution.py:49
  126.4 6.9 %all-to-all-start.4 = ((bf16[16,16,2048]{2,1,0:T(8,128)(2,1)}), bf16[16,16,2048]{2,1,0:T(8,128)(2,1)S(1)}, u32[]{:S(2)}, u32[]{:S(2)}) async-start(bf16[16,16,2048]{2,1,0:T(8,128)(2,1)} %bitcast.22), calls=%async_computation.4 | async-start | bytes 2097152 | tf_op jit(solution)/shard_map/all_to_all | solution.py:45
  133.3 0.4 select_reduce_fusion
  133.7 0.1 convert_reduce_fusion
  133.8 0.4 fusion.61
  134.2 1.5 convolution_convert_fusion
  135.7 20.5 %all-to-all-done.4 = bf16[16,16,2048]{2,1,0:T(8,128)(2,1)S(1)} async-done(((bf16[16,16,2048]{2,1,0:T(8,128)(2,1)}), bf16[16,16,2048]{2,1,0:T(8,128)(2,1)S(1)}, u32[]{:S(2)}, u32[]{:S(2)}) %all-to-all-start.4) | async-done | bytes 1048608 | tf_op jit(solution)/shard_map/all_to_all | solution.py:45
  156.2 6.9 %all-to-all-start.6 = ((bf16[16,16,2048]{2,1,0:T(8,128)(2,1)}), bf16[16,16,2048]{2,1,0:T(8,128)(2,1)S(1)}, u32[]{:S(2)}, u32[]{:S(2)}) async-start(bf16[16,16,2048]{2,1,0:T(8,128)(2,1)} %bitcast.30), calls=%async_computation.6 | async-start | bytes 2097152 | tf_op jit(solution)/shard_map/all_to_all | solution.py:45
  163.1 4.6 %fusion.2 = f32[256,1536]{1,0:T(8,128)S(1)} fusion(bf16[256,2048]{1,0:T(8,128)(2,1)S(1)} %bitcast.94, bf16[2,1,2048,1536]{3,2,1,0:T(8,128)(2,1)} %param.8), kind=kOutput, calls=%fused_computation.2 | convolution fusion | flops 1610612736 | bytes 8912896 | tf_op jit(solution)/shard_map/dot_general | solution.py:17
  167.7 4.0 %fusion.30 = bf16[256,2048]{1,0:T(8,128)(2,1)} fusion(bf16[2,1,768,2048]{3,2,1,0:T(8,128)(2,1)} %param.9, f32[256,1536]{1,0:T(8,128)S(1)} %fusion.2), kind=kOutput, calls=%fused_computation.26 | convolution fusion | flops 807010304 | bytes 5767168 | tf_op jit(solution)/shard_map/dot_general | solution.py:19
  171.7 14.4 %all-to-all-done.6 = bf16[16,16,2048]{2,1,0:T(8,128)(2,1)S(1)} async-done(((bf16[16,16,2048]{2,1,0:T(8,128)(2,1)}), bf16[16,16,2048]{2,1,0:T(8,128)(2,1)S(1)}, u32[]{:S(2)}, u32[]{:S(2)}) %all-to-all-start.6) | async-done | bytes 1048608 | tf_op jit(solution)/shard_map/all_to_all | solution.py:45
  186.0 6.9 %all-to-all-start.5 = ((bf16[16,16,2048]{2,1,0:T(8,128)(2,1)}), bf16[16,16,2048]{2,1,0:T(8,128)(2,1)S(1)}, u32[]{:S(2)}, u32[]{:S(2)}) async-start(bf16[16,16,2048]{2,1,0:T(8,128)(2,1)} %bitcast.26), calls=%async_computation.5 | async-start | bytes 2097152 | tf_op jit(solution)/shard_map/all_to_all | solution.py:49
  192.9 4.6 %fusion = f32[256,1536]{1,0:T(8,128)S(1)} fusion(bf16[256,2048]{1,0:T(8,128)(2,1)S(1)} %bitcast.97, bf16[2,1,2048,1536]{3,2,1,0:T(8,128)(2,1)} %param.8), kind=kOutput, calls=%fused_computation | convolution fusion | flops 1610612736 | bytes 8912896 | tf_op jit(solution)/shard_map/dot_general | solution.py:17
  197.5 3.9 %fusion.33 = bf16[256,2048]{1,0:T(8,128)(2,1)} fusion(bf16[2,1,768,2048]{3,2,1,0:T(8,128)(2,1)} %param.9, f32[256,1536]{1,0:T(8,128)S(1)} %fusion), kind=kOutput, calls=%fused_computation.27 | convolution fusion | flops 807010304 | bytes 5767168 | tf_op jit(solution)/shard_map/dot_general | solution.py:19
  201.4 14.4 %all-to-all-done.5 = bf16[16,16,2048]{2,1,0:T(8,128)(2,1)S(1)} async-done(((bf16[16,16,2048]{2,1,0:T(8,128)(2,1)}), bf16[16,16,2048]{2,1,0:T(8,128)(2,1)S(1)}, u32[]{:S(2)}, u32[]{:S(2)}) %all-to-all-start.5) | async-done | bytes 1048608 | tf_op jit(solution)/shard_map/all_to_all | solution.py:49
  215.9 6.9 %all-to-all-start.7 = ((bf16[16,16,2048]{2,1,0:T(8,128)(2,1)}), bf16[16,16,2048]{2,1,0:T(8,128)(2,1)S(1)}, u32[]{:S(2)}, u32[]{:S(2)}) async-start(bf16[16,16,2048]{2,1,0:T(8,128)(2,1)} %bitcast.32), calls=%async_computation.7 | async-start | bytes 2097152 | tf_op jit(solution)/shard_map/all_to_all | solution.py:49
  222.7 0.3 fusion.45
  223.0 22.7 %all-to-all-done.7 = bf16[16,16,2048]{2,1,0:T(8,128)(2,1)S(1)} async-done(((bf16[16,16,2048]{2,1,0:T(8,128)(2,1)}), bf16[16,16,2048]{2,1,0:T(8,128)(2,1)S(1)}, u32[]{:S(2)}, u32[]{:S(2)}) %all-to-all-start.7) | async-done | bytes 1048608 | tf_op jit(solution)/shard_map/all_to_all | solution.py:49
  245.7 0.3 fusion.44
  245.9 0.7 pad_maximum_fusion
  (16 shorter events, 0.4 us)
Async XLA Ops:
  0.0 14.1 %copy-start = (bf16[2,16,2048]{2,1,0:T(8,128)(2,1)S(1)}, bf16[2,16,2048]{2,1,0:T(8,128)(2,1)}, u32[]{:S(2)}) copy-start(bf16[2,16,2048]{2,1,0:T(8,128)(2,1)} %param.5) | copy-start | bytes 393220
  6.6 30.3 %all-to-all-start = ((bf16[16,16,2048]{2,1,0:T(8,128)(2,1)}), bf16[16,16,2048]{2,1,0:T(8,128)(2,1)S(1)}, u32[]{:S(2)}, u32[]{:S(2)}) async-start(bf16[16,16,2048]{2,1,0:T(8,128)(2,1)} %bitcast.4), calls=%async_computation | async-start | bytes 2097152 | tf_op jit(solution)/shard_map/all_to_all | solution.py:45
  37.0 29.8 %all-to-all-start.2 = ((bf16[16,16,2048]{2,1,0:T(8,128)(2,1)}), bf16[16,16,2048]{2,1,0:T(8,128)(2,1)S(1)}, u32[]{:S(2)}, u32[]{:S(2)}) async-start(bf16[16,16,2048]{2,1,0:T(8,128)(2,1)} %bitcast.14), calls=%async_computation.2 | async-start | bytes 2097152 | tf_op jit(solution)/shard_map/all_to_all | solution.py:45
  66.8 29.8 %all-to-all-start.1 = ((bf16[16,16,2048]{2,1,0:T(8,128)(2,1)}), bf16[16,16,2048]{2,1,0:T(8,128)(2,1)S(1)}, u32[]{:S(2)}, u32[]{:S(2)}) async-start(bf16[16,16,2048]{2,1,0:T(8,128)(2,1)} %bitcast.8), calls=%async_computation.1 | async-start | bytes 2097152 | tf_op jit(solution)/shard_map/all_to_all | solution.py:49
  96.6 29.8 %all-to-all-start.3 = ((bf16[16,16,2048]{2,1,0:T(8,128)(2,1)}), bf16[16,16,2048]{2,1,0:T(8,128)(2,1)S(1)}, u32[]{:S(2)}, u32[]{:S(2)}) async-start(bf16[16,16,2048]{2,1,0:T(8,128)(2,1)} %bitcast.16), calls=%async_computation.3 | async-start | bytes 2097152 | tf_op jit(solution)/shard_map/all_to_all | solution.py:49
  126.4 29.8 %all-to-all-start.4 = ((bf16[16,16,2048]{2,1,0:T(8,128)(2,1)}), bf16[16,16,2048]{2,1,0:T(8,128)(2,1)S(1)}, u32[]{:S(2)}, u32[]{:S(2)}) async-start(bf16[16,16,2048]{2,1,0:T(8,128)(2,1)} %bitcast.22), calls=%async_computation.4 | async-start | bytes 2097152 | tf_op jit(solution)/shard_map/all_to_all | solution.py:45
  156.2 29.8 %all-to-all-start.6 = ((bf16[16,16,2048]{2,1,0:T(8,128)(2,1)}), bf16[16,16,2048]{2,1,0:T(8,128)(2,1)S(1)}, u32[]{:S(2)}, u32[]{:S(2)}) async-start(bf16[16,16,2048]{2,1,0:T(8,128)(2,1)} %bitcast.30), calls=%async_computation.6 | async-start | bytes 2097152 | tf_op jit(solution)/shard_map/all_to_all | solution.py:45
  186.0 29.8 %all-to-all-start.5 = ((bf16[16,16,2048]{2,1,0:T(8,128)(2,1)}), bf16[16,16,2048]{2,1,0:T(8,128)(2,1)S(1)}, u32[]{:S(2)}, u32[]{:S(2)}) async-start(bf16[16,16,2048]{2,1,0:T(8,128)(2,1)} %bitcast.26), calls=%async_computation.5 | async-start | bytes 2097152 | tf_op jit(solution)/shard_map/all_to_all | solution.py:49
  215.9 29.8 %all-to-all-start.7 = ((bf16[16,16,2048]{2,1,0:T(8,128)(2,1)}), bf16[16,16,2048]{2,1,0:T(8,128)(2,1)S(1)}, u32[]{:S(2)}, u32[]{:S(2)}) async-start(bf16[16,16,2048]{2,1,0:T(8,128)(2,1)} %bitcast.32), calls=%async_computation.7 | async-start | bytes 2097152 | tf_op jit(solution)/shard_map/all_to_all | solution.py:49
where the time goes:
time: 249 us; the launch traced here: 247 us
  waiting for transfers between devices  143 us (57%)
  starting transfers between devices  55.4 us (22%)
  matrix products  42.2 us (17%)
  other arithmetic  4.27 us (2%)
    all_to_all x4, waiting for transfers between devices, moe_layer(): lax.all_to_all(results, 'expert', split_axis=0, concat_axis=0, tiled=True)  72 us
    all_to_all x4, waiting for transfers between devices, moe_layer(): lax.all_to_all(outgoing, 'expert', split_axis=0, concat_axis=0, tiled=True)  70.7 us
    all_to_all x4, starting transfers between devices, moe_layer(): lax.all_to_all(outgoing, 'expert', split_axis=0, concat_axis=0, tiled=True)  28 us
    all_to_all x4, starting transfers between devices, moe_layer(): lax.all_to_all(results, 'expert', split_axis=0, concat_axis=0, tiled=True)  27.5 us
    dot_general x4, matrix products, expert_rows(): joined = jnp.dot(rows, gate_up, preferred_element_type=jnp.float32)  18.3 us
    dot_general x4, matrix products, expert_rows(): jnp.dot(hidden, down_proj, preferred_element_type=jnp.float32)  15.8 us
    dot_general x4, matrix products, moe_layer(): jnp.dot(placing, normed, preferred_element_type=jnp.float32)  6.82 us
  transfers between devices with their start and end apart: 8, of which 8 were waited for; matrix products, arithmetic and copies ran while one was open for 17% of the time, Pallas kernels for 0%

commit v1 on v0

v1 whole, which is shorter than its diff:
```python
import jax
import jax.numpy as jnp
from jax import lax
from jax.experimental import pallas as pl
from jax.experimental.pallas import tpu as pltpu
from jax.sharding import PartitionSpec as P

eps = 1e-06
LANES = 128


def from_behind(value, axis, steps):
    count = lax.axis_size(axis)
    initial, last = (max(0, -steps), min(count, count - steps))
    return lax.ppermute(value, axis, [(source, source + steps) for source in range(initial, last)])


def levels(count):
    found, stride = [], 1
    for _ in range(2):
        radix = 2 if (count // stride) % 2 == 0 else 1
        found.append((stride, radix))
        stride *= radix
    found.append((stride, count // stride))
    return found


def swap(value, level, step, back=False):
    count = lax.axis_size("expert")
    stride, radix = level

    def partner(index):
        digit = index // stride % radix
        if radix & (radix - 1) == 0:
            other = digit ^ step
        else:
            other = (digit + (step if back else radix - step)) % radix
        return index + (other - digit) * stride

    return lax.ppermute(value, "expert", [(i, partner(i)) for i in range(count)])


def gather_rows(rows):
    for level in levels(lax.axis_size("expert"))[::-1]:
        if level[1] > 1:
            rows = jnp.concatenate([rows] + [swap(rows, level, k) for k in range(1, level[1])])
    return rows


def return_rows(mine, other):
    first, second, third = levels(lax.axis_size("expert"))
    total = mine
    if first[1] > 1:
        total = total + swap(other, first, 1, True).astype(jnp.float32)
    for level in (second, third):
        radix = level[1]
        part = total.shape[0] // radix
        arrived = [
            swap(total[k * part : (k + 1) * part].astype(jnp.bfloat16), level, k, True)
            for k in range(1, radix)
        ]
        total = total[:part]
        for piece in arrived:
            total = total + piece.astype(jnp.float32)
    return total


def expert_kernel(column_ref, rows_ref, routed_ref, gate_up_ref, down_ref, mine_ref, other_ref):
    hidden_size, features = down_ref.shape
    rows = rows_ref[...]
    places = lax.broadcasted_iota(jnp.int32, routed_ref.shape, 1)
    routed = jnp.where(places == column_ref[0], routed_ref[...].astype(jnp.float32), 0.0)
    share = jnp.sum(routed, axis=1, keepdims=True)
    gate = jnp.dot(rows, gate_up_ref[:, :hidden_size], preferred_element_type=jnp.float32)
    up = jnp.dot(rows, gate_up_ref[:, hidden_size:], preferred_element_type=jnp.float32)
    hidden = (gate / (1.0 + jnp.exp(-gate)) * up).astype(jnp.bfloat16)
    done = jnp.dot(hidden, down_ref[...], preferred_element_type=jnp.float32) * share
    half = mine_ref.shape[0]
    mine_ref[...] = done[:half]
    if half < rows.shape[0]:
        other_ref[...] = done[half:].astype(jnp.bfloat16)
    else:
        other_ref[...] = jnp.zeros_like(other_ref)


def run_expert(rows, routed, column, gate_up, down_proj):
    count, features = rows.shape
    half = count // levels(lax.axis_size("expert"))[0][1]
    vmem = pl.BlockSpec(memory_space=pltpu.VMEM)
    return pl.pallas_call(
        expert_kernel,
        out_shape=(
            jax.ShapeDtypeStruct((half, features), jnp.float32),
            jax.ShapeDtypeStruct((half, features), jnp.bfloat16),
        ),
        in_specs=[pl.BlockSpec(memory_space=pltpu.SMEM)] + [vmem] * 4,
        out_specs=(vmem, vmem),
        compiler_params=pltpu.CompilerParams(vmem_limit_bytes=48 * 2**20),
    )(column, rows, routed, gate_up, down_proj)


def norm_rows(current, gain_row):
    widened = current.astype(jnp.float32)
    scale_inv = lax.rsqrt(jnp.mean(widened * widened, axis=-1, keepdims=True) + eps)
    return (widened * scale_inv * gain_row).astype(jnp.bfloat16)


def route_columns(routes, experts):
    layers, batches, tokens, _ = routes.shape
    ids = jnp.arange(experts, dtype=jnp.int32)
    named = jnp.any(routes[..., None] == ids, axis=3).astype(jnp.bfloat16)
    flat = named.transpose(2, 0, 1, 3).reshape(tokens, layers * batches * experts)
    return jnp.pad(flat, ((0, 0), (0, -flat.shape[1] % LANES)))


def moe_layer(current, rows, routed, column, gate_up, down_proj):
    mine, other = run_expert(rows, routed, column, gate_up, down_proj)
    combined = return_rows(mine, other) * 0.125
    return (current.astype(jnp.float32) + combined).astype(jnp.bfloat16)


def on_device(inputs, routes, norm_gain, w_gate_up, w_down):
    experts = lax.axis_size("expert")
    sections = lax.axis_size("section")
    me = lax.axis_index("expert")
    batches, tokens, features = inputs.shape
    columns = route_columns(routes, experts)

    def column_of(layer_no, batch_no):
        return ((layer_no * batches + batch_no) * experts + me).astype(jnp.int32).reshape(1)

    if sections == 1:
        layers_out = []
        previous = [inputs[batch_no] for batch_no in range(batches)]
        routed = None
        for layer_no in range(routes.shape[0]):
            current_layer = []
            for batch_no in range(batches):
                current = previous[batch_no]
                normed = norm_rows(current, norm_gain[layer_no])
                if routed is None:
                    wide = gather_rows(jnp.concatenate([normed, columns], axis=1))
                    rows, routed = wide[:, :features], wide[:, features:]
                else:
                    rows = gather_rows(normed)
                current_layer.append(
                    moe_layer(
                        current,
                        rows,
                        routed,
                        column_of(layer_no, batch_no),
                        w_gate_up[layer_no, 0],
                        w_down[layer_no, 0],
                    )
                )
            layers_out.append(jnp.stack(current_layer))
            previous = current_layer
        return jnp.stack(layers_out)
    segment_no = lax.axis_index("section")
    routed = gather_rows(columns)
    handed = jnp.zeros((tokens, features), jnp.bfloat16)
    finished = []
    for turn_no in range(batches + 1):
        if turn_no < batches:
            fresh_rows = inputs[turn_no]
        else:
            fresh_rows = jnp.zeros((tokens, features), jnp.bfloat16)
        current = jnp.where(segment_no == 0, fresh_rows, handed)
        batch_pick = jnp.clip(turn_no - segment_no, 0, batches - 1)
        rows = gather_rows(norm_rows(current, norm_gain[0]))
        result = moe_layer(
            current, rows, routed, column_of(0, batch_pick), w_gate_up[0, 0], w_down[0, 0]
        )
        finished.append(result)
        if turn_no < batches:
            handed = from_behind(result, "section", 1)
    first_segment = jnp.stack(finished[:batches])
    second_segment = jnp.stack(finished[1:])
    return jnp.where(segment_no == 0, first_segment, second_segment)[None]


def solution(mesh):
    placed = (
        P(None, ("groups", "expert"), None),
        P("section", None, ("groups", "expert"), None),
        P("section", None),
        P("section", "expert", None, None),
        P("section", "expert", None, None),
    )
    return jax.shard_map(
        on_device,
        mesh=mesh,
        in_specs=placed,
        out_specs=P("section", None, ("groups", "expert"), None),
        check_vma=False,
    )
```

time: 249 us -> 158 us (0.63)
  waiting for transfers between devices: 143 us -> 33.1 us
  matrix products: 42.2 us -> 0 us
  local copies, waits for them, and re-layouts: 1.88 us -> 42.3 us
  Pallas kernels: 0 us -> 23.3 us
  starting transfers between devices: 55.4 us -> 49.9 us
  other arithmetic: 4.27 us -> 7.91 us
    all_to_all x8 -> x0, waiting for transfers between devices: 143 us -> none  [the longest x4 72 us: moe_layer(): lax.all_to_all(results, 'expert', split_axis=0, concat_axis=0, tiled=True)]
    all_to_all x8 -> x0, starting transfers between devices: 55.4 us -> none  [the longest x4 28 us: moe_layer(): lax.all_to_all(outgoing, 'expert', split_axis=0, concat_axis=0, tiled=True)]
    ppermute x0 -> x40, starting transfers between devices: none -> 49.9 us  [swap(): lax.ppermute(value, 'expert', [(i, partner(i)) for i in range(count)])]
    dot_general x16 -> x0, matrix products: 42.2 us -> none  [the longest x4 18.3 us: expert_rows(): joined = jnp.dot(rows, gate_up, preferred_element_type=jnp.float32)]
    ppermute x0 -> x40, waiting for transfers between devices: none -> 33.1 us  [swap(): lax.ppermute(value, 'expert', [(i, partner(i)) for i in range(count)])]
    pallas_call x0 -> x4, Pallas kernels: none -> 23.3 us  [run_expert(): pl.pallas_call(expert_kernel, out_shape=(jax.ShapeDtypeStruct((half, feat...]
    squeeze x0 -> x2, local copies, waits for them, and re-layouts: none -> 15.5 us  [the longest x1 10.2 us: on_device(): w_gate_up[layer_no, 0]]
    unnamed x2 -> x34, local copies, waits for them, and re-layouts: 0.01 us -> 13.7 us
  transfers between devices with their start and end apart: 8 -> 40, of which waited for: 8 -> 15; matrix products, arithmetic and copies ran while one was open for 17% -> 24% of each run, Pallas kernels for 0% -> 11%
where the time goes in v1:
time: 158 us; the launch traced here: 157 us
  starting transfers between devices  49.9 us (32%)
  local copies, waits for them, and re-layouts  42.3 us (27%)
  waiting for transfers between devices  33.1 us (21%)
  Pallas kernels  23.3 us (15%)
  other arithmetic  7.91 us (5%)
    ppermute x40, starting transfers between devices, swap(): lax.ppermute(value, 'expert', [(i, partner(i)) for i in range(count)])  49.9 us
    ppermute x40, waiting for transfers between devices, swap(): lax.ppermute(value, 'expert', [(i, partner(i)) for i in range(count)])  33.1 us
    pallas_call x4, Pallas kernels, run_expert(): pl.pallas_call(expert_kernel, out_shape=(jax.ShapeDtypeStruct((half, feat...  23.3 us
    unnamed x34, local copies, waits for them, and re-layouts  13.7 us
    concatenate x8, local copies, waits for them, and re-layouts, gather_rows(): jnp.concatenate([rows] + [swap(rows, level, k) for k in range(1, level[1])])  10.9 us
    squeeze x1, local copies, waits for them, and re-layouts, on_device(): w_gate_up[layer_no, 0]  10.2 us
    squeeze x1, local copies, waits for them, and re-layouts, on_device(): w_down[layer_no, 0]  5.33 us
  transfers between devices with their start and end apart: 40, of which 15 were waited for; matrix products, arithmetic and copies ran while one was open for 24% of the time, Pallas kernels for 11%

profile of v1, /device:TPU:0, one launch (start us, length us, event | category | flops | bytes accessed | tf_op | source)
XLA Modules:
  0.0 156.9 jit_solution(1859797406882480946)
XLA Ops:
  0.0 1.0 fusion.9
  1.8 1.5 constant_dynamic-update-slice_fusion.15
  3.4 3.0 %collective-permute-start.10 = (bf16[16,2048]{1,0:T(8,128)(2,1)S(1)}, bf16[16,2048]{1,0:T(8,128)(2,1)S(1)}, u32[]{:S(2)}, u32[]{:S(2)}) collective-permute-start(bf16[16,2048]{1,0:T(8,128)(2,1)S(1)} %get-tuple-element.40), channel_id=1, source_target_pairs={{0,4},{1,5},{2,6},{3,7},{4,0},{5,1},{6,2},{7,3},{8,12},{9,13},{10,... | collective-permute-start | bytes 196616 | tf_op jit(solution)/shard_map/ppermute | solution.py:40
  6.4 2.6 %collective-permute-start.11 = (bf16[16,2048]{1,0:T(8,128)(2,1)S(1)}, bf16[16,2048]{1,0:T(8,128)(2,1)S(1)}, u32[]{:S(2)}, u32[]{:S(2)}) collective-permute-start(bf16[16,2048]{1,0:T(8,128)(2,1)S(1)} %get-tuple-element.40), channel_id=1, source_target_pairs={{0,8},{1,9},{2,10},{3,11},{4,12},{5,13},{6,14},{7,15},{8,0},{9,1},... | collective-permute-start | bytes 196616 | tf_op jit(solution)/shard_map/ppermute | solution.py:40
  12.6 3.5 %collective-permute-start.1 = (bf16[16,2176]{1,0:T(8,128)(2,1)S(1)}, bf16[16,2176]{1,0:T(8,128)(2,1)S(1)}, u32[]{:S(2)}, u32[]{:S(2)}) collective-permute-start(bf16[16,2176]{1,0:T(8,128)(2,1)S(1)} %get-tuple-element.75), channel_id=1, source_target_pairs={{0,8},{1,9},{2,10},{3,11},{4,12},{5,13},{6,14},{7,15},{8,0},{9,1},... | collective-permute-start | bytes 208904 | tf_op jit(solution)/shard_map/ppermute | solution.py:40
  16.1 10.2 %slice_bitcast_fusion = (bf16[2048,1536]{1,0:T(8,128)(2,1)}, bf16[2048,1536]{1,0:T(8,128)(2,1)}) fusion(bf16[2,1,2048,1536]{3,2,1,0:T(8,128)(2,1)} %param.8), kind=kLoop, calls=%fused_computation | loop fusion | bytes 25165824 | tf_op jit(solution)/shard_map/squeeze | solution.py:152
  26.5 1.8 %collective-permute-start.13 = (bf16[64,2048]{1,0:T(8,128)(2,1)S(1)}, bf16[64,2048]{1,0:T(8,128)(2,1)S(1)}, u32[]{:S(2)}, u32[]{:S(2)}) collective-permute-start(bf16[64,2048]{1,0:T(8,128)(2,1)S(1)} %pad_maximum_fusion.1), channel_id=1, source_target_pairs={{0,2},{1,3},{2,0},{3,1},{4,6},{5,7},{6,4},{7,5},{8,10},{9,11},{10,... | collective-permute-start | bytes 786440 | tf_op jit(solution)/shard_map/ppermute | solution.py:40
  30.1 2.4 %collective-permute-done.2 = bf16[16,2176]{1,0:T(8,128)(2,1)S(1)} collective-permute-done((bf16[16,2176]{1,0:T(8,128)(2,1)S(1)}, bf16[16,2176]{1,0:T(8,128)(2,1)S(1)}, u32[]{:S(2)}, u32[]{:S(2)}) %collective-permute-start.2) | collective-permute-done | bytes 69664 | tf_op jit(solution)/shard_map/ppermute | solution.py:40
  32.5 1.6 %collective-permute-start.3 = (bf16[64,2176]{1,0:T(8,128)(2,1)S(1)}, bf16[64,2176]{1,0:T(8,128)(2,1)S(1)}, u32[]{:S(2)}, u32[]{:S(2)}) collective-permute-start(bf16[64,2176]{1,0:T(8,128)(2,1)S(1)} %pad_maximum_fusion), channel_id=1, source_target_pairs={{0,2},{1,3},{2,0},{3,1},{4,6},{5,7},{6,4},{7,5},{8,10},{9,11},{10,... | collective-permute-start | bytes 835592 | tf_op jit(solution)/shard_map/ppermute | solution.py:40
  36.8 2.4 %collective-permute-done.3 = bf16[64,2176]{1,0:T(8,128)(2,1)S(1)} collective-permute-done((bf16[64,2176]{1,0:T(8,128)(2,1)S(1)}, bf16[64,2176]{1,0:T(8,128)(2,1)S(1)}, u32[]{:S(2)}, u32[]{:S(2)}) %collective-permute-start.3) | collective-permute-done | bytes 278560 | tf_op jit(solution)/shard_map/ppermute | solution.py:40
  39.9 1.0 copy-done.6
  40.9 5.3 %slice_bitcast_fusion.2 = (bf16[768,2048]{1,0:T(8,128)(2,1)S(1)}, bf16[768,2048]{1,0:T(8,128)(2,1)}) fusion(bf16[2,1,768,2048]{3,2,1,0:T(8,128)(2,1)} %param.9), kind=kLoop, calls=%fused_computation.2 | loop fusion | bytes 12582912 | tf_op jit(solution)/shard_map/squeeze | solution.py:153
  46.2 1.9 %constant_dynamic-update-slice_fusion.16.rows_ref = bf16[256,2048]{1,0:T(8,128)(2,1)} fusion(bf16[256,2048]{1,0:T(8,128)(2,1)} %copy-done.2, bf16[128,2048]{1,0:T(8,128)(2,1)} %collective-permute-done.14), kind=kLoop, calls=%fused_computation.85 | loop fusion | bytes 1048576 | tf_op jit(solution)/shard_map/concatenate | solution.py:46
  48.1 2.0 %constant_dynamic-update-slice_fusion.5 = bf16[256,2176]{1,0:T(8,128)(2,1)} fusion(bf16[256,2176]{1,0:T(8,128)(2,1)} %copy-done.6, bf16[128,2176]{1,0:T(8,128)(2,1)} %collective-permute-done.4), kind=kLoop, calls=%fused_computation.74 | loop fusion | bytes 1114112 | tf_op jit(solution)/shard_map/concatenate | solution.py:46
  50.9 1.9 %copy-done = bf16[768,2048]{1,0:T(8,128)(2,1)S(1)} copy-done((bf16[768,2048]{1,0:T(8,128)(2,1)S(1)}, bf16[768,2048]{1,0:T(8,128)(2,1)}, u32[]{:S(2)}) %copy-start) | copy-done | bytes 3145752
  52.8 5.5 %shard_map.56 = (f32[128,2048]{1,0:T(8,128)S(1)}, bf16[128,2048]{1,0:T(8,128)(2,1)S(1)}) custom-call(s32[1]{0:T(128)} %bitcast.10.column_ref, bf16[256,2048]{1,0:T(8,128)(2,1)S(1)} %copy-done.3, bf16[256,128]{1,0:T(8,128)(2,1)S(1)} %slice.159.routed_ref, bf16[2048,1536]{1,0:T(8,128)(2,1)} %get-tuple-element.42.gate_up_ref, bf16[768,2048]{1,0:T(8,128)(2,1)S(1)} %copy-done), custom_call_target="tpu_custom_call" | custom-call | tf_op jit(solution)/shard_map/pallas_call | solution.py:90
  59.1 5.4 %shard_map.55 = (f32[128,2048]{1,0:T(8,128)S(1)}, bf16[128,2048]{1,0:T(8,128)(2,1)S(1)}) custom-call(s32[1]{0:T(128)} %bitcast.1.column_ref, bf16[256,2048]{1,0:T(8,128)(2,1)S(1)} %slice.158.rows_ref, bf16[256,128]{1,0:T(8,128)(2,1)S(1)} %slice.159.routed_ref, bf16[2048,1536]{1,0:T(8,128)(2,1)} %get-tuple-element.42.gate_up_ref, bf16[768,2048]{1,0:T(8,128)(2,1)S(1)} %copy-done.1), custom_call_target="tpu_custom_call" | custom-call | tf_op jit(solution)/shard_map/pallas_call | solution.py:90
  64.7 1.6 %collective-permute-start.16 = (bf16[64,2048]{1,0:T(8,128)(2,1)S(1)}, bf16[64,2048]{1,0:T(8,128)(2,1)S(1)}, u32[]{:S(2)}, u32[]{:S(2)}) collective-permute-start(bf16[64,2048]{1,0:T(8,128)(2,1)S(1)} %slice.244), channel_id=1, source_target_pairs={{0,2},{1,3},{2,0},{3,1},{4,6},{5,7},{6,4},{7,5},{8,10},{9,11},{10,... | collective-permute-start | bytes 786440 | tf_op jit(solution)/shard_map/ppermute | solution.py:40
  66.6 1.6 %collective-permute-start.6 = (bf16[64,2048]{1,0:T(8,128)(2,1)S(1)}, bf16[64,2048]{1,0:T(8,128)(2,1)S(1)}, u32[]{:S(2)}, u32[]{:S(2)}) collective-permute-start(bf16[64,2048]{1,0:T(8,128)(2,1)S(1)} %slice.245), channel_id=1, source_target_pairs={{0,2},{1,3},{2,0},{3,1},{4,6},{5,7},{6,4},{7,5},{8,10},{9,11},{10,... | collective-permute-start | bytes 786440 | tf_op jit(solution)/shard_map/ppermute | solution.py:40
  68.2 5.7 %collective-permute-done.16 = bf16[64,2048]{1,0:T(8,128)(2,1)S(1)} collective-permute-done((bf16[64,2048]{1,0:T(8,128)(2,1)S(1)}, bf16[64,2048]{1,0:T(8,128)(2,1)S(1)}, u32[]{:S(2)}, u32[]{:S(2)}) %collective-permute-start.16) | collective-permute-done | bytes 262176 | tf_op jit(solution)/shard_map/ppermute | solution.py:40
  74.6 3.5 %collective-permute-start.18 = (bf16[16,2048]{1,0:T(8,128)(2,1)S(1)}, bf16[16,2048]{1,0:T(8,128)(2,1)S(1)}, u32[]{:S(2)}, u32[]{:S(2)}) collective-permute-start(bf16[16,2048]{1,0:T(8,128)(2,1)S(1)} %get-tuple-element.62), channel_id=1, source_target_pairs={{0,8},{1,9},{2,10},{3,11},{4,12},{5,13},{6,14},{7,15},{8,0},{9,1},... | collective-permute-start | bytes 196616 | tf_op jit(solution)/shard_map/ppermute | solution.py:40
  79.8 3.5 %collective-permute-start.8 = (bf16[16,2048]{1,0:T(8,128)(2,1)S(1)}, bf16[16,2048]{1,0:T(8,128)(2,1)S(1)}, u32[]{:S(2)}, u32[]{:S(2)}) collective-permute-start(bf16[16,2048]{1,0:T(8,128)(2,1)S(1)} %get-tuple-element.54), channel_id=1, source_target_pairs={{0,8},{1,9},{2,10},{3,11},{4,12},{5,13},{6,14},{7,15},{8,0},{9,1},... | collective-permute-start | bytes 196616 | tf_op jit(solution)/shard_map/ppermute | solution.py:40
  83.7 1.4 collective-permute-done.19
  85.0 3.4 %collective-permute-done.8 = bf16[16,2048]{1,0:T(8,128)(2,1)S(1)} collective-permute-done((bf16[16,2048]{1,0:T(8,128)(2,1)S(1)}, bf16[16,2048]{1,0:T(8,128)(2,1)S(1)}, u32[]{:S(2)}, u32[]{:S(2)}) %collective-permute-start.8) | collective-permute-done | bytes 65568 | tf_op jit(solution)/shard_map/ppermute | solution.py:40
  88.4 1.1 collective-permute-done.9
  90.5 0.9 collective-permute-start.20
  91.4 1.1 collective-permute-start.21
  92.5 2.4 %collective-permute-start.22 = (bf16[16,2048]{1,0:T(8,128)(2,1)S(1)}, bf16[16,2048]{1,0:T(8,128)(2,1)S(1)}, u32[]{:S(2)}, u32[]{:S(2)}) collective-permute-start(bf16[16,2048]{1,0:T(8,128)(2,1)S(1)} %get-tuple-element.26), channel_id=1, source_target_pairs={{0,12},{1,13},{2,14},{3,15},{4,8},{5,9},{6,10},{7,11},{8,4},{9,5},... | collective-permute-start | bytes 196616 | tf_op jit(solution)/shard_map/ppermute | solution.py:40
  95.6 2.0 %collective-permute-start.31 = (bf16[16,2048]{1,0:T(8,128)(2,1)S(1)}, bf16[16,2048]{1,0:T(8,128)(2,1)S(1)}, u32[]{:S(2)}, u32[]{:S(2)}) collective-permute-start(bf16[16,2048]{1,0:T(8,128)(2,1)S(1)} %get-tuple-element.97), channel_id=1, source_target_pairs={{0,8},{1,9},{2,10},{3,11},{4,12},{5,13},{6,14},{7,15},{8,0},{9,1},... | collective-permute-start | bytes 196616 | tf_op jit(solution)/shard_map/ppermute | solution.py:40
  98.2 2.4 %collective-permute-start.32 = (bf16[16,2048]{1,0:T(8,128)(2,1)S(1)}, bf16[16,2048]{1,0:T(8,128)(2,1)S(1)}, u32[]{:S(2)}, u32[]{:S(2)}) collective-permute-start(bf16[16,2048]{1,0:T(8,128)(2,1)S(1)} %get-tuple-element.97), channel_id=1, source_target_pairs={{0,12},{1,13},{2,14},{3,15},{4,8},{5,9},{6,10},{7,11},{8,4},{9,5},... | collective-permute-start | bytes 196616 | tf_op jit(solution)/shard_map/ppermute | solution.py:40
  100.6 1.6 %collective-permute-start.23 = (bf16[64,2048]{1,0:T(8,128)(2,1)S(1)}, bf16[64,2048]{1,0:T(8,128)(2,1)S(1)}, u32[]{:S(2)}, u32[]{:S(2)}) collective-permute-start(bf16[64,2048]{1,0:T(8,128)(2,1)S(1)} %pad_maximum_fusion.2), channel_id=1, source_target_pairs={{0,2},{1,3},{2,0},{3,1},{4,6},{5,7},{6,4},{7,5},{8,10},{9,11},{10,... | collective-permute-start | bytes 786440 | tf_op jit(solution)/shard_map/ppermute | solution.py:40
  103.0 1.3 collective-permute-done.32
  104.4 1.6 %collective-permute-start.33 = (bf16[64,2048]{1,0:T(8,128)(2,1)S(1)}, bf16[64,2048]{1,0:T(8,128)(2,1)S(1)}, u32[]{:S(2)}, u32[]{:S(2)}) collective-permute-start(bf16[64,2048]{1,0:T(8,128)(2,1)S(1)} %pad_maximum_fusion.3), channel_id=1, source_target_pairs={{0,2},{1,3},{2,0},{3,1},{4,6},{5,7},{6,4},{7,5},{8,10},{9,11},{10,... | collective-permute-start | bytes 786440 | tf_op jit(solution)/shard_map/ppermute | solution.py:40
  112.5 1.9 %constant_dynamic-update-slice_fusion.27.rows_ref = bf16[256,2048]{1,0:T(8,128)(2,1)} fusion(bf16[256,2048]{1,0:T(8,128)(2,1)} %get-tuple-element.51, bf16[128,2048]{1,0:T(8,128)(2,1)} %collective-permute-done.24), kind=kLoop, calls=%fused_computation.96 | loop fusion | bytes 1048576 | tf_op jit(solution)/shard_map/concatenate | solution.py:46
  114.5 6.6 %shard_map.57 = (f32[128,2048]{1,0:T(8,128)S(1)}, bf16[128,2048]{1,0:T(8,128)(2,1)}) custom-call(s32[1]{0:T(128)} %bitcast.14.column_ref, bf16[256,2048]{1,0:T(8,128)(2,1)} %constant_dynamic-update-slice_fusion.27.rows_ref, bf16[256,128]{1,0:T(8,128)(2,1)S(1)} %slice.159.routed_ref, bf16[2048,1536]{1,0:T(8,128)(2,1)} %get-tuple-element.41.gate_up_ref, ...), custom_call_target="tpu_custom_call" | custom-call | tf_op jit(solution)/shard_map/pallas_call | solution.py:90
  121.0 1.0 copy-done.4
  122.6 1.9 %constant_dynamic-update-slice_fusion.38.rows_ref = bf16[256,2048]{1,0:T(8,128)(2,1)} fusion(bf16[256,2048]{1,0:T(8,128)(2,1)} %get-tuple-element.59, bf16[128,2048]{1,0:T(8,128)(2,1)} %collective-permute-done.34), kind=kLoop, calls=%fused_computation.107 | loop fusion | bytes 1048576 | tf_op jit(solution)/shard_map/concatenate | solution.py:46
  124.5 5.8 %shard_map.58 = (f32[128,2048]{1,0:T(8,128)S(1)}, bf16[128,2048]{1,0:T(8,128)(2,1)S(1)}) custom-call(s32[1]{0:T(128)} %bitcast.19.column_ref, bf16[256,2048]{1,0:T(8,128)(2,1)} %constant_dynamic-update-slice_fusion.38.rows_ref, bf16[256,128]{1,0:T(8,128)(2,1)S(1)} %slice.159.routed_ref, bf16[2048,1536]{1,0:T(8,128)(2,1)} %get-tuple-element.41.gate_up_ref, ...), custom_call_target="tpu_custom_call" | custom-call | tf_op jit(solution)/shard_map/pallas_call | solution.py:90
  130.4 1.1 convert_add_fusion.1
  131.6 1.6 %collective-permute-start.26 = (bf16[64,2048]{1,0:T(8,128)(2,1)S(1)}, bf16[64,2048]{1,0:T(8,128)(2,1)S(1)}, u32[]{:S(2)}, u32[]{:S(2)}) collective-permute-start(bf16[64,2048]{1,0:T(8,128)(2,1)S(1)} %slice.243), channel_id=1, source_target_pairs={{0,2},{1,3},{2,0},{3,1},{4,6},{5,7},{6,4},{7,5},{8,10},{9,11},{10,... | collective-permute-start | bytes 786440 | tf_op jit(solution)/shard_map/ppermute | solution.py:40
  134.0 6.8 %collective-permute-done.26 = bf16[64,2048]{1,0:T(8,128)(2,1)S(1)} collective-permute-done((bf16[64,2048]{1,0:T(8,128)(2,1)S(1)}, bf16[64,2048]{1,0:T(8,128)(2,1)S(1)}, u32[]{:S(2)}, u32[]{:S(2)}) %collective-permute-start.26) | collective-permute-done | bytes 262176 | tf_op jit(solution)/shard_map/ppermute | solution.py:40
  140.9 2.1 %collective-permute-start.27 = (bf16[16,2048]{1,0:T(8,128)(2,1)S(1)}, bf16[16,2048]{1,0:T(8,128)(2,1)S(1)}, u32[]{:S(2)}, u32[]{:S(2)}) collective-permute-start(bf16[16,2048]{1,0:T(8,128)(2,1)S(1)} %get-tuple-element.47), channel_id=1, source_target_pairs={{0,4},{1,5},{2,6},{3,7},{4,0},{5,1},{6,2},{7,3},{8,12},{9,13},{10,... | collective-permute-start | bytes 196616 | tf_op jit(solution)/shard_map/ppermute | solution.py:40
  143.9 1.5 collective-permute-start.29
  146.1 2.1 %collective-permute-start.37 = (bf16[16,2048]{1,0:T(8,128)(2,1)S(1)}, bf16[16,2048]{1,0:T(8,128)(2,1)S(1)}, u32[]{:S(2)}, u32[]{:S(2)}) collective-permute-start(bf16[16,2048]{1,0:T(8,128)(2,1)S(1)} %get-tuple-element.55), channel_id=1, source_target_pairs={{0,4},{1,5},{2,6},{3,7},{4,0},{5,1},{6,2},{7,3},{8,12},{9,13},{10,... | collective-permute-start | bytes 196616 | tf_op jit(solution)/shard_map/ppermute | solution.py:40
  148.2 0.9 collective-permute-start.38
  149.1 1.5 collective-permute-start.39
  150.7 1.3 collective-permute-done.37
  151.9 4.1 %collective-permute-done.38 = bf16[16,2048]{1,0:T(8,128)(2,1)S(1)} collective-permute-done((bf16[16,2048]{1,0:T(8,128)(2,1)S(1)}, bf16[16,2048]{1,0:T(8,128)(2,1)S(1)}, u32[]{:S(2)}, u32[]{:S(2)}) %collective-permute-start.38) | collective-permute-done | bytes 65568 | tf_op jit(solution)/shard_map/ppermute | solution.py:40
  (121 shorter events, 28.3 us)
Async XLA Ops:
  3.4 22.9 %collective-permute-start.10 = (bf16[16,2048]{1,0:T(8,128)(2,1)S(1)}, bf16[16,2048]{1,0:T(8,128)(2,1)S(1)}, u32[]{:S(2)}, u32[]{:S(2)}) collective-permute-start(bf16[16,2048]{1,0:T(8,128)(2,1)S(1)} %get-tuple-element.40), channel_id=1, source_target_pairs={{0,4},{1,5},{2,6},{3,7},{4,0},{5,1},{6,2},{7,3},{8,12},{9,13},{10,... | collective-permute-start | bytes 196616 | tf_op jit(solution)/shard_map/ppermute | solution.py:40
  6.4 20.0 %collective-permute-start.11 = (bf16[16,2048]{1,0:T(8,128)(2,1)S(1)}, bf16[16,2048]{1,0:T(8,128)(2,1)S(1)}, u32[]{:S(2)}, u32[]{:S(2)}) collective-permute-start(bf16[16,2048]{1,0:T(8,128)(2,1)S(1)} %get-tuple-element.40), channel_id=1, source_target_pairs={{0,8},{1,9},{2,10},{3,11},{4,12},{5,13},{6,14},{7,15},{8,0},{9,1},... | collective-permute-start | bytes 196616 | tf_op jit(solution)/shard_map/ppermute | solution.py:40
  9.0 17.4 %collective-permute-start.12 = (bf16[16,2048]{1,0:T(8,128)(2,1)S(1)}, bf16[16,2048]{1,0:T(8,128)(2,1)S(1)}, u32[]{:S(2)}, u32[]{:S(2)}) collective-permute-start(bf16[16,2048]{1,0:T(8,128)(2,1)S(1)} %get-tuple-element.40), channel_id=1, source_target_pairs={{0,12},{1,13},{2,14},{3,15},{4,8},{5,9},{6,10},{7,11},{8,4},{9,5},... | collective-permute-start | bytes 196616 | tf_op jit(solution)/shard_map/ppermute | solution.py:40
  11.7 18.4 %collective-permute-start = (bf16[16,2176]{1,0:T(8,128)(2,1)S(1)}, bf16[16,2176]{1,0:T(8,128)(2,1)S(1)}, u32[]{:S(2)}, u32[]{:S(2)}) collective-permute-start(bf16[16,2176]{1,0:T(8,128)(2,1)S(1)} %get-tuple-element.75), channel_id=1, source_target_pairs={{0,4},{1,5},{2,6},{3,7},{4,0},{5,1},{6,2},{7,3},{8,12},{9,13},{10,... | collective-permute-start | bytes 208904 | tf_op jit(solution)/shard_map/ppermute | solution.py:40
  12.6 17.5 %collective-permute-start.1 = (bf16[16,2176]{1,0:T(8,128)(2,1)S(1)}, bf16[16,2176]{1,0:T(8,128)(2,1)S(1)}, u32[]{:S(2)}, u32[]{:S(2)}) collective-permute-start(bf16[16,2176]{1,0:T(8,128)(2,1)S(1)} %get-tuple-element.75), channel_id=1, source_target_pairs={{0,8},{1,9},{2,10},{3,11},{4,12},{5,13},{6,14},{7,15},{8,0},{9,1},... | collective-permute-start | bytes 208904 | tf_op jit(solution)/shard_map/ppermute | solution.py:40
  26.3 6.2 %collective-permute-start.2 = (bf16[16,2176]{1,0:T(8,128)(2,1)S(1)}, bf16[16,2176]{1,0:T(8,128)(2,1)S(1)}, u32[]{:S(2)}, u32[]{:S(2)}) collective-permute-start(bf16[16,2176]{1,0:T(8,128)(2,1)S(1)} %get-tuple-element.75), channel_id=1, source_target_pairs={{0,12},{1,13},{2,14},{3,15},{4,8},{5,9},{6,10},{7,11},{8,4},{9,5},... | collective-permute-start | bytes 208904 | tf_op jit(solution)/shard_map/ppermute | solution.py:40
  26.5 9.6 %collective-permute-start.13 = (bf16[64,2048]{1,0:T(8,128)(2,1)S(1)}, bf16[64,2048]{1,0:T(8,128)(2,1)S(1)}, u32[]{:S(2)}, u32[]{:S(2)}) collective-permute-start(bf16[64,2048]{1,0:T(8,128)(2,1)S(1)} %pad_maximum_fusion.1), channel_id=1, source_target_pairs={{0,2},{1,3},{2,0},{3,1},{4,6},{5,7},{6,4},{7,5},{8,10},{9,11},{10,... | collective-permute-start | bytes 786440 | tf_op jit(solution)/shard_map/ppermute | solution.py:40
  32.5 6.6 %collective-permute-start.3 = (bf16[64,2176]{1,0:T(8,128)(2,1)S(1)}, bf16[64,2176]{1,0:T(8,128)(2,1)S(1)}, u32[]{:S(2)}, u32[]{:S(2)}) collective-permute-start(bf16[64,2176]{1,0:T(8,128)(2,1)S(1)} %pad_maximum_fusion), channel_id=1, source_target_pairs={{0,2},{1,3},{2,0},{3,1},{4,6},{5,7},{6,4},{7,5},{8,10},{9,11},{10,... | collective-permute-start | bytes 835592 | tf_op jit(solution)/shard_map/ppermute | solution.py:40
  36.8 3.1 %copy-start.2 = (bf16[256,2048]{1,0:T(8,128)(2,1)}, bf16[256,2048]{1,0:T(8,128)(2,1)S(1)}, u32[]{:S(2)}) copy-start(bf16[256,2048]{1,0:T(8,128)(2,1)S(1)} %get-tuple-element.64) | copy-start | bytes 3145732
  36.8 9.5 %collective-permute-start.14 = (bf16[128,2048]{1,0:T(8,128)(2,1)}, bf16[128,2048]{1,0:T(8,128)(2,1)}, u32[]{:S(2)}, u32[]{:S(2)}) collective-permute-start(bf16[128,2048]{1,0:T(8,128)(2,1)} %get-tuple-element.63), channel_id=1, source_target_pairs={{0,1},{1,0},{2,3},{3,2},{4,5},{5,4},{6,7},{7,6},{8,9},{9,8},{10,11... | collective-permute-start | bytes 1572872 | tf_op jit(solution)/shard_map/ppermute | solution.py:40
  40.9 7.2 %collective-permute-start.4 = (bf16[128,2176]{1,0:T(8,128)(2,1)}, bf16[128,2176]{1,0:T(8,128)(2,1)}, u32[]{:S(2)}, u32[]{:S(2)}) collective-permute-start(bf16[128,2176]{1,0:T(8,128)(2,1)} %get-tuple-element.45), channel_id=1, source_target_pairs={{0,1},{1,0},{2,3},{3,2},{4,5},{5,4},{6,7},{7,6},{8,9},{9,8},{10,11... | collective-permute-start | bytes 1671176 | tf_op jit(solution)/shard_map/ppermute | solution.py:40
  48.1 2.8 %copy-start.3 = (bf16[256,2048]{1,0:T(8,128)(2,1)S(1)}, bf16[256,2048]{1,0:T(8,128)(2,1)}, u32[]{:S(2)}) copy-start(bf16[256,2048]{1,0:T(8,128)(2,1)} %constant_dynamic-update-slice_fusion.16.rows_ref) | copy-start | bytes 3145732
  50.9 1.9 %copy-start = (bf16[768,2048]{1,0:T(8,128)(2,1)S(1)}, bf16[768,2048]{1,0:T(8,128)(2,1)}, u32[]{:S(2)}) copy-start(bf16[768,2048]{1,0:T(8,128)(2,1)} %get-tuple-element.44.down_ref) | copy-start | bytes 9437188
  52.8 6.1 %copy-start.7 = (bf16[256,2176]{1,0:T(8,128)(2,1)S(1)}, bf16[256,2176]{1,0:T(8,128)(2,1)}, u32[]{:S(2)}) copy-start(bf16[256,2176]{1,0:T(8,128)(2,1)} %constant_dynamic-update-slice_fusion.5) | copy-start | bytes 3342340
  52.8 6.3 %copy-start.1 = (bf16[768,2048]{1,0:T(8,128)(2,1)S(1)}, bf16[768,2048]{1,0:T(8,128)(2,1)}, u32[]{:S(2)}) copy-start(bf16[768,2048]{1,0:T(8,128)(2,1)} %get-tuple-element.44.down_ref) | copy-start | bytes 9437188
  58.4 6.2 %collective-permute-start.15 = (bf16[128,2048]{1,0:T(8,128)(2,1)S(1)}, bf16[128,2048]{1,0:T(8,128)(2,1)S(1)}, u32[]{:S(2)}, u32[]{:S(2)}) collective-permute-start(bf16[128,2048]{1,0:T(8,128)(2,1)S(1)} %get-tuple-element.16), channel_id=1, source_target_pairs={{0,1},{1,0},{2,3},{3,2},{4,5},{5,4},{6,7},{7,6},{8,9},{9,8},{10,11... | collective-permute-start | bytes 1572872 | tf_op jit(solution)/shard_map/ppermute | solution.py:40
  64.5 2.0 %collective-permute-start.5 = (bf16[128,2048]{1,0:T(8,128)(2,1)S(1)}, bf16[128,2048]{1,0:T(8,128)(2,1)S(1)}, u32[]{:S(2)}, u32[]{:S(2)}) collective-permute-start(bf16[128,2048]{1,0:T(8,128)(2,1)S(1)} %get-tuple-element.14), channel_id=1, source_target_pairs={{0,1},{1,0},{2,3},{3,2},{4,5},{5,4},{6,7},{7,6},{8,9},{9,8},{10,11... | collective-permute-start | bytes 1572872 | tf_op jit(solution)/shard_map/ppermute | solution.py:40
  64.7 9.2 %collective-permute-start.16 = (bf16[64,2048]{1,0:T(8,128)(2,1)S(1)}, bf16[64,2048]{1,0:T(8,128)(2,1)S(1)}, u32[]{:S(2)}, u32[]{:S(2)}) collective-permute-start(bf16[64,2048]{1,0:T(8,128)(2,1)S(1)} %slice.244), channel_id=1, source_target_pairs={{0,2},{1,3},{2,0},{3,1},{4,6},{5,7},{6,4},{7,5},{8,10},{9,11},{10,... | collective-permute-start | bytes 786440 | tf_op jit(solution)/shard_map/ppermute | solution.py:40
  66.6 12.5 %collective-permute-start.6 = (bf16[64,2048]{1,0:T(8,128)(2,1)S(1)}, bf16[64,2048]{1,0:T(8,128)(2,1)S(1)}, u32[]{:S(2)}, u32[]{:S(2)}) collective-permute-start(bf16[64,2048]{1,0:T(8,128)(2,1)S(1)} %slice.245), channel_id=1, source_target_pairs={{0,2},{1,3},{2,0},{3,1},{4,6},{5,7},{6,4},{7,5},{8,10},{9,11},{10,... | collective-permute-start | bytes 786440 | tf_op jit(solution)/shard_map/ppermute | solution.py:40
  74.0 15.6 %copy-start.8 = (bf16[2,16,2048]{2,1,0:T(8,128)(2,1)S(1)}, bf16[2,16,2048]{2,1,0:T(8,128)(2,1)}, u32[]{:S(2)}) copy-start(bf16[2,16,2048]{2,1,0:T(8,128)(2,1)} %param.5) | copy-start | bytes 393220
  74.0 9.4 %collective-permute-start.17 = (bf16[16,2048]{1,0:T(8,128)(2,1)S(1)}, bf16[16,2048]{1,0:T(8,128)(2,1)S(1)}, u32[]{:S(2)}, u32[]{:S(2)}) collective-permute-start(bf16[16,2048]{1,0:T(8,128)(2,1)S(1)} %get-tuple-element.60), channel_id=1, source_target_pairs={{0,4},{1,5},{2,6},{3,7},{4,0},{5,1},{6,2},{7,3},{8,12},{9,13},{10,... | collective-permute-start | bytes 196616 | tf_op jit(solution)/shard_map/ppermute | solution.py:40
  74.6 9.1 %collective-permute-start.18 = (bf16[16,2048]{1,0:T(8,128)(2,1)S(1)}, bf16[16,2048]{1,0:T(8,128)(2,1)S(1)}, u32[]{:S(2)}, u32[]{:S(2)}) collective-permute-start(bf16[16,2048]{1,0:T(8,128)(2,1)S(1)} %get-tuple-element.62), channel_id=1, source_target_pairs={{0,8},{1,9},{2,10},{3,11},{4,12},{5,13},{6,14},{7,15},{8,0},{9,1},... | collective-permute-start | bytes 196616 | tf_op jit(solution)/shard_map/ppermute | solution.py:40
  78.1 6.9 %collective-permute-start.19 = (bf16[16,2048]{1,0:T(8,128)(2,1)S(1)}, bf16[16,2048]{1,0:T(8,128)(2,1)S(1)}, u32[]{:S(2)}, u32[]{:S(2)}) collective-permute-start(bf16[16,2048]{1,0:T(8,128)(2,1)S(1)} %get-tuple-element.61), channel_id=1, source_target_pairs={{0,12},{1,13},{2,14},{3,15},{4,8},{5,9},{6,10},{7,11},{8,4},{9,5},... | collective-permute-start | bytes 196616 | tf_op jit(solution)/shard_map/ppermute | solution.py:40
  79.2 5.8 %collective-permute-start.7 = (bf16[16,2048]{1,0:T(8,128)(2,1)S(1)}, bf16[16,2048]{1,0:T(8,128)(2,1)S(1)}, u32[]{:S(2)}, u32[]{:S(2)}) collective-permute-start(bf16[16,2048]{1,0:T(8,128)(2,1)S(1)} %get-tuple-element.52), channel_id=1, source_target_pairs={{0,4},{1,5},{2,6},{3,7},{4,0},{5,1},{6,2},{7,3},{8,12},{9,13},{10,... | collective-permute-start | bytes 196616 | tf_op jit(solution)/shard_map/ppermute | solution.py:40
  79.8 8.6 %collective-permute-start.8 = (bf16[16,2048]{1,0:T(8,128)(2,1)S(1)}, bf16[16,2048]{1,0:T(8,128)(2,1)S(1)}, u32[]{:S(2)}, u32[]{:S(2)}) collective-permute-start(bf16[16,2048]{1,0:T(8,128)(2,1)S(1)} %get-tuple-element.54), channel_id=1, source_target_pairs={{0,8},{1,9},{2,10},{3,11},{4,12},{5,13},{6,14},{7,15},{8,0},{9,1},... | collective-permute-start | bytes 196616 | tf_op jit(solution)/shard_map/ppermute | solution.py:40
  83.3 6.2 %collective-permute-start.9 = (bf16[16,2048]{1,0:T(8,128)(2,1)S(1)}, bf16[16,2048]{1,0:T(8,128)(2,1)S(1)}, u32[]{:S(2)}, u32[]{:S(2)}) collective-permute-start(bf16[16,2048]{1,0:T(8,128)(2,1)S(1)} %get-tuple-element.53), channel_id=1, source_target_pairs={{0,12},{1,13},{2,14},{3,15},{4,8},{5,9},{6,10},{7,11},{8,4},{9,5},... | collective-permute-start | bytes 196616 | tf_op jit(solution)/shard_map/ppermute | solution.py:40
  90.5 7.7 %collective-permute-start.20 = (bf16[16,2048]{1,0:T(8,128)(2,1)S(1)}, bf16[16,2048]{1,0:T(8,128)(2,1)S(1)}, u32[]{:S(2)}, u32[]{:S(2)}) collective-permute-start(bf16[16,2048]{1,0:T(8,128)(2,1)S(1)} %get-tuple-element.26), channel_id=1, source_target_pairs={{0,4},{1,5},{2,6},{3,7},{4,0},{5,1},{6,2},{7,3},{8,12},{9,13},{10,... | collective-permute-start | bytes 196616 | tf_op jit(solution)/shard_map/ppermute | solution.py:40
  91.4 9.1 %collective-permute-start.21 = (bf16[16,2048]{1,0:T(8,128)(2,1)S(1)}, bf16[16,2048]{1,0:T(8,128)(2,1)S(1)}, u32[]{:S(2)}, u32[]{:S(2)}) collective-permute-start(bf16[16,2048]{1,0:T(8,128)(2,1)S(1)} %get-tuple-element.26), channel_id=1, source_target_pairs={{0,8},{1,9},{2,10},{3,11},{4,12},{5,13},{6,14},{7,15},{8,0},{9,1},... | collective-permute-start | bytes 196616 | tf_op jit(solution)/shard_map/ppermute | solution.py:40
  92.5 8.0 %collective-permute-start.22 = (bf16[16,2048]{1,0:T(8,128)(2,1)S(1)}, bf16[16,2048]{1,0:T(8,128)(2,1)S(1)}, u32[]{:S(2)}, u32[]{:S(2)}) collective-permute-start(bf16[16,2048]{1,0:T(8,128)(2,1)S(1)} %get-tuple-element.26), channel_id=1, source_target_pairs={{0,12},{1,13},{2,14},{3,15},{4,8},{5,9},{6,10},{7,11},{8,4},{9,5},... | collective-permute-start | bytes 196616 | tf_op jit(solution)/shard_map/ppermute | solution.py:40
  95.5 6.6 %collective-permute-start.30 = (bf16[16,2048]{1,0:T(8,128)(2,1)S(1)}, bf16[16,2048]{1,0:T(8,128)(2,1)S(1)}, u32[]{:S(2)}, u32[]{:S(2)}) collective-permute-start(bf16[16,2048]{1,0:T(8,128)(2,1)S(1)} %get-tuple-element.97), channel_id=1, source_target_pairs={{0,4},{1,5},{2,6},{3,7},{4,0},{5,1},{6,2},{7,3},{8,12},{9,13},{10,... | collective-permute-start | bytes 196616 | tf_op jit(solution)/shard_map/ppermute | solution.py:40
  95.6 7.4 %collective-permute-start.31 = (bf16[16,2048]{1,0:T(8,128)(2,1)S(1)}, bf16[16,2048]{1,0:T(8,128)(2,1)S(1)}, u32[]{:S(2)}, u32[]{:S(2)}) collective-permute-start(bf16[16,2048]{1,0:T(8,128)(2,1)S(1)} %get-tuple-element.97), channel_id=1, source_target_pairs={{0,8},{1,9},{2,10},{3,11},{4,12},{5,13},{6,14},{7,15},{8,0},{9,1},... | collective-permute-start | bytes 196616 | tf_op jit(solution)/shard_map/ppermute | solution.py:40
  98.2 6.2 %collective-permute-start.32 = (bf16[16,2048]{1,0:T(8,128)(2,1)S(1)}, bf16[16,2048]{1,0:T(8,128)(2,1)S(1)}, u32[]{:S(2)}, u32[]{:S(2)}) collective-permute-start(bf16[16,2048]{1,0:T(8,128)(2,1)S(1)} %get-tuple-element.97), channel_id=1, source_target_pairs={{0,12},{1,13},{2,14},{3,15},{4,8},{5,9},{6,10},{7,11},{8,4},{9,5},... | collective-permute-start | bytes 196616 | tf_op jit(solution)/shard_map/ppermute | solution.py:40
  100.6 8.7 %collective-permute-start.23 = (bf16[64,2048]{1,0:T(8,128)(2,1)S(1)}, bf16[64,2048]{1,0:T(8,128)(2,1)S(1)}, u32[]{:S(2)}, u32[]{:S(2)}) collective-permute-start(bf16[64,2048]{1,0:T(8,128)(2,1)S(1)} %pad_maximum_fusion.2), channel_id=1, source_target_pairs={{0,2},{1,3},{2,0},{3,1},{4,6},{5,7},{6,4},{7,5},{8,10},{9,11},{10,... | collective-permute-start | bytes 786440 | tf_op jit(solution)/shard_map/ppermute | solution.py:40
  104.4 7.3 %collective-permute-start.33 = (bf16[64,2048]{1,0:T(8,128)(2,1)S(1)}, bf16[64,2048]{1,0:T(8,128)(2,1)S(1)}, u32[]{:S(2)}, u32[]{:S(2)}) collective-permute-start(bf16[64,2048]{1,0:T(8,128)(2,1)S(1)} %pad_maximum_fusion.3), channel_id=1, source_target_pairs={{0,2},{1,3},{2,0},{3,1},{4,6},{5,7},{6,4},{7,5},{8,10},{9,11},{10,... | collective-permute-start | bytes 786440 | tf_op jit(solution)/shard_map/ppermute | solution.py:40
  110.1 2.4 %collective-permute-start.24 = (bf16[128,2048]{1,0:T(8,128)(2,1)}, bf16[128,2048]{1,0:T(8,128)(2,1)}, u32[]{:S(2)}, u32[]{:S(2)}) collective-permute-start(bf16[128,2048]{1,0:T(8,128)(2,1)} %get-tuple-element.50), channel_id=1, source_target_pairs={{0,1},{1,0},{2,3},{3,2},{4,5},{5,4},{6,7},{7,6},{8,9},{9,8},{10,11... | collective-permute-start | bytes 1572872 | tf_op jit(solution)/shard_map/ppermute | solution.py:40
  112.5 10.0 %collective-permute-start.34 = (bf16[128,2048]{1,0:T(8,128)(2,1)}, bf16[128,2048]{1,0:T(8,128)(2,1)}, u32[]{:S(2)}, u32[]{:S(2)}) collective-permute-start(bf16[128,2048]{1,0:T(8,128)(2,1)} %get-tuple-element.58), channel_id=1, source_target_pairs={{0,1},{1,0},{2,3},{3,2},{4,5},{5,4},{6,7},{7,6},{8,9},{9,8},{10,11... | collective-permute-start | bytes 1572872 | tf_op jit(solution)/shard_map/ppermute | solution.py:40
  121.0 1.0 copy-start.4
  122.1 8.3 %collective-permute-start.25 = (bf16[128,2048]{1,0:T(8,128)(2,1)}, bf16[128,2048]{1,0:T(8,128)(2,1)}, u32[]{:S(2)}, u32[]{:S(2)}) collective-permute-start(bf16[128,2048]{1,0:T(8,128)(2,1)} %get-tuple-element.18), channel_id=1, source_target_pairs={{0,1},{1,0},{2,3},{3,2},{4,5},{5,4},{6,7},{7,6},{8,9},{9,8},{10,11... | collective-permute-start | bytes 1572872 | tf_op jit(solution)/shard_map/ppermute | solution.py:40
  124.5 5.9 %copy-start.5 = (f32[128,2048]{1,0:T(8,128)S(1)}, f32[128,2048]{1,0:T(8,128)}, u32[]{:S(2)}) copy-start(f32[128,2048]{1,0:T(8,128)} %copy-done.4) | copy-start | bytes 3145732
  130.3 2.9 %collective-permute-start.35 = (bf16[128,2048]{1,0:T(8,128)(2,1)S(1)}, bf16[128,2048]{1,0:T(8,128)(2,1)S(1)}, u32[]{:S(2)}, u32[]{:S(2)}) collective-permute-start(bf16[128,2048]{1,0:T(8,128)(2,1)S(1)} %get-tuple-element.20), channel_id=1, source_target_pairs={{0,1},{1,0},{2,3},{3,2},{4,5},{5,4},{6,7},{7,6},{8,9},{9,8},{10,11... | collective-permute-start | bytes 1572872 | tf_op jit(solution)/shard_map/ppermute | solution.py:40
  131.6 9.2 %collective-permute-start.26 = (bf16[64,2048]{1,0:T(8,128)(2,1)S(1)}, bf16[64,2048]{1,0:T(8,128)(2,1)S(1)}, u32[]{:S(2)}, u32[]{:S(2)}) collective-permute-start(bf16[64,2048]{1,0:T(8,128)(2,1)S(1)} %slice.243), channel_id=1, source_target_pairs={{0,2},{1,3},{2,0},{3,1},{4,6},{5,7},{6,4},{7,5},{8,10},{9,11},{10,... | collective-permute-start | bytes 786440 | tf_op jit(solution)/shard_map/ppermute | solution.py:40
  133.3 12.7 %collective-permute-start.36 = (bf16[64,2048]{1,0:T(8,128)(2,1)S(1)}, bf16[64,2048]{1,0:T(8,128)(2,1)S(1)}, u32[]{:S(2)}, u32[]{:S(2)}) collective-permute-start(bf16[64,2048]{1,0:T(8,128)(2,1)S(1)} %slice.242), channel_id=1, source_target_pairs={{0,2},{1,3},{2,0},{3,1},{4,6},{5,7},{6,4},{7,5},{8,10},{9,11},{10,... | collective-permute-start | bytes 786440 | tf_op jit(solution)/shard_map/ppermute | solution.py:40
  140.9 8.2 %collective-permute-start.27 = (bf16[16,2048]{1,0:T(8,128)(2,1)S(1)}, bf16[16,2048]{1,0:T(8,128)(2,1)S(1)}, u32[]{:S(2)}, u32[]{:S(2)}) collective-permute-start(bf16[16,2048]{1,0:T(8,128)(2,1)S(1)} %get-tuple-element.47), channel_id=1, source_target_pairs={{0,4},{1,5},{2,6},{3,7},{4,0},{5,1},{6,2},{7,3},{8,12},{9,13},{10,... | collective-permute-start | bytes 196616 | tf_op jit(solution)/shard_map/ppermute | solution.py:40
  142.9 7.7 %collective-permute-start.28 = (bf16[16,2048]{1,0:T(8,128)(2,1)S(1)}, bf16[16,2048]{1,0:T(8,128)(2,1)S(1)}, u32[]{:S(2)}, u32[]{:S(2)}) collective-permute-start(bf16[16,2048]{1,0:T(8,128)(2,1)S(1)} %get-tuple-element.49), channel_id=1, source_target_pairs={{0,8},{1,9},{2,10},{3,11},{4,12},{5,13},{6,14},{7,15},{8,0},{9,1},... | collective-permute-start | bytes 196616 | tf_op jit(solution)/shard_map/ppermute | solution.py:40
  143.9 6.7 %collective-permute-start.29 = (bf16[16,2048]{1,0:T(8,128)(2,1)S(1)}, bf16[16,2048]{1,0:T(8,128)(2,1)S(1)}, u32[]{:S(2)}, u32[]{:S(2)}) collective-permute-start(bf16[16,2048]{1,0:T(8,128)(2,1)S(1)} %get-tuple-element.48), channel_id=1, source_target_pairs={{0,12},{1,13},{2,14},{3,15},{4,8},{5,9},{6,10},{7,11},{8,4},{9,5},... | collective-permute-start | bytes 196616 | tf_op jit(solution)/shard_map/ppermute | solution.py:40
  146.1 5.9 %collective-permute-start.37 = (bf16[16,2048]{1,0:T(8,128)(2,1)S(1)}, bf16[16,2048]{1,0:T(8,128)(2,1)S(1)}, u32[]{:S(2)}, u32[]{:S(2)}) collective-permute-start(bf16[16,2048]{1,0:T(8,128)(2,1)S(1)} %get-tuple-element.55), channel_id=1, source_target_pairs={{0,4},{1,5},{2,6},{3,7},{4,0},{5,1},{6,2},{7,3},{8,12},{9,13},{10,... | collective-permute-start | bytes 196616 | tf_op jit(solution)/shard_map/ppermute | solution.py:40
  148.2 7.9 %collective-permute-start.38 = (bf16[16,2048]{1,0:T(8,128)(2,1)S(1)}, bf16[16,2048]{1,0:T(8,128)(2,1)S(1)}, u32[]{:S(2)}, u32[]{:S(2)}) collective-permute-start(bf16[16,2048]{1,0:T(8,128)(2,1)S(1)} %get-tuple-element.57), channel_id=1, source_target_pairs={{0,8},{1,9},{2,10},{3,11},{4,12},{5,13},{6,14},{7,15},{8,0},{9,1},... | collective-permute-start | bytes 196616 | tf_op jit(solution)/shard_map/ppermute | solution.py:40
  149.1 6.9 %collective-permute-start.39 = (bf16[16,2048]{1,0:T(8,128)(2,1)S(1)}, bf16[16,2048]{1,0:T(8,128)(2,1)S(1)}, u32[]{:S(2)}, u32[]{:S(2)}) collective-permute-start(bf16[16,2048]{1,0:T(8,128)(2,1)S(1)} %get-tuple-element.56), channel_id=1, source_target_pairs={{0,12},{1,13},{2,14},{3,15},{4,8},{5,9},{6,10},{7,11},{8,4},{9,5},... | collective-permute-start | bytes 196616 | tf_op jit(solution)/shard_map/ppermute | solution.py:40
  (1 other events, 1.0 us)

commit v2 on v0

v2 whole, which is shorter than its diff:
```python
import functools

import jax
import jax.numpy as jnp
from jax import lax
from jax.experimental import pallas as pl
from jax.experimental.pallas import tpu as pltpu
from jax.sharding import PartitionSpec as P

eps = 1e-06
LANES = 128
MIB = 2**20
VMEM = pl.BlockSpec(memory_space=pltpu.VMEM)
SMEM = pl.BlockSpec(memory_space=pltpu.SMEM)
ANY = pl.BlockSpec(memory_space=pl.ANY)
bf16, f32 = jnp.bfloat16, jnp.float32


def from_behind(value, axis, steps):
    count = lax.axis_size(axis)
    initial, last = (max(0, -steps), min(count, count - steps))
    return lax.ppermute(value, axis, [(source, source + steps) for source in range(initial, last)])


def call(kernel, outs, specs, *operands, scratch=(), limit=8, flops=0):
    shapes = tuple(jax.ShapeDtypeStruct(shape, dtype) for shape, dtype in outs)
    moved = sum(x.size * x.dtype.itemsize for x in operands + shapes)
    return pl.pallas_call(
        kernel,
        out_shape=shapes,
        in_specs=specs,
        out_specs=(VMEM,) * len(outs),
        scratch_shapes=scratch,
        compiler_params=pltpu.CompilerParams(vmem_limit_bytes=limit * MIB),
        cost_estimate=pl.CostEstimate(flops=flops, bytes_accessed=moved, transcendentals=0),
    )(*operands)


def swap(value, stride, step, radix, back=False):
    count = lax.axis_size("expert")

    def partner(index):
        digit = index // stride % radix
        if radix & (radix - 1) == 0:
            other = digit ^ step
        else:
            other = (digit + (step if back else radix - step)) % radix
        return index + (other - digit) * stride

    return lax.ppermute(value, "expert", [(i, partner(i)) for i in range(count)])


def join_kernel(*refs):
    *parts, whole = refs
    rows = parts[0].shape[0]
    for k, part in enumerate(parts):
        whole[k * rows : (k + 1) * rows] = part[...]


def gather_rows(rows):
    far = lax.axis_size("expert") // 4
    tokens, width = rows.shape
    parts = [rows] + [swap(rows, 4, k, far) for k in range(1, far)]
    (near,) = call(join_kernel, [((far * tokens, width), rows.dtype)], [VMEM] * far, *parts)
    beside = swap(near, 2, 1, 2)
    return [near, beside, swap(near, 1, 1, 2), swap(beside, 1, 1, 2)]


def sum_kernel(mine, arrived, total):
    total[...] = (mine[...] + arrived[...].astype(f32)).astype(total.dtype)


def split_kernel(mine, near, beside, kept, *sent):
    rows = kept.shape[0]
    total = mine[...] + near[...].astype(f32) + beside[...].astype(f32)
    kept[...] = total[:rows]
    for k, piece in enumerate(sent, 1):
        piece[...] = total[k * rows : (k + 1) * rows].astype(piece.dtype)


def return_rows(mine_near, mine_beside, other_near, other_beside):
    far = lax.axis_size("expert") // 4
    shape = mine_near.shape
    tokens, width = shape[0] // far, shape[1]
    arrived_beside = swap(other_beside, 1, 1, 2, True)
    arrived_near = swap(other_near, 1, 1, 2, True)
    (leaving,) = call(sum_kernel, [(shape, bf16)], [VMEM] * 2, mine_beside, arrived_beside)
    beside = swap(leaving, 2, 1, 2, True)
    kept, *sent = call(
        split_kernel,
        [((tokens, width), f32)] + [((tokens, width), bf16)] * (far - 1),
        [VMEM] * 3,
        mine_near,
        arrived_near,
        beside,
    )
    return [kept] + [swap(piece, 4, k, far, True) for k, piece in enumerate(sent, 1)]


def normed_rows(widened, gain_row):
    scale_inv = lax.rsqrt(jnp.mean(widened * widened, axis=-1, keepdims=True) + eps)
    return (widened * scale_inv * gain_row).astype(bf16)


def open_kernel(batch_no, experts, current_ref, routes_ref, gain_ref, wide_ref):
    features = current_ref.shape[-1]
    rows = current_ref[...] if batch_no is None else current_ref[batch_no]
    wide_ref[:, :features] = normed_rows(rows.astype(f32), gain_ref[0:1])
    layers, batches, tokens, top = routes_ref.shape
    places = lax.broadcasted_iota(jnp.int32, (tokens, wide_ref.shape[1] - features), 1)
    chosen = jnp.zeros(places.shape, f32)
    for layer_no in range(layers):
        for batch in range(batches):
            named = routes_ref[layer_no, batch] + (layer_no * batches + batch) * experts
            for k in range(top):
                chosen = jnp.where(places == named[:, k : k + 1], 1.0, chosen)
    wide_ref[:, features:] = chosen.astype(bf16)


def norm_kernel(batch_no, layer_no, current_ref, gain_ref, normed_ref):
    normed_ref[...] = normed_rows(
        current_ref[batch_no].astype(f32), gain_ref[layer_no : layer_no + 1]
    )


def total_rows(current, kept, sent):
    total = kept[...]
    for piece in sent:
        total = total + piece[...].astype(f32)
    return (current.astype(f32) + total * 0.125).astype(bf16)


def close_kernel(batch_no, layer_no, current_ref, gain_ref, kept, *refs):
    *sent, out_ref, normed_ref = refs
    current = current_ref[...] if batch_no is None else current_ref[batch_no]
    out = total_rows(current, kept, sent)
    out_ref[...] = out
    normed_ref[...] = normed_rows(out.astype(f32), gain_ref[layer_no : layer_no + 1])


def end_kernel(earlier, current_ref, kept, *refs):
    sent, before, outs_ref = refs[: -earlier - 1], refs[-earlier - 1 : -1], refs[-1]
    layers, batches = outs_ref.shape[:2]
    for place, done in enumerate(before):
        outs_ref[place // batches, place % batches] = done[...]
    outs_ref[earlier // batches, earlier % batches] = total_rows(current_ref[...], kept, sent)


def load_kernel(layer_no, cuts, gate_up_hbm, down_hbm, gate_up_ref, down_ref, sems):
    copies = []
    for source, target in ((gate_up_hbm, gate_up_ref), (down_hbm, down_ref)):
        rows = target.shape[0] // cuts
        for cut in range(cuts):
            span = pl.ds(cut * rows, rows)
            copies.append(
                pltpu.make_async_copy(
                    source.at[layer_no, 0, span], target.at[span], sems.at[len(copies)]
                )
            )
    for copy in copies:
        copy.start()
    for copy in copies:
        copy.wait()


def load_weights(layer_no, w_gate_up, w_down):
    cuts = 4
    return call(
        functools.partial(load_kernel, layer_no, cuts),
        [(w_gate_up.shape[2:], bf16), (w_down.shape[2:], bf16)],
        [ANY] * 2,
        w_gate_up,
        w_down,
        scratch=[pltpu.SemaphoreType.DMA((2 * cuts,))],
        limit=12,
    )


def tile_of(extent, most):
    size = most
    while extent % size:
        size //= 2
    return size


def expert_kernel(first_column, wide, me_ref, *refs):
    if wide:
        parts, refs = refs[:4], refs[4:]
        gate_up_ref, down_ref, *outs, routed_ref, rows_ref, hidden_ref = refs
    else:
        parts, refs = refs[:4], refs[4:]
        routed_ref, gate_up_ref, down_ref, *outs, rows_ref, hidden_ref = refs
    hidden_size, features = down_ref.shape
    quarter = parts[0].shape[0]
    for k, part in enumerate(parts):
        span = slice(k * quarter, (k + 1) * quarter)
        rows_ref[span] = part[:, :features]
        if wide:
            routed_ref[span] = part[:, features:]
    places = lax.broadcasted_iota(jnp.int32, routed_ref.shape, 1)
    chosen = jnp.where(places == me_ref[0] + first_column, routed_ref[...].astype(f32), 0.0)
    share = jnp.sum(chosen, axis=1, keepdims=True)
    rows = rows_ref[...]
    size = tile_of(hidden_size, 256)
    for low in range(0, hidden_size, size):
        span, beside = slice(low, low + size), slice(hidden_size + low, hidden_size + low + size)
        gate = jnp.dot(rows, gate_up_ref[:, span], preferred_element_type=f32)
        up = jnp.dot(rows, gate_up_ref[:, beside], preferred_element_type=f32)
        hidden_ref[:, span] = (gate / (1.0 + jnp.exp(-gate)) * up).astype(bf16)
    hidden = hidden_ref[...]
    size = tile_of(features, 512)
    for low in range(0, features, size):
        span = slice(low, low + size)
        done = jnp.dot(hidden, down_ref[:, span], preferred_element_type=f32) * share
        for k, out in enumerate(outs):
            out[:, span] = done[k * quarter : (k + 1) * quarter].astype(out.dtype)


def run_expert(parts, routed, me, first_column, weights):
    gate_up, down_proj = weights
    hidden_size, features = down_proj.shape
    quarter, width = parts[0].shape
    count = 4 * quarter
    wide = routed is None
    outs = [((quarter, features), f32)] * 2 + [((quarter, features), bf16)] * 2
    if wide:
        outs = outs + [((count, width - features), bf16)]
    found = call(
        functools.partial(expert_kernel, first_column, wide),
        outs,
        [SMEM] + [VMEM] * (6 if wide else 7),
        me,
        *parts,
        *([] if wide else [routed]),
        gate_up,
        down_proj,
        scratch=[pltpu.VMEM((count, features), bf16), pltpu.VMEM((count, hidden_size), bf16)],
        limit=24,
        flops=6 * count * features * hidden_size,
    )
    return found[:4], found[4] if wide else routed


def open_rows(batch_no, current, routes, gain, experts):
    tokens, features = current.shape[-2:]
    columns = routes.shape[0] * routes.shape[1] * experts
    width = features + columns + -columns % LANES
    (wide,) = call(
        functools.partial(open_kernel, batch_no, experts),
        [((tokens, width), bf16)],
        [VMEM] * 3,
        current,
        routes,
        gain,
    )
    return wide


def close_rows(batch_no, layer_no, current, gain, returned):
    shape = current.shape[-2:]
    return call(
        functools.partial(close_kernel, batch_no, layer_no),
        [(shape, bf16)] * 2,
        [VMEM] * (2 + len(returned)),
        current,
        gain,
        *returned,
    )


def on_device(inputs, routes, norm_gain, w_gate_up, w_down):
    experts = lax.axis_size("expert")
    sections = lax.axis_size("section")
    me = lax.axis_index("expert").astype(jnp.int32).reshape(1)
    batches, tokens, features = inputs.shape
    layers = routes.shape[0]
    weights = [load_weights(layer_no, w_gate_up, w_down) for layer_no in range(layers)]
    if sections == 1:
        outs, routed = [], None
        currents = [inputs] * batches
        normed = [open_rows(0, inputs, routes, norm_gain, experts)]
        for batch_no in range(1, batches):
            normed += call(
                functools.partial(norm_kernel, batch_no, 0),
                [((tokens, features), bf16)],
                [VMEM] * 2,
                inputs,
                norm_gain,
            )
        for layer_no in range(layers):
            for batch_no in range(batches):
                column = (layer_no * batches + batch_no) * experts
                parts = gather_rows(normed[batch_no])
                found, routed = run_expert(parts, routed, me, column, weights[layer_no])
                returned = return_rows(*found)
                current = currents[batch_no]
                if len(outs) == layers * batches - 1:
                    (whole,) = call(
                        functools.partial(end_kernel, len(outs)),
                        [((layers, batches, tokens, features), bf16)],
                        [VMEM] * (1 + len(returned) + len(outs)),
                        current,
                        *returned,
                        *outs,
                    )
                    return whole
                which = batch_no if layer_no == 0 else None
                following = min(layer_no + 1, layers - 1)
                done, after = close_rows(which, following, current, norm_gain, returned)
                outs.append(done)
                currents[batch_no], normed[batch_no] = done, after
    segment_no = lax.axis_index("section")
    handed = jnp.zeros((tokens, features), bf16)
    finished = []
    for turn_no in range(batches + 1):
        if turn_no < batches:
            fresh_rows = inputs[turn_no]
        else:
            fresh_rows = jnp.zeros((tokens, features), bf16)
        current = jnp.where(segment_no == 0, fresh_rows, handed)
        batch_pick = jnp.clip(turn_no - segment_no, 0, batches - 1)
        parts = gather_rows(open_rows(None, current, routes, norm_gain, experts))
        found, _ = run_expert(parts, None, me + batch_pick * experts, 0, weights[0])
        result, _ = close_rows(None, 0, current, norm_gain, return_rows(*found))
        finished.append(result)
        if turn_no < batches:
            handed = from_behind(result, "section", 1)
    first_segment = jnp.stack(finished[:batches])
    second_segment = jnp.stack(finished[1:])
    return jnp.where(segment_no == 0, first_segment, second_segment)[None]


def solution(mesh):
    placed = (
        P(None, ("groups", "expert"), None),
        P("section", None, ("groups", "expert"), None),
        P("section", None),
        P("section", "expert", None, None),
        P("section", "expert", None, None),
    )
    return jax.shard_map(
        on_device,
        mesh=mesh,
        in_specs=placed,
        out_specs=P("section", None, ("groups", "expert"), None),
        check_vma=False,
    )
```

time: 249 us -> 134 us (0.54)
  waiting for transfers between devices: 143 us -> 55.6 us
  matrix products: 42.2 us -> 0 us
  Pallas kernels: 0 us -> 17.2 us
  local copies, waits for them, and re-layouts: 1.88 us -> 11.4 us
  starting transfers between devices: 55.4 us -> 49 us
  other arithmetic: 4.27 us -> 0.01 us
    all_to_all x8 -> x0, waiting for transfers between devices: 143 us -> none  [the longest x4 72 us: moe_layer(): lax.all_to_all(results, 'expert', split_axis=0, concat_axis=0, tiled=True)]
    ppermute x0 -> x48, waiting for transfers between devices: none -> 55.6 us  [swap(): lax.ppermute(value, 'expert', [(i, partner(i)) for i in range(count)])]
    all_to_all x8 -> x0, starting transfers between devices: 55.4 us -> none  [the longest x4 28 us: moe_layer(): lax.all_to_all(outgoing, 'expert', split_axis=0, concat_axis=0, tiled=True)]
    ppermute x0 -> x48, starting transfers between devices: none -> 49 us  [swap(): lax.ppermute(value, 'expert', [(i, partner(i)) for i in range(count)])]
    dot_general x16 -> x0, matrix products: 42.2 us -> none  [the longest x4 18.3 us: expert_rows(): joined = jnp.dot(rows, gate_up, preferred_element_type=jnp.float32)]
    pallas_call x0 -> x24, Pallas kernels: none -> 17.2 us  [call(): pl.pallas_call(kernel, out_shape=shapes, in_specs=specs, out_specs=(VMEM,...]
    unnamed x2 -> x27, local copies, waits for them, and re-layouts: 0.01 us -> 11.4 us
    reduce_sum x12 -> x0, other arithmetic: 3.34 us -> none  [the longest x3 1.51 us: moe_layer(): jnp.sum(onehot * (expert_ids[None, None, :] * capacity + before[:, None,...]
  transfers between devices with their start and end apart: 8 -> 48, of which waited for: 8 -> 19; matrix products, arithmetic and copies ran while one was open for 17% -> 0% of each run, Pallas kernels for 0% -> 12%
where the time goes in v2:
time: 134 us
  waiting for transfers between devices  55.6 us (41%)
  starting transfers between devices  49 us (37%)
  Pallas kernels  17.2 us (13%)
  local copies, waits for them, and re-layouts  11.4 us (9%)
    ppermute x48, waiting for transfers between devices, swap(): lax.ppermute(value, 'expert', [(i, partner(i)) for i in range(count)])  55.6 us
    ppermute x48, starting transfers between devices, swap(): lax.ppermute(value, 'expert', [(i, partner(i)) for i in range(count)])  49 us
    pallas_call x24, Pallas kernels, call(): pl.pallas_call(kernel, out_shape=shapes, in_specs=specs, out_specs=(VMEM,...  17.2 us
    unnamed x27, local copies, waits for them, and re-layouts  11.4 us
  transfers between devices with their start and end apart: 48, of which 19 were waited for; matrix products, arithmetic and copies ran while one was open for 0% of the time, Pallas kernels for 12%

profile of v2, /device:TPU:0, one launch (start us, length us, event | category | flops | bytes accessed | tf_op | source)
XLA Modules:
  0.0 133.6 jit_solution(13197216589443460561)
XLA Ops:
  0.8 0.9 copy-done.2
  2.6 3.1 %collective-permute-start.6 = (bf16[16,2176]{1,0:T(8,128)(2,1)S(1)}, bf16[16,2176]{1,0:T(8,128)(2,1)S(1)}, u32[]{:S(2)}, u32[]{:S(2)}) collective-permute-start(bf16[16,2176]{1,0:T(8,128)(2,1)S(1)} %shard_map.57.refs_0_), channel_id=1, source_target_pairs={{0,4},{1,5},{2,6},{3,7},{4,0},{5,1},{6,2},{7,3},{8,12},{9,13},{10,... | collective-permute-start | bytes 208904 | tf_op jit(solution)/shard_map/ppermute | solution.py:50
  5.7 2.6 %collective-permute-start.7 = (bf16[16,2176]{1,0:T(8,128)(2,1)S(1)}, bf16[16,2176]{1,0:T(8,128)(2,1)S(1)}, u32[]{:S(2)}, u32[]{:S(2)}) collective-permute-start(bf16[16,2176]{1,0:T(8,128)(2,1)S(1)} %shard_map.57.refs_0_), channel_id=1, source_target_pairs={{0,8},{1,9},{2,10},{3,11},{4,12},{5,13},{6,14},{7,15},{8,0},{9,1},... | collective-permute-start | bytes 208904 | tf_op jit(solution)/shard_map/ppermute | solution.py:50
  8.3 4.9 %collective-permute-done.7.refs_2_ = bf16[16,2176]{1,0:T(8,128)(2,1)S(1)} collective-permute-done((bf16[16,2176]{1,0:T(8,128)(2,1)S(1)}, bf16[16,2176]{1,0:T(8,128)(2,1)S(1)}, u32[]{:S(2)}, u32[]{:S(2)}) %collective-permute-start.7) | collective-permute-done | bytes 69664 | tf_op jit(solution)/shard_map/ppermute | solution.py:50
  13.2 1.3 collective-permute-done.8.refs_3_
  14.5 1.6 %collective-permute-start.9 = (bf16[64,2176]{1,0:T(8,128)(2,1)S(1)}, bf16[64,2176]{1,0:T(8,128)(2,1)S(1)}, u32[]{:S(2)}, u32[]{:S(2)}) collective-permute-start(bf16[64,2176]{1,0:T(8,128)(2,1)S(1)} %shard_map.58.refs_0_), channel_id=1, source_target_pairs={{0,2},{1,3},{2,0},{3,1},{4,6},{5,7},{6,4},{7,5},{8,10},{9,11},{10,... | collective-permute-start | bytes 835592 | tf_op jit(solution)/shard_map/ppermute | solution.py:50
  16.1 0.9 copy-done.3
  18.7 1.7 %collective-permute-start.1 = (bf16[16,2048]{1,0:T(8,128)(2,1)S(1)}, bf16[16,2048]{1,0:T(8,128)(2,1)S(1)}, u32[]{:S(2)}, u32[]{:S(2)}) collective-permute-start(bf16[16,2048]{1,0:T(8,128)(2,1)S(1)} %shard_map.55.refs_0_), channel_id=1, source_target_pairs={{0,8},{1,9},{2,10},{3,11},{4,12},{5,13},{6,14},{7,15},{8,0},{9,1},... | collective-permute-start | bytes 196616 | tf_op jit(solution)/shard_map/ppermute | solution.py:50
  20.4 1.9 %collective-permute-start.2 = (bf16[16,2048]{1,0:T(8,128)(2,1)S(1)}, bf16[16,2048]{1,0:T(8,128)(2,1)S(1)}, u32[]{:S(2)}, u32[]{:S(2)}) collective-permute-start(bf16[16,2048]{1,0:T(8,128)(2,1)S(1)} %shard_map.55.refs_0_), channel_id=1, source_target_pairs={{0,12},{1,13},{2,14},{3,15},{4,8},{5,9},{6,10},{7,11},{8,4},{9,5},... | collective-permute-start | bytes 196616 | tf_op jit(solution)/shard_map/ppermute | solution.py:50
  22.3 1.6 %collective-permute-done.1.refs_2_ = bf16[16,2048]{1,0:T(8,128)(2,1)S(1)} collective-permute-done((bf16[16,2048]{1,0:T(8,128)(2,1)S(1)}, bf16[16,2048]{1,0:T(8,128)(2,1)S(1)}, u32[]{:S(2)}, u32[]{:S(2)}) %collective-permute-start.1) | collective-permute-done | bytes 65568 | tf_op jit(solution)/shard_map/ppermute | solution.py:50
  23.9 2.5 %collective-permute-done.2.refs_3_ = bf16[16,2048]{1,0:T(8,128)(2,1)S(1)} collective-permute-done((bf16[16,2048]{1,0:T(8,128)(2,1)S(1)}, bf16[16,2048]{1,0:T(8,128)(2,1)S(1)}, u32[]{:S(2)}, u32[]{:S(2)}) %collective-permute-start.2) | collective-permute-done | bytes 65568 | tf_op jit(solution)/shard_map/ppermute | solution.py:50
  27.6 5.5 %collective-permute-done.3.refs_1_ = bf16[64,2048]{1,0:T(8,128)(2,1)} collective-permute-done((bf16[64,2048]{1,0:T(8,128)(2,1)S(1)}, bf16[64,2048]{1,0:T(8,128)(2,1)}, u32[]{:S(2)}, u32[]{:S(2)}) %collective-permute-start.3) | collective-permute-done | bytes 262176 | tf_op jit(solution)/shard_map/ppermute | solution.py:50
  33.1 4.6 %copy-done = bf16[2,1,2048,1536]{3,2,1,0:T(8,128)(2,1)S(1)} copy-done((bf16[2,1,2048,1536]{3,2,1,0:T(8,128)(2,1)S(1)}, bf16[2,1,2048,1536]{3,2,1,0:T(8,128)(2,1)}, u32[]{:S(2)}) %copy-start) | copy-done | bytes 12582936
  37.6 2.8 %copy-done.1 = bf16[2,1,768,2048]{3,2,1,0:T(8,128)(2,1)S(1)} copy-done((bf16[2,1,768,2048]{3,2,1,0:T(8,128)(2,1)S(1)}, bf16[2,1,768,2048]{3,2,1,0:T(8,128)(2,1)}, u32[]{:S(2)}) %copy-start.1) | copy-done | bytes 6291480
  41.2 3.8 %shard_map.60 = (f32[64,2048]{1,0:T(8,128)S(1)}, f32[64,2048]{1,0:T(8,128)S(1)}, bf16[64,2048]{1,0:T(8,128)(2,1)S(1)}, bf16[64,2048]{1,0:T(8,128)(2,1)S(1)}, bf16[256,128]{1,0:T(8,128)(2,1)S(1)}) custom-call(s32[1]{0:T(128)} %bitcast.me_ref, bf16[64,2176]{1,0:T(8,128)(2,1)S(1)} %shard_map.58.refs_0_, bf16[64,2176]{1,0:T(8,128)(2,1)S(1)} %collective-permute-done.9.refs_1_, ...), custom_call_target="tpu_custom_call" | custom-call | flops 2415919104 | bytes 12189700 | tf_op jit(solution)/shard_map/pallas_call | solution.py:28
  45.6 3.9 %shard_map.61 = (f32[64,2048]{1,0:T(8,128)S(1)}, f32[64,2048]{1,0:T(8,128)S(1)}, bf16[64,2048]{1,0:T(8,128)(2,1)S(1)}, bf16[64,2048]{1,0:T(8,128)(2,1)S(1)}) custom-call(s32[1]{0:T(128)} %bitcast.me_ref, bf16[64,2048]{1,0:T(8,128)(2,1)S(1)} %shard_map.56.refs_0_, bf16[64,2048]{1,0:T(8,128)(2,1)} %collective-permute-done.3.refs_1_, ...), custom_call_target="tpu_custom_call" | custom-call | flops 2415919104 | bytes 12124164 | tf_op jit(solution)/shard_map/pallas_call | solution.py:28
  51.2 1.2 collective-permute-start.14
  52.4 7.0 %collective-permute-done.32.beside = bf16[64,2048]{1,0:T(8,128)(2,1)S(1)} collective-permute-done((bf16[64,2048]{1,0:T(8,128)(2,1)S(1)}, bf16[64,2048]{1,0:T(8,128)(2,1)S(1)}, u32[]{:S(2)}, u32[]{:S(2)}) %collective-permute-start.32) | collective-permute-done | bytes 262176 | tf_op jit(solution)/shard_map/ppermute | solution.py:50
  59.6 2.5 %collective-permute-start.34 = (bf16[16,2048]{1,0:T(8,128)(2,1)S(1)}, bf16[16,2048]{1,0:T(8,128)(2,1)S(1)}, u32[]{:S(2)}, u32[]{:S(2)}) collective-permute-start(bf16[16,2048]{1,0:T(8,128)(2,1)S(1)} %get-tuple-element.76), channel_id=1, source_target_pairs={{0,8},{1,9},{2,10},{3,11},{4,12},{5,13},{6,14},{7,15},{8,0},{9,1},... | collective-permute-start | bytes 196616 | tf_op jit(solution)/shard_map/ppermute | solution.py:50
  62.1 1.9 %collective-permute-start.35 = (bf16[16,2048]{1,0:T(8,128)(2,1)S(1)}, bf16[16,2048]{1,0:T(8,128)(2,1)S(1)}, u32[]{:S(2)}, u32[]{:S(2)}) collective-permute-start(bf16[16,2048]{1,0:T(8,128)(2,1)S(1)} %get-tuple-element.77), channel_id=1, source_target_pairs={{0,12},{1,13},{2,14},{3,15},{4,8},{5,9},{6,10},{7,11},{8,4},{9,5},... | collective-permute-start | bytes 196616 | tf_op jit(solution)/shard_map/ppermute | solution.py:50
  63.9 2.3 %collective-permute-done.34.refs_1_ = bf16[16,2048]{1,0:T(8,128)(2,1)S(1)} collective-permute-done((bf16[16,2048]{1,0:T(8,128)(2,1)S(1)}, bf16[16,2048]{1,0:T(8,128)(2,1)S(1)}, u32[]{:S(2)}, u32[]{:S(2)}) %collective-permute-start.34) | collective-permute-done | bytes 65568 | tf_op jit(solution)/shard_map/ppermute | solution.py:50
  66.2 2.3 %collective-permute-done.35.refs_2_ = bf16[16,2048]{1,0:T(8,128)(2,1)S(1)} collective-permute-done((bf16[16,2048]{1,0:T(8,128)(2,1)S(1)}, bf16[16,2048]{1,0:T(8,128)(2,1)S(1)}, u32[]{:S(2)}, u32[]{:S(2)}) %collective-permute-start.35) | collective-permute-done | bytes 65568 | tf_op jit(solution)/shard_map/ppermute | solution.py:50
  68.7 2.3 %collective-permute-start.37 = (bf16[16,2048]{1,0:T(8,128)(2,1)S(1)}, bf16[16,2048]{1,0:T(8,128)(2,1)S(1)}, u32[]{:S(2)}, u32[]{:S(2)}) collective-permute-start(bf16[16,2048]{1,0:T(8,128)(2,1)S(1)} %get-tuple-element.79.refs_0_), channel_id=1, source_target_pairs={{0,8},{1,9},{2,10},{3,11},{4,12},{5,13},{6,14},{7,15},{8,0},{9,1},... | collective-permute-start | bytes 196616 | tf_op jit(solution)/shard_map/ppermute | solution.py:50
  71.1 2.0 %collective-permute-start.38 = (bf16[16,2048]{1,0:T(8,128)(2,1)S(1)}, bf16[16,2048]{1,0:T(8,128)(2,1)S(1)}, u32[]{:S(2)}, u32[]{:S(2)}) collective-permute-start(bf16[16,2048]{1,0:T(8,128)(2,1)S(1)} %get-tuple-element.79.refs_0_), channel_id=1, source_target_pairs={{0,12},{1,13},{2,14},{3,15},{4,8},{5,9},{6,10},{7,11},{8,4},{9,5},... | collective-permute-start | bytes 196616 | tf_op jit(solution)/shard_map/ppermute | solution.py:50
  73.1 0.9 collective-permute-done.37.refs_2_
  74.0 3.3 %collective-permute-done.38.refs_3_ = bf16[16,2048]{1,0:T(8,128)(2,1)S(1)} collective-permute-done((bf16[16,2048]{1,0:T(8,128)(2,1)S(1)}, bf16[16,2048]{1,0:T(8,128)(2,1)S(1)}, u32[]{:S(2)}, u32[]{:S(2)}) %collective-permute-start.38) | collective-permute-done | bytes 65568 | tf_op jit(solution)/shard_map/ppermute | solution.py:50
  77.3 1.0 collective-permute-start.39
  78.5 2.5 %collective-permute-start.16 = (bf16[16,2048]{1,0:T(8,128)(2,1)S(1)}, bf16[16,2048]{1,0:T(8,128)(2,1)S(1)}, u32[]{:S(2)}, u32[]{:S(2)}) collective-permute-start(bf16[16,2048]{1,0:T(8,128)(2,1)S(1)} %get-tuple-element.56), channel_id=1, source_target_pairs={{0,8},{1,9},{2,10},{3,11},{4,12},{5,13},{6,14},{7,15},{8,0},{9,1},... | collective-permute-start | bytes 196616 | tf_op jit(solution)/shard_map/ppermute | solution.py:50
  81.0 1.9 %collective-permute-start.17 = (bf16[16,2048]{1,0:T(8,128)(2,1)S(1)}, bf16[16,2048]{1,0:T(8,128)(2,1)S(1)}, u32[]{:S(2)}, u32[]{:S(2)}) collective-permute-start(bf16[16,2048]{1,0:T(8,128)(2,1)S(1)} %get-tuple-element.57), channel_id=1, source_target_pairs={{0,12},{1,13},{2,14},{3,15},{4,8},{5,9},{6,10},{7,11},{8,4},{9,5},... | collective-permute-start | bytes 196616 | tf_op jit(solution)/shard_map/ppermute | solution.py:50
  82.9 1.6 %collective-permute-done.15.refs_0_ = bf16[16,2048]{1,0:T(8,128)(2,1)S(1)} collective-permute-done((bf16[16,2048]{1,0:T(8,128)(2,1)S(1)}, bf16[16,2048]{1,0:T(8,128)(2,1)S(1)}, u32[]{:S(2)}, u32[]{:S(2)}) %collective-permute-start.15) | collective-permute-done | bytes 65568 | tf_op jit(solution)/shard_map/ppermute | solution.py:50
  84.4 2.8 %collective-permute-done.17.refs_2_ = bf16[16,2048]{1,0:T(8,128)(2,1)S(1)} collective-permute-done((bf16[16,2048]{1,0:T(8,128)(2,1)S(1)}, bf16[16,2048]{1,0:T(8,128)(2,1)S(1)}, u32[]{:S(2)}, u32[]{:S(2)}) %collective-permute-start.17) | collective-permute-done | bytes 65568 | tf_op jit(solution)/shard_map/ppermute | solution.py:50
  87.4 1.6 %collective-permute-start.18 = (bf16[16,2048]{1,0:T(8,128)(2,1)S(1)}, bf16[16,2048]{1,0:T(8,128)(2,1)S(1)}, u32[]{:S(2)}, u32[]{:S(2)}) collective-permute-start(bf16[16,2048]{1,0:T(8,128)(2,1)S(1)} %get-tuple-element.59.refs_0_), channel_id=1, source_target_pairs={{0,4},{1,5},{2,6},{3,7},{4,0},{5,1},{6,2},{7,3},{8,12},{9,13},{10,... | collective-permute-start | bytes 196616 | tf_op jit(solution)/shard_map/ppermute | solution.py:50
  89.0 0.9 collective-permute-start.19
  90.0 1.9 %collective-permute-start.20 = (bf16[16,2048]{1,0:T(8,128)(2,1)S(1)}, bf16[16,2048]{1,0:T(8,128)(2,1)S(1)}, u32[]{:S(2)}, u32[]{:S(2)}) collective-permute-start(bf16[16,2048]{1,0:T(8,128)(2,1)S(1)} %get-tuple-element.59.refs_0_), channel_id=1, source_target_pairs={{0,12},{1,13},{2,14},{3,15},{4,8},{5,9},{6,10},{7,11},{8,4},{9,5},... | collective-permute-start | bytes 196616 | tf_op jit(solution)/shard_map/ppermute | solution.py:50
  91.9 3.0 %collective-permute-done.19.refs_2_ = bf16[16,2048]{1,0:T(8,128)(2,1)S(1)} collective-permute-done((bf16[16,2048]{1,0:T(8,128)(2,1)S(1)}, bf16[16,2048]{1,0:T(8,128)(2,1)S(1)}, u32[]{:S(2)}, u32[]{:S(2)}) %collective-permute-start.19) | collective-permute-done | bytes 65568 | tf_op jit(solution)/shard_map/ppermute | solution.py:50
  94.9 1.2 collective-permute-done.20.refs_3_
  96.2 1.5 %collective-permute-start.21 = (bf16[64,2048]{1,0:T(8,128)(2,1)S(1)}, bf16[64,2048]{1,0:T(8,128)(2,1)S(1)}, u32[]{:S(2)}, u32[]{:S(2)}) collective-permute-start(bf16[64,2048]{1,0:T(8,128)(2,1)S(1)} %shard_map.65.refs_0_), channel_id=1, source_target_pairs={{0,2},{1,3},{2,0},{3,1},{4,6},{5,7},{6,4},{7,5},{8,10},{9,11},{10,... | collective-permute-start | bytes 786440 | tf_op jit(solution)/shard_map/ppermute | solution.py:50
  98.2 4.4 %collective-permute-done.21.refs_1_ = bf16[64,2048]{1,0:T(8,128)(2,1)S(1)} collective-permute-done((bf16[64,2048]{1,0:T(8,128)(2,1)S(1)}, bf16[64,2048]{1,0:T(8,128)(2,1)S(1)}, u32[]{:S(2)}, u32[]{:S(2)}) %collective-permute-start.21) | collective-permute-done | bytes 262176 | tf_op jit(solution)/shard_map/ppermute | solution.py:50
  103.4 2.7 %shard_map.74 = (f32[64,2048]{1,0:T(8,128)S(1)}, f32[64,2048]{1,0:T(8,128)S(1)}, bf16[64,2048]{1,0:T(8,128)(2,1)S(1)}, bf16[64,2048]{1,0:T(8,128)(2,1)S(1)}) custom-call(s32[1]{0:T(128)} %bitcast.me_ref, bf16[64,2048]{1,0:T(8,128)(2,1)S(1)} %shard_map.73.refs_0_, bf16[64,2048]{1,0:T(8,128)(2,1)S(1)} %collective-permute-done.39.refs_1_, ...), custom_call_target="tpu_custom_call" | custom-call | flops 2415919104 | bytes 12124164 | tf_op jit(solution)/shard_map/pallas_call | solution.py:28
  106.7 2.7 %shard_map.67 = (f32[64,2048]{1,0:T(8,128)S(1)}, f32[64,2048]{1,0:T(8,128)S(1)}, bf16[64,2048]{1,0:T(8,128)(2,1)S(1)}, bf16[64,2048]{1,0:T(8,128)(2,1)S(1)}) custom-call(s32[1]{0:T(128)} %bitcast.me_ref, bf16[64,2048]{1,0:T(8,128)(2,1)S(1)} %shard_map.65.refs_0_, bf16[64,2048]{1,0:T(8,128)(2,1)S(1)} %collective-permute-done.21.refs_1_, ...), custom_call_target="tpu_custom_call" | custom-call | flops 2415919104 | bytes 12124164 | tf_op jit(solution)/shard_map/pallas_call | solution.py:28
  110.0 1.5 %collective-permute-start.44 = (bf16[64,2048]{1,0:T(8,128)(2,1)S(1)}, bf16[64,2048]{1,0:T(8,128)(2,1)S(1)}, u32[]{:S(2)}, u32[]{:S(2)}) collective-permute-start(bf16[64,2048]{1,0:T(8,128)(2,1)S(1)} %shard_map.75), channel_id=1, source_target_pairs={{0,2},{1,3},{2,0},{3,1},{4,6},{5,7},{6,4},{7,5},{8,10},{9,11},{10,... | collective-permute-start | bytes 786440 | tf_op jit(solution)/shard_map/ppermute | solution.py:50
  111.5 1.0 collective-permute-start.26
  112.5 6.7 %collective-permute-done.44.beside = bf16[64,2048]{1,0:T(8,128)(2,1)S(1)} collective-permute-done((bf16[64,2048]{1,0:T(8,128)(2,1)S(1)}, bf16[64,2048]{1,0:T(8,128)(2,1)S(1)}, u32[]{:S(2)}, u32[]{:S(2)}) %collective-permute-start.44) | collective-permute-done | bytes 262176 | tf_op jit(solution)/shard_map/ppermute | solution.py:50
  120.1 1.7 %collective-permute-start.46 = (bf16[16,2048]{1,0:T(8,128)(2,1)S(1)}, bf16[16,2048]{1,0:T(8,128)(2,1)S(1)}, u32[]{:S(2)}, u32[]{:S(2)}) collective-permute-start(bf16[16,2048]{1,0:T(8,128)(2,1)S(1)} %get-tuple-element.86), channel_id=1, source_target_pairs={{0,8},{1,9},{2,10},{3,11},{4,12},{5,13},{6,14},{7,15},{8,0},{9,1},... | collective-permute-start | bytes 196616 | tf_op jit(solution)/shard_map/ppermute | solution.py:50
  121.8 2.0 %collective-permute-start.47 = (bf16[16,2048]{1,0:T(8,128)(2,1)S(1)}, bf16[16,2048]{1,0:T(8,128)(2,1)S(1)}, u32[]{:S(2)}, u32[]{:S(2)}) collective-permute-start(bf16[16,2048]{1,0:T(8,128)(2,1)S(1)} %get-tuple-element.87), channel_id=1, source_target_pairs={{0,12},{1,13},{2,14},{3,15},{4,8},{5,9},{6,10},{7,11},{8,4},{9,5},... | collective-permute-start | bytes 196616 | tf_op jit(solution)/shard_map/ppermute | solution.py:50
  124.8 1.7 %collective-permute-start.28 = (bf16[16,2048]{1,0:T(8,128)(2,1)S(1)}, bf16[16,2048]{1,0:T(8,128)(2,1)S(1)}, u32[]{:S(2)}, u32[]{:S(2)}) collective-permute-start(bf16[16,2048]{1,0:T(8,128)(2,1)S(1)} %get-tuple-element.68), channel_id=1, source_target_pairs={{0,8},{1,9},{2,10},{3,11},{4,12},{5,13},{6,14},{7,15},{8,0},{9,1},... | collective-permute-start | bytes 196616 | tf_op jit(solution)/shard_map/ppermute | solution.py:50
  126.5 2.0 %collective-permute-start.29 = (bf16[16,2048]{1,0:T(8,128)(2,1)S(1)}, bf16[16,2048]{1,0:T(8,128)(2,1)S(1)}, u32[]{:S(2)}, u32[]{:S(2)}) collective-permute-start(bf16[16,2048]{1,0:T(8,128)(2,1)S(1)} %get-tuple-element.69), channel_id=1, source_target_pairs={{0,12},{1,13},{2,14},{3,15},{4,8},{5,9},{6,10},{7,11},{8,4},{9,5},... | collective-permute-start | bytes 196616 | tf_op jit(solution)/shard_map/ppermute | solution.py:50
  129.3 3.5 %collective-permute-done.28.refs_1_ = bf16[16,2048]{1,0:T(8,128)(2,1)S(1)} collective-permute-done((bf16[16,2048]{1,0:T(8,128)(2,1)S(1)}, bf16[16,2048]{1,0:T(8,128)(2,1)S(1)}, u32[]{:S(2)}, u32[]{:S(2)}) %collective-permute-start.28) | collective-permute-done | bytes 65568 | tf_op jit(solution)/shard_map/ppermute | solution.py:50
  (101 shorter events, 14.2 us)
Async XLA Ops:
  2.6 5.7 %collective-permute-start.6 = (bf16[16,2176]{1,0:T(8,128)(2,1)S(1)}, bf16[16,2176]{1,0:T(8,128)(2,1)S(1)}, u32[]{:S(2)}, u32[]{:S(2)}) collective-permute-start(bf16[16,2176]{1,0:T(8,128)(2,1)S(1)} %shard_map.57.refs_0_), channel_id=1, source_target_pairs={{0,4},{1,5},{2,6},{3,7},{4,0},{5,1},{6,2},{7,3},{8,12},{9,13},{10,... | collective-permute-start | bytes 208904 | tf_op jit(solution)/shard_map/ppermute | solution.py:50
  5.7 7.5 %collective-permute-start.7 = (bf16[16,2176]{1,0:T(8,128)(2,1)S(1)}, bf16[16,2176]{1,0:T(8,128)(2,1)S(1)}, u32[]{:S(2)}, u32[]{:S(2)}) collective-permute-start(bf16[16,2176]{1,0:T(8,128)(2,1)S(1)} %shard_map.57.refs_0_), channel_id=1, source_target_pairs={{0,8},{1,9},{2,10},{3,11},{4,12},{5,13},{6,14},{7,15},{8,0},{9,1},... | collective-permute-start | bytes 208904 | tf_op jit(solution)/shard_map/ppermute | solution.py:50
  8.3 6.2 %collective-permute-start.8 = (bf16[16,2176]{1,0:T(8,128)(2,1)S(1)}, bf16[16,2176]{1,0:T(8,128)(2,1)S(1)}, u32[]{:S(2)}, u32[]{:S(2)}) collective-permute-start(bf16[16,2176]{1,0:T(8,128)(2,1)S(1)} %shard_map.57.refs_0_), channel_id=1, source_target_pairs={{0,12},{1,13},{2,14},{3,15},{4,8},{5,9},{6,10},{7,11},{8,4},{9,5},... | collective-permute-start | bytes 208904 | tf_op jit(solution)/shard_map/ppermute | solution.py:50
  14.5 12.6 %collective-permute-start.9 = (bf16[64,2176]{1,0:T(8,128)(2,1)S(1)}, bf16[64,2176]{1,0:T(8,128)(2,1)S(1)}, u32[]{:S(2)}, u32[]{:S(2)}) collective-permute-start(bf16[64,2176]{1,0:T(8,128)(2,1)S(1)} %shard_map.58.refs_0_), channel_id=1, source_target_pairs={{0,2},{1,3},{2,0},{3,1},{4,6},{5,7},{6,4},{7,5},{8,10},{9,11},{10,... | collective-permute-start | bytes 835592 | tf_op jit(solution)/shard_map/ppermute | solution.py:50
  17.8 4.5 %collective-permute-start = (bf16[16,2048]{1,0:T(8,128)(2,1)S(1)}, bf16[16,2048]{1,0:T(8,128)(2,1)S(1)}, u32[]{:S(2)}, u32[]{:S(2)}) collective-permute-start(bf16[16,2048]{1,0:T(8,128)(2,1)S(1)} %shard_map.55.refs_0_), channel_id=1, source_target_pairs={{0,4},{1,5},{2,6},{3,7},{4,0},{5,1},{6,2},{7,3},{8,12},{9,13},{10,... | collective-permute-start | bytes 196616 | tf_op jit(solution)/shard_map/ppermute | solution.py:50
  18.7 5.3 %collective-permute-start.1 = (bf16[16,2048]{1,0:T(8,128)(2,1)S(1)}, bf16[16,2048]{1,0:T(8,128)(2,1)S(1)}, u32[]{:S(2)}, u32[]{:S(2)}) collective-permute-start(bf16[16,2048]{1,0:T(8,128)(2,1)S(1)} %shard_map.55.refs_0_), channel_id=1, source_target_pairs={{0,8},{1,9},{2,10},{3,11},{4,12},{5,13},{6,14},{7,15},{8,0},{9,1},... | collective-permute-start | bytes 196616 | tf_op jit(solution)/shard_map/ppermute | solution.py:50
  20.4 6.1 %collective-permute-start.2 = (bf16[16,2048]{1,0:T(8,128)(2,1)S(1)}, bf16[16,2048]{1,0:T(8,128)(2,1)S(1)}, u32[]{:S(2)}, u32[]{:S(2)}) collective-permute-start(bf16[16,2048]{1,0:T(8,128)(2,1)S(1)} %shard_map.55.refs_0_), channel_id=1, source_target_pairs={{0,12},{1,13},{2,14},{3,15},{4,8},{5,9},{6,10},{7,11},{8,4},{9,5},... | collective-permute-start | bytes 196616 | tf_op jit(solution)/shard_map/ppermute | solution.py:50
  26.5 6.5 %collective-permute-start.3 = (bf16[64,2048]{1,0:T(8,128)(2,1)S(1)}, bf16[64,2048]{1,0:T(8,128)(2,1)}, u32[]{:S(2)}, u32[]{:S(2)}) collective-permute-start(bf16[64,2048]{1,0:T(8,128)(2,1)S(1)} %shard_map.56.refs_0_), channel_id=1, source_target_pairs={{0,2},{1,3},{2,0},{3,1},{4,6},{5,7},{6,4},{7,5},{8,10},{9,11},{10,... | collective-permute-start | bytes 786440 | tf_op jit(solution)/shard_map/ppermute | solution.py:50
  27.1 14.1 %collective-permute-start.10 = (bf16[64,2176]{1,0:T(8,128)(2,1)S(1)}, bf16[64,2176]{1,0:T(8,128)(2,1)}, u32[]{:S(2)}, u32[]{:S(2)}) collective-permute-start(bf16[64,2176]{1,0:T(8,128)(2,1)S(1)} %shard_map.58.refs_0_), channel_id=1, source_target_pairs={{0,1},{1,0},{2,3},{3,2},{4,5},{5,4},{6,7},{7,6},{8,9},{9,8},{10,11... | collective-permute-start | bytes 835592 | tf_op jit(solution)/shard_map/ppermute | solution.py:50
  27.1 14.1 %collective-permute-start.11 = (bf16[64,2176]{1,0:T(8,128)(2,1)S(1)}, bf16[64,2176]{1,0:T(8,128)(2,1)}, u32[]{:S(2)}, u32[]{:S(2)}) collective-permute-start(bf16[64,2176]{1,0:T(8,128)(2,1)S(1)} %collective-permute-done.9.refs_1_), channel_id=1, source_target_pairs={{0,1},{1,0},{2,3},{3,2},{4,5},{5,4},{6,7},{7,6},{8,9},{9,8},{10,11... | collective-permute-start | bytes 835592 | tf_op jit(solution)/shard_map/ppermute | solution.py:50
  27.6 18.0 %collective-permute-start.4 = (bf16[64,2048]{1,0:T(8,128)(2,1)S(1)}, bf16[64,2048]{1,0:T(8,128)(2,1)}, u32[]{:S(2)}, u32[]{:S(2)}) collective-permute-start(bf16[64,2048]{1,0:T(8,128)(2,1)S(1)} %shard_map.56.refs_0_), channel_id=1, source_target_pairs={{0,1},{1,0},{2,3},{3,2},{4,5},{5,4},{6,7},{7,6},{8,9},{9,8},{10,11... | collective-permute-start | bytes 786440 | tf_op jit(solution)/shard_map/ppermute | solution.py:50
  33.0 12.5 %collective-permute-start.5 = (bf16[64,2048]{1,0:T(8,128)(2,1)}, bf16[64,2048]{1,0:T(8,128)(2,1)}, u32[]{:S(2)}, u32[]{:S(2)}) collective-permute-start(bf16[64,2048]{1,0:T(8,128)(2,1)} %collective-permute-done.3.refs_1_), channel_id=1, source_target_pairs={{0,1},{1,0},{2,3},{3,2},{4,5},{5,4},{6,7},{7,6},{8,9},{9,8},{10,11... | collective-permute-start | bytes 786440 | tf_op jit(solution)/shard_map/ppermute | solution.py:50
  45.0 5.1 %collective-permute-start.31 = (bf16[64,2048]{1,0:T(8,128)(2,1)S(1)}, bf16[64,2048]{1,0:T(8,128)(2,1)S(1)}, u32[]{:S(2)}, u32[]{:S(2)}) collective-permute-start(bf16[64,2048]{1,0:T(8,128)(2,1)S(1)} %get-tuple-element.73), channel_id=1, source_target_pairs={{0,1},{1,0},{2,3},{3,2},{4,5},{5,4},{6,7},{7,6},{8,9},{9,8},{10,11... | collective-permute-start | bytes 786440 | tf_op jit(solution)/shard_map/ppermute | solution.py:50
  49.5 1.6 %collective-permute-start.13 = (bf16[64,2048]{1,0:T(8,128)(2,1)S(1)}, bf16[64,2048]{1,0:T(8,128)(2,1)S(1)}, u32[]{:S(2)}, u32[]{:S(2)}) collective-permute-start(bf16[64,2048]{1,0:T(8,128)(2,1)S(1)} %get-tuple-element.53), channel_id=1, source_target_pairs={{0,1},{1,0},{2,3},{3,2},{4,5},{5,4},{6,7},{7,6},{8,9},{9,8},{10,11... | collective-permute-start | bytes 786440 | tf_op jit(solution)/shard_map/ppermute | solution.py:50
  49.7 2.7 %collective-permute-start.30 = (bf16[64,2048]{1,0:T(8,128)(2,1)S(1)}, bf16[64,2048]{1,0:T(8,128)(2,1)S(1)}, u32[]{:S(2)}, u32[]{:S(2)}) collective-permute-start(bf16[64,2048]{1,0:T(8,128)(2,1)S(1)} %get-tuple-element.71), channel_id=1, source_target_pairs={{0,1},{1,0},{2,3},{3,2},{4,5},{5,4},{6,7},{7,6},{8,9},{9,8},{10,11... | collective-permute-start | bytes 786440 | tf_op jit(solution)/shard_map/ppermute | solution.py:50
  50.2 9.2 %collective-permute-start.32 = (bf16[64,2048]{1,0:T(8,128)(2,1)S(1)}, bf16[64,2048]{1,0:T(8,128)(2,1)S(1)}, u32[]{:S(2)}, u32[]{:S(2)}) collective-permute-start(bf16[64,2048]{1,0:T(8,128)(2,1)S(1)} %shard_map.70), channel_id=1, source_target_pairs={{0,2},{1,3},{2,0},{3,1},{4,6},{5,7},{6,4},{7,5},{8,10},{9,11},{10,... | collective-permute-start | bytes 786440 | tf_op jit(solution)/shard_map/ppermute | solution.py:50
  50.8 27.6 %collective-permute-start.12 = (bf16[64,2048]{1,0:T(8,128)(2,1)S(1)}, bf16[64,2048]{1,0:T(8,128)(2,1)S(1)}, u32[]{:S(2)}, u32[]{:S(2)}) collective-permute-start(bf16[64,2048]{1,0:T(8,128)(2,1)S(1)} %get-tuple-element.51), channel_id=1, source_target_pairs={{0,1},{1,0},{2,3},{3,2},{4,5},{5,4},{6,7},{7,6},{8,9},{9,8},{10,11... | collective-permute-start | bytes 786440 | tf_op jit(solution)/shard_map/ppermute | solution.py:50
  51.2 27.1 %collective-permute-start.14 = (bf16[64,2048]{1,0:T(8,128)(2,1)S(1)}, bf16[64,2048]{1,0:T(8,128)(2,1)S(1)}, u32[]{:S(2)}, u32[]{:S(2)}) collective-permute-start(bf16[64,2048]{1,0:T(8,128)(2,1)S(1)} %shard_map.62), channel_id=1, source_target_pairs={{0,2},{1,3},{2,0},{3,1},{4,6},{5,7},{6,4},{7,5},{8,10},{9,11},{10,... | collective-permute-start | bytes 786440 | tf_op jit(solution)/shard_map/ppermute | solution.py:50
  59.5 4.5 %collective-permute-start.33 = (bf16[16,2048]{1,0:T(8,128)(2,1)S(1)}, bf16[16,2048]{1,0:T(8,128)(2,1)S(1)}, u32[]{:S(2)}, u32[]{:S(2)}) collective-permute-start(bf16[16,2048]{1,0:T(8,128)(2,1)S(1)} %get-tuple-element.75), channel_id=1, source_target_pairs={{0,4},{1,5},{2,6},{3,7},{4,0},{5,1},{6,2},{7,3},{8,12},{9,13},{10,... | collective-permute-start | bytes 196616 | tf_op jit(solution)/shard_map/ppermute | solution.py:50
  59.6 6.6 %collective-permute-start.34 = (bf16[16,2048]{1,0:T(8,128)(2,1)S(1)}, bf16[16,2048]{1,0:T(8,128)(2,1)S(1)}, u32[]{:S(2)}, u32[]{:S(2)}) collective-permute-start(bf16[16,2048]{1,0:T(8,128)(2,1)S(1)} %get-tuple-element.76), channel_id=1, source_target_pairs={{0,8},{1,9},{2,10},{3,11},{4,12},{5,13},{6,14},{7,15},{8,0},{9,1},... | collective-permute-start | bytes 196616 | tf_op jit(solution)/shard_map/ppermute | solution.py:50
  62.1 6.4 %collective-permute-start.35 = (bf16[16,2048]{1,0:T(8,128)(2,1)S(1)}, bf16[16,2048]{1,0:T(8,128)(2,1)S(1)}, u32[]{:S(2)}, u32[]{:S(2)}) collective-permute-start(bf16[16,2048]{1,0:T(8,128)(2,1)S(1)} %get-tuple-element.77), channel_id=1, source_target_pairs={{0,12},{1,13},{2,14},{3,15},{4,8},{5,9},{6,10},{7,11},{8,4},{9,5},... | collective-permute-start | bytes 196616 | tf_op jit(solution)/shard_map/ppermute | solution.py:50
  68.7 4.5 %collective-permute-start.36 = (bf16[16,2048]{1,0:T(8,128)(2,1)S(1)}, bf16[16,2048]{1,0:T(8,128)(2,1)S(1)}, u32[]{:S(2)}, u32[]{:S(2)}) collective-permute-start(bf16[16,2048]{1,0:T(8,128)(2,1)S(1)} %get-tuple-element.79.refs_0_), channel_id=1, source_target_pairs={{0,4},{1,5},{2,6},{3,7},{4,0},{5,1},{6,2},{7,3},{8,12},{9,13},{10,... | collective-permute-start | bytes 196616 | tf_op jit(solution)/shard_map/ppermute | solution.py:50
  68.7 5.2 %collective-permute-start.37 = (bf16[16,2048]{1,0:T(8,128)(2,1)S(1)}, bf16[16,2048]{1,0:T(8,128)(2,1)S(1)}, u32[]{:S(2)}, u32[]{:S(2)}) collective-permute-start(bf16[16,2048]{1,0:T(8,128)(2,1)S(1)} %get-tuple-element.79.refs_0_), channel_id=1, source_target_pairs={{0,8},{1,9},{2,10},{3,11},{4,12},{5,13},{6,14},{7,15},{8,0},{9,1},... | collective-permute-start | bytes 196616 | tf_op jit(solution)/shard_map/ppermute | solution.py:50
  71.1 6.2 %collective-permute-start.38 = (bf16[16,2048]{1,0:T(8,128)(2,1)S(1)}, bf16[16,2048]{1,0:T(8,128)(2,1)S(1)}, u32[]{:S(2)}, u32[]{:S(2)}) collective-permute-start(bf16[16,2048]{1,0:T(8,128)(2,1)S(1)} %get-tuple-element.79.refs_0_), channel_id=1, source_target_pairs={{0,12},{1,13},{2,14},{3,15},{4,8},{5,9},{6,10},{7,11},{8,4},{9,5},... | collective-permute-start | bytes 196616 | tf_op jit(solution)/shard_map/ppermute | solution.py:50
  77.3 20.3 %collective-permute-start.39 = (bf16[64,2048]{1,0:T(8,128)(2,1)S(1)}, bf16[64,2048]{1,0:T(8,128)(2,1)S(1)}, u32[]{:S(2)}, u32[]{:S(2)}) collective-permute-start(bf16[64,2048]{1,0:T(8,128)(2,1)S(1)} %shard_map.73.refs_0_), channel_id=1, source_target_pairs={{0,2},{1,3},{2,0},{3,1},{4,6},{5,7},{6,4},{7,5},{8,10},{9,11},{10,... | collective-permute-start | bytes 786440 | tf_op jit(solution)/shard_map/ppermute | solution.py:50
  78.4 6.0 %collective-permute-start.15 = (bf16[16,2048]{1,0:T(8,128)(2,1)S(1)}, bf16[16,2048]{1,0:T(8,128)(2,1)S(1)}, u32[]{:S(2)}, u32[]{:S(2)}) collective-permute-start(bf16[16,2048]{1,0:T(8,128)(2,1)S(1)} %get-tuple-element.55), channel_id=1, source_target_pairs={{0,4},{1,5},{2,6},{3,7},{4,0},{5,1},{6,2},{7,3},{8,12},{9,13},{10,... | collective-permute-start | bytes 196616 | tf_op jit(solution)/shard_map/ppermute | solution.py:50
  78.5 6.0 %collective-permute-start.16 = (bf16[16,2048]{1,0:T(8,128)(2,1)S(1)}, bf16[16,2048]{1,0:T(8,128)(2,1)S(1)}, u32[]{:S(2)}, u32[]{:S(2)}) collective-permute-start(bf16[16,2048]{1,0:T(8,128)(2,1)S(1)} %get-tuple-element.56), channel_id=1, source_target_pairs={{0,8},{1,9},{2,10},{3,11},{4,12},{5,13},{6,14},{7,15},{8,0},{9,1},... | collective-permute-start | bytes 196616 | tf_op jit(solution)/shard_map/ppermute | solution.py:50
  81.0 6.3 %collective-permute-start.17 = (bf16[16,2048]{1,0:T(8,128)(2,1)S(1)}, bf16[16,2048]{1,0:T(8,128)(2,1)S(1)}, u32[]{:S(2)}, u32[]{:S(2)}) collective-permute-start(bf16[16,2048]{1,0:T(8,128)(2,1)S(1)} %get-tuple-element.57), channel_id=1, source_target_pairs={{0,12},{1,13},{2,14},{3,15},{4,8},{5,9},{6,10},{7,11},{8,4},{9,5},... | collective-permute-start | bytes 196616 | tf_op jit(solution)/shard_map/ppermute | solution.py:50
  87.4 4.5 %collective-permute-start.18 = (bf16[16,2048]{1,0:T(8,128)(2,1)S(1)}, bf16[16,2048]{1,0:T(8,128)(2,1)S(1)}, u32[]{:S(2)}, u32[]{:S(2)}) collective-permute-start(bf16[16,2048]{1,0:T(8,128)(2,1)S(1)} %get-tuple-element.59.refs_0_), channel_id=1, source_target_pairs={{0,4},{1,5},{2,6},{3,7},{4,0},{5,1},{6,2},{7,3},{8,12},{9,13},{10,... | collective-permute-start | bytes 196616 | tf_op jit(solution)/shard_map/ppermute | solution.py:50
  89.0 5.9 %collective-permute-start.19 = (bf16[16,2048]{1,0:T(8,128)(2,1)S(1)}, bf16[16,2048]{1,0:T(8,128)(2,1)S(1)}, u32[]{:S(2)}, u32[]{:S(2)}) collective-permute-start(bf16[16,2048]{1,0:T(8,128)(2,1)S(1)} %get-tuple-element.59.refs_0_), channel_id=1, source_target_pairs={{0,8},{1,9},{2,10},{3,11},{4,12},{5,13},{6,14},{7,15},{8,0},{9,1},... | collective-permute-start | bytes 196616 | tf_op jit(solution)/shard_map/ppermute | solution.py:50
  90.0 6.2 %collective-permute-start.20 = (bf16[16,2048]{1,0:T(8,128)(2,1)S(1)}, bf16[16,2048]{1,0:T(8,128)(2,1)S(1)}, u32[]{:S(2)}, u32[]{:S(2)}) collective-permute-start(bf16[16,2048]{1,0:T(8,128)(2,1)S(1)} %get-tuple-element.59.refs_0_), channel_id=1, source_target_pairs={{0,12},{1,13},{2,14},{3,15},{4,8},{5,9},{6,10},{7,11},{8,4},{9,5},... | collective-permute-start | bytes 196616 | tf_op jit(solution)/shard_map/ppermute | solution.py:50
  96.2 6.4 %collective-permute-start.21 = (bf16[64,2048]{1,0:T(8,128)(2,1)S(1)}, bf16[64,2048]{1,0:T(8,128)(2,1)S(1)}, u32[]{:S(2)}, u32[]{:S(2)}) collective-permute-start(bf16[64,2048]{1,0:T(8,128)(2,1)S(1)} %shard_map.65.refs_0_), channel_id=1, source_target_pairs={{0,2},{1,3},{2,0},{3,1},{4,6},{5,7},{6,4},{7,5},{8,10},{9,11},{10,... | collective-permute-start | bytes 786440 | tf_op jit(solution)/shard_map/ppermute | solution.py:50
  97.7 5.8 %collective-permute-start.40 = (bf16[64,2048]{1,0:T(8,128)(2,1)S(1)}, bf16[64,2048]{1,0:T(8,128)(2,1)S(1)}, u32[]{:S(2)}, u32[]{:S(2)}) collective-permute-start(bf16[64,2048]{1,0:T(8,128)(2,1)S(1)} %shard_map.73.refs_0_), channel_id=1, source_target_pairs={{0,1},{1,0},{2,3},{3,2},{4,5},{5,4},{6,7},{7,6},{8,9},{9,8},{10,11... | collective-permute-start | bytes 786440 | tf_op jit(solution)/shard_map/ppermute | solution.py:50
  97.7 5.8 %collective-permute-start.41 = (bf16[64,2048]{1,0:T(8,128)(2,1)S(1)}, bf16[64,2048]{1,0:T(8,128)(2,1)S(1)}, u32[]{:S(2)}, u32[]{:S(2)}) collective-permute-start(bf16[64,2048]{1,0:T(8,128)(2,1)S(1)} %collective-permute-done.39.refs_1_), channel_id=1, source_target_pairs={{0,1},{1,0},{2,3},{3,2},{4,5},{5,4},{6,7},{7,6},{8,9},{9,8},{10,11... | collective-permute-start | bytes 786440 | tf_op jit(solution)/shard_map/ppermute | solution.py:50
  98.2 8.5 %collective-permute-start.22 = (bf16[64,2048]{1,0:T(8,128)(2,1)S(1)}, bf16[64,2048]{1,0:T(8,128)(2,1)S(1)}, u32[]{:S(2)}, u32[]{:S(2)}) collective-permute-start(bf16[64,2048]{1,0:T(8,128)(2,1)S(1)} %shard_map.65.refs_0_), channel_id=1, source_target_pairs={{0,1},{1,0},{2,3},{3,2},{4,5},{5,4},{6,7},{7,6},{8,9},{9,8},{10,11... | collective-permute-start | bytes 786440 | tf_op jit(solution)/shard_map/ppermute | solution.py:50
  102.6 4.1 %collective-permute-start.23 = (bf16[64,2048]{1,0:T(8,128)(2,1)S(1)}, bf16[64,2048]{1,0:T(8,128)(2,1)S(1)}, u32[]{:S(2)}, u32[]{:S(2)}) collective-permute-start(bf16[64,2048]{1,0:T(8,128)(2,1)S(1)} %collective-permute-done.21.refs_1_), channel_id=1, source_target_pairs={{0,1},{1,0},{2,3},{3,2},{4,5},{5,4},{6,7},{7,6},{8,9},{9,8},{10,11... | collective-permute-start | bytes 786440 | tf_op jit(solution)/shard_map/ppermute | solution.py:50
  106.1 3.8 %collective-permute-start.43 = (bf16[64,2048]{1,0:T(8,128)(2,1)S(1)}, bf16[64,2048]{1,0:T(8,128)(2,1)S(1)}, u32[]{:S(2)}, u32[]{:S(2)}) collective-permute-start(bf16[64,2048]{1,0:T(8,128)(2,1)S(1)} %get-tuple-element.83), channel_id=1, source_target_pairs={{0,1},{1,0},{2,3},{3,2},{4,5},{5,4},{6,7},{7,6},{8,9},{9,8},{10,11... | collective-permute-start | bytes 786440 | tf_op jit(solution)/shard_map/ppermute | solution.py:50
  109.3 2.1 %collective-permute-start.25 = (bf16[64,2048]{1,0:T(8,128)(2,1)S(1)}, bf16[64,2048]{1,0:T(8,128)(2,1)S(1)}, u32[]{:S(2)}, u32[]{:S(2)}) collective-permute-start(bf16[64,2048]{1,0:T(8,128)(2,1)S(1)} %get-tuple-element.65), channel_id=1, source_target_pairs={{0,1},{1,0},{2,3},{3,2},{4,5},{5,4},{6,7},{7,6},{8,9},{9,8},{10,11... | collective-permute-start | bytes 786440 | tf_op jit(solution)/shard_map/ppermute | solution.py:50
  109.4 3.0 %collective-permute-start.42 = (bf16[64,2048]{1,0:T(8,128)(2,1)S(1)}, bf16[64,2048]{1,0:T(8,128)(2,1)S(1)}, u32[]{:S(2)}, u32[]{:S(2)}) collective-permute-start(bf16[64,2048]{1,0:T(8,128)(2,1)S(1)} %get-tuple-element.81), channel_id=1, source_target_pairs={{0,1},{1,0},{2,3},{3,2},{4,5},{5,4},{6,7},{7,6},{8,9},{9,8},{10,11... | collective-permute-start | bytes 786440 | tf_op jit(solution)/shard_map/ppermute | solution.py:50
  110.0 9.2 %collective-permute-start.44 = (bf16[64,2048]{1,0:T(8,128)(2,1)S(1)}, bf16[64,2048]{1,0:T(8,128)(2,1)S(1)}, u32[]{:S(2)}, u32[]{:S(2)}) collective-permute-start(bf16[64,2048]{1,0:T(8,128)(2,1)S(1)} %shard_map.75), channel_id=1, source_target_pairs={{0,2},{1,3},{2,0},{3,1},{4,6},{5,7},{6,4},{7,5},{8,10},{9,11},{10,... | collective-permute-start | bytes 786440 | tf_op jit(solution)/shard_map/ppermute | solution.py:50
  111.4 12.3 %collective-permute-start.24 = (bf16[64,2048]{1,0:T(8,128)(2,1)S(1)}, bf16[64,2048]{1,0:T(8,128)(2,1)S(1)}, u32[]{:S(2)}, u32[]{:S(2)}) collective-permute-start(bf16[64,2048]{1,0:T(8,128)(2,1)S(1)} %get-tuple-element.63), channel_id=1, source_target_pairs={{0,1},{1,0},{2,3},{3,2},{4,5},{5,4},{6,7},{7,6},{8,9},{9,8},{10,11... | collective-permute-start | bytes 786440 | tf_op jit(solution)/shard_map/ppermute | solution.py:50
  111.5 12.4 %collective-permute-start.26 = (bf16[64,2048]{1,0:T(8,128)(2,1)S(1)}, bf16[64,2048]{1,0:T(8,128)(2,1)S(1)}, u32[]{:S(2)}, u32[]{:S(2)}) collective-permute-start(bf16[64,2048]{1,0:T(8,128)(2,1)S(1)} %shard_map.68), channel_id=1, source_target_pairs={{0,2},{1,3},{2,0},{3,1},{4,6},{5,7},{6,4},{7,5},{8,10},{9,11},{10,... | collective-permute-start | bytes 786440 | tf_op jit(solution)/shard_map/ppermute | solution.py:50
  119.3 7.3 %collective-permute-start.45 = (bf16[16,2048]{1,0:T(8,128)(2,1)S(1)}, bf16[16,2048]{1,0:T(8,128)(2,1)S(1)}, u32[]{:S(2)}, u32[]{:S(2)}) collective-permute-start(bf16[16,2048]{1,0:T(8,128)(2,1)S(1)} %get-tuple-element.85), channel_id=1, source_target_pairs={{0,4},{1,5},{2,6},{3,7},{4,0},{5,1},{6,2},{7,3},{8,12},{9,13},{10,... | collective-permute-start | bytes 196616 | tf_op jit(solution)/shard_map/ppermute | solution.py:50
  120.1 8.5 %collective-permute-start.46 = (bf16[16,2048]{1,0:T(8,128)(2,1)S(1)}, bf16[16,2048]{1,0:T(8,128)(2,1)S(1)}, u32[]{:S(2)}, u32[]{:S(2)}) collective-permute-start(bf16[16,2048]{1,0:T(8,128)(2,1)S(1)} %get-tuple-element.86), channel_id=1, source_target_pairs={{0,8},{1,9},{2,10},{3,11},{4,12},{5,13},{6,14},{7,15},{8,0},{9,1},... | collective-permute-start | bytes 196616 | tf_op jit(solution)/shard_map/ppermute | solution.py:50
  121.8 6.7 %collective-permute-start.47 = (bf16[16,2048]{1,0:T(8,128)(2,1)S(1)}, bf16[16,2048]{1,0:T(8,128)(2,1)S(1)}, u32[]{:S(2)}, u32[]{:S(2)}) collective-permute-start(bf16[16,2048]{1,0:T(8,128)(2,1)S(1)} %get-tuple-element.87), channel_id=1, source_target_pairs={{0,12},{1,13},{2,14},{3,15},{4,8},{5,9},{6,10},{7,11},{8,4},{9,5},... | collective-permute-start | bytes 196616 | tf_op jit(solution)/shard_map/ppermute | solution.py:50
  124.1 5.3 %collective-permute-start.27 = (bf16[16,2048]{1,0:T(8,128)(2,1)S(1)}, bf16[16,2048]{1,0:T(8,128)(2,1)S(1)}, u32[]{:S(2)}, u32[]{:S(2)}) collective-permute-start(bf16[16,2048]{1,0:T(8,128)(2,1)S(1)} %get-tuple-element.67), channel_id=1, source_target_pairs={{0,4},{1,5},{2,6},{3,7},{4,0},{5,1},{6,2},{7,3},{8,12},{9,13},{10,... | collective-permute-start | bytes 196616 | tf_op jit(solution)/shard_map/ppermute | solution.py:50
  124.8 8.0 %collective-permute-start.28 = (bf16[16,2048]{1,0:T(8,128)(2,1)S(1)}, bf16[16,2048]{1,0:T(8,128)(2,1)S(1)}, u32[]{:S(2)}, u32[]{:S(2)}) collective-permute-start(bf16[16,2048]{1,0:T(8,128)(2,1)S(1)} %get-tuple-element.68), channel_id=1, source_target_pairs={{0,8},{1,9},{2,10},{3,11},{4,12},{5,13},{6,14},{7,15},{8,0},{9,1},... | collective-permute-start | bytes 196616 | tf_op jit(solution)/shard_map/ppermute | solution.py:50
  126.5 6.3 %collective-permute-start.29 = (bf16[16,2048]{1,0:T(8,128)(2,1)S(1)}, bf16[16,2048]{1,0:T(8,128)(2,1)S(1)}, u32[]{:S(2)}, u32[]{:S(2)}) collective-permute-start(bf16[16,2048]{1,0:T(8,128)(2,1)S(1)} %get-tuple-element.69), channel_id=1, source_target_pairs={{0,12},{1,13},{2,14},{3,15},{4,8},{5,9},{6,10},{7,11},{8,4},{9,5},... | collective-permute-start | bytes 196616 | tf_op jit(solution)/shard_map/ppermute | solution.py:50
  (13 other events, 350.4 us)

commit v3 on v2

v3 whole, which is shorter than its diff:
```python
import functools

import jax
import jax.numpy as jnp
from jax import lax
from jax.experimental import pallas as pl
from jax.experimental.pallas import tpu as pltpu
from jax.sharding import PartitionSpec as P

eps = 1e-06
LANES = 128
MIB = 2**20
VMEM = pl.BlockSpec(memory_space=pltpu.VMEM)
SMEM = pl.BlockSpec(memory_space=pltpu.SMEM)
ANY = pl.BlockSpec(memory_space=pl.ANY)
bf16, f32 = jnp.bfloat16, jnp.float32


def from_behind(value, axis, steps):
    count = lax.axis_size(axis)
    initial, last = (max(0, -steps), min(count, count - steps))
    return lax.ppermute(value, axis, [(source, source + steps) for source in range(initial, last)])


def call(kernel, outs, specs, *operands, scratch=(), limit=8, flops=0, after=()):
    shapes = tuple(jax.ShapeDtypeStruct(shape, dtype) for shape, dtype in outs)
    moved = sum(x.size * x.dtype.itemsize for x in operands + shapes)
    operands = (*after, *operands)
    return pl.pallas_call(
        lambda *refs: kernel(*refs[len(after) :]),
        out_shape=shapes,
        in_specs=[ANY] * len(after) + specs,
        out_specs=(VMEM,) * len(outs),
        scratch_shapes=scratch,
        compiler_params=pltpu.CompilerParams(vmem_limit_bytes=limit * MIB),
        cost_estimate=pl.CostEstimate(flops=flops, bytes_accessed=moved, transcendentals=0),
    )(*operands)


def swap(value, stride, step, radix, back=False):
    count = lax.axis_size("expert")

    def partner(index):
        digit = index // stride % radix
        if radix & (radix - 1) == 0:
            other = digit ^ step
        else:
            other = (digit + (step if back else radix - step)) % radix
        return index + (other - digit) * stride

    return lax.ppermute(value, "expert", [(i, partner(i)) for i in range(count)])


def join_kernel(count, *refs):
    parts, wholes = refs[:count], refs[count:]
    rows, size = parts[0].shape[0], count // len(wholes)
    for k, part in enumerate(parts):
        wholes[k // size][k % size * rows : (k % size + 1) * rows] = part[...]


def gather_rows(rows):
    far = lax.axis_size("expert") // 4
    tokens, width = rows.shape
    parts = [rows] + [swap(rows, 4, k, far) for k in range(1, far)]
    shape = (far // 2 * tokens, width)
    batches = []
    for near in call(
        functools.partial(join_kernel, far),
        [(shape, rows.dtype)] * 2,
        [VMEM] * far,
        *parts[far // 2 :],
        *parts[: far // 2],
    ):
        beside = swap(near, 2, 1, 2)
        batches.append([near, beside, swap(near, 1, 1, 2), swap(beside, 1, 1, 2)])
    return batches


def sum_kernel(mine, arrived, total):
    total[...] = (mine[...] + arrived[...].astype(f32)).astype(total.dtype)


def split_kernel(mine, near, beside, *pieces):
    rows = pieces[0].shape[0]
    total = mine[...] + near[...].astype(f32) + beside[...].astype(f32)
    for k, piece in enumerate(pieces):
        piece[...] = total[k * rows : (k + 1) * rows].astype(piece.dtype)


def leave_pair(found):
    mine_near, mine_beside, other_near, other_beside = found
    arrived_beside = swap(other_beside, 1, 1, 2, True)
    arrived_near = swap(other_near, 1, 1, 2, True)
    (leaving,) = call(
        sum_kernel, [(mine_beside.shape, bf16)], [VMEM] * 2, mine_beside, arrived_beside
    )
    return mine_near, arrived_near, leaving


def return_rows(batches, tokens):
    far = lax.axis_size("expert") // 4
    returned, steps, earlier = {}, [range(far // 2, far), range(far // 2)], ()
    for (mine_near, arrived_near, leaving), distances in zip(batches, steps):
        shape = mine_near.shape
        beside = swap(leaving, 2, 1, 2, True)
        pieces = call(
            split_kernel,
            [((tokens, shape[1]), bf16 if k else f32) for k in distances],
            [VMEM] * 3,
            mine_near,
            arrived_near,
            beside,
            after=earlier,
        )
        earlier = (pieces[-1],)
        for k, piece in zip(distances, pieces):
            returned[k] = swap(piece, 4, k, far, True) if k else piece
    return [returned[k] for k in range(far)]


def normed_rows(widened, gain_row):
    scale_inv = lax.rsqrt(jnp.mean(widened * widened, axis=-1, keepdims=True) + eps)
    return (widened * scale_inv * gain_row).astype(bf16)


def open_kernel(experts, current_hbm, routes_hbm, gain_hbm, wide_ref, current, routes, gain, sems):
    pairs = ((current_hbm, current), (routes_hbm, routes), (gain_hbm, gain))
    copies = [pltpu.make_async_copy(a, b, sems.at[k]) for k, (a, b) in enumerate(pairs)]
    for copy in copies:
        copy.start()
    for copy in copies:
        copy.wait()
    features = current.shape[-1]
    layers, batches, top, tokens = routes.shape
    columns = wide_ref.shape[1] - features
    wide_ref[:, :features] = normed_rows(current[...].astype(f32), gain[0:1])
    places = lax.broadcasted_iota(jnp.int32, (columns, tokens), 0)
    same = lax.broadcasted_iota(jnp.int32, (tokens, tokens), 0) == lax.broadcasted_iota(
        jnp.int32, (tokens, tokens), 1
    )
    for batch in range(batches):
        chosen = jnp.zeros(places.shape, f32)
        for layer_no in range(layers):
            named = routes[layer_no, batch] + layer_no * experts
            for k in range(top):
                chosen = jnp.where(places == named[k : k + 1], 1.0, chosen)
        turned = lax.dot_general(
            same.astype(bf16),
            chosen.astype(bf16),
            (((1,), (1,)), ((), ())),
            preferred_element_type=f32,
        )
        wide_ref[batch * tokens : (batch + 1) * tokens, features:] = turned.astype(bf16)


def total_rows(current, kept, sent):
    total = kept[...]
    for piece in sent:
        total = total + piece[...].astype(f32)
    return (current.astype(f32) + total * 0.125).astype(bf16)


def close_kernel(layer_no, current_ref, gain_ref, kept, *refs):
    *sent, out_ref, normed_ref = refs
    out = total_rows(current_ref[...], kept, sent)
    out_ref[...] = out
    normed_ref[...] = normed_rows(out.astype(f32), gain_ref[layer_no : layer_no + 1])


def end_kernel(earlier, current_ref, kept, *refs):
    sent, before, outs_ref = refs[: len(refs) - earlier - 1], refs[-earlier - 1 : -1], refs[-1]
    layers, batches, tokens, _ = outs_ref.shape
    done = [ref[...] for ref in before] + [total_rows(current_ref[...], kept, sent)]
    for layer_no in range(layers):
        for batch in range(batches):
            outs_ref[layer_no, batch] = done[layer_no][batch * tokens : (batch + 1) * tokens]


def load_kernel(layer_no, cuts, gate_up_hbm, down_hbm, gate_up_ref, down_ref, sems):
    copies = []
    for source, target in ((gate_up_hbm, gate_up_ref), (down_hbm, down_ref)):
        rows = target.shape[0] // cuts
        for cut in range(cuts):
            span = pl.ds(cut * rows, rows)
            copies.append(
                pltpu.make_async_copy(
                    source.at[layer_no, 0, span], target.at[span], sems.at[len(copies)]
                )
            )
    for copy in copies:
        copy.start()
    for copy in copies:
        copy.wait()


def load_weights(layer_no, w_gate_up, w_down):
    cuts = 4
    return call(
        functools.partial(load_kernel, layer_no, cuts),
        [(w_gate_up.shape[2:], bf16), (w_down.shape[2:], bf16)],
        [ANY] * 2,
        in_hbm(w_gate_up),
        in_hbm(w_down),
        scratch=[pltpu.SemaphoreType.DMA((2 * cuts,))],
        limit=12,
    )


def tile_of(extent, most):
    size = most
    while extent % size:
        size //= 2
    return size


def expert_kernel(first_column, wide, me_ref, *refs):
    if wide:
        parts, refs = refs[:4], refs[4:]
        gate_up_ref, down_ref, *outs, routed_ref, rows_ref, hidden_ref = refs
    else:
        parts, refs = refs[:4], refs[4:]
        routed_ref, gate_up_ref, down_ref, *outs, rows_ref, hidden_ref = refs
    hidden_size, features = down_ref.shape
    quarter = parts[0].shape[0]
    for k, part in enumerate(parts):
        span = slice(k * quarter, (k + 1) * quarter)
        rows_ref[span] = part[:, :features]
        if wide:
            routed_ref[span] = part[:, features:]
    places = lax.broadcasted_iota(jnp.int32, routed_ref.shape, 1)
    chosen = jnp.where(places == me_ref[0] + first_column, routed_ref[...].astype(f32), 0.0)
    share = jnp.sum(chosen, axis=1, keepdims=True)
    rows = rows_ref[...]
    size = tile_of(hidden_size, 256)
    for low in range(0, hidden_size, size):
        span, beside = slice(low, low + size), slice(hidden_size + low, hidden_size + low + size)
        gate = jnp.dot(rows, gate_up_ref[:, span], preferred_element_type=f32)
        up = jnp.dot(rows, gate_up_ref[:, beside], preferred_element_type=f32)
        hidden_ref[:, span] = (gate / (1.0 + jnp.exp(-gate)) * up).astype(bf16)
    hidden = hidden_ref[...]
    size = tile_of(features, 512)
    for low in range(0, features, size):
        span = slice(low, low + size)
        done = jnp.dot(hidden, down_ref[:, span], preferred_element_type=f32) * share
        for k, out in enumerate(outs):
            out[:, span] = done[k * quarter : (k + 1) * quarter].astype(out.dtype)


def run_expert(parts, routed, me, first_column, weights, after):
    gate_up, down_proj = weights
    hidden_size, features = down_proj.shape
    quarter, width = parts[0].shape
    count = 4 * quarter
    wide = routed is None
    outs = [((quarter, features), f32)] * 2 + [((quarter, features), bf16)] * 2
    if wide:
        outs = outs + [((count, width - features), bf16)]
    found = call(
        functools.partial(expert_kernel, first_column, wide),
        outs,
        [SMEM] + [VMEM] * (6 if wide else 7),
        me,
        *parts,
        *([] if wide else [routed]),
        gate_up,
        down_proj,
        scratch=[pltpu.VMEM((count, features), bf16), pltpu.VMEM((count, hidden_size), bf16)],
        limit=24,
        after=after,
        flops=6 * count * features * hidden_size,
    )
    return found[:4], found[4] if wide else routed


def in_hbm(array):
    return pltpu.with_memory_space_constraint(array, pltpu.HBM)


def open_rows(current, routes, gain, experts):
    batches, tokens, features = current.shape
    rows = batches * tokens
    columns = routes.shape[0] * experts
    width = features + columns + -columns % LANES
    current, routes = current.reshape(rows, features), jnp.swapaxes(routes, 2, 3)
    (wide,) = call(
        functools.partial(open_kernel, experts),
        [((rows, width), bf16)],
        [ANY] * 3,
        in_hbm(current),
        in_hbm(routes),
        in_hbm(gain),
        scratch=[
            pltpu.VMEM(current.shape, bf16),
            pltpu.VMEM(routes.shape, jnp.int32),
            pltpu.VMEM(gain.shape, f32),
            pltpu.SemaphoreType.DMA((3,)),
        ],
    )
    return wide


def run_layer(rows, routed, me, first_column, weights):
    found, columns = [], []
    batches = gather_rows(rows)
    after = (batches[-1][0],)
    for place, parts in enumerate(batches):
        outs, kept = run_expert(
            parts, None if routed is None else routed[place], me, first_column, weights, after
        )
        found.append(leave_pair(outs))
        after = (found[-1][2],)
        columns.append(kept)
    return return_rows(found, rows.shape[0]), columns


def close_rows(layer_no, current, gain, returned):
    return call(
        functools.partial(close_kernel, layer_no),
        [(current.shape, bf16)] * 2,
        [VMEM] * (2 + len(returned)),
        current,
        gain,
        *returned,
    )


def on_device(inputs, routes, norm_gain, w_gate_up, w_down):
    experts = lax.axis_size("expert")
    sections = lax.axis_size("section")
    me = lax.axis_index("expert").astype(jnp.int32).reshape(1)
    batches, tokens, features = inputs.shape
    layers = routes.shape[0]
    weights = [load_weights(layer_no, w_gate_up, w_down) for layer_no in range(layers)]
    if sections == 1:
        outs, routed = [], None
        current = inputs.reshape(batches * tokens, features)
        rows = open_rows(inputs, routes, norm_gain, experts)
        for layer_no in range(layers):
            returned, routed = run_layer(rows, routed, me, layer_no * experts, weights[layer_no])
            if layer_no == layers - 1:
                (whole,) = call(
                    functools.partial(end_kernel, len(outs)),
                    [((layers, batches, tokens, features), bf16)],
                    [VMEM] * (1 + len(returned) + len(outs)),
                    current,
                    *returned,
                    *outs,
                )
                return whole
            current, rows = close_rows(layer_no + 1, current, norm_gain, returned)
            outs.append(current)
    segment_no = lax.axis_index("section")
    handed = jnp.zeros((tokens, features), bf16)
    finished = []
    for turn_no in range(batches + 1):
        if turn_no < batches:
            fresh_rows = inputs[turn_no]
        else:
            fresh_rows = jnp.zeros((tokens, features), bf16)
        current = jnp.where(segment_no == 0, fresh_rows, handed)
        batch_pick = jnp.clip(turn_no - segment_no, 0, batches - 1)
        turn_routes = lax.dynamic_slice_in_dim(routes, batch_pick, 1, 1)
        rows = open_rows(current[None], turn_routes, norm_gain, experts)
        returned, _ = run_layer(rows, None, me, 0, weights[0])
        result, _ = close_rows(0, current, norm_gain, returned)
        finished.append(result)
        if turn_no < batches:
            handed = from_behind(result, "section", 1)
    first_segment = jnp.stack(finished[:batches])
    second_segment = jnp.stack(finished[1:])
    return jnp.where(segment_no == 0, first_segment, second_segment)[None]


def solution(mesh):
    placed = (
        P(None, ("groups", "expert"), None),
        P("section", None, ("groups", "expert"), None),
        P("section", None),
        P("section", "expert", None, None),
        P("section", "expert", None, None),
    )
    return jax.shard_map(
        on_device,
        mesh=mesh,
        in_specs=placed,
        out_specs=P("section", None, ("groups", "expert"), None),
        check_vma=False,
    )
```

time: 134 us -> 122 us (0.910)
  local copies, waits for them, and re-layouts: 11.4 us -> 0.01 us
  starting transfers between devices: 49 us -> 38.3 us
  waiting for transfers between devices: 55.6 us -> 61.9 us
  Pallas kernels: 17.2 us -> 21 us
    unnamed x27 -> x4, local copies, waits for them, and re-layouts: 11.4 us -> 0.01 us
    ppermute x48 -> x36, starting transfers between devices: 49 us -> 38.3 us  [swap(): lax.ppermute(value, 'expert', [(i, partner(i)) for i in range(count)])]
    ppermute x48 -> x36, waiting for transfers between devices: 55.6 us -> 61.9 us  [swap(): lax.ppermute(value, 'expert', [(i, partner(i)) for i in range(count)])]
    pallas_call x24 -> x19, Pallas kernels: 17.2 us -> 21 us  [call(): pl.pallas_call(lambda *refs: kernel(*refs[len(after):]), out_shape=shapes...]
  transfers between devices with their start and end apart: 48 -> 36, of which waited for: 19 -> 17; matrix products, arithmetic and copies ran while one was open for 0% -> 0% of each run, Pallas kernels for 12% -> 11%
where the time goes in v3:
time: 122 us; the launch traced here: 121 us
  waiting for transfers between devices  61.9 us (51%)
  starting transfers between devices  38.3 us (31%)
  Pallas kernels  21 us (17%)
    ppermute x36, waiting for transfers between devices, swap(): lax.ppermute(value, 'expert', [(i, partner(i)) for i in range(count)])  61.9 us
    ppermute x36, starting transfers between devices, swap(): lax.ppermute(value, 'expert', [(i, partner(i)) for i in range(count)])  38.3 us
    pallas_call x19, Pallas kernels, call(): pl.pallas_call(lambda *refs: kernel(*refs[len(after):]), out_shape=shapes...  21 us
  transfers between devices with their start and end apart: 36, of which 17 were waited for; matrix products, arithmetic and copies ran while one was open for 0% of the time, Pallas kernels for 11%

profile of v3, /device:TPU:0, one launch (start us, length us, event | category | flops | bytes accessed | tf_op | source)
XLA Modules:
  0.0 121.4 jit_solution(3470990547639692874)
XLA Ops:
  0.0 1.2 shard_map.55.refs_2_
  1.2 4.1 %collective-permute-start = (bf16[32,2176]{1,0:T(8,128)(2,1)S(1)}, bf16[32,2176]{1,0:T(8,128)(2,1)S(1)}, u32[]{:S(2)}, u32[]{:S(2)}) collective-permute-start(bf16[32,2176]{1,0:T(8,128)(2,1)S(1)} %shard_map.55.refs_2_), channel_id=1, source_target_pairs={{0,8},{1,9},{2,10},{3,11},{4,12},{5,13},{6,14},{7,15},{8,0},{9,1},... | collective-permute-start | bytes 417800 | tf_op jit(solution)/shard_map/ppermute | solution.py:51
  5.3 1.3 %collective-permute-start.1 = (bf16[32,2176]{1,0:T(8,128)(2,1)S(1)}, bf16[32,2176]{1,0:T(8,128)(2,1)S(1)}, u32[]{:S(2)}, u32[]{:S(2)}) collective-permute-start(bf16[32,2176]{1,0:T(8,128)(2,1)S(1)} %shard_map.55.refs_2_), channel_id=1, source_target_pairs={{0,12},{1,13},{2,14},{3,15},{4,8},{5,9},{6,10},{7,11},{8,4},{9,5},... | collective-permute-start | bytes 417800 | tf_op jit(solution)/shard_map/ppermute | solution.py:51
  6.9 8.9 %collective-permute-done.refs_0_ = bf16[32,2176]{1,0:T(8,128)(2,1)S(1)} collective-permute-done((bf16[32,2176]{1,0:T(8,128)(2,1)S(1)}, bf16[32,2176]{1,0:T(8,128)(2,1)S(1)}, u32[]{:S(2)}, u32[]{:S(2)}) %collective-permute-start) | collective-permute-done | bytes 139296 | tf_op jit(solution)/shard_map/ppermute | solution.py:51
  15.8 0.5 collective-permute-done.2.refs_3_
  16.4 1.6 %collective-permute-start.3 = (bf16[64,2176]{1,0:T(8,128)(2,1)S(1)}, bf16[64,2176]{1,0:T(8,128)(2,1)S(1)}, u32[]{:S(2)}, u32[]{:S(2)}) collective-permute-start(bf16[64,2176]{1,0:T(8,128)(2,1)S(1)} %get-tuple-element.42.refs_2_), channel_id=1, source_target_pairs={{0,2},{1,3},{2,0},{3,1},{4,6},{5,7},{6,4},{7,5},{8,10},{9,11},{10,... | collective-permute-start | bytes 835592 | tf_op jit(solution)/shard_map/ppermute | solution.py:51
  18.0 0.5 collective-permute-start.9
  18.5 7.5 %collective-permute-done.3.refs_3_ = bf16[64,2176]{1,0:T(8,128)(2,1)S(1)} collective-permute-done((bf16[64,2176]{1,0:T(8,128)(2,1)S(1)}, bf16[64,2176]{1,0:T(8,128)(2,1)S(1)}, u32[]{:S(2)}, u32[]{:S(2)}) %collective-permute-start.3) | collective-permute-done | bytes 278560 | tf_op jit(solution)/shard_map/ppermute | solution.py:51
  26.0 3.7 %shard_map.57 = (bf16[2048,1536]{1,0:T(8,128)(2,1)S(1)}, bf16[768,2048]{1,0:T(8,128)(2,1)S(1)}) custom-call(bf16[2,1,2048,1536]{3,2,1,0:T(8,128)(2,1)} %refs_0_.3, bf16[2,1,768,2048]{3,2,1,0:T(8,128)(2,1)} %refs_1_.5), custom_call_target="tpu_custom_call" | custom-call | bytes 28311552 | tf_op jit(solution)/shard_map/pallas_call | solution.py:29
  29.7 0.6 collective-permute-start.10
  30.4 2.7 %shard_map.58 = (f32[64,2048]{1,0:T(8,128)S(1)}, f32[64,2048]{1,0:T(8,128)S(1)}, bf16[64,2048]{1,0:T(8,128)(2,1)S(1)}, bf16[64,2048]{1,0:T(8,128)(2,1)S(1)}, bf16[256,128]{1,0:T(8,128)(2,1)S(1)}) custom-call(bf16[64,2176]{1,0:T(8,128)(2,1)S(1)} %get-tuple-element.41.refs_0_.refs_2_, s32[1]{0:T(128)} %bitcast.2.refs_1_, ...), custom_call_target="tpu_custom_call" | custom-call | flops 2415919104 | bytes 12189700 | tf_op jit(solution)/shard_map/pallas_call | solution.py:29
  33.0 0.5 collective-permute-start.7
  33.5 1.2 collective-permute-done.7.refs_1_
  34.8 2.7 %shard_map.61 = (f32[64,2048]{1,0:T(8,128)S(1)}, f32[64,2048]{1,0:T(8,128)S(1)}, bf16[64,2048]{1,0:T(8,128)(2,1)S(1)}, bf16[64,2048]{1,0:T(8,128)(2,1)S(1)}, bf16[256,128]{1,0:T(8,128)(2,1)S(1)}) custom-call(bf16[64,2048]{1,0:T(8,128)(2,1)S(1)} %shard_map.59.refs_0_, s32[1]{0:T(128)} %bitcast.2.refs_1_, ...), custom_call_target="tpu_custom_call" | custom-call | flops 2415919104 | bytes 12189700 | tf_op jit(solution)/shard_map/pallas_call | solution.py:29
  37.5 0.4 collective-permute-start.13
  38.0 1.3 %collective-permute-start.8 = (bf16[64,2048]{1,0:T(8,128)(2,1)S(1)}, bf16[64,2048]{1,0:T(8,128)(2,1)S(1)}, u32[]{:S(2)}, u32[]{:S(2)}) collective-permute-start(bf16[64,2048]{1,0:T(8,128)(2,1)S(1)} %shard_map.59.refs_0_), channel_id=1, source_target_pairs={{0,2},{1,3},{2,0},{3,1},{4,6},{5,7},{6,4},{7,5},{8,10},{9,11},{10,... | collective-permute-start | bytes 786440 | tf_op jit(solution)/shard_map/ppermute | solution.py:51
  39.5 1.0 collective-permute-start.14
  40.5 6.7 %collective-permute-done.8.refs_2_ = bf16[64,2048]{1,0:T(8,128)(2,1)S(1)} collective-permute-done((bf16[64,2048]{1,0:T(8,128)(2,1)S(1)}, bf16[64,2048]{1,0:T(8,128)(2,1)S(1)}, u32[]{:S(2)}, u32[]{:S(2)}) %collective-permute-start.8) | collective-permute-done | bytes 262176 | tf_op jit(solution)/shard_map/ppermute | solution.py:51
  47.3 5.1 %collective-permute-start.16 = (bf16[32,2048]{1,0:T(8,128)(2,1)S(1)}, bf16[32,2048]{1,0:T(8,128)(2,1)S(1)}, u32[]{:S(2)}, u32[]{:S(2)}) collective-permute-start(bf16[32,2048]{1,0:T(8,128)(2,1)S(1)} %get-tuple-element.56), channel_id=1, source_target_pairs={{0,8},{1,9},{2,10},{3,11},{4,12},{5,13},{6,14},{7,15},{8,0},{9,1},... | collective-permute-start | bytes 393224 | tf_op jit(solution)/shard_map/ppermute | solution.py:51
  52.3 0.4 collective-permute-start.17
  52.9 2.6 %collective-permute-start.15 = (bf16[32,2048]{1,0:T(8,128)(2,1)S(1)}, bf16[32,2048]{1,0:T(8,128)(2,1)S(1)}, u32[]{:S(2)}, u32[]{:S(2)}) collective-permute-start(bf16[32,2048]{1,0:T(8,128)(2,1)S(1)} %get-tuple-element.55), channel_id=1, source_target_pairs={{0,4},{1,5},{2,6},{3,7},{4,0},{5,1},{6,2},{7,3},{8,12},{9,13},{10,... | collective-permute-start | bytes 393224 | tf_op jit(solution)/shard_map/ppermute | solution.py:51
  55.5 5.5 %collective-permute-done.16.refs_4_ = bf16[32,2048]{1,0:T(8,128)(2,1)S(1)} collective-permute-done((bf16[32,2048]{1,0:T(8,128)(2,1)S(1)}, bf16[32,2048]{1,0:T(8,128)(2,1)S(1)}, u32[]{:S(2)}, u32[]{:S(2)}) %collective-permute-start.16) | collective-permute-done | bytes 131104 | tf_op jit(solution)/shard_map/ppermute | solution.py:51
  60.9 2.4 %collective-permute-done.15.refs_3_ = bf16[32,2048]{1,0:T(8,128)(2,1)S(1)} collective-permute-done((bf16[32,2048]{1,0:T(8,128)(2,1)S(1)}, bf16[32,2048]{1,0:T(8,128)(2,1)S(1)}, u32[]{:S(2)}, u32[]{:S(2)}) %collective-permute-start.15) | collective-permute-done | bytes 131104 | tf_op jit(solution)/shard_map/ppermute | solution.py:51
  63.5 0.6 collective-permute-start.18
  64.1 2.6 %collective-permute-start.19 = (bf16[32,2048]{1,0:T(8,128)(2,1)S(1)}, bf16[32,2048]{1,0:T(8,128)(2,1)S(1)}, u32[]{:S(2)}, u32[]{:S(2)}) collective-permute-start(bf16[32,2048]{1,0:T(8,128)(2,1)S(1)} %get-tuple-element.58.refs_2_), channel_id=1, source_target_pairs={{0,12},{1,13},{2,14},{3,15},{4,8},{5,9},{6,10},{7,11},{8,4},{9,5},... | collective-permute-start | bytes 393224 | tf_op jit(solution)/shard_map/ppermute | solution.py:51
  66.7 0.4 collective-permute-start.20
  67.1 8.6 %collective-permute-done.18.refs_0_ = bf16[32,2048]{1,0:T(8,128)(2,1)S(1)} collective-permute-done((bf16[32,2048]{1,0:T(8,128)(2,1)S(1)}, bf16[32,2048]{1,0:T(8,128)(2,1)S(1)}, u32[]{:S(2)}, u32[]{:S(2)}) %collective-permute-start.18) | collective-permute-done | bytes 131104 | tf_op jit(solution)/shard_map/ppermute | solution.py:51
  75.7 1.1 collective-permute-done.20.refs_3_
  76.8 1.6 %collective-permute-start.21 = (bf16[64,2048]{1,0:T(8,128)(2,1)S(1)}, bf16[64,2048]{1,0:T(8,128)(2,1)S(1)}, u32[]{:S(2)}, u32[]{:S(2)}) collective-permute-start(bf16[64,2048]{1,0:T(8,128)(2,1)S(1)} %get-tuple-element.60.refs_2_), channel_id=1, source_target_pairs={{0,2},{1,3},{2,0},{3,1},{4,6},{5,7},{6,4},{7,5},{8,10},{9,11},{10,... | collective-permute-start | bytes 786440 | tf_op jit(solution)/shard_map/ppermute | solution.py:51
  78.4 5.7 %collective-permute-done.21.refs_3_ = bf16[64,2048]{1,0:T(8,128)(2,1)S(1)} collective-permute-done((bf16[64,2048]{1,0:T(8,128)(2,1)S(1)}, bf16[64,2048]{1,0:T(8,128)(2,1)S(1)}, u32[]{:S(2)}, u32[]{:S(2)}) %collective-permute-start.21) | collective-permute-done | bytes 262176 | tf_op jit(solution)/shard_map/ppermute | solution.py:51
  84.1 1.5 %collective-permute-start.27 = (bf16[64,2048]{1,0:T(8,128)(2,1)S(1)}, bf16[64,2048]{1,0:T(8,128)(2,1)S(1)}, u32[]{:S(2)}, u32[]{:S(2)}) collective-permute-start(bf16[64,2048]{1,0:T(8,128)(2,1)S(1)} %get-tuple-element.59.refs_0_.refs_2_), channel_id=1, source_target_pairs={{0,2},{1,3},{2,0},{3,1},{4,6},{5,7},{6,4},{7,5},{8,10},{9,11},{10,... | collective-permute-start | bytes 786440 | tf_op jit(solution)/shard_map/ppermute | solution.py:51
  85.6 3.7 %shard_map.66 = (bf16[2048,1536]{1,0:T(8,128)(2,1)S(1)}, bf16[768,2048]{1,0:T(8,128)(2,1)S(1)}) custom-call(bf16[2,1,2048,1536]{3,2,1,0:T(8,128)(2,1)} %refs_0_.3, bf16[2,1,768,2048]{3,2,1,0:T(8,128)(2,1)} %refs_1_.5), custom_call_target="tpu_custom_call" | custom-call | bytes 28311552 | tf_op jit(solution)/shard_map/pallas_call | solution.py:29
  89.4 2.7 %shard_map.67 = (f32[64,2048]{1,0:T(8,128)S(1)}, f32[64,2048]{1,0:T(8,128)S(1)}, bf16[64,2048]{1,0:T(8,128)(2,1)S(1)}, bf16[64,2048]{1,0:T(8,128)(2,1)S(1)}) custom-call(bf16[64,2048]{1,0:T(8,128)(2,1)S(1)} %get-tuple-element.59.refs_0_.refs_2_, s32[1]{0:T(128)} %bitcast.2.refs_1_, bf16[64,2048]{1,0:T(8,128)(2,1)S(1)} %get-tuple-element.60.refs_2_, ...), custom_call_target="tpu_custom_call" | custom-call | flops 2415919104 | bytes 12124164 | tf_op jit(solution)/shard_map/pallas_call | solution.py:29
  92.1 0.3 collective-permute-start.25
  92.9 0.8 collective-permute-done.25.refs_1_
  93.7 0.3 collective-permute-done.28.refs_4_
  94.1 0.4 collective-permute-done.29.refs_5_
  94.4 2.7 %shard_map.70 = (f32[64,2048]{1,0:T(8,128)S(1)}, f32[64,2048]{1,0:T(8,128)S(1)}, bf16[64,2048]{1,0:T(8,128)(2,1)S(1)}, bf16[64,2048]{1,0:T(8,128)(2,1)S(1)}) custom-call(bf16[64,2048]{1,0:T(8,128)(2,1)S(1)} %shard_map.68.refs_0_, s32[1]{0:T(128)} %bitcast.2.refs_1_, bf16[64,2048]{1,0:T(8,128)(2,1)S(1)} %get-tuple-element.59.refs_0_.refs_2_, ...), custom_call_target="tpu_custom_call" | custom-call | flops 2415919104 | bytes 12124164 | tf_op jit(solution)/shard_map/pallas_call | solution.py:29
  97.1 0.3 collective-permute-start.31
  97.7 1.5 %collective-permute-start.26 = (bf16[64,2048]{1,0:T(8,128)(2,1)S(1)}, bf16[64,2048]{1,0:T(8,128)(2,1)S(1)}, u32[]{:S(2)}, u32[]{:S(2)}) collective-permute-start(bf16[64,2048]{1,0:T(8,128)(2,1)S(1)} %shard_map.68.refs_0_), channel_id=1, source_target_pairs={{0,2},{1,3},{2,0},{3,1},{4,6},{5,7},{6,4},{7,5},{8,10},{9,11},{10,... | collective-permute-start | bytes 786440 | tf_op jit(solution)/shard_map/ppermute | solution.py:51
  99.2 1.1 collective-permute-start.32
  100.3 6.5 %collective-permute-done.26.refs_2_ = bf16[64,2048]{1,0:T(8,128)(2,1)S(1)} collective-permute-done((bf16[64,2048]{1,0:T(8,128)(2,1)S(1)}, bf16[64,2048]{1,0:T(8,128)(2,1)S(1)}, u32[]{:S(2)}, u32[]{:S(2)}) %collective-permute-start.26) | collective-permute-done | bytes 262176 | tf_op jit(solution)/shard_map/ppermute | solution.py:51
  106.9 2.0 %collective-permute-start.34 = (bf16[32,2048]{1,0:T(8,128)(2,1)S(1)}, bf16[32,2048]{1,0:T(8,128)(2,1)S(1)}, u32[]{:S(2)}, u32[]{:S(2)}) collective-permute-start(bf16[32,2048]{1,0:T(8,128)(2,1)S(1)} %get-tuple-element.76), channel_id=1, source_target_pairs={{0,8},{1,9},{2,10},{3,11},{4,12},{5,13},{6,14},{7,15},{8,0},{9,1},... | collective-permute-start | bytes 393224 | tf_op jit(solution)/shard_map/ppermute | solution.py:51
  108.9 3.4 %collective-permute-start.35 = (bf16[32,2048]{1,0:T(8,128)(2,1)S(1)}, bf16[32,2048]{1,0:T(8,128)(2,1)S(1)}, u32[]{:S(2)}, u32[]{:S(2)}) collective-permute-start(bf16[32,2048]{1,0:T(8,128)(2,1)S(1)} %get-tuple-element.68.refs_0_), channel_id=1, source_target_pairs={{0,12},{1,13},{2,14},{3,15},{4,8},{5,9},{6,10},{7,11},{8,4},{9,5},... | collective-permute-start | bytes 393224 | tf_op jit(solution)/shard_map/ppermute | solution.py:51
  112.4 2.5 %collective-permute-start.33 = (bf16[32,2048]{1,0:T(8,128)(2,1)S(1)}, bf16[32,2048]{1,0:T(8,128)(2,1)S(1)}, u32[]{:S(2)}, u32[]{:S(2)}) collective-permute-start(bf16[32,2048]{1,0:T(8,128)(2,1)S(1)} %get-tuple-element.75), channel_id=1, source_target_pairs={{0,4},{1,5},{2,6},{3,7},{4,0},{5,1},{6,2},{7,3},{8,12},{9,13},{10,... | collective-permute-start | bytes 393224 | tf_op jit(solution)/shard_map/ppermute | solution.py:51
  114.8 4.4 %collective-permute-done.34.refs_3_ = bf16[32,2048]{1,0:T(8,128)(2,1)S(1)} collective-permute-done((bf16[32,2048]{1,0:T(8,128)(2,1)S(1)}, bf16[32,2048]{1,0:T(8,128)(2,1)S(1)}, u32[]{:S(2)}, u32[]{:S(2)}) %collective-permute-start.34) | collective-permute-done | bytes 131104 | tf_op jit(solution)/shard_map/ppermute | solution.py:51
  119.2 1.4 %collective-permute-done.33.refs_2_ = bf16[32,2048]{1,0:T(8,128)(2,1)S(1)} collective-permute-done((bf16[32,2048]{1,0:T(8,128)(2,1)S(1)}, bf16[32,2048]{1,0:T(8,128)(2,1)S(1)}, u32[]{:S(2)}, u32[]{:S(2)}) %collective-permute-start.33) | collective-permute-done | bytes 131104 | tf_op jit(solution)/shard_map/ppermute | solution.py:51
  120.6 0.8 shard_map.73
  (47 shorter events, 2.2 us)
Async XLA Ops:
  1.2 14.6 %collective-permute-start = (bf16[32,2176]{1,0:T(8,128)(2,1)S(1)}, bf16[32,2176]{1,0:T(8,128)(2,1)S(1)}, u32[]{:S(2)}, u32[]{:S(2)}) collective-permute-start(bf16[32,2176]{1,0:T(8,128)(2,1)S(1)} %shard_map.55.refs_2_), channel_id=1, source_target_pairs={{0,8},{1,9},{2,10},{3,11},{4,12},{5,13},{6,14},{7,15},{8,0},{9,1},... | collective-permute-start | bytes 417800 | tf_op jit(solution)/shard_map/ppermute | solution.py:51
  5.3 10.5 %collective-permute-start.1 = (bf16[32,2176]{1,0:T(8,128)(2,1)S(1)}, bf16[32,2176]{1,0:T(8,128)(2,1)S(1)}, u32[]{:S(2)}, u32[]{:S(2)}) collective-permute-start(bf16[32,2176]{1,0:T(8,128)(2,1)S(1)} %shard_map.55.refs_2_), channel_id=1, source_target_pairs={{0,12},{1,13},{2,14},{3,15},{4,8},{5,9},{6,10},{7,11},{8,4},{9,5},... | collective-permute-start | bytes 417800 | tf_op jit(solution)/shard_map/ppermute | solution.py:51
  6.7 9.7 %collective-permute-start.2 = (bf16[32,2176]{1,0:T(8,128)(2,1)S(1)}, bf16[32,2176]{1,0:T(8,128)(2,1)S(1)}, u32[]{:S(2)}, u32[]{:S(2)}) collective-permute-start(bf16[32,2176]{1,0:T(8,128)(2,1)S(1)} %shard_map.55.refs_2_), channel_id=1, source_target_pairs={{0,4},{1,5},{2,6},{3,7},{4,0},{5,1},{6,2},{7,3},{8,12},{9,13},{10,... | collective-permute-start | bytes 417800 | tf_op jit(solution)/shard_map/ppermute | solution.py:51
  16.4 9.6 %collective-permute-start.3 = (bf16[64,2176]{1,0:T(8,128)(2,1)S(1)}, bf16[64,2176]{1,0:T(8,128)(2,1)S(1)}, u32[]{:S(2)}, u32[]{:S(2)}) collective-permute-start(bf16[64,2176]{1,0:T(8,128)(2,1)S(1)} %get-tuple-element.42.refs_2_), channel_id=1, source_target_pairs={{0,2},{1,3},{2,0},{3,1},{4,6},{5,7},{6,4},{7,5},{8,10},{9,11},{10,... | collective-permute-start | bytes 835592 | tf_op jit(solution)/shard_map/ppermute | solution.py:51
  18.0 12.3 %collective-permute-start.9 = (bf16[64,2176]{1,0:T(8,128)(2,1)S(1)}, bf16[64,2176]{1,0:T(8,128)(2,1)S(1)}, u32[]{:S(2)}, u32[]{:S(2)}) collective-permute-start(bf16[64,2176]{1,0:T(8,128)(2,1)S(1)} %get-tuple-element.41.refs_0_.refs_2_), channel_id=1, source_target_pairs={{0,2},{1,3},{2,0},{3,1},{4,6},{5,7},{6,4},{7,5},{8,10},{9,11},{10,... | collective-permute-start | bytes 835592 | tf_op jit(solution)/shard_map/ppermute | solution.py:51
  18.5 11.9 %collective-permute-start.4 = (bf16[64,2176]{1,0:T(8,128)(2,1)S(1)}, bf16[64,2176]{1,0:T(8,128)(2,1)S(1)}, u32[]{:S(2)}, u32[]{:S(2)}) collective-permute-start(bf16[64,2176]{1,0:T(8,128)(2,1)S(1)} %get-tuple-element.42.refs_2_), channel_id=1, source_target_pairs={{0,1},{1,0},{2,3},{3,2},{4,5},{5,4},{6,7},{7,6},{8,9},{9,8},{10,11... | collective-permute-start | bytes 835592 | tf_op jit(solution)/shard_map/ppermute | solution.py:51
  26.0 4.4 %collective-permute-start.5 = (bf16[64,2176]{1,0:T(8,128)(2,1)S(1)}, bf16[64,2176]{1,0:T(8,128)(2,1)S(1)}, u32[]{:S(2)}, u32[]{:S(2)}) collective-permute-start(bf16[64,2176]{1,0:T(8,128)(2,1)S(1)} %collective-permute-done.3.refs_3_), channel_id=1, source_target_pairs={{0,1},{1,0},{2,3},{3,2},{4,5},{5,4},{6,7},{7,6},{8,9},{9,8},{10,11... | collective-permute-start | bytes 835592 | tf_op jit(solution)/shard_map/ppermute | solution.py:51
  29.7 5.1 %collective-permute-start.10 = (bf16[64,2176]{1,0:T(8,128)(2,1)S(1)}, bf16[64,2176]{1,0:T(8,128)(2,1)S(1)}, u32[]{:S(2)}, u32[]{:S(2)}) collective-permute-start(bf16[64,2176]{1,0:T(8,128)(2,1)S(1)} %get-tuple-element.41.refs_0_.refs_2_), channel_id=1, source_target_pairs={{0,1},{1,0},{2,3},{3,2},{4,5},{5,4},{6,7},{7,6},{8,9},{9,8},{10,11... | collective-permute-start | bytes 835592 | tf_op jit(solution)/shard_map/ppermute | solution.py:51
  30.3 4.5 %collective-permute-start.11 = (bf16[64,2176]{1,0:T(8,128)(2,1)S(1)}, bf16[64,2176]{1,0:T(8,128)(2,1)S(1)}, u32[]{:S(2)}, u32[]{:S(2)}) collective-permute-start(bf16[64,2176]{1,0:T(8,128)(2,1)S(1)} %collective-permute-done.9.refs_3_), channel_id=1, source_target_pairs={{0,1},{1,0},{2,3},{3,2},{4,5},{5,4},{6,7},{7,6},{8,9},{9,8},{10,11... | collective-permute-start | bytes 835592 | tf_op jit(solution)/shard_map/ppermute | solution.py:51
  33.0 1.7 %collective-permute-start.7 = (bf16[64,2048]{1,0:T(8,128)(2,1)S(1)}, bf16[64,2048]{1,0:T(8,128)(2,1)S(1)}, u32[]{:S(2)}, u32[]{:S(2)}) collective-permute-start(bf16[64,2048]{1,0:T(8,128)(2,1)S(1)} %get-tuple-element.48), channel_id=1, source_target_pairs={{0,1},{1,0},{2,3},{3,2},{4,5},{5,4},{6,7},{7,6},{8,9},{9,8},{10,11... | collective-permute-start | bytes 786440 | tf_op jit(solution)/shard_map/ppermute | solution.py:51
  34.8 28.6 %copy-start = (bf16[2,16,2048]{2,1,0:T(8,128)(2,1)S(1)}, bf16[2,16,2048]{2,1,0:T(8,128)(2,1)}, u32[]{:S(2)}) copy-start(bf16[2,16,2048]{2,1,0:T(8,128)(2,1)} %param.5) | copy-start | bytes 393220
  34.8 28.5 %copy-start.1 = (f32[2,2048]{1,0:T(2,128)S(1)}, f32[2,2048]{1,0:T(2,128)}, u32[]{:S(2)}) copy-start(f32[2,2048]{1,0:T(2,128)} %refs_1_.4) | copy-start | bytes 49156
  37.5 2.0 %collective-permute-start.13 = (bf16[64,2048]{1,0:T(8,128)(2,1)S(1)}, bf16[64,2048]{1,0:T(8,128)(2,1)S(1)}, u32[]{:S(2)}, u32[]{:S(2)}) collective-permute-start(bf16[64,2048]{1,0:T(8,128)(2,1)S(1)} %get-tuple-element.53), channel_id=1, source_target_pairs={{0,1},{1,0},{2,3},{3,2},{4,5},{5,4},{6,7},{7,6},{8,9},{9,8},{10,11... | collective-permute-start | bytes 786440 | tf_op jit(solution)/shard_map/ppermute | solution.py:51
  37.9 2.6 %collective-permute-start.6 = (bf16[64,2048]{1,0:T(8,128)(2,1)S(1)}, bf16[64,2048]{1,0:T(8,128)(2,1)S(1)}, u32[]{:S(2)}, u32[]{:S(2)}) collective-permute-start(bf16[64,2048]{1,0:T(8,128)(2,1)S(1)} %get-tuple-element.46), channel_id=1, source_target_pairs={{0,1},{1,0},{2,3},{3,2},{4,5},{5,4},{6,7},{7,6},{8,9},{9,8},{10,11... | collective-permute-start | bytes 786440 | tf_op jit(solution)/shard_map/ppermute | solution.py:51
  38.0 9.1 %collective-permute-start.8 = (bf16[64,2048]{1,0:T(8,128)(2,1)S(1)}, bf16[64,2048]{1,0:T(8,128)(2,1)S(1)}, u32[]{:S(2)}, u32[]{:S(2)}) collective-permute-start(bf16[64,2048]{1,0:T(8,128)(2,1)S(1)} %shard_map.59.refs_0_), channel_id=1, source_target_pairs={{0,2},{1,3},{2,0},{3,1},{4,6},{5,7},{6,4},{7,5},{8,10},{9,11},{10,... | collective-permute-start | bytes 786440 | tf_op jit(solution)/shard_map/ppermute | solution.py:51
  39.4 13.4 %collective-permute-start.12 = (bf16[64,2048]{1,0:T(8,128)(2,1)S(1)}, bf16[64,2048]{1,0:T(8,128)(2,1)S(1)}, u32[]{:S(2)}, u32[]{:S(2)}) collective-permute-start(bf16[64,2048]{1,0:T(8,128)(2,1)S(1)} %get-tuple-element.51), channel_id=1, source_target_pairs={{0,1},{1,0},{2,3},{3,2},{4,5},{5,4},{6,7},{7,6},{8,9},{9,8},{10,11... | collective-permute-start | bytes 786440 | tf_op jit(solution)/shard_map/ppermute | solution.py:51
  39.5 13.3 %collective-permute-start.14 = (bf16[64,2048]{1,0:T(8,128)(2,1)S(1)}, bf16[64,2048]{1,0:T(8,128)(2,1)S(1)}, u32[]{:S(2)}, u32[]{:S(2)}) collective-permute-start(bf16[64,2048]{1,0:T(8,128)(2,1)S(1)} %shard_map.62), channel_id=1, source_target_pairs={{0,2},{1,3},{2,0},{3,1},{4,6},{5,7},{6,4},{7,5},{8,10},{9,11},{10,... | collective-permute-start | bytes 786440 | tf_op jit(solution)/shard_map/ppermute | solution.py:51
  47.3 13.7 %collective-permute-start.16 = (bf16[32,2048]{1,0:T(8,128)(2,1)S(1)}, bf16[32,2048]{1,0:T(8,128)(2,1)S(1)}, u32[]{:S(2)}, u32[]{:S(2)}) collective-permute-start(bf16[32,2048]{1,0:T(8,128)(2,1)S(1)} %get-tuple-element.56), channel_id=1, source_target_pairs={{0,8},{1,9},{2,10},{3,11},{4,12},{5,13},{6,14},{7,15},{8,0},{9,1},... | collective-permute-start | bytes 393224 | tf_op jit(solution)/shard_map/ppermute | solution.py:51
  52.3 8.6 %collective-permute-start.17 = (bf16[32,2048]{1,0:T(8,128)(2,1)S(1)}, bf16[32,2048]{1,0:T(8,128)(2,1)S(1)}, u32[]{:S(2)}, u32[]{:S(2)}) collective-permute-start(bf16[32,2048]{1,0:T(8,128)(2,1)S(1)} %get-tuple-element.49.refs_0_), channel_id=1, source_target_pairs={{0,12},{1,13},{2,14},{3,15},{4,8},{5,9},{6,10},{7,11},{8,4},{9,5},... | collective-permute-start | bytes 393224 | tf_op jit(solution)/shard_map/ppermute | solution.py:51
  52.9 10.4 %collective-permute-start.15 = (bf16[32,2048]{1,0:T(8,128)(2,1)S(1)}, bf16[32,2048]{1,0:T(8,128)(2,1)S(1)}, u32[]{:S(2)}, u32[]{:S(2)}) collective-permute-start(bf16[32,2048]{1,0:T(8,128)(2,1)S(1)} %get-tuple-element.55), channel_id=1, source_target_pairs={{0,4},{1,5},{2,6},{3,7},{4,0},{5,1},{6,2},{7,3},{8,12},{9,13},{10,... | collective-permute-start | bytes 393224 | tf_op jit(solution)/shard_map/ppermute | solution.py:51
  63.5 12.1 %collective-permute-start.18 = (bf16[32,2048]{1,0:T(8,128)(2,1)S(1)}, bf16[32,2048]{1,0:T(8,128)(2,1)S(1)}, u32[]{:S(2)}, u32[]{:S(2)}) collective-permute-start(bf16[32,2048]{1,0:T(8,128)(2,1)S(1)} %get-tuple-element.58.refs_2_), channel_id=1, source_target_pairs={{0,8},{1,9},{2,10},{3,11},{4,12},{5,13},{6,14},{7,15},{8,0},{9,1},... | collective-permute-start | bytes 393224 | tf_op jit(solution)/shard_map/ppermute | solution.py:51
  64.1 11.5 %collective-permute-start.19 = (bf16[32,2048]{1,0:T(8,128)(2,1)S(1)}, bf16[32,2048]{1,0:T(8,128)(2,1)S(1)}, u32[]{:S(2)}, u32[]{:S(2)}) collective-permute-start(bf16[32,2048]{1,0:T(8,128)(2,1)S(1)} %get-tuple-element.58.refs_2_), channel_id=1, source_target_pairs={{0,12},{1,13},{2,14},{3,15},{4,8},{5,9},{6,10},{7,11},{8,4},{9,5},... | collective-permute-start | bytes 393224 | tf_op jit(solution)/shard_map/ppermute | solution.py:51
  66.7 10.1 %collective-permute-start.20 = (bf16[32,2048]{1,0:T(8,128)(2,1)S(1)}, bf16[32,2048]{1,0:T(8,128)(2,1)S(1)}, u32[]{:S(2)}, u32[]{:S(2)}) collective-permute-start(bf16[32,2048]{1,0:T(8,128)(2,1)S(1)} %get-tuple-element.58.refs_2_), channel_id=1, source_target_pairs={{0,4},{1,5},{2,6},{3,7},{4,0},{5,1},{6,2},{7,3},{8,12},{9,13},{10,... | collective-permute-start | bytes 393224 | tf_op jit(solution)/shard_map/ppermute | solution.py:51
  76.8 7.3 %collective-permute-start.21 = (bf16[64,2048]{1,0:T(8,128)(2,1)S(1)}, bf16[64,2048]{1,0:T(8,128)(2,1)S(1)}, u32[]{:S(2)}, u32[]{:S(2)}) collective-permute-start(bf16[64,2048]{1,0:T(8,128)(2,1)S(1)} %get-tuple-element.60.refs_2_), channel_id=1, source_target_pairs={{0,2},{1,3},{2,0},{3,1},{4,6},{5,7},{6,4},{7,5},{8,10},{9,11},{10,... | collective-permute-start | bytes 786440 | tf_op jit(solution)/shard_map/ppermute | solution.py:51
  78.4 11.0 %collective-permute-start.22 = (bf16[64,2048]{1,0:T(8,128)(2,1)S(1)}, bf16[64,2048]{1,0:T(8,128)(2,1)S(1)}, u32[]{:S(2)}, u32[]{:S(2)}) collective-permute-start(bf16[64,2048]{1,0:T(8,128)(2,1)S(1)} %get-tuple-element.60.refs_2_), channel_id=1, source_target_pairs={{0,1},{1,0},{2,3},{3,2},{4,5},{5,4},{6,7},{7,6},{8,9},{9,8},{10,11... | collective-permute-start | bytes 786440 | tf_op jit(solution)/shard_map/ppermute | solution.py:51
  84.1 5.3 %collective-permute-start.23 = (bf16[64,2048]{1,0:T(8,128)(2,1)S(1)}, bf16[64,2048]{1,0:T(8,128)(2,1)S(1)}, u32[]{:S(2)}, u32[]{:S(2)}) collective-permute-start(bf16[64,2048]{1,0:T(8,128)(2,1)S(1)} %collective-permute-done.21.refs_3_), channel_id=1, source_target_pairs={{0,1},{1,0},{2,3},{3,2},{4,5},{5,4},{6,7},{7,6},{8,9},{9,8},{10,11... | collective-permute-start | bytes 786440 | tf_op jit(solution)/shard_map/ppermute | solution.py:51
  84.1 8.7 %collective-permute-start.27 = (bf16[64,2048]{1,0:T(8,128)(2,1)S(1)}, bf16[64,2048]{1,0:T(8,128)(2,1)S(1)}, u32[]{:S(2)}, u32[]{:S(2)}) collective-permute-start(bf16[64,2048]{1,0:T(8,128)(2,1)S(1)} %get-tuple-element.59.refs_0_.refs_2_), channel_id=1, source_target_pairs={{0,2},{1,3},{2,0},{3,1},{4,6},{5,7},{6,4},{7,5},{8,10},{9,11},{10,... | collective-permute-start | bytes 786440 | tf_op jit(solution)/shard_map/ppermute | solution.py:51
  92.1 1.6 %collective-permute-start.25 = (bf16[64,2048]{1,0:T(8,128)(2,1)S(1)}, bf16[64,2048]{1,0:T(8,128)(2,1)S(1)}, u32[]{:S(2)}, u32[]{:S(2)}) collective-permute-start(bf16[64,2048]{1,0:T(8,128)(2,1)S(1)} %get-tuple-element.67), channel_id=1, source_target_pairs={{0,1},{1,0},{2,3},{3,2},{4,5},{5,4},{6,7},{7,6},{8,9},{9,8},{10,11... | collective-permute-start | bytes 786440 | tf_op jit(solution)/shard_map/ppermute | solution.py:51
  92.4 1.7 %collective-permute-start.28 = (bf16[64,2048]{1,0:T(8,128)(2,1)S(1)}, bf16[64,2048]{1,0:T(8,128)(2,1)S(1)}, u32[]{:S(2)}, u32[]{:S(2)}) collective-permute-start(bf16[64,2048]{1,0:T(8,128)(2,1)S(1)} %get-tuple-element.59.refs_0_.refs_2_), channel_id=1, source_target_pairs={{0,1},{1,0},{2,3},{3,2},{4,5},{5,4},{6,7},{7,6},{8,9},{9,8},{10,11... | collective-permute-start | bytes 786440 | tf_op jit(solution)/shard_map/ppermute | solution.py:51
  92.8 1.6 %collective-permute-start.29 = (bf16[64,2048]{1,0:T(8,128)(2,1)S(1)}, bf16[64,2048]{1,0:T(8,128)(2,1)S(1)}, u32[]{:S(2)}, u32[]{:S(2)}) collective-permute-start(bf16[64,2048]{1,0:T(8,128)(2,1)S(1)} %collective-permute-done.27.refs_3_), channel_id=1, source_target_pairs={{0,1},{1,0},{2,3},{3,2},{4,5},{5,4},{6,7},{7,6},{8,9},{9,8},{10,11... | collective-permute-start | bytes 786440 | tf_op jit(solution)/shard_map/ppermute | solution.py:51
  97.1 2.0 %collective-permute-start.31 = (bf16[64,2048]{1,0:T(8,128)(2,1)S(1)}, bf16[64,2048]{1,0:T(8,128)(2,1)S(1)}, u32[]{:S(2)}, u32[]{:S(2)}) collective-permute-start(bf16[64,2048]{1,0:T(8,128)(2,1)S(1)} %get-tuple-element.73), channel_id=1, source_target_pairs={{0,1},{1,0},{2,3},{3,2},{4,5},{5,4},{6,7},{7,6},{8,9},{9,8},{10,11... | collective-permute-start | bytes 786440 | tf_op jit(solution)/shard_map/ppermute | solution.py:51
  97.4 2.9 %collective-permute-start.24 = (bf16[64,2048]{1,0:T(8,128)(2,1)S(1)}, bf16[64,2048]{1,0:T(8,128)(2,1)S(1)}, u32[]{:S(2)}, u32[]{:S(2)}) collective-permute-start(bf16[64,2048]{1,0:T(8,128)(2,1)S(1)} %get-tuple-element.65), channel_id=1, source_target_pairs={{0,1},{1,0},{2,3},{3,2},{4,5},{5,4},{6,7},{7,6},{8,9},{9,8},{10,11... | collective-permute-start | bytes 786440 | tf_op jit(solution)/shard_map/ppermute | solution.py:51
  97.7 9.1 %collective-permute-start.26 = (bf16[64,2048]{1,0:T(8,128)(2,1)S(1)}, bf16[64,2048]{1,0:T(8,128)(2,1)S(1)}, u32[]{:S(2)}, u32[]{:S(2)}) collective-permute-start(bf16[64,2048]{1,0:T(8,128)(2,1)S(1)} %shard_map.68.refs_0_), channel_id=1, source_target_pairs={{0,2},{1,3},{2,0},{3,1},{4,6},{5,7},{6,4},{7,5},{8,10},{9,11},{10,... | collective-permute-start | bytes 786440 | tf_op jit(solution)/shard_map/ppermute | solution.py:51
  99.1 13.1 %collective-permute-start.30 = (bf16[64,2048]{1,0:T(8,128)(2,1)S(1)}, bf16[64,2048]{1,0:T(8,128)(2,1)S(1)}, u32[]{:S(2)}, u32[]{:S(2)}) collective-permute-start(bf16[64,2048]{1,0:T(8,128)(2,1)S(1)} %get-tuple-element.71), channel_id=1, source_target_pairs={{0,1},{1,0},{2,3},{3,2},{4,5},{5,4},{6,7},{7,6},{8,9},{9,8},{10,11... | collective-permute-start | bytes 786440 | tf_op jit(solution)/shard_map/ppermute | solution.py:51
  99.2 13.1 %collective-permute-start.32 = (bf16[64,2048]{1,0:T(8,128)(2,1)S(1)}, bf16[64,2048]{1,0:T(8,128)(2,1)S(1)}, u32[]{:S(2)}, u32[]{:S(2)}) collective-permute-start(bf16[64,2048]{1,0:T(8,128)(2,1)S(1)} %shard_map.71), channel_id=1, source_target_pairs={{0,2},{1,3},{2,0},{3,1},{4,6},{5,7},{6,4},{7,5},{8,10},{9,11},{10,... | collective-permute-start | bytes 786440 | tf_op jit(solution)/shard_map/ppermute | solution.py:51
  106.9 12.3 %collective-permute-start.34 = (bf16[32,2048]{1,0:T(8,128)(2,1)S(1)}, bf16[32,2048]{1,0:T(8,128)(2,1)S(1)}, u32[]{:S(2)}, u32[]{:S(2)}) collective-permute-start(bf16[32,2048]{1,0:T(8,128)(2,1)S(1)} %get-tuple-element.76), channel_id=1, source_target_pairs={{0,8},{1,9},{2,10},{3,11},{4,12},{5,13},{6,14},{7,15},{8,0},{9,1},... | collective-permute-start | bytes 393224 | tf_op jit(solution)/shard_map/ppermute | solution.py:51
  108.9 10.3 %collective-permute-start.35 = (bf16[32,2048]{1,0:T(8,128)(2,1)S(1)}, bf16[32,2048]{1,0:T(8,128)(2,1)S(1)}, u32[]{:S(2)}, u32[]{:S(2)}) collective-permute-start(bf16[32,2048]{1,0:T(8,128)(2,1)S(1)} %get-tuple-element.68.refs_0_), channel_id=1, source_target_pairs={{0,12},{1,13},{2,14},{3,15},{4,8},{5,9},{6,10},{7,11},{8,4},{9,5},... | collective-permute-start | bytes 393224 | tf_op jit(solution)/shard_map/ppermute | solution.py:51
  112.4 8.2 %collective-permute-start.33 = (bf16[32,2048]{1,0:T(8,128)(2,1)S(1)}, bf16[32,2048]{1,0:T(8,128)(2,1)S(1)}, u32[]{:S(2)}, u32[]{:S(2)}) collective-permute-start(bf16[32,2048]{1,0:T(8,128)(2,1)S(1)} %get-tuple-element.75), channel_id=1, source_target_pairs={{0,4},{1,5},{2,6},{3,7},{4,0},{5,1},{6,2},{7,3},{8,12},{9,13},{10,... | collective-permute-start | bytes 393224 | tf_op jit(solution)/shard_map/ppermute | solution.py:51

commit v4 on v3

--- a/solution.py
+++ b/solution.py
@@ -22,9 +22,8 @@
     return lax.ppermute(value, axis, [(source, source + steps) for source in range(initial, last)])
 
 
-def call(kernel, outs, specs, *operands, scratch=(), limit=8, flops=0, after=()):
+def call(kernel, outs, specs, *operands, scratch=(), limit=8, after=()):
     shapes = tuple(jax.ShapeDtypeStruct(shape, dtype) for shape, dtype in outs)
-    moved = sum(x.size * x.dtype.itemsize for x in operands + shapes)
     operands = (*after, *operands)
     return pl.pallas_call(
         lambda *refs: kernel(*refs[len(after) :]),
@@ -33,7 +32,7 @@
         out_specs=(VMEM,) * len(outs),
         scratch_shapes=scratch,
         compiler_params=pltpu.CompilerParams(vmem_limit_bytes=limit * MIB),
-        cost_estimate=pl.CostEstimate(flops=flops, bytes_accessed=moved, transcendentals=0),
+        cost_estimate=pl.CostEstimate(flops=0, bytes_accessed=0, transcendentals=0),
     )(*operands)
 
 
@@ -58,7 +57,7 @@
         wholes[k // size][k % size * rows : (k % size + 1) * rows] = part[...]
 
 
-def gather_rows(rows):
+def gather_rows(rows, after):
     far = lax.axis_size("expert") // 4
     tokens, width = rows.shape
     parts = [rows] + [swap(rows, 4, k, far) for k in range(1, far)]
@@ -70,6 +69,7 @@
         [VMEM] * far,
         *parts[far // 2 :],
         *parts[: far // 2],
+        after=after,
     ):
         beside = swap(near, 2, 1, 2)
         batches.append([near, beside, swap(near, 1, 1, 2), swap(beside, 1, 1, 2)])
@@ -87,21 +87,21 @@
         piece[...] = total[k * rows : (k + 1) * rows].astype(piece.dtype)
 
 
-def leave_pair(found):
-    mine_near, mine_beside, other_near, other_beside = found
-    arrived_beside = swap(other_beside, 1, 1, 2, True)
-    arrived_near = swap(other_near, 1, 1, 2, True)
-    (leaving,) = call(
-        sum_kernel, [(mine_beside.shape, bf16)], [VMEM] * 2, mine_beside, arrived_beside
-    )
-    return mine_near, arrived_near, leaving
-
-
 def return_rows(batches, tokens):
     far = lax.axis_size("expert") // 4
     returned, steps, earlier = {}, [range(far // 2, far), range(far // 2)], ()
-    for (mine_near, arrived_near, leaving), distances in zip(batches, steps):
+    for (mine_near, mine_beside, other_near, other_beside), distances in zip(batches, steps):
         shape = mine_near.shape
+        arrived_beside = swap(other_beside, 1, 1, 2, True)
+        arrived_near = swap(other_near, 1, 1, 2, True)
+        (leaving,) = call(
+            sum_kernel,
+            [(shape, bf16)],
+            [VMEM] * 2,
+            mine_beside,
+            arrived_beside,
+            after=earlier,
+        )
         beside = swap(leaving, 2, 1, 2, True)
         pieces = call(
             split_kernel,
@@ -110,7 +110,6 @@
             mine_near,
             arrived_near,
             beside,
-            after=earlier,
         )
         earlier = (pieces[-1],)
         for k, piece in zip(distances, pieces):
@@ -176,7 +175,8 @@
             outs_ref[layer_no, batch] = done[layer_no][batch * tokens : (batch + 1) * tokens]
 
 
-def load_kernel(layer_no, cuts, gate_up_hbm, down_hbm, gate_up_ref, down_ref, sems):
+def load_kernel(layer_no, cuts, gate_up_hbm, down_hbm, gate_up_ref, down_ref, token, sems):
+    token[...] = jnp.zeros_like(token)
     copies = []
     for source, target in ((gate_up_hbm, gate_up_ref), (down_hbm, down_ref)):
         rows = target.shape[0] // cuts
@@ -193,16 +193,17 @@
         copy.wait()
 
 
-def load_weights(layer_no, w_gate_up, w_down):
+def load_weights(layer_no, w_gate_up, w_down, after=()):
     cuts = 4
     return call(
         functools.partial(load_kernel, layer_no, cuts),
-        [(w_gate_up.shape[2:], bf16), (w_down.shape[2:], bf16)],
+        [(w_gate_up.shape[2:], bf16), (w_down.shape[2:], bf16), ((8, LANES), f32)],
         [ANY] * 2,
         in_hbm(w_gate_up),
         in_hbm(w_down),
         scratch=[pltpu.SemaphoreType.DMA((2 * cuts,))],
         limit=12,
+        after=after,
     )
 
 
@@ -247,7 +248,7 @@
 
 
 def run_expert(parts, routed, me, first_column, weights, after):
-    gate_up, down_proj = weights
+    gate_up, down_proj, _ = weights
     hidden_size, features = down_proj.shape
     quarter, width = parts[0].shape
     count = 4 * quarter
@@ -267,7 +268,6 @@
         scratch=[pltpu.VMEM((count, features), bf16), pltpu.VMEM((count, hidden_size), bf16)],
         limit=24,
         after=after,
-        flops=6 * count * features * hidden_size,
     )
     return found[:4], found[4] if wide else routed
 
@@ -299,21 +299,21 @@
     return wide
 
 
-def run_layer(rows, routed, me, first_column, weights):
+def run_layer(rows, routed, me, first_column, weights, loaded=()):
     found, columns = [], []
-    batches = gather_rows(rows)
-    after = (batches[-1][0],)
+    batches = gather_rows(rows, loaded)
+    after = ()
     for place, parts in enumerate(batches):
         outs, kept = run_expert(
             parts, None if routed is None else routed[place], me, first_column, weights, after
         )
-        found.append(leave_pair(outs))
-        after = (found[-1][2],)
+        after = (outs[0],)
+        found.append(outs)
         columns.append(kept)
-    return return_rows(found, rows.shape[0]), columns
-
-
-def close_rows(layer_no, current, gain, returned):
+    return return_rows(found, rows.shape[0]), columns, after
+
+
+def close_rows(layer_no, current, gain, returned, after=()):
     return call(
         functools.partial(close_kernel, layer_no),
         [(current.shape, bf16)] * 2,
@@ -321,6 +321,7 @@
         current,
         gain,
         *returned,
+        after=after,
     )
 
 
@@ -330,13 +331,15 @@
     me = lax.axis_index("expert").astype(jnp.int32).reshape(1)
     batches, tokens, features = inputs.shape
     layers = routes.shape[0]
-    weights = [load_weights(layer_no, w_gate_up, w_down) for layer_no in range(layers)]
+    weights = load_weights(0, w_gate_up, w_down)
     if sections == 1:
         outs, routed = [], None
         current = inputs.reshape(batches * tokens, features)
         rows = open_rows(inputs, routes, norm_gain, experts)
         for layer_no in range(layers):
-            returned, routed = run_layer(rows, routed, me, layer_no * experts, weights[layer_no])
+            returned, routed, worked = run_layer(
+                rows, routed, me, layer_no * experts, weights, weights[2:]
+            )
             if layer_no == layers - 1:
                 (whole,) = call(
                     functools.partial(end_kernel, len(outs)),
@@ -347,7 +350,8 @@
                     *outs,
                 )
                 return whole
-            current, rows = close_rows(layer_no + 1, current, norm_gain, returned)
+            weights = load_weights(layer_no + 1, w_gate_up, w_down, worked)
+            current, rows = close_rows(layer_no + 1, current, norm_gain, returned, weights[2:])
             outs.append(current)
     segment_no = lax.axis_index("section")
     handed = jnp.zeros((tokens, features), bf16)
@@ -361,7 +365,7 @@
         batch_pick = jnp.clip(turn_no - segment_no, 0, batches - 1)
         turn_routes = lax.dynamic_slice_in_dim(routes, batch_pick, 1, 1)
         rows = open_rows(current[None], turn_routes, norm_gain, experts)
-        returned, _ = run_layer(rows, None, me, 0, weights[0])
+        returned, _, _ = run_layer(rows, None, me, 0, weights)
         result, _ = close_rows(0, current, norm_gain, returned)
         finished.append(result)
         if turn_no < batches:

time: 122 us -> 126 us (1.033)
  local copies, waits for them, and re-layouts: 0.01 us -> 5.46 us
  waiting for transfers between devices: 61.9 us -> 57.1 us
  Pallas kernels: 21 us -> 24 us
    unnamed x4 -> x8, local copies, waits for them, and re-layouts: 0.01 us -> 5.46 us
    ppermute x36, waiting for transfers between devices: 61.9 us -> 57.1 us  [swap(): lax.ppermute(value, 'expert', [(i, partner(i)) for i in range(count)])]
    pallas_call x19, Pallas kernels: 21 us -> 24 us  [call(): pl.pallas_call(lambda *refs: kernel(*refs[len(after):]), out_shape=shapes...]
  transfers between devices with their start and end apart: 36 -> 36, of which waited for: 17 -> 15; matrix products, arithmetic and copies ran while one was open for 0% -> 0% of each run, Pallas kernels for 11% -> 17%
where the time goes in v4:
time: 126 us; the launch traced here: 125 us
  waiting for transfers between devices  57.1 us (45%)
  starting transfers between devices  38.7 us (31%)
  Pallas kernels  24 us (19%)
  local copies, waits for them, and re-layouts  5.46 us (4%)
    ppermute x36, waiting for transfers between devices, swap(): lax.ppermute(value, 'expert', [(i, partner(i)) for i in range(count)])  57.1 us
    ppermute x36, starting transfers between devices, swap(): lax.ppermute(value, 'expert', [(i, partner(i)) for i in range(count)])  38.7 us
    pallas_call x19, Pallas kernels, call(): pl.pallas_call(lambda *refs: kernel(*refs[len(after):]), out_shape=shapes...  24 us
    unnamed x8, local copies, waits for them, and re-layouts  5.46 us
  transfers between devices with their start and end apart: 36, of which 15 were waited for; matrix products, arithmetic and copies ran while one was open for 0% of the time, Pallas kernels for 17%

profile of v4, /device:TPU:0, one launch (start us, length us, event | category | flops | bytes accessed | tf_op | source)
XLA Modules:
  0.0 125.5 jit_solution(9050785924639216909)
XLA Ops:
  0.0 1.2 shard_map.56.refs_3_
  1.2 4.1 %collective-permute-start = (bf16[32,2176]{1,0:T(8,128)(2,1)S(1)}, bf16[32,2176]{1,0:T(8,128)(2,1)S(1)}, u32[]{:S(2)}, u32[]{:S(2)}) collective-permute-start(bf16[32,2176]{1,0:T(8,128)(2,1)S(1)} %shard_map.56.refs_3_), channel_id=1, source_target_pairs={{0,8},{1,9},{2,10},{3,11},{4,12},{5,13},{6,14},{7,15},{8,0},{9,1},... | collective-permute-start | bytes 417800 | tf_op jit(solution)/shard_map/ppermute | solution.py:50
  5.3 1.3 %collective-permute-start.1 = (bf16[32,2176]{1,0:T(8,128)(2,1)S(1)}, bf16[32,2176]{1,0:T(8,128)(2,1)S(1)}, u32[]{:S(2)}, u32[]{:S(2)}) collective-permute-start(bf16[32,2176]{1,0:T(8,128)(2,1)S(1)} %shard_map.56.refs_3_), channel_id=1, source_target_pairs={{0,12},{1,13},{2,14},{3,15},{4,8},{5,9},{6,10},{7,11},{8,4},{9,5},... | collective-permute-start | bytes 417800 | tf_op jit(solution)/shard_map/ppermute | solution.py:50
  6.9 3.7 %shard_map.55 = (bf16[2048,1536]{1,0:T(8,128)(2,1)S(1)}, bf16[768,2048]{1,0:T(8,128)(2,1)S(1)}, f32[8,128]{1,0:T(8,128)S(1)}) custom-call(bf16[2,1,2048,1536]{3,2,1,0:T(8,128)(2,1)} %refs_1_.3, bf16[2,1,768,2048]{3,2,1,0:T(8,128)(2,1)} %refs_2_.4), custom_call_target="tpu_custom_call" | custom-call | tf_op jit(solution)/shard_map/pallas_call | solution.py:28
  10.7 2.7 %copy-done = bf16[2048,1536]{1,0:T(8,128)(2,1)} copy-done((bf16[2048,1536]{1,0:T(8,128)(2,1)}, bf16[2048,1536]{1,0:T(8,128)(2,1)S(1)}, u32[]{:S(2)}) %copy-start) | copy-done | bytes 6291480
  13.3 2.5 %collective-permute-done.refs_1_ = bf16[32,2176]{1,0:T(8,128)(2,1)S(1)} collective-permute-done((bf16[32,2176]{1,0:T(8,128)(2,1)S(1)}, bf16[32,2176]{1,0:T(8,128)(2,1)S(1)}, u32[]{:S(2)}, u32[]{:S(2)}) %collective-permute-start) | collective-permute-done | bytes 139296 | tf_op jit(solution)/shard_map/ppermute | solution.py:50
  15.8 0.5 collective-permute-done.2.refs_4_
  16.4 0.7 shard_map.57
  17.1 1.6 %collective-permute-start.3 = (bf16[64,2176]{1,0:T(8,128)(2,1)}, bf16[64,2176]{1,0:T(8,128)(2,1)}, u32[]{:S(2)}, u32[]{:S(2)}) collective-permute-start(bf16[64,2176]{1,0:T(8,128)(2,1)} %get-tuple-element.44.refs_1_), channel_id=1, source_target_pairs={{0,2},{1,3},{2,0},{3,1},{4,6},{5,7},{6,4},{7,5},{8,10},{9,11},{10,... | collective-permute-start | bytes 835592 | tf_op jit(solution)/shard_map/ppermute | solution.py:50
  18.7 0.5 collective-permute-start.6
  19.1 7.8 %collective-permute-done.3.refs_2_ = bf16[64,2176]{1,0:T(8,128)(2,1)} collective-permute-done((bf16[64,2176]{1,0:T(8,128)(2,1)}, bf16[64,2176]{1,0:T(8,128)(2,1)}, u32[]{:S(2)}, u32[]{:S(2)}) %collective-permute-start.3) | collective-permute-done | bytes 278560 | tf_op jit(solution)/shard_map/ppermute | solution.py:50
  26.9 0.5 collective-permute-start.7
  27.4 2.5 %collective-permute-done.6.refs_3_ = bf16[64,2176]{1,0:T(8,128)(2,1)} collective-permute-done((bf16[64,2176]{1,0:T(8,128)(2,1)S(1)}, bf16[64,2176]{1,0:T(8,128)(2,1)}, u32[]{:S(2)}, u32[]{:S(2)}) %collective-permute-start.6) | collective-permute-done | bytes 278560 | tf_op jit(solution)/shard_map/ppermute | solution.py:50
  29.9 2.8 %copy-done.1 = bf16[2048,1536]{1,0:T(8,128)(2,1)S(1)} copy-done((bf16[2048,1536]{1,0:T(8,128)(2,1)S(1)}, bf16[2048,1536]{1,0:T(8,128)(2,1)}, u32[]{:S(2)}) %copy-start.1) | copy-done | bytes 6291480
  32.7 3.8 %shard_map.58 = (f32[64,2048]{1,0:T(8,128)S(1)}, f32[64,2048]{1,0:T(8,128)S(1)}, bf16[64,2048]{1,0:T(8,128)(2,1)S(1)}, bf16[64,2048]{1,0:T(8,128)(2,1)S(1)}, bf16[256,128]{1,0:T(8,128)(2,1)S(1)}) custom-call(s32[1]{0:T(128)} %bitcast.refs_0_.refs_1_, bf16[64,2176]{1,0:T(8,128)(2,1)} %get-tuple-element.44.refs_1_, ...), custom_call_target="tpu_custom_call" | custom-call | tf_op jit(solution)/shard_map/pallas_call | solution.py:28
  36.5 0.6 collective-permute-start.11
  37.2 3.7 %shard_map.59 = (f32[64,2048]{1,0:T(8,128)S(1)}, f32[64,2048]{1,0:T(8,128)S(1)}, bf16[64,2048]{1,0:T(8,128)(2,1)S(1)}, bf16[64,2048]{1,0:T(8,128)(2,1)S(1)}, bf16[256,128]{1,0:T(8,128)(2,1)S(1)}) custom-call(f32[64,2048]{1,0:T(8,128)S(1)} %get-tuple-element.47.refs_0_, s32[1]{0:T(128)} %bitcast.refs_0_.refs_1_, ...), custom_call_target="tpu_custom_call" | custom-call | tf_op jit(solution)/shard_map/pallas_call | solution.py:28
  41.0 1.4 %collective-permute-start.12 = (bf16[64,2048]{1,0:T(8,128)(2,1)S(1)}, bf16[64,2048]{1,0:T(8,128)(2,1)S(1)}, u32[]{:S(2)}, u32[]{:S(2)}) collective-permute-start(bf16[64,2048]{1,0:T(8,128)(2,1)S(1)} %shard_map.61), channel_id=1, source_target_pairs={{0,2},{1,3},{2,0},{3,1},{4,6},{5,7},{6,4},{7,5},{8,10},{9,11},{10,... | collective-permute-start | bytes 786440 | tf_op jit(solution)/shard_map/ppermute | solution.py:50
  42.9 6.8 %collective-permute-done.12.refs_2_ = bf16[64,2048]{1,0:T(8,128)(2,1)S(1)} collective-permute-done((bf16[64,2048]{1,0:T(8,128)(2,1)S(1)}, bf16[64,2048]{1,0:T(8,128)(2,1)S(1)}, u32[]{:S(2)}, u32[]{:S(2)}) %collective-permute-start.12) | collective-permute-done | bytes 262176 | tf_op jit(solution)/shard_map/ppermute | solution.py:50
  49.9 1.4 %collective-permute-start.14 = (bf16[64,2048]{1,0:T(8,128)(2,1)S(1)}, bf16[64,2048]{1,0:T(8,128)(2,1)S(1)}, u32[]{:S(2)}, u32[]{:S(2)}) collective-permute-start(bf16[64,2048]{1,0:T(8,128)(2,1)S(1)} %shard_map.63), channel_id=1, source_target_pairs={{0,2},{1,3},{2,0},{3,1},{4,6},{5,7},{6,4},{7,5},{8,10},{9,11},{10,... | collective-permute-start | bytes 786440 | tf_op jit(solution)/shard_map/ppermute | solution.py:50
  51.3 4.7 %collective-permute-start.17 = (bf16[32,2048]{1,0:T(8,128)(2,1)S(1)}, bf16[32,2048]{1,0:T(8,128)(2,1)S(1)}, u32[]{:S(2)}, u32[]{:S(2)}) collective-permute-start(bf16[32,2048]{1,0:T(8,128)(2,1)S(1)} %get-tuple-element.55.refs_0_), channel_id=1, source_target_pairs={{0,12},{1,13},{2,14},{3,15},{4,8},{5,9},{6,10},{7,11},{8,4},{9,5},... | collective-permute-start | bytes 393224 | tf_op jit(solution)/shard_map/ppermute | solution.py:50
  56.0 1.8 %collective-permute-start.16 = (bf16[32,2048]{1,0:T(8,128)(2,1)S(1)}, bf16[32,2048]{1,0:T(8,128)(2,1)S(1)}, u32[]{:S(2)}, u32[]{:S(2)}) collective-permute-start(bf16[32,2048]{1,0:T(8,128)(2,1)S(1)} %get-tuple-element.60), channel_id=1, source_target_pairs={{0,8},{1,9},{2,10},{3,11},{4,12},{5,13},{6,14},{7,15},{8,0},{9,1},... | collective-permute-start | bytes 393224 | tf_op jit(solution)/shard_map/ppermute | solution.py:50
  58.0 4.5 %collective-permute-start.15 = (bf16[32,2048]{1,0:T(8,128)(2,1)S(1)}, bf16[32,2048]{1,0:T(8,128)(2,1)S(1)}, u32[]{:S(2)}, u32[]{:S(2)}) collective-permute-start(bf16[32,2048]{1,0:T(8,128)(2,1)S(1)} %get-tuple-element.59), channel_id=1, source_target_pairs={{0,4},{1,5},{2,6},{3,7},{4,0},{5,1},{6,2},{7,3},{8,12},{9,13},{10,... | collective-permute-start | bytes 393224 | tf_op jit(solution)/shard_map/ppermute | solution.py:50
  62.4 3.7 %shard_map.60 = (bf16[2048,1536]{1,0:T(8,128)(2,1)S(1)}, bf16[768,2048]{1,0:T(8,128)(2,1)S(1)}, f32[8,128]{1,0:T(8,128)S(1)}) custom-call(f32[64,2048]{1,0:T(8,128)S(1)} %get-tuple-element.49.refs_0_, bf16[2,1,2048,1536]{3,2,1,0:T(8,128)(2,1)} %refs_1_.3, bf16[2,1,768,2048]{3,2,1,0:T(8,128)(2,1)} %refs_2_.4), custom_call_target="tpu_custom_call" | custom-call | tf_op jit(solution)/shard_map/pallas_call | solution.py:28
  66.2 1.4 %collective-permute-done.16.refs_5_ = bf16[32,2048]{1,0:T(8,128)(2,1)S(1)} collective-permute-done((bf16[32,2048]{1,0:T(8,128)(2,1)S(1)}, bf16[32,2048]{1,0:T(8,128)(2,1)S(1)}, u32[]{:S(2)}, u32[]{:S(2)}) %collective-permute-start.16) | collective-permute-done | bytes 131104 | tf_op jit(solution)/shard_map/ppermute | solution.py:50
  67.6 0.6 collective-permute-done.15.refs_4_
  68.4 1.6 %collective-permute-start.18 = (bf16[32,2048]{1,0:T(8,128)(2,1)S(1)}, bf16[32,2048]{1,0:T(8,128)(2,1)S(1)}, u32[]{:S(2)}, u32[]{:S(2)}) collective-permute-start(bf16[32,2048]{1,0:T(8,128)(2,1)S(1)} %get-tuple-element.62.refs_3_), channel_id=1, source_target_pairs={{0,8},{1,9},{2,10},{3,11},{4,12},{5,13},{6,14},{7,15},{8,0},{9,1},... | collective-permute-start | bytes 393224 | tf_op jit(solution)/shard_map/ppermute | solution.py:50
  70.0 2.0 %collective-permute-start.19 = (bf16[32,2048]{1,0:T(8,128)(2,1)S(1)}, bf16[32,2048]{1,0:T(8,128)(2,1)S(1)}, u32[]{:S(2)}, u32[]{:S(2)}) collective-permute-start(bf16[32,2048]{1,0:T(8,128)(2,1)S(1)} %get-tuple-element.62.refs_3_), channel_id=1, source_target_pairs={{0,12},{1,13},{2,14},{3,15},{4,8},{5,9},{6,10},{7,11},{8,4},{9,5},... | collective-permute-start | bytes 393224 | tf_op jit(solution)/shard_map/ppermute | solution.py:50
  71.9 0.5 collective-permute-start.20
  72.4 8.3 %collective-permute-done.18.refs_1_ = bf16[32,2048]{1,0:T(8,128)(2,1)S(1)} collective-permute-done((bf16[32,2048]{1,0:T(8,128)(2,1)S(1)}, bf16[32,2048]{1,0:T(8,128)(2,1)S(1)}, u32[]{:S(2)}, u32[]{:S(2)}) %collective-permute-start.18) | collective-permute-done | bytes 131104 | tf_op jit(solution)/shard_map/ppermute | solution.py:50
  81.0 0.5 collective-permute-start.21
  81.5 1.6 %collective-permute-start.24 = (bf16[64,2048]{1,0:T(8,128)(2,1)S(1)}, bf16[64,2048]{1,0:T(8,128)(2,1)S(1)}, u32[]{:S(2)}, u32[]{:S(2)}) collective-permute-start(bf16[64,2048]{1,0:T(8,128)(2,1)S(1)} %get-tuple-element.68.refs_2_), channel_id=1, source_target_pairs={{0,2},{1,3},{2,0},{3,1},{4,6},{5,7},{6,4},{7,5},{8,10},{9,11},{10,... | collective-permute-start | bytes 786440 | tf_op jit(solution)/shard_map/ppermute | solution.py:50
  83.1 7.2 %collective-permute-done.21.refs_2_ = bf16[64,2048]{1,0:T(8,128)(2,1)S(1)} collective-permute-done((bf16[64,2048]{1,0:T(8,128)(2,1)S(1)}, bf16[64,2048]{1,0:T(8,128)(2,1)S(1)}, u32[]{:S(2)}, u32[]{:S(2)}) %collective-permute-start.21) | collective-permute-done | bytes 262176 | tf_op jit(solution)/shard_map/ppermute | solution.py:50
  90.3 0.5 collective-permute-start.25
  90.8 2.4 %collective-permute-done.24.refs_3_ = bf16[64,2048]{1,0:T(8,128)(2,1)S(1)} collective-permute-done((bf16[64,2048]{1,0:T(8,128)(2,1)S(1)}, bf16[64,2048]{1,0:T(8,128)(2,1)S(1)}, u32[]{:S(2)}, u32[]{:S(2)}) %collective-permute-start.24) | collective-permute-done | bytes 262176 | tf_op jit(solution)/shard_map/ppermute | solution.py:50
  93.2 2.7 %shard_map.67 = (f32[64,2048]{1,0:T(8,128)S(1)}, f32[64,2048]{1,0:T(8,128)S(1)}, bf16[64,2048]{1,0:T(8,128)(2,1)S(1)}, bf16[64,2048]{1,0:T(8,128)(2,1)S(1)}) custom-call(s32[1]{0:T(128)} %bitcast.refs_0_.refs_1_, bf16[64,2048]{1,0:T(8,128)(2,1)S(1)} %get-tuple-element.63.refs_1_, bf16[64,2048]{1,0:T(8,128)(2,1)S(1)} %collective-permute-done.21.refs_2_, ...), custom_call_target="tpu_custom_call" | custom-call | tf_op jit(solution)/shard_map/pallas_call | solution.py:28
  95.9 0.6 collective-permute-start.29
  96.5 2.7 %shard_map.68 = (f32[64,2048]{1,0:T(8,128)S(1)}, f32[64,2048]{1,0:T(8,128)S(1)}, bf16[64,2048]{1,0:T(8,128)(2,1)S(1)}, bf16[64,2048]{1,0:T(8,128)(2,1)S(1)}) custom-call(f32[64,2048]{1,0:T(8,128)S(1)} %get-tuple-element.67.refs_0_, s32[1]{0:T(128)} %bitcast.refs_0_.refs_1_, bf16[64,2048]{1,0:T(8,128)(2,1)S(1)} %get-tuple-element.68.refs_2_, ...), custom_call_target="tpu_custom_call" | custom-call | tf_op jit(solution)/shard_map/pallas_call | solution.py:28
  99.3 0.3 collective-permute-start.30
  100.1 7.9 %collective-permute-done.30.refs_2_ = bf16[64,2048]{1,0:T(8,128)(2,1)S(1)} collective-permute-done((bf16[64,2048]{1,0:T(8,128)(2,1)S(1)}, bf16[64,2048]{1,0:T(8,128)(2,1)S(1)}, u32[]{:S(2)}, u32[]{:S(2)}) %collective-permute-start.30) | collective-permute-done | bytes 262176 | tf_op jit(solution)/shard_map/ppermute | solution.py:50
  108.2 0.4 collective-permute-start.32
  108.5 2.3 %collective-permute-start.35 = (bf16[32,2048]{1,0:T(8,128)(2,1)S(1)}, bf16[32,2048]{1,0:T(8,128)(2,1)S(1)}, u32[]{:S(2)}, u32[]{:S(2)}) collective-permute-start(bf16[32,2048]{1,0:T(8,128)(2,1)S(1)} %get-tuple-element.75.refs_0_), channel_id=1, source_target_pairs={{0,12},{1,13},{2,14},{3,15},{4,8},{5,9},{6,10},{7,11},{8,4},{9,5},... | collective-permute-start | bytes 393224 | tf_op jit(solution)/shard_map/ppermute | solution.py:50
  110.8 2.0 %collective-permute-start.34 = (bf16[32,2048]{1,0:T(8,128)(2,1)S(1)}, bf16[32,2048]{1,0:T(8,128)(2,1)S(1)}, u32[]{:S(2)}, u32[]{:S(2)}) collective-permute-start(bf16[32,2048]{1,0:T(8,128)(2,1)S(1)} %get-tuple-element.80), channel_id=1, source_target_pairs={{0,8},{1,9},{2,10},{3,11},{4,12},{5,13},{6,14},{7,15},{8,0},{9,1},... | collective-permute-start | bytes 393224 | tf_op jit(solution)/shard_map/ppermute | solution.py:50
  112.8 3.3 %collective-permute-done.32.refs_2_ = bf16[64,2048]{1,0:T(8,128)(2,1)S(1)} collective-permute-done((bf16[64,2048]{1,0:T(8,128)(2,1)S(1)}, bf16[64,2048]{1,0:T(8,128)(2,1)S(1)}, u32[]{:S(2)}, u32[]{:S(2)}) %collective-permute-start.32) | collective-permute-done | bytes 262176 | tf_op jit(solution)/shard_map/ppermute | solution.py:50
  116.2 2.7 %collective-permute-start.33 = (bf16[32,2048]{1,0:T(8,128)(2,1)S(1)}, bf16[32,2048]{1,0:T(8,128)(2,1)S(1)}, u32[]{:S(2)}, u32[]{:S(2)}) collective-permute-start(bf16[32,2048]{1,0:T(8,128)(2,1)S(1)} %get-tuple-element.79), channel_id=1, source_target_pairs={{0,4},{1,5},{2,6},{3,7},{4,0},{5,1},{6,2},{7,3},{8,12},{9,13},{10,... | collective-permute-start | bytes 393224 | tf_op jit(solution)/shard_map/ppermute | solution.py:50
  118.9 4.8 %collective-permute-done.34.refs_3_ = bf16[32,2048]{1,0:T(8,128)(2,1)S(1)} collective-permute-done((bf16[32,2048]{1,0:T(8,128)(2,1)S(1)}, bf16[32,2048]{1,0:T(8,128)(2,1)S(1)}, u32[]{:S(2)}, u32[]{:S(2)}) %collective-permute-start.34) | collective-permute-done | bytes 131104 | tf_op jit(solution)/shard_map/ppermute | solution.py:50
  123.7 1.0 collective-permute-done.33.refs_2_
  124.7 0.8 shard_map.73
  (51 shorter events, 2.6 us)
Async XLA Ops:
  1.2 14.6 %collective-permute-start = (bf16[32,2176]{1,0:T(8,128)(2,1)S(1)}, bf16[32,2176]{1,0:T(8,128)(2,1)S(1)}, u32[]{:S(2)}, u32[]{:S(2)}) collective-permute-start(bf16[32,2176]{1,0:T(8,128)(2,1)S(1)} %shard_map.56.refs_3_), channel_id=1, source_target_pairs={{0,8},{1,9},{2,10},{3,11},{4,12},{5,13},{6,14},{7,15},{8,0},{9,1},... | collective-permute-start | bytes 417800 | tf_op jit(solution)/shard_map/ppermute | solution.py:50
  5.3 10.5 %collective-permute-start.1 = (bf16[32,2176]{1,0:T(8,128)(2,1)S(1)}, bf16[32,2176]{1,0:T(8,128)(2,1)S(1)}, u32[]{:S(2)}, u32[]{:S(2)}) collective-permute-start(bf16[32,2176]{1,0:T(8,128)(2,1)S(1)} %shard_map.56.refs_3_), channel_id=1, source_target_pairs={{0,12},{1,13},{2,14},{3,15},{4,8},{5,9},{6,10},{7,11},{8,4},{9,5},... | collective-permute-start | bytes 417800 | tf_op jit(solution)/shard_map/ppermute | solution.py:50
  6.7 9.7 %collective-permute-start.2 = (bf16[32,2176]{1,0:T(8,128)(2,1)S(1)}, bf16[32,2176]{1,0:T(8,128)(2,1)S(1)}, u32[]{:S(2)}, u32[]{:S(2)}) collective-permute-start(bf16[32,2176]{1,0:T(8,128)(2,1)S(1)} %shard_map.56.refs_3_), channel_id=1, source_target_pairs={{0,4},{1,5},{2,6},{3,7},{4,0},{5,1},{6,2},{7,3},{8,12},{9,13},{10,... | collective-permute-start | bytes 417800 | tf_op jit(solution)/shard_map/ppermute | solution.py:50
  10.7 2.7 %copy-start = (bf16[2048,1536]{1,0:T(8,128)(2,1)}, bf16[2048,1536]{1,0:T(8,128)(2,1)S(1)}, u32[]{:S(2)}) copy-start(bf16[2048,1536]{1,0:T(8,128)(2,1)S(1)} %get-tuple-element.45.refs_5_.refs_6_) | copy-start | bytes 18874372
  17.1 9.8 %collective-permute-start.3 = (bf16[64,2176]{1,0:T(8,128)(2,1)}, bf16[64,2176]{1,0:T(8,128)(2,1)}, u32[]{:S(2)}, u32[]{:S(2)}) collective-permute-start(bf16[64,2176]{1,0:T(8,128)(2,1)} %get-tuple-element.44.refs_1_), channel_id=1, source_target_pairs={{0,2},{1,3},{2,0},{3,1},{4,6},{5,7},{6,4},{7,5},{8,10},{9,11},{10,... | collective-permute-start | bytes 835592 | tf_op jit(solution)/shard_map/ppermute | solution.py:50
  18.7 11.2 %collective-permute-start.6 = (bf16[64,2176]{1,0:T(8,128)(2,1)S(1)}, bf16[64,2176]{1,0:T(8,128)(2,1)}, u32[]{:S(2)}, u32[]{:S(2)}) collective-permute-start(bf16[64,2176]{1,0:T(8,128)(2,1)S(1)} %get-tuple-element.48.refs_2_), channel_id=1, source_target_pairs={{0,2},{1,3},{2,0},{3,1},{4,6},{5,7},{6,4},{7,5},{8,10},{9,11},{10,... | collective-permute-start | bytes 835592 | tf_op jit(solution)/shard_map/ppermute | solution.py:50
  19.1 10.8 %collective-permute-start.4 = (bf16[64,2176]{1,0:T(8,128)(2,1)}, bf16[64,2176]{1,0:T(8,128)(2,1)}, u32[]{:S(2)}, u32[]{:S(2)}) collective-permute-start(bf16[64,2176]{1,0:T(8,128)(2,1)} %get-tuple-element.44.refs_1_), channel_id=1, source_target_pairs={{0,1},{1,0},{2,3},{3,2},{4,5},{5,4},{6,7},{7,6},{8,9},{9,8},{10,11... | collective-permute-start | bytes 835592 | tf_op jit(solution)/shard_map/ppermute | solution.py:50
  26.9 3.0 %collective-permute-start.5 = (bf16[64,2176]{1,0:T(8,128)(2,1)}, bf16[64,2176]{1,0:T(8,128)(2,1)}, u32[]{:S(2)}, u32[]{:S(2)}) collective-permute-start(bf16[64,2176]{1,0:T(8,128)(2,1)} %collective-permute-done.3.refs_2_), channel_id=1, source_target_pairs={{0,1},{1,0},{2,3},{3,2},{4,5},{5,4},{6,7},{7,6},{8,9},{9,8},{10,11... | collective-permute-start | bytes 835592 | tf_op jit(solution)/shard_map/ppermute | solution.py:50
  26.9 10.3 %collective-permute-start.7 = (bf16[64,2176]{1,0:T(8,128)(2,1)S(1)}, bf16[64,2176]{1,0:T(8,128)(2,1)}, u32[]{:S(2)}, u32[]{:S(2)}) collective-permute-start(bf16[64,2176]{1,0:T(8,128)(2,1)S(1)} %get-tuple-element.48.refs_2_), channel_id=1, source_target_pairs={{0,1},{1,0},{2,3},{3,2},{4,5},{5,4},{6,7},{7,6},{8,9},{9,8},{10,11... | collective-permute-start | bytes 835592 | tf_op jit(solution)/shard_map/ppermute | solution.py:50
  29.9 7.3 %collective-permute-start.8 = (bf16[64,2176]{1,0:T(8,128)(2,1)}, bf16[64,2176]{1,0:T(8,128)(2,1)}, u32[]{:S(2)}, u32[]{:S(2)}) collective-permute-start(bf16[64,2176]{1,0:T(8,128)(2,1)} %collective-permute-done.6.refs_3_), channel_id=1, source_target_pairs={{0,1},{1,0},{2,3},{3,2},{4,5},{5,4},{6,7},{7,6},{8,9},{9,8},{10,11... | collective-permute-start | bytes 835592 | tf_op jit(solution)/shard_map/ppermute | solution.py:50
  29.9 2.8 %copy-start.1 = (bf16[2048,1536]{1,0:T(8,128)(2,1)S(1)}, bf16[2048,1536]{1,0:T(8,128)(2,1)}, u32[]{:S(2)}) copy-start(bf16[2048,1536]{1,0:T(8,128)(2,1)} %copy-done) | copy-start | bytes 18874372
  36.5 4.4 %collective-permute-start.11 = (bf16[64,2048]{1,0:T(8,128)(2,1)S(1)}, bf16[64,2048]{1,0:T(8,128)(2,1)S(1)}, u32[]{:S(2)}, u32[]{:S(2)}) collective-permute-start(bf16[64,2048]{1,0:T(8,128)(2,1)S(1)} %get-tuple-element.54), channel_id=1, source_target_pairs={{0,1},{1,0},{2,3},{3,2},{4,5},{5,4},{6,7},{7,6},{8,9},{9,8},{10,11... | collective-permute-start | bytes 786440 | tf_op jit(solution)/shard_map/ppermute | solution.py:50
  37.1 5.8 %collective-permute-start.10 = (bf16[64,2048]{1,0:T(8,128)(2,1)S(1)}, bf16[64,2048]{1,0:T(8,128)(2,1)S(1)}, u32[]{:S(2)}, u32[]{:S(2)}) collective-permute-start(bf16[64,2048]{1,0:T(8,128)(2,1)S(1)} %get-tuple-element.52), channel_id=1, source_target_pairs={{0,1},{1,0},{2,3},{3,2},{4,5},{5,4},{6,7},{7,6},{8,9},{9,8},{10,11... | collective-permute-start | bytes 786440 | tf_op jit(solution)/shard_map/ppermute | solution.py:50
  41.0 8.7 %collective-permute-start.12 = (bf16[64,2048]{1,0:T(8,128)(2,1)S(1)}, bf16[64,2048]{1,0:T(8,128)(2,1)S(1)}, u32[]{:S(2)}, u32[]{:S(2)}) collective-permute-start(bf16[64,2048]{1,0:T(8,128)(2,1)S(1)} %shard_map.61), channel_id=1, source_target_pairs={{0,2},{1,3},{2,0},{3,1},{4,6},{5,7},{6,4},{7,5},{8,10},{9,11},{10,... | collective-permute-start | bytes 786440 | tf_op jit(solution)/shard_map/ppermute | solution.py:50
  42.4 7.4 %collective-permute-start.13 = (bf16[64,2048]{1,0:T(8,128)(2,1)S(1)}, bf16[64,2048]{1,0:T(8,128)(2,1)S(1)}, u32[]{:S(2)}, u32[]{:S(2)}) collective-permute-start(bf16[64,2048]{1,0:T(8,128)(2,1)S(1)} %get-tuple-element.57), channel_id=1, source_target_pairs={{0,1},{1,0},{2,3},{3,2},{4,5},{5,4},{6,7},{7,6},{8,9},{9,8},{10,11... | collective-permute-start | bytes 786440 | tf_op jit(solution)/shard_map/ppermute | solution.py:50
  42.6 15.3 %collective-permute-start.9 = (bf16[64,2048]{1,0:T(8,128)(2,1)S(1)}, bf16[64,2048]{1,0:T(8,128)(2,1)S(1)}, u32[]{:S(2)}, u32[]{:S(2)}) collective-permute-start(bf16[64,2048]{1,0:T(8,128)(2,1)S(1)} %get-tuple-element.51), channel_id=1, source_target_pairs={{0,1},{1,0},{2,3},{3,2},{4,5},{5,4},{6,7},{7,6},{8,9},{9,8},{10,11... | collective-permute-start | bytes 786440 | tf_op jit(solution)/shard_map/ppermute | solution.py:50
  49.9 8.0 %collective-permute-start.14 = (bf16[64,2048]{1,0:T(8,128)(2,1)S(1)}, bf16[64,2048]{1,0:T(8,128)(2,1)S(1)}, u32[]{:S(2)}, u32[]{:S(2)}) collective-permute-start(bf16[64,2048]{1,0:T(8,128)(2,1)S(1)} %shard_map.63), channel_id=1, source_target_pairs={{0,2},{1,3},{2,0},{3,1},{4,6},{5,7},{6,4},{7,5},{8,10},{9,11},{10,... | collective-permute-start | bytes 786440 | tf_op jit(solution)/shard_map/ppermute | solution.py:50
  51.3 16.3 %collective-permute-start.17 = (bf16[32,2048]{1,0:T(8,128)(2,1)S(1)}, bf16[32,2048]{1,0:T(8,128)(2,1)S(1)}, u32[]{:S(2)}, u32[]{:S(2)}) collective-permute-start(bf16[32,2048]{1,0:T(8,128)(2,1)S(1)} %get-tuple-element.55.refs_0_), channel_id=1, source_target_pairs={{0,12},{1,13},{2,14},{3,15},{4,8},{5,9},{6,10},{7,11},{8,4},{9,5},... | collective-permute-start | bytes 393224 | tf_op jit(solution)/shard_map/ppermute | solution.py:50
  56.0 11.6 %collective-permute-start.16 = (bf16[32,2048]{1,0:T(8,128)(2,1)S(1)}, bf16[32,2048]{1,0:T(8,128)(2,1)S(1)}, u32[]{:S(2)}, u32[]{:S(2)}) collective-permute-start(bf16[32,2048]{1,0:T(8,128)(2,1)S(1)} %get-tuple-element.60), channel_id=1, source_target_pairs={{0,8},{1,9},{2,10},{3,11},{4,12},{5,13},{6,14},{7,15},{8,0},{9,1},... | collective-permute-start | bytes 393224 | tf_op jit(solution)/shard_map/ppermute | solution.py:50
  57.9 10.3 %copy-start.2 = (bf16[2,16,2048]{2,1,0:T(8,128)(2,1)S(1)}, bf16[2,16,2048]{2,1,0:T(8,128)(2,1)}, u32[]{:S(2)}) copy-start(bf16[2,16,2048]{2,1,0:T(8,128)(2,1)} %param.5) | copy-start | bytes 393220
  57.9 10.3 %copy-start.3 = (f32[2,2048]{1,0:T(2,128)S(1)}, f32[2,2048]{1,0:T(2,128)}, u32[]{:S(2)}) copy-start(f32[2,2048]{1,0:T(2,128)} %refs_2_.5) | copy-start | bytes 49156
  58.0 10.2 %collective-permute-start.15 = (bf16[32,2048]{1,0:T(8,128)(2,1)S(1)}, bf16[32,2048]{1,0:T(8,128)(2,1)S(1)}, u32[]{:S(2)}, u32[]{:S(2)}) collective-permute-start(bf16[32,2048]{1,0:T(8,128)(2,1)S(1)} %get-tuple-element.59), channel_id=1, source_target_pairs={{0,4},{1,5},{2,6},{3,7},{4,0},{5,1},{6,2},{7,3},{8,12},{9,13},{10,... | collective-permute-start | bytes 393224 | tf_op jit(solution)/shard_map/ppermute | solution.py:50
  68.4 12.3 %collective-permute-start.18 = (bf16[32,2048]{1,0:T(8,128)(2,1)S(1)}, bf16[32,2048]{1,0:T(8,128)(2,1)S(1)}, u32[]{:S(2)}, u32[]{:S(2)}) collective-permute-start(bf16[32,2048]{1,0:T(8,128)(2,1)S(1)} %get-tuple-element.62.refs_3_), channel_id=1, source_target_pairs={{0,8},{1,9},{2,10},{3,11},{4,12},{5,13},{6,14},{7,15},{8,0},{9,1},... | collective-permute-start | bytes 393224 | tf_op jit(solution)/shard_map/ppermute | solution.py:50
  70.0 10.8 %collective-permute-start.19 = (bf16[32,2048]{1,0:T(8,128)(2,1)S(1)}, bf16[32,2048]{1,0:T(8,128)(2,1)S(1)}, u32[]{:S(2)}, u32[]{:S(2)}) collective-permute-start(bf16[32,2048]{1,0:T(8,128)(2,1)S(1)} %get-tuple-element.62.refs_3_), channel_id=1, source_target_pairs={{0,12},{1,13},{2,14},{3,15},{4,8},{5,9},{6,10},{7,11},{8,4},{9,5},... | collective-permute-start | bytes 393224 | tf_op jit(solution)/shard_map/ppermute | solution.py:50
  71.9 9.0 %collective-permute-start.20 = (bf16[32,2048]{1,0:T(8,128)(2,1)S(1)}, bf16[32,2048]{1,0:T(8,128)(2,1)S(1)}, u32[]{:S(2)}, u32[]{:S(2)}) collective-permute-start(bf16[32,2048]{1,0:T(8,128)(2,1)S(1)} %get-tuple-element.62.refs_3_), channel_id=1, source_target_pairs={{0,4},{1,5},{2,6},{3,7},{4,0},{5,1},{6,2},{7,3},{8,12},{9,13},{10,... | collective-permute-start | bytes 393224 | tf_op jit(solution)/shard_map/ppermute | solution.py:50
  81.0 9.3 %collective-permute-start.21 = (bf16[64,2048]{1,0:T(8,128)(2,1)S(1)}, bf16[64,2048]{1,0:T(8,128)(2,1)S(1)}, u32[]{:S(2)}, u32[]{:S(2)}) collective-permute-start(bf16[64,2048]{1,0:T(8,128)(2,1)S(1)} %get-tuple-element.63.refs_1_), channel_id=1, source_target_pairs={{0,2},{1,3},{2,0},{3,1},{4,6},{5,7},{6,4},{7,5},{8,10},{9,11},{10,... | collective-permute-start | bytes 786440 | tf_op jit(solution)/shard_map/ppermute | solution.py:50
  81.5 11.6 %collective-permute-start.24 = (bf16[64,2048]{1,0:T(8,128)(2,1)S(1)}, bf16[64,2048]{1,0:T(8,128)(2,1)S(1)}, u32[]{:S(2)}, u32[]{:S(2)}) collective-permute-start(bf16[64,2048]{1,0:T(8,128)(2,1)S(1)} %get-tuple-element.68.refs_2_), channel_id=1, source_target_pairs={{0,2},{1,3},{2,0},{3,1},{4,6},{5,7},{6,4},{7,5},{8,10},{9,11},{10,... | collective-permute-start | bytes 786440 | tf_op jit(solution)/shard_map/ppermute | solution.py:50
  83.1 10.1 %collective-permute-start.22 = (bf16[64,2048]{1,0:T(8,128)(2,1)S(1)}, bf16[64,2048]{1,0:T(8,128)(2,1)S(1)}, u32[]{:S(2)}, u32[]{:S(2)}) collective-permute-start(bf16[64,2048]{1,0:T(8,128)(2,1)S(1)} %get-tuple-element.63.refs_1_), channel_id=1, source_target_pairs={{0,1},{1,0},{2,3},{3,2},{4,5},{5,4},{6,7},{7,6},{8,9},{9,8},{10,11... | collective-permute-start | bytes 786440 | tf_op jit(solution)/shard_map/ppermute | solution.py:50
  90.3 2.9 %collective-permute-start.23 = (bf16[64,2048]{1,0:T(8,128)(2,1)S(1)}, bf16[64,2048]{1,0:T(8,128)(2,1)S(1)}, u32[]{:S(2)}, u32[]{:S(2)}) collective-permute-start(bf16[64,2048]{1,0:T(8,128)(2,1)S(1)} %collective-permute-done.21.refs_2_), channel_id=1, source_target_pairs={{0,1},{1,0},{2,3},{3,2},{4,5},{5,4},{6,7},{7,6},{8,9},{9,8},{10,11... | collective-permute-start | bytes 786440 | tf_op jit(solution)/shard_map/ppermute | solution.py:50
  90.3 6.2 %collective-permute-start.25 = (bf16[64,2048]{1,0:T(8,128)(2,1)S(1)}, bf16[64,2048]{1,0:T(8,128)(2,1)S(1)}, u32[]{:S(2)}, u32[]{:S(2)}) collective-permute-start(bf16[64,2048]{1,0:T(8,128)(2,1)S(1)} %get-tuple-element.68.refs_2_), channel_id=1, source_target_pairs={{0,1},{1,0},{2,3},{3,2},{4,5},{5,4},{6,7},{7,6},{8,9},{9,8},{10,11... | collective-permute-start | bytes 786440 | tf_op jit(solution)/shard_map/ppermute | solution.py:50
  93.2 3.3 %collective-permute-start.26 = (bf16[64,2048]{1,0:T(8,128)(2,1)S(1)}, bf16[64,2048]{1,0:T(8,128)(2,1)S(1)}, u32[]{:S(2)}, u32[]{:S(2)}) collective-permute-start(bf16[64,2048]{1,0:T(8,128)(2,1)S(1)} %collective-permute-done.24.refs_3_), channel_id=1, source_target_pairs={{0,1},{1,0},{2,3},{3,2},{4,5},{5,4},{6,7},{7,6},{8,9},{9,8},{10,11... | collective-permute-start | bytes 786440 | tf_op jit(solution)/shard_map/ppermute | solution.py:50
  95.9 3.3 %collective-permute-start.29 = (bf16[64,2048]{1,0:T(8,128)(2,1)S(1)}, bf16[64,2048]{1,0:T(8,128)(2,1)S(1)}, u32[]{:S(2)}, u32[]{:S(2)}) collective-permute-start(bf16[64,2048]{1,0:T(8,128)(2,1)S(1)} %get-tuple-element.74), channel_id=1, source_target_pairs={{0,1},{1,0},{2,3},{3,2},{4,5},{5,4},{6,7},{7,6},{8,9},{9,8},{10,11... | collective-permute-start | bytes 786440 | tf_op jit(solution)/shard_map/ppermute | solution.py:50
  96.4 3.7 %collective-permute-start.28 = (bf16[64,2048]{1,0:T(8,128)(2,1)S(1)}, bf16[64,2048]{1,0:T(8,128)(2,1)S(1)}, u32[]{:S(2)}, u32[]{:S(2)}) collective-permute-start(bf16[64,2048]{1,0:T(8,128)(2,1)S(1)} %get-tuple-element.72), channel_id=1, source_target_pairs={{0,1},{1,0},{2,3},{3,2},{4,5},{5,4},{6,7},{7,6},{8,9},{9,8},{10,11... | collective-permute-start | bytes 786440 | tf_op jit(solution)/shard_map/ppermute | solution.py:50
  99.3 8.7 %collective-permute-start.30 = (bf16[64,2048]{1,0:T(8,128)(2,1)S(1)}, bf16[64,2048]{1,0:T(8,128)(2,1)S(1)}, u32[]{:S(2)}, u32[]{:S(2)}) collective-permute-start(bf16[64,2048]{1,0:T(8,128)(2,1)S(1)} %shard_map.69), channel_id=1, source_target_pairs={{0,2},{1,3},{2,0},{3,1},{4,6},{5,7},{6,4},{7,5},{8,10},{9,11},{10,... | collective-permute-start | bytes 786440 | tf_op jit(solution)/shard_map/ppermute | solution.py:50
  99.6 8.5 %collective-permute-start.31 = (bf16[64,2048]{1,0:T(8,128)(2,1)S(1)}, bf16[64,2048]{1,0:T(8,128)(2,1)S(1)}, u32[]{:S(2)}, u32[]{:S(2)}) collective-permute-start(bf16[64,2048]{1,0:T(8,128)(2,1)S(1)} %get-tuple-element.77), channel_id=1, source_target_pairs={{0,1},{1,0},{2,3},{3,2},{4,5},{5,4},{6,7},{7,6},{8,9},{9,8},{10,11... | collective-permute-start | bytes 786440 | tf_op jit(solution)/shard_map/ppermute | solution.py:50
  99.8 13.0 %collective-permute-start.27 = (bf16[64,2048]{1,0:T(8,128)(2,1)S(1)}, bf16[64,2048]{1,0:T(8,128)(2,1)S(1)}, u32[]{:S(2)}, u32[]{:S(2)}) collective-permute-start(bf16[64,2048]{1,0:T(8,128)(2,1)S(1)} %get-tuple-element.71), channel_id=1, source_target_pairs={{0,1},{1,0},{2,3},{3,2},{4,5},{5,4},{6,7},{7,6},{8,9},{9,8},{10,11... | collective-permute-start | bytes 786440 | tf_op jit(solution)/shard_map/ppermute | solution.py:50
  108.2 7.9 %collective-permute-start.32 = (bf16[64,2048]{1,0:T(8,128)(2,1)S(1)}, bf16[64,2048]{1,0:T(8,128)(2,1)S(1)}, u32[]{:S(2)}, u32[]{:S(2)}) collective-permute-start(bf16[64,2048]{1,0:T(8,128)(2,1)S(1)} %shard_map.71), channel_id=1, source_target_pairs={{0,2},{1,3},{2,0},{3,1},{4,6},{5,7},{6,4},{7,5},{8,10},{9,11},{10,... | collective-permute-start | bytes 786440 | tf_op jit(solution)/shard_map/ppermute | solution.py:50
  108.5 15.2 %collective-permute-start.35 = (bf16[32,2048]{1,0:T(8,128)(2,1)S(1)}, bf16[32,2048]{1,0:T(8,128)(2,1)S(1)}, u32[]{:S(2)}, u32[]{:S(2)}) collective-permute-start(bf16[32,2048]{1,0:T(8,128)(2,1)S(1)} %get-tuple-element.75.refs_0_), channel_id=1, source_target_pairs={{0,12},{1,13},{2,14},{3,15},{4,8},{5,9},{6,10},{7,11},{8,4},{9,5},... | collective-permute-start | bytes 393224 | tf_op jit(solution)/shard_map/ppermute | solution.py:50
  110.8 12.9 %collective-permute-start.34 = (bf16[32,2048]{1,0:T(8,128)(2,1)S(1)}, bf16[32,2048]{1,0:T(8,128)(2,1)S(1)}, u32[]{:S(2)}, u32[]{:S(2)}) collective-permute-start(bf16[32,2048]{1,0:T(8,128)(2,1)S(1)} %get-tuple-element.80), channel_id=1, source_target_pairs={{0,8},{1,9},{2,10},{3,11},{4,12},{5,13},{6,14},{7,15},{8,0},{9,1},... | collective-permute-start | bytes 393224 | tf_op jit(solution)/shard_map/ppermute | solution.py:50
  116.2 8.5 %collective-permute-start.33 = (bf16[32,2048]{1,0:T(8,128)(2,1)S(1)}, bf16[32,2048]{1,0:T(8,128)(2,1)S(1)}, u32[]{:S(2)}, u32[]{:S(2)}) collective-permute-start(bf16[32,2048]{1,0:T(8,128)(2,1)S(1)} %get-tuple-element.79), channel_id=1, source_target_pairs={{0,4},{1,5},{2,6},{3,7},{4,0},{5,1},{6,2},{7,3},{8,12},{9,13},{10,... | collective-permute-start | bytes 393224 | tf_op jit(solution)/shard_map/ppermute | solution.py:50

commit v5 on v4

--- a/solution.py
+++ b/solution.py
@@ -11,7 +11,6 @@
 LANES = 128
 MIB = 2**20
 VMEM = pl.BlockSpec(memory_space=pltpu.VMEM)
-SMEM = pl.BlockSpec(memory_space=pltpu.SMEM)
 ANY = pl.BlockSpec(memory_space=pl.ANY)
 bf16, f32 = jnp.bfloat16, jnp.float32
 
@@ -57,12 +56,16 @@
         wholes[k // size][k % size * rows : (k % size + 1) * rows] = part[...]
 
 
+def held(value, until):
+    return lax.optimization_barrier((value, until))[0] if until is not None else value
+
+
 def gather_rows(rows, after):
     far = lax.axis_size("expert") // 4
     tokens, width = rows.shape
     parts = [rows] + [swap(rows, 4, k, far) for k in range(1, far)]
     shape = (far // 2 * tokens, width)
-    batches = []
+    batches, beside = [], None
     for near in call(
         functools.partial(join_kernel, far),
         [(shape, rows.dtype)] * 2,
@@ -71,8 +74,9 @@
         *parts[: far // 2],
         after=after,
     ):
+        near = held(near, beside)
         beside = swap(near, 2, 1, 2)
-        batches.append([near, beside, swap(near, 1, 1, 2), swap(beside, 1, 1, 2)])
+        batches.append([near, beside])
     return batches
 
 
@@ -87,34 +91,35 @@
         piece[...] = total[k * rows : (k + 1) * rows].astype(piece.dtype)
 
 
-def return_rows(batches, tokens):
+def leave_pair(found, after):
+    mine_near, mine_beside, other_near, other_beside = found
+    arrived_beside = swap(other_beside, 1, 1, 2, True)
+    arrived_near = swap(other_near, 1, 1, 2, True)
+    (leaving,) = call(
+        sum_kernel,
+        [(mine_beside.shape, bf16)],
+        [VMEM] * 2,
+        mine_beside,
+        arrived_beside,
+        after=after,
+    )
+    return mine_near, arrived_near, leaving
+
+
+def split_rows(left, distances, tokens):
     far = lax.axis_size("expert") // 4
-    returned, steps, earlier = {}, [range(far // 2, far), range(far // 2)], ()
-    for (mine_near, mine_beside, other_near, other_beside), distances in zip(batches, steps):
-        shape = mine_near.shape
-        arrived_beside = swap(other_beside, 1, 1, 2, True)
-        arrived_near = swap(other_near, 1, 1, 2, True)
-        (leaving,) = call(
-            sum_kernel,
-            [(shape, bf16)],
-            [VMEM] * 2,
-            mine_beside,
-            arrived_beside,
-            after=earlier,
-        )
-        beside = swap(leaving, 2, 1, 2, True)
-        pieces = call(
-            split_kernel,
-            [((tokens, shape[1]), bf16 if k else f32) for k in distances],
-            [VMEM] * 3,
-            mine_near,
-            arrived_near,
-            beside,
-        )
-        earlier = (pieces[-1],)
-        for k, piece in zip(distances, pieces):
-            returned[k] = swap(piece, 4, k, far, True) if k else piece
-    return [returned[k] for k in range(far)]
+    mine_near, arrived_near, leaving = left
+    beside = swap(leaving, 2, 1, 2, True)
+    pieces = call(
+        split_kernel,
+        [((tokens, leaving.shape[1]), bf16 if k else f32) for k in distances],
+        [VMEM] * 3,
+        mine_near,
+        arrived_near,
+        beside,
+    )
+    arrived = [swap(piece, 4, k, far, True) if k else piece for k, piece in zip(distances, pieces)]
+    return arrived, pieces[-1]
 
 
 def normed_rows(widened, gain_row):
@@ -214,7 +219,7 @@
     return size
 
 
-def expert_kernel(first_column, wide, me_ref, *refs):
+def expert_kernel(first_column, wide, *refs):
     if wide:
         parts, refs = refs[:4], refs[4:]
         gate_up_ref, down_ref, *outs, routed_ref, rows_ref, hidden_ref = refs
@@ -229,7 +234,8 @@
         if wide:
             routed_ref[span] = part[:, features:]
     places = lax.broadcasted_iota(jnp.int32, routed_ref.shape, 1)
-    chosen = jnp.where(places == me_ref[0] + first_column, routed_ref[...].astype(f32), 0.0)
+    column = first_column + lax.axis_index("expert")
+    chosen = jnp.where(places == column, routed_ref[...].astype(f32), 0.0)
     share = jnp.sum(chosen, axis=1, keepdims=True)
     rows = rows_ref[...]
     size = tile_of(hidden_size, 256)
@@ -247,7 +253,7 @@
             out[:, span] = done[k * quarter : (k + 1) * quarter].astype(out.dtype)
 
 
-def run_expert(parts, routed, me, first_column, weights, after):
+def run_expert(parts, routed, first_column, weights, after):
     gate_up, down_proj, _ = weights
     hidden_size, features = down_proj.shape
     quarter, width = parts[0].shape
@@ -259,8 +265,7 @@
     found = call(
         functools.partial(expert_kernel, first_column, wide),
         outs,
-        [SMEM] + [VMEM] * (6 if wide else 7),
-        me,
+        [VMEM] * (6 if wide else 7),
         *parts,
         *([] if wide else [routed]),
         gate_up,
@@ -299,18 +304,22 @@
     return wide
 
 
-def run_layer(rows, routed, me, first_column, weights, loaded=()):
-    found, columns = [], []
-    batches = gather_rows(rows, loaded)
-    after = ()
-    for place, parts in enumerate(batches):
+def run_layer(rows, routed, first_column, weights, loaded=()):
+    far, tokens = lax.axis_size("expert") // 4, rows.shape[0]
+    columns, returned, after, worked = [], [], (), ()
+    distances = [range(far // 2, far), range(far // 2)]
+    for place, (near, beside) in enumerate(gather_rows(rows, loaded)):
+        beside = held(beside, left[2] if place else None)
+        parts = [near, beside, swap(near, 1, 1, 2), swap(beside, 1, 1, 2)]
         outs, kept = run_expert(
-            parts, None if routed is None else routed[place], me, first_column, weights, after
+            parts, None if routed is None else routed[place], first_column, weights, worked
         )
-        after = (outs[0],)
-        found.append(outs)
         columns.append(kept)
-    return return_rows(found, rows.shape[0]), columns, after
+        left = leave_pair(outs, after)
+        arrived, last = split_rows(left, distances[place], tokens)
+        returned = arrived + returned
+        after, worked = (last,), (left[2],)
+    return returned, columns, (outs[0],)
 
 
 def close_rows(layer_no, current, gain, returned, after=()):
@@ -328,7 +337,6 @@
 def on_device(inputs, routes, norm_gain, w_gate_up, w_down):
     experts = lax.axis_size("expert")
     sections = lax.axis_size("section")
-    me = lax.axis_index("expert").astype(jnp.int32).reshape(1)
     batches, tokens, features = inputs.shape
     layers = routes.shape[0]
     weights = load_weights(0, w_gate_up, w_down)
@@ -338,7 +346,7 @@
         rows = open_rows(inputs, routes, norm_gain, experts)
         for layer_no in range(layers):
             returned, routed, worked = run_layer(
-                rows, routed, me, layer_no * experts, weights, weights[2:]
+                rows, routed, layer_no * experts, weights, weights[2:]
             )
             if layer_no == layers - 1:
                 (whole,) = call(
@@ -365,7 +373,7 @@
         batch_pick = jnp.clip(turn_no - segment_no, 0, batches - 1)
         turn_routes = lax.dynamic_slice_in_dim(routes, batch_pick, 1, 1)
         rows = open_rows(current[None], turn_routes, norm_gain, experts)
-        returned, _, _ = run_layer(rows, None, me, 0, weights)
+        returned, _, _ = run_layer(rows, None, 0, weights)
         result, _ = close_rows(0, current, norm_gain, returned)
         finished.append(result)
         if turn_no < batches:

time: 126 us -> 119 us (0.944)
  local copies, waits for them, and re-layouts: 5.46 us -> 0.01 us
  starting transfers between devices: 38.7 us -> 43.4 us
  Pallas kernels: 24 us -> 20.7 us
  waiting for transfers between devices: 57.1 us -> 54.8 us
    unnamed x8 -> x4, local copies, waits for them, and re-layouts: 5.46 us -> 0.01 us
    ppermute x36, starting transfers between devices: 38.7 us -> 43.4 us  [swap(): lax.ppermute(value, 'expert', [(i, partner(i)) for i in range(count)])]
    pallas_call x19, Pallas kernels: 24 us -> 20.7 us  [call(): pl.pallas_call(lambda *refs: kernel(*refs[len(after):]), out_shape=shapes...]
    ppermute x36, waiting for transfers between devices: 57.1 us -> 54.8 us  [swap(): lax.ppermute(value, 'expert', [(i, partner(i)) for i in range(count)])]
  transfers between devices with their start and end apart: 36 -> 36, of which waited for: 15 -> 17; matrix products, arithmetic and copies ran while one was open for 0% -> 0% of each run, Pallas kernels for 17% -> 13%
where the time goes in v5:
time: 119 us
  waiting for transfers between devices  54.8 us (46%)
  starting transfers between devices  43.4 us (36%)
  Pallas kernels  20.7 us (17%)
    ppermute x36, waiting for transfers between devices, swap(): lax.ppermute(value, 'expert', [(i, partner(i)) for i in range(count)])  54.8 us
    ppermute x36, starting transfers between devices, swap(): lax.ppermute(value, 'expert', [(i, partner(i)) for i in range(count)])  43.4 us
    pallas_call x19, Pallas kernels, call(): pl.pallas_call(lambda *refs: kernel(*refs[len(after):]), out_shape=shapes...  20.7 us
  transfers between devices with their start and end apart: 36, of which 17 were waited for; matrix products, arithmetic and copies ran while one was open for 0% of the time, Pallas kernels for 13%

profile of v5, /device:TPU:0, one launch (start us, length us, event | category | flops | bytes accessed | tf_op | source)
XLA Modules:
  0.0 119.2 jit_solution(742741171633330526)
XLA Ops:
  0.0 1.2 %shard_map.56.refs_3_ = bf16[32,2176]{1,0:T(8,128)(2,1)S(1)} custom-call(bf16[32,2048]{1,0:T(8,128)(2,1)} %bitcast.2, s32[2,2,8,16]{3,2,1,0:T(8,128)} %bitcast.4, f32[2,2048]{1,0:T(2,128)} %refs_2_.5), custom_call_target="tpu_custom_call" | custom-call | tf_op jit(solution)/shard_map/pallas_call | solution.py:27
  1.2 4.1 %collective-permute-start = (bf16[32,2176]{1,0:T(8,128)(2,1)S(1)}, bf16[32,2176]{1,0:T(8,128)(2,1)S(1)}, u32[]{:S(2)}, u32[]{:S(2)}) collective-permute-start(bf16[32,2176]{1,0:T(8,128)(2,1)S(1)} %shard_map.56.refs_3_), channel_id=1, source_target_pairs={{0,8},{1,9},{2,10},{3,11},{4,12},{5,13},{6,14},{7,15},{8,0},{9,1},... | collective-permute-start | bytes 417800 | tf_op jit(solution)/shard_map/ppermute | solution.py:49
  5.3 1.3 %collective-permute-start.1 = (bf16[32,2176]{1,0:T(8,128)(2,1)S(1)}, bf16[32,2176]{1,0:T(8,128)(2,1)S(1)}, u32[]{:S(2)}, u32[]{:S(2)}) collective-permute-start(bf16[32,2176]{1,0:T(8,128)(2,1)S(1)} %shard_map.56.refs_3_), channel_id=1, source_target_pairs={{0,12},{1,13},{2,14},{3,15},{4,8},{5,9},{6,10},{7,11},{8,4},{9,5},... | collective-permute-start | bytes 417800 | tf_op jit(solution)/shard_map/ppermute | solution.py:49
  6.9 3.7 %shard_map.55 = (bf16[2048,1536]{1,0:T(8,128)(2,1)S(1)}, bf16[768,2048]{1,0:T(8,128)(2,1)S(1)}, f32[8,128]{1,0:T(8,128)S(1)}) custom-call(bf16[2,1,2048,1536]{3,2,1,0:T(8,128)(2,1)} %refs_1_.3, bf16[2,1,768,2048]{3,2,1,0:T(8,128)(2,1)} %refs_2_.4), custom_call_target="tpu_custom_call" | custom-call | tf_op jit(solution)/shard_map/pallas_call | solution.py:27
  10.7 5.2 %collective-permute-done.refs_1_ = bf16[32,2176]{1,0:T(8,128)(2,1)S(1)} collective-permute-done((bf16[32,2176]{1,0:T(8,128)(2,1)S(1)}, bf16[32,2176]{1,0:T(8,128)(2,1)S(1)}, u32[]{:S(2)}, u32[]{:S(2)}) %collective-permute-start) | collective-permute-done | bytes 139296 | tf_op jit(solution)/shard_map/ppermute | solution.py:49
  15.8 0.5 collective-permute-done.2.refs_4_
  16.4 1.6 %collective-permute-start.3 = (bf16[64,2176]{1,0:T(8,128)(2,1)S(1)}, bf16[64,2176]{1,0:T(8,128)(2,1)S(1)}, u32[]{:S(2)}, u32[]{:S(2)}) collective-permute-start(bf16[64,2176]{1,0:T(8,128)(2,1)S(1)} %get-tuple-element.48.refs_0_), channel_id=1, source_target_pairs={{0,2},{1,3},{2,0},{3,1},{4,6},{5,7},{6,4},{7,5},{8,10},{9,11},{10,... | collective-permute-start | bytes 835592 | tf_op jit(solution)/shard_map/ppermute | solution.py:49
  18.0 5.0 %collective-permute-done.3.refs_1_ = bf16[64,2176]{1,0:T(8,128)(2,1)S(1)} collective-permute-done((bf16[64,2176]{1,0:T(8,128)(2,1)S(1)}, bf16[64,2176]{1,0:T(8,128)(2,1)S(1)}, u32[]{:S(2)}, u32[]{:S(2)}) %collective-permute-start.3) | collective-permute-done | bytes 278560 | tf_op jit(solution)/shard_map/ppermute | solution.py:49
  23.0 1.6 %collective-permute-start.7 = (bf16[64,2176]{1,0:T(8,128)(2,1)S(1)}, bf16[64,2176]{1,0:T(8,128)(2,1)S(1)}, u32[]{:S(2)}, u32[]{:S(2)}) collective-permute-start(bf16[64,2176]{1,0:T(8,128)(2,1)S(1)} %get-tuple-element.54.refs_1_), channel_id=1, source_target_pairs={{0,2},{1,3},{2,0},{3,1},{4,6},{5,7},{6,4},{7,5},{8,10},{9,11},{10,... | collective-permute-start | bytes 835592 | tf_op jit(solution)/shard_map/ppermute | solution.py:49
  24.6 2.6 %shard_map.58 = (f32[64,2048]{1,0:T(8,128)S(1)}, f32[64,2048]{1,0:T(8,128)S(1)}, bf16[64,2048]{1,0:T(8,128)(2,1)S(1)}, bf16[64,2048]{1,0:T(8,128)(2,1)S(1)}, bf16[256,128]{1,0:T(8,128)(2,1)S(1)}) custom-call(bf16[64,2176]{1,0:T(8,128)(2,1)S(1)} %get-tuple-element.48.refs_0_, bf16[64,2176]{1,0:T(8,128)(2,1)S(1)} %collective-permute-done.3.refs_1_, ...), custom_call_target="tpu_custom_call" | custom-call | tf_op jit(solution)/shard_map/pallas_call | solution.py:27
  27.2 0.3 collective-permute-start.6
  27.8 1.0 collective-permute-done.6.refs_1_
  28.9 3.2 %collective-permute-done.7.refs_2_ = bf16[64,2176]{1,0:T(8,128)(2,1)S(1)} collective-permute-done((bf16[64,2176]{1,0:T(8,128)(2,1)S(1)}, bf16[64,2176]{1,0:T(8,128)(2,1)S(1)}, u32[]{:S(2)}, u32[]{:S(2)}) %collective-permute-start.7) | collective-permute-done | bytes 278560 | tf_op jit(solution)/shard_map/ppermute | solution.py:49
  32.1 0.5 collective-permute-start.11
  32.6 1.6 %collective-permute-start.12 = (bf16[64,2048]{1,0:T(8,128)(2,1)S(1)}, bf16[64,2048]{1,0:T(8,128)(2,1)S(1)}, u32[]{:S(2)}, u32[]{:S(2)}) collective-permute-start(bf16[64,2048]{1,0:T(8,128)(2,1)S(1)} %shard_map.59.refs_0_), channel_id=1, source_target_pairs={{0,2},{1,3},{2,0},{3,1},{4,6},{5,7},{6,4},{7,5},{8,10},{9,11},{10,... | collective-permute-start | bytes 786440 | tf_op jit(solution)/shard_map/ppermute | solution.py:49
  34.2 2.6 %shard_map.60 = (f32[64,2048]{1,0:T(8,128)S(1)}, f32[64,2048]{1,0:T(8,128)S(1)}, bf16[64,2048]{1,0:T(8,128)(2,1)S(1)}, bf16[64,2048]{1,0:T(8,128)(2,1)S(1)}, bf16[256,128]{1,0:T(8,128)(2,1)S(1)}) custom-call(bf16[64,2048]{1,0:T(8,128)(2,1)S(1)} %shard_map.59.refs_0_, bf16[64,2176]{1,0:T(8,128)(2,1)S(1)} %get-tuple-element.54.refs_1_, ...), custom_call_target="tpu_custom_call" | custom-call | tf_op jit(solution)/shard_map/pallas_call | solution.py:27
  36.9 3.9 %collective-permute-done.12.refs_2_ = bf16[64,2048]{1,0:T(8,128)(2,1)S(1)} collective-permute-done((bf16[64,2048]{1,0:T(8,128)(2,1)S(1)}, bf16[64,2048]{1,0:T(8,128)(2,1)S(1)}, u32[]{:S(2)}, u32[]{:S(2)}) %collective-permute-start.12) | collective-permute-done | bytes 262176 | tf_op jit(solution)/shard_map/ppermute | solution.py:49
  41.0 1.6 %collective-permute-start.14 = (bf16[64,2048]{1,0:T(8,128)(2,1)S(1)}, bf16[64,2048]{1,0:T(8,128)(2,1)S(1)}, u32[]{:S(2)}, u32[]{:S(2)}) collective-permute-start(bf16[64,2048]{1,0:T(8,128)(2,1)S(1)} %shard_map.63), channel_id=1, source_target_pairs={{0,2},{1,3},{2,0},{3,1},{4,6},{5,7},{6,4},{7,5},{8,10},{9,11},{10,... | collective-permute-start | bytes 786440 | tf_op jit(solution)/shard_map/ppermute | solution.py:49
  42.7 4.4 %collective-permute-start.17 = (bf16[32,2048]{1,0:T(8,128)(2,1)S(1)}, bf16[32,2048]{1,0:T(8,128)(2,1)S(1)}, u32[]{:S(2)}, u32[]{:S(2)}) collective-permute-start(bf16[32,2048]{1,0:T(8,128)(2,1)S(1)} %get-tuple-element.61.refs_0_), channel_id=1, source_target_pairs={{0,12},{1,13},{2,14},{3,15},{4,8},{5,9},{6,10},{7,11},{8,4},{9,5},... | collective-permute-start | bytes 393224 | tf_op jit(solution)/shard_map/ppermute | solution.py:49
  47.1 1.8 %collective-permute-start.16 = (bf16[32,2048]{1,0:T(8,128)(2,1)S(1)}, bf16[32,2048]{1,0:T(8,128)(2,1)S(1)}, u32[]{:S(2)}, u32[]{:S(2)}) collective-permute-start(bf16[32,2048]{1,0:T(8,128)(2,1)S(1)} %get-tuple-element.66), channel_id=1, source_target_pairs={{0,8},{1,9},{2,10},{3,11},{4,12},{5,13},{6,14},{7,15},{8,0},{9,1},... | collective-permute-start | bytes 393224 | tf_op jit(solution)/shard_map/ppermute | solution.py:49
  48.9 0.9 collective-permute-done.14.refs_2_
  49.9 4.5 %collective-permute-start.15 = (bf16[32,2048]{1,0:T(8,128)(2,1)S(1)}, bf16[32,2048]{1,0:T(8,128)(2,1)S(1)}, u32[]{:S(2)}, u32[]{:S(2)}) collective-permute-start(bf16[32,2048]{1,0:T(8,128)(2,1)S(1)} %get-tuple-element.65), channel_id=1, source_target_pairs={{0,4},{1,5},{2,6},{3,7},{4,0},{5,1},{6,2},{7,3},{8,12},{9,13},{10,... | collective-permute-start | bytes 393224 | tf_op jit(solution)/shard_map/ppermute | solution.py:49
  54.4 3.7 %shard_map.61 = (bf16[2048,1536]{1,0:T(8,128)(2,1)S(1)}, bf16[768,2048]{1,0:T(8,128)(2,1)S(1)}, f32[8,128]{1,0:T(8,128)S(1)}) custom-call(f32[64,2048]{1,0:T(8,128)S(1)} %get-tuple-element.56.refs_0_, bf16[2,1,2048,1536]{3,2,1,0:T(8,128)(2,1)} %refs_1_.3, bf16[2,1,768,2048]{3,2,1,0:T(8,128)(2,1)} %refs_2_.4), custom_call_target="tpu_custom_call" | custom-call | tf_op jit(solution)/shard_map/pallas_call | solution.py:27
  58.1 1.4 %collective-permute-done.16.refs_5_ = bf16[32,2048]{1,0:T(8,128)(2,1)S(1)} collective-permute-done((bf16[32,2048]{1,0:T(8,128)(2,1)S(1)}, bf16[32,2048]{1,0:T(8,128)(2,1)S(1)}, u32[]{:S(2)}, u32[]{:S(2)}) %collective-permute-start.16) | collective-permute-done | bytes 131104 | tf_op jit(solution)/shard_map/ppermute | solution.py:49
  59.5 1.0 collective-permute-done.15.refs_4_
  60.8 1.5 %collective-permute-start.18 = (bf16[32,2048]{1,0:T(8,128)(2,1)S(1)}, bf16[32,2048]{1,0:T(8,128)(2,1)S(1)}, u32[]{:S(2)}, u32[]{:S(2)}) collective-permute-start(bf16[32,2048]{1,0:T(8,128)(2,1)S(1)} %get-tuple-element.68.refs_3_), channel_id=1, source_target_pairs={{0,8},{1,9},{2,10},{3,11},{4,12},{5,13},{6,14},{7,15},{8,0},{9,1},... | collective-permute-start | bytes 393224 | tf_op jit(solution)/shard_map/ppermute | solution.py:49
  62.3 2.0 %collective-permute-start.19 = (bf16[32,2048]{1,0:T(8,128)(2,1)S(1)}, bf16[32,2048]{1,0:T(8,128)(2,1)S(1)}, u32[]{:S(2)}, u32[]{:S(2)}) collective-permute-start(bf16[32,2048]{1,0:T(8,128)(2,1)S(1)} %get-tuple-element.68.refs_3_), channel_id=1, source_target_pairs={{0,12},{1,13},{2,14},{3,15},{4,8},{5,9},{6,10},{7,11},{8,4},{9,5},... | collective-permute-start | bytes 393224 | tf_op jit(solution)/shard_map/ppermute | solution.py:49
  64.3 0.5 collective-permute-start.20
  64.8 8.0 %collective-permute-done.18.refs_1_ = bf16[32,2048]{1,0:T(8,128)(2,1)S(1)} collective-permute-done((bf16[32,2048]{1,0:T(8,128)(2,1)S(1)}, bf16[32,2048]{1,0:T(8,128)(2,1)S(1)}, u32[]{:S(2)}, u32[]{:S(2)}) %collective-permute-start.18) | collective-permute-done | bytes 131104 | tf_op jit(solution)/shard_map/ppermute | solution.py:49
  72.8 0.5 collective-permute-done.20.refs_4_
  73.3 1.8 %collective-permute-start.21 = (bf16[64,2048]{1,0:T(8,128)(2,1)S(1)}, bf16[64,2048]{1,0:T(8,128)(2,1)S(1)}, u32[]{:S(2)}, u32[]{:S(2)}) collective-permute-start(bf16[64,2048]{1,0:T(8,128)(2,1)S(1)} %get-tuple-element.69.refs_0_), channel_id=1, source_target_pairs={{0,2},{1,3},{2,0},{3,1},{4,6},{5,7},{6,4},{7,5},{8,10},{9,11},{10,... | collective-permute-start | bytes 786440 | tf_op jit(solution)/shard_map/ppermute | solution.py:49
  75.1 5.1 %collective-permute-done.21.refs_1_ = bf16[64,2048]{1,0:T(8,128)(2,1)S(1)} collective-permute-done((bf16[64,2048]{1,0:T(8,128)(2,1)S(1)}, bf16[64,2048]{1,0:T(8,128)(2,1)S(1)}, u32[]{:S(2)}, u32[]{:S(2)}) %collective-permute-start.21) | collective-permute-done | bytes 262176 | tf_op jit(solution)/shard_map/ppermute | solution.py:49
  80.3 1.5 %collective-permute-done.23.refs_3_ = bf16[64,2048]{1,0:T(8,128)(2,1)S(1)} collective-permute-done((bf16[64,2048]{1,0:T(8,128)(2,1)S(1)}, bf16[64,2048]{1,0:T(8,128)(2,1)S(1)}, u32[]{:S(2)}, u32[]{:S(2)}) %collective-permute-start.23) | collective-permute-done | bytes 262176 | tf_op jit(solution)/shard_map/ppermute | solution.py:49
  81.8 2.6 %shard_map.67 = (f32[64,2048]{1,0:T(8,128)S(1)}, f32[64,2048]{1,0:T(8,128)S(1)}, bf16[64,2048]{1,0:T(8,128)(2,1)S(1)}, bf16[64,2048]{1,0:T(8,128)(2,1)S(1)}) custom-call(bf16[64,2048]{1,0:T(8,128)(2,1)S(1)} %get-tuple-element.69.refs_0_, bf16[64,2048]{1,0:T(8,128)(2,1)S(1)} %collective-permute-done.21.refs_1_, ...), custom_call_target="tpu_custom_call" | custom-call | tf_op jit(solution)/shard_map/pallas_call | solution.py:27
  84.6 1.8 %collective-permute-start.25 = (bf16[64,2048]{1,0:T(8,128)(2,1)S(1)}, bf16[64,2048]{1,0:T(8,128)(2,1)S(1)}, u32[]{:S(2)}, u32[]{:S(2)}) collective-permute-start(bf16[64,2048]{1,0:T(8,128)(2,1)S(1)} %get-tuple-element.76.refs_1_), channel_id=1, source_target_pairs={{0,2},{1,3},{2,0},{3,1},{4,6},{5,7},{6,4},{7,5},{8,10},{9,11},{10,... | collective-permute-start | bytes 786440 | tf_op jit(solution)/shard_map/ppermute | solution.py:49
  86.5 6.7 %collective-permute-done.25.refs_2_ = bf16[64,2048]{1,0:T(8,128)(2,1)S(1)} collective-permute-done((bf16[64,2048]{1,0:T(8,128)(2,1)S(1)}, bf16[64,2048]{1,0:T(8,128)(2,1)S(1)}, u32[]{:S(2)}, u32[]{:S(2)}) %collective-permute-start.25) | collective-permute-done | bytes 262176 | tf_op jit(solution)/shard_map/ppermute | solution.py:49
  93.2 0.5 collective-permute-start.29
  93.7 1.7 %collective-permute-start.30 = (bf16[64,2048]{1,0:T(8,128)(2,1)S(1)}, bf16[64,2048]{1,0:T(8,128)(2,1)S(1)}, u32[]{:S(2)}, u32[]{:S(2)}) collective-permute-start(bf16[64,2048]{1,0:T(8,128)(2,1)S(1)} %shard_map.68.refs_0_), channel_id=1, source_target_pairs={{0,2},{1,3},{2,0},{3,1},{4,6},{5,7},{6,4},{7,5},{8,10},{9,11},{10,... | collective-permute-start | bytes 786440 | tf_op jit(solution)/shard_map/ppermute | solution.py:49
  95.4 2.6 %shard_map.69 = (f32[64,2048]{1,0:T(8,128)S(1)}, f32[64,2048]{1,0:T(8,128)S(1)}, bf16[64,2048]{1,0:T(8,128)(2,1)S(1)}, bf16[64,2048]{1,0:T(8,128)(2,1)S(1)}) custom-call(bf16[64,2048]{1,0:T(8,128)(2,1)S(1)} %shard_map.68.refs_0_, bf16[64,2048]{1,0:T(8,128)(2,1)S(1)} %get-tuple-element.76.refs_1_, bf16[64,2048]{1,0:T(8,128)(2,1)S(1)} %collective-permute-done.25.refs_2_, ...), custom_call_target="tpu_custom_call" | custom-call | tf_op jit(solution)/shard_map/pallas_call | solution.py:27
  98.1 0.5 collective-permute-start.28
  98.6 3.3 %collective-permute-done.30.refs_2_ = bf16[64,2048]{1,0:T(8,128)(2,1)S(1)} collective-permute-done((bf16[64,2048]{1,0:T(8,128)(2,1)S(1)}, bf16[64,2048]{1,0:T(8,128)(2,1)S(1)}, u32[]{:S(2)}, u32[]{:S(2)}) %collective-permute-start.30) | collective-permute-done | bytes 262176 | tf_op jit(solution)/shard_map/ppermute | solution.py:49
  102.1 1.8 %collective-permute-start.32 = (bf16[64,2048]{1,0:T(8,128)(2,1)S(1)}, bf16[64,2048]{1,0:T(8,128)(2,1)S(1)}, u32[]{:S(2)}, u32[]{:S(2)}) collective-permute-start(bf16[64,2048]{1,0:T(8,128)(2,1)S(1)} %shard_map.71), channel_id=1, source_target_pairs={{0,2},{1,3},{2,0},{3,1},{4,6},{5,7},{6,4},{7,5},{8,10},{9,11},{10,... | collective-permute-start | bytes 786440 | tf_op jit(solution)/shard_map/ppermute | solution.py:49
  103.9 2.3 %collective-permute-start.35 = (bf16[32,2048]{1,0:T(8,128)(2,1)S(1)}, bf16[32,2048]{1,0:T(8,128)(2,1)S(1)}, u32[]{:S(2)}, u32[]{:S(2)}) collective-permute-start(bf16[32,2048]{1,0:T(8,128)(2,1)S(1)} %get-tuple-element.83.refs_0_), channel_id=1, source_target_pairs={{0,12},{1,13},{2,14},{3,15},{4,8},{5,9},{6,10},{7,11},{8,4},{9,5},... | collective-permute-start | bytes 393224 | tf_op jit(solution)/shard_map/ppermute | solution.py:49
  106.1 1.9 %collective-permute-start.34 = (bf16[32,2048]{1,0:T(8,128)(2,1)S(1)}, bf16[32,2048]{1,0:T(8,128)(2,1)S(1)}, u32[]{:S(2)}, u32[]{:S(2)}) collective-permute-start(bf16[32,2048]{1,0:T(8,128)(2,1)S(1)} %get-tuple-element.88), channel_id=1, source_target_pairs={{0,8},{1,9},{2,10},{3,11},{4,12},{5,13},{6,14},{7,15},{8,0},{9,1},... | collective-permute-start | bytes 393224 | tf_op jit(solution)/shard_map/ppermute | solution.py:49
  108.0 1.5 %collective-permute-done.32.refs_2_ = bf16[64,2048]{1,0:T(8,128)(2,1)S(1)} collective-permute-done((bf16[64,2048]{1,0:T(8,128)(2,1)S(1)}, bf16[64,2048]{1,0:T(8,128)(2,1)S(1)}, u32[]{:S(2)}, u32[]{:S(2)}) %collective-permute-start.32) | collective-permute-done | bytes 262176 | tf_op jit(solution)/shard_map/ppermute | solution.py:49
  109.6 2.8 %collective-permute-start.33 = (bf16[32,2048]{1,0:T(8,128)(2,1)S(1)}, bf16[32,2048]{1,0:T(8,128)(2,1)S(1)}, u32[]{:S(2)}, u32[]{:S(2)}) collective-permute-start(bf16[32,2048]{1,0:T(8,128)(2,1)S(1)} %get-tuple-element.87), channel_id=1, source_target_pairs={{0,4},{1,5},{2,6},{3,7},{4,0},{5,1},{6,2},{7,3},{8,12},{9,13},{10,... | collective-permute-start | bytes 393224 | tf_op jit(solution)/shard_map/ppermute | solution.py:49
  112.3 6.0 %collective-permute-done.34.refs_3_ = bf16[32,2048]{1,0:T(8,128)(2,1)S(1)} collective-permute-done((bf16[32,2048]{1,0:T(8,128)(2,1)S(1)}, bf16[32,2048]{1,0:T(8,128)(2,1)S(1)}, u32[]{:S(2)}, u32[]{:S(2)}) %collective-permute-start.34) | collective-permute-done | bytes 131104 | tf_op jit(solution)/shard_map/ppermute | solution.py:49
  118.4 0.8 shard_map.73
  (47 shorter events, 1.9 us)
Async XLA Ops:
  1.2 14.6 %collective-permute-start = (bf16[32,2176]{1,0:T(8,128)(2,1)S(1)}, bf16[32,2176]{1,0:T(8,128)(2,1)S(1)}, u32[]{:S(2)}, u32[]{:S(2)}) collective-permute-start(bf16[32,2176]{1,0:T(8,128)(2,1)S(1)} %shard_map.56.refs_3_), channel_id=1, source_target_pairs={{0,8},{1,9},{2,10},{3,11},{4,12},{5,13},{6,14},{7,15},{8,0},{9,1},... | collective-permute-start | bytes 417800 | tf_op jit(solution)/shard_map/ppermute | solution.py:49
  5.3 10.5 %collective-permute-start.1 = (bf16[32,2176]{1,0:T(8,128)(2,1)S(1)}, bf16[32,2176]{1,0:T(8,128)(2,1)S(1)}, u32[]{:S(2)}, u32[]{:S(2)}) collective-permute-start(bf16[32,2176]{1,0:T(8,128)(2,1)S(1)} %shard_map.56.refs_3_), channel_id=1, source_target_pairs={{0,12},{1,13},{2,14},{3,15},{4,8},{5,9},{6,10},{7,11},{8,4},{9,5},... | collective-permute-start | bytes 417800 | tf_op jit(solution)/shard_map/ppermute | solution.py:49
  6.7 9.7 %collective-permute-start.2 = (bf16[32,2176]{1,0:T(8,128)(2,1)S(1)}, bf16[32,2176]{1,0:T(8,128)(2,1)S(1)}, u32[]{:S(2)}, u32[]{:S(2)}) collective-permute-start(bf16[32,2176]{1,0:T(8,128)(2,1)S(1)} %shard_map.56.refs_3_), channel_id=1, source_target_pairs={{0,4},{1,5},{2,6},{3,7},{4,0},{5,1},{6,2},{7,3},{8,12},{9,13},{10,... | collective-permute-start | bytes 417800 | tf_op jit(solution)/shard_map/ppermute | solution.py:49
  16.4 6.6 %collective-permute-start.3 = (bf16[64,2176]{1,0:T(8,128)(2,1)S(1)}, bf16[64,2176]{1,0:T(8,128)(2,1)S(1)}, u32[]{:S(2)}, u32[]{:S(2)}) collective-permute-start(bf16[64,2176]{1,0:T(8,128)(2,1)S(1)} %get-tuple-element.48.refs_0_), channel_id=1, source_target_pairs={{0,2},{1,3},{2,0},{3,1},{4,6},{5,7},{6,4},{7,5},{8,10},{9,11},{10,... | collective-permute-start | bytes 835592 | tf_op jit(solution)/shard_map/ppermute | solution.py:49
  18.0 6.6 %collective-permute-start.4 = (bf16[64,2176]{1,0:T(8,128)(2,1)S(1)}, bf16[64,2176]{1,0:T(8,128)(2,1)S(1)}, u32[]{:S(2)}, u32[]{:S(2)}) collective-permute-start(bf16[64,2176]{1,0:T(8,128)(2,1)S(1)} %get-tuple-element.48.refs_0_), channel_id=1, source_target_pairs={{0,1},{1,0},{2,3},{3,2},{4,5},{5,4},{6,7},{7,6},{8,9},{9,8},{10,11... | collective-permute-start | bytes 835592 | tf_op jit(solution)/shard_map/ppermute | solution.py:49
  23.0 1.6 %collective-permute-start.5 = (bf16[64,2176]{1,0:T(8,128)(2,1)S(1)}, bf16[64,2176]{1,0:T(8,128)(2,1)S(1)}, u32[]{:S(2)}, u32[]{:S(2)}) collective-permute-start(bf16[64,2176]{1,0:T(8,128)(2,1)S(1)} %collective-permute-done.3.refs_1_), channel_id=1, source_target_pairs={{0,1},{1,0},{2,3},{3,2},{4,5},{5,4},{6,7},{7,6},{8,9},{9,8},{10,11... | collective-permute-start | bytes 835592 | tf_op jit(solution)/shard_map/ppermute | solution.py:49
  23.0 9.1 %collective-permute-start.7 = (bf16[64,2176]{1,0:T(8,128)(2,1)S(1)}, bf16[64,2176]{1,0:T(8,128)(2,1)S(1)}, u32[]{:S(2)}, u32[]{:S(2)}) collective-permute-start(bf16[64,2176]{1,0:T(8,128)(2,1)S(1)} %get-tuple-element.54.refs_1_), channel_id=1, source_target_pairs={{0,2},{1,3},{2,0},{3,1},{4,6},{5,7},{6,4},{7,5},{8,10},{9,11},{10,... | collective-permute-start | bytes 835592 | tf_op jit(solution)/shard_map/ppermute | solution.py:49
  27.2 1.6 %collective-permute-start.6 = (bf16[64,2048]{1,0:T(8,128)(2,1)S(1)}, bf16[64,2048]{1,0:T(8,128)(2,1)S(1)}, u32[]{:S(2)}, u32[]{:S(2)}) collective-permute-start(bf16[64,2048]{1,0:T(8,128)(2,1)S(1)} %get-tuple-element.52), channel_id=1, source_target_pairs={{0,1},{1,0},{2,3},{3,2},{4,5},{5,4},{6,7},{7,6},{8,9},{9,8},{10,11... | collective-permute-start | bytes 786440 | tf_op jit(solution)/shard_map/ppermute | solution.py:49
  27.5 6.7 %collective-permute-start.8 = (bf16[64,2176]{1,0:T(8,128)(2,1)S(1)}, bf16[64,2176]{1,0:T(8,128)(2,1)S(1)}, u32[]{:S(2)}, u32[]{:S(2)}) collective-permute-start(bf16[64,2176]{1,0:T(8,128)(2,1)S(1)} %get-tuple-element.54.refs_1_), channel_id=1, source_target_pairs={{0,1},{1,0},{2,3},{3,2},{4,5},{5,4},{6,7},{7,6},{8,9},{9,8},{10,11... | collective-permute-start | bytes 835592 | tf_op jit(solution)/shard_map/ppermute | solution.py:49
  32.1 2.1 %collective-permute-start.9 = (bf16[64,2176]{1,0:T(8,128)(2,1)S(1)}, bf16[64,2176]{1,0:T(8,128)(2,1)S(1)}, u32[]{:S(2)}, u32[]{:S(2)}) collective-permute-start(bf16[64,2176]{1,0:T(8,128)(2,1)S(1)} %collective-permute-done.7.refs_2_), channel_id=1, source_target_pairs={{0,1},{1,0},{2,3},{3,2},{4,5},{5,4},{6,7},{7,6},{8,9},{9,8},{10,11... | collective-permute-start | bytes 835592 | tf_op jit(solution)/shard_map/ppermute | solution.py:49
  32.1 4.8 %collective-permute-start.11 = (bf16[64,2048]{1,0:T(8,128)(2,1)S(1)}, bf16[64,2048]{1,0:T(8,128)(2,1)S(1)}, u32[]{:S(2)}, u32[]{:S(2)}) collective-permute-start(bf16[64,2048]{1,0:T(8,128)(2,1)S(1)} %get-tuple-element.60), channel_id=1, source_target_pairs={{0,1},{1,0},{2,3},{3,2},{4,5},{5,4},{6,7},{7,6},{8,9},{9,8},{10,11... | collective-permute-start | bytes 786440 | tf_op jit(solution)/shard_map/ppermute | solution.py:49
  32.6 8.2 %collective-permute-start.12 = (bf16[64,2048]{1,0:T(8,128)(2,1)S(1)}, bf16[64,2048]{1,0:T(8,128)(2,1)S(1)}, u32[]{:S(2)}, u32[]{:S(2)}) collective-permute-start(bf16[64,2048]{1,0:T(8,128)(2,1)S(1)} %shard_map.59.refs_0_), channel_id=1, source_target_pairs={{0,2},{1,3},{2,0},{3,1},{4,6},{5,7},{6,4},{7,5},{8,10},{9,11},{10,... | collective-permute-start | bytes 786440 | tf_op jit(solution)/shard_map/ppermute | solution.py:49
  36.8 4.2 %collective-permute-start.13 = (bf16[64,2048]{1,0:T(8,128)(2,1)S(1)}, bf16[64,2048]{1,0:T(8,128)(2,1)S(1)}, u32[]{:S(2)}, u32[]{:S(2)}) collective-permute-start(bf16[64,2048]{1,0:T(8,128)(2,1)S(1)} %get-tuple-element.63), channel_id=1, source_target_pairs={{0,1},{1,0},{2,3},{3,2},{4,5},{5,4},{6,7},{7,6},{8,9},{9,8},{10,11... | collective-permute-start | bytes 786440 | tf_op jit(solution)/shard_map/ppermute | solution.py:49
  40.9 8.1 %collective-permute-start.10 = (bf16[64,2048]{1,0:T(8,128)(2,1)S(1)}, bf16[64,2048]{1,0:T(8,128)(2,1)S(1)}, u32[]{:S(2)}, u32[]{:S(2)}) collective-permute-start(bf16[64,2048]{1,0:T(8,128)(2,1)S(1)} %get-tuple-element.58), channel_id=1, source_target_pairs={{0,1},{1,0},{2,3},{3,2},{4,5},{5,4},{6,7},{7,6},{8,9},{9,8},{10,11... | collective-permute-start | bytes 786440 | tf_op jit(solution)/shard_map/ppermute | solution.py:49
  41.0 8.8 %collective-permute-start.14 = (bf16[64,2048]{1,0:T(8,128)(2,1)S(1)}, bf16[64,2048]{1,0:T(8,128)(2,1)S(1)}, u32[]{:S(2)}, u32[]{:S(2)}) collective-permute-start(bf16[64,2048]{1,0:T(8,128)(2,1)S(1)} %shard_map.63), channel_id=1, source_target_pairs={{0,2},{1,3},{2,0},{3,1},{4,6},{5,7},{6,4},{7,5},{8,10},{9,11},{10,... | collective-permute-start | bytes 786440 | tf_op jit(solution)/shard_map/ppermute | solution.py:49
  42.7 16.8 %collective-permute-start.17 = (bf16[32,2048]{1,0:T(8,128)(2,1)S(1)}, bf16[32,2048]{1,0:T(8,128)(2,1)S(1)}, u32[]{:S(2)}, u32[]{:S(2)}) collective-permute-start(bf16[32,2048]{1,0:T(8,128)(2,1)S(1)} %get-tuple-element.61.refs_0_), channel_id=1, source_target_pairs={{0,12},{1,13},{2,14},{3,15},{4,8},{5,9},{6,10},{7,11},{8,4},{9,5},... | collective-permute-start | bytes 393224 | tf_op jit(solution)/shard_map/ppermute | solution.py:49
  47.1 12.4 %collective-permute-start.16 = (bf16[32,2048]{1,0:T(8,128)(2,1)S(1)}, bf16[32,2048]{1,0:T(8,128)(2,1)S(1)}, u32[]{:S(2)}, u32[]{:S(2)}) collective-permute-start(bf16[32,2048]{1,0:T(8,128)(2,1)S(1)} %get-tuple-element.66), channel_id=1, source_target_pairs={{0,8},{1,9},{2,10},{3,11},{4,12},{5,13},{6,14},{7,15},{8,0},{9,1},... | collective-permute-start | bytes 393224 | tf_op jit(solution)/shard_map/ppermute | solution.py:49
  49.9 10.7 %copy-start = (bf16[2,16,2048]{2,1,0:T(8,128)(2,1)S(1)}, bf16[2,16,2048]{2,1,0:T(8,128)(2,1)}, u32[]{:S(2)}) copy-start(bf16[2,16,2048]{2,1,0:T(8,128)(2,1)} %param.5) | copy-start | bytes 393220
  49.9 10.7 %copy-start.1 = (f32[2,2048]{1,0:T(2,128)S(1)}, f32[2,2048]{1,0:T(2,128)}, u32[]{:S(2)}) copy-start(f32[2,2048]{1,0:T(2,128)} %refs_2_.5) | copy-start | bytes 49156
  49.9 10.6 %collective-permute-start.15 = (bf16[32,2048]{1,0:T(8,128)(2,1)S(1)}, bf16[32,2048]{1,0:T(8,128)(2,1)S(1)}, u32[]{:S(2)}, u32[]{:S(2)}) collective-permute-start(bf16[32,2048]{1,0:T(8,128)(2,1)S(1)} %get-tuple-element.65), channel_id=1, source_target_pairs={{0,4},{1,5},{2,6},{3,7},{4,0},{5,1},{6,2},{7,3},{8,12},{9,13},{10,... | collective-permute-start | bytes 393224 | tf_op jit(solution)/shard_map/ppermute | solution.py:49
  60.8 12.0 %collective-permute-start.18 = (bf16[32,2048]{1,0:T(8,128)(2,1)S(1)}, bf16[32,2048]{1,0:T(8,128)(2,1)S(1)}, u32[]{:S(2)}, u32[]{:S(2)}) collective-permute-start(bf16[32,2048]{1,0:T(8,128)(2,1)S(1)} %get-tuple-element.68.refs_3_), channel_id=1, source_target_pairs={{0,8},{1,9},{2,10},{3,11},{4,12},{5,13},{6,14},{7,15},{8,0},{9,1},... | collective-permute-start | bytes 393224 | tf_op jit(solution)/shard_map/ppermute | solution.py:49
  62.3 10.5 %collective-permute-start.19 = (bf16[32,2048]{1,0:T(8,128)(2,1)S(1)}, bf16[32,2048]{1,0:T(8,128)(2,1)S(1)}, u32[]{:S(2)}, u32[]{:S(2)}) collective-permute-start(bf16[32,2048]{1,0:T(8,128)(2,1)S(1)} %get-tuple-element.68.refs_3_), channel_id=1, source_target_pairs={{0,12},{1,13},{2,14},{3,15},{4,8},{5,9},{6,10},{7,11},{8,4},{9,5},... | collective-permute-start | bytes 393224 | tf_op jit(solution)/shard_map/ppermute | solution.py:49
  64.3 9.0 %collective-permute-start.20 = (bf16[32,2048]{1,0:T(8,128)(2,1)S(1)}, bf16[32,2048]{1,0:T(8,128)(2,1)S(1)}, u32[]{:S(2)}, u32[]{:S(2)}) collective-permute-start(bf16[32,2048]{1,0:T(8,128)(2,1)S(1)} %get-tuple-element.68.refs_3_), channel_id=1, source_target_pairs={{0,4},{1,5},{2,6},{3,7},{4,0},{5,1},{6,2},{7,3},{8,12},{9,13},{10,... | collective-permute-start | bytes 393224 | tf_op jit(solution)/shard_map/ppermute | solution.py:49
  73.3 6.9 %collective-permute-start.21 = (bf16[64,2048]{1,0:T(8,128)(2,1)S(1)}, bf16[64,2048]{1,0:T(8,128)(2,1)S(1)}, u32[]{:S(2)}, u32[]{:S(2)}) collective-permute-start(bf16[64,2048]{1,0:T(8,128)(2,1)S(1)} %get-tuple-element.69.refs_0_), channel_id=1, source_target_pairs={{0,2},{1,3},{2,0},{3,1},{4,6},{5,7},{6,4},{7,5},{8,10},{9,11},{10,... | collective-permute-start | bytes 786440 | tf_op jit(solution)/shard_map/ppermute | solution.py:49
  75.1 5.1 %collective-permute-start.22 = (bf16[64,2048]{1,0:T(8,128)(2,1)S(1)}, bf16[64,2048]{1,0:T(8,128)(2,1)S(1)}, u32[]{:S(2)}, u32[]{:S(2)}) collective-permute-start(bf16[64,2048]{1,0:T(8,128)(2,1)S(1)} %get-tuple-element.69.refs_0_), channel_id=1, source_target_pairs={{0,1},{1,0},{2,3},{3,2},{4,5},{5,4},{6,7},{7,6},{8,9},{9,8},{10,11... | collective-permute-start | bytes 786440 | tf_op jit(solution)/shard_map/ppermute | solution.py:49
  80.2 1.5 %collective-permute-start.23 = (bf16[64,2048]{1,0:T(8,128)(2,1)S(1)}, bf16[64,2048]{1,0:T(8,128)(2,1)S(1)}, u32[]{:S(2)}, u32[]{:S(2)}) collective-permute-start(bf16[64,2048]{1,0:T(8,128)(2,1)S(1)} %collective-permute-done.21.refs_1_), channel_id=1, source_target_pairs={{0,1},{1,0},{2,3},{3,2},{4,5},{5,4},{6,7},{7,6},{8,9},{9,8},{10,11... | collective-permute-start | bytes 786440 | tf_op jit(solution)/shard_map/ppermute | solution.py:49
  84.4 2.0 %collective-permute-start.24 = (bf16[64,2048]{1,0:T(8,128)(2,1)S(1)}, bf16[64,2048]{1,0:T(8,128)(2,1)S(1)}, u32[]{:S(2)}, u32[]{:S(2)}) collective-permute-start(bf16[64,2048]{1,0:T(8,128)(2,1)S(1)} %get-tuple-element.74), channel_id=1, source_target_pairs={{0,1},{1,0},{2,3},{3,2},{4,5},{5,4},{6,7},{7,6},{8,9},{9,8},{10,11... | collective-permute-start | bytes 786440 | tf_op jit(solution)/shard_map/ppermute | solution.py:49
  84.6 8.6 %collective-permute-start.25 = (bf16[64,2048]{1,0:T(8,128)(2,1)S(1)}, bf16[64,2048]{1,0:T(8,128)(2,1)S(1)}, u32[]{:S(2)}, u32[]{:S(2)}) collective-permute-start(bf16[64,2048]{1,0:T(8,128)(2,1)S(1)} %get-tuple-element.76.refs_1_), channel_id=1, source_target_pairs={{0,2},{1,3},{2,0},{3,1},{4,6},{5,7},{6,4},{7,5},{8,10},{9,11},{10,... | collective-permute-start | bytes 786440 | tf_op jit(solution)/shard_map/ppermute | solution.py:49
  86.4 9.1 %collective-permute-start.26 = (bf16[64,2048]{1,0:T(8,128)(2,1)S(1)}, bf16[64,2048]{1,0:T(8,128)(2,1)S(1)}, u32[]{:S(2)}, u32[]{:S(2)}) collective-permute-start(bf16[64,2048]{1,0:T(8,128)(2,1)S(1)} %get-tuple-element.76.refs_1_), channel_id=1, source_target_pairs={{0,1},{1,0},{2,3},{3,2},{4,5},{5,4},{6,7},{7,6},{8,9},{9,8},{10,11... | collective-permute-start | bytes 786440 | tf_op jit(solution)/shard_map/ppermute | solution.py:49
  93.2 2.3 %collective-permute-start.27 = (bf16[64,2048]{1,0:T(8,128)(2,1)S(1)}, bf16[64,2048]{1,0:T(8,128)(2,1)S(1)}, u32[]{:S(2)}, u32[]{:S(2)}) collective-permute-start(bf16[64,2048]{1,0:T(8,128)(2,1)S(1)} %collective-permute-done.25.refs_2_), channel_id=1, source_target_pairs={{0,1},{1,0},{2,3},{3,2},{4,5},{5,4},{6,7},{7,6},{8,9},{9,8},{10,11... | collective-permute-start | bytes 786440 | tf_op jit(solution)/shard_map/ppermute | solution.py:49
  93.2 5.5 %collective-permute-start.29 = (bf16[64,2048]{1,0:T(8,128)(2,1)S(1)}, bf16[64,2048]{1,0:T(8,128)(2,1)S(1)}, u32[]{:S(2)}, u32[]{:S(2)}) collective-permute-start(bf16[64,2048]{1,0:T(8,128)(2,1)S(1)} %get-tuple-element.82), channel_id=1, source_target_pairs={{0,1},{1,0},{2,3},{3,2},{4,5},{5,4},{6,7},{7,6},{8,9},{9,8},{10,11... | collective-permute-start | bytes 786440 | tf_op jit(solution)/shard_map/ppermute | solution.py:49
  93.7 8.2 %collective-permute-start.30 = (bf16[64,2048]{1,0:T(8,128)(2,1)S(1)}, bf16[64,2048]{1,0:T(8,128)(2,1)S(1)}, u32[]{:S(2)}, u32[]{:S(2)}) collective-permute-start(bf16[64,2048]{1,0:T(8,128)(2,1)S(1)} %shard_map.68.refs_0_), channel_id=1, source_target_pairs={{0,2},{1,3},{2,0},{3,1},{4,6},{5,7},{6,4},{7,5},{8,10},{9,11},{10,... | collective-permute-start | bytes 786440 | tf_op jit(solution)/shard_map/ppermute | solution.py:49
  98.1 3.9 %collective-permute-start.31 = (bf16[64,2048]{1,0:T(8,128)(2,1)S(1)}, bf16[64,2048]{1,0:T(8,128)(2,1)S(1)}, u32[]{:S(2)}, u32[]{:S(2)}) collective-permute-start(bf16[64,2048]{1,0:T(8,128)(2,1)S(1)} %get-tuple-element.85), channel_id=1, source_target_pairs={{0,1},{1,0},{2,3},{3,2},{4,5},{5,4},{6,7},{7,6},{8,9},{9,8},{10,11... | collective-permute-start | bytes 786440 | tf_op jit(solution)/shard_map/ppermute | solution.py:49
  98.1 9.9 %collective-permute-start.28 = (bf16[64,2048]{1,0:T(8,128)(2,1)S(1)}, bf16[64,2048]{1,0:T(8,128)(2,1)S(1)}, u32[]{:S(2)}, u32[]{:S(2)}) collective-permute-start(bf16[64,2048]{1,0:T(8,128)(2,1)S(1)} %get-tuple-element.80), channel_id=1, source_target_pairs={{0,1},{1,0},{2,3},{3,2},{4,5},{5,4},{6,7},{7,6},{8,9},{9,8},{10,11... | collective-permute-start | bytes 786440 | tf_op jit(solution)/shard_map/ppermute | solution.py:49
  102.1 7.4 %collective-permute-start.32 = (bf16[64,2048]{1,0:T(8,128)(2,1)S(1)}, bf16[64,2048]{1,0:T(8,128)(2,1)S(1)}, u32[]{:S(2)}, u32[]{:S(2)}) collective-permute-start(bf16[64,2048]{1,0:T(8,128)(2,1)S(1)} %shard_map.71), channel_id=1, source_target_pairs={{0,2},{1,3},{2,0},{3,1},{4,6},{5,7},{6,4},{7,5},{8,10},{9,11},{10,... | collective-permute-start | bytes 786440 | tf_op jit(solution)/shard_map/ppermute | solution.py:49
  103.9 14.5 %collective-permute-start.35 = (bf16[32,2048]{1,0:T(8,128)(2,1)S(1)}, bf16[32,2048]{1,0:T(8,128)(2,1)S(1)}, u32[]{:S(2)}, u32[]{:S(2)}) collective-permute-start(bf16[32,2048]{1,0:T(8,128)(2,1)S(1)} %get-tuple-element.83.refs_0_), channel_id=1, source_target_pairs={{0,12},{1,13},{2,14},{3,15},{4,8},{5,9},{6,10},{7,11},{8,4},{9,5},... | collective-permute-start | bytes 393224 | tf_op jit(solution)/shard_map/ppermute | solution.py:49
  106.1 12.2 %collective-permute-start.34 = (bf16[32,2048]{1,0:T(8,128)(2,1)S(1)}, bf16[32,2048]{1,0:T(8,128)(2,1)S(1)}, u32[]{:S(2)}, u32[]{:S(2)}) collective-permute-start(bf16[32,2048]{1,0:T(8,128)(2,1)S(1)} %get-tuple-element.88), channel_id=1, source_target_pairs={{0,8},{1,9},{2,10},{3,11},{4,12},{5,13},{6,14},{7,15},{8,0},{9,1},... | collective-permute-start | bytes 393224 | tf_op jit(solution)/shard_map/ppermute | solution.py:49
  109.6 8.8 %collective-permute-start.33 = (bf16[32,2048]{1,0:T(8,128)(2,1)S(1)}, bf16[32,2048]{1,0:T(8,128)(2,1)S(1)}, u32[]{:S(2)}, u32[]{:S(2)}) collective-permute-start(bf16[32,2048]{1,0:T(8,128)(2,1)S(1)} %get-tuple-element.87), channel_id=1, source_target_pairs={{0,4},{1,5},{2,6},{3,7},{4,0},{5,1},{6,2},{7,3},{8,12},{9,13},{10,... | collective-permute-start | bytes 393224 | tf_op jit(solution)/shard_map/ppermute | solution.py:49

commit v6 on v5

--- a/solution.py
+++ b/solution.py
@@ -10,6 +10,7 @@
 eps = 1e-06
 LANES = 128
 MIB = 2**20
+WAIT = 6 * 10**9
 VMEM = pl.BlockSpec(memory_space=pltpu.VMEM)
 ANY = pl.BlockSpec(memory_space=pl.ANY)
 bf16, f32 = jnp.bfloat16, jnp.float32
@@ -21,7 +22,7 @@
     return lax.ppermute(value, axis, [(source, source + steps) for source in range(initial, last)])
 
 
-def call(kernel, outs, specs, *operands, scratch=(), limit=8, after=()):
+def call(kernel, outs, specs, *operands, scratch=(), limit=8, after=(), weight=0):
     shapes = tuple(jax.ShapeDtypeStruct(shape, dtype) for shape, dtype in outs)
     operands = (*after, *operands)
     return pl.pallas_call(
@@ -31,7 +32,7 @@
         out_specs=(VMEM,) * len(outs),
         scratch_shapes=scratch,
         compiler_params=pltpu.CompilerParams(vmem_limit_bytes=limit * MIB),
-        cost_estimate=pl.CostEstimate(flops=0, bytes_accessed=0, transcendentals=0),
+        cost_estimate=pl.CostEstimate(flops=weight, bytes_accessed=0, transcendentals=0),
     )(*operands)
 
 
@@ -49,35 +50,27 @@
     return lax.ppermute(value, "expert", [(i, partner(i)) for i in range(count)])
 
 
-def join_kernel(count, *refs):
-    parts, wholes = refs[:count], refs[count:]
-    rows, size = parts[0].shape[0], count // len(wholes)
+def join_kernel(*refs):
+    *parts, whole = refs
+    rows = parts[0].shape[0]
     for k, part in enumerate(parts):
-        wholes[k // size][k % size * rows : (k % size + 1) * rows] = part[...]
+        whole[k * rows : (k + 1) * rows] = part[...]
+
+
+def join_rows(parts, after, weight):
+    tokens, width = parts[0].shape
+    return call(
+        join_kernel,
+        [((len(parts) * tokens, width), parts[0].dtype)],
+        [VMEM] * len(parts),
+        *parts,
+        after=after,
+        weight=weight,
+    )[0]
 
 
 def held(value, until):
-    return lax.optimization_barrier((value, until))[0] if until is not None else value
-
-
-def gather_rows(rows, after):
-    far = lax.axis_size("expert") // 4
-    tokens, width = rows.shape
-    parts = [rows] + [swap(rows, 4, k, far) for k in range(1, far)]
-    shape = (far // 2 * tokens, width)
-    batches, beside = [], None
-    for near in call(
-        functools.partial(join_kernel, far),
-        [(shape, rows.dtype)] * 2,
-        [VMEM] * far,
-        *parts[far // 2 :],
-        *parts[: far // 2],
-        after=after,
-    ):
-        near = held(near, beside)
-        beside = swap(near, 2, 1, 2)
-        batches.append([near, beside])
-    return batches
+    return lax.optimization_barrier((value, until))[0]
 
 
 def sum_kernel(mine, arrived, total):
@@ -106,13 +99,11 @@
     return mine_near, arrived_near, leaving
 
 
-def split_rows(left, distances, tokens):
+def split_rows(mine_near, arrived_near, beside, distances, tokens):
     far = lax.axis_size("expert") // 4
-    mine_near, arrived_near, leaving = left
-    beside = swap(leaving, 2, 1, 2, True)
     pieces = call(
         split_kernel,
-        [((tokens, leaving.shape[1]), bf16 if k else f32) for k in distances],
+        [((tokens, beside.shape[1]), bf16 if k else f32) for k in distances],
         [VMEM] * 3,
         mine_near,
         arrived_near,
@@ -306,20 +297,29 @@
 
 def run_layer(rows, routed, first_column, weights, loaded=()):
     far, tokens = lax.axis_size("expert") // 4, rows.shape[0]
-    columns, returned, after, worked = [], [], (), ()
-    distances = [range(far // 2, far), range(far // 2)]
-    for place, (near, beside) in enumerate(gather_rows(rows, loaded)):
-        beside = held(beside, left[2] if place else None)
+    routed = routed or [None, None]
+    half = far // 2
+    sent = [rows] + [swap(rows, 4, k, far) for k in range(1, far)]
+    first = join_rows(sent[:half], loaded, 0)
+    first_beside = swap(first, 2, 1, 2)
+    second = join_rows(sent[half:], (first,), WAIT)
+    second_beside = swap(second, 2, 1, 2)
+
+    def worked(near, beside, routed, until):
+        beside = held(beside, until)
         parts = [near, beside, swap(near, 1, 1, 2), swap(beside, 1, 1, 2)]
-        outs, kept = run_expert(
-            parts, None if routed is None else routed[place], first_column, weights, worked
-        )
-        columns.append(kept)
-        left = leave_pair(outs, after)
-        arrived, last = split_rows(left, distances[place], tokens)
-        returned = arrived + returned
-        after, worked = (last,), (left[2],)
-    return returned, columns, (outs[0],)
+        outs, columns = run_expert(parts, routed, first_column, weights, (until,))
+        return outs, columns
+
+    outs, first_columns = worked(first, first_beside, routed[0], second)
+    mine, near, leaving = leave_pair(outs, ())
+    outs2, second_columns = worked(second, second_beside, routed[1], outs[0])
+    first_back = swap(held(leaving, second_beside), 2, 1, 2, True)
+    arrived, last = split_rows(mine, near, first_back, range(half), tokens)
+    mine2, near2, leaving2 = leave_pair(outs2, (last,))
+    second_back = swap(leaving2, 2, 1, 2, True)
+    arrived += split_rows(mine2, near2, second_back, range(half, far), tokens)[0]
+    return arrived, [first_columns, second_columns], (outs2[0],)
 
 
 def close_rows(layer_no, current, gain, returned, after=()):

time: 119 us -> 113 us (0.950)
  starting transfers between devices: 43.4 us -> 36.1 us
    ppermute x36, starting transfers between devices: 43.4 us -> 36.1 us  [swap(): lax.ppermute(value, 'expert', [(i, partner(i)) for i in range(count)])]
    pallas_call x19 -> x21, Pallas kernels: 20.7 us -> 20.8 us  [call(): pl.pallas_call(lambda *refs: kernel(*refs[len(after):]), out_shape=shapes...]
  transfers between devices with their start and end apart: 36 -> 36, of which waited for: 17 -> 14; matrix products, arithmetic and copies ran while one was open for 0% -> 0% of each run, Pallas kernels for 13% -> 16%
where the time goes in v6:
time: 113 us; the launch traced here: 112 us
  waiting for transfers between devices  55.4 us (49%)
  starting transfers between devices  36.1 us (32%)
  Pallas kernels  20.8 us (18%)
    ppermute x36, waiting for transfers between devices, swap(): lax.ppermute(value, 'expert', [(i, partner(i)) for i in range(count)])  55.4 us
    ppermute x36, starting transfers between devices, swap(): lax.ppermute(value, 'expert', [(i, partner(i)) for i in range(count)])  36.1 us
    pallas_call x21, Pallas kernels, call(): pl.pallas_call(lambda *refs: kernel(*refs[len(after):]), out_shape=shapes...  20.8 us
  transfers between devices with their start and end apart: 36, of which 14 were waited for; matrix products, arithmetic and copies ran while one was open for 0% of the time, Pallas kernels for 16%

profile of v6, /device:TPU:0, one launch (start us, length us, event | category | flops | bytes accessed | tf_op | source)
XLA Modules:
  0.0 112.5 jit_solution(1643794919041974861)
XLA Ops:
  0.0 1.2 %shard_map.56.refs_1_ = bf16[32,2176]{1,0:T(8,128)(2,1)S(1)} custom-call(bf16[32,2048]{1,0:T(8,128)(2,1)} %bitcast.2, s32[2,2,8,16]{3,2,1,0:T(8,128)} %bitcast.4, f32[2,2048]{1,0:T(2,128)} %refs_2_.5), custom_call_target="tpu_custom_call" | custom-call | tf_op jit(solution)/shard_map/pallas_call | solution.py:28
  1.2 3.1 %collective-permute-start = (bf16[32,2176]{1,0:T(8,128)(2,1)S(1)}, bf16[32,2176]{1,0:T(8,128)(2,1)S(1)}, u32[]{:S(2)}, u32[]{:S(2)}) collective-permute-start(bf16[32,2176]{1,0:T(8,128)(2,1)S(1)} %shard_map.56.refs_1_), channel_id=1, source_target_pairs={{0,4},{1,5},{2,6},{3,7},{4,0},{5,1},{6,2},{7,3},{8,12},{9,13},{10,... | collective-permute-start | bytes 417800 | tf_op jit(solution)/shard_map/ppermute | solution.py:50
  4.3 2.5 %collective-permute-start.2 = (bf16[32,2176]{1,0:T(8,128)(2,1)S(1)}, bf16[32,2176]{1,0:T(8,128)(2,1)S(1)}, u32[]{:S(2)}, u32[]{:S(2)}) collective-permute-start(bf16[32,2176]{1,0:T(8,128)(2,1)S(1)} %shard_map.56.refs_1_), channel_id=1, source_target_pairs={{0,12},{1,13},{2,14},{3,15},{4,8},{5,9},{6,10},{7,11},{8,4},{9,5},... | collective-permute-start | bytes 417800 | tf_op jit(solution)/shard_map/ppermute | solution.py:50
  6.8 0.1 collective-permute-start.1
  6.9 3.7 %shard_map.55 = (bf16[2048,1536]{1,0:T(8,128)(2,1)S(1)}, bf16[768,2048]{1,0:T(8,128)(2,1)S(1)}, f32[8,128]{1,0:T(8,128)S(1)}) custom-call(bf16[2,1,2048,1536]{3,2,1,0:T(8,128)(2,1)} %refs_1_.3, bf16[2,1,768,2048]{3,2,1,0:T(8,128)(2,1)} %refs_2_.4), custom_call_target="tpu_custom_call" | custom-call | tf_op jit(solution)/shard_map/pallas_call | solution.py:28
  10.8 1.6 %collective-permute-start.3 = (bf16[64,2176]{1,0:T(8,128)(2,1)S(1)}, bf16[64,2176]{1,0:T(8,128)(2,1)S(1)}, u32[]{:S(2)}, u32[]{:S(2)}) collective-permute-start(bf16[64,2176]{1,0:T(8,128)(2,1)S(1)} %shard_map.57.refs_0_.refs_1_), channel_id=1, source_target_pairs={{0,2},{1,3},{2,0},{3,1},{4,6},{5,7},{6,4},{7,5},{8,10},{9,11},{10,... | collective-permute-start | bytes 835592 | tf_op jit(solution)/shard_map/ppermute | solution.py:50
  12.4 2.0 %collective-permute-done.2.refs_2_ = bf16[32,2176]{1,0:T(8,128)(2,1)S(1)} collective-permute-done((bf16[32,2176]{1,0:T(8,128)(2,1)S(1)}, bf16[32,2176]{1,0:T(8,128)(2,1)S(1)}, u32[]{:S(2)}, u32[]{:S(2)}) %collective-permute-start.2) | collective-permute-done | bytes 139296 | tf_op jit(solution)/shard_map/ppermute | solution.py:50
  14.4 4.8 %collective-permute-done.1.refs_1_ = bf16[32,2176]{1,0:T(8,128)(2,1)S(1)} collective-permute-done((bf16[32,2176]{1,0:T(8,128)(2,1)S(1)}, bf16[32,2176]{1,0:T(8,128)(2,1)S(1)}, u32[]{:S(2)}, u32[]{:S(2)}) %collective-permute-start.1) | collective-permute-done | bytes 139296 | tf_op jit(solution)/shard_map/ppermute | solution.py:50
  19.3 0.6 collective-permute-done.3.refs_2_
  19.9 1.5 %collective-permute-start.6 = (bf16[64,2176]{1,0:T(8,128)(2,1)S(1)}, bf16[64,2176]{1,0:T(8,128)(2,1)S(1)}, u32[]{:S(2)}, u32[]{:S(2)}) collective-permute-start(bf16[64,2176]{1,0:T(8,128)(2,1)S(1)} %shard_map.58.refs_0_.refs_1_), channel_id=1, source_target_pairs={{0,2},{1,3},{2,0},{3,1},{4,6},{5,7},{6,4},{7,5},{8,10},{9,11},{10,... | collective-permute-start | bytes 835592 | tf_op jit(solution)/shard_map/ppermute | solution.py:50
  21.4 0.2 collective-permute-start.7
  21.6 2.6 %shard_map.59 = (f32[64,2048]{1,0:T(8,128)S(1)}, f32[64,2048]{1,0:T(8,128)S(1)}, bf16[64,2048]{1,0:T(8,128)(2,1)S(1)}, bf16[64,2048]{1,0:T(8,128)(2,1)S(1)}, bf16[256,128]{1,0:T(8,128)(2,1)S(1)}) custom-call(bf16[64,2176]{1,0:T(8,128)(2,1)S(1)} %shard_map.58.refs_0_.refs_1_, bf16[64,2176]{1,0:T(8,128)(2,1)S(1)} %shard_map.57.refs_0_.refs_1_, ...), custom_call_target="tpu_custom_call" | custom-call | tf_op jit(solution)/shard_map/pallas_call | solution.py:28
  24.2 4.7 %collective-permute-done.6.refs_2_ = bf16[64,2176]{1,0:T(8,128)(2,1)S(1)} collective-permute-done((bf16[64,2176]{1,0:T(8,128)(2,1)S(1)}, bf16[64,2176]{1,0:T(8,128)(2,1)S(1)}, u32[]{:S(2)}, u32[]{:S(2)}) %collective-permute-start.6) | collective-permute-done | bytes 278560 | tf_op jit(solution)/shard_map/ppermute | solution.py:50
  28.9 0.5 collective-permute-start.10
  29.4 1.4 %collective-permute-done.10.refs_1_ = bf16[64,2048]{1,0:T(8,128)(2,1)S(1)} collective-permute-done((bf16[64,2048]{1,0:T(8,128)(2,1)S(1)}, bf16[64,2048]{1,0:T(8,128)(2,1)S(1)}, u32[]{:S(2)}, u32[]{:S(2)}) %collective-permute-start.10) | collective-permute-done | bytes 262176 | tf_op jit(solution)/shard_map/ppermute | solution.py:50
  30.9 1.6 %collective-permute-start.11 = (bf16[64,2048]{1,0:T(8,128)(2,1)S(1)}, bf16[64,2048]{1,0:T(8,128)(2,1)S(1)}, u32[]{:S(2)}, u32[]{:S(2)}) collective-permute-start(bf16[64,2048]{1,0:T(8,128)(2,1)S(1)} %shard_map.62), channel_id=1, source_target_pairs={{0,2},{1,3},{2,0},{3,1},{4,6},{5,7},{6,4},{7,5},{8,10},{9,11},{10,... | collective-permute-start | bytes 786440 | tf_op jit(solution)/shard_map/ppermute | solution.py:50
  32.5 2.6 %shard_map.60 = (f32[64,2048]{1,0:T(8,128)S(1)}, f32[64,2048]{1,0:T(8,128)S(1)}, bf16[64,2048]{1,0:T(8,128)(2,1)S(1)}, bf16[64,2048]{1,0:T(8,128)(2,1)S(1)}, bf16[256,128]{1,0:T(8,128)(2,1)S(1)}) custom-call(f32[64,2048]{1,0:T(8,128)S(1)} %get-tuple-element.49.refs_0_, bf16[64,2176]{1,0:T(8,128)(2,1)S(1)} %shard_map.58.refs_0_.refs_1_, ...), custom_call_target="tpu_custom_call" | custom-call | tf_op jit(solution)/shard_map/pallas_call | solution.py:28
  35.2 0.5 collective-permute-start.13
  35.7 3.6 %collective-permute-done.11.refs_2_ = bf16[64,2048]{1,0:T(8,128)(2,1)S(1)} collective-permute-done((bf16[64,2048]{1,0:T(8,128)(2,1)S(1)}, bf16[64,2048]{1,0:T(8,128)(2,1)S(1)}, u32[]{:S(2)}, u32[]{:S(2)}) %collective-permute-start.11) | collective-permute-done | bytes 262176 | tf_op jit(solution)/shard_map/ppermute | solution.py:50
  39.5 1.6 %collective-permute-start.15 = (bf16[64,2048]{1,0:T(8,128)(2,1)S(1)}, bf16[64,2048]{1,0:T(8,128)(2,1)S(1)}, u32[]{:S(2)}, u32[]{:S(2)}) collective-permute-start(bf16[64,2048]{1,0:T(8,128)(2,1)S(1)} %shard_map.64), channel_id=1, source_target_pairs={{0,2},{1,3},{2,0},{3,1},{4,6},{5,7},{6,4},{7,5},{8,10},{9,11},{10,... | collective-permute-start | bytes 786440 | tf_op jit(solution)/shard_map/ppermute | solution.py:50
  41.1 1.8 %collective-permute-start.12 = (bf16[32,2048]{1,0:T(8,128)(2,1)S(1)}, bf16[32,2048]{1,0:T(8,128)(2,1)S(1)}, u32[]{:S(2)}, u32[]{:S(2)}) collective-permute-start(bf16[32,2048]{1,0:T(8,128)(2,1)S(1)} %get-tuple-element.58.refs_0_), channel_id=1, source_target_pairs={{0,4},{1,5},{2,6},{3,7},{4,0},{5,1},{6,2},{7,3},{8,12},{9,13},{10,... | collective-permute-start | bytes 393224 | tf_op jit(solution)/shard_map/ppermute | solution.py:50
  42.9 4.2 %collective-permute-done.15.refs_2_ = bf16[64,2048]{1,0:T(8,128)(2,1)S(1)} collective-permute-done((bf16[64,2048]{1,0:T(8,128)(2,1)S(1)}, bf16[64,2048]{1,0:T(8,128)(2,1)S(1)}, u32[]{:S(2)}, u32[]{:S(2)}) %collective-permute-start.15) | collective-permute-done | bytes 262176 | tf_op jit(solution)/shard_map/ppermute | solution.py:50
  47.1 0.1 shard_map.65
  47.1 2.9 %collective-permute-start.16 = (bf16[32,2048]{1,0:T(8,128)(2,1)S(1)}, bf16[32,2048]{1,0:T(8,128)(2,1)S(1)}, u32[]{:S(2)}, u32[]{:S(2)}) collective-permute-start(bf16[32,2048]{1,0:T(8,128)(2,1)S(1)} %get-tuple-element.62), channel_id=1, source_target_pairs={{0,8},{1,9},{2,10},{3,11},{4,12},{5,13},{6,14},{7,15},{8,0},{9,1},... | collective-permute-start | bytes 393224 | tf_op jit(solution)/shard_map/ppermute | solution.py:50
  50.0 1.3 %collective-permute-start.17 = (bf16[32,2048]{1,0:T(8,128)(2,1)S(1)}, bf16[32,2048]{1,0:T(8,128)(2,1)S(1)}, u32[]{:S(2)}, u32[]{:S(2)}) collective-permute-start(bf16[32,2048]{1,0:T(8,128)(2,1)S(1)} %get-tuple-element.63), channel_id=1, source_target_pairs={{0,12},{1,13},{2,14},{3,15},{4,8},{5,9},{6,10},{7,11},{8,4},{9,5},... | collective-permute-start | bytes 393224 | tf_op jit(solution)/shard_map/ppermute | solution.py:50
  51.4 3.7 %shard_map.61 = (bf16[2048,1536]{1,0:T(8,128)(2,1)S(1)}, bf16[768,2048]{1,0:T(8,128)(2,1)S(1)}, f32[8,128]{1,0:T(8,128)S(1)}) custom-call(f32[64,2048]{1,0:T(8,128)S(1)} %get-tuple-element.51.refs_0_, bf16[2,1,2048,1536]{3,2,1,0:T(8,128)(2,1)} %refs_1_.3, bf16[2,1,768,2048]{3,2,1,0:T(8,128)(2,1)} %refs_2_.4), custom_call_target="tpu_custom_call" | custom-call | tf_op jit(solution)/shard_map/pallas_call | solution.py:28
  55.1 3.8 %collective-permute-done.16.refs_5_ = bf16[32,2048]{1,0:T(8,128)(2,1)S(1)} collective-permute-done((bf16[32,2048]{1,0:T(8,128)(2,1)S(1)}, bf16[32,2048]{1,0:T(8,128)(2,1)S(1)}, u32[]{:S(2)}, u32[]{:S(2)}) %collective-permute-start.16) | collective-permute-done | bytes 131104 | tf_op jit(solution)/shard_map/ppermute | solution.py:50
  58.9 0.2 shard_map.66
  59.1 2.2 %collective-permute-start.18 = (bf16[32,2048]{1,0:T(8,128)(2,1)S(1)}, bf16[32,2048]{1,0:T(8,128)(2,1)S(1)}, u32[]{:S(2)}, u32[]{:S(2)}) collective-permute-start(bf16[32,2048]{1,0:T(8,128)(2,1)S(1)} %get-tuple-element.65.refs_1_), channel_id=1, source_target_pairs={{0,4},{1,5},{2,6},{3,7},{4,0},{5,1},{6,2},{7,3},{8,12},{9,13},{10,... | collective-permute-start | bytes 393224 | tf_op jit(solution)/shard_map/ppermute | solution.py:50
  61.3 3.2 %collective-permute-start.20 = (bf16[32,2048]{1,0:T(8,128)(2,1)S(1)}, bf16[32,2048]{1,0:T(8,128)(2,1)S(1)}, u32[]{:S(2)}, u32[]{:S(2)}) collective-permute-start(bf16[32,2048]{1,0:T(8,128)(2,1)S(1)} %get-tuple-element.65.refs_1_), channel_id=1, source_target_pairs={{0,12},{1,13},{2,14},{3,15},{4,8},{5,9},{6,10},{7,11},{8,4},{9,5},... | collective-permute-start | bytes 393224 | tf_op jit(solution)/shard_map/ppermute | solution.py:50
  64.7 1.6 %collective-permute-start.21 = (bf16[64,2048]{1,0:T(8,128)(2,1)S(1)}, bf16[64,2048]{1,0:T(8,128)(2,1)S(1)}, u32[]{:S(2)}, u32[]{:S(2)}) collective-permute-start(bf16[64,2048]{1,0:T(8,128)(2,1)S(1)} %shard_map.67.refs_0_.refs_1_), channel_id=1, source_target_pairs={{0,2},{1,3},{2,0},{3,1},{4,6},{5,7},{6,4},{7,5},{8,10},{9,11},{10,... | collective-permute-start | bytes 786440 | tf_op jit(solution)/shard_map/ppermute | solution.py:50
  66.3 5.6 %collective-permute-done.20.refs_2_ = bf16[32,2048]{1,0:T(8,128)(2,1)S(1)} collective-permute-done((bf16[32,2048]{1,0:T(8,128)(2,1)S(1)}, bf16[32,2048]{1,0:T(8,128)(2,1)S(1)}, u32[]{:S(2)}, u32[]{:S(2)}) %collective-permute-start.20) | collective-permute-done | bytes 131104 | tf_op jit(solution)/shard_map/ppermute | solution.py:50
  71.9 3.2 %collective-permute-done.19.refs_1_ = bf16[32,2048]{1,0:T(8,128)(2,1)S(1)} collective-permute-done((bf16[32,2048]{1,0:T(8,128)(2,1)S(1)}, bf16[32,2048]{1,0:T(8,128)(2,1)S(1)}, u32[]{:S(2)}, u32[]{:S(2)}) %collective-permute-start.19) | collective-permute-done | bytes 131104 | tf_op jit(solution)/shard_map/ppermute | solution.py:50
  75.2 1.6 %collective-permute-start.26 = (bf16[64,2048]{1,0:T(8,128)(2,1)S(1)}, bf16[64,2048]{1,0:T(8,128)(2,1)S(1)}, u32[]{:S(2)}, u32[]{:S(2)}) collective-permute-start(bf16[64,2048]{1,0:T(8,128)(2,1)S(1)} %shard_map.68.refs_0_.refs_1_), channel_id=1, source_target_pairs={{0,2},{1,3},{2,0},{3,1},{4,6},{5,7},{6,4},{7,5},{8,10},{9,11},{10,... | collective-permute-start | bytes 786440 | tf_op jit(solution)/shard_map/ppermute | solution.py:50
  76.8 2.6 %shard_map.69 = (f32[64,2048]{1,0:T(8,128)S(1)}, f32[64,2048]{1,0:T(8,128)S(1)}, bf16[64,2048]{1,0:T(8,128)(2,1)S(1)}, bf16[64,2048]{1,0:T(8,128)(2,1)S(1)}) custom-call(bf16[64,2048]{1,0:T(8,128)(2,1)S(1)} %shard_map.68.refs_0_.refs_1_, bf16[64,2048]{1,0:T(8,128)(2,1)S(1)} %shard_map.67.refs_0_.refs_1_, ...), custom_call_target="tpu_custom_call" | custom-call | tf_op jit(solution)/shard_map/pallas_call | solution.py:28
  79.4 0.2 collective-permute-start.25
  79.7 0.3 collective-permute-start.29
  80.0 3.9 %collective-permute-done.26.refs_2_ = bf16[64,2048]{1,0:T(8,128)(2,1)S(1)} collective-permute-done((bf16[64,2048]{1,0:T(8,128)(2,1)S(1)}, bf16[64,2048]{1,0:T(8,128)(2,1)S(1)}, u32[]{:S(2)}, u32[]{:S(2)}) %collective-permute-start.26) | collective-permute-done | bytes 262176 | tf_op jit(solution)/shard_map/ppermute | solution.py:50
  83.9 0.5 collective-permute-start.24
  84.5 1.6 %collective-permute-start.27 = (bf16[64,2048]{1,0:T(8,128)(2,1)S(1)}, bf16[64,2048]{1,0:T(8,128)(2,1)S(1)}, u32[]{:S(2)}, u32[]{:S(2)}) collective-permute-start(bf16[64,2048]{1,0:T(8,128)(2,1)S(1)} %shard_map.70), channel_id=1, source_target_pairs={{0,2},{1,3},{2,0},{3,1},{4,6},{5,7},{6,4},{7,5},{8,10},{9,11},{10,... | collective-permute-start | bytes 786440 | tf_op jit(solution)/shard_map/ppermute | solution.py:50
  86.1 2.6 %shard_map.72 = (f32[64,2048]{1,0:T(8,128)S(1)}, f32[64,2048]{1,0:T(8,128)S(1)}, bf16[64,2048]{1,0:T(8,128)(2,1)S(1)}, bf16[64,2048]{1,0:T(8,128)(2,1)S(1)}) custom-call(f32[64,2048]{1,0:T(8,128)S(1)} %get-tuple-element.70.refs_0_, bf16[64,2048]{1,0:T(8,128)(2,1)S(1)} %shard_map.68.refs_0_.refs_1_, bf16[64,2048]{1,0:T(8,128)(2,1)S(1)} %collective-permute-done.26.refs_2_, ...), custom_call_target="tpu_custom_call" | custom-call | tf_op jit(solution)/shard_map/pallas_call | solution.py:28
  88.8 0.5 collective-permute-start.31
  89.3 3.5 %collective-permute-done.27.refs_2_ = bf16[64,2048]{1,0:T(8,128)(2,1)S(1)} collective-permute-done((bf16[64,2048]{1,0:T(8,128)(2,1)S(1)}, bf16[64,2048]{1,0:T(8,128)(2,1)S(1)}, u32[]{:S(2)}, u32[]{:S(2)}) %collective-permute-start.27) | collective-permute-done | bytes 262176 | tf_op jit(solution)/shard_map/ppermute | solution.py:50
  92.9 1.6 %collective-permute-start.33 = (bf16[64,2048]{1,0:T(8,128)(2,1)S(1)}, bf16[64,2048]{1,0:T(8,128)(2,1)S(1)}, u32[]{:S(2)}, u32[]{:S(2)}) collective-permute-start(bf16[64,2048]{1,0:T(8,128)(2,1)S(1)} %shard_map.73), channel_id=1, source_target_pairs={{0,2},{1,3},{2,0},{3,1},{4,6},{5,7},{6,4},{7,5},{8,10},{9,11},{10,... | collective-permute-start | bytes 786440 | tf_op jit(solution)/shard_map/ppermute | solution.py:50
  94.5 5.8 %collective-permute-done.33.refs_2_ = bf16[64,2048]{1,0:T(8,128)(2,1)S(1)} collective-permute-done((bf16[64,2048]{1,0:T(8,128)(2,1)S(1)}, bf16[64,2048]{1,0:T(8,128)(2,1)S(1)}, u32[]{:S(2)}, u32[]{:S(2)}) %collective-permute-start.33) | collective-permute-done | bytes 262176 | tf_op jit(solution)/shard_map/ppermute | solution.py:50
  100.4 3.2 %collective-permute-start.34 = (bf16[32,2048]{1,0:T(8,128)(2,1)S(1)}, bf16[32,2048]{1,0:T(8,128)(2,1)S(1)}, u32[]{:S(2)}, u32[]{:S(2)}) collective-permute-start(bf16[32,2048]{1,0:T(8,128)(2,1)S(1)} %get-tuple-element.83), channel_id=1, source_target_pairs={{0,8},{1,9},{2,10},{3,11},{4,12},{5,13},{6,14},{7,15},{8,0},{9,1},... | collective-permute-start | bytes 393224 | tf_op jit(solution)/shard_map/ppermute | solution.py:50
  103.6 8.0 %collective-permute-done.34.refs_3_ = bf16[32,2048]{1,0:T(8,128)(2,1)S(1)} collective-permute-done((bf16[32,2048]{1,0:T(8,128)(2,1)S(1)}, bf16[32,2048]{1,0:T(8,128)(2,1)S(1)}, u32[]{:S(2)}, u32[]{:S(2)}) %collective-permute-start.34) | collective-permute-done | bytes 131104 | tf_op jit(solution)/shard_map/ppermute | solution.py:50
  111.7 0.8 shard_map.75
  (49 shorter events, 0.9 us)
Async XLA Ops:
  1.2 9.4 %collective-permute-start = (bf16[32,2176]{1,0:T(8,128)(2,1)S(1)}, bf16[32,2176]{1,0:T(8,128)(2,1)S(1)}, u32[]{:S(2)}, u32[]{:S(2)}) collective-permute-start(bf16[32,2176]{1,0:T(8,128)(2,1)S(1)} %shard_map.56.refs_1_), channel_id=1, source_target_pairs={{0,4},{1,5},{2,6},{3,7},{4,0},{5,1},{6,2},{7,3},{8,12},{9,13},{10,... | collective-permute-start | bytes 417800 | tf_op jit(solution)/shard_map/ppermute | solution.py:50
  4.3 10.1 %collective-permute-start.2 = (bf16[32,2176]{1,0:T(8,128)(2,1)S(1)}, bf16[32,2176]{1,0:T(8,128)(2,1)S(1)}, u32[]{:S(2)}, u32[]{:S(2)}) collective-permute-start(bf16[32,2176]{1,0:T(8,128)(2,1)S(1)} %shard_map.56.refs_1_), channel_id=1, source_target_pairs={{0,12},{1,13},{2,14},{3,15},{4,8},{5,9},{6,10},{7,11},{8,4},{9,5},... | collective-permute-start | bytes 417800 | tf_op jit(solution)/shard_map/ppermute | solution.py:50
  6.8 12.5 %collective-permute-start.1 = (bf16[32,2176]{1,0:T(8,128)(2,1)S(1)}, bf16[32,2176]{1,0:T(8,128)(2,1)S(1)}, u32[]{:S(2)}, u32[]{:S(2)}) collective-permute-start(bf16[32,2176]{1,0:T(8,128)(2,1)S(1)} %shard_map.56.refs_1_), channel_id=1, source_target_pairs={{0,8},{1,9},{2,10},{3,11},{4,12},{5,13},{6,14},{7,15},{8,0},{9,1},... | collective-permute-start | bytes 417800 | tf_op jit(solution)/shard_map/ppermute | solution.py:50
  10.7 10.9 %collective-permute-start.4 = (bf16[64,2176]{1,0:T(8,128)(2,1)S(1)}, bf16[64,2176]{1,0:T(8,128)(2,1)S(1)}, u32[]{:S(2)}, u32[]{:S(2)}) collective-permute-start(bf16[64,2176]{1,0:T(8,128)(2,1)S(1)} %shard_map.57.refs_0_.refs_1_), channel_id=1, source_target_pairs={{0,1},{1,0},{2,3},{3,2},{4,5},{5,4},{6,7},{7,6},{8,9},{9,8},{10,11... | collective-permute-start | bytes 835592 | tf_op jit(solution)/shard_map/ppermute | solution.py:50
  10.8 9.1 %collective-permute-start.3 = (bf16[64,2176]{1,0:T(8,128)(2,1)S(1)}, bf16[64,2176]{1,0:T(8,128)(2,1)S(1)}, u32[]{:S(2)}, u32[]{:S(2)}) collective-permute-start(bf16[64,2176]{1,0:T(8,128)(2,1)S(1)} %shard_map.57.refs_0_.refs_1_), channel_id=1, source_target_pairs={{0,2},{1,3},{2,0},{3,1},{4,6},{5,7},{6,4},{7,5},{8,10},{9,11},{10,... | collective-permute-start | bytes 835592 | tf_op jit(solution)/shard_map/ppermute | solution.py:50
  19.8 1.8 %collective-permute-start.5 = (bf16[64,2176]{1,0:T(8,128)(2,1)S(1)}, bf16[64,2176]{1,0:T(8,128)(2,1)S(1)}, u32[]{:S(2)}, u32[]{:S(2)}) collective-permute-start(bf16[64,2176]{1,0:T(8,128)(2,1)S(1)} %collective-permute-done.3.refs_2_), channel_id=1, source_target_pairs={{0,1},{1,0},{2,3},{3,2},{4,5},{5,4},{6,7},{7,6},{8,9},{9,8},{10,11... | collective-permute-start | bytes 835592 | tf_op jit(solution)/shard_map/ppermute | solution.py:50
  19.9 9.1 %collective-permute-start.6 = (bf16[64,2176]{1,0:T(8,128)(2,1)S(1)}, bf16[64,2176]{1,0:T(8,128)(2,1)S(1)}, u32[]{:S(2)}, u32[]{:S(2)}) collective-permute-start(bf16[64,2176]{1,0:T(8,128)(2,1)S(1)} %shard_map.58.refs_0_.refs_1_), channel_id=1, source_target_pairs={{0,2},{1,3},{2,0},{3,1},{4,6},{5,7},{6,4},{7,5},{8,10},{9,11},{10,... | collective-permute-start | bytes 835592 | tf_op jit(solution)/shard_map/ppermute | solution.py:50
  21.4 11.1 %collective-permute-start.7 = (bf16[64,2176]{1,0:T(8,128)(2,1)S(1)}, bf16[64,2176]{1,0:T(8,128)(2,1)S(1)}, u32[]{:S(2)}, u32[]{:S(2)}) collective-permute-start(bf16[64,2176]{1,0:T(8,128)(2,1)S(1)} %shard_map.58.refs_0_.refs_1_), channel_id=1, source_target_pairs={{0,1},{1,0},{2,3},{3,2},{4,5},{5,4},{6,7},{7,6},{8,9},{9,8},{10,11... | collective-permute-start | bytes 835592 | tf_op jit(solution)/shard_map/ppermute | solution.py:50
  28.9 3.6 %collective-permute-start.8 = (bf16[64,2176]{1,0:T(8,128)(2,1)S(1)}, bf16[64,2176]{1,0:T(8,128)(2,1)S(1)}, u32[]{:S(2)}, u32[]{:S(2)}) collective-permute-start(bf16[64,2176]{1,0:T(8,128)(2,1)S(1)} %collective-permute-done.6.refs_2_), channel_id=1, source_target_pairs={{0,1},{1,0},{2,3},{3,2},{4,5},{5,4},{6,7},{7,6},{8,9},{9,8},{10,11... | collective-permute-start | bytes 835592 | tf_op jit(solution)/shard_map/ppermute | solution.py:50
  28.9 1.9 %collective-permute-start.10 = (bf16[64,2048]{1,0:T(8,128)(2,1)S(1)}, bf16[64,2048]{1,0:T(8,128)(2,1)S(1)}, u32[]{:S(2)}, u32[]{:S(2)}) collective-permute-start(bf16[64,2048]{1,0:T(8,128)(2,1)S(1)} %get-tuple-element.55), channel_id=1, source_target_pairs={{0,1},{1,0},{2,3},{3,2},{4,5},{5,4},{6,7},{7,6},{8,9},{9,8},{10,11... | collective-permute-start | bytes 786440 | tf_op jit(solution)/shard_map/ppermute | solution.py:50
  29.4 6.3 %collective-permute-start.9 = (bf16[64,2048]{1,0:T(8,128)(2,1)S(1)}, bf16[64,2048]{1,0:T(8,128)(2,1)S(1)}, u32[]{:S(2)}, u32[]{:S(2)}) collective-permute-start(bf16[64,2048]{1,0:T(8,128)(2,1)S(1)} %get-tuple-element.53), channel_id=1, source_target_pairs={{0,1},{1,0},{2,3},{3,2},{4,5},{5,4},{6,7},{7,6},{8,9},{9,8},{10,11... | collective-permute-start | bytes 786440 | tf_op jit(solution)/shard_map/ppermute | solution.py:50
  30.9 8.4 %collective-permute-start.11 = (bf16[64,2048]{1,0:T(8,128)(2,1)S(1)}, bf16[64,2048]{1,0:T(8,128)(2,1)S(1)}, u32[]{:S(2)}, u32[]{:S(2)}) collective-permute-start(bf16[64,2048]{1,0:T(8,128)(2,1)S(1)} %shard_map.62), channel_id=1, source_target_pairs={{0,2},{1,3},{2,0},{3,1},{4,6},{5,7},{6,4},{7,5},{8,10},{9,11},{10,... | collective-permute-start | bytes 786440 | tf_op jit(solution)/shard_map/ppermute | solution.py:50
  35.1 4.3 %collective-permute-start.14 = (bf16[64,2048]{1,0:T(8,128)(2,1)S(1)}, bf16[64,2048]{1,0:T(8,128)(2,1)S(1)}, u32[]{:S(2)}, u32[]{:S(2)}) collective-permute-start(bf16[64,2048]{1,0:T(8,128)(2,1)S(1)} %get-tuple-element.61), channel_id=1, source_target_pairs={{0,1},{1,0},{2,3},{3,2},{4,5},{5,4},{6,7},{7,6},{8,9},{9,8},{10,11... | collective-permute-start | bytes 786440 | tf_op jit(solution)/shard_map/ppermute | solution.py:50
  35.2 7.7 %collective-permute-start.13 = (bf16[64,2048]{1,0:T(8,128)(2,1)S(1)}, bf16[64,2048]{1,0:T(8,128)(2,1)S(1)}, u32[]{:S(2)}, u32[]{:S(2)}) collective-permute-start(bf16[64,2048]{1,0:T(8,128)(2,1)S(1)} %get-tuple-element.59), channel_id=1, source_target_pairs={{0,1},{1,0},{2,3},{3,2},{4,5},{5,4},{6,7},{7,6},{8,9},{9,8},{10,11... | collective-permute-start | bytes 786440 | tf_op jit(solution)/shard_map/ppermute | solution.py:50
  39.5 7.6 %collective-permute-start.15 = (bf16[64,2048]{1,0:T(8,128)(2,1)S(1)}, bf16[64,2048]{1,0:T(8,128)(2,1)S(1)}, u32[]{:S(2)}, u32[]{:S(2)}) collective-permute-start(bf16[64,2048]{1,0:T(8,128)(2,1)S(1)} %shard_map.64), channel_id=1, source_target_pairs={{0,2},{1,3},{2,0},{3,1},{4,6},{5,7},{6,4},{7,5},{8,10},{9,11},{10,... | collective-permute-start | bytes 786440 | tf_op jit(solution)/shard_map/ppermute | solution.py:50
  41.1 14.1 %collective-permute-start.12 = (bf16[32,2048]{1,0:T(8,128)(2,1)S(1)}, bf16[32,2048]{1,0:T(8,128)(2,1)S(1)}, u32[]{:S(2)}, u32[]{:S(2)}) collective-permute-start(bf16[32,2048]{1,0:T(8,128)(2,1)S(1)} %get-tuple-element.58.refs_0_), channel_id=1, source_target_pairs={{0,4},{1,5},{2,6},{3,7},{4,0},{5,1},{6,2},{7,3},{8,12},{9,13},{10,... | collective-permute-start | bytes 393224 | tf_op jit(solution)/shard_map/ppermute | solution.py:50
  47.1 11.8 %collective-permute-start.16 = (bf16[32,2048]{1,0:T(8,128)(2,1)S(1)}, bf16[32,2048]{1,0:T(8,128)(2,1)S(1)}, u32[]{:S(2)}, u32[]{:S(2)}) collective-permute-start(bf16[32,2048]{1,0:T(8,128)(2,1)S(1)} %get-tuple-element.62), channel_id=1, source_target_pairs={{0,8},{1,9},{2,10},{3,11},{4,12},{5,13},{6,14},{7,15},{8,0},{9,1},... | collective-permute-start | bytes 393224 | tf_op jit(solution)/shard_map/ppermute | solution.py:50
  50.0 8.9 %copy-start = (bf16[2,16,2048]{2,1,0:T(8,128)(2,1)S(1)}, bf16[2,16,2048]{2,1,0:T(8,128)(2,1)}, u32[]{:S(2)}) copy-start(bf16[2,16,2048]{2,1,0:T(8,128)(2,1)} %param.5) | copy-start | bytes 393220
  50.0 8.9 %copy-start.1 = (f32[2,2048]{1,0:T(2,128)S(1)}, f32[2,2048]{1,0:T(2,128)}, u32[]{:S(2)}) copy-start(f32[2,2048]{1,0:T(2,128)} %refs_2_.5) | copy-start | bytes 49156
  50.0 8.9 %collective-permute-start.17 = (bf16[32,2048]{1,0:T(8,128)(2,1)S(1)}, bf16[32,2048]{1,0:T(8,128)(2,1)S(1)}, u32[]{:S(2)}, u32[]{:S(2)}) collective-permute-start(bf16[32,2048]{1,0:T(8,128)(2,1)S(1)} %get-tuple-element.63), channel_id=1, source_target_pairs={{0,12},{1,13},{2,14},{3,15},{4,8},{5,9},{6,10},{7,11},{8,4},{9,5},... | collective-permute-start | bytes 393224 | tf_op jit(solution)/shard_map/ppermute | solution.py:50
  59.1 5.4 %collective-permute-start.18 = (bf16[32,2048]{1,0:T(8,128)(2,1)S(1)}, bf16[32,2048]{1,0:T(8,128)(2,1)S(1)}, u32[]{:S(2)}, u32[]{:S(2)}) collective-permute-start(bf16[32,2048]{1,0:T(8,128)(2,1)S(1)} %get-tuple-element.65.refs_1_), channel_id=1, source_target_pairs={{0,4},{1,5},{2,6},{3,7},{4,0},{5,1},{6,2},{7,3},{8,12},{9,13},{10,... | collective-permute-start | bytes 393224 | tf_op jit(solution)/shard_map/ppermute | solution.py:50
  61.3 10.5 %collective-permute-start.20 = (bf16[32,2048]{1,0:T(8,128)(2,1)S(1)}, bf16[32,2048]{1,0:T(8,128)(2,1)S(1)}, u32[]{:S(2)}, u32[]{:S(2)}) collective-permute-start(bf16[32,2048]{1,0:T(8,128)(2,1)S(1)} %get-tuple-element.65.refs_1_), channel_id=1, source_target_pairs={{0,12},{1,13},{2,14},{3,15},{4,8},{5,9},{6,10},{7,11},{8,4},{9,5},... | collective-permute-start | bytes 393224 | tf_op jit(solution)/shard_map/ppermute | solution.py:50
  64.6 10.5 %collective-permute-start.19 = (bf16[32,2048]{1,0:T(8,128)(2,1)S(1)}, bf16[32,2048]{1,0:T(8,128)(2,1)S(1)}, u32[]{:S(2)}, u32[]{:S(2)}) collective-permute-start(bf16[32,2048]{1,0:T(8,128)(2,1)S(1)} %get-tuple-element.65.refs_1_), channel_id=1, source_target_pairs={{0,8},{1,9},{2,10},{3,11},{4,12},{5,13},{6,14},{7,15},{8,0},{9,1},... | collective-permute-start | bytes 393224 | tf_op jit(solution)/shard_map/ppermute | solution.py:50
  64.6 12.2 %collective-permute-start.22 = (bf16[64,2048]{1,0:T(8,128)(2,1)S(1)}, bf16[64,2048]{1,0:T(8,128)(2,1)S(1)}, u32[]{:S(2)}, u32[]{:S(2)}) collective-permute-start(bf16[64,2048]{1,0:T(8,128)(2,1)S(1)} %shard_map.67.refs_0_.refs_1_), channel_id=1, source_target_pairs={{0,1},{1,0},{2,3},{3,2},{4,5},{5,4},{6,7},{7,6},{8,9},{9,8},{10,11... | collective-permute-start | bytes 786440 | tf_op jit(solution)/shard_map/ppermute | solution.py:50
  64.7 10.5 %collective-permute-start.21 = (bf16[64,2048]{1,0:T(8,128)(2,1)S(1)}, bf16[64,2048]{1,0:T(8,128)(2,1)S(1)}, u32[]{:S(2)}, u32[]{:S(2)}) collective-permute-start(bf16[64,2048]{1,0:T(8,128)(2,1)S(1)} %shard_map.67.refs_0_.refs_1_), channel_id=1, source_target_pairs={{0,2},{1,3},{2,0},{3,1},{4,6},{5,7},{6,4},{7,5},{8,10},{9,11},{10,... | collective-permute-start | bytes 786440 | tf_op jit(solution)/shard_map/ppermute | solution.py:50
  75.1 1.7 %collective-permute-start.23 = (bf16[64,2048]{1,0:T(8,128)(2,1)S(1)}, bf16[64,2048]{1,0:T(8,128)(2,1)S(1)}, u32[]{:S(2)}, u32[]{:S(2)}) collective-permute-start(bf16[64,2048]{1,0:T(8,128)(2,1)S(1)} %collective-permute-done.21.refs_2_), channel_id=1, source_target_pairs={{0,1},{1,0},{2,3},{3,2},{4,5},{5,4},{6,7},{7,6},{8,9},{9,8},{10,11... | collective-permute-start | bytes 786440 | tf_op jit(solution)/shard_map/ppermute | solution.py:50
  75.2 8.7 %collective-permute-start.26 = (bf16[64,2048]{1,0:T(8,128)(2,1)S(1)}, bf16[64,2048]{1,0:T(8,128)(2,1)S(1)}, u32[]{:S(2)}, u32[]{:S(2)}) collective-permute-start(bf16[64,2048]{1,0:T(8,128)(2,1)S(1)} %shard_map.68.refs_0_.refs_1_), channel_id=1, source_target_pairs={{0,2},{1,3},{2,0},{3,1},{4,6},{5,7},{6,4},{7,5},{8,10},{9,11},{10,... | collective-permute-start | bytes 786440 | tf_op jit(solution)/shard_map/ppermute | solution.py:50
  79.4 5.0 %collective-permute-start.25 = (bf16[64,2048]{1,0:T(8,128)(2,1)S(1)}, bf16[64,2048]{1,0:T(8,128)(2,1)S(1)}, u32[]{:S(2)}, u32[]{:S(2)}) collective-permute-start(bf16[64,2048]{1,0:T(8,128)(2,1)S(1)} %get-tuple-element.73), channel_id=1, source_target_pairs={{0,1},{1,0},{2,3},{3,2},{4,5},{5,4},{6,7},{7,6},{8,9},{9,8},{10,11... | collective-permute-start | bytes 786440 | tf_op jit(solution)/shard_map/ppermute | solution.py:50
  79.7 6.4 %collective-permute-start.29 = (bf16[64,2048]{1,0:T(8,128)(2,1)S(1)}, bf16[64,2048]{1,0:T(8,128)(2,1)S(1)}, u32[]{:S(2)}, u32[]{:S(2)}) collective-permute-start(bf16[64,2048]{1,0:T(8,128)(2,1)S(1)} %shard_map.68.refs_0_.refs_1_), channel_id=1, source_target_pairs={{0,1},{1,0},{2,3},{3,2},{4,5},{5,4},{6,7},{7,6},{8,9},{9,8},{10,11... | collective-permute-start | bytes 786440 | tf_op jit(solution)/shard_map/ppermute | solution.py:50
  83.9 2.2 %collective-permute-start.30 = (bf16[64,2048]{1,0:T(8,128)(2,1)S(1)}, bf16[64,2048]{1,0:T(8,128)(2,1)S(1)}, u32[]{:S(2)}, u32[]{:S(2)}) collective-permute-start(bf16[64,2048]{1,0:T(8,128)(2,1)S(1)} %collective-permute-done.26.refs_2_), channel_id=1, source_target_pairs={{0,1},{1,0},{2,3},{3,2},{4,5},{5,4},{6,7},{7,6},{8,9},{9,8},{10,11... | collective-permute-start | bytes 786440 | tf_op jit(solution)/shard_map/ppermute | solution.py:50
  83.9 5.4 %collective-permute-start.24 = (bf16[64,2048]{1,0:T(8,128)(2,1)S(1)}, bf16[64,2048]{1,0:T(8,128)(2,1)S(1)}, u32[]{:S(2)}, u32[]{:S(2)}) collective-permute-start(bf16[64,2048]{1,0:T(8,128)(2,1)S(1)} %get-tuple-element.71), channel_id=1, source_target_pairs={{0,1},{1,0},{2,3},{3,2},{4,5},{5,4},{6,7},{7,6},{8,9},{9,8},{10,11... | collective-permute-start | bytes 786440 | tf_op jit(solution)/shard_map/ppermute | solution.py:50
  84.5 8.3 %collective-permute-start.27 = (bf16[64,2048]{1,0:T(8,128)(2,1)S(1)}, bf16[64,2048]{1,0:T(8,128)(2,1)S(1)}, u32[]{:S(2)}, u32[]{:S(2)}) collective-permute-start(bf16[64,2048]{1,0:T(8,128)(2,1)S(1)} %shard_map.70), channel_id=1, source_target_pairs={{0,2},{1,3},{2,0},{3,1},{4,6},{5,7},{6,4},{7,5},{8,10},{9,11},{10,... | collective-permute-start | bytes 786440 | tf_op jit(solution)/shard_map/ppermute | solution.py:50
  88.7 4.2 %collective-permute-start.32 = (bf16[64,2048]{1,0:T(8,128)(2,1)S(1)}, bf16[64,2048]{1,0:T(8,128)(2,1)S(1)}, u32[]{:S(2)}, u32[]{:S(2)}) collective-permute-start(bf16[64,2048]{1,0:T(8,128)(2,1)S(1)} %get-tuple-element.82), channel_id=1, source_target_pairs={{0,1},{1,0},{2,3},{3,2},{4,5},{5,4},{6,7},{7,6},{8,9},{9,8},{10,11... | collective-permute-start | bytes 786440 | tf_op jit(solution)/shard_map/ppermute | solution.py:50
  88.8 5.7 %collective-permute-start.31 = (bf16[64,2048]{1,0:T(8,128)(2,1)S(1)}, bf16[64,2048]{1,0:T(8,128)(2,1)S(1)}, u32[]{:S(2)}, u32[]{:S(2)}) collective-permute-start(bf16[64,2048]{1,0:T(8,128)(2,1)S(1)} %get-tuple-element.80), channel_id=1, source_target_pairs={{0,1},{1,0},{2,3},{3,2},{4,5},{5,4},{6,7},{7,6},{8,9},{9,8},{10,11... | collective-permute-start | bytes 786440 | tf_op jit(solution)/shard_map/ppermute | solution.py:50
  92.9 7.4 %collective-permute-start.33 = (bf16[64,2048]{1,0:T(8,128)(2,1)S(1)}, bf16[64,2048]{1,0:T(8,128)(2,1)S(1)}, u32[]{:S(2)}, u32[]{:S(2)}) collective-permute-start(bf16[64,2048]{1,0:T(8,128)(2,1)S(1)} %shard_map.73), channel_id=1, source_target_pairs={{0,2},{1,3},{2,0},{3,1},{4,6},{5,7},{6,4},{7,5},{8,10},{9,11},{10,... | collective-permute-start | bytes 786440 | tf_op jit(solution)/shard_map/ppermute | solution.py:50
  94.5 9.1 %collective-permute-start.28 = (bf16[32,2048]{1,0:T(8,128)(2,1)S(1)}, bf16[32,2048]{1,0:T(8,128)(2,1)S(1)}, u32[]{:S(2)}, u32[]{:S(2)}) collective-permute-start(bf16[32,2048]{1,0:T(8,128)(2,1)S(1)} %get-tuple-element.76.refs_0_), channel_id=1, source_target_pairs={{0,4},{1,5},{2,6},{3,7},{4,0},{5,1},{6,2},{7,3},{8,12},{9,13},{10,... | collective-permute-start | bytes 393224 | tf_op jit(solution)/shard_map/ppermute | solution.py:50
  100.4 11.2 %collective-permute-start.34 = (bf16[32,2048]{1,0:T(8,128)(2,1)S(1)}, bf16[32,2048]{1,0:T(8,128)(2,1)S(1)}, u32[]{:S(2)}, u32[]{:S(2)}) collective-permute-start(bf16[32,2048]{1,0:T(8,128)(2,1)S(1)} %get-tuple-element.83), channel_id=1, source_target_pairs={{0,8},{1,9},{2,10},{3,11},{4,12},{5,13},{6,14},{7,15},{8,0},{9,1},... | collective-permute-start | bytes 393224 | tf_op jit(solution)/shard_map/ppermute | solution.py:50
  103.6 8.1 %collective-permute-start.35 = (bf16[32,2048]{1,0:T(8,128)(2,1)S(1)}, bf16[32,2048]{1,0:T(8,128)(2,1)S(1)}, u32[]{:S(2)}, u32[]{:S(2)}) collective-permute-start(bf16[32,2048]{1,0:T(8,128)(2,1)S(1)} %get-tuple-element.84), channel_id=1, source_target_pairs={{0,12},{1,13},{2,14},{3,15},{4,8},{5,9},{6,10},{7,11},{8,4},{9,5},... | collective-permute-start | bytes 393224 | tf_op jit(solution)/shard_map/ppermute | solution.py:50

commit v7 on v6

--- a/solution.py
+++ b/solution.py
@@ -73,8 +73,10 @@
     return lax.optimization_barrier((value, until))[0]
 
 
-def sum_kernel(mine, arrived, total):
-    total[...] = (mine[...] + arrived[...].astype(f32)).astype(total.dtype)
+def sum_kernel(mine, upper, lower, total):
+    half = upper.shape[0]
+    total[:half] = (mine[:half] + upper[...].astype(f32)).astype(total.dtype)
+    total[half:] = (mine[half:] + lower[...].astype(f32)).astype(total.dtype)
 
 
 def split_kernel(mine, near, beside, *pieces):
@@ -85,15 +87,15 @@
 
 
 def leave_pair(found, after):
-    mine_near, mine_beside, other_near, other_beside = found
-    arrived_beside = swap(other_beside, 1, 1, 2, True)
+    mine_near, mine_beside, other_near, *other_beside = found
+    arrived_beside = [swap(half, 1, 1, 2, True) for half in other_beside]
     arrived_near = swap(other_near, 1, 1, 2, True)
     (leaving,) = call(
         sum_kernel,
         [(mine_beside.shape, bf16)],
-        [VMEM] * 2,
+        [VMEM] * 3,
         mine_beside,
-        arrived_beside,
+        *arrived_beside,
         after=after,
     )
     return mine_near, arrived_near, leaving
@@ -240,8 +242,10 @@
     for low in range(0, features, size):
         span = slice(low, low + size)
         done = jnp.dot(hidden, down_ref[:, span], preferred_element_type=f32) * share
-        for k, out in enumerate(outs):
-            out[:, span] = done[k * quarter : (k + 1) * quarter].astype(out.dtype)
+        first = 0
+        for out in outs:
+            out[:, span] = done[first : first + out.shape[0]].astype(out.dtype)
+            first += out.shape[0]
 
 
 def run_expert(parts, routed, first_column, weights, after):
@@ -250,7 +254,8 @@
     quarter, width = parts[0].shape
     count = 4 * quarter
     wide = routed is None
-    outs = [((quarter, features), f32)] * 2 + [((quarter, features), bf16)] * 2
+    outs = [((quarter, features), f32)] * 2 + [((quarter, features), bf16)]
+    outs += [((quarter // 2, features), bf16)] * 2
     if wide:
         outs = outs + [((count, width - features), bf16)]
     found = call(
@@ -265,7 +270,7 @@
         limit=24,
         after=after,
     )
-    return found[:4], found[4] if wide else routed
+    return found[:5], found[5] if wide else routed
 
 
 def in_hbm(array):
@@ -308,13 +313,12 @@
     def worked(near, beside, routed, until):
         beside = held(beside, until)
         parts = [near, beside, swap(near, 1, 1, 2), swap(beside, 1, 1, 2)]
-        outs, columns = run_expert(parts, routed, first_column, weights, (until,))
-        return outs, columns
+        return run_expert(parts, routed, first_column, weights, (until,))
 
     outs, first_columns = worked(first, first_beside, routed[0], second)
     mine, near, leaving = leave_pair(outs, ())
-    outs2, second_columns = worked(second, second_beside, routed[1], outs[0])
-    first_back = swap(held(leaving, second_beside), 2, 1, 2, True)
+    first_back = swap(leaving, 2, 1, 2, True)
+    outs2, second_columns = worked(second, second_beside, routed[1], leaving)
     arrived, last = split_rows(mine, near, first_back, range(half), tokens)
     mine2, near2, leaving2 = leave_pair(outs2, (last,))
     second_back = swap(leaving2, 2, 1, 2, True)

time: 113 us -> 113 us (level)
    ppermute x36 -> x40, starting transfers between devices: 36.1 us -> 36.9 us  [swap(): lax.ppermute(value, 'expert', [(i, partner(i)) for i in range(count)])]
    ppermute x36 -> x40, waiting for transfers between devices: 55.4 us -> 55.4 us  [swap(): lax.ppermute(value, 'expert', [(i, partner(i)) for i in range(count)])]
  transfers between devices with their start and end apart: 36 -> 40, of which waited for: 14 -> 17; matrix products, arithmetic and copies ran while one was open for 0% -> 0% of each run, Pallas kernels for 16% -> 16%
where the time goes in v7:
time: 113 us
  waiting for transfers between devices  55.4 us (49%)
  starting transfers between devices  36.9 us (33%)
  Pallas kernels  20.7 us (18%)
    ppermute x40, waiting for transfers between devices, swap(): lax.ppermute(value, 'expert', [(i, partner(i)) for i in range(count)])  55.4 us
    ppermute x40, starting transfers between devices, swap(): lax.ppermute(value, 'expert', [(i, partner(i)) for i in range(count)])  36.9 us
    pallas_call x21, Pallas kernels, call(): pl.pallas_call(lambda *refs: kernel(*refs[len(after):]), out_shape=shapes...  20.7 us
  transfers between devices with their start and end apart: 40, of which 17 were waited for; matrix products, arithmetic and copies ran while one was open for 0% of the time, Pallas kernels for 16%

profile of v7, /device:TPU:0, one launch (start us, length us, event | category | flops | bytes accessed | tf_op | source)
XLA Modules:
  0.0 113.3 jit_solution(13209668820481981075)
XLA Ops:
  0.0 1.2 %shard_map.56.refs_1_ = bf16[32,2176]{1,0:T(8,128)(2,1)S(1)} custom-call(bf16[32,2048]{1,0:T(8,128)(2,1)} %bitcast.2, s32[2,2,8,16]{3,2,1,0:T(8,128)} %bitcast.4, f32[2,2048]{1,0:T(2,128)} %refs_2_.5), custom_call_target="tpu_custom_call" | custom-call | tf_op jit(solution)/shard_map/pallas_call | solution.py:28
  1.2 3.1 %collective-permute-start = (bf16[32,2176]{1,0:T(8,128)(2,1)S(1)}, bf16[32,2176]{1,0:T(8,128)(2,1)S(1)}, u32[]{:S(2)}, u32[]{:S(2)}) collective-permute-start(bf16[32,2176]{1,0:T(8,128)(2,1)S(1)} %shard_map.56.refs_1_), channel_id=1, source_target_pairs={{0,4},{1,5},{2,6},{3,7},{4,0},{5,1},{6,2},{7,3},{8,12},{9,13},{10,... | collective-permute-start | bytes 417800 | tf_op jit(solution)/shard_map/ppermute | solution.py:50
  4.3 2.5 %collective-permute-start.2 = (bf16[32,2176]{1,0:T(8,128)(2,1)S(1)}, bf16[32,2176]{1,0:T(8,128)(2,1)S(1)}, u32[]{:S(2)}, u32[]{:S(2)}) collective-permute-start(bf16[32,2176]{1,0:T(8,128)(2,1)S(1)} %shard_map.56.refs_1_), channel_id=1, source_target_pairs={{0,12},{1,13},{2,14},{3,15},{4,8},{5,9},{6,10},{7,11},{8,4},{9,5},... | collective-permute-start | bytes 417800 | tf_op jit(solution)/shard_map/ppermute | solution.py:50
  6.9 3.7 %shard_map.55 = (bf16[2048,1536]{1,0:T(8,128)(2,1)S(1)}, bf16[768,2048]{1,0:T(8,128)(2,1)S(1)}, f32[8,128]{1,0:T(8,128)S(1)}) custom-call(bf16[2,1,2048,1536]{3,2,1,0:T(8,128)(2,1)} %refs_1_.3, bf16[2,1,768,2048]{3,2,1,0:T(8,128)(2,1)} %refs_2_.4), custom_call_target="tpu_custom_call" | custom-call | tf_op jit(solution)/shard_map/pallas_call | solution.py:28
  10.8 1.6 %collective-permute-start.3 = (bf16[64,2176]{1,0:T(8,128)(2,1)S(1)}, bf16[64,2176]{1,0:T(8,128)(2,1)S(1)}, u32[]{:S(2)}, u32[]{:S(2)}) collective-permute-start(bf16[64,2176]{1,0:T(8,128)(2,1)S(1)} %shard_map.57.refs_0_.refs_1_), channel_id=1, source_target_pairs={{0,2},{1,3},{2,0},{3,1},{4,6},{5,7},{6,4},{7,5},{8,10},{9,11},{10,... | collective-permute-start | bytes 835592 | tf_op jit(solution)/shard_map/ppermute | solution.py:50
  12.4 2.0 %collective-permute-done.2.refs_2_ = bf16[32,2176]{1,0:T(8,128)(2,1)S(1)} collective-permute-done((bf16[32,2176]{1,0:T(8,128)(2,1)S(1)}, bf16[32,2176]{1,0:T(8,128)(2,1)S(1)}, u32[]{:S(2)}, u32[]{:S(2)}) %collective-permute-start.2) | collective-permute-done | bytes 139296 | tf_op jit(solution)/shard_map/ppermute | solution.py:50
  14.4 4.8 %collective-permute-done.1.refs_1_ = bf16[32,2176]{1,0:T(8,128)(2,1)S(1)} collective-permute-done((bf16[32,2176]{1,0:T(8,128)(2,1)S(1)}, bf16[32,2176]{1,0:T(8,128)(2,1)S(1)}, u32[]{:S(2)}, u32[]{:S(2)}) %collective-permute-start.1) | collective-permute-done | bytes 139296 | tf_op jit(solution)/shard_map/ppermute | solution.py:50
  19.3 0.6 collective-permute-done.3.refs_2_
  19.9 1.5 %collective-permute-start.8 = (bf16[64,2176]{1,0:T(8,128)(2,1)S(1)}, bf16[64,2176]{1,0:T(8,128)(2,1)S(1)}, u32[]{:S(2)}, u32[]{:S(2)}) collective-permute-start(bf16[64,2176]{1,0:T(8,128)(2,1)S(1)} %shard_map.58.refs_0_.refs_1_), channel_id=1, source_target_pairs={{0,2},{1,3},{2,0},{3,1},{4,6},{5,7},{6,4},{7,5},{8,10},{9,11},{10,... | collective-permute-start | bytes 835592 | tf_op jit(solution)/shard_map/ppermute | solution.py:50
  21.4 2.6 %shard_map.59 = (f32[64,2048]{1,0:T(8,128)S(1)}, f32[64,2048]{1,0:T(8,128)S(1)}, bf16[64,2048]{1,0:T(8,128)(2,1)S(1)}, bf16[32,2048]{1,0:T(8,128)(2,1)S(1)}, bf1...) custom-call(bf16[64,2176]{1,0:T(8,128)(2,1)S(1)} %shard_map.58.refs_0_.refs_1_, ...), custom_call_target="tpu_custom_call" | custom-call | tf_op jit(solution)/shard_map/pallas_call | solution.py:28
  24.0 0.3 collective-permute-start.6
  24.3 0.3 collective-permute-start.7
  24.8 0.6 collective-permute-done.6.refs_1_
  25.7 3.2 %collective-permute-done.8.refs_2_ = bf16[64,2176]{1,0:T(8,128)(2,1)S(1)} collective-permute-done((bf16[64,2176]{1,0:T(8,128)(2,1)S(1)}, bf16[64,2176]{1,0:T(8,128)(2,1)S(1)}, u32[]{:S(2)}, u32[]{:S(2)}) %collective-permute-start.8) | collective-permute-done | bytes 278560 | tf_op jit(solution)/shard_map/ppermute | solution.py:50
  28.9 0.5 collective-permute-start.11
  29.4 1.5 %collective-permute-start.12 = (bf16[64,2048]{1,0:T(8,128)(2,1)S(1)}, bf16[64,2048]{1,0:T(8,128)(2,1)S(1)}, u32[]{:S(2)}, u32[]{:S(2)}) collective-permute-start(bf16[64,2048]{1,0:T(8,128)(2,1)S(1)} %shard_map.60.refs_0_), channel_id=1, source_target_pairs={{0,2},{1,3},{2,0},{3,1},{4,6},{5,7},{6,4},{7,5},{8,10},{9,11},{10,... | collective-permute-start | bytes 786440 | tf_op jit(solution)/shard_map/ppermute | solution.py:50
  31.0 2.6 %shard_map.61 = (f32[64,2048]{1,0:T(8,128)S(1)}, f32[64,2048]{1,0:T(8,128)S(1)}, bf16[64,2048]{1,0:T(8,128)(2,1)S(1)}, bf16[32,2048]{1,0:T(8,128)(2,1)S(1)}, bf1...) custom-call(bf16[64,2048]{1,0:T(8,128)(2,1)S(1)} %shard_map.60.refs_0_, ...), custom_call_target="tpu_custom_call" | custom-call | tf_op jit(solution)/shard_map/pallas_call | solution.py:28
  33.7 0.5 collective-permute-start.16
  34.2 3.5 %collective-permute-done.12.refs_2_ = bf16[64,2048]{1,0:T(8,128)(2,1)S(1)} collective-permute-done((bf16[64,2048]{1,0:T(8,128)(2,1)S(1)}, bf16[64,2048]{1,0:T(8,128)(2,1)S(1)}, u32[]{:S(2)}, u32[]{:S(2)}) %collective-permute-start.12) | collective-permute-done | bytes 262176 | tf_op jit(solution)/shard_map/ppermute | solution.py:50
  37.9 1.6 %collective-permute-start.17 = (bf16[64,2048]{1,0:T(8,128)(2,1)S(1)}, bf16[64,2048]{1,0:T(8,128)(2,1)S(1)}, u32[]{:S(2)}, u32[]{:S(2)}) collective-permute-start(bf16[64,2048]{1,0:T(8,128)(2,1)S(1)} %shard_map.64), channel_id=1, source_target_pairs={{0,2},{1,3},{2,0},{3,1},{4,6},{5,7},{6,4},{7,5},{8,10},{9,11},{10,... | collective-permute-start | bytes 786440 | tf_op jit(solution)/shard_map/ppermute | solution.py:50
  39.5 1.8 %collective-permute-start.13 = (bf16[32,2048]{1,0:T(8,128)(2,1)S(1)}, bf16[32,2048]{1,0:T(8,128)(2,1)S(1)}, u32[]{:S(2)}, u32[]{:S(2)}) collective-permute-start(bf16[32,2048]{1,0:T(8,128)(2,1)S(1)} %get-tuple-element.60.refs_0_), channel_id=1, source_target_pairs={{0,4},{1,5},{2,6},{3,7},{4,0},{5,1},{6,2},{7,3},{8,12},{9,13},{10,... | collective-permute-start | bytes 393224 | tf_op jit(solution)/shard_map/ppermute | solution.py:50
  41.3 5.4 %collective-permute-done.17.refs_2_ = bf16[64,2048]{1,0:T(8,128)(2,1)S(1)} collective-permute-done((bf16[64,2048]{1,0:T(8,128)(2,1)S(1)}, bf16[64,2048]{1,0:T(8,128)(2,1)S(1)}, u32[]{:S(2)}, u32[]{:S(2)}) %collective-permute-start.17) | collective-permute-done | bytes 262176 | tf_op jit(solution)/shard_map/ppermute | solution.py:50
  46.7 2.9 %collective-permute-start.18 = (bf16[32,2048]{1,0:T(8,128)(2,1)S(1)}, bf16[32,2048]{1,0:T(8,128)(2,1)S(1)}, u32[]{:S(2)}, u32[]{:S(2)}) collective-permute-start(bf16[32,2048]{1,0:T(8,128)(2,1)S(1)} %get-tuple-element.65), channel_id=1, source_target_pairs={{0,8},{1,9},{2,10},{3,11},{4,12},{5,13},{6,14},{7,15},{8,0},{9,1},... | collective-permute-start | bytes 393224 | tf_op jit(solution)/shard_map/ppermute | solution.py:50
  49.6 1.3 %collective-permute-start.19 = (bf16[32,2048]{1,0:T(8,128)(2,1)S(1)}, bf16[32,2048]{1,0:T(8,128)(2,1)S(1)}, u32[]{:S(2)}, u32[]{:S(2)}) collective-permute-start(bf16[32,2048]{1,0:T(8,128)(2,1)S(1)} %get-tuple-element.66), channel_id=1, source_target_pairs={{0,12},{1,13},{2,14},{3,15},{4,8},{5,9},{6,10},{7,11},{8,4},{9,5},... | collective-permute-start | bytes 393224 | tf_op jit(solution)/shard_map/ppermute | solution.py:50
  50.9 3.7 %shard_map.62 = (bf16[2048,1536]{1,0:T(8,128)(2,1)S(1)}, bf16[768,2048]{1,0:T(8,128)(2,1)S(1)}, f32[8,128]{1,0:T(8,128)S(1)}) custom-call(f32[64,2048]{1,0:T(8,128)S(1)} %get-tuple-element.55.refs_0_, bf16[2,1,2048,1536]{3,2,1,0:T(8,128)(2,1)} %refs_1_.3, bf16[2,1,768,2048]{3,2,1,0:T(8,128)(2,1)} %refs_2_.4), custom_call_target="tpu_custom_call" | custom-call | tf_op jit(solution)/shard_map/pallas_call | solution.py:28
  54.7 5.0 %collective-permute-done.18.refs_5_ = bf16[32,2048]{1,0:T(8,128)(2,1)S(1)} collective-permute-done((bf16[32,2048]{1,0:T(8,128)(2,1)S(1)}, bf16[32,2048]{1,0:T(8,128)(2,1)S(1)}, u32[]{:S(2)}, u32[]{:S(2)}) %collective-permute-start.18) | collective-permute-done | bytes 131104 | tf_op jit(solution)/shard_map/ppermute | solution.py:50
  59.7 0.2 shard_map.66
  59.9 2.3 %collective-permute-start.20 = (bf16[32,2048]{1,0:T(8,128)(2,1)S(1)}, bf16[32,2048]{1,0:T(8,128)(2,1)S(1)}, u32[]{:S(2)}, u32[]{:S(2)}) collective-permute-start(bf16[32,2048]{1,0:T(8,128)(2,1)S(1)} %get-tuple-element.68.refs_1_), channel_id=1, source_target_pairs={{0,4},{1,5},{2,6},{3,7},{4,0},{5,1},{6,2},{7,3},{8,12},{9,13},{10,... | collective-permute-start | bytes 393224 | tf_op jit(solution)/shard_map/ppermute | solution.py:50
  62.2 3.2 %collective-permute-start.22 = (bf16[32,2048]{1,0:T(8,128)(2,1)S(1)}, bf16[32,2048]{1,0:T(8,128)(2,1)S(1)}, u32[]{:S(2)}, u32[]{:S(2)}) collective-permute-start(bf16[32,2048]{1,0:T(8,128)(2,1)S(1)} %get-tuple-element.68.refs_1_), channel_id=1, source_target_pairs={{0,12},{1,13},{2,14},{3,15},{4,8},{5,9},{6,10},{7,11},{8,4},{9,5},... | collective-permute-start | bytes 393224 | tf_op jit(solution)/shard_map/ppermute | solution.py:50
  65.6 1.6 %collective-permute-start.23 = (bf16[64,2048]{1,0:T(8,128)(2,1)S(1)}, bf16[64,2048]{1,0:T(8,128)(2,1)S(1)}, u32[]{:S(2)}, u32[]{:S(2)}) collective-permute-start(bf16[64,2048]{1,0:T(8,128)(2,1)S(1)} %shard_map.67.refs_0_.refs_1_), channel_id=1, source_target_pairs={{0,2},{1,3},{2,0},{3,1},{4,6},{5,7},{6,4},{7,5},{8,10},{9,11},{10,... | collective-permute-start | bytes 786440 | tf_op jit(solution)/shard_map/ppermute | solution.py:50
  67.2 5.6 %collective-permute-done.22.refs_2_ = bf16[32,2048]{1,0:T(8,128)(2,1)S(1)} collective-permute-done((bf16[32,2048]{1,0:T(8,128)(2,1)S(1)}, bf16[32,2048]{1,0:T(8,128)(2,1)S(1)}, u32[]{:S(2)}, u32[]{:S(2)}) %collective-permute-start.22) | collective-permute-done | bytes 131104 | tf_op jit(solution)/shard_map/ppermute | solution.py:50
  72.7 3.3 %collective-permute-done.21.refs_1_ = bf16[32,2048]{1,0:T(8,128)(2,1)S(1)} collective-permute-done((bf16[32,2048]{1,0:T(8,128)(2,1)S(1)}, bf16[32,2048]{1,0:T(8,128)(2,1)S(1)}, u32[]{:S(2)}, u32[]{:S(2)}) %collective-permute-start.21) | collective-permute-done | bytes 131104 | tf_op jit(solution)/shard_map/ppermute | solution.py:50
  76.2 1.6 %collective-permute-start.31 = (bf16[64,2048]{1,0:T(8,128)(2,1)S(1)}, bf16[64,2048]{1,0:T(8,128)(2,1)S(1)}, u32[]{:S(2)}, u32[]{:S(2)}) collective-permute-start(bf16[64,2048]{1,0:T(8,128)(2,1)S(1)} %shard_map.68.refs_0_.refs_1_), channel_id=1, source_target_pairs={{0,2},{1,3},{2,0},{3,1},{4,6},{5,7},{6,4},{7,5},{8,10},{9,11},{10,... | collective-permute-start | bytes 786440 | tf_op jit(solution)/shard_map/ppermute | solution.py:50
  77.7 2.6 %shard_map.69 = (f32[64,2048]{1,0:T(8,128)S(1)}, f32[64,2048]{1,0:T(8,128)S(1)}, bf16[64,2048]{1,0:T(8,128)(2,1)S(1)}, bf16[32,2048]{1,0:T(8,128)(2,1)S(1)}, bf16[32,2048]{1,0:T(8,128)(2,1)S(1)}) custom-call(bf16[64,2048]{1,0:T(8,128)(2,1)S(1)} %shard_map.68.refs_0_.refs_1_, bf16[64,2048]{1,0:T(8,128)(2,1)S(1)} %shard_map.67.refs_0_.refs_1_, ...), custom_call_target="tpu_custom_call" | custom-call | tf_op jit(solution)/shard_map/pallas_call | solution.py:28
  80.4 0.2 collective-permute-start.27
  80.6 0.3 collective-permute-start.28
  81.1 0.7 collective-permute-done.27.refs_1_
  82.0 2.9 %collective-permute-done.31.refs_2_ = bf16[64,2048]{1,0:T(8,128)(2,1)S(1)} collective-permute-done((bf16[64,2048]{1,0:T(8,128)(2,1)S(1)}, bf16[64,2048]{1,0:T(8,128)(2,1)S(1)}, u32[]{:S(2)}, u32[]{:S(2)}) %collective-permute-start.31) | collective-permute-done | bytes 262176 | tf_op jit(solution)/shard_map/ppermute | solution.py:50
  84.9 0.5 collective-permute-start.26
  85.4 1.5 %collective-permute-start.29 = (bf16[64,2048]{1,0:T(8,128)(2,1)S(1)}, bf16[64,2048]{1,0:T(8,128)(2,1)S(1)}, u32[]{:S(2)}, u32[]{:S(2)}) collective-permute-start(bf16[64,2048]{1,0:T(8,128)(2,1)S(1)} %shard_map.70.refs_0_), channel_id=1, source_target_pairs={{0,2},{1,3},{2,0},{3,1},{4,6},{5,7},{6,4},{7,5},{8,10},{9,11},{10,... | collective-permute-start | bytes 786440 | tf_op jit(solution)/shard_map/ppermute | solution.py:50
  86.9 2.6 %shard_map.72 = (f32[64,2048]{1,0:T(8,128)S(1)}, f32[64,2048]{1,0:T(8,128)S(1)}, bf16[64,2048]{1,0:T(8,128)(2,1)S(1)}, bf16[32,2048]{1,0:T(8,128)(2,1)S(1)}, bf16[32,2048]{1,0:T(8,128)(2,1)S(1)}) custom-call(bf16[64,2048]{1,0:T(8,128)(2,1)S(1)} %shard_map.70.refs_0_, bf16[64,2048]{1,0:T(8,128)(2,1)S(1)} %shard_map.68.refs_0_.refs_1_, ...), custom_call_target="tpu_custom_call" | custom-call | tf_op jit(solution)/shard_map/pallas_call | solution.py:28
  89.6 0.5 collective-permute-start.36
  90.2 3.4 %collective-permute-done.29.refs_2_ = bf16[64,2048]{1,0:T(8,128)(2,1)S(1)} collective-permute-done((bf16[64,2048]{1,0:T(8,128)(2,1)S(1)}, bf16[64,2048]{1,0:T(8,128)(2,1)S(1)}, u32[]{:S(2)}, u32[]{:S(2)}) %collective-permute-start.29) | collective-permute-done | bytes 262176 | tf_op jit(solution)/shard_map/ppermute | solution.py:50
  93.8 1.6 %collective-permute-start.37 = (bf16[64,2048]{1,0:T(8,128)(2,1)S(1)}, bf16[64,2048]{1,0:T(8,128)(2,1)S(1)}, u32[]{:S(2)}, u32[]{:S(2)}) collective-permute-start(bf16[64,2048]{1,0:T(8,128)(2,1)S(1)} %shard_map.73), channel_id=1, source_target_pairs={{0,2},{1,3},{2,0},{3,1},{4,6},{5,7},{6,4},{7,5},{8,10},{9,11},{10,... | collective-permute-start | bytes 786440 | tf_op jit(solution)/shard_map/ppermute | solution.py:50
  95.3 5.8 %collective-permute-done.37.refs_2_ = bf16[64,2048]{1,0:T(8,128)(2,1)S(1)} collective-permute-done((bf16[64,2048]{1,0:T(8,128)(2,1)S(1)}, bf16[64,2048]{1,0:T(8,128)(2,1)S(1)}, u32[]{:S(2)}, u32[]{:S(2)}) %collective-permute-start.37) | collective-permute-done | bytes 262176 | tf_op jit(solution)/shard_map/ppermute | solution.py:50
  101.3 3.1 %collective-permute-start.38 = (bf16[32,2048]{1,0:T(8,128)(2,1)S(1)}, bf16[32,2048]{1,0:T(8,128)(2,1)S(1)}, u32[]{:S(2)}, u32[]{:S(2)}) collective-permute-start(bf16[32,2048]{1,0:T(8,128)(2,1)S(1)} %get-tuple-element.87), channel_id=1, source_target_pairs={{0,8},{1,9},{2,10},{3,11},{4,12},{5,13},{6,14},{7,15},{8,0},{9,1},... | collective-permute-start | bytes 393224 | tf_op jit(solution)/shard_map/ppermute | solution.py:50
  104.4 8.1 %collective-permute-done.38.refs_3_ = bf16[32,2048]{1,0:T(8,128)(2,1)S(1)} collective-permute-done((bf16[32,2048]{1,0:T(8,128)(2,1)S(1)}, bf16[32,2048]{1,0:T(8,128)(2,1)S(1)}, u32[]{:S(2)}, u32[]{:S(2)}) %collective-permute-start.38) | collective-permute-done | bytes 131104 | tf_op jit(solution)/shard_map/ppermute | solution.py:50
  112.5 0.8 shard_map.75
  (57 shorter events, 2.1 us)
Async XLA Ops:
  1.2 9.4 %collective-permute-start = (bf16[32,2176]{1,0:T(8,128)(2,1)S(1)}, bf16[32,2176]{1,0:T(8,128)(2,1)S(1)}, u32[]{:S(2)}, u32[]{:S(2)}) collective-permute-start(bf16[32,2176]{1,0:T(8,128)(2,1)S(1)} %shard_map.56.refs_1_), channel_id=1, source_target_pairs={{0,4},{1,5},{2,6},{3,7},{4,0},{5,1},{6,2},{7,3},{8,12},{9,13},{10,... | collective-permute-start | bytes 417800 | tf_op jit(solution)/shard_map/ppermute | solution.py:50
  4.3 10.1 %collective-permute-start.2 = (bf16[32,2176]{1,0:T(8,128)(2,1)S(1)}, bf16[32,2176]{1,0:T(8,128)(2,1)S(1)}, u32[]{:S(2)}, u32[]{:S(2)}) collective-permute-start(bf16[32,2176]{1,0:T(8,128)(2,1)S(1)} %shard_map.56.refs_1_), channel_id=1, source_target_pairs={{0,12},{1,13},{2,14},{3,15},{4,8},{5,9},{6,10},{7,11},{8,4},{9,5},... | collective-permute-start | bytes 417800 | tf_op jit(solution)/shard_map/ppermute | solution.py:50
  6.8 12.5 %collective-permute-start.1 = (bf16[32,2176]{1,0:T(8,128)(2,1)S(1)}, bf16[32,2176]{1,0:T(8,128)(2,1)S(1)}, u32[]{:S(2)}, u32[]{:S(2)}) collective-permute-start(bf16[32,2176]{1,0:T(8,128)(2,1)S(1)} %shard_map.56.refs_1_), channel_id=1, source_target_pairs={{0,8},{1,9},{2,10},{3,11},{4,12},{5,13},{6,14},{7,15},{8,0},{9,1},... | collective-permute-start | bytes 417800 | tf_op jit(solution)/shard_map/ppermute | solution.py:50
  10.7 10.7 %collective-permute-start.4 = (bf16[64,2176]{1,0:T(8,128)(2,1)S(1)}, bf16[64,2176]{1,0:T(8,128)(2,1)S(1)}, u32[]{:S(2)}, u32[]{:S(2)}) collective-permute-start(bf16[64,2176]{1,0:T(8,128)(2,1)S(1)} %shard_map.57.refs_0_.refs_1_), channel_id=1, source_target_pairs={{0,1},{1,0},{2,3},{3,2},{4,5},{5,4},{6,7},{7,6},{8,9},{9,8},{10,11... | collective-permute-start | bytes 835592 | tf_op jit(solution)/shard_map/ppermute | solution.py:50
  10.8 9.1 %collective-permute-start.3 = (bf16[64,2176]{1,0:T(8,128)(2,1)S(1)}, bf16[64,2176]{1,0:T(8,128)(2,1)S(1)}, u32[]{:S(2)}, u32[]{:S(2)}) collective-permute-start(bf16[64,2176]{1,0:T(8,128)(2,1)S(1)} %shard_map.57.refs_0_.refs_1_), channel_id=1, source_target_pairs={{0,2},{1,3},{2,0},{3,1},{4,6},{5,7},{6,4},{7,5},{8,10},{9,11},{10,... | collective-permute-start | bytes 835592 | tf_op jit(solution)/shard_map/ppermute | solution.py:50
  19.8 1.6 %collective-permute-start.5 = (bf16[64,2176]{1,0:T(8,128)(2,1)S(1)}, bf16[64,2176]{1,0:T(8,128)(2,1)S(1)}, u32[]{:S(2)}, u32[]{:S(2)}) collective-permute-start(bf16[64,2176]{1,0:T(8,128)(2,1)S(1)} %collective-permute-done.3.refs_2_), channel_id=1, source_target_pairs={{0,1},{1,0},{2,3},{3,2},{4,5},{5,4},{6,7},{7,6},{8,9},{9,8},{10,11... | collective-permute-start | bytes 835592 | tf_op jit(solution)/shard_map/ppermute | solution.py:50
  19.9 9.1 %collective-permute-start.8 = (bf16[64,2176]{1,0:T(8,128)(2,1)S(1)}, bf16[64,2176]{1,0:T(8,128)(2,1)S(1)}, u32[]{:S(2)}, u32[]{:S(2)}) collective-permute-start(bf16[64,2176]{1,0:T(8,128)(2,1)S(1)} %shard_map.58.refs_0_.refs_1_), channel_id=1, source_target_pairs={{0,2},{1,3},{2,0},{3,1},{4,6},{5,7},{6,4},{7,5},{8,10},{9,11},{10,... | collective-permute-start | bytes 835592 | tf_op jit(solution)/shard_map/ppermute | solution.py:50
  24.0 1.4 %collective-permute-start.6 = (bf16[32,2048]{1,0:T(8,128)(2,1)S(1)}, bf16[32,2048]{1,0:T(8,128)(2,1)S(1)}, u32[]{:S(2)}, u32[]{:S(2)}) collective-permute-start(bf16[32,2048]{1,0:T(8,128)(2,1)S(1)} %get-tuple-element.52), channel_id=1, source_target_pairs={{0,1},{1,0},{2,3},{3,2},{4,5},{5,4},{6,7},{7,6},{8,9},{9,8},{10,11... | collective-permute-start | bytes 393224 | tf_op jit(solution)/shard_map/ppermute | solution.py:50
  24.3 1.3 %collective-permute-start.7 = (bf16[32,2048]{1,0:T(8,128)(2,1)S(1)}, bf16[32,2048]{1,0:T(8,128)(2,1)S(1)}, u32[]{:S(2)}, u32[]{:S(2)}) collective-permute-start(bf16[32,2048]{1,0:T(8,128)(2,1)S(1)} %get-tuple-element.53), channel_id=1, source_target_pairs={{0,1},{1,0},{2,3},{3,2},{4,5},{5,4},{6,7},{7,6},{8,9},{9,8},{10,11... | collective-permute-start | bytes 393224 | tf_op jit(solution)/shard_map/ppermute | solution.py:50
  24.6 6.4 %collective-permute-start.9 = (bf16[64,2176]{1,0:T(8,128)(2,1)S(1)}, bf16[64,2176]{1,0:T(8,128)(2,1)S(1)}, u32[]{:S(2)}, u32[]{:S(2)}) collective-permute-start(bf16[64,2176]{1,0:T(8,128)(2,1)S(1)} %shard_map.58.refs_0_.refs_1_), channel_id=1, source_target_pairs={{0,1},{1,0},{2,3},{3,2},{4,5},{5,4},{6,7},{7,6},{8,9},{9,8},{10,11... | collective-permute-start | bytes 835592 | tf_op jit(solution)/shard_map/ppermute | solution.py:50
  28.9 2.0 %collective-permute-start.10 = (bf16[64,2176]{1,0:T(8,128)(2,1)S(1)}, bf16[64,2176]{1,0:T(8,128)(2,1)S(1)}, u32[]{:S(2)}, u32[]{:S(2)}) collective-permute-start(bf16[64,2176]{1,0:T(8,128)(2,1)S(1)} %collective-permute-done.8.refs_2_), channel_id=1, source_target_pairs={{0,1},{1,0},{2,3},{3,2},{4,5},{5,4},{6,7},{7,6},{8,9},{9,8},{10,11... | collective-permute-start | bytes 835592 | tf_op jit(solution)/shard_map/ppermute | solution.py:50
  28.9 5.2 %collective-permute-start.11 = (bf16[64,2048]{1,0:T(8,128)(2,1)S(1)}, bf16[64,2048]{1,0:T(8,128)(2,1)S(1)}, u32[]{:S(2)}, u32[]{:S(2)}) collective-permute-start(bf16[64,2048]{1,0:T(8,128)(2,1)S(1)} %get-tuple-element.58), channel_id=1, source_target_pairs={{0,1},{1,0},{2,3},{3,2},{4,5},{5,4},{6,7},{7,6},{8,9},{9,8},{10,11... | collective-permute-start | bytes 786440 | tf_op jit(solution)/shard_map/ppermute | solution.py:50
  29.4 8.2 %collective-permute-start.12 = (bf16[64,2048]{1,0:T(8,128)(2,1)S(1)}, bf16[64,2048]{1,0:T(8,128)(2,1)S(1)}, u32[]{:S(2)}, u32[]{:S(2)}) collective-permute-start(bf16[64,2048]{1,0:T(8,128)(2,1)S(1)} %shard_map.60.refs_0_), channel_id=1, source_target_pairs={{0,2},{1,3},{2,0},{3,1},{4,6},{5,7},{6,4},{7,5},{8,10},{9,11},{10,... | collective-permute-start | bytes 786440 | tf_op jit(solution)/shard_map/ppermute | solution.py:50
  33.6 4.2 %collective-permute-start.15 = (bf16[32,2048]{1,0:T(8,128)(2,1)S(1)}, bf16[32,2048]{1,0:T(8,128)(2,1)S(1)}, u32[]{:S(2)}, u32[]{:S(2)}) collective-permute-start(bf16[32,2048]{1,0:T(8,128)(2,1)S(1)} %get-tuple-element.63), channel_id=1, source_target_pairs={{0,1},{1,0},{2,3},{3,2},{4,5},{5,4},{6,7},{7,6},{8,9},{9,8},{10,11... | collective-permute-start | bytes 393224 | tf_op jit(solution)/shard_map/ppermute | solution.py:50
  33.7 4.2 %collective-permute-start.16 = (bf16[32,2048]{1,0:T(8,128)(2,1)S(1)}, bf16[32,2048]{1,0:T(8,128)(2,1)S(1)}, u32[]{:S(2)}, u32[]{:S(2)}) collective-permute-start(bf16[32,2048]{1,0:T(8,128)(2,1)S(1)} %get-tuple-element.64), channel_id=1, source_target_pairs={{0,1},{1,0},{2,3},{3,2},{4,5},{5,4},{6,7},{7,6},{8,9},{9,8},{10,11... | collective-permute-start | bytes 393224 | tf_op jit(solution)/shard_map/ppermute | solution.py:50
  37.7 3.5 %collective-permute-start.14 = (bf16[64,2048]{1,0:T(8,128)(2,1)S(1)}, bf16[64,2048]{1,0:T(8,128)(2,1)S(1)}, u32[]{:S(2)}, u32[]{:S(2)}) collective-permute-start(bf16[64,2048]{1,0:T(8,128)(2,1)S(1)} %get-tuple-element.61), channel_id=1, source_target_pairs={{0,1},{1,0},{2,3},{3,2},{4,5},{5,4},{6,7},{7,6},{8,9},{9,8},{10,11... | collective-permute-start | bytes 786440 | tf_op jit(solution)/shard_map/ppermute | solution.py:50
  37.9 8.8 %collective-permute-start.17 = (bf16[64,2048]{1,0:T(8,128)(2,1)S(1)}, bf16[64,2048]{1,0:T(8,128)(2,1)S(1)}, u32[]{:S(2)}, u32[]{:S(2)}) collective-permute-start(bf16[64,2048]{1,0:T(8,128)(2,1)S(1)} %shard_map.64), channel_id=1, source_target_pairs={{0,2},{1,3},{2,0},{3,1},{4,6},{5,7},{6,4},{7,5},{8,10},{9,11},{10,... | collective-permute-start | bytes 786440 | tf_op jit(solution)/shard_map/ppermute | solution.py:50
  39.5 15.2 %collective-permute-start.13 = (bf16[32,2048]{1,0:T(8,128)(2,1)S(1)}, bf16[32,2048]{1,0:T(8,128)(2,1)S(1)}, u32[]{:S(2)}, u32[]{:S(2)}) collective-permute-start(bf16[32,2048]{1,0:T(8,128)(2,1)S(1)} %get-tuple-element.60.refs_0_), channel_id=1, source_target_pairs={{0,4},{1,5},{2,6},{3,7},{4,0},{5,1},{6,2},{7,3},{8,12},{9,13},{10,... | collective-permute-start | bytes 393224 | tf_op jit(solution)/shard_map/ppermute | solution.py:50
  46.7 12.9 %collective-permute-start.18 = (bf16[32,2048]{1,0:T(8,128)(2,1)S(1)}, bf16[32,2048]{1,0:T(8,128)(2,1)S(1)}, u32[]{:S(2)}, u32[]{:S(2)}) collective-permute-start(bf16[32,2048]{1,0:T(8,128)(2,1)S(1)} %get-tuple-element.65), channel_id=1, source_target_pairs={{0,8},{1,9},{2,10},{3,11},{4,12},{5,13},{6,14},{7,15},{8,0},{9,1},... | collective-permute-start | bytes 393224 | tf_op jit(solution)/shard_map/ppermute | solution.py:50
  49.6 10.1 %copy-start = (bf16[2,16,2048]{2,1,0:T(8,128)(2,1)S(1)}, bf16[2,16,2048]{2,1,0:T(8,128)(2,1)}, u32[]{:S(2)}) copy-start(bf16[2,16,2048]{2,1,0:T(8,128)(2,1)} %param.5) | copy-start | bytes 393220
  49.6 10.1 %copy-start.1 = (f32[2,2048]{1,0:T(2,128)S(1)}, f32[2,2048]{1,0:T(2,128)}, u32[]{:S(2)}) copy-start(f32[2,2048]{1,0:T(2,128)} %refs_2_.5) | copy-start | bytes 49156
  49.6 10.1 %collective-permute-start.19 = (bf16[32,2048]{1,0:T(8,128)(2,1)S(1)}, bf16[32,2048]{1,0:T(8,128)(2,1)S(1)}, u32[]{:S(2)}, u32[]{:S(2)}) collective-permute-start(bf16[32,2048]{1,0:T(8,128)(2,1)S(1)} %get-tuple-element.66), channel_id=1, source_target_pairs={{0,12},{1,13},{2,14},{3,15},{4,8},{5,9},{6,10},{7,11},{8,4},{9,5},... | collective-permute-start | bytes 393224 | tf_op jit(solution)/shard_map/ppermute | solution.py:50
  59.9 5.6 %collective-permute-start.20 = (bf16[32,2048]{1,0:T(8,128)(2,1)S(1)}, bf16[32,2048]{1,0:T(8,128)(2,1)S(1)}, u32[]{:S(2)}, u32[]{:S(2)}) collective-permute-start(bf16[32,2048]{1,0:T(8,128)(2,1)S(1)} %get-tuple-element.68.refs_1_), channel_id=1, source_target_pairs={{0,4},{1,5},{2,6},{3,7},{4,0},{5,1},{6,2},{7,3},{8,12},{9,13},{10,... | collective-permute-start | bytes 393224 | tf_op jit(solution)/shard_map/ppermute | solution.py:50
  62.2 10.5 %collective-permute-start.22 = (bf16[32,2048]{1,0:T(8,128)(2,1)S(1)}, bf16[32,2048]{1,0:T(8,128)(2,1)S(1)}, u32[]{:S(2)}, u32[]{:S(2)}) collective-permute-start(bf16[32,2048]{1,0:T(8,128)(2,1)S(1)} %get-tuple-element.68.refs_1_), channel_id=1, source_target_pairs={{0,12},{1,13},{2,14},{3,15},{4,8},{5,9},{6,10},{7,11},{8,4},{9,5},... | collective-permute-start | bytes 393224 | tf_op jit(solution)/shard_map/ppermute | solution.py:50
  65.5 10.6 %collective-permute-start.21 = (bf16[32,2048]{1,0:T(8,128)(2,1)S(1)}, bf16[32,2048]{1,0:T(8,128)(2,1)S(1)}, u32[]{:S(2)}, u32[]{:S(2)}) collective-permute-start(bf16[32,2048]{1,0:T(8,128)(2,1)S(1)} %get-tuple-element.68.refs_1_), channel_id=1, source_target_pairs={{0,8},{1,9},{2,10},{3,11},{4,12},{5,13},{6,14},{7,15},{8,0},{9,1},... | collective-permute-start | bytes 393224 | tf_op jit(solution)/shard_map/ppermute | solution.py:50
  65.5 12.3 %collective-permute-start.24 = (bf16[64,2048]{1,0:T(8,128)(2,1)S(1)}, bf16[64,2048]{1,0:T(8,128)(2,1)S(1)}, u32[]{:S(2)}, u32[]{:S(2)}) collective-permute-start(bf16[64,2048]{1,0:T(8,128)(2,1)S(1)} %shard_map.67.refs_0_.refs_1_), channel_id=1, source_target_pairs={{0,1},{1,0},{2,3},{3,2},{4,5},{5,4},{6,7},{7,6},{8,9},{9,8},{10,11... | collective-permute-start | bytes 786440 | tf_op jit(solution)/shard_map/ppermute | solution.py:50
  65.6 10.5 %collective-permute-start.23 = (bf16[64,2048]{1,0:T(8,128)(2,1)S(1)}, bf16[64,2048]{1,0:T(8,128)(2,1)S(1)}, u32[]{:S(2)}, u32[]{:S(2)}) collective-permute-start(bf16[64,2048]{1,0:T(8,128)(2,1)S(1)} %shard_map.67.refs_0_.refs_1_), channel_id=1, source_target_pairs={{0,2},{1,3},{2,0},{3,1},{4,6},{5,7},{6,4},{7,5},{8,10},{9,11},{10,... | collective-permute-start | bytes 786440 | tf_op jit(solution)/shard_map/ppermute | solution.py:50
  76.1 1.7 %collective-permute-start.25 = (bf16[64,2048]{1,0:T(8,128)(2,1)S(1)}, bf16[64,2048]{1,0:T(8,128)(2,1)S(1)}, u32[]{:S(2)}, u32[]{:S(2)}) collective-permute-start(bf16[64,2048]{1,0:T(8,128)(2,1)S(1)} %collective-permute-done.23.refs_2_), channel_id=1, source_target_pairs={{0,1},{1,0},{2,3},{3,2},{4,5},{5,4},{6,7},{7,6},{8,9},{9,8},{10,11... | collective-permute-start | bytes 786440 | tf_op jit(solution)/shard_map/ppermute | solution.py:50
  76.2 8.7 %collective-permute-start.31 = (bf16[64,2048]{1,0:T(8,128)(2,1)S(1)}, bf16[64,2048]{1,0:T(8,128)(2,1)S(1)}, u32[]{:S(2)}, u32[]{:S(2)}) collective-permute-start(bf16[64,2048]{1,0:T(8,128)(2,1)S(1)} %shard_map.68.refs_0_.refs_1_), channel_id=1, source_target_pairs={{0,2},{1,3},{2,0},{3,1},{4,6},{5,7},{6,4},{7,5},{8,10},{9,11},{10,... | collective-permute-start | bytes 786440 | tf_op jit(solution)/shard_map/ppermute | solution.py:50
  80.4 1.4 %collective-permute-start.27 = (bf16[32,2048]{1,0:T(8,128)(2,1)S(1)}, bf16[32,2048]{1,0:T(8,128)(2,1)S(1)}, u32[]{:S(2)}, u32[]{:S(2)}) collective-permute-start(bf16[32,2048]{1,0:T(8,128)(2,1)S(1)} %get-tuple-element.76), channel_id=1, source_target_pairs={{0,1},{1,0},{2,3},{3,2},{4,5},{5,4},{6,7},{7,6},{8,9},{9,8},{10,11... | collective-permute-start | bytes 393224 | tf_op jit(solution)/shard_map/ppermute | solution.py:50
  80.6 1.4 %collective-permute-start.28 = (bf16[32,2048]{1,0:T(8,128)(2,1)S(1)}, bf16[32,2048]{1,0:T(8,128)(2,1)S(1)}, u32[]{:S(2)}, u32[]{:S(2)}) collective-permute-start(bf16[32,2048]{1,0:T(8,128)(2,1)S(1)} %get-tuple-element.77), channel_id=1, source_target_pairs={{0,1},{1,0},{2,3},{3,2},{4,5},{5,4},{6,7},{7,6},{8,9},{9,8},{10,11... | collective-permute-start | bytes 393224 | tf_op jit(solution)/shard_map/ppermute | solution.py:50
  80.9 6.0 %collective-permute-start.32 = (bf16[64,2048]{1,0:T(8,128)(2,1)S(1)}, bf16[64,2048]{1,0:T(8,128)(2,1)S(1)}, u32[]{:S(2)}, u32[]{:S(2)}) collective-permute-start(bf16[64,2048]{1,0:T(8,128)(2,1)S(1)} %shard_map.68.refs_0_.refs_1_), channel_id=1, source_target_pairs={{0,1},{1,0},{2,3},{3,2},{4,5},{5,4},{6,7},{7,6},{8,9},{9,8},{10,11... | collective-permute-start | bytes 786440 | tf_op jit(solution)/shard_map/ppermute | solution.py:50
  84.9 2.0 %collective-permute-start.33 = (bf16[64,2048]{1,0:T(8,128)(2,1)S(1)}, bf16[64,2048]{1,0:T(8,128)(2,1)S(1)}, u32[]{:S(2)}, u32[]{:S(2)}) collective-permute-start(bf16[64,2048]{1,0:T(8,128)(2,1)S(1)} %collective-permute-done.31.refs_2_), channel_id=1, source_target_pairs={{0,1},{1,0},{2,3},{3,2},{4,5},{5,4},{6,7},{7,6},{8,9},{9,8},{10,11... | collective-permute-start | bytes 786440 | tf_op jit(solution)/shard_map/ppermute | solution.py:50
  84.9 5.3 %collective-permute-start.26 = (bf16[64,2048]{1,0:T(8,128)(2,1)S(1)}, bf16[64,2048]{1,0:T(8,128)(2,1)S(1)}, u32[]{:S(2)}, u32[]{:S(2)}) collective-permute-start(bf16[64,2048]{1,0:T(8,128)(2,1)S(1)} %get-tuple-element.74), channel_id=1, source_target_pairs={{0,1},{1,0},{2,3},{3,2},{4,5},{5,4},{6,7},{7,6},{8,9},{9,8},{10,11... | collective-permute-start | bytes 786440 | tf_op jit(solution)/shard_map/ppermute | solution.py:50
  85.4 8.2 %collective-permute-start.29 = (bf16[64,2048]{1,0:T(8,128)(2,1)S(1)}, bf16[64,2048]{1,0:T(8,128)(2,1)S(1)}, u32[]{:S(2)}, u32[]{:S(2)}) collective-permute-start(bf16[64,2048]{1,0:T(8,128)(2,1)S(1)} %shard_map.70.refs_0_), channel_id=1, source_target_pairs={{0,2},{1,3},{2,0},{3,1},{4,6},{5,7},{6,4},{7,5},{8,10},{9,11},{10,... | collective-permute-start | bytes 786440 | tf_op jit(solution)/shard_map/ppermute | solution.py:50
  89.5 4.2 %collective-permute-start.35 = (bf16[32,2048]{1,0:T(8,128)(2,1)S(1)}, bf16[32,2048]{1,0:T(8,128)(2,1)S(1)}, u32[]{:S(2)}, u32[]{:S(2)}) collective-permute-start(bf16[32,2048]{1,0:T(8,128)(2,1)S(1)} %get-tuple-element.85), channel_id=1, source_target_pairs={{0,1},{1,0},{2,3},{3,2},{4,5},{5,4},{6,7},{7,6},{8,9},{9,8},{10,11... | collective-permute-start | bytes 393224 | tf_op jit(solution)/shard_map/ppermute | solution.py:50
  89.6 4.1 %collective-permute-start.36 = (bf16[32,2048]{1,0:T(8,128)(2,1)S(1)}, bf16[32,2048]{1,0:T(8,128)(2,1)S(1)}, u32[]{:S(2)}, u32[]{:S(2)}) collective-permute-start(bf16[32,2048]{1,0:T(8,128)(2,1)S(1)} %get-tuple-element.86), channel_id=1, source_target_pairs={{0,1},{1,0},{2,3},{3,2},{4,5},{5,4},{6,7},{7,6},{8,9},{9,8},{10,11... | collective-permute-start | bytes 393224 | tf_op jit(solution)/shard_map/ppermute | solution.py:50
  90.1 5.2 %collective-permute-start.34 = (bf16[64,2048]{1,0:T(8,128)(2,1)S(1)}, bf16[64,2048]{1,0:T(8,128)(2,1)S(1)}, u32[]{:S(2)}, u32[]{:S(2)}) collective-permute-start(bf16[64,2048]{1,0:T(8,128)(2,1)S(1)} %get-tuple-element.83), channel_id=1, source_target_pairs={{0,1},{1,0},{2,3},{3,2},{4,5},{5,4},{6,7},{7,6},{8,9},{9,8},{10,11... | collective-permute-start | bytes 786440 | tf_op jit(solution)/shard_map/ppermute | solution.py:50
  93.8 7.4 %collective-permute-start.37 = (bf16[64,2048]{1,0:T(8,128)(2,1)S(1)}, bf16[64,2048]{1,0:T(8,128)(2,1)S(1)}, u32[]{:S(2)}, u32[]{:S(2)}) collective-permute-start(bf16[64,2048]{1,0:T(8,128)(2,1)S(1)} %shard_map.73), channel_id=1, source_target_pairs={{0,2},{1,3},{2,0},{3,1},{4,6},{5,7},{6,4},{7,5},{8,10},{9,11},{10,... | collective-permute-start | bytes 786440 | tf_op jit(solution)/shard_map/ppermute | solution.py:50
  95.3 9.1 %collective-permute-start.30 = (bf16[32,2048]{1,0:T(8,128)(2,1)S(1)}, bf16[32,2048]{1,0:T(8,128)(2,1)S(1)}, u32[]{:S(2)}, u32[]{:S(2)}) collective-permute-start(bf16[32,2048]{1,0:T(8,128)(2,1)S(1)} %get-tuple-element.79.refs_0_), channel_id=1, source_target_pairs={{0,4},{1,5},{2,6},{3,7},{4,0},{5,1},{6,2},{7,3},{8,12},{9,13},{10,... | collective-permute-start | bytes 393224 | tf_op jit(solution)/shard_map/ppermute | solution.py:50
  101.3 11.2 %collective-permute-start.38 = (bf16[32,2048]{1,0:T(8,128)(2,1)S(1)}, bf16[32,2048]{1,0:T(8,128)(2,1)S(1)}, u32[]{:S(2)}, u32[]{:S(2)}) collective-permute-start(bf16[32,2048]{1,0:T(8,128)(2,1)S(1)} %get-tuple-element.87), channel_id=1, source_target_pairs={{0,8},{1,9},{2,10},{3,11},{4,12},{5,13},{6,14},{7,15},{8,0},{9,1},... | collective-permute-start | bytes 393224 | tf_op jit(solution)/shard_map/ppermute | solution.py:50
  104.4 8.1 %collective-permute-start.39 = (bf16[32,2048]{1,0:T(8,128)(2,1)S(1)}, bf16[32,2048]{1,0:T(8,128)(2,1)S(1)}, u32[]{:S(2)}, u32[]{:S(2)}) collective-permute-start(bf16[32,2048]{1,0:T(8,128)(2,1)S(1)} %get-tuple-element.88), channel_id=1, source_target_pairs={{0,12},{1,13},{2,14},{3,15},{4,8},{5,9},{6,10},{7,11},{8,4},{9,5},... | collective-permute-start | bytes 393224 | tf_op jit(solution)/shard_map/ppermute | solution.py:50

commit v8 on v5

--- a/solution.py
+++ b/solution.py
@@ -10,6 +10,7 @@
 eps = 1e-06
 LANES = 128
 MIB = 2**20
+CUTS = 2
 VMEM = pl.BlockSpec(memory_space=pltpu.VMEM)
 ANY = pl.BlockSpec(memory_space=pl.ANY)
 bf16, f32 = jnp.bfloat16, jnp.float32
@@ -54,6 +55,17 @@
     rows, size = parts[0].shape[0], count // len(wholes)
     for k, part in enumerate(parts):
         wholes[k // size][k % size * rows : (k % size + 1) * rows] = part[...]
+
+
+def cut_kernel(whole, *parts):
+    rows = parts[0].shape[0]
+    for k, part in enumerate(parts):
+        part[...] = whole[k * rows : (k + 1) * rows]
+
+
+def cut_rows(whole, count, after):
+    shape = (whole.shape[0] // count, whole.shape[1])
+    return call(cut_kernel, [(shape, whole.dtype)] * count, [VMEM], whole, after=after)
 
 
 def held(value, until):
@@ -80,8 +92,10 @@
     return batches
 
 
-def sum_kernel(mine, arrived, total):
-    total[...] = (mine[...] + arrived[...].astype(f32)).astype(total.dtype)
+def sum_kernel(mine, upper, lower, total):
+    half = upper.shape[0]
+    total[:half] = (mine[:half] + upper[...].astype(f32)).astype(total.dtype)
+    total[half:] = (mine[half:] + lower[...].astype(f32)).astype(total.dtype)
 
 
 def split_kernel(mine, near, beside, *pieces):
@@ -92,15 +106,15 @@
 
 
 def leave_pair(found, after):
-    mine_near, mine_beside, other_near, other_beside = found
-    arrived_beside = swap(other_beside, 1, 1, 2, True)
+    mine_near, mine_beside, other_near, *other_beside = found
+    arrived_beside = [swap(half, 1, 1, 2, True) for half in other_beside]
     arrived_near = swap(other_near, 1, 1, 2, True)
     (leaving,) = call(
         sum_kernel,
         [(mine_beside.shape, bf16)],
-        [VMEM] * 2,
+        [VMEM] * 3,
         mine_beside,
-        arrived_beside,
+        *arrived_beside,
         after=after,
     )
     return mine_near, arrived_near, leaving
@@ -219,17 +233,17 @@
     return size
 
 
-def expert_kernel(first_column, wide, *refs):
+def expert_kernel(count, first_column, wide, *refs):
+    parts, refs = refs[:count], refs[count:]
     if wide:
-        parts, refs = refs[:4], refs[4:]
         gate_up_ref, down_ref, *outs, routed_ref, rows_ref, hidden_ref = refs
     else:
-        parts, refs = refs[:4], refs[4:]
         routed_ref, gate_up_ref, down_ref, *outs, rows_ref, hidden_ref = refs
     hidden_size, features = down_ref.shape
-    quarter = parts[0].shape[0]
-    for k, part in enumerate(parts):
-        span = slice(k * quarter, (k + 1) * quarter)
+    first = 0
+    for part in parts:
+        span = slice(first, first + part.shape[0])
+        first += part.shape[0]
         rows_ref[span] = part[:, :features]
         if wide:
             routed_ref[span] = part[:, features:]
@@ -249,23 +263,27 @@
     for low in range(0, features, size):
         span = slice(low, low + size)
         done = jnp.dot(hidden, down_ref[:, span], preferred_element_type=f32) * share
-        for k, out in enumerate(outs):
-            out[:, span] = done[k * quarter : (k + 1) * quarter].astype(out.dtype)
+        first = 0
+        for out in outs:
+            out[:, span] = done[first : first + out.shape[0]].astype(out.dtype)
+            first += out.shape[0]
 
 
 def run_expert(parts, routed, first_column, weights, after):
     gate_up, down_proj, _ = weights
     hidden_size, features = down_proj.shape
-    quarter, width = parts[0].shape
-    count = 4 * quarter
+    width = parts[0].shape[1]
+    count = sum(part.shape[0] for part in parts)
+    quarter = count // 4
     wide = routed is None
-    outs = [((quarter, features), f32)] * 2 + [((quarter, features), bf16)] * 2
+    outs = [((quarter, features), f32)] * 2 + [((quarter, features), bf16)]
+    outs += [((quarter // 2, features), bf16)] * 2
     if wide:
         outs = outs + [((count, width - features), bf16)]
     found = call(
-        functools.partial(expert_kernel, first_column, wide),
+        functools.partial(expert_kernel, len(parts), first_column, wide),
         outs,
-        [VMEM] * (6 if wide else 7),
+        [VMEM] * (len(parts) + (2 if wide else 3)),
         *parts,
         *([] if wide else [routed]),
         gate_up,
@@ -274,7 +292,7 @@
         limit=24,
         after=after,
     )
-    return found[:4], found[4] if wide else routed
+    return found[:5], found[5] if wide else routed
 
 
 def in_hbm(array):
@@ -309,8 +327,8 @@
     columns, returned, after, worked = [], [], (), ()
     distances = [range(far // 2, far), range(far // 2)]
     for place, (near, beside) in enumerate(gather_rows(rows, loaded)):
-        beside = held(beside, left[2] if place else None)
-        parts = [near, beside, swap(near, 1, 1, 2), swap(beside, 1, 1, 2)]
+        parts = [near, *cut_rows(beside, CUTS, (left[2],))] if place else [near, beside]
+        parts += [swap(part, 1, 1, 2) for part in parts]
         outs, kept = run_expert(
             parts, None if routed is None else routed[place], first_column, weights, worked
         )

time: 119 us -> 115 us (0.966)
  starting transfers between devices: 43.4 us -> 39.9 us
    ppermute x36 -> x42, starting transfers between devices: 43.4 us -> 39.9 us  [swap(): lax.ppermute(value, 'expert', [(i, partner(i)) for i in range(count)])]
    ppermute x36 -> x42, waiting for transfers between devices: 54.8 us -> 53.8 us  [swap(): lax.ppermute(value, 'expert', [(i, partner(i)) for i in range(count)])]
    pallas_call x19 -> x21, Pallas kernels: 20.7 us -> 20.8 us  [call(): pl.pallas_call(lambda *refs: kernel(*refs[len(after):]), out_shape=shapes...]
  transfers between devices with their start and end apart: 36 -> 42, of which waited for: 17 -> 22; matrix products, arithmetic and copies ran while one was open for 0% -> 0% of each run, Pallas kernels for 13% -> 16%
where the time goes in v8:
time: 115 us
  waiting for transfers between devices  53.8 us (47%)
  starting transfers between devices  39.9 us (35%)
  Pallas kernels  20.8 us (18%)
    ppermute x42, waiting for transfers between devices, swap(): lax.ppermute(value, 'expert', [(i, partner(i)) for i in range(count)])  53.8 us
    ppermute x42, starting transfers between devices, swap(): lax.ppermute(value, 'expert', [(i, partner(i)) for i in range(count)])  39.9 us
    pallas_call x21, Pallas kernels, call(): pl.pallas_call(lambda *refs: kernel(*refs[len(after):]), out_shape=shapes...  20.8 us
  transfers between devices with their start and end apart: 42, of which 22 were waited for; matrix products, arithmetic and copies ran while one was open for 0% of the time, Pallas kernels for 16%

profile of v8, /device:TPU:0, one launch (start us, length us, event | category | flops | bytes accessed | tf_op | source)
XLA Modules:
  0.0 114.7 jit_solution(6693722719171608077)
XLA Ops:
  0.0 1.2 %shard_map.56.refs_3_ = bf16[32,2176]{1,0:T(8,128)(2,1)S(1)} custom-call(bf16[32,2048]{1,0:T(8,128)(2,1)} %bitcast.2, s32[2,2,8,16]{3,2,1,0:T(8,128)} %bitcast.4, f32[2,2048]{1,0:T(2,128)} %refs_2_.5), custom_call_target="tpu_custom_call" | custom-call | tf_op jit(solution)/shard_map/pallas_call | solution.py:28
  1.2 4.1 %collective-permute-start = (bf16[32,2176]{1,0:T(8,128)(2,1)S(1)}, bf16[32,2176]{1,0:T(8,128)(2,1)S(1)}, u32[]{:S(2)}, u32[]{:S(2)}) collective-permute-start(bf16[32,2176]{1,0:T(8,128)(2,1)S(1)} %shard_map.56.refs_3_), channel_id=1, source_target_pairs={{0,8},{1,9},{2,10},{3,11},{4,12},{5,13},{6,14},{7,15},{8,0},{9,1},... | collective-permute-start | bytes 417800 | tf_op jit(solution)/shard_map/ppermute | solution.py:50
  5.3 1.3 %collective-permute-start.1 = (bf16[32,2176]{1,0:T(8,128)(2,1)S(1)}, bf16[32,2176]{1,0:T(8,128)(2,1)S(1)}, u32[]{:S(2)}, u32[]{:S(2)}) collective-permute-start(bf16[32,2176]{1,0:T(8,128)(2,1)S(1)} %shard_map.56.refs_3_), channel_id=1, source_target_pairs={{0,12},{1,13},{2,14},{3,15},{4,8},{5,9},{6,10},{7,11},{8,4},{9,5},... | collective-permute-start | bytes 417800 | tf_op jit(solution)/shard_map/ppermute | solution.py:50
  6.9 3.7 %shard_map.55 = (bf16[2048,1536]{1,0:T(8,128)(2,1)S(1)}, bf16[768,2048]{1,0:T(8,128)(2,1)S(1)}, f32[8,128]{1,0:T(8,128)S(1)}) custom-call(bf16[2,1,2048,1536]{3,2,1,0:T(8,128)(2,1)} %refs_1_.3, bf16[2,1,768,2048]{3,2,1,0:T(8,128)(2,1)} %refs_2_.4), custom_call_target="tpu_custom_call" | custom-call | tf_op jit(solution)/shard_map/pallas_call | solution.py:28
  10.7 5.2 %collective-permute-done.refs_1_ = bf16[32,2176]{1,0:T(8,128)(2,1)S(1)} collective-permute-done((bf16[32,2176]{1,0:T(8,128)(2,1)S(1)}, bf16[32,2176]{1,0:T(8,128)(2,1)S(1)}, u32[]{:S(2)}, u32[]{:S(2)}) %collective-permute-start) | collective-permute-done | bytes 139296 | tf_op jit(solution)/shard_map/ppermute | solution.py:50
  15.8 0.5 collective-permute-done.2.refs_4_
  16.4 1.6 %collective-permute-start.3 = (bf16[64,2176]{1,0:T(8,128)(2,1)S(1)}, bf16[64,2176]{1,0:T(8,128)(2,1)S(1)}, u32[]{:S(2)}, u32[]{:S(2)}) collective-permute-start(bf16[64,2176]{1,0:T(8,128)(2,1)S(1)} %get-tuple-element.54.refs_0_), channel_id=1, source_target_pairs={{0,2},{1,3},{2,0},{3,1},{4,6},{5,7},{6,4},{7,5},{8,10},{9,11},{10,... | collective-permute-start | bytes 835592 | tf_op jit(solution)/shard_map/ppermute | solution.py:50
  18.0 5.0 %collective-permute-done.3.refs_1_ = bf16[64,2176]{1,0:T(8,128)(2,1)S(1)} collective-permute-done((bf16[64,2176]{1,0:T(8,128)(2,1)S(1)}, bf16[64,2176]{1,0:T(8,128)(2,1)S(1)}, u32[]{:S(2)}, u32[]{:S(2)}) %collective-permute-start.3) | collective-permute-done | bytes 278560 | tf_op jit(solution)/shard_map/ppermute | solution.py:50
  23.0 1.6 %collective-permute-start.8 = (bf16[64,2176]{1,0:T(8,128)(2,1)S(1)}, bf16[64,2176]{1,0:T(8,128)(2,1)S(1)}, u32[]{:S(2)}, u32[]{:S(2)}) collective-permute-start(bf16[64,2176]{1,0:T(8,128)(2,1)S(1)} %get-tuple-element.61.refs_1_), channel_id=1, source_target_pairs={{0,2},{1,3},{2,0},{3,1},{4,6},{5,7},{6,4},{7,5},{8,10},{9,11},{10,... | collective-permute-start | bytes 835592 | tf_op jit(solution)/shard_map/ppermute | solution.py:50
  24.8 2.6 %shard_map.58 = (f32[64,2048]{1,0:T(8,128)S(1)}, f32[64,2048]{1,0:T(8,128)S(1)}, bf16[64,2048]{1,0:T(8,128)(2,1)S(1)}, bf16[32,2048]{1,0:T(8,128)(2,1)S(1)}, bf1...) custom-call(bf16[64,2176]{1,0:T(8,128)(2,1)S(1)} %get-tuple-element.54.refs_0_, ...), custom_call_target="tpu_custom_call" | custom-call | tf_op jit(solution)/shard_map/pallas_call | solution.py:28
  28.0 0.8 collective-permute-done.6.refs_1_
  29.2 2.9 %collective-permute-done.8.refs_1_ = bf16[64,2176]{1,0:T(8,128)(2,1)S(1)} collective-permute-done((bf16[64,2176]{1,0:T(8,128)(2,1)S(1)}, bf16[64,2176]{1,0:T(8,128)(2,1)S(1)}, u32[]{:S(2)}, u32[]{:S(2)}) %collective-permute-start.8) | collective-permute-done | bytes 278560 | tf_op jit(solution)/shard_map/ppermute | solution.py:50
  32.2 0.5 collective-permute-start.11
  32.8 1.6 %collective-permute-start.14 = (bf16[64,2048]{1,0:T(8,128)(2,1)S(1)}, bf16[64,2048]{1,0:T(8,128)(2,1)S(1)}, u32[]{:S(2)}, u32[]{:S(2)}) collective-permute-start(bf16[64,2048]{1,0:T(8,128)(2,1)S(1)} %shard_map.59.refs_0_), channel_id=1, source_target_pairs={{0,2},{1,3},{2,0},{3,1},{4,6},{5,7},{6,4},{7,5},{8,10},{9,11},{10,... | collective-permute-start | bytes 786440 | tf_op jit(solution)/shard_map/ppermute | solution.py:50
  34.3 2.6 %shard_map.61 = (f32[64,2048]{1,0:T(8,128)S(1)}, f32[64,2048]{1,0:T(8,128)S(1)}, bf16[64,2048]{1,0:T(8,128)(2,1)S(1)}, bf16[32,2048]{1,0:T(8,128)(2,1)S(1)}, bf1...) custom-call(bf16[64,2048]{1,0:T(8,128)(2,1)S(1)} %shard_map.59.refs_0_, ...), custom_call_target="tpu_custom_call" | custom-call | tf_op jit(solution)/shard_map/pallas_call | solution.py:28
  37.7 3.7 %collective-permute-done.14.refs_2_ = bf16[64,2048]{1,0:T(8,128)(2,1)S(1)} collective-permute-done((bf16[64,2048]{1,0:T(8,128)(2,1)S(1)}, bf16[64,2048]{1,0:T(8,128)(2,1)S(1)}, u32[]{:S(2)}, u32[]{:S(2)}) %collective-permute-start.14) | collective-permute-done | bytes 262176 | tf_op jit(solution)/shard_map/ppermute | solution.py:50
  41.6 1.6 %collective-permute-start.17 = (bf16[64,2048]{1,0:T(8,128)(2,1)S(1)}, bf16[64,2048]{1,0:T(8,128)(2,1)S(1)}, u32[]{:S(2)}, u32[]{:S(2)}) collective-permute-start(bf16[64,2048]{1,0:T(8,128)(2,1)S(1)} %shard_map.64), channel_id=1, source_target_pairs={{0,2},{1,3},{2,0},{3,1},{4,6},{5,7},{6,4},{7,5},{8,10},{9,11},{10,... | collective-permute-start | bytes 786440 | tf_op jit(solution)/shard_map/ppermute | solution.py:50
  43.2 4.4 %collective-permute-start.20 = (bf16[32,2048]{1,0:T(8,128)(2,1)S(1)}, bf16[32,2048]{1,0:T(8,128)(2,1)S(1)}, u32[]{:S(2)}, u32[]{:S(2)}) collective-permute-start(bf16[32,2048]{1,0:T(8,128)(2,1)S(1)} %get-tuple-element.69.refs_0_), channel_id=1, source_target_pairs={{0,12},{1,13},{2,14},{3,15},{4,8},{5,9},{6,10},{7,11},{8,4},{9,5},... | collective-permute-start | bytes 393224 | tf_op jit(solution)/shard_map/ppermute | solution.py:50
  47.7 1.8 %collective-permute-start.19 = (bf16[32,2048]{1,0:T(8,128)(2,1)S(1)}, bf16[32,2048]{1,0:T(8,128)(2,1)S(1)}, u32[]{:S(2)}, u32[]{:S(2)}) collective-permute-start(bf16[32,2048]{1,0:T(8,128)(2,1)S(1)} %get-tuple-element.75), channel_id=1, source_target_pairs={{0,8},{1,9},{2,10},{3,11},{4,12},{5,13},{6,14},{7,15},{8,0},{9,1},... | collective-permute-start | bytes 393224 | tf_op jit(solution)/shard_map/ppermute | solution.py:50
  49.6 4.5 %collective-permute-start.18 = (bf16[32,2048]{1,0:T(8,128)(2,1)S(1)}, bf16[32,2048]{1,0:T(8,128)(2,1)S(1)}, u32[]{:S(2)}, u32[]{:S(2)}) collective-permute-start(bf16[32,2048]{1,0:T(8,128)(2,1)S(1)} %get-tuple-element.74), channel_id=1, source_target_pairs={{0,4},{1,5},{2,6},{3,7},{4,0},{5,1},{6,2},{7,3},{8,12},{9,13},{10,... | collective-permute-start | bytes 393224 | tf_op jit(solution)/shard_map/ppermute | solution.py:50
  54.1 3.7 %shard_map.62 = (bf16[2048,1536]{1,0:T(8,128)(2,1)S(1)}, bf16[768,2048]{1,0:T(8,128)(2,1)S(1)}, f32[8,128]{1,0:T(8,128)S(1)}) custom-call(f32[64,2048]{1,0:T(8,128)S(1)} %get-tuple-element.64.refs_0_, bf16[2,1,2048,1536]{3,2,1,0:T(8,128)(2,1)} %refs_1_.3, bf16[2,1,768,2048]{3,2,1,0:T(8,128)(2,1)} %refs_2_.4), custom_call_target="tpu_custom_call" | custom-call | tf_op jit(solution)/shard_map/pallas_call | solution.py:28
  57.8 1.4 %collective-permute-done.19.refs_5_ = bf16[32,2048]{1,0:T(8,128)(2,1)S(1)} collective-permute-done((bf16[32,2048]{1,0:T(8,128)(2,1)S(1)}, bf16[32,2048]{1,0:T(8,128)(2,1)S(1)}, u32[]{:S(2)}, u32[]{:S(2)}) %collective-permute-start.19) | collective-permute-done | bytes 131104 | tf_op jit(solution)/shard_map/ppermute | solution.py:50
  59.2 0.6 collective-permute-done.18.refs_4_
  60.1 1.6 %collective-permute-start.21 = (bf16[32,2048]{1,0:T(8,128)(2,1)S(1)}, bf16[32,2048]{1,0:T(8,128)(2,1)S(1)}, u32[]{:S(2)}, u32[]{:S(2)}) collective-permute-start(bf16[32,2048]{1,0:T(8,128)(2,1)S(1)} %get-tuple-element.77.refs_3_), channel_id=1, source_target_pairs={{0,8},{1,9},{2,10},{3,11},{4,12},{5,13},{6,14},{7,15},{8,0},{9,1},... | collective-permute-start | bytes 393224 | tf_op jit(solution)/shard_map/ppermute | solution.py:50
  61.6 2.0 %collective-permute-start.22 = (bf16[32,2048]{1,0:T(8,128)(2,1)S(1)}, bf16[32,2048]{1,0:T(8,128)(2,1)S(1)}, u32[]{:S(2)}, u32[]{:S(2)}) collective-permute-start(bf16[32,2048]{1,0:T(8,128)(2,1)S(1)} %get-tuple-element.77.refs_3_), channel_id=1, source_target_pairs={{0,12},{1,13},{2,14},{3,15},{4,8},{5,9},{6,10},{7,11},{8,4},{9,5},... | collective-permute-start | bytes 393224 | tf_op jit(solution)/shard_map/ppermute | solution.py:50
  63.6 0.5 collective-permute-start.23
  64.1 8.3 %collective-permute-done.21.refs_1_ = bf16[32,2048]{1,0:T(8,128)(2,1)S(1)} collective-permute-done((bf16[32,2048]{1,0:T(8,128)(2,1)S(1)}, bf16[32,2048]{1,0:T(8,128)(2,1)S(1)}, u32[]{:S(2)}, u32[]{:S(2)}) %collective-permute-start.21) | collective-permute-done | bytes 131104 | tf_op jit(solution)/shard_map/ppermute | solution.py:50
  72.7 0.5 collective-permute-start.24
  73.2 6.0 %collective-permute-done.24.refs_1_ = bf16[64,2048]{1,0:T(8,128)(2,1)S(1)} collective-permute-done((bf16[64,2048]{1,0:T(8,128)(2,1)S(1)}, bf16[64,2048]{1,0:T(8,128)(2,1)S(1)}, u32[]{:S(2)}, u32[]{:S(2)}) %collective-permute-start.24) | collective-permute-done | bytes 262176 | tf_op jit(solution)/shard_map/ppermute | solution.py:50
  79.2 0.4 collective-permute-start.29
  79.6 1.2 %collective-permute-done.26.refs_3_ = bf16[64,2048]{1,0:T(8,128)(2,1)S(1)} collective-permute-done((bf16[64,2048]{1,0:T(8,128)(2,1)S(1)}, bf16[64,2048]{1,0:T(8,128)(2,1)S(1)}, u32[]{:S(2)}, u32[]{:S(2)}) %collective-permute-start.26) | collective-permute-done | bytes 262176 | tf_op jit(solution)/shard_map/ppermute | solution.py:50
  80.8 2.6 %shard_map.68 = (f32[64,2048]{1,0:T(8,128)S(1)}, f32[64,2048]{1,0:T(8,128)S(1)}, bf16[64,2048]{1,0:T(8,128)(2,1)S(1)}, bf16[32,2048]{1,0:T(8,128)(2,1)S(1)}, bf16[32,2048]{1,0:T(8,128)(2,1)S(1)}) custom-call(bf16[64,2048]{1,0:T(8,128)(2,1)S(1)} %get-tuple-element.78.refs_0_, bf16[64,2048]{1,0:T(8,128)(2,1)S(1)} %collective-permute-done.24.refs_1_, ...), custom_call_target="tpu_custom_call" | custom-call | tf_op jit(solution)/shard_map/pallas_call | solution.py:28
  83.6 0.4 collective-permute-start.28
  84.1 0.7 collective-permute-done.27.refs_1_
  85.0 2.9 %collective-permute-done.29.refs_1_ = bf16[64,2048]{1,0:T(8,128)(2,1)S(1)} collective-permute-done((bf16[64,2048]{1,0:T(8,128)(2,1)S(1)}, bf16[64,2048]{1,0:T(8,128)(2,1)S(1)}, u32[]{:S(2)}, u32[]{:S(2)}) %collective-permute-start.29) | collective-permute-done | bytes 262176 | tf_op jit(solution)/shard_map/ppermute | solution.py:50
  88.0 0.5 collective-permute-start.32
  89.0 0.4 collective-permute-done.31.refs_5_
  89.6 2.6 %shard_map.71 = (f32[64,2048]{1,0:T(8,128)S(1)}, f32[64,2048]{1,0:T(8,128)S(1)}, bf16[64,2048]{1,0:T(8,128)(2,1)S(1)}, bf16[32,2048]{1,0:T(8,128)(2,1)S(1)}, bf16[32,2048]{1,0:T(8,128)(2,1)S(1)}) custom-call(bf16[64,2048]{1,0:T(8,128)(2,1)S(1)} %shard_map.69.refs_0_, bf16[64,2048]{1,0:T(8,128)(2,1)S(1)} %get-tuple-element.86.refs_1_, ...), custom_call_target="tpu_custom_call" | custom-call | tf_op jit(solution)/shard_map/pallas_call | solution.py:28
  92.2 0.4 collective-permute-start.36
  93.1 4.2 %collective-permute-done.35.refs_2_ = bf16[64,2048]{1,0:T(8,128)(2,1)S(1)} collective-permute-done((bf16[64,2048]{1,0:T(8,128)(2,1)S(1)}, bf16[64,2048]{1,0:T(8,128)(2,1)S(1)}, u32[]{:S(2)}, u32[]{:S(2)}) %collective-permute-start.35) | collective-permute-done | bytes 262176 | tf_op jit(solution)/shard_map/ppermute | solution.py:50
  97.4 0.4 collective-permute-start.38
  97.9 2.3 %collective-permute-start.41 = (bf16[32,2048]{1,0:T(8,128)(2,1)S(1)}, bf16[32,2048]{1,0:T(8,128)(2,1)S(1)}, u32[]{:S(2)}, u32[]{:S(2)}) collective-permute-start(bf16[32,2048]{1,0:T(8,128)(2,1)S(1)} %get-tuple-element.94.refs_0_), channel_id=1, source_target_pairs={{0,12},{1,13},{2,14},{3,15},{4,8},{5,9},{6,10},{7,11},{8,4},{9,5},... | collective-permute-start | bytes 393224 | tf_op jit(solution)/shard_map/ppermute | solution.py:50
  100.1 2.0 %collective-permute-start.40 = (bf16[32,2048]{1,0:T(8,128)(2,1)S(1)}, bf16[32,2048]{1,0:T(8,128)(2,1)S(1)}, u32[]{:S(2)}, u32[]{:S(2)}) collective-permute-start(bf16[32,2048]{1,0:T(8,128)(2,1)S(1)} %get-tuple-element.100), channel_id=1, source_target_pairs={{0,8},{1,9},{2,10},{3,11},{4,12},{5,13},{6,14},{7,15},{8,0},{9,1},... | collective-permute-start | bytes 393224 | tf_op jit(solution)/shard_map/ppermute | solution.py:50
  102.1 3.3 %collective-permute-done.38.refs_2_ = bf16[64,2048]{1,0:T(8,128)(2,1)S(1)} collective-permute-done((bf16[64,2048]{1,0:T(8,128)(2,1)S(1)}, bf16[64,2048]{1,0:T(8,128)(2,1)S(1)}, u32[]{:S(2)}, u32[]{:S(2)}) %collective-permute-start.38) | collective-permute-done | bytes 262176 | tf_op jit(solution)/shard_map/ppermute | solution.py:50
  105.5 2.7 %collective-permute-start.39 = (bf16[32,2048]{1,0:T(8,128)(2,1)S(1)}, bf16[32,2048]{1,0:T(8,128)(2,1)S(1)}, u32[]{:S(2)}, u32[]{:S(2)}) collective-permute-start(bf16[32,2048]{1,0:T(8,128)(2,1)S(1)} %get-tuple-element.99), channel_id=1, source_target_pairs={{0,4},{1,5},{2,6},{3,7},{4,0},{5,1},{6,2},{7,3},{8,12},{9,13},{10,... | collective-permute-start | bytes 393224 | tf_op jit(solution)/shard_map/ppermute | solution.py:50
  108.2 4.8 %collective-permute-done.40.refs_3_ = bf16[32,2048]{1,0:T(8,128)(2,1)S(1)} collective-permute-done((bf16[32,2048]{1,0:T(8,128)(2,1)S(1)}, bf16[32,2048]{1,0:T(8,128)(2,1)S(1)}, u32[]{:S(2)}, u32[]{:S(2)}) %collective-permute-start.40) | collective-permute-done | bytes 131104 | tf_op jit(solution)/shard_map/ppermute | solution.py:50
  113.0 1.0 collective-permute-done.39.refs_2_
  113.9 0.8 shard_map.75
  (61 shorter events, 5.1 us)
Async XLA Ops:
  1.2 14.6 %collective-permute-start = (bf16[32,2176]{1,0:T(8,128)(2,1)S(1)}, bf16[32,2176]{1,0:T(8,128)(2,1)S(1)}, u32[]{:S(2)}, u32[]{:S(2)}) collective-permute-start(bf16[32,2176]{1,0:T(8,128)(2,1)S(1)} %shard_map.56.refs_3_), channel_id=1, source_target_pairs={{0,8},{1,9},{2,10},{3,11},{4,12},{5,13},{6,14},{7,15},{8,0},{9,1},... | collective-permute-start | bytes 417800 | tf_op jit(solution)/shard_map/ppermute | solution.py:50
  5.3 10.5 %collective-permute-start.1 = (bf16[32,2176]{1,0:T(8,128)(2,1)S(1)}, bf16[32,2176]{1,0:T(8,128)(2,1)S(1)}, u32[]{:S(2)}, u32[]{:S(2)}) collective-permute-start(bf16[32,2176]{1,0:T(8,128)(2,1)S(1)} %shard_map.56.refs_3_), channel_id=1, source_target_pairs={{0,12},{1,13},{2,14},{3,15},{4,8},{5,9},{6,10},{7,11},{8,4},{9,5},... | collective-permute-start | bytes 417800 | tf_op jit(solution)/shard_map/ppermute | solution.py:50
  6.7 9.7 %collective-permute-start.2 = (bf16[32,2176]{1,0:T(8,128)(2,1)S(1)}, bf16[32,2176]{1,0:T(8,128)(2,1)S(1)}, u32[]{:S(2)}, u32[]{:S(2)}) collective-permute-start(bf16[32,2176]{1,0:T(8,128)(2,1)S(1)} %shard_map.56.refs_3_), channel_id=1, source_target_pairs={{0,4},{1,5},{2,6},{3,7},{4,0},{5,1},{6,2},{7,3},{8,12},{9,13},{10,... | collective-permute-start | bytes 417800 | tf_op jit(solution)/shard_map/ppermute | solution.py:50
  16.4 6.6 %collective-permute-start.3 = (bf16[64,2176]{1,0:T(8,128)(2,1)S(1)}, bf16[64,2176]{1,0:T(8,128)(2,1)S(1)}, u32[]{:S(2)}, u32[]{:S(2)}) collective-permute-start(bf16[64,2176]{1,0:T(8,128)(2,1)S(1)} %get-tuple-element.54.refs_0_), channel_id=1, source_target_pairs={{0,2},{1,3},{2,0},{3,1},{4,6},{5,7},{6,4},{7,5},{8,10},{9,11},{10,... | collective-permute-start | bytes 835592 | tf_op jit(solution)/shard_map/ppermute | solution.py:50
  18.0 6.8 %collective-permute-start.4 = (bf16[64,2176]{1,0:T(8,128)(2,1)S(1)}, bf16[64,2176]{1,0:T(8,128)(2,1)S(1)}, u32[]{:S(2)}, u32[]{:S(2)}) collective-permute-start(bf16[64,2176]{1,0:T(8,128)(2,1)S(1)} %get-tuple-element.54.refs_0_), channel_id=1, source_target_pairs={{0,1},{1,0},{2,3},{3,2},{4,5},{5,4},{6,7},{7,6},{8,9},{9,8},{10,11... | collective-permute-start | bytes 835592 | tf_op jit(solution)/shard_map/ppermute | solution.py:50
  23.0 1.8 %collective-permute-start.5 = (bf16[64,2176]{1,0:T(8,128)(2,1)S(1)}, bf16[64,2176]{1,0:T(8,128)(2,1)S(1)}, u32[]{:S(2)}, u32[]{:S(2)}) collective-permute-start(bf16[64,2176]{1,0:T(8,128)(2,1)S(1)} %collective-permute-done.3.refs_1_), channel_id=1, source_target_pairs={{0,1},{1,0},{2,3},{3,2},{4,5},{5,4},{6,7},{7,6},{8,9},{9,8},{10,11... | collective-permute-start | bytes 835592 | tf_op jit(solution)/shard_map/ppermute | solution.py:50
  23.0 9.1 %collective-permute-start.8 = (bf16[64,2176]{1,0:T(8,128)(2,1)S(1)}, bf16[64,2176]{1,0:T(8,128)(2,1)S(1)}, u32[]{:S(2)}, u32[]{:S(2)}) collective-permute-start(bf16[64,2176]{1,0:T(8,128)(2,1)S(1)} %get-tuple-element.61.refs_1_), channel_id=1, source_target_pairs={{0,2},{1,3},{2,0},{3,1},{4,6},{5,7},{6,4},{7,5},{8,10},{9,11},{10,... | collective-permute-start | bytes 835592 | tf_op jit(solution)/shard_map/ppermute | solution.py:50
  24.6 9.8 %collective-permute-start.9 = (bf16[64,2176]{1,0:T(8,128)(2,1)S(1)}, bf16[64,2176]{1,0:T(8,128)(2,1)S(1)}, u32[]{:S(2)}, u32[]{:S(2)}) collective-permute-start(bf16[64,2176]{1,0:T(8,128)(2,1)S(1)} %get-tuple-element.61.refs_1_), channel_id=1, source_target_pairs={{0,1},{1,0},{2,3},{3,2},{4,5},{5,4},{6,7},{7,6},{8,9},{9,8},{10,11... | collective-permute-start | bytes 835592 | tf_op jit(solution)/shard_map/ppermute | solution.py:50
  27.4 1.4 %collective-permute-start.6 = (bf16[32,2048]{1,0:T(8,128)(2,1)S(1)}, bf16[32,2048]{1,0:T(8,128)(2,1)S(1)}, u32[]{:S(2)}, u32[]{:S(2)}) collective-permute-start(bf16[32,2048]{1,0:T(8,128)(2,1)S(1)} %get-tuple-element.58), channel_id=1, source_target_pairs={{0,1},{1,0},{2,3},{3,2},{4,5},{5,4},{6,7},{7,6},{8,9},{9,8},{10,11... | collective-permute-start | bytes 393224 | tf_op jit(solution)/shard_map/ppermute | solution.py:50
  27.8 1.3 %collective-permute-start.7 = (bf16[32,2048]{1,0:T(8,128)(2,1)S(1)}, bf16[32,2048]{1,0:T(8,128)(2,1)S(1)}, u32[]{:S(2)}, u32[]{:S(2)}) collective-permute-start(bf16[32,2048]{1,0:T(8,128)(2,1)S(1)} %get-tuple-element.59), channel_id=1, source_target_pairs={{0,1},{1,0},{2,3},{3,2},{4,5},{5,4},{6,7},{7,6},{8,9},{9,8},{10,11... | collective-permute-start | bytes 393224 | tf_op jit(solution)/shard_map/ppermute | solution.py:50
  32.1 2.2 %collective-permute-start.10 = (bf16[32,2176]{1,0:T(8,128)(2,1)S(1)}, bf16[32,2176]{1,0:T(8,128)(2,1)S(1)}, u32[]{:S(2)}, u32[]{:S(2)}) collective-permute-start(bf16[32,2176]{1,0:T(8,128)(2,1)S(1)} %get-tuple-element.62.refs_2_), channel_id=1, source_target_pairs={{0,1},{1,0},{2,3},{3,2},{4,5},{5,4},{6,7},{7,6},{8,9},{9,8},{10,11... | collective-permute-start | bytes 417800 | tf_op jit(solution)/shard_map/ppermute | solution.py:50
  32.2 2.2 %collective-permute-start.11 = (bf16[32,2176]{1,0:T(8,128)(2,1)S(1)}, bf16[32,2176]{1,0:T(8,128)(2,1)S(1)}, u32[]{:S(2)}, u32[]{:S(2)}) collective-permute-start(bf16[32,2176]{1,0:T(8,128)(2,1)S(1)} %get-tuple-element.63.refs_3_), channel_id=1, source_target_pairs={{0,1},{1,0},{2,3},{3,2},{4,5},{5,4},{6,7},{7,6},{8,9},{9,8},{10,11... | collective-permute-start | bytes 417800 | tf_op jit(solution)/shard_map/ppermute | solution.py:50
  32.7 5.0 %collective-permute-start.13 = (bf16[64,2048]{1,0:T(8,128)(2,1)S(1)}, bf16[64,2048]{1,0:T(8,128)(2,1)S(1)}, u32[]{:S(2)}, u32[]{:S(2)}) collective-permute-start(bf16[64,2048]{1,0:T(8,128)(2,1)S(1)} %get-tuple-element.68), channel_id=1, source_target_pairs={{0,1},{1,0},{2,3},{3,2},{4,5},{5,4},{6,7},{7,6},{8,9},{9,8},{10,11... | collective-permute-start | bytes 786440 | tf_op jit(solution)/shard_map/ppermute | solution.py:50
  32.8 8.7 %collective-permute-start.14 = (bf16[64,2048]{1,0:T(8,128)(2,1)S(1)}, bf16[64,2048]{1,0:T(8,128)(2,1)S(1)}, u32[]{:S(2)}, u32[]{:S(2)}) collective-permute-start(bf16[64,2048]{1,0:T(8,128)(2,1)S(1)} %shard_map.59.refs_0_), channel_id=1, source_target_pairs={{0,2},{1,3},{2,0},{3,1},{4,6},{5,7},{6,4},{7,5},{8,10},{9,11},{10,... | collective-permute-start | bytes 786440 | tf_op jit(solution)/shard_map/ppermute | solution.py:50
  37.0 4.5 %collective-permute-start.15 = (bf16[32,2048]{1,0:T(8,128)(2,1)S(1)}, bf16[32,2048]{1,0:T(8,128)(2,1)S(1)}, u32[]{:S(2)}, u32[]{:S(2)}) collective-permute-start(bf16[32,2048]{1,0:T(8,128)(2,1)S(1)} %get-tuple-element.71), channel_id=1, source_target_pairs={{0,1},{1,0},{2,3},{3,2},{4,5},{5,4},{6,7},{7,6},{8,9},{9,8},{10,11... | collective-permute-start | bytes 393224 | tf_op jit(solution)/shard_map/ppermute | solution.py:50
  37.2 4.3 %collective-permute-start.16 = (bf16[32,2048]{1,0:T(8,128)(2,1)S(1)}, bf16[32,2048]{1,0:T(8,128)(2,1)S(1)}, u32[]{:S(2)}, u32[]{:S(2)}) collective-permute-start(bf16[32,2048]{1,0:T(8,128)(2,1)S(1)} %get-tuple-element.72), channel_id=1, source_target_pairs={{0,1},{1,0},{2,3},{3,2},{4,5},{5,4},{6,7},{7,6},{8,9},{9,8},{10,11... | collective-permute-start | bytes 393224 | tf_op jit(solution)/shard_map/ppermute | solution.py:50
  37.5 11.9 %collective-permute-start.12 = (bf16[64,2048]{1,0:T(8,128)(2,1)S(1)}, bf16[64,2048]{1,0:T(8,128)(2,1)S(1)}, u32[]{:S(2)}, u32[]{:S(2)}) collective-permute-start(bf16[64,2048]{1,0:T(8,128)(2,1)S(1)} %get-tuple-element.66), channel_id=1, source_target_pairs={{0,1},{1,0},{2,3},{3,2},{4,5},{5,4},{6,7},{7,6},{8,9},{9,8},{10,11... | collective-permute-start | bytes 786440 | tf_op jit(solution)/shard_map/ppermute | solution.py:50
  41.6 7.9 %collective-permute-start.17 = (bf16[64,2048]{1,0:T(8,128)(2,1)S(1)}, bf16[64,2048]{1,0:T(8,128)(2,1)S(1)}, u32[]{:S(2)}, u32[]{:S(2)}) collective-permute-start(bf16[64,2048]{1,0:T(8,128)(2,1)S(1)} %shard_map.64), channel_id=1, source_target_pairs={{0,2},{1,3},{2,0},{3,1},{4,6},{5,7},{6,4},{7,5},{8,10},{9,11},{10,... | collective-permute-start | bytes 786440 | tf_op jit(solution)/shard_map/ppermute | solution.py:50
  43.2 16.0 %collective-permute-start.20 = (bf16[32,2048]{1,0:T(8,128)(2,1)S(1)}, bf16[32,2048]{1,0:T(8,128)(2,1)S(1)}, u32[]{:S(2)}, u32[]{:S(2)}) collective-permute-start(bf16[32,2048]{1,0:T(8,128)(2,1)S(1)} %get-tuple-element.69.refs_0_), channel_id=1, source_target_pairs={{0,12},{1,13},{2,14},{3,15},{4,8},{5,9},{6,10},{7,11},{8,4},{9,5},... | collective-permute-start | bytes 393224 | tf_op jit(solution)/shard_map/ppermute | solution.py:50
  47.7 11.6 %collective-permute-start.19 = (bf16[32,2048]{1,0:T(8,128)(2,1)S(1)}, bf16[32,2048]{1,0:T(8,128)(2,1)S(1)}, u32[]{:S(2)}, u32[]{:S(2)}) collective-permute-start(bf16[32,2048]{1,0:T(8,128)(2,1)S(1)} %get-tuple-element.75), channel_id=1, source_target_pairs={{0,8},{1,9},{2,10},{3,11},{4,12},{5,13},{6,14},{7,15},{8,0},{9,1},... | collective-permute-start | bytes 393224 | tf_op jit(solution)/shard_map/ppermute | solution.py:50
  49.6 10.2 %copy-start = (bf16[2,16,2048]{2,1,0:T(8,128)(2,1)S(1)}, bf16[2,16,2048]{2,1,0:T(8,128)(2,1)}, u32[]{:S(2)}) copy-start(bf16[2,16,2048]{2,1,0:T(8,128)(2,1)} %param.5) | copy-start | bytes 393220
  49.6 10.2 %copy-start.1 = (f32[2,2048]{1,0:T(2,128)S(1)}, f32[2,2048]{1,0:T(2,128)}, u32[]{:S(2)}) copy-start(f32[2,2048]{1,0:T(2,128)} %refs_2_.5) | copy-start | bytes 49156
  49.6 10.2 %collective-permute-start.18 = (bf16[32,2048]{1,0:T(8,128)(2,1)S(1)}, bf16[32,2048]{1,0:T(8,128)(2,1)S(1)}, u32[]{:S(2)}, u32[]{:S(2)}) collective-permute-start(bf16[32,2048]{1,0:T(8,128)(2,1)S(1)} %get-tuple-element.74), channel_id=1, source_target_pairs={{0,4},{1,5},{2,6},{3,7},{4,0},{5,1},{6,2},{7,3},{8,12},{9,13},{10,... | collective-permute-start | bytes 393224 | tf_op jit(solution)/shard_map/ppermute | solution.py:50
  60.1 12.3 %collective-permute-start.21 = (bf16[32,2048]{1,0:T(8,128)(2,1)S(1)}, bf16[32,2048]{1,0:T(8,128)(2,1)S(1)}, u32[]{:S(2)}, u32[]{:S(2)}) collective-permute-start(bf16[32,2048]{1,0:T(8,128)(2,1)S(1)} %get-tuple-element.77.refs_3_), channel_id=1, source_target_pairs={{0,8},{1,9},{2,10},{3,11},{4,12},{5,13},{6,14},{7,15},{8,0},{9,1},... | collective-permute-start | bytes 393224 | tf_op jit(solution)/shard_map/ppermute | solution.py:50
  61.6 10.8 %collective-permute-start.22 = (bf16[32,2048]{1,0:T(8,128)(2,1)S(1)}, bf16[32,2048]{1,0:T(8,128)(2,1)S(1)}, u32[]{:S(2)}, u32[]{:S(2)}) collective-permute-start(bf16[32,2048]{1,0:T(8,128)(2,1)S(1)} %get-tuple-element.77.refs_3_), channel_id=1, source_target_pairs={{0,12},{1,13},{2,14},{3,15},{4,8},{5,9},{6,10},{7,11},{8,4},{9,5},... | collective-permute-start | bytes 393224 | tf_op jit(solution)/shard_map/ppermute | solution.py:50
  63.6 9.0 %collective-permute-start.23 = (bf16[32,2048]{1,0:T(8,128)(2,1)S(1)}, bf16[32,2048]{1,0:T(8,128)(2,1)S(1)}, u32[]{:S(2)}, u32[]{:S(2)}) collective-permute-start(bf16[32,2048]{1,0:T(8,128)(2,1)S(1)} %get-tuple-element.77.refs_3_), channel_id=1, source_target_pairs={{0,4},{1,5},{2,6},{3,7},{4,0},{5,1},{6,2},{7,3},{8,12},{9,13},{10,... | collective-permute-start | bytes 393224 | tf_op jit(solution)/shard_map/ppermute | solution.py:50
  72.7 6.6 %collective-permute-start.24 = (bf16[64,2048]{1,0:T(8,128)(2,1)S(1)}, bf16[64,2048]{1,0:T(8,128)(2,1)S(1)}, u32[]{:S(2)}, u32[]{:S(2)}) collective-permute-start(bf16[64,2048]{1,0:T(8,128)(2,1)S(1)} %get-tuple-element.78.refs_0_), channel_id=1, source_target_pairs={{0,2},{1,3},{2,0},{3,1},{4,6},{5,7},{6,4},{7,5},{8,10},{9,11},{10,... | collective-permute-start | bytes 786440 | tf_op jit(solution)/shard_map/ppermute | solution.py:50
  73.2 6.4 %collective-permute-start.25 = (bf16[64,2048]{1,0:T(8,128)(2,1)S(1)}, bf16[64,2048]{1,0:T(8,128)(2,1)S(1)}, u32[]{:S(2)}, u32[]{:S(2)}) collective-permute-start(bf16[64,2048]{1,0:T(8,128)(2,1)S(1)} %get-tuple-element.78.refs_0_), channel_id=1, source_target_pairs={{0,1},{1,0},{2,3},{3,2},{4,5},{5,4},{6,7},{7,6},{8,9},{9,8},{10,11... | collective-permute-start | bytes 786440 | tf_op jit(solution)/shard_map/ppermute | solution.py:50
  79.2 1.5 %collective-permute-start.26 = (bf16[64,2048]{1,0:T(8,128)(2,1)S(1)}, bf16[64,2048]{1,0:T(8,128)(2,1)S(1)}, u32[]{:S(2)}, u32[]{:S(2)}) collective-permute-start(bf16[64,2048]{1,0:T(8,128)(2,1)S(1)} %collective-permute-done.24.refs_1_), channel_id=1, source_target_pairs={{0,1},{1,0},{2,3},{3,2},{4,5},{5,4},{6,7},{7,6},{8,9},{9,8},{10,11... | collective-permute-start | bytes 786440 | tf_op jit(solution)/shard_map/ppermute | solution.py:50
  79.2 8.7 %collective-permute-start.29 = (bf16[64,2048]{1,0:T(8,128)(2,1)S(1)}, bf16[64,2048]{1,0:T(8,128)(2,1)S(1)}, u32[]{:S(2)}, u32[]{:S(2)}) collective-permute-start(bf16[64,2048]{1,0:T(8,128)(2,1)S(1)} %get-tuple-element.86.refs_1_), channel_id=1, source_target_pairs={{0,2},{1,3},{2,0},{3,1},{4,6},{5,7},{6,4},{7,5},{8,10},{9,11},{10,... | collective-permute-start | bytes 786440 | tf_op jit(solution)/shard_map/ppermute | solution.py:50
  83.4 1.4 %collective-permute-start.27 = (bf16[32,2048]{1,0:T(8,128)(2,1)S(1)}, bf16[32,2048]{1,0:T(8,128)(2,1)S(1)}, u32[]{:S(2)}, u32[]{:S(2)}) collective-permute-start(bf16[32,2048]{1,0:T(8,128)(2,1)S(1)} %get-tuple-element.83), channel_id=1, source_target_pairs={{0,1},{1,0},{2,3},{3,2},{4,5},{5,4},{6,7},{7,6},{8,9},{9,8},{10,11... | collective-permute-start | bytes 393224 | tf_op jit(solution)/shard_map/ppermute | solution.py:50
  83.6 1.4 %collective-permute-start.28 = (bf16[32,2048]{1,0:T(8,128)(2,1)S(1)}, bf16[32,2048]{1,0:T(8,128)(2,1)S(1)}, u32[]{:S(2)}, u32[]{:S(2)}) collective-permute-start(bf16[32,2048]{1,0:T(8,128)(2,1)S(1)} %get-tuple-element.84), channel_id=1, source_target_pairs={{0,1},{1,0},{2,3},{3,2},{4,5},{5,4},{6,7},{7,6},{8,9},{9,8},{10,11... | collective-permute-start | bytes 393224 | tf_op jit(solution)/shard_map/ppermute | solution.py:50
  83.9 5.0 %collective-permute-start.30 = (bf16[64,2048]{1,0:T(8,128)(2,1)S(1)}, bf16[64,2048]{1,0:T(8,128)(2,1)S(1)}, u32[]{:S(2)}, u32[]{:S(2)}) collective-permute-start(bf16[64,2048]{1,0:T(8,128)(2,1)S(1)} %get-tuple-element.86.refs_1_), channel_id=1, source_target_pairs={{0,1},{1,0},{2,3},{3,2},{4,5},{5,4},{6,7},{7,6},{8,9},{9,8},{10,11... | collective-permute-start | bytes 786440 | tf_op jit(solution)/shard_map/ppermute | solution.py:50
  88.0 1.4 %collective-permute-start.31 = (bf16[32,2048]{1,0:T(8,128)(2,1)S(1)}, bf16[32,2048]{1,0:T(8,128)(2,1)S(1)}, u32[]{:S(2)}, u32[]{:S(2)}) collective-permute-start(bf16[32,2048]{1,0:T(8,128)(2,1)S(1)} %get-tuple-element.87.refs_2_), channel_id=1, source_target_pairs={{0,1},{1,0},{2,3},{3,2},{4,5},{5,4},{6,7},{7,6},{8,9},{9,8},{10,11... | collective-permute-start | bytes 393224 | tf_op jit(solution)/shard_map/ppermute | solution.py:50
  88.0 1.5 %collective-permute-start.32 = (bf16[32,2048]{1,0:T(8,128)(2,1)S(1)}, bf16[32,2048]{1,0:T(8,128)(2,1)S(1)}, u32[]{:S(2)}, u32[]{:S(2)}) collective-permute-start(bf16[32,2048]{1,0:T(8,128)(2,1)S(1)} %get-tuple-element.88.refs_3_), channel_id=1, source_target_pairs={{0,1},{1,0},{2,3},{3,2},{4,5},{5,4},{6,7},{7,6},{8,9},{9,8},{10,11... | collective-permute-start | bytes 393224 | tf_op jit(solution)/shard_map/ppermute | solution.py:50
  88.5 4.5 %collective-permute-start.34 = (bf16[64,2048]{1,0:T(8,128)(2,1)S(1)}, bf16[64,2048]{1,0:T(8,128)(2,1)S(1)}, u32[]{:S(2)}, u32[]{:S(2)}) collective-permute-start(bf16[64,2048]{1,0:T(8,128)(2,1)S(1)} %get-tuple-element.93), channel_id=1, source_target_pairs={{0,1},{1,0},{2,3},{3,2},{4,5},{5,4},{6,7},{7,6},{8,9},{9,8},{10,11... | collective-permute-start | bytes 786440 | tf_op jit(solution)/shard_map/ppermute | solution.py:50
  88.6 8.7 %collective-permute-start.35 = (bf16[64,2048]{1,0:T(8,128)(2,1)S(1)}, bf16[64,2048]{1,0:T(8,128)(2,1)S(1)}, u32[]{:S(2)}, u32[]{:S(2)}) collective-permute-start(bf16[64,2048]{1,0:T(8,128)(2,1)S(1)} %shard_map.69.refs_0_), channel_id=1, source_target_pairs={{0,2},{1,3},{2,0},{3,1},{4,6},{5,7},{6,4},{7,5},{8,10},{9,11},{10,... | collective-permute-start | bytes 786440 | tf_op jit(solution)/shard_map/ppermute | solution.py:50
  92.2 5.2 %collective-permute-start.36 = (bf16[32,2048]{1,0:T(8,128)(2,1)S(1)}, bf16[32,2048]{1,0:T(8,128)(2,1)S(1)}, u32[]{:S(2)}, u32[]{:S(2)}) collective-permute-start(bf16[32,2048]{1,0:T(8,128)(2,1)S(1)} %get-tuple-element.96), channel_id=1, source_target_pairs={{0,1},{1,0},{2,3},{3,2},{4,5},{5,4},{6,7},{7,6},{8,9},{9,8},{10,11... | collective-permute-start | bytes 393224 | tf_op jit(solution)/shard_map/ppermute | solution.py:50
  92.6 4.8 %collective-permute-start.37 = (bf16[32,2048]{1,0:T(8,128)(2,1)S(1)}, bf16[32,2048]{1,0:T(8,128)(2,1)S(1)}, u32[]{:S(2)}, u32[]{:S(2)}) collective-permute-start(bf16[32,2048]{1,0:T(8,128)(2,1)S(1)} %get-tuple-element.97), channel_id=1, source_target_pairs={{0,1},{1,0},{2,3},{3,2},{4,5},{5,4},{6,7},{7,6},{8,9},{9,8},{10,11... | collective-permute-start | bytes 393224 | tf_op jit(solution)/shard_map/ppermute | solution.py:50
  92.8 9.3 %collective-permute-start.33 = (bf16[64,2048]{1,0:T(8,128)(2,1)S(1)}, bf16[64,2048]{1,0:T(8,128)(2,1)S(1)}, u32[]{:S(2)}, u32[]{:S(2)}) collective-permute-start(bf16[64,2048]{1,0:T(8,128)(2,1)S(1)} %get-tuple-element.91), channel_id=1, source_target_pairs={{0,1},{1,0},{2,3},{3,2},{4,5},{5,4},{6,7},{7,6},{8,9},{9,8},{10,11... | collective-permute-start | bytes 786440 | tf_op jit(solution)/shard_map/ppermute | solution.py:50
  97.4 7.9 %collective-permute-start.38 = (bf16[64,2048]{1,0:T(8,128)(2,1)S(1)}, bf16[64,2048]{1,0:T(8,128)(2,1)S(1)}, u32[]{:S(2)}, u32[]{:S(2)}) collective-permute-start(bf16[64,2048]{1,0:T(8,128)(2,1)S(1)} %shard_map.73), channel_id=1, source_target_pairs={{0,2},{1,3},{2,0},{3,1},{4,6},{5,7},{6,4},{7,5},{8,10},{9,11},{10,... | collective-permute-start | bytes 786440 | tf_op jit(solution)/shard_map/ppermute | solution.py:50
  97.9 15.1 %collective-permute-start.41 = (bf16[32,2048]{1,0:T(8,128)(2,1)S(1)}, bf16[32,2048]{1,0:T(8,128)(2,1)S(1)}, u32[]{:S(2)}, u32[]{:S(2)}) collective-permute-start(bf16[32,2048]{1,0:T(8,128)(2,1)S(1)} %get-tuple-element.94.refs_0_), channel_id=1, source_target_pairs={{0,12},{1,13},{2,14},{3,15},{4,8},{5,9},{6,10},{7,11},{8,4},{9,5},... | collective-permute-start | bytes 393224 | tf_op jit(solution)/shard_map/ppermute | solution.py:50
  100.1 12.9 %collective-permute-start.40 = (bf16[32,2048]{1,0:T(8,128)(2,1)S(1)}, bf16[32,2048]{1,0:T(8,128)(2,1)S(1)}, u32[]{:S(2)}, u32[]{:S(2)}) collective-permute-start(bf16[32,2048]{1,0:T(8,128)(2,1)S(1)} %get-tuple-element.100), channel_id=1, source_target_pairs={{0,8},{1,9},{2,10},{3,11},{4,12},{5,13},{6,14},{7,15},{8,0},{9,1},... | collective-permute-start | bytes 393224 | tf_op jit(solution)/shard_map/ppermute | solution.py:50
  105.5 8.5 %collective-permute-start.39 = (bf16[32,2048]{1,0:T(8,128)(2,1)S(1)}, bf16[32,2048]{1,0:T(8,128)(2,1)S(1)}, u32[]{:S(2)}, u32[]{:S(2)}) collective-permute-start(bf16[32,2048]{1,0:T(8,128)(2,1)S(1)} %get-tuple-element.99), channel_id=1, source_target_pairs={{0,4},{1,5},{2,6},{3,7},{4,0},{5,1},{6,2},{7,3},{8,12},{9,13},{10,... | collective-permute-start | bytes 393224 | tf_op jit(solution)/shard_map/ppermute | solution.py:50

commit v9 on v7

--- a/solution.py
+++ b/solution.py
@@ -10,6 +10,7 @@
 eps = 1e-06
 LANES = 128
 MIB = 2**20
+CUTS = 2
 WAIT = 6 * 10**9
 VMEM = pl.BlockSpec(memory_space=pltpu.VMEM)
 ANY = pl.BlockSpec(memory_space=pl.ANY)
@@ -73,10 +74,12 @@
     return lax.optimization_barrier((value, until))[0]
 
 
-def sum_kernel(mine, upper, lower, total):
-    half = upper.shape[0]
-    total[:half] = (mine[:half] + upper[...].astype(f32)).astype(total.dtype)
-    total[half:] = (mine[half:] + lower[...].astype(f32)).astype(total.dtype)
+def sum_kernel(mine, *refs):
+    *parts, total = refs
+    rows = parts[0].shape[0]
+    for k, part in enumerate(parts):
+        span = slice(k * rows, (k + 1) * rows)
+        total[span] = (mine[span] + part[...].astype(f32)).astype(total.dtype)
 
 
 def split_kernel(mine, near, beside, *pieces):
@@ -93,7 +96,7 @@
     (leaving,) = call(
         sum_kernel,
         [(mine_beside.shape, bf16)],
-        [VMEM] * 3,
+        [VMEM] * (1 + CUTS),
         mine_beside,
         *arrived_beside,
         after=after,
@@ -212,17 +215,17 @@
     return size
 
 
-def expert_kernel(first_column, wide, *refs):
+def expert_kernel(count, first_column, wide, *refs):
+    parts, refs = refs[:count], refs[count:]
     if wide:
-        parts, refs = refs[:4], refs[4:]
         gate_up_ref, down_ref, *outs, routed_ref, rows_ref, hidden_ref = refs
     else:
-        parts, refs = refs[:4], refs[4:]
         routed_ref, gate_up_ref, down_ref, *outs, rows_ref, hidden_ref = refs
     hidden_size, features = down_ref.shape
-    quarter = parts[0].shape[0]
-    for k, part in enumerate(parts):
-        span = slice(k * quarter, (k + 1) * quarter)
+    first = 0
+    for part in parts:
+        span = slice(first, first + part.shape[0])
+        first += part.shape[0]
         rows_ref[span] = part[:, :features]
         if wide:
             routed_ref[span] = part[:, features:]
@@ -251,17 +254,18 @@
 def run_expert(parts, routed, first_column, weights, after):
     gate_up, down_proj, _ = weights
     hidden_size, features = down_proj.shape
-    quarter, width = parts[0].shape
-    count = 4 * quarter
+    width = parts[0].shape[1]
+    count = sum(part.shape[0] for part in parts)
+    quarter = count // 4
     wide = routed is None
     outs = [((quarter, features), f32)] * 2 + [((quarter, features), bf16)]
-    outs += [((quarter // 2, features), bf16)] * 2
+    outs += [((quarter // CUTS, features), bf16)] * CUTS
     if wide:
         outs = outs + [((count, width - features), bf16)]
     found = call(
-        functools.partial(expert_kernel, first_column, wide),
+        functools.partial(expert_kernel, len(parts), first_column, wide),
         outs,
-        [VMEM] * (6 if wide else 7),
+        [VMEM] * (len(parts) + (2 if wide else 3)),
         *parts,
         *([] if wide else [routed]),
         gate_up,
@@ -270,7 +274,7 @@
         limit=24,
         after=after,
     )
-    return found[:5], found[5] if wide else routed
+    return found[: 3 + CUTS], found[3 + CUTS] if wide else routed
 
 
 def in_hbm(array):
@@ -304,26 +308,29 @@
     far, tokens = lax.axis_size("expert") // 4, rows.shape[0]
     routed = routed or [None, None]
     half = far // 2
-    sent = [rows] + [swap(rows, 4, k, far) for k in range(1, far)]
-    first = join_rows(sent[:half], loaded, 0)
+    sent = [rows] + [swap(rows, 4, k, far) for k in range(1, half)]
+    first = join_rows(sent, loaded, 0)
     first_beside = swap(first, 2, 1, 2)
-    second = join_rows(sent[half:], (first,), WAIT)
-    second_beside = swap(second, 2, 1, 2)
-
-    def worked(near, beside, routed, until):
-        beside = held(beside, until)
-        parts = [near, beside, swap(near, 1, 1, 2), swap(beside, 1, 1, 2)]
-        return run_expert(parts, routed, first_column, weights, (until,))
-
-    outs, first_columns = worked(first, first_beside, routed[0], second)
+    crossed = join_rows([swap(rows, 4, half, far)], (first,), WAIT)
+    second = [crossed] + [swap(crossed, 4, k, far) for k in range(1, half)]
+    second_beside = [swap(crossed, 2, 1, 2)]
+    for piece in second[1:]:
+        second_beside.append(swap(held(piece, (second_beside[0], first_beside)), 2, 1, 2))
+
+    def worked(near, beside, routed, after):
+        parts = near + beside
+        parts += [swap(piece, 1, 1, 2) for piece in parts]
+        return run_expert(parts, routed, first_column, weights, after)
+
+    outs, second_columns = worked(second, second_beside, routed[1], ())
     mine, near, leaving = leave_pair(outs, ())
-    first_back = swap(leaving, 2, 1, 2, True)
-    outs2, second_columns = worked(second, second_beside, routed[1], leaving)
-    arrived, last = split_rows(mine, near, first_back, range(half), tokens)
-    mine2, near2, leaving2 = leave_pair(outs2, (last,))
-    second_back = swap(leaving2, 2, 1, 2, True)
-    arrived += split_rows(mine2, near2, second_back, range(half, far), tokens)[0]
-    return arrived, [first_columns, second_columns], (outs2[0],)
+    back = swap(leaving, 2, 1, 2, True)
+    far_arrived, last = split_rows(mine, near, back, range(half, far), tokens)
+    outs, first_columns = worked([first], [first_beside], routed[0], (leaving,))
+    mine, near, leaving = leave_pair(outs, (last,))
+    back = swap(leaving, 2, 1, 2, True)
+    arrived, _ = split_rows(mine, near, back, range(half), tokens)
+    return arrived + far_arrived, [first_columns, second_columns], (outs[0],)
 
 
 def close_rows(layer_no, current, gain, returned, after=()):

time: 113 us -> 108 us (0.956)
  waiting for transfers between devices: 55.4 us -> 52.4 us
  starting transfers between devices: 36.9 us -> 34 us
    ppermute x40 -> x46, waiting for transfers between devices: 55.4 us -> 52.4 us  [swap(): lax.ppermute(value, 'expert', [(i, partner(i)) for i in range(count)])]
    ppermute x40 -> x46, starting transfers between devices: 36.9 us -> 34 us  [swap(): lax.ppermute(value, 'expert', [(i, partner(i)) for i in range(count)])]
  transfers between devices with their start and end apart: 40 -> 46, of which waited for: 17 -> 23; matrix products, arithmetic and copies ran while one was open for 0% -> 0% of each run, Pallas kernels for 16% -> 15%
where the time goes in v9:
time: 108 us; the launch traced here: 107 us
  waiting for transfers between devices  52.4 us (49%)
  starting transfers between devices  34 us (31%)
  Pallas kernels  20.7 us (19%)
    ppermute x46, waiting for transfers between devices, swap(): lax.ppermute(value, 'expert', [(i, partner(i)) for i in range(count)])  52.4 us
    ppermute x46, starting transfers between devices, swap(): lax.ppermute(value, 'expert', [(i, partner(i)) for i in range(count)])  34 us
    pallas_call x21, Pallas kernels, call(): pl.pallas_call(lambda *refs: kernel(*refs[len(after):]), out_shape=shapes...  20.7 us
  transfers between devices with their start and end apart: 46, of which 23 were waited for; matrix products, arithmetic and copies ran while one was open for 0% of the time, Pallas kernels for 15%

profile of v9, /device:TPU:0, one launch (start us, length us, event | category | flops | bytes accessed | tf_op | source)
XLA Modules:
  0.0 107.5 jit_solution(1328810305468358191)
XLA Ops:
  0.0 1.2 %shard_map.56.refs_1_ = bf16[32,2176]{1,0:T(8,128)(2,1)S(1)} custom-call(bf16[32,2048]{1,0:T(8,128)(2,1)} %bitcast.2, s32[2,2,8,16]{3,2,1,0:T(8,128)} %bitcast.4, f32[2,2048]{1,0:T(2,128)} %refs_2_.5), custom_call_target="tpu_custom_call" | custom-call | tf_op jit(solution)/shard_map/pallas_call | solution.py:29
  1.2 3.1 %collective-permute-start = (bf16[32,2176]{1,0:T(8,128)(2,1)S(1)}, bf16[32,2176]{1,0:T(8,128)(2,1)S(1)}, u32[]{:S(2)}, u32[]{:S(2)}) collective-permute-start(bf16[32,2176]{1,0:T(8,128)(2,1)S(1)} %shard_map.56.refs_1_), channel_id=1, source_target_pairs={{0,4},{1,5},{2,6},{3,7},{4,0},{5,1},{6,2},{7,3},{8,12},{9,13},{10,... | collective-permute-start | bytes 417800 | tf_op jit(solution)/shard_map/ppermute | solution.py:51
  4.3 2.6 %collective-permute-start.1 = (bf16[32,2176]{1,0:T(8,128)(2,1)S(1)}, bf16[32,2176]{1,0:T(8,128)(2,1)S(1)}, u32[]{:S(2)}, u32[]{:S(2)}) collective-permute-start(bf16[32,2176]{1,0:T(8,128)(2,1)S(1)} %shard_map.56.refs_1_), channel_id=1, source_target_pairs={{0,8},{1,9},{2,10},{3,11},{4,12},{5,13},{6,14},{7,15},{8,0},{9,1},... | collective-permute-start | bytes 417800 | tf_op jit(solution)/shard_map/ppermute | solution.py:51
  6.9 3.7 %shard_map.55 = (bf16[2048,1536]{1,0:T(8,128)(2,1)S(1)}, bf16[768,2048]{1,0:T(8,128)(2,1)S(1)}, f32[8,128]{1,0:T(8,128)S(1)}) custom-call(bf16[2,1,2048,1536]{3,2,1,0:T(8,128)(2,1)} %refs_1_.3, bf16[2,1,768,2048]{3,2,1,0:T(8,128)(2,1)} %refs_2_.4), custom_call_target="tpu_custom_call" | custom-call | tf_op jit(solution)/shard_map/pallas_call | solution.py:29
  10.7 1.6 %collective-permute-start.4 = (bf16[64,2176]{1,0:T(8,128)(2,1)S(1)}, bf16[64,2176]{1,0:T(8,128)(2,1)S(1)}, u32[]{:S(2)}, u32[]{:S(2)}) collective-permute-start(bf16[64,2176]{1,0:T(8,128)(2,1)S(1)} %shard_map.57.refs_0_.refs_1_), channel_id=1, source_target_pairs={{0,2},{1,3},{2,0},{3,1},{4,6},{5,7},{6,4},{7,5},{8,10},{9,11},{10,... | collective-permute-start | bytes 835592 | tf_op jit(solution)/shard_map/ppermute | solution.py:51
  12.3 1.1 %collective-permute-done.1.refs_1_ = bf16[32,2176]{1,0:T(8,128)(2,1)S(1)} collective-permute-done((bf16[32,2176]{1,0:T(8,128)(2,1)S(1)}, bf16[32,2176]{1,0:T(8,128)(2,1)S(1)}, u32[]{:S(2)}, u32[]{:S(2)}) %collective-permute-start.1) | collective-permute-done | bytes 139296 | tf_op jit(solution)/shard_map/ppermute | solution.py:51
  13.4 0.5 collective-permute-start.2
  13.9 1.5 %collective-permute-start.3 = (bf16[32,2176]{1,0:T(8,128)(2,1)S(1)}, bf16[32,2176]{1,0:T(8,128)(2,1)S(1)}, u32[]{:S(2)}, u32[]{:S(2)}) collective-permute-start(bf16[32,2176]{1,0:T(8,128)(2,1)S(1)} %shard_map.58.refs_0_), channel_id=1, source_target_pairs={{0,2},{1,3},{2,0},{3,1},{4,6},{5,7},{6,4},{7,5},{8,10},{9,11},{10,... | collective-permute-start | bytes 417800 | tf_op jit(solution)/shard_map/ppermute | solution.py:51
  15.4 3.1 %collective-permute-done.2.refs_1_ = bf16[32,2176]{1,0:T(8,128)(2,1)S(1)} collective-permute-done((bf16[32,2176]{1,0:T(8,128)(2,1)S(1)}, bf16[32,2176]{1,0:T(8,128)(2,1)S(1)}, u32[]{:S(2)}, u32[]{:S(2)}) %collective-permute-start.2) | collective-permute-done | bytes 139296 | tf_op jit(solution)/shard_map/ppermute | solution.py:51
  18.5 3.1 %collective-permute-done.3.refs_2_ = bf16[32,2176]{1,0:T(8,128)(2,1)S(1)} collective-permute-done((bf16[32,2176]{1,0:T(8,128)(2,1)S(1)}, bf16[32,2176]{1,0:T(8,128)(2,1)S(1)}, u32[]{:S(2)}, u32[]{:S(2)}) %collective-permute-start.3) | collective-permute-done | bytes 139296 | tf_op jit(solution)/shard_map/ppermute | solution.py:51
  21.6 1.5 %collective-permute-start.5 = (bf16[32,2176]{1,0:T(8,128)(2,1)S(1)}, bf16[32,2176]{1,0:T(8,128)(2,1)S(1)}, u32[]{:S(2)}, u32[]{:S(2)}) collective-permute-start(bf16[32,2176]{1,0:T(8,128)(2,1)S(1)} %collective-permute-done.2.refs_1_), channel_id=1, source_target_pairs={{0,2},{1,3},{2,0},{3,1},{4,6},{5,7},{6,4},{7,5},{8,10},{9,11},{10,... | collective-permute-start | bytes 417800 | tf_op jit(solution)/shard_map/ppermute | solution.py:51
  23.1 0.5 collective-permute-start.7
  23.6 3.0 %collective-permute-done.5.refs_3_ = bf16[32,2176]{1,0:T(8,128)(2,1)S(1)} collective-permute-done((bf16[32,2176]{1,0:T(8,128)(2,1)S(1)}, bf16[32,2176]{1,0:T(8,128)(2,1)S(1)}, u32[]{:S(2)}, u32[]{:S(2)}) %collective-permute-start.5) | collective-permute-done | bytes 139296 | tf_op jit(solution)/shard_map/ppermute | solution.py:51
  26.6 0.5 collective-permute-start.12
  27.2 0.8 collective-permute-done.9.refs_7_
  28.0 2.6 %shard_map.59 = (f32[64,2048]{1,0:T(8,128)S(1)}, f32[64,2048]{1,0:T(8,128)S(1)}, bf16[64,2048]{1,0:T(8,128)(2,1)S(1)}, bf16[32,2048]{1,0:T(8,128)(2,1)S(1)}, bf1...) custom-call(bf16[32,2176]{1,0:T(8,128)(2,1)S(1)} %shard_map.58.refs_0_, ...), custom_call_target="tpu_custom_call" | custom-call | tf_op jit(solution)/shard_map/pallas_call | solution.py:29
  31.3 0.7 collective-permute-done.10.refs_1_
  32.3 1.6 %collective-permute-start.16 = (bf16[64,2048]{1,0:T(8,128)(2,1)S(1)}, bf16[64,2048]{1,0:T(8,128)(2,1)S(1)}, u32[]{:S(2)}, u32[]{:S(2)}) collective-permute-start(bf16[64,2048]{1,0:T(8,128)(2,1)S(1)} %shard_map.60.refs_0_), channel_id=1, source_target_pairs={{0,2},{1,3},{2,0},{3,1},{4,6},{5,7},{6,4},{7,5},{8,10},{9,11},{10,... | collective-permute-start | bytes 786440 | tf_op jit(solution)/shard_map/ppermute | solution.py:51
  33.9 2.6 %shard_map.61 = (f32[64,2048]{1,0:T(8,128)S(1)}, f32[64,2048]{1,0:T(8,128)S(1)}, bf16[64,2048]{1,0:T(8,128)(2,1)S(1)}, bf16[32,2048]{1,0:T(8,128)(2,1)S(1)}, bf1...) custom-call(bf16[64,2048]{1,0:T(8,128)(2,1)S(1)} %shard_map.60.refs_0_, ...), custom_call_target="tpu_custom_call" | custom-call | tf_op jit(solution)/shard_map/pallas_call | solution.py:29
  37.1 3.7 %collective-permute-done.16.refs_2_ = bf16[64,2048]{1,0:T(8,128)(2,1)S(1)} collective-permute-done((bf16[64,2048]{1,0:T(8,128)(2,1)S(1)}, bf16[64,2048]{1,0:T(8,128)(2,1)S(1)}, u32[]{:S(2)}, u32[]{:S(2)}) %collective-permute-start.16) | collective-permute-done | bytes 262176 | tf_op jit(solution)/shard_map/ppermute | solution.py:51
  41.0 1.6 %collective-permute-start.19 = (bf16[64,2048]{1,0:T(8,128)(2,1)S(1)}, bf16[64,2048]{1,0:T(8,128)(2,1)S(1)}, u32[]{:S(2)}, u32[]{:S(2)}) collective-permute-start(bf16[64,2048]{1,0:T(8,128)(2,1)S(1)} %shard_map.64), channel_id=1, source_target_pairs={{0,2},{1,3},{2,0},{3,1},{4,6},{5,7},{6,4},{7,5},{8,10},{9,11},{10,... | collective-permute-start | bytes 786440 | tf_op jit(solution)/shard_map/ppermute | solution.py:51
  42.6 2.5 %collective-permute-start.22 = (bf16[32,2048]{1,0:T(8,128)(2,1)S(1)}, bf16[32,2048]{1,0:T(8,128)(2,1)S(1)}, u32[]{:S(2)}, u32[]{:S(2)}) collective-permute-start(bf16[32,2048]{1,0:T(8,128)(2,1)S(1)} %get-tuple-element.57.refs_0_), channel_id=1, source_target_pairs={{0,12},{1,13},{2,14},{3,15},{4,8},{5,9},{6,10},{7,11},{8,4},{9,5},... | collective-permute-start | bytes 393224 | tf_op jit(solution)/shard_map/ppermute | solution.py:51
  45.1 3.7 %collective-permute-done.19.refs_2_ = bf16[64,2048]{1,0:T(8,128)(2,1)S(1)} collective-permute-done((bf16[64,2048]{1,0:T(8,128)(2,1)S(1)}, bf16[64,2048]{1,0:T(8,128)(2,1)S(1)}, u32[]{:S(2)}, u32[]{:S(2)}) %collective-permute-start.19) | collective-permute-done | bytes 262176 | tf_op jit(solution)/shard_map/ppermute | solution.py:51
  48.9 0.5 collective-permute-start.20
  49.4 3.7 %shard_map.62 = (bf16[2048,1536]{1,0:T(8,128)(2,1)S(1)}, bf16[768,2048]{1,0:T(8,128)(2,1)S(1)}, f32[8,128]{1,0:T(8,128)S(1)}) custom-call(f32[64,2048]{1,0:T(8,128)S(1)} %get-tuple-element.52.refs_0_, bf16[2,1,2048,1536]{3,2,1,0:T(8,128)(2,1)} %refs_1_.3, bf16[2,1,768,2048]{3,2,1,0:T(8,128)(2,1)} %refs_2_.4), custom_call_target="tpu_custom_call" | custom-call | tf_op jit(solution)/shard_map/pallas_call | solution.py:29
  53.2 2.8 %collective-permute-done.21.refs_5_ = bf16[32,2048]{1,0:T(8,128)(2,1)S(1)} collective-permute-done((bf16[32,2048]{1,0:T(8,128)(2,1)S(1)}, bf16[32,2048]{1,0:T(8,128)(2,1)S(1)}, u32[]{:S(2)}, u32[]{:S(2)}) %collective-permute-start.21) | collective-permute-done | bytes 131104 | tf_op jit(solution)/shard_map/ppermute | solution.py:51
  56.7 2.8 %collective-permute-start.24 = (bf16[32,2048]{1,0:T(8,128)(2,1)S(1)}, bf16[32,2048]{1,0:T(8,128)(2,1)S(1)}, u32[]{:S(2)}, u32[]{:S(2)}) collective-permute-start(bf16[32,2048]{1,0:T(8,128)(2,1)S(1)} %get-tuple-element.65.refs_1_), channel_id=1, source_target_pairs={{0,8},{1,9},{2,10},{3,11},{4,12},{5,13},{6,14},{7,15},{8,0},{9,1},... | collective-permute-start | bytes 393224 | tf_op jit(solution)/shard_map/ppermute | solution.py:51
  59.5 3.4 %collective-permute-done.23.refs_2_ = bf16[32,2048]{1,0:T(8,128)(2,1)S(1)} collective-permute-done((bf16[32,2048]{1,0:T(8,128)(2,1)S(1)}, bf16[32,2048]{1,0:T(8,128)(2,1)S(1)}, u32[]{:S(2)}, u32[]{:S(2)}) %collective-permute-start.23) | collective-permute-done | bytes 131104 | tf_op jit(solution)/shard_map/ppermute | solution.py:51
  62.9 1.1 %collective-permute-start.27 = (bf16[64,2048]{1,0:T(8,128)(2,1)S(1)}, bf16[64,2048]{1,0:T(8,128)(2,1)S(1)}, u32[]{:S(2)}, u32[]{:S(2)}) collective-permute-start(bf16[64,2048]{1,0:T(8,128)(2,1)S(1)} %shard_map.67.refs_0_.refs_1_), channel_id=1, source_target_pairs={{0,2},{1,3},{2,0},{3,1},{4,6},{5,7},{6,4},{7,5},{8,10},{9,11},{10,... | collective-permute-start | bytes 786440 | tf_op jit(solution)/shard_map/ppermute | solution.py:51
  64.0 1.0 collective-permute-done.24.refs_1_
  65.2 1.1 collective-permute-start.26
  66.3 3.8 %collective-permute-done.25.refs_1_ = bf16[32,2048]{1,0:T(8,128)(2,1)S(1)} collective-permute-done((bf16[32,2048]{1,0:T(8,128)(2,1)S(1)}, bf16[32,2048]{1,0:T(8,128)(2,1)S(1)}, u32[]{:S(2)}, u32[]{:S(2)}) %collective-permute-start.25) | collective-permute-done | bytes 131104 | tf_op jit(solution)/shard_map/ppermute | solution.py:51
  70.1 2.0 %collective-permute-done.26.refs_2_ = bf16[32,2048]{1,0:T(8,128)(2,1)S(1)} collective-permute-done((bf16[32,2048]{1,0:T(8,128)(2,1)S(1)}, bf16[32,2048]{1,0:T(8,128)(2,1)S(1)}, u32[]{:S(2)}, u32[]{:S(2)}) %collective-permute-start.26) | collective-permute-done | bytes 131104 | tf_op jit(solution)/shard_map/ppermute | solution.py:51
  72.1 1.1 %collective-permute-start.28 = (bf16[32,2048]{1,0:T(8,128)(2,1)S(1)}, bf16[32,2048]{1,0:T(8,128)(2,1)S(1)}, u32[]{:S(2)}, u32[]{:S(2)}) collective-permute-start(bf16[32,2048]{1,0:T(8,128)(2,1)S(1)} %collective-permute-done.25.refs_1_), channel_id=1, source_target_pairs={{0,2},{1,3},{2,0},{3,1},{4,6},{5,7},{6,4},{7,5},{8,10},{9,11},{10,... | collective-permute-start | bytes 393224 | tf_op jit(solution)/shard_map/ppermute | solution.py:51
  73.2 0.5 collective-permute-start.30
  73.7 3.4 %collective-permute-done.28.refs_3_ = bf16[32,2048]{1,0:T(8,128)(2,1)S(1)} collective-permute-done((bf16[32,2048]{1,0:T(8,128)(2,1)S(1)}, bf16[32,2048]{1,0:T(8,128)(2,1)S(1)}, u32[]{:S(2)}, u32[]{:S(2)}) %collective-permute-start.28) | collective-permute-done | bytes 131104 | tf_op jit(solution)/shard_map/ppermute | solution.py:51
  77.1 1.3 %collective-permute-done.32.refs_7_ = bf16[32,2048]{1,0:T(8,128)(2,1)S(1)} collective-permute-done((bf16[32,2048]{1,0:T(8,128)(2,1)S(1)}, bf16[32,2048]{1,0:T(8,128)(2,1)S(1)}, u32[]{:S(2)}, u32[]{:S(2)}) %collective-permute-start.32) | collective-permute-done | bytes 131104 | tf_op jit(solution)/shard_map/ppermute | solution.py:51
  78.4 2.6 %shard_map.69 = (f32[64,2048]{1,0:T(8,128)S(1)}, f32[64,2048]{1,0:T(8,128)S(1)}, bf16[64,2048]{1,0:T(8,128)(2,1)S(1)}, bf16[32,2048]{1,0:T(8,128)(2,1)S(1)}, bf16[32,2048]{1,0:T(8,128)(2,1)S(1)}) custom-call(bf16[32,2048]{1,0:T(8,128)(2,1)S(1)} %shard_map.68.refs_0_, bf16[32,2048]{1,0:T(8,128)(2,1)S(1)} %collective-permute-done.25.refs_1_, ...), custom_call_target="tpu_custom_call" | custom-call | tf_op jit(solution)/shard_map/pallas_call | solution.py:29
  82.7 1.1 %collective-permute-start.39 = (bf16[64,2048]{1,0:T(8,128)(2,1)S(1)}, bf16[64,2048]{1,0:T(8,128)(2,1)S(1)}, u32[]{:S(2)}, u32[]{:S(2)}) collective-permute-start(bf16[64,2048]{1,0:T(8,128)(2,1)S(1)} %shard_map.70.refs_0_), channel_id=1, source_target_pairs={{0,2},{1,3},{2,0},{3,1},{4,6},{5,7},{6,4},{7,5},{8,10},{9,11},{10,... | collective-permute-start | bytes 786440 | tf_op jit(solution)/shard_map/ppermute | solution.py:51
  83.8 2.6 %shard_map.71 = (f32[64,2048]{1,0:T(8,128)S(1)}, f32[64,2048]{1,0:T(8,128)S(1)}, bf16[64,2048]{1,0:T(8,128)(2,1)S(1)}, bf16[32,2048]{1,0:T(8,128)(2,1)S(1)}, bf16[32,2048]{1,0:T(8,128)(2,1)S(1)}) custom-call(bf16[64,2048]{1,0:T(8,128)(2,1)S(1)} %shard_map.70.refs_0_, bf16[64,2048]{1,0:T(8,128)(2,1)S(1)} %shard_map.67.refs_0_.refs_1_, ...), custom_call_target="tpu_custom_call" | custom-call | tf_op jit(solution)/shard_map/pallas_call | solution.py:29
  87.1 4.2 %collective-permute-done.39.refs_2_ = bf16[64,2048]{1,0:T(8,128)(2,1)S(1)} collective-permute-done((bf16[64,2048]{1,0:T(8,128)(2,1)S(1)}, bf16[64,2048]{1,0:T(8,128)(2,1)S(1)}, u32[]{:S(2)}, u32[]{:S(2)}) %collective-permute-start.39) | collective-permute-done | bytes 262176 | tf_op jit(solution)/shard_map/ppermute | solution.py:51
  91.5 1.1 %collective-permute-start.42 = (bf16[64,2048]{1,0:T(8,128)(2,1)S(1)}, bf16[64,2048]{1,0:T(8,128)(2,1)S(1)}, u32[]{:S(2)}, u32[]{:S(2)}) collective-permute-start(bf16[64,2048]{1,0:T(8,128)(2,1)S(1)} %shard_map.73), channel_id=1, source_target_pairs={{0,2},{1,3},{2,0},{3,1},{4,6},{5,7},{6,4},{7,5},{8,10},{9,11},{10,... | collective-permute-start | bytes 786440 | tf_op jit(solution)/shard_map/ppermute | solution.py:51
  92.6 3.1 %collective-permute-start.45 = (bf16[32,2048]{1,0:T(8,128)(2,1)S(1)}, bf16[32,2048]{1,0:T(8,128)(2,1)S(1)}, u32[]{:S(2)}, u32[]{:S(2)}) collective-permute-start(bf16[32,2048]{1,0:T(8,128)(2,1)S(1)} %get-tuple-element.78.refs_0_), channel_id=1, source_target_pairs={{0,12},{1,13},{2,14},{3,15},{4,8},{5,9},{6,10},{7,11},{8,4},{9,5},... | collective-permute-start | bytes 393224 | tf_op jit(solution)/shard_map/ppermute | solution.py:51
  95.7 3.5 %collective-permute-done.42.refs_2_ = bf16[64,2048]{1,0:T(8,128)(2,1)S(1)} collective-permute-done((bf16[64,2048]{1,0:T(8,128)(2,1)S(1)}, bf16[64,2048]{1,0:T(8,128)(2,1)S(1)}, u32[]{:S(2)}, u32[]{:S(2)}) %collective-permute-start.42) | collective-permute-done | bytes 262176 | tf_op jit(solution)/shard_map/ppermute | solution.py:51
  99.3 0.5 collective-permute-start.43
  99.9 6.1 %collective-permute-done.44.refs_3_ = bf16[32,2048]{1,0:T(8,128)(2,1)S(1)} collective-permute-done((bf16[32,2048]{1,0:T(8,128)(2,1)S(1)}, bf16[32,2048]{1,0:T(8,128)(2,1)S(1)}, u32[]{:S(2)}, u32[]{:S(2)}) %collective-permute-start.44) | collective-permute-done | bytes 131104 | tf_op jit(solution)/shard_map/ppermute | solution.py:51
  106.0 0.7 collective-permute-done.43.refs_2_
  106.7 0.8 shard_map.75
  (69 shorter events, 5.3 us)
Async XLA Ops:
  1.2 9.4 %collective-permute-start = (bf16[32,2176]{1,0:T(8,128)(2,1)S(1)}, bf16[32,2176]{1,0:T(8,128)(2,1)S(1)}, u32[]{:S(2)}, u32[]{:S(2)}) collective-permute-start(bf16[32,2176]{1,0:T(8,128)(2,1)S(1)} %shard_map.56.refs_1_), channel_id=1, source_target_pairs={{0,4},{1,5},{2,6},{3,7},{4,0},{5,1},{6,2},{7,3},{8,12},{9,13},{10,... | collective-permute-start | bytes 417800 | tf_op jit(solution)/shard_map/ppermute | solution.py:51
  4.3 9.1 %collective-permute-start.1 = (bf16[32,2176]{1,0:T(8,128)(2,1)S(1)}, bf16[32,2176]{1,0:T(8,128)(2,1)S(1)}, u32[]{:S(2)}, u32[]{:S(2)}) collective-permute-start(bf16[32,2176]{1,0:T(8,128)(2,1)S(1)} %shard_map.56.refs_1_), channel_id=1, source_target_pairs={{0,8},{1,9},{2,10},{3,11},{4,12},{5,13},{6,14},{7,15},{8,0},{9,1},... | collective-permute-start | bytes 417800 | tf_op jit(solution)/shard_map/ppermute | solution.py:51
  10.7 10.9 %collective-permute-start.4 = (bf16[64,2176]{1,0:T(8,128)(2,1)S(1)}, bf16[64,2176]{1,0:T(8,128)(2,1)S(1)}, u32[]{:S(2)}, u32[]{:S(2)}) collective-permute-start(bf16[64,2176]{1,0:T(8,128)(2,1)S(1)} %shard_map.57.refs_0_.refs_1_), channel_id=1, source_target_pairs={{0,2},{1,3},{2,0},{3,1},{4,6},{5,7},{6,4},{7,5},{8,10},{9,11},{10,... | collective-permute-start | bytes 835592 | tf_op jit(solution)/shard_map/ppermute | solution.py:51
  13.4 5.1 %collective-permute-start.2 = (bf16[32,2176]{1,0:T(8,128)(2,1)S(1)}, bf16[32,2176]{1,0:T(8,128)(2,1)S(1)}, u32[]{:S(2)}, u32[]{:S(2)}) collective-permute-start(bf16[32,2176]{1,0:T(8,128)(2,1)S(1)} %shard_map.58.refs_0_), channel_id=1, source_target_pairs={{0,4},{1,5},{2,6},{3,7},{4,0},{5,1},{6,2},{7,3},{8,12},{9,13},{10,... | collective-permute-start | bytes 417800 | tf_op jit(solution)/shard_map/ppermute | solution.py:51
  13.9 7.7 %collective-permute-start.3 = (bf16[32,2176]{1,0:T(8,128)(2,1)S(1)}, bf16[32,2176]{1,0:T(8,128)(2,1)S(1)}, u32[]{:S(2)}, u32[]{:S(2)}) collective-permute-start(bf16[32,2176]{1,0:T(8,128)(2,1)S(1)} %shard_map.58.refs_0_), channel_id=1, source_target_pairs={{0,2},{1,3},{2,0},{3,1},{4,6},{5,7},{6,4},{7,5},{8,10},{9,11},{10,... | collective-permute-start | bytes 417800 | tf_op jit(solution)/shard_map/ppermute | solution.py:51
  21.6 5.1 %collective-permute-start.5 = (bf16[32,2176]{1,0:T(8,128)(2,1)S(1)}, bf16[32,2176]{1,0:T(8,128)(2,1)S(1)}, u32[]{:S(2)}, u32[]{:S(2)}) collective-permute-start(bf16[32,2176]{1,0:T(8,128)(2,1)S(1)} %collective-permute-done.2.refs_1_), channel_id=1, source_target_pairs={{0,2},{1,3},{2,0},{3,1},{4,6},{5,7},{6,4},{7,5},{8,10},{9,11},{10,... | collective-permute-start | bytes 417800 | tf_op jit(solution)/shard_map/ppermute | solution.py:51
  23.1 4.0 %collective-permute-start.6 = (bf16[32,2176]{1,0:T(8,128)(2,1)S(1)}, bf16[32,2176]{1,0:T(8,128)(2,1)S(1)}, u32[]{:S(2)}, u32[]{:S(2)}) collective-permute-start(bf16[32,2176]{1,0:T(8,128)(2,1)S(1)} %shard_map.58.refs_0_), channel_id=1, source_target_pairs={{0,1},{1,0},{2,3},{3,2},{4,5},{5,4},{6,7},{7,6},{8,9},{9,8},{10,11... | collective-permute-start | bytes 417800 | tf_op jit(solution)/shard_map/ppermute | solution.py:51
  23.1 4.1 %collective-permute-start.7 = (bf16[32,2176]{1,0:T(8,128)(2,1)S(1)}, bf16[32,2176]{1,0:T(8,128)(2,1)S(1)}, u32[]{:S(2)}, u32[]{:S(2)}) collective-permute-start(bf16[32,2176]{1,0:T(8,128)(2,1)S(1)} %collective-permute-done.2.refs_1_), channel_id=1, source_target_pairs={{0,1},{1,0},{2,3},{3,2},{4,5},{5,4},{6,7},{7,6},{8,9},{9,8},{10,11... | collective-permute-start | bytes 417800 | tf_op jit(solution)/shard_map/ppermute | solution.py:51
  23.6 3.6 %collective-permute-start.8 = (bf16[32,2176]{1,0:T(8,128)(2,1)S(1)}, bf16[32,2176]{1,0:T(8,128)(2,1)S(1)}, u32[]{:S(2)}, u32[]{:S(2)}) collective-permute-start(bf16[32,2176]{1,0:T(8,128)(2,1)S(1)} %collective-permute-done.3.refs_2_), channel_id=1, source_target_pairs={{0,1},{1,0},{2,3},{3,2},{4,5},{5,4},{6,7},{7,6},{8,9},{9,8},{10,11... | collective-permute-start | bytes 417800 | tf_op jit(solution)/shard_map/ppermute | solution.py:51
  26.6 1.4 %collective-permute-start.9 = (bf16[32,2176]{1,0:T(8,128)(2,1)S(1)}, bf16[32,2176]{1,0:T(8,128)(2,1)S(1)}, u32[]{:S(2)}, u32[]{:S(2)}) collective-permute-start(bf16[32,2176]{1,0:T(8,128)(2,1)S(1)} %collective-permute-done.5.refs_3_), channel_id=1, source_target_pairs={{0,1},{1,0},{2,3},{3,2},{4,5},{5,4},{6,7},{7,6},{8,9},{9,8},{10,11... | collective-permute-start | bytes 417800 | tf_op jit(solution)/shard_map/ppermute | solution.py:51
  26.6 7.2 %collective-permute-start.12 = (bf16[64,2176]{1,0:T(8,128)(2,1)S(1)}, bf16[64,2176]{1,0:T(8,128)(2,1)S(1)}, u32[]{:S(2)}, u32[]{:S(2)}) collective-permute-start(bf16[64,2176]{1,0:T(8,128)(2,1)S(1)} %shard_map.57.refs_0_.refs_1_), channel_id=1, source_target_pairs={{0,1},{1,0},{2,3},{3,2},{4,5},{5,4},{6,7},{7,6},{8,9},{9,8},{10,11... | collective-permute-start | bytes 835592 | tf_op jit(solution)/shard_map/ppermute | solution.py:51
  27.2 6.7 %collective-permute-start.13 = (bf16[64,2176]{1,0:T(8,128)(2,1)S(1)}, bf16[64,2176]{1,0:T(8,128)(2,1)S(1)}, u32[]{:S(2)}, u32[]{:S(2)}) collective-permute-start(bf16[64,2176]{1,0:T(8,128)(2,1)S(1)} %collective-permute-done.4.refs_2_), channel_id=1, source_target_pairs={{0,1},{1,0},{2,3},{3,2},{4,5},{5,4},{6,7},{7,6},{8,9},{9,8},{10,11... | collective-permute-start | bytes 835592 | tf_op jit(solution)/shard_map/ppermute | solution.py:51
  30.6 1.4 %collective-permute-start.10 = (bf16[32,2048]{1,0:T(8,128)(2,1)S(1)}, bf16[32,2048]{1,0:T(8,128)(2,1)S(1)}, u32[]{:S(2)}, u32[]{:S(2)}) collective-permute-start(bf16[32,2048]{1,0:T(8,128)(2,1)S(1)} %get-tuple-element.50), channel_id=1, source_target_pairs={{0,1},{1,0},{2,3},{3,2},{4,5},{5,4},{6,7},{7,6},{8,9},{9,8},{10,11... | collective-permute-start | bytes 393224 | tf_op jit(solution)/shard_map/ppermute | solution.py:51
  30.8 1.4 %collective-permute-start.11 = (bf16[32,2048]{1,0:T(8,128)(2,1)S(1)}, bf16[32,2048]{1,0:T(8,128)(2,1)S(1)}, u32[]{:S(2)}, u32[]{:S(2)}) collective-permute-start(bf16[32,2048]{1,0:T(8,128)(2,1)S(1)} %get-tuple-element.51), channel_id=1, source_target_pairs={{0,1},{1,0},{2,3},{3,2},{4,5},{5,4},{6,7},{7,6},{8,9},{9,8},{10,11... | collective-permute-start | bytes 393224 | tf_op jit(solution)/shard_map/ppermute | solution.py:51
  31.2 5.9 %collective-permute-start.15 = (bf16[64,2048]{1,0:T(8,128)(2,1)S(1)}, bf16[64,2048]{1,0:T(8,128)(2,1)S(1)}, u32[]{:S(2)}, u32[]{:S(2)}) collective-permute-start(bf16[64,2048]{1,0:T(8,128)(2,1)S(1)} %get-tuple-element.56), channel_id=1, source_target_pairs={{0,1},{1,0},{2,3},{3,2},{4,5},{5,4},{6,7},{7,6},{8,9},{9,8},{10,11... | collective-permute-start | bytes 786440 | tf_op jit(solution)/shard_map/ppermute | solution.py:51
  32.3 8.6 %collective-permute-start.16 = (bf16[64,2048]{1,0:T(8,128)(2,1)S(1)}, bf16[64,2048]{1,0:T(8,128)(2,1)S(1)}, u32[]{:S(2)}, u32[]{:S(2)}) collective-permute-start(bf16[64,2048]{1,0:T(8,128)(2,1)S(1)} %shard_map.60.refs_0_), channel_id=1, source_target_pairs={{0,2},{1,3},{2,0},{3,1},{4,6},{5,7},{6,4},{7,5},{8,10},{9,11},{10,... | collective-permute-start | bytes 786440 | tf_op jit(solution)/shard_map/ppermute | solution.py:51
  36.5 4.5 %collective-permute-start.17 = (bf16[32,2048]{1,0:T(8,128)(2,1)S(1)}, bf16[32,2048]{1,0:T(8,128)(2,1)S(1)}, u32[]{:S(2)}, u32[]{:S(2)}) collective-permute-start(bf16[32,2048]{1,0:T(8,128)(2,1)S(1)} %get-tuple-element.59), channel_id=1, source_target_pairs={{0,1},{1,0},{2,3},{3,2},{4,5},{5,4},{6,7},{7,6},{8,9},{9,8},{10,11... | collective-permute-start | bytes 393224 | tf_op jit(solution)/shard_map/ppermute | solution.py:51
  36.6 4.4 %collective-permute-start.18 = (bf16[32,2048]{1,0:T(8,128)(2,1)S(1)}, bf16[32,2048]{1,0:T(8,128)(2,1)S(1)}, u32[]{:S(2)}, u32[]{:S(2)}) collective-permute-start(bf16[32,2048]{1,0:T(8,128)(2,1)S(1)} %get-tuple-element.60), channel_id=1, source_target_pairs={{0,1},{1,0},{2,3},{3,2},{4,5},{5,4},{6,7},{7,6},{8,9},{9,8},{10,11... | collective-permute-start | bytes 393224 | tf_op jit(solution)/shard_map/ppermute | solution.py:51
  37.1 8.1 %collective-permute-start.14 = (bf16[64,2048]{1,0:T(8,128)(2,1)S(1)}, bf16[64,2048]{1,0:T(8,128)(2,1)S(1)}, u32[]{:S(2)}, u32[]{:S(2)}) collective-permute-start(bf16[64,2048]{1,0:T(8,128)(2,1)S(1)} %get-tuple-element.54), channel_id=1, source_target_pairs={{0,1},{1,0},{2,3},{3,2},{4,5},{5,4},{6,7},{7,6},{8,9},{9,8},{10,11... | collective-permute-start | bytes 786440 | tf_op jit(solution)/shard_map/ppermute | solution.py:51
  41.0 7.8 %collective-permute-start.19 = (bf16[64,2048]{1,0:T(8,128)(2,1)S(1)}, bf16[64,2048]{1,0:T(8,128)(2,1)S(1)}, u32[]{:S(2)}, u32[]{:S(2)}) collective-permute-start(bf16[64,2048]{1,0:T(8,128)(2,1)S(1)} %shard_map.64), channel_id=1, source_target_pairs={{0,2},{1,3},{2,0},{3,1},{4,6},{5,7},{6,4},{7,5},{8,10},{9,11},{10,... | collective-permute-start | bytes 786440 | tf_op jit(solution)/shard_map/ppermute | solution.py:51
  42.6 13.4 %collective-permute-start.22 = (bf16[32,2048]{1,0:T(8,128)(2,1)S(1)}, bf16[32,2048]{1,0:T(8,128)(2,1)S(1)}, u32[]{:S(2)}, u32[]{:S(2)}) collective-permute-start(bf16[32,2048]{1,0:T(8,128)(2,1)S(1)} %get-tuple-element.57.refs_0_), channel_id=1, source_target_pairs={{0,12},{1,13},{2,14},{3,15},{4,8},{5,9},{6,10},{7,11},{8,4},{9,5},... | collective-permute-start | bytes 393224 | tf_op jit(solution)/shard_map/ppermute | solution.py:51
  45.1 10.9 %collective-permute-start.21 = (bf16[32,2048]{1,0:T(8,128)(2,1)S(1)}, bf16[32,2048]{1,0:T(8,128)(2,1)S(1)}, u32[]{:S(2)}, u32[]{:S(2)}) collective-permute-start(bf16[32,2048]{1,0:T(8,128)(2,1)S(1)} %get-tuple-element.63), channel_id=1, source_target_pairs={{0,8},{1,9},{2,10},{3,11},{4,12},{5,13},{6,14},{7,15},{8,0},{9,1},... | collective-permute-start | bytes 393224 | tf_op jit(solution)/shard_map/ppermute | solution.py:51
  48.9 7.5 %copy-start = (bf16[2,16,2048]{2,1,0:T(8,128)(2,1)S(1)}, bf16[2,16,2048]{2,1,0:T(8,128)(2,1)}, u32[]{:S(2)}) copy-start(bf16[2,16,2048]{2,1,0:T(8,128)(2,1)} %param.5) | copy-start | bytes 393220
  48.9 7.5 %copy-start.1 = (f32[2,2048]{1,0:T(2,128)S(1)}, f32[2,2048]{1,0:T(2,128)}, u32[]{:S(2)}) copy-start(f32[2,2048]{1,0:T(2,128)} %refs_2_.5) | copy-start | bytes 49156
  48.9 7.5 %collective-permute-start.20 = (bf16[32,2048]{1,0:T(8,128)(2,1)S(1)}, bf16[32,2048]{1,0:T(8,128)(2,1)S(1)}, u32[]{:S(2)}, u32[]{:S(2)}) collective-permute-start(bf16[32,2048]{1,0:T(8,128)(2,1)S(1)} %get-tuple-element.62), channel_id=1, source_target_pairs={{0,4},{1,5},{2,6},{3,7},{4,0},{5,1},{6,2},{7,3},{8,12},{9,13},{10,... | collective-permute-start | bytes 393224 | tf_op jit(solution)/shard_map/ppermute | solution.py:51
  56.6 6.2 %collective-permute-start.23 = (bf16[32,2048]{1,0:T(8,128)(2,1)S(1)}, bf16[32,2048]{1,0:T(8,128)(2,1)S(1)}, u32[]{:S(2)}, u32[]{:S(2)}) collective-permute-start(bf16[32,2048]{1,0:T(8,128)(2,1)S(1)} %get-tuple-element.65.refs_1_), channel_id=1, source_target_pairs={{0,4},{1,5},{2,6},{3,7},{4,0},{5,1},{6,2},{7,3},{8,12},{9,13},{10,... | collective-permute-start | bytes 393224 | tf_op jit(solution)/shard_map/ppermute | solution.py:51
  56.7 8.3 %collective-permute-start.24 = (bf16[32,2048]{1,0:T(8,128)(2,1)S(1)}, bf16[32,2048]{1,0:T(8,128)(2,1)S(1)}, u32[]{:S(2)}, u32[]{:S(2)}) collective-permute-start(bf16[32,2048]{1,0:T(8,128)(2,1)S(1)} %get-tuple-element.65.refs_1_), channel_id=1, source_target_pairs={{0,8},{1,9},{2,10},{3,11},{4,12},{5,13},{6,14},{7,15},{8,0},{9,1},... | collective-permute-start | bytes 393224 | tf_op jit(solution)/shard_map/ppermute | solution.py:51
  62.9 9.2 %collective-permute-start.27 = (bf16[64,2048]{1,0:T(8,128)(2,1)S(1)}, bf16[64,2048]{1,0:T(8,128)(2,1)S(1)}, u32[]{:S(2)}, u32[]{:S(2)}) collective-permute-start(bf16[64,2048]{1,0:T(8,128)(2,1)S(1)} %shard_map.67.refs_0_.refs_1_), channel_id=1, source_target_pairs={{0,2},{1,3},{2,0},{3,1},{4,6},{5,7},{6,4},{7,5},{8,10},{9,11},{10,... | collective-permute-start | bytes 786440 | tf_op jit(solution)/shard_map/ppermute | solution.py:51
  65.1 5.0 %collective-permute-start.25 = (bf16[32,2048]{1,0:T(8,128)(2,1)S(1)}, bf16[32,2048]{1,0:T(8,128)(2,1)S(1)}, u32[]{:S(2)}, u32[]{:S(2)}) collective-permute-start(bf16[32,2048]{1,0:T(8,128)(2,1)S(1)} %shard_map.68.refs_0_), channel_id=1, source_target_pairs={{0,4},{1,5},{2,6},{3,7},{4,0},{5,1},{6,2},{7,3},{8,12},{9,13},{10,... | collective-permute-start | bytes 393224 | tf_op jit(solution)/shard_map/ppermute | solution.py:51
  65.2 6.9 %collective-permute-start.26 = (bf16[32,2048]{1,0:T(8,128)(2,1)S(1)}, bf16[32,2048]{1,0:T(8,128)(2,1)S(1)}, u32[]{:S(2)}, u32[]{:S(2)}) collective-permute-start(bf16[32,2048]{1,0:T(8,128)(2,1)S(1)} %shard_map.68.refs_0_), channel_id=1, source_target_pairs={{0,2},{1,3},{2,0},{3,1},{4,6},{5,7},{6,4},{7,5},{8,10},{9,11},{10,... | collective-permute-start | bytes 393224 | tf_op jit(solution)/shard_map/ppermute | solution.py:51
  72.1 5.0 %collective-permute-start.28 = (bf16[32,2048]{1,0:T(8,128)(2,1)S(1)}, bf16[32,2048]{1,0:T(8,128)(2,1)S(1)}, u32[]{:S(2)}, u32[]{:S(2)}) collective-permute-start(bf16[32,2048]{1,0:T(8,128)(2,1)S(1)} %collective-permute-done.25.refs_1_), channel_id=1, source_target_pairs={{0,2},{1,3},{2,0},{3,1},{4,6},{5,7},{6,4},{7,5},{8,10},{9,11},{10,... | collective-permute-start | bytes 393224 | tf_op jit(solution)/shard_map/ppermute | solution.py:51
  73.2 3.9 %collective-permute-start.29 = (bf16[32,2048]{1,0:T(8,128)(2,1)S(1)}, bf16[32,2048]{1,0:T(8,128)(2,1)S(1)}, u32[]{:S(2)}, u32[]{:S(2)}) collective-permute-start(bf16[32,2048]{1,0:T(8,128)(2,1)S(1)} %shard_map.68.refs_0_), channel_id=1, source_target_pairs={{0,1},{1,0},{2,3},{3,2},{4,5},{5,4},{6,7},{7,6},{8,9},{9,8},{10,11... | collective-permute-start | bytes 393224 | tf_op jit(solution)/shard_map/ppermute | solution.py:51
  73.2 3.9 %collective-permute-start.30 = (bf16[32,2048]{1,0:T(8,128)(2,1)S(1)}, bf16[32,2048]{1,0:T(8,128)(2,1)S(1)}, u32[]{:S(2)}, u32[]{:S(2)}) collective-permute-start(bf16[32,2048]{1,0:T(8,128)(2,1)S(1)} %collective-permute-done.25.refs_1_), channel_id=1, source_target_pairs={{0,1},{1,0},{2,3},{3,2},{4,5},{5,4},{6,7},{7,6},{8,9},{9,8},{10,11... | collective-permute-start | bytes 393224 | tf_op jit(solution)/shard_map/ppermute | solution.py:51
  73.7 3.4 %collective-permute-start.31 = (bf16[32,2048]{1,0:T(8,128)(2,1)S(1)}, bf16[32,2048]{1,0:T(8,128)(2,1)S(1)}, u32[]{:S(2)}, u32[]{:S(2)}) collective-permute-start(bf16[32,2048]{1,0:T(8,128)(2,1)S(1)} %collective-permute-done.26.refs_2_), channel_id=1, source_target_pairs={{0,1},{1,0},{2,3},{3,2},{4,5},{5,4},{6,7},{7,6},{8,9},{9,8},{10,11... | collective-permute-start | bytes 393224 | tf_op jit(solution)/shard_map/ppermute | solution.py:51
  77.1 1.3 %collective-permute-start.32 = (bf16[32,2048]{1,0:T(8,128)(2,1)S(1)}, bf16[32,2048]{1,0:T(8,128)(2,1)S(1)}, u32[]{:S(2)}, u32[]{:S(2)}) collective-permute-start(bf16[32,2048]{1,0:T(8,128)(2,1)S(1)} %collective-permute-done.28.refs_3_), channel_id=1, source_target_pairs={{0,1},{1,0},{2,3},{3,2},{4,5},{5,4},{6,7},{7,6},{8,9},{9,8},{10,11... | collective-permute-start | bytes 393224 | tf_op jit(solution)/shard_map/ppermute | solution.py:51
  81.0 1.4 %collective-permute-start.33 = (bf16[32,2048]{1,0:T(8,128)(2,1)S(1)}, bf16[32,2048]{1,0:T(8,128)(2,1)S(1)}, u32[]{:S(2)}, u32[]{:S(2)}) collective-permute-start(bf16[32,2048]{1,0:T(8,128)(2,1)S(1)} %get-tuple-element.71), channel_id=1, source_target_pairs={{0,1},{1,0},{2,3},{3,2},{4,5},{5,4},{6,7},{7,6},{8,9},{9,8},{10,11... | collective-permute-start | bytes 393224 | tf_op jit(solution)/shard_map/ppermute | solution.py:51
  81.3 1.4 %collective-permute-start.34 = (bf16[32,2048]{1,0:T(8,128)(2,1)S(1)}, bf16[32,2048]{1,0:T(8,128)(2,1)S(1)}, u32[]{:S(2)}, u32[]{:S(2)}) collective-permute-start(bf16[32,2048]{1,0:T(8,128)(2,1)S(1)} %get-tuple-element.72), channel_id=1, source_target_pairs={{0,1},{1,0},{2,3},{3,2},{4,5},{5,4},{6,7},{7,6},{8,9},{9,8},{10,11... | collective-permute-start | bytes 393224 | tf_op jit(solution)/shard_map/ppermute | solution.py:51
  81.6 2.2 %collective-permute-start.35 = (bf16[64,2048]{1,0:T(8,128)(2,1)S(1)}, bf16[64,2048]{1,0:T(8,128)(2,1)S(1)}, u32[]{:S(2)}, u32[]{:S(2)}) collective-permute-start(bf16[64,2048]{1,0:T(8,128)(2,1)S(1)} %shard_map.67.refs_0_.refs_1_), channel_id=1, source_target_pairs={{0,1},{1,0},{2,3},{3,2},{4,5},{5,4},{6,7},{7,6},{8,9},{9,8},{10,11... | collective-permute-start | bytes 786440 | tf_op jit(solution)/shard_map/ppermute | solution.py:51
  81.8 2.1 %collective-permute-start.36 = (bf16[64,2048]{1,0:T(8,128)(2,1)S(1)}, bf16[64,2048]{1,0:T(8,128)(2,1)S(1)}, u32[]{:S(2)}, u32[]{:S(2)}) collective-permute-start(bf16[64,2048]{1,0:T(8,128)(2,1)S(1)} %collective-permute-done.27.refs_2_), channel_id=1, source_target_pairs={{0,1},{1,0},{2,3},{3,2},{4,5},{5,4},{6,7},{7,6},{8,9},{9,8},{10,11... | collective-permute-start | bytes 786440 | tf_op jit(solution)/shard_map/ppermute | solution.py:51
  82.1 5.0 %collective-permute-start.38 = (bf16[64,2048]{1,0:T(8,128)(2,1)S(1)}, bf16[64,2048]{1,0:T(8,128)(2,1)S(1)}, u32[]{:S(2)}, u32[]{:S(2)}) collective-permute-start(bf16[64,2048]{1,0:T(8,128)(2,1)S(1)} %get-tuple-element.77), channel_id=1, source_target_pairs={{0,1},{1,0},{2,3},{3,2},{4,5},{5,4},{6,7},{7,6},{8,9},{9,8},{10,11... | collective-permute-start | bytes 786440 | tf_op jit(solution)/shard_map/ppermute | solution.py:51
  82.7 8.6 %collective-permute-start.39 = (bf16[64,2048]{1,0:T(8,128)(2,1)S(1)}, bf16[64,2048]{1,0:T(8,128)(2,1)S(1)}, u32[]{:S(2)}, u32[]{:S(2)}) collective-permute-start(bf16[64,2048]{1,0:T(8,128)(2,1)S(1)} %shard_map.70.refs_0_), channel_id=1, source_target_pairs={{0,2},{1,3},{2,0},{3,1},{4,6},{5,7},{6,4},{7,5},{8,10},{9,11},{10,... | collective-permute-start | bytes 786440 | tf_op jit(solution)/shard_map/ppermute | solution.py:51
  86.5 4.9 %collective-permute-start.40 = (bf16[32,2048]{1,0:T(8,128)(2,1)S(1)}, bf16[32,2048]{1,0:T(8,128)(2,1)S(1)}, u32[]{:S(2)}, u32[]{:S(2)}) collective-permute-start(bf16[32,2048]{1,0:T(8,128)(2,1)S(1)} %get-tuple-element.80), channel_id=1, source_target_pairs={{0,1},{1,0},{2,3},{3,2},{4,5},{5,4},{6,7},{7,6},{8,9},{9,8},{10,11... | collective-permute-start | bytes 393224 | tf_op jit(solution)/shard_map/ppermute | solution.py:51
  86.6 4.8 %collective-permute-start.41 = (bf16[32,2048]{1,0:T(8,128)(2,1)S(1)}, bf16[32,2048]{1,0:T(8,128)(2,1)S(1)}, u32[]{:S(2)}, u32[]{:S(2)}) collective-permute-start(bf16[32,2048]{1,0:T(8,128)(2,1)S(1)} %get-tuple-element.81), channel_id=1, source_target_pairs={{0,1},{1,0},{2,3},{3,2},{4,5},{5,4},{6,7},{7,6},{8,9},{9,8},{10,11... | collective-permute-start | bytes 393224 | tf_op jit(solution)/shard_map/ppermute | solution.py:51
  87.0 8.7 %collective-permute-start.37 = (bf16[64,2048]{1,0:T(8,128)(2,1)S(1)}, bf16[64,2048]{1,0:T(8,128)(2,1)S(1)}, u32[]{:S(2)}, u32[]{:S(2)}) collective-permute-start(bf16[64,2048]{1,0:T(8,128)(2,1)S(1)} %get-tuple-element.75), channel_id=1, source_target_pairs={{0,1},{1,0},{2,3},{3,2},{4,5},{5,4},{6,7},{7,6},{8,9},{9,8},{10,11... | collective-permute-start | bytes 786440 | tf_op jit(solution)/shard_map/ppermute | solution.py:51
  91.5 7.8 %collective-permute-start.42 = (bf16[64,2048]{1,0:T(8,128)(2,1)S(1)}, bf16[64,2048]{1,0:T(8,128)(2,1)S(1)}, u32[]{:S(2)}, u32[]{:S(2)}) collective-permute-start(bf16[64,2048]{1,0:T(8,128)(2,1)S(1)} %shard_map.73), channel_id=1, source_target_pairs={{0,2},{1,3},{2,0},{3,1},{4,6},{5,7},{6,4},{7,5},{8,10},{9,11},{10,... | collective-permute-start | bytes 786440 | tf_op jit(solution)/shard_map/ppermute | solution.py:51
  92.6 13.4 %collective-permute-start.45 = (bf16[32,2048]{1,0:T(8,128)(2,1)S(1)}, bf16[32,2048]{1,0:T(8,128)(2,1)S(1)}, u32[]{:S(2)}, u32[]{:S(2)}) collective-permute-start(bf16[32,2048]{1,0:T(8,128)(2,1)S(1)} %get-tuple-element.78.refs_0_), channel_id=1, source_target_pairs={{0,12},{1,13},{2,14},{3,15},{4,8},{5,9},{6,10},{7,11},{8,4},{9,5},... | collective-permute-start | bytes 393224 | tf_op jit(solution)/shard_map/ppermute | solution.py:51
  95.7 10.3 %collective-permute-start.44 = (bf16[32,2048]{1,0:T(8,128)(2,1)S(1)}, bf16[32,2048]{1,0:T(8,128)(2,1)S(1)}, u32[]{:S(2)}, u32[]{:S(2)}) collective-permute-start(bf16[32,2048]{1,0:T(8,128)(2,1)S(1)} %get-tuple-element.84), channel_id=1, source_target_pairs={{0,8},{1,9},{2,10},{3,11},{4,12},{5,13},{6,14},{7,15},{8,0},{9,1},... | collective-permute-start | bytes 393224 | tf_op jit(solution)/shard_map/ppermute | solution.py:51
  99.3 7.3 %collective-permute-start.43 = (bf16[32,2048]{1,0:T(8,128)(2,1)S(1)}, bf16[32,2048]{1,0:T(8,128)(2,1)S(1)}, u32[]{:S(2)}, u32[]{:S(2)}) collective-permute-start(bf16[32,2048]{1,0:T(8,128)(2,1)S(1)} %get-tuple-element.83), channel_id=1, source_target_pairs={{0,4},{1,5},{2,6},{3,7},{4,0},{5,1},{6,2},{7,3},{8,12},{9,13},{10,... | collective-permute-start | bytes 393224 | tf_op jit(solution)/shard_map/ppermute | solution.py:51

commit v10 on v9

--- a/solution.py
+++ b/solution.py
@@ -10,7 +10,6 @@
 eps = 1e-06
 LANES = 128
 MIB = 2**20
-CUTS = 2
 WAIT = 6 * 10**9
 VMEM = pl.BlockSpec(memory_space=pltpu.VMEM)
 ANY = pl.BlockSpec(memory_space=pl.ANY)
@@ -74,29 +73,45 @@
     return lax.optimization_barrier((value, until))[0]
 
 
-def sum_kernel(mine, *refs):
-    *parts, total = refs
-    rows = parts[0].shape[0]
-    for k, part in enumerate(parts):
-        span = slice(k * rows, (k + 1) * rows)
-        total[span] = (mine[span] + part[...].astype(f32)).astype(total.dtype)
-
-
-def split_kernel(mine, near, beside, *pieces):
+def sum_kernel(count, mine, *refs):
+    parts, totals = refs[:count], refs[count:]
+    size, rows = parts[0].shape[0], totals[0].shape[0]
+    grain = min(size, rows)
+    for low in range(0, mine.shape[0], grain):
+        part, total = parts[low // size], totals[low // rows]
+        inside = slice(low % size, low % size + grain)
+        total[low % rows : low % rows + grain] = (
+            mine[low : low + grain] + part[inside].astype(f32)
+        ).astype(total.dtype)
+
+
+def apart_kernel(first, count, mine, near, *refs):
+    beside, pieces = refs[:count], refs[count:]
     rows = pieces[0].shape[0]
-    total = mine[...] + near[...].astype(f32) + beside[...].astype(f32)
-    for k, piece in enumerate(pieces):
-        piece[...] = total[k * rows : (k + 1) * rows].astype(piece.dtype)
-
-
-def leave_pair(found, after):
+    for k in range(count):
+        span = slice((first + k) * rows, (first + k + 1) * rows)
+        total = mine[span] + near[span].astype(f32) + beside[k][...].astype(f32)
+        pieces[k][...] = total.astype(pieces[k].dtype)
+
+
+def cross_kernel(mine, near, beside, *refs):
+    *arrived, out = refs
+    rows = out.shape[0]
+    total = mine[:rows] + near[:rows].astype(f32) + beside[...].astype(f32)
+    for piece in arrived:
+        total = total + piece[...].astype(f32)
+    out[...] = total.astype(out.dtype)
+
+
+def leave_pair(found, count, after):
     mine_near, mine_beside, other_near, *other_beside = found
     arrived_beside = [swap(half, 1, 1, 2, True) for half in other_beside]
     arrived_near = swap(other_near, 1, 1, 2, True)
-    (leaving,) = call(
-        sum_kernel,
-        [(mine_beside.shape, bf16)],
-        [VMEM] * (1 + CUTS),
+    rows, width = mine_beside.shape
+    leaving = call(
+        functools.partial(sum_kernel, len(other_beside)),
+        [((rows // count, width), bf16)] * count,
+        [VMEM] * (1 + len(other_beside)),
         mine_beside,
         *arrived_beside,
         after=after,
@@ -104,18 +119,24 @@
     return mine_near, arrived_near, leaving
 
 
-def split_rows(mine_near, arrived_near, beside, distances, tokens):
-    far = lax.axis_size("expert") // 4
-    pieces = call(
-        split_kernel,
-        [((tokens, beside.shape[1]), bf16 if k else f32) for k in distances],
-        [VMEM] * 3,
-        mine_near,
-        arrived_near,
-        beside,
-    )
-    arrived = [swap(piece, 4, k, far, True) if k else piece for k, piece in zip(distances, pieces)]
-    return arrived, pieces[-1]
+def cross_rows(mine, near, beside):
+    far, count = lax.axis_size("expert") // 4, len(beside)
+    shape = beside[0].shape
+    hops, arrived = [], []
+    if count > 1:
+        hops = call(
+            functools.partial(apart_kernel, 1, count - 1),
+            [(shape, bf16)] * (count - 1),
+            [VMEM] * (count + 1),
+            mine,
+            near,
+            *beside[1:],
+        )
+        arrived = [swap(piece, 4, k, far, True) for k, piece in enumerate(hops, 1)]
+    (crossing,) = call(
+        cross_kernel, [(shape, bf16)], [VMEM] * (3 + len(arrived)), mine, near, beside[0], *arrived
+    )
+    return swap(crossing, 4, count, far, True), tuple(hops[-1:])
 
 
 def normed_rows(widened, gain_row):
@@ -251,7 +272,7 @@
             first += out.shape[0]
 
 
-def run_expert(parts, routed, first_column, weights, after):
+def run_expert(parts, routed, first_column, weights, cuts, after):
     gate_up, down_proj, _ = weights
     hidden_size, features = down_proj.shape
     width = parts[0].shape[1]
@@ -259,7 +280,7 @@
     quarter = count // 4
     wide = routed is None
     outs = [((quarter, features), f32)] * 2 + [((quarter, features), bf16)]
-    outs += [((quarter // CUTS, features), bf16)] * CUTS
+    outs += [((quarter // cuts, features), bf16)] * cuts
     if wide:
         outs = outs + [((count, width - features), bf16)]
     found = call(
@@ -274,7 +295,7 @@
         limit=24,
         after=after,
     )
-    return found[: 3 + CUTS], found[3 + CUTS] if wide else routed
+    return found[: 3 + cuts], found[3 + cuts] if wide else routed
 
 
 def in_hbm(array):
@@ -305,7 +326,7 @@
 
 
 def run_layer(rows, routed, first_column, weights, loaded=()):
-    far, tokens = lax.axis_size("expert") // 4, rows.shape[0]
+    far = lax.axis_size("expert") // 4
     routed = routed or [None, None]
     half = far // 2
     sent = [rows] + [swap(rows, 4, k, far) for k in range(1, half)]
@@ -317,20 +338,28 @@
     for piece in second[1:]:
         second_beside.append(swap(held(piece, (second_beside[0], first_beside)), 2, 1, 2))
 
-    def worked(near, beside, routed, after):
+    def worked(near, beside, routed, cuts, after):
         parts = near + beside
         parts += [swap(piece, 1, 1, 2) for piece in parts]
-        return run_expert(parts, routed, first_column, weights, after)
-
-    outs, second_columns = worked(second, second_beside, routed[1], ())
-    mine, near, leaving = leave_pair(outs, ())
-    back = swap(leaving, 2, 1, 2, True)
-    far_arrived, last = split_rows(mine, near, back, range(half, far), tokens)
-    outs, first_columns = worked([first], [first_beside], routed[0], (leaving,))
-    mine, near, leaving = leave_pair(outs, (last,))
-    back = swap(leaving, 2, 1, 2, True)
-    arrived, _ = split_rows(mine, near, back, range(half), tokens)
-    return arrived + far_arrived, [first_columns, second_columns], (outs[0],)
+        return run_expert(parts, routed, first_column, weights, cuts, after)
+
+    outs, second_columns = worked(second, second_beside, routed[1], 2, ())
+    mine, near, leaving = leave_pair(outs, half, ())
+    back = [swap(piece, 2, 1, 2, True) for piece in leaving]
+    crossed_back, hopped = cross_rows(mine, near, back)
+    outs, first_columns = worked([first], [first_beside], routed[0], 4, tuple(leaving[-1:]))
+    mine, near, leaving = leave_pair(outs, half, (*hopped, back[0]))
+    back = [swap(piece, 2, 1, 2, True) for piece in leaving]
+    pieces = call(
+        functools.partial(apart_kernel, 0, half),
+        [(rows.shape[:1] + mine.shape[1:], bf16 if k else f32) for k in range(half)],
+        [VMEM] * (2 + half),
+        mine,
+        near,
+        *back,
+    )
+    arrived = [swap(piece, 4, k, far, True) if k else piece for k, piece in enumerate(pieces)]
+    return [*arrived, crossed_back], [first_columns, second_columns], (outs[0],)
 
 
 def close_rows(layer_no, current, gain, returned, after=()):

time: 108 us -> 108 us (level)
  starting transfers between devices: 34 us -> 38.6 us
  waiting for transfers between devices: 52.4 us -> 48.3 us
    ppermute x46 -> x54, starting transfers between devices: 34 us -> 38.6 us  [swap(): lax.ppermute(value, 'expert', [(i, partner(i)) for i in range(count)])]
    ppermute x46 -> x54, waiting for transfers between devices: 52.4 us -> 48.3 us  [swap(): lax.ppermute(value, 'expert', [(i, partner(i)) for i in range(count)])]
    pallas_call x21 -> x23, Pallas kernels: 20.7 us -> 20.7 us  [call(): pl.pallas_call(lambda *refs: kernel(*refs[len(after):]), out_shape=shapes...]
  transfers between devices with their start and end apart: 46 -> 54, of which waited for: 23 -> 31; matrix products, arithmetic and copies ran while one was open for 0% -> 0% of each run, Pallas kernels for 15% -> 17%
where the time goes in v10:
time: 108 us
  waiting for transfers between devices  48.3 us (45%)
  starting transfers between devices  38.6 us (36%)
  Pallas kernels  20.7 us (19%)
    ppermute x54, waiting for transfers between devices, swap(): lax.ppermute(value, 'expert', [(i, partner(i)) for i in range(count)])  48.3 us
    ppermute x54, starting transfers between devices, swap(): lax.ppermute(value, 'expert', [(i, partner(i)) for i in range(count)])  38.6 us
    pallas_call x23, Pallas kernels, call(): pl.pallas_call(lambda *refs: kernel(*refs[len(after):]), out_shape=shapes...  20.7 us
  transfers between devices with their start and end apart: 54, of which 31 were waited for; matrix products, arithmetic and copies ran while one was open for 0% of the time, Pallas kernels for 17%

profile of v10, /device:TPU:0, one launch (start us, length us, event | category | flops | bytes accessed | tf_op | source)
XLA Modules:
  0.0 107.9 jit_solution(9639635269005413261)
XLA Ops:
  0.0 1.2 %shard_map.56.refs_1_ = bf16[32,2176]{1,0:T(8,128)(2,1)S(1)} custom-call(bf16[32,2048]{1,0:T(8,128)(2,1)} %bitcast.2, s32[2,2,8,16]{3,2,1,0:T(8,128)} %bitcast.4, f32[2,2048]{1,0:T(2,128)} %refs_2_.5), custom_call_target="tpu_custom_call" | custom-call | tf_op jit(solution)/shard_map/pallas_call | solution.py:28
  1.2 3.1 %collective-permute-start = (bf16[32,2176]{1,0:T(8,128)(2,1)S(1)}, bf16[32,2176]{1,0:T(8,128)(2,1)S(1)}, u32[]{:S(2)}, u32[]{:S(2)}) collective-permute-start(bf16[32,2176]{1,0:T(8,128)(2,1)S(1)} %shard_map.56.refs_1_), channel_id=1, source_target_pairs={{0,4},{1,5},{2,6},{3,7},{4,0},{5,1},{6,2},{7,3},{8,12},{9,13},{10,... | collective-permute-start | bytes 417800 | tf_op jit(solution)/shard_map/ppermute | solution.py:50
  4.3 2.6 %collective-permute-start.1 = (bf16[32,2176]{1,0:T(8,128)(2,1)S(1)}, bf16[32,2176]{1,0:T(8,128)(2,1)S(1)}, u32[]{:S(2)}, u32[]{:S(2)}) collective-permute-start(bf16[32,2176]{1,0:T(8,128)(2,1)S(1)} %shard_map.56.refs_1_), channel_id=1, source_target_pairs={{0,8},{1,9},{2,10},{3,11},{4,12},{5,13},{6,14},{7,15},{8,0},{9,1},... | collective-permute-start | bytes 417800 | tf_op jit(solution)/shard_map/ppermute | solution.py:50
  6.9 3.7 %shard_map.55 = (bf16[2048,1536]{1,0:T(8,128)(2,1)S(1)}, bf16[768,2048]{1,0:T(8,128)(2,1)S(1)}, f32[8,128]{1,0:T(8,128)S(1)}) custom-call(bf16[2,1,2048,1536]{3,2,1,0:T(8,128)(2,1)} %refs_1_.3, bf16[2,1,768,2048]{3,2,1,0:T(8,128)(2,1)} %refs_2_.4), custom_call_target="tpu_custom_call" | custom-call | tf_op jit(solution)/shard_map/pallas_call | solution.py:28
  10.7 1.6 %collective-permute-start.4 = (bf16[64,2176]{1,0:T(8,128)(2,1)S(1)}, bf16[64,2176]{1,0:T(8,128)(2,1)S(1)}, u32[]{:S(2)}, u32[]{:S(2)}) collective-permute-start(bf16[64,2176]{1,0:T(8,128)(2,1)S(1)} %shard_map.57.refs_0_.refs_1_), channel_id=1, source_target_pairs={{0,2},{1,3},{2,0},{3,1},{4,6},{5,7},{6,4},{7,5},{8,10},{9,11},{10,... | collective-permute-start | bytes 835592 | tf_op jit(solution)/shard_map/ppermute | solution.py:50
  12.3 1.1 %collective-permute-done.1.refs_1_ = bf16[32,2176]{1,0:T(8,128)(2,1)S(1)} collective-permute-done((bf16[32,2176]{1,0:T(8,128)(2,1)S(1)}, bf16[32,2176]{1,0:T(8,128)(2,1)S(1)}, u32[]{:S(2)}, u32[]{:S(2)}) %collective-permute-start.1) | collective-permute-done | bytes 139296 | tf_op jit(solution)/shard_map/ppermute | solution.py:50
  13.9 1.5 %collective-permute-start.3 = (bf16[32,2176]{1,0:T(8,128)(2,1)S(1)}, bf16[32,2176]{1,0:T(8,128)(2,1)S(1)}, u32[]{:S(2)}, u32[]{:S(2)}) collective-permute-start(bf16[32,2176]{1,0:T(8,128)(2,1)S(1)} %shard_map.58.refs_0_), channel_id=1, source_target_pairs={{0,2},{1,3},{2,0},{3,1},{4,6},{5,7},{6,4},{7,5},{8,10},{9,11},{10,... | collective-permute-start | bytes 417800 | tf_op jit(solution)/shard_map/ppermute | solution.py:50
  15.4 3.1 %collective-permute-done.2.refs_1_ = bf16[32,2176]{1,0:T(8,128)(2,1)S(1)} collective-permute-done((bf16[32,2176]{1,0:T(8,128)(2,1)S(1)}, bf16[32,2176]{1,0:T(8,128)(2,1)S(1)}, u32[]{:S(2)}, u32[]{:S(2)}) %collective-permute-start.2) | collective-permute-done | bytes 139296 | tf_op jit(solution)/shard_map/ppermute | solution.py:50
  18.5 3.1 %collective-permute-done.3.refs_2_ = bf16[32,2176]{1,0:T(8,128)(2,1)S(1)} collective-permute-done((bf16[32,2176]{1,0:T(8,128)(2,1)S(1)}, bf16[32,2176]{1,0:T(8,128)(2,1)S(1)}, u32[]{:S(2)}, u32[]{:S(2)}) %collective-permute-start.3) | collective-permute-done | bytes 139296 | tf_op jit(solution)/shard_map/ppermute | solution.py:50
  21.6 1.5 %collective-permute-start.5 = (bf16[32,2176]{1,0:T(8,128)(2,1)S(1)}, bf16[32,2176]{1,0:T(8,128)(2,1)S(1)}, u32[]{:S(2)}, u32[]{:S(2)}) collective-permute-start(bf16[32,2176]{1,0:T(8,128)(2,1)S(1)} %collective-permute-done.2.refs_1_), channel_id=1, source_target_pairs={{0,2},{1,3},{2,0},{3,1},{4,6},{5,7},{6,4},{7,5},{8,10},{9,11},{10,... | collective-permute-start | bytes 417800 | tf_op jit(solution)/shard_map/ppermute | solution.py:50
  23.6 3.0 %collective-permute-done.5.refs_3_ = bf16[32,2176]{1,0:T(8,128)(2,1)S(1)} collective-permute-done((bf16[32,2176]{1,0:T(8,128)(2,1)S(1)}, bf16[32,2176]{1,0:T(8,128)(2,1)S(1)}, u32[]{:S(2)}, u32[]{:S(2)}) %collective-permute-start.5) | collective-permute-done | bytes 139296 | tf_op jit(solution)/shard_map/ppermute | solution.py:50
  27.2 0.8 collective-permute-done.9.refs_7_
  28.0 2.6 %shard_map.59 = (f32[64,2048]{1,0:T(8,128)S(1)}, f32[64,2048]{1,0:T(8,128)S(1)}, bf16[64,2048]{1,0:T(8,128)(2,1)S(1)}, bf16[32,2048]{1,0:T(8,128)(2,1)S(1)}, bf1...) custom-call(bf16[32,2176]{1,0:T(8,128)(2,1)S(1)} %shard_map.58.refs_0_, ...), custom_call_target="tpu_custom_call" | custom-call | tf_op jit(solution)/shard_map/pallas_call | solution.py:28
  31.3 0.7 collective-permute-done.10.refs_1_
  32.3 1.6 %collective-permute-start.16 = (bf16[32,2048]{1,0:T(8,128)(2,1)S(1)}, bf16[32,2048]{1,0:T(8,128)(2,1)S(1)}, u32[]{:S(2)}, u32[]{:S(2)}) collective-permute-start(bf16[32,2048]{1,0:T(8,128)(2,1)S(1)} %get-tuple-element.60.refs_0_), channel_id=1, source_target_pairs={{0,2},{1,3},{2,0},{3,1},{4,6},{5,7},{6,4},{7,5},{8,10},{9,11},{10,... | collective-permute-start | bytes 393224 | tf_op jit(solution)/shard_map/ppermute | solution.py:50
  33.9 2.6 %shard_map.61 = (f32[64,2048]{1,0:T(8,128)S(1)}, f32[64,2048]{1,0:T(8,128)S(1)}, bf16[64,2048]{1,0:T(8,128)(2,1)S(1)}, bf16[16,2048]{1,0:T(8,128)(2,1)S(1)}, bf1...) custom-call(bf16[32,2048]{1,0:T(8,128)(2,1)S(1)} %get-tuple-element., ...), custom_call_target="tpu_custom_call" | custom-call | tf_op jit(solution)/shard_map/pallas_call | solution.py:28
  36.6 0.5 collective-permute-start.17
  39.6 2.9 %collective-permute-done.17.refs_1_.refs_2_ = bf16[32,2048]{1,0:T(8,128)(2,1)S(1)} collective-permute-done((bf16[32,2048]{1,0:T(8,128)(2,1)S(1)}, bf16[32,2048]{1,0:T(8,128)(2,1)S(1)}, u32[]{:S(2)}, u32[]{:S(2)}) %collective-permute-start.17) | collective-permute-done | bytes 131104 | tf_op jit(solution)/shard_map/ppermute | solution.py:50
  42.5 0.6 collective-permute-start.22
  43.1 1.5 %collective-permute-start.23 = (bf16[32,2048]{1,0:T(8,128)(2,1)S(1)}, bf16[32,2048]{1,0:T(8,128)(2,1)S(1)}, u32[]{:S(2)}, u32[]{:S(2)}) collective-permute-start(bf16[32,2048]{1,0:T(8,128)(2,1)S(1)} %get-tuple-element.73), channel_id=1, source_target_pairs={{0,2},{1,3},{2,0},{3,1},{4,6},{5,7},{6,4},{7,5},{8,10},{9,11},{10,... | collective-permute-start | bytes 393224 | tf_op jit(solution)/shard_map/ppermute | solution.py:50
  44.7 1.4 %collective-permute-start.26 = (bf16[32,2048]{1,0:T(8,128)(2,1)S(1)}, bf16[32,2048]{1,0:T(8,128)(2,1)S(1)}, u32[]{:S(2)}, u32[]{:S(2)}) collective-permute-start(bf16[32,2048]{1,0:T(8,128)(2,1)S(1)} %shard_map.66), channel_id=1, source_target_pairs={{0,8},{1,9},{2,10},{3,11},{4,12},{5,13},{6,14},{7,15},{8,0},{9,1},... | collective-permute-start | bytes 393224 | tf_op jit(solution)/shard_map/ppermute | solution.py:50
  46.1 2.9 %collective-permute-done.22.refs_2_ = bf16[32,2048]{1,0:T(8,128)(2,1)S(1)} collective-permute-done((bf16[32,2048]{1,0:T(8,128)(2,1)S(1)}, bf16[32,2048]{1,0:T(8,128)(2,1)S(1)}, u32[]{:S(2)}, u32[]{:S(2)}) %collective-permute-start.22) | collective-permute-done | bytes 131104 | tf_op jit(solution)/shard_map/ppermute | solution.py:50
  49.0 1.5 %collective-permute-done.23.refs_3_ = bf16[32,2048]{1,0:T(8,128)(2,1)S(1)} collective-permute-done((bf16[32,2048]{1,0:T(8,128)(2,1)S(1)}, bf16[32,2048]{1,0:T(8,128)(2,1)S(1)}, u32[]{:S(2)}, u32[]{:S(2)}) %collective-permute-start.23) | collective-permute-done | bytes 131104 | tf_op jit(solution)/shard_map/ppermute | solution.py:50
  51.1 3.7 %shard_map.62 = (bf16[2048,1536]{1,0:T(8,128)(2,1)S(1)}, bf16[768,2048]{1,0:T(8,128)(2,1)S(1)}, f32[8,128]{1,0:T(8,128)S(1)}) custom-call(f32[64,2048]{1,0:T(8,128)S(1)} %get-tuple-element.61.refs_0_, bf16[2,1,2048,1536]{3,2,1,0:T(8,128)(2,1)} %refs_1_.3, bf16[2,1,768,2048]{3,2,1,0:T(8,128)(2,1)} %refs_2_.4), custom_call_target="tpu_custom_call" | custom-call | tf_op jit(solution)/shard_map/pallas_call | solution.py:28
  54.9 1.0 collective-permute-done.24.refs_4_
  56.1 0.6 collective-permute-start.27
  56.7 2.6 %collective-permute-start.28 = (bf16[32,2048]{1,0:T(8,128)(2,1)S(1)}, bf16[32,2048]{1,0:T(8,128)(2,1)S(1)}, u32[]{:S(2)}, u32[]{:S(2)}) collective-permute-start(bf16[32,2048]{1,0:T(8,128)(2,1)S(1)} %get-tuple-element.77.refs_1_), channel_id=1, source_target_pairs={{0,8},{1,9},{2,10},{3,11},{4,12},{5,13},{6,14},{7,15},{8,0},{9,1},... | collective-permute-start | bytes 393224 | tf_op jit(solution)/shard_map/ppermute | solution.py:50
  59.3 2.8 %collective-permute-done.27.refs_2_ = bf16[32,2048]{1,0:T(8,128)(2,1)S(1)} collective-permute-done((bf16[32,2048]{1,0:T(8,128)(2,1)S(1)}, bf16[32,2048]{1,0:T(8,128)(2,1)S(1)}, u32[]{:S(2)}, u32[]{:S(2)}) %collective-permute-start.27) | collective-permute-done | bytes 131104 | tf_op jit(solution)/shard_map/ppermute | solution.py:50
  62.2 2.9 %collective-permute-start.31 = (bf16[64,2048]{1,0:T(8,128)(2,1)S(1)}, bf16[64,2048]{1,0:T(8,128)(2,1)S(1)}, u32[]{:S(2)}, u32[]{:S(2)}) collective-permute-start(bf16[64,2048]{1,0:T(8,128)(2,1)S(1)} %shard_map.68.refs_0_.refs_1_), channel_id=1, source_target_pairs={{0,2},{1,3},{2,0},{3,1},{4,6},{5,7},{6,4},{7,5},{8,10},{9,11},{10,... | collective-permute-start | bytes 786440 | tf_op jit(solution)/shard_map/ppermute | solution.py:50
  65.2 1.9 %collective-permute-start.30 = (bf16[32,2048]{1,0:T(8,128)(2,1)S(1)}, bf16[32,2048]{1,0:T(8,128)(2,1)S(1)}, u32[]{:S(2)}, u32[]{:S(2)}) collective-permute-start(bf16[32,2048]{1,0:T(8,128)(2,1)S(1)} %shard_map.69.refs_0_), channel_id=1, source_target_pairs={{0,2},{1,3},{2,0},{3,1},{4,6},{5,7},{6,4},{7,5},{8,10},{9,11},{10,... | collective-permute-start | bytes 393224 | tf_op jit(solution)/shard_map/ppermute | solution.py:50
  67.1 3.1 %collective-permute-done.29.refs_1_ = bf16[32,2048]{1,0:T(8,128)(2,1)S(1)} collective-permute-done((bf16[32,2048]{1,0:T(8,128)(2,1)S(1)}, bf16[32,2048]{1,0:T(8,128)(2,1)S(1)}, u32[]{:S(2)}, u32[]{:S(2)}) %collective-permute-start.29) | collective-permute-done | bytes 131104 | tf_op jit(solution)/shard_map/ppermute | solution.py:50
  70.2 2.1 %collective-permute-done.30.refs_2_ = bf16[32,2048]{1,0:T(8,128)(2,1)S(1)} collective-permute-done((bf16[32,2048]{1,0:T(8,128)(2,1)S(1)}, bf16[32,2048]{1,0:T(8,128)(2,1)S(1)}, u32[]{:S(2)}, u32[]{:S(2)}) %collective-permute-start.30) | collective-permute-done | bytes 131104 | tf_op jit(solution)/shard_map/ppermute | solution.py:50
  72.3 2.0 %collective-permute-start.32 = (bf16[32,2048]{1,0:T(8,128)(2,1)S(1)}, bf16[32,2048]{1,0:T(8,128)(2,1)S(1)}, u32[]{:S(2)}, u32[]{:S(2)}) collective-permute-start(bf16[32,2048]{1,0:T(8,128)(2,1)S(1)} %collective-permute-done.29.refs_1_), channel_id=1, source_target_pairs={{0,2},{1,3},{2,0},{3,1},{4,6},{5,7},{6,4},{7,5},{8,10},{9,11},{10,... | collective-permute-start | bytes 393224 | tf_op jit(solution)/shard_map/ppermute | solution.py:50
  74.8 2.4 %collective-permute-done.32.refs_3_ = bf16[32,2048]{1,0:T(8,128)(2,1)S(1)} collective-permute-done((bf16[32,2048]{1,0:T(8,128)(2,1)S(1)}, bf16[32,2048]{1,0:T(8,128)(2,1)S(1)}, u32[]{:S(2)}, u32[]{:S(2)}) %collective-permute-start.32) | collective-permute-done | bytes 131104 | tf_op jit(solution)/shard_map/ppermute | solution.py:50
  77.8 0.8 collective-permute-done.36.refs_7_
  78.6 2.6 %shard_map.70 = (f32[64,2048]{1,0:T(8,128)S(1)}, f32[64,2048]{1,0:T(8,128)S(1)}, bf16[64,2048]{1,0:T(8,128)(2,1)S(1)}, bf16[32,2048]{1,0:T(8,128)(2,1)S(1)}, bf16[32,2048]{1,0:T(8,128)(2,1)S(1)}) custom-call(bf16[32,2048]{1,0:T(8,128)(2,1)S(1)} %shard_map.69.refs_0_, bf16[32,2048]{1,0:T(8,128)(2,1)S(1)} %collective-permute-done.29.refs_1_, ...), custom_call_target="tpu_custom_call" | custom-call | tf_op jit(solution)/shard_map/pallas_call | solution.py:28
  82.0 0.7 collective-permute-done.37.refs_1_
  82.9 2.1 %collective-permute-start.43 = (bf16[32,2048]{1,0:T(8,128)(2,1)S(1)}, bf16[32,2048]{1,0:T(8,128)(2,1)S(1)}, u32[]{:S(2)}, u32[]{:S(2)}) collective-permute-start(bf16[32,2048]{1,0:T(8,128)(2,1)S(1)} %get-tuple-element.85.refs_0_), channel_id=1, source_target_pairs={{0,2},{1,3},{2,0},{3,1},{4,6},{5,7},{6,4},{7,5},{8,10},{9,11},{10,... | collective-permute-start | bytes 393224 | tf_op jit(solution)/shard_map/ppermute | solution.py:50
  85.0 2.6 %shard_map.72 = (f32[64,2048]{1,0:T(8,128)S(1)}, f32[64,2048]{1,0:T(8,128)S(1)}, bf16[64,2048]{1,0:T(8,128)(2,1)S(1)}, bf16[16,2048]{1,0:T(8,128)(2,1)S(1)}, bf1...) custom-call(bf16[32,2048]{1,0:T(8,128)(2,1)S(1)} %get-tuple-element.85.refs_0_, ...), custom_call_target="tpu_custom_call" | custom-call | tf_op jit(solution)/shard_map/pallas_call | solution.py:28
  88.2 0.7 collective-permute-done.45.refs_3_
  90.7 2.9 %collective-permute-done.44.refs_1_.refs_2_ = bf16[32,2048]{1,0:T(8,128)(2,1)S(1)} collective-permute-done((bf16[32,2048]{1,0:T(8,128)(2,1)S(1)}, bf16[32,2048]{1,0:T(8,128)(2,1)S(1)}, u32[]{:S(2)}, u32[]{:S(2)}) %collective-permute-start.44) | collective-permute-done | bytes 131104 | tf_op jit(solution)/shard_map/ppermute | solution.py:50
  94.0 1.8 %collective-permute-start.50 = (bf16[32,2048]{1,0:T(8,128)(2,1)S(1)}, bf16[32,2048]{1,0:T(8,128)(2,1)S(1)}, u32[]{:S(2)}, u32[]{:S(2)}) collective-permute-start(bf16[32,2048]{1,0:T(8,128)(2,1)S(1)} %get-tuple-element.98), channel_id=1, source_target_pairs={{0,2},{1,3},{2,0},{3,1},{4,6},{5,7},{6,4},{7,5},{8,10},{9,11},{10,... | collective-permute-start | bytes 393224 | tf_op jit(solution)/shard_map/ppermute | solution.py:50
  95.8 1.1 %collective-permute-start.53 = (bf16[32,2048]{1,0:T(8,128)(2,1)S(1)}, bf16[32,2048]{1,0:T(8,128)(2,1)S(1)}, u32[]{:S(2)}, u32[]{:S(2)}) collective-permute-start(bf16[32,2048]{1,0:T(8,128)(2,1)S(1)} %shard_map.76), channel_id=1, source_target_pairs={{0,8},{1,9},{2,10},{3,11},{4,12},{5,13},{6,14},{7,15},{8,0},{9,1},... | collective-permute-start | bytes 393224 | tf_op jit(solution)/shard_map/ppermute | solution.py:50
  96.9 3.2 %collective-permute-done.49.refs_2_ = bf16[32,2048]{1,0:T(8,128)(2,1)S(1)} collective-permute-done((bf16[32,2048]{1,0:T(8,128)(2,1)S(1)}, bf16[32,2048]{1,0:T(8,128)(2,1)S(1)}, u32[]{:S(2)}, u32[]{:S(2)}) %collective-permute-start.49) | collective-permute-done | bytes 131104 | tf_op jit(solution)/shard_map/ppermute | solution.py:50
  100.1 1.5 %collective-permute-done.50.refs_3_ = bf16[32,2048]{1,0:T(8,128)(2,1)S(1)} collective-permute-done((bf16[32,2048]{1,0:T(8,128)(2,1)S(1)}, bf16[32,2048]{1,0:T(8,128)(2,1)S(1)}, u32[]{:S(2)}, u32[]{:S(2)}) %collective-permute-start.50) | collective-permute-done | bytes 131104 | tf_op jit(solution)/shard_map/ppermute | solution.py:50
  101.8 2.7 %collective-permute-done.53.refs_3_ = bf16[32,2048]{1,0:T(8,128)(2,1)S(1)} collective-permute-done((bf16[32,2048]{1,0:T(8,128)(2,1)S(1)}, bf16[32,2048]{1,0:T(8,128)(2,1)S(1)}, u32[]{:S(2)}, u32[]{:S(2)}) %collective-permute-start.53) | collective-permute-done | bytes 131104 | tf_op jit(solution)/shard_map/ppermute | solution.py:50
  104.4 2.7 %collective-permute-done.51.refs_2_ = bf16[32,2048]{1,0:T(8,128)(2,1)S(1)} collective-permute-done((bf16[32,2048]{1,0:T(8,128)(2,1)S(1)}, bf16[32,2048]{1,0:T(8,128)(2,1)S(1)}, u32[]{:S(2)}, u32[]{:S(2)}) %collective-permute-start.51) | collective-permute-done | bytes 131104 | tf_op jit(solution)/shard_map/ppermute | solution.py:50
  107.1 0.8 shard_map.77
  (87 shorter events, 11.0 us)
Async XLA Ops:
  1.2 9.4 %collective-permute-start = (bf16[32,2176]{1,0:T(8,128)(2,1)S(1)}, bf16[32,2176]{1,0:T(8,128)(2,1)S(1)}, u32[]{:S(2)}, u32[]{:S(2)}) collective-permute-start(bf16[32,2176]{1,0:T(8,128)(2,1)S(1)} %shard_map.56.refs_1_), channel_id=1, source_target_pairs={{0,4},{1,5},{2,6},{3,7},{4,0},{5,1},{6,2},{7,3},{8,12},{9,13},{10,... | collective-permute-start | bytes 417800 | tf_op jit(solution)/shard_map/ppermute | solution.py:50
  4.3 9.1 %collective-permute-start.1 = (bf16[32,2176]{1,0:T(8,128)(2,1)S(1)}, bf16[32,2176]{1,0:T(8,128)(2,1)S(1)}, u32[]{:S(2)}, u32[]{:S(2)}) collective-permute-start(bf16[32,2176]{1,0:T(8,128)(2,1)S(1)} %shard_map.56.refs_1_), channel_id=1, source_target_pairs={{0,8},{1,9},{2,10},{3,11},{4,12},{5,13},{6,14},{7,15},{8,0},{9,1},... | collective-permute-start | bytes 417800 | tf_op jit(solution)/shard_map/ppermute | solution.py:50
  10.7 10.9 %collective-permute-start.4 = (bf16[64,2176]{1,0:T(8,128)(2,1)S(1)}, bf16[64,2176]{1,0:T(8,128)(2,1)S(1)}, u32[]{:S(2)}, u32[]{:S(2)}) collective-permute-start(bf16[64,2176]{1,0:T(8,128)(2,1)S(1)} %shard_map.57.refs_0_.refs_1_), channel_id=1, source_target_pairs={{0,2},{1,3},{2,0},{3,1},{4,6},{5,7},{6,4},{7,5},{8,10},{9,11},{10,... | collective-permute-start | bytes 835592 | tf_op jit(solution)/shard_map/ppermute | solution.py:50
  13.4 5.1 %collective-permute-start.2 = (bf16[32,2176]{1,0:T(8,128)(2,1)S(1)}, bf16[32,2176]{1,0:T(8,128)(2,1)S(1)}, u32[]{:S(2)}, u32[]{:S(2)}) collective-permute-start(bf16[32,2176]{1,0:T(8,128)(2,1)S(1)} %shard_map.58.refs_0_), channel_id=1, source_target_pairs={{0,4},{1,5},{2,6},{3,7},{4,0},{5,1},{6,2},{7,3},{8,12},{9,13},{10,... | collective-permute-start | bytes 417800 | tf_op jit(solution)/shard_map/ppermute | solution.py:50
  13.9 7.7 %collective-permute-start.3 = (bf16[32,2176]{1,0:T(8,128)(2,1)S(1)}, bf16[32,2176]{1,0:T(8,128)(2,1)S(1)}, u32[]{:S(2)}, u32[]{:S(2)}) collective-permute-start(bf16[32,2176]{1,0:T(8,128)(2,1)S(1)} %shard_map.58.refs_0_), channel_id=1, source_target_pairs={{0,2},{1,3},{2,0},{3,1},{4,6},{5,7},{6,4},{7,5},{8,10},{9,11},{10,... | collective-permute-start | bytes 417800 | tf_op jit(solution)/shard_map/ppermute | solution.py:50
  21.6 5.1 %collective-permute-start.5 = (bf16[32,2176]{1,0:T(8,128)(2,1)S(1)}, bf16[32,2176]{1,0:T(8,128)(2,1)S(1)}, u32[]{:S(2)}, u32[]{:S(2)}) collective-permute-start(bf16[32,2176]{1,0:T(8,128)(2,1)S(1)} %collective-permute-done.2.refs_1_), channel_id=1, source_target_pairs={{0,2},{1,3},{2,0},{3,1},{4,6},{5,7},{6,4},{7,5},{8,10},{9,11},{10,... | collective-permute-start | bytes 417800 | tf_op jit(solution)/shard_map/ppermute | solution.py:50
  23.1 4.0 %collective-permute-start.6 = (bf16[32,2176]{1,0:T(8,128)(2,1)S(1)}, bf16[32,2176]{1,0:T(8,128)(2,1)S(1)}, u32[]{:S(2)}, u32[]{:S(2)}) collective-permute-start(bf16[32,2176]{1,0:T(8,128)(2,1)S(1)} %shard_map.58.refs_0_), channel_id=1, source_target_pairs={{0,1},{1,0},{2,3},{3,2},{4,5},{5,4},{6,7},{7,6},{8,9},{9,8},{10,11... | collective-permute-start | bytes 417800 | tf_op jit(solution)/shard_map/ppermute | solution.py:50
  23.1 4.1 %collective-permute-start.7 = (bf16[32,2176]{1,0:T(8,128)(2,1)S(1)}, bf16[32,2176]{1,0:T(8,128)(2,1)S(1)}, u32[]{:S(2)}, u32[]{:S(2)}) collective-permute-start(bf16[32,2176]{1,0:T(8,128)(2,1)S(1)} %collective-permute-done.2.refs_1_), channel_id=1, source_target_pairs={{0,1},{1,0},{2,3},{3,2},{4,5},{5,4},{6,7},{7,6},{8,9},{9,8},{10,11... | collective-permute-start | bytes 417800 | tf_op jit(solution)/shard_map/ppermute | solution.py:50
  23.6 3.6 %collective-permute-start.8 = (bf16[32,2176]{1,0:T(8,128)(2,1)S(1)}, bf16[32,2176]{1,0:T(8,128)(2,1)S(1)}, u32[]{:S(2)}, u32[]{:S(2)}) collective-permute-start(bf16[32,2176]{1,0:T(8,128)(2,1)S(1)} %collective-permute-done.3.refs_2_), channel_id=1, source_target_pairs={{0,1},{1,0},{2,3},{3,2},{4,5},{5,4},{6,7},{7,6},{8,9},{9,8},{10,11... | collective-permute-start | bytes 417800 | tf_op jit(solution)/shard_map/ppermute | solution.py:50
  26.6 1.4 %collective-permute-start.9 = (bf16[32,2176]{1,0:T(8,128)(2,1)S(1)}, bf16[32,2176]{1,0:T(8,128)(2,1)S(1)}, u32[]{:S(2)}, u32[]{:S(2)}) collective-permute-start(bf16[32,2176]{1,0:T(8,128)(2,1)S(1)} %collective-permute-done.5.refs_3_), channel_id=1, source_target_pairs={{0,1},{1,0},{2,3},{3,2},{4,5},{5,4},{6,7},{7,6},{8,9},{9,8},{10,11... | collective-permute-start | bytes 417800 | tf_op jit(solution)/shard_map/ppermute | solution.py:50
  26.6 7.2 %collective-permute-start.12 = (bf16[64,2176]{1,0:T(8,128)(2,1)S(1)}, bf16[64,2176]{1,0:T(8,128)(2,1)S(1)}, u32[]{:S(2)}, u32[]{:S(2)}) collective-permute-start(bf16[64,2176]{1,0:T(8,128)(2,1)S(1)} %shard_map.57.refs_0_.refs_1_), channel_id=1, source_target_pairs={{0,1},{1,0},{2,3},{3,2},{4,5},{5,4},{6,7},{7,6},{8,9},{9,8},{10,11... | collective-permute-start | bytes 835592 | tf_op jit(solution)/shard_map/ppermute | solution.py:50
  27.2 6.7 %collective-permute-start.13 = (bf16[64,2176]{1,0:T(8,128)(2,1)S(1)}, bf16[64,2176]{1,0:T(8,128)(2,1)S(1)}, u32[]{:S(2)}, u32[]{:S(2)}) collective-permute-start(bf16[64,2176]{1,0:T(8,128)(2,1)S(1)} %collective-permute-done.4.refs_2_), channel_id=1, source_target_pairs={{0,1},{1,0},{2,3},{3,2},{4,5},{5,4},{6,7},{7,6},{8,9},{9,8},{10,11... | collective-permute-start | bytes 835592 | tf_op jit(solution)/shard_map/ppermute | solution.py:50
  30.6 1.4 %collective-permute-start.10 = (bf16[32,2048]{1,0:T(8,128)(2,1)S(1)}, bf16[32,2048]{1,0:T(8,128)(2,1)S(1)}, u32[]{:S(2)}, u32[]{:S(2)}) collective-permute-start(bf16[32,2048]{1,0:T(8,128)(2,1)S(1)} %get-tuple-element.58), channel_id=1, source_target_pairs={{0,1},{1,0},{2,3},{3,2},{4,5},{5,4},{6,7},{7,6},{8,9},{9,8},{10,11... | collective-permute-start | bytes 393224 | tf_op jit(solution)/shard_map/ppermute | solution.py:50
  30.8 1.4 %collective-permute-start.11 = (bf16[32,2048]{1,0:T(8,128)(2,1)S(1)}, bf16[32,2048]{1,0:T(8,128)(2,1)S(1)}, u32[]{:S(2)}, u32[]{:S(2)}) collective-permute-start(bf16[32,2048]{1,0:T(8,128)(2,1)S(1)} %get-tuple-element.59), channel_id=1, source_target_pairs={{0,1},{1,0},{2,3},{3,2},{4,5},{5,4},{6,7},{7,6},{8,9},{9,8},{10,11... | collective-permute-start | bytes 393224 | tf_op jit(solution)/shard_map/ppermute | solution.py:50
  31.2 7.1 %collective-permute-start.15 = (bf16[64,2048]{1,0:T(8,128)(2,1)S(1)}, bf16[64,2048]{1,0:T(8,128)(2,1)S(1)}, u32[]{:S(2)}, u32[]{:S(2)}) collective-permute-start(bf16[64,2048]{1,0:T(8,128)(2,1)S(1)} %get-tuple-element.65), channel_id=1, source_target_pairs={{0,1},{1,0},{2,3},{3,2},{4,5},{5,4},{6,7},{7,6},{8,9},{9,8},{10,11... | collective-permute-start | bytes 786440 | tf_op jit(solution)/shard_map/ppermute | solution.py:50
  32.3 5.8 %collective-permute-start.16 = (bf16[32,2048]{1,0:T(8,128)(2,1)S(1)}, bf16[32,2048]{1,0:T(8,128)(2,1)S(1)}, u32[]{:S(2)}, u32[]{:S(2)}) collective-permute-start(bf16[32,2048]{1,0:T(8,128)(2,1)S(1)} %get-tuple-element.60.refs_0_), channel_id=1, source_target_pairs={{0,2},{1,3},{2,0},{3,1},{4,6},{5,7},{6,4},{7,5},{8,10},{9,11},{10,... | collective-permute-start | bytes 393224 | tf_op jit(solution)/shard_map/ppermute | solution.py:50
  36.5 1.3 %collective-permute-start.18 = (bf16[16,2048]{1,0:T(8,128)(2,1)S(1)}, bf16[16,2048]{1,0:T(8,128)(2,1)S(1)}, u32[]{:S(2)}, u32[]{:S(2)}) collective-permute-start(bf16[16,2048]{1,0:T(8,128)(2,1)S(1)} %get-tuple-element.68), channel_id=1, source_target_pairs={{0,1},{1,0},{2,3},{3,2},{4,5},{5,4},{6,7},{7,6},{8,9},{9,8},{10,11... | collective-permute-start | bytes 196616 | tf_op jit(solution)/shard_map/ppermute | solution.py:50
  36.6 5.9 %collective-permute-start.17 = (bf16[32,2048]{1,0:T(8,128)(2,1)S(1)}, bf16[32,2048]{1,0:T(8,128)(2,1)S(1)}, u32[]{:S(2)}, u32[]{:S(2)}) collective-permute-start(bf16[32,2048]{1,0:T(8,128)(2,1)S(1)} %get-tuple-element.66), channel_id=1, source_target_pairs={{0,2},{1,3},{2,0},{3,1},{4,6},{5,7},{6,4},{7,5},{8,10},{9,11},{10,... | collective-permute-start | bytes 393224 | tf_op jit(solution)/shard_map/ppermute | solution.py:50
  37.1 13.3 %collective-permute-start.14 = (bf16[64,2048]{1,0:T(8,128)(2,1)S(1)}, bf16[64,2048]{1,0:T(8,128)(2,1)S(1)}, u32[]{:S(2)}, u32[]{:S(2)}) collective-permute-start(bf16[64,2048]{1,0:T(8,128)(2,1)S(1)} %get-tuple-element.63), channel_id=1, source_target_pairs={{0,1},{1,0},{2,3},{3,2},{4,5},{5,4},{6,7},{7,6},{8,9},{9,8},{10,11... | collective-permute-start | bytes 786440 | tf_op jit(solution)/shard_map/ppermute | solution.py:50
  38.1 1.4 %collective-permute-start.20 = (bf16[16,2048]{1,0:T(8,128)(2,1)S(1)}, bf16[16,2048]{1,0:T(8,128)(2,1)S(1)}, u32[]{:S(2)}, u32[]{:S(2)}) collective-permute-start(bf16[16,2048]{1,0:T(8,128)(2,1)S(1)} %get-tuple-element.70), channel_id=1, source_target_pairs={{0,1},{1,0},{2,3},{3,2},{4,5},{5,4},{6,7},{7,6},{8,9},{9,8},{10,11... | collective-permute-start | bytes 196616 | tf_op jit(solution)/shard_map/ppermute | solution.py:50
  39.1 5.6 %collective-permute-start.25 = (bf16[32,2048]{1,0:T(8,128)(2,1)S(1)}, bf16[32,2048]{1,0:T(8,128)(2,1)S(1)}, u32[]{:S(2)}, u32[]{:S(2)}) collective-permute-start(bf16[32,2048]{1,0:T(8,128)(2,1)S(1)} %shard_map.63.refs_0_), channel_id=1, source_target_pairs={{0,4},{1,5},{2,6},{3,7},{4,0},{5,1},{6,2},{7,3},{8,12},{9,13},{10,... | collective-permute-start | bytes 393224 | tf_op jit(solution)/shard_map/ppermute | solution.py:50
  42.5 6.5 %collective-permute-start.22 = (bf16[32,2048]{1,0:T(8,128)(2,1)S(1)}, bf16[32,2048]{1,0:T(8,128)(2,1)S(1)}, u32[]{:S(2)}, u32[]{:S(2)}) collective-permute-start(bf16[32,2048]{1,0:T(8,128)(2,1)S(1)} %get-tuple-element.72), channel_id=1, source_target_pairs={{0,2},{1,3},{2,0},{3,1},{4,6},{5,7},{6,4},{7,5},{8,10},{9,11},{10,... | collective-permute-start | bytes 393224 | tf_op jit(solution)/shard_map/ppermute | solution.py:50
  43.1 7.4 %collective-permute-start.23 = (bf16[32,2048]{1,0:T(8,128)(2,1)S(1)}, bf16[32,2048]{1,0:T(8,128)(2,1)S(1)}, u32[]{:S(2)}, u32[]{:S(2)}) collective-permute-start(bf16[32,2048]{1,0:T(8,128)(2,1)S(1)} %get-tuple-element.73), channel_id=1, source_target_pairs={{0,2},{1,3},{2,0},{3,1},{4,6},{5,7},{6,4},{7,5},{8,10},{9,11},{10,... | collective-permute-start | bytes 393224 | tf_op jit(solution)/shard_map/ppermute | solution.py:50
  44.7 10.2 %collective-permute-start.26 = (bf16[32,2048]{1,0:T(8,128)(2,1)S(1)}, bf16[32,2048]{1,0:T(8,128)(2,1)S(1)}, u32[]{:S(2)}, u32[]{:S(2)}) collective-permute-start(bf16[32,2048]{1,0:T(8,128)(2,1)S(1)} %shard_map.66), channel_id=1, source_target_pairs={{0,8},{1,9},{2,10},{3,11},{4,12},{5,13},{6,14},{7,15},{8,0},{9,1},... | collective-permute-start | bytes 393224 | tf_op jit(solution)/shard_map/ppermute | solution.py:50
  50.6 5.3 %collective-permute-start.24 = (bf16[32,2048]{1,0:T(8,128)(2,1)S(1)}, bf16[32,2048]{1,0:T(8,128)(2,1)S(1)}, u32[]{:S(2)}, u32[]{:S(2)}) collective-permute-start(bf16[32,2048]{1,0:T(8,128)(2,1)S(1)} %get-tuple-element.75), channel_id=1, source_target_pairs={{0,4},{1,5},{2,6},{3,7},{4,0},{5,1},{6,2},{7,3},{8,12},{9,13},{10,... | collective-permute-start | bytes 393224 | tf_op jit(solution)/shard_map/ppermute | solution.py:50
  56.1 6.1 %collective-permute-start.27 = (bf16[32,2048]{1,0:T(8,128)(2,1)S(1)}, bf16[32,2048]{1,0:T(8,128)(2,1)S(1)}, u32[]{:S(2)}, u32[]{:S(2)}) collective-permute-start(bf16[32,2048]{1,0:T(8,128)(2,1)S(1)} %get-tuple-element.77.refs_1_), channel_id=1, source_target_pairs={{0,4},{1,5},{2,6},{3,7},{4,0},{5,1},{6,2},{7,3},{8,12},{9,13},{10,... | collective-permute-start | bytes 393224 | tf_op jit(solution)/shard_map/ppermute | solution.py:50
  56.7 8.4 %collective-permute-start.28 = (bf16[32,2048]{1,0:T(8,128)(2,1)S(1)}, bf16[32,2048]{1,0:T(8,128)(2,1)S(1)}, u32[]{:S(2)}, u32[]{:S(2)}) collective-permute-start(bf16[32,2048]{1,0:T(8,128)(2,1)S(1)} %get-tuple-element.77.refs_1_), channel_id=1, source_target_pairs={{0,8},{1,9},{2,10},{3,11},{4,12},{5,13},{6,14},{7,15},{8,0},{9,1},... | collective-permute-start | bytes 393224 | tf_op jit(solution)/shard_map/ppermute | solution.py:50
  62.2 10.1 %collective-permute-start.31 = (bf16[64,2048]{1,0:T(8,128)(2,1)S(1)}, bf16[64,2048]{1,0:T(8,128)(2,1)S(1)}, u32[]{:S(2)}, u32[]{:S(2)}) collective-permute-start(bf16[64,2048]{1,0:T(8,128)(2,1)S(1)} %shard_map.68.refs_0_.refs_1_), channel_id=1, source_target_pairs={{0,2},{1,3},{2,0},{3,1},{4,6},{5,7},{6,4},{7,5},{8,10},{9,11},{10,... | collective-permute-start | bytes 786440 | tf_op jit(solution)/shard_map/ppermute | solution.py:50
  65.1 5.0 %collective-permute-start.29 = (bf16[32,2048]{1,0:T(8,128)(2,1)S(1)}, bf16[32,2048]{1,0:T(8,128)(2,1)S(1)}, u32[]{:S(2)}, u32[]{:S(2)}) collective-permute-start(bf16[32,2048]{1,0:T(8,128)(2,1)S(1)} %shard_map.69.refs_0_), channel_id=1, source_target_pairs={{0,4},{1,5},{2,6},{3,7},{4,0},{5,1},{6,2},{7,3},{8,12},{9,13},{10,... | collective-permute-start | bytes 393224 | tf_op jit(solution)/shard_map/ppermute | solution.py:50
  65.2 7.1 %collective-permute-start.30 = (bf16[32,2048]{1,0:T(8,128)(2,1)S(1)}, bf16[32,2048]{1,0:T(8,128)(2,1)S(1)}, u32[]{:S(2)}, u32[]{:S(2)}) collective-permute-start(bf16[32,2048]{1,0:T(8,128)(2,1)S(1)} %shard_map.69.refs_0_), channel_id=1, source_target_pairs={{0,2},{1,3},{2,0},{3,1},{4,6},{5,7},{6,4},{7,5},{8,10},{9,11},{10,... | collective-permute-start | bytes 393224 | tf_op jit(solution)/shard_map/ppermute | solution.py:50
  72.3 5.0 %collective-permute-start.32 = (bf16[32,2048]{1,0:T(8,128)(2,1)S(1)}, bf16[32,2048]{1,0:T(8,128)(2,1)S(1)}, u32[]{:S(2)}, u32[]{:S(2)}) collective-permute-start(bf16[32,2048]{1,0:T(8,128)(2,1)S(1)} %collective-permute-done.29.refs_1_), channel_id=1, source_target_pairs={{0,2},{1,3},{2,0},{3,1},{4,6},{5,7},{6,4},{7,5},{8,10},{9,11},{10,... | collective-permute-start | bytes 393224 | tf_op jit(solution)/shard_map/ppermute | solution.py:50
  74.3 3.5 %collective-permute-start.33 = (bf16[32,2048]{1,0:T(8,128)(2,1)S(1)}, bf16[32,2048]{1,0:T(8,128)(2,1)S(1)}, u32[]{:S(2)}, u32[]{:S(2)}) collective-permute-start(bf16[32,2048]{1,0:T(8,128)(2,1)S(1)} %shard_map.69.refs_0_), channel_id=1, source_target_pairs={{0,1},{1,0},{2,3},{3,2},{4,5},{5,4},{6,7},{7,6},{8,9},{9,8},{10,11... | collective-permute-start | bytes 393224 | tf_op jit(solution)/shard_map/ppermute | solution.py:50
  74.3 3.5 %collective-permute-start.34 = (bf16[32,2048]{1,0:T(8,128)(2,1)S(1)}, bf16[32,2048]{1,0:T(8,128)(2,1)S(1)}, u32[]{:S(2)}, u32[]{:S(2)}) collective-permute-start(bf16[32,2048]{1,0:T(8,128)(2,1)S(1)} %collective-permute-done.29.refs_1_), channel_id=1, source_target_pairs={{0,1},{1,0},{2,3},{3,2},{4,5},{5,4},{6,7},{7,6},{8,9},{9,8},{10,11... | collective-permute-start | bytes 393224 | tf_op jit(solution)/shard_map/ppermute | solution.py:50
  74.8 3.0 %collective-permute-start.35 = (bf16[32,2048]{1,0:T(8,128)(2,1)S(1)}, bf16[32,2048]{1,0:T(8,128)(2,1)S(1)}, u32[]{:S(2)}, u32[]{:S(2)}) collective-permute-start(bf16[32,2048]{1,0:T(8,128)(2,1)S(1)} %collective-permute-done.30.refs_2_), channel_id=1, source_target_pairs={{0,1},{1,0},{2,3},{3,2},{4,5},{5,4},{6,7},{7,6},{8,9},{9,8},{10,11... | collective-permute-start | bytes 393224 | tf_op jit(solution)/shard_map/ppermute | solution.py:50
  77.3 1.3 %collective-permute-start.36 = (bf16[32,2048]{1,0:T(8,128)(2,1)S(1)}, bf16[32,2048]{1,0:T(8,128)(2,1)S(1)}, u32[]{:S(2)}, u32[]{:S(2)}) collective-permute-start(bf16[32,2048]{1,0:T(8,128)(2,1)S(1)} %collective-permute-done.32.refs_3_), channel_id=1, source_target_pairs={{0,1},{1,0},{2,3},{3,2},{4,5},{5,4},{6,7},{7,6},{8,9},{9,8},{10,11... | collective-permute-start | bytes 393224 | tf_op jit(solution)/shard_map/ppermute | solution.py:50
  77.3 7.7 %collective-permute-start.39 = (bf16[64,2048]{1,0:T(8,128)(2,1)S(1)}, bf16[64,2048]{1,0:T(8,128)(2,1)S(1)}, u32[]{:S(2)}, u32[]{:S(2)}) collective-permute-start(bf16[64,2048]{1,0:T(8,128)(2,1)S(1)} %shard_map.68.refs_0_.refs_1_), channel_id=1, source_target_pairs={{0,1},{1,0},{2,3},{3,2},{4,5},{5,4},{6,7},{7,6},{8,9},{9,8},{10,11... | collective-permute-start | bytes 786440 | tf_op jit(solution)/shard_map/ppermute | solution.py:50
  77.8 7.2 %collective-permute-start.40 = (bf16[64,2048]{1,0:T(8,128)(2,1)S(1)}, bf16[64,2048]{1,0:T(8,128)(2,1)S(1)}, u32[]{:S(2)}, u32[]{:S(2)}) collective-permute-start(bf16[64,2048]{1,0:T(8,128)(2,1)S(1)} %collective-permute-done.31.refs_2_), channel_id=1, source_target_pairs={{0,1},{1,0},{2,3},{3,2},{4,5},{5,4},{6,7},{7,6},{8,9},{9,8},{10,11... | collective-permute-start | bytes 786440 | tf_op jit(solution)/shard_map/ppermute | solution.py:50
  81.2 1.4 %collective-permute-start.37 = (bf16[32,2048]{1,0:T(8,128)(2,1)S(1)}, bf16[32,2048]{1,0:T(8,128)(2,1)S(1)}, u32[]{:S(2)}, u32[]{:S(2)}) collective-permute-start(bf16[32,2048]{1,0:T(8,128)(2,1)S(1)} %get-tuple-element.83), channel_id=1, source_target_pairs={{0,1},{1,0},{2,3},{3,2},{4,5},{5,4},{6,7},{7,6},{8,9},{9,8},{10,11... | collective-permute-start | bytes 393224 | tf_op jit(solution)/shard_map/ppermute | solution.py:50
  81.5 1.4 %collective-permute-start.38 = (bf16[32,2048]{1,0:T(8,128)(2,1)S(1)}, bf16[32,2048]{1,0:T(8,128)(2,1)S(1)}, u32[]{:S(2)}, u32[]{:S(2)}) collective-permute-start(bf16[32,2048]{1,0:T(8,128)(2,1)S(1)} %get-tuple-element.84), channel_id=1, source_target_pairs={{0,1},{1,0},{2,3},{3,2},{4,5},{5,4},{6,7},{7,6},{8,9},{9,8},{10,11... | collective-permute-start | bytes 393224 | tf_op jit(solution)/shard_map/ppermute | solution.py:50
  81.8 7.3 %collective-permute-start.42 = (bf16[64,2048]{1,0:T(8,128)(2,1)S(1)}, bf16[64,2048]{1,0:T(8,128)(2,1)S(1)}, u32[]{:S(2)}, u32[]{:S(2)}) collective-permute-start(bf16[64,2048]{1,0:T(8,128)(2,1)S(1)} %get-tuple-element.90), channel_id=1, source_target_pairs={{0,1},{1,0},{2,3},{3,2},{4,5},{5,4},{6,7},{7,6},{8,9},{9,8},{10,11... | collective-permute-start | bytes 786440 | tf_op jit(solution)/shard_map/ppermute | solution.py:50
  82.9 6.6 %collective-permute-start.43 = (bf16[32,2048]{1,0:T(8,128)(2,1)S(1)}, bf16[32,2048]{1,0:T(8,128)(2,1)S(1)}, u32[]{:S(2)}, u32[]{:S(2)}) collective-permute-start(bf16[32,2048]{1,0:T(8,128)(2,1)S(1)} %get-tuple-element.85.refs_0_), channel_id=1, source_target_pairs={{0,2},{1,3},{2,0},{3,1},{4,6},{5,7},{6,4},{7,5},{8,10},{9,11},{10,... | collective-permute-start | bytes 393224 | tf_op jit(solution)/shard_map/ppermute | solution.py:50
  87.7 5.9 %collective-permute-start.44 = (bf16[32,2048]{1,0:T(8,128)(2,1)S(1)}, bf16[32,2048]{1,0:T(8,128)(2,1)S(1)}, u32[]{:S(2)}, u32[]{:S(2)}) collective-permute-start(bf16[32,2048]{1,0:T(8,128)(2,1)S(1)} %get-tuple-element.91), channel_id=1, source_target_pairs={{0,2},{1,3},{2,0},{3,1},{4,6},{5,7},{6,4},{7,5},{8,10},{9,11},{10,... | collective-permute-start | bytes 393224 | tf_op jit(solution)/shard_map/ppermute | solution.py:50
  88.0 8.9 %collective-permute-start.41 = (bf16[64,2048]{1,0:T(8,128)(2,1)S(1)}, bf16[64,2048]{1,0:T(8,128)(2,1)S(1)}, u32[]{:S(2)}, u32[]{:S(2)}) collective-permute-start(bf16[64,2048]{1,0:T(8,128)(2,1)S(1)} %get-tuple-element.88), channel_id=1, source_target_pairs={{0,1},{1,0},{2,3},{3,2},{4,5},{5,4},{6,7},{7,6},{8,9},{9,8},{10,11... | collective-permute-start | bytes 786440 | tf_op jit(solution)/shard_map/ppermute | solution.py:50
  90.2 5.6 %collective-permute-start.52 = (bf16[32,2048]{1,0:T(8,128)(2,1)S(1)}, bf16[32,2048]{1,0:T(8,128)(2,1)S(1)}, u32[]{:S(2)}, u32[]{:S(2)}) collective-permute-start(bf16[32,2048]{1,0:T(8,128)(2,1)S(1)} %shard_map.73.refs_0_), channel_id=1, source_target_pairs={{0,4},{1,5},{2,6},{3,7},{4,0},{5,1},{6,2},{7,3},{8,12},{9,13},{10,... | collective-permute-start | bytes 393224 | tf_op jit(solution)/shard_map/ppermute | solution.py:50
  93.7 6.5 %collective-permute-start.49 = (bf16[32,2048]{1,0:T(8,128)(2,1)S(1)}, bf16[32,2048]{1,0:T(8,128)(2,1)S(1)}, u32[]{:S(2)}, u32[]{:S(2)}) collective-permute-start(bf16[32,2048]{1,0:T(8,128)(2,1)S(1)} %get-tuple-element.97), channel_id=1, source_target_pairs={{0,2},{1,3},{2,0},{3,1},{4,6},{5,7},{6,4},{7,5},{8,10},{9,11},{10,... | collective-permute-start | bytes 393224 | tf_op jit(solution)/shard_map/ppermute | solution.py:50
  94.0 7.6 %collective-permute-start.50 = (bf16[32,2048]{1,0:T(8,128)(2,1)S(1)}, bf16[32,2048]{1,0:T(8,128)(2,1)S(1)}, u32[]{:S(2)}, u32[]{:S(2)}) collective-permute-start(bf16[32,2048]{1,0:T(8,128)(2,1)S(1)} %get-tuple-element.98), channel_id=1, source_target_pairs={{0,2},{1,3},{2,0},{3,1},{4,6},{5,7},{6,4},{7,5},{8,10},{9,11},{10,... | collective-permute-start | bytes 393224 | tf_op jit(solution)/shard_map/ppermute | solution.py:50
  95.8 8.6 %collective-permute-start.53 = (bf16[32,2048]{1,0:T(8,128)(2,1)S(1)}, bf16[32,2048]{1,0:T(8,128)(2,1)S(1)}, u32[]{:S(2)}, u32[]{:S(2)}) collective-permute-start(bf16[32,2048]{1,0:T(8,128)(2,1)S(1)} %shard_map.76), channel_id=1, source_target_pairs={{0,8},{1,9},{2,10},{3,11},{4,12},{5,13},{6,14},{7,15},{8,0},{9,1},... | collective-permute-start | bytes 393224 | tf_op jit(solution)/shard_map/ppermute | solution.py:50
  101.7 5.4 %collective-permute-start.51 = (bf16[32,2048]{1,0:T(8,128)(2,1)S(1)}, bf16[32,2048]{1,0:T(8,128)(2,1)S(1)}, u32[]{:S(2)}, u32[]{:S(2)}) collective-permute-start(bf16[32,2048]{1,0:T(8,128)(2,1)S(1)} %get-tuple-element.100), channel_id=1, source_target_pairs={{0,4},{1,5},{2,6},{3,7},{4,0},{5,1},{6,2},{7,3},{8,12},{9,13},{10,... | collective-permute-start | bytes 393224 | tf_op jit(solution)/shard_map/ppermute | solution.py:50
  (8 other events, 18.3 us)

commit v11 on v10

--- a/solution.py
+++ b/solution.py
@@ -86,12 +86,13 @@
 
 
 def apart_kernel(first, count, mine, near, *refs):
-    beside, pieces = refs[:count], refs[count:]
+    beside, pieces = refs[:-count], refs[-count:]
     rows = pieces[0].shape[0]
-    for k in range(count):
+    for k, piece in enumerate(pieces):
         span = slice((first + k) * rows, (first + k + 1) * rows)
-        total = mine[span] + near[span].astype(f32) + beside[k][...].astype(f32)
-        pieces[k][...] = total.astype(pieces[k].dtype)
+        part = beside[k][...] if len(beside) == count else beside[0][span]
+        total = mine[span] + near[span].astype(f32) + part.astype(f32)
+        piece[...] = total.astype(piece.dtype)
 
 
 def cross_kernel(mine, near, beside, *refs):
@@ -122,7 +123,7 @@
 def cross_rows(mine, near, beside):
     far, count = lax.axis_size("expert") // 4, len(beside)
     shape = beside[0].shape
-    hops, arrived = [], []
+    arrived = []
     if count > 1:
         hops = call(
             functools.partial(apart_kernel, 1, count - 1),
@@ -136,7 +137,7 @@
     (crossing,) = call(
         cross_kernel, [(shape, bf16)], [VMEM] * (3 + len(arrived)), mine, near, beside[0], *arrived
     )
-    return swap(crossing, 4, count, far, True), tuple(hops[-1:])
+    return swap(crossing, 4, count, far, True)
 
 
 def normed_rows(widened, gain_row):
@@ -272,7 +273,7 @@
             first += out.shape[0]
 
 
-def run_expert(parts, routed, first_column, weights, cuts, after):
+def run_expert(parts, routed, first_column, weights, after):
     gate_up, down_proj, _ = weights
     hidden_size, features = down_proj.shape
     width = parts[0].shape[1]
@@ -280,7 +281,7 @@
     quarter = count // 4
     wide = routed is None
     outs = [((quarter, features), f32)] * 2 + [((quarter, features), bf16)]
-    outs += [((quarter // cuts, features), bf16)] * cuts
+    outs += [((quarter // 2, features), bf16)] * 2
     if wide:
         outs = outs + [((count, width - features), bf16)]
     found = call(
@@ -295,7 +296,7 @@
         limit=24,
         after=after,
     )
-    return found[: 3 + cuts], found[3 + cuts] if wide else routed
+    return found[:5], found[5] if wide else routed
 
 
 def in_hbm(array):
@@ -338,25 +339,28 @@
     for piece in second[1:]:
         second_beside.append(swap(held(piece, (second_beside[0], first_beside)), 2, 1, 2))
 
-    def worked(near, beside, routed, cuts, after):
+    def worked(near, beside, routed, after):
         parts = near + beside
         parts += [swap(piece, 1, 1, 2) for piece in parts]
-        return run_expert(parts, routed, first_column, weights, cuts, after)
-
-    outs, second_columns = worked(second, second_beside, routed[1], 2, ())
-    mine, near, leaving = leave_pair(outs, half, ())
-    back = [swap(piece, 2, 1, 2, True) for piece in leaving]
-    crossed_back, hopped = cross_rows(mine, near, back)
-    outs, first_columns = worked([first], [first_beside], routed[0], 4, tuple(leaving[-1:]))
-    mine, near, leaving = leave_pair(outs, half, (*hopped, back[0]))
-    back = [swap(piece, 2, 1, 2, True) for piece in leaving]
+        return run_expert(parts, routed, first_column, weights, after)
+
+    first_beside = held(first_beside, (second[-1], second_beside[0]))
+    outs, first_columns = worked([first], [first_beside], routed[0], (second[-1],))
+    mine1, near1, leaving1 = leave_pair(outs, 1, ())
+    second_beside[-1] = held(second_beside[-1], outs[0])
+    outs, second_columns = worked(second, second_beside, routed[1], tuple(leaving1))
+    mine2, near2, leaving2 = leave_pair(outs, half, ())
+    back2 = [swap(piece, 2, 1, 2, True) for piece in leaving2]
+    back1 = [swap(held(piece, back2[0]), 2, 1, 2, True) for piece in leaving1]
+    crossed_back = cross_rows(mine2, near2, back2)
     pieces = call(
         functools.partial(apart_kernel, 0, half),
-        [(rows.shape[:1] + mine.shape[1:], bf16 if k else f32) for k in range(half)],
-        [VMEM] * (2 + half),
-        mine,
-        near,
-        *back,
+        [(rows.shape[:1] + mine1.shape[1:], bf16 if k else f32) for k in range(half)],
+        [VMEM] * (2 + len(back1)),
+        mine1,
+        near1,
+        *back1,
+        after=tuple(leaving2),
     )
     arrived = [swap(piece, 4, k, far, True) if k else piece for k, piece in enumerate(pieces)]
     return [*arrived, crossed_back], [first_columns, second_columns], (outs[0],)

time: 108 us -> 106 us (0.981)
  starting transfers between devices: 38.6 us -> 34.7 us
  waiting for transfers between devices: 48.3 us -> 50 us
    ppermute x54 -> x48, starting transfers between devices: 38.6 us -> 34.7 us  [swap(): lax.ppermute(value, 'expert', [(i, partner(i)) for i in range(count)])]
    ppermute x54 -> x48, waiting for transfers between devices: 48.3 us -> 50 us  [swap(): lax.ppermute(value, 'expert', [(i, partner(i)) for i in range(count)])]
  transfers between devices with their start and end apart: 54 -> 48, of which waited for: 31 -> 26; matrix products, arithmetic and copies ran while one was open for 0% -> 0% of each run, Pallas kernels for 17% -> 13%
where the time goes in v11:
time: 106 us
  waiting for transfers between devices  50 us (47%)
  starting transfers between devices  34.7 us (33%)
  Pallas kernels  20.8 us (20%)
    ppermute x48, waiting for transfers between devices, swap(): lax.ppermute(value, 'expert', [(i, partner(i)) for i in range(count)])  50 us
    ppermute x48, starting transfers between devices, swap(): lax.ppermute(value, 'expert', [(i, partner(i)) for i in range(count)])  34.7 us
    pallas_call x23, Pallas kernels, call(): pl.pallas_call(lambda *refs: kernel(*refs[len(after):]), out_shape=shapes...  20.8 us
  transfers between devices with their start and end apart: 48, of which 26 were waited for; matrix products, arithmetic and copies ran while one was open for 0% of the time, Pallas kernels for 13%

profile of v11, /device:TPU:0, one launch (start us, length us, event | category | flops | bytes accessed | tf_op | source)
XLA Modules:
  0.0 105.8 jit_solution(112941645089606648)
XLA Ops:
  0.0 1.2 %shard_map.56.refs_1_ = bf16[32,2176]{1,0:T(8,128)(2,1)S(1)} custom-call(bf16[32,2048]{1,0:T(8,128)(2,1)} %bitcast.2, s32[2,2,8,16]{3,2,1,0:T(8,128)} %bitcast.4, f32[2,2048]{1,0:T(2,128)} %refs_2_.5), custom_call_target="tpu_custom_call" | custom-call | tf_op jit(solution)/shard_map/pallas_call | solution.py:28
  1.2 3.1 %collective-permute-start = (bf16[32,2176]{1,0:T(8,128)(2,1)S(1)}, bf16[32,2176]{1,0:T(8,128)(2,1)S(1)}, u32[]{:S(2)}, u32[]{:S(2)}) collective-permute-start(bf16[32,2176]{1,0:T(8,128)(2,1)S(1)} %shard_map.56.refs_1_), channel_id=1, source_target_pairs={{0,4},{1,5},{2,6},{3,7},{4,0},{5,1},{6,2},{7,3},{8,12},{9,13},{10,... | collective-permute-start | bytes 417800 | tf_op jit(solution)/shard_map/ppermute | solution.py:50
  4.3 2.6 %collective-permute-start.1 = (bf16[32,2176]{1,0:T(8,128)(2,1)S(1)}, bf16[32,2176]{1,0:T(8,128)(2,1)S(1)}, u32[]{:S(2)}, u32[]{:S(2)}) collective-permute-start(bf16[32,2176]{1,0:T(8,128)(2,1)S(1)} %shard_map.56.refs_1_), channel_id=1, source_target_pairs={{0,8},{1,9},{2,10},{3,11},{4,12},{5,13},{6,14},{7,15},{8,0},{9,1},... | collective-permute-start | bytes 417800 | tf_op jit(solution)/shard_map/ppermute | solution.py:50
  6.9 3.7 %shard_map.55 = (bf16[2048,1536]{1,0:T(8,128)(2,1)S(1)}, bf16[768,2048]{1,0:T(8,128)(2,1)S(1)}, f32[8,128]{1,0:T(8,128)S(1)}) custom-call(bf16[2,1,2048,1536]{3,2,1,0:T(8,128)(2,1)} %refs_1_.3, bf16[2,1,768,2048]{3,2,1,0:T(8,128)(2,1)} %refs_2_.4), custom_call_target="tpu_custom_call" | custom-call | tf_op jit(solution)/shard_map/pallas_call | solution.py:28
  10.7 1.6 %collective-permute-start.3 = (bf16[64,2176]{1,0:T(8,128)(2,1)S(1)}, bf16[64,2176]{1,0:T(8,128)(2,1)S(1)}, u32[]{:S(2)}, u32[]{:S(2)}) collective-permute-start(bf16[64,2176]{1,0:T(8,128)(2,1)S(1)} %shard_map.57.refs_0_.refs_1_), channel_id=1, source_target_pairs={{0,2},{1,3},{2,0},{3,1},{4,6},{5,7},{6,4},{7,5},{8,10},{9,11},{10,... | collective-permute-start | bytes 835592 | tf_op jit(solution)/shard_map/ppermute | solution.py:50
  12.3 1.1 %collective-permute-done.1.refs_1_ = bf16[32,2176]{1,0:T(8,128)(2,1)S(1)} collective-permute-done((bf16[32,2176]{1,0:T(8,128)(2,1)S(1)}, bf16[32,2176]{1,0:T(8,128)(2,1)S(1)}, u32[]{:S(2)}, u32[]{:S(2)}) %collective-permute-start.1) | collective-permute-done | bytes 139296 | tf_op jit(solution)/shard_map/ppermute | solution.py:50
  13.4 1.6 %collective-permute-start.4 = (bf16[32,2176]{1,0:T(8,128)(2,1)S(1)}, bf16[32,2176]{1,0:T(8,128)(2,1)S(1)}, u32[]{:S(2)}, u32[]{:S(2)}) collective-permute-start(bf16[32,2176]{1,0:T(8,128)(2,1)S(1)} %shard_map.58.refs_1_), channel_id=1, source_target_pairs={{0,2},{1,3},{2,0},{3,1},{4,6},{5,7},{6,4},{7,5},{8,10},{9,11},{10,... | collective-permute-start | bytes 417800 | tf_op jit(solution)/shard_map/ppermute | solution.py:50
  15.4 6.2 %collective-permute-done.4.refs_3_ = bf16[32,2176]{1,0:T(8,128)(2,1)S(1)} collective-permute-done((bf16[32,2176]{1,0:T(8,128)(2,1)S(1)}, bf16[32,2176]{1,0:T(8,128)(2,1)S(1)}, u32[]{:S(2)}, u32[]{:S(2)}) %collective-permute-start.4) | collective-permute-done | bytes 139296 | tf_op jit(solution)/shard_map/ppermute | solution.py:50
  21.6 1.6 %collective-permute-start.9 = (bf16[32,2176]{1,0:T(8,128)(2,1)S(1)}, bf16[32,2176]{1,0:T(8,128)(2,1)S(1)}, u32[]{:S(2)}, u32[]{:S(2)}) collective-permute-start(bf16[32,2176]{1,0:T(8,128)(2,1)S(1)} %collective-permute-done.2.refs_0_.refs_2_), channel_id=1, source_target_pairs={{0,2},{1,3},{2,0},{3,1},{4,6},{5,7},{6,4},{7,5},{8,10},{9,11},{10,... | collective-permute-start | bytes 417800 | tf_op jit(solution)/shard_map/ppermute | solution.py:50
  23.2 2.6 %shard_map.59 = (f32[64,2048]{1,0:T(8,128)S(1)}, f32[64,2048]{1,0:T(8,128)S(1)}, bf16[64,2048]{1,0:T(8,128)(2,1)S(1)}, bf16[32,2048]{1,0:T(8,128)(2,1)S(1)}, bf1...) custom-call(bf16[32,2176]{1,0:T(8,128)(2,1)S(1)} %collective-permute-done.2.refs_0_.refs_2_, ...), custom_call_target="tpu_custom_call" | custom-call | tf_op jit(solution)/shard_map/pallas_call | solution.py:28
  26.9 0.8 collective-permute-done.9.refs_4_
  28.2 1.0 collective-permute-done.8.refs_2_
  29.3 2.6 %shard_map.61 = (f32[64,2048]{1,0:T(8,128)S(1)}, f32[64,2048]{1,0:T(8,128)S(1)}, bf16[64,2048]{1,0:T(8,128)(2,1)S(1)}, bf16[32,2048]{1,0:T(8,128)(2,1)S(1)}, bf1...) custom-call(bf16[64,2048]{1,0:T(8,128)(2,1)S(1)} %shard_map.60.refs_0_, bf16[32,2176]{1,0:T(8,128)(2,1)S(1)} %shard_map.58.refs_1_, ...), custom_call_target="tpu_custom_call" | custom-call | tf_op jit(solution)/shard_map/pallas_call | solution.py:28
  32.9 0.5 collective-permute-done.14.refs_1_
  33.7 1.6 %collective-permute-start.17 = (bf16[32,2048]{1,0:T(8,128)(2,1)S(1)}, bf16[32,2048]{1,0:T(8,128)(2,1)S(1)}, u32[]{:S(2)}, u32[]{:S(2)}) collective-permute-start(bf16[32,2048]{1,0:T(8,128)(2,1)S(1)} %get-tuple-element.66.refs_0_), channel_id=1, source_target_pairs={{0,2},{1,3},{2,0},{3,1},{4,6},{5,7},{6,4},{7,5},{8,10},{9,11},{10,... | collective-permute-start | bytes 393224 | tf_op jit(solution)/shard_map/ppermute | solution.py:50
  35.8 4.3 %collective-permute-done.17.refs_2_ = bf16[32,2048]{1,0:T(8,128)(2,1)S(1)} collective-permute-done((bf16[32,2048]{1,0:T(8,128)(2,1)S(1)}, bf16[32,2048]{1,0:T(8,128)(2,1)S(1)}, u32[]{:S(2)}, u32[]{:S(2)}) %collective-permute-start.17) | collective-permute-done | bytes 131104 | tf_op jit(solution)/shard_map/ppermute | solution.py:50
  40.1 1.5 %collective-permute-start.18 = (bf16[64,2048]{1,0:T(8,128)(2,1)S(1)}, bf16[64,2048]{1,0:T(8,128)(2,1)S(1)}, u32[]{:S(2)}, u32[]{:S(2)}) collective-permute-start(bf16[64,2048]{1,0:T(8,128)(2,1)S(1)} %shard_map.60.refs_0_), channel_id=1, source_target_pairs={{0,2},{1,3},{2,0},{3,1},{4,6},{5,7},{6,4},{7,5},{8,10},{9,11},{10,... | collective-permute-start | bytes 786440 | tf_op jit(solution)/shard_map/ppermute | solution.py:50
  41.7 1.3 %collective-permute-done.21.refs_2_ = bf16[32,2048]{1,0:T(8,128)(2,1)S(1)} collective-permute-done((bf16[32,2048]{1,0:T(8,128)(2,1)S(1)}, bf16[32,2048]{1,0:T(8,128)(2,1)S(1)}, u32[]{:S(2)}, u32[]{:S(2)}) %collective-permute-start.21) | collective-permute-done | bytes 131104 | tf_op jit(solution)/shard_map/ppermute | solution.py:50
  43.5 4.5 %collective-permute-done.22.refs_3_ = bf16[32,2048]{1,0:T(8,128)(2,1)S(1)} collective-permute-done((bf16[32,2048]{1,0:T(8,128)(2,1)S(1)}, bf16[32,2048]{1,0:T(8,128)(2,1)S(1)}, u32[]{:S(2)}, u32[]{:S(2)}) %collective-permute-start.22) | collective-permute-done | bytes 131104 | tf_op jit(solution)/shard_map/ppermute | solution.py:50
  48.1 1.1 %collective-permute-start.23 = (bf16[32,2048]{1,0:T(8,128)(2,1)S(1)}, bf16[32,2048]{1,0:T(8,128)(2,1)S(1)}, u32[]{:S(2)}, u32[]{:S(2)}) collective-permute-start(bf16[32,2048]{1,0:T(8,128)(2,1)S(1)} %shard_map.66), channel_id=1, source_target_pairs={{0,8},{1,9},{2,10},{3,11},{4,12},{5,13},{6,14},{7,15},{8,0},{9,1},... | collective-permute-start | bytes 393224 | tf_op jit(solution)/shard_map/ppermute | solution.py:50
  49.4 2.1 %collective-permute-start.19 = (bf16[32,2048]{1,0:T(8,128)(2,1)S(1)}, bf16[32,2048]{1,0:T(8,128)(2,1)S(1)}, u32[]{:S(2)}, u32[]{:S(2)}) collective-permute-start(bf16[32,2048]{1,0:T(8,128)(2,1)S(1)} %get-tuple-element.71), channel_id=1, source_target_pairs={{0,4},{1,5},{2,6},{3,7},{4,0},{5,1},{6,2},{7,3},{8,12},{9,13},{10,... | collective-permute-start | bytes 393224 | tf_op jit(solution)/shard_map/ppermute | solution.py:50
  51.4 3.7 %shard_map.62 = (bf16[2048,1536]{1,0:T(8,128)(2,1)S(1)}, bf16[768,2048]{1,0:T(8,128)(2,1)S(1)}, f32[8,128]{1,0:T(8,128)S(1)}) custom-call(f32[64,2048]{1,0:T(8,128)S(1)} %get-tuple-element.61.refs_0_, bf16[2,1,2048,1536]{3,2,1,0:T(8,128)(2,1)} %refs_1_.3, bf16[2,1,768,2048]{3,2,1,0:T(8,128)(2,1)} %refs_2_.4), custom_call_target="tpu_custom_call" | custom-call | tf_op jit(solution)/shard_map/pallas_call | solution.py:28
  55.4 0.6 collective-permute-done.19.refs_4_
  56.2 1.2 %collective-permute-start.24 = (bf16[32,2048]{1,0:T(8,128)(2,1)S(1)}, bf16[32,2048]{1,0:T(8,128)(2,1)S(1)}, u32[]{:S(2)}, u32[]{:S(2)}) collective-permute-start(bf16[32,2048]{1,0:T(8,128)(2,1)S(1)} %get-tuple-element.74.refs_1_), channel_id=1, source_target_pairs={{0,4},{1,5},{2,6},{3,7},{4,0},{5,1},{6,2},{7,3},{8,12},{9,13},{10,... | collective-permute-start | bytes 393224 | tf_op jit(solution)/shard_map/ppermute | solution.py:50
  57.4 1.0 collective-permute-start.25
  58.4 2.9 %collective-permute-done.24.refs_2_ = bf16[32,2048]{1,0:T(8,128)(2,1)S(1)} collective-permute-done((bf16[32,2048]{1,0:T(8,128)(2,1)S(1)}, bf16[32,2048]{1,0:T(8,128)(2,1)S(1)}, u32[]{:S(2)}, u32[]{:S(2)}) %collective-permute-start.24) | collective-permute-done | bytes 131104 | tf_op jit(solution)/shard_map/ppermute | solution.py:50
  61.3 1.6 %collective-permute-start.27 = (bf16[64,2048]{1,0:T(8,128)(2,1)S(1)}, bf16[64,2048]{1,0:T(8,128)(2,1)S(1)}, u32[]{:S(2)}, u32[]{:S(2)}) collective-permute-start(bf16[64,2048]{1,0:T(8,128)(2,1)S(1)} %shard_map.68.refs_0_.refs_1_), channel_id=1, source_target_pairs={{0,2},{1,3},{2,0},{3,1},{4,6},{5,7},{6,4},{7,5},{8,10},{9,11},{10,... | collective-permute-start | bytes 786440 | tf_op jit(solution)/shard_map/ppermute | solution.py:50
  62.9 1.9 %collective-permute-done.25.refs_1_ = bf16[32,2048]{1,0:T(8,128)(2,1)S(1)} collective-permute-done((bf16[32,2048]{1,0:T(8,128)(2,1)S(1)}, bf16[32,2048]{1,0:T(8,128)(2,1)S(1)}, u32[]{:S(2)}, u32[]{:S(2)}) %collective-permute-start.25) | collective-permute-done | bytes 131104 | tf_op jit(solution)/shard_map/ppermute | solution.py:50
  64.8 1.4 %collective-permute-start.28 = (bf16[32,2048]{1,0:T(8,128)(2,1)S(1)}, bf16[32,2048]{1,0:T(8,128)(2,1)S(1)}, u32[]{:S(2)}, u32[]{:S(2)}) collective-permute-start(bf16[32,2048]{1,0:T(8,128)(2,1)S(1)} %shard_map.69.refs_1_), channel_id=1, source_target_pairs={{0,2},{1,3},{2,0},{3,1},{4,6},{5,7},{6,4},{7,5},{8,10},{9,11},{10,... | collective-permute-start | bytes 393224 | tf_op jit(solution)/shard_map/ppermute | solution.py:50
  66.2 0.6 collective-permute-start.26
  66.9 3.0 %collective-permute-done.28.refs_3_ = bf16[32,2048]{1,0:T(8,128)(2,1)S(1)} collective-permute-done((bf16[32,2048]{1,0:T(8,128)(2,1)S(1)}, bf16[32,2048]{1,0:T(8,128)(2,1)S(1)}, u32[]{:S(2)}, u32[]{:S(2)}) %collective-permute-start.28) | collective-permute-done | bytes 131104 | tf_op jit(solution)/shard_map/ppermute | solution.py:50
  69.8 1.4 %collective-permute-done.26.refs_0_.refs_2_ = bf16[32,2048]{1,0:T(8,128)(2,1)S(1)} collective-permute-done((bf16[32,2048]{1,0:T(8,128)(2,1)S(1)}, bf16[32,2048]{1,0:T(8,128)(2,1)S(1)}, u32[]{:S(2)}, u32[]{:S(2)}) %collective-permute-start.26) | collective-permute-done | bytes 131104 | tf_op jit(solution)/shard_map/ppermute | solution.py:50
  71.2 0.6 collective-permute-start.33
  71.9 0.9 collective-permute-done.30.refs_4_
  72.8 2.6 %shard_map.70 = (f32[64,2048]{1,0:T(8,128)S(1)}, f32[64,2048]{1,0:T(8,128)S(1)}, bf16[64,2048]{1,0:T(8,128)(2,1)S(1)}, bf16[32,2048]{1,0:T(8,128)(2,1)S(1)}, bf16[32,2048]{1,0:T(8,128)(2,1)S(1)}) custom-call(bf16[32,2048]{1,0:T(8,128)(2,1)S(1)} %collective-permute-done.26.refs_0_.refs_2_, bf16[64,2048]{1,0:T(8,128)(2,1)S(1)} %shard_map.68.refs_0_.refs_1_, ...), custom_call_target="tpu_custom_call" | custom-call | tf_op jit(solution)/shard_map/pallas_call | solution.py:28
  76.5 0.7 collective-permute-done.33.refs_4_
  77.6 0.8 collective-permute-done.32.refs_2_
  78.7 2.6 %shard_map.72 = (f32[64,2048]{1,0:T(8,128)S(1)}, f32[64,2048]{1,0:T(8,128)S(1)}, bf16[64,2048]{1,0:T(8,128)(2,1)S(1)}, bf16[32,2048]{1,0:T(8,128)(2,1)S(1)}, bf16[32,2048]{1,0:T(8,128)(2,1)S(1)}) custom-call(bf16[64,2048]{1,0:T(8,128)(2,1)S(1)} %shard_map.71.refs_0_, bf16[32,2048]{1,0:T(8,128)(2,1)S(1)} %shard_map.69.refs_1_, ...), custom_call_target="tpu_custom_call" | custom-call | tf_op jit(solution)/shard_map/pallas_call | solution.py:28
  83.1 0.7 collective-permute-start.41
  83.8 1.4 %collective-permute-start.45 = (bf16[32,2048]{1,0:T(8,128)(2,1)S(1)}, bf16[32,2048]{1,0:T(8,128)(2,1)S(1)}, u32[]{:S(2)}, u32[]{:S(2)}) collective-permute-start(bf16[32,2048]{1,0:T(8,128)(2,1)S(1)} %get-tuple-element.90.refs_1_), channel_id=1, source_target_pairs={{0,2},{1,3},{2,0},{3,1},{4,6},{5,7},{6,4},{7,5},{8,10},{9,11},{10,... | collective-permute-start | bytes 393224 | tf_op jit(solution)/shard_map/ppermute | solution.py:50
  85.2 4.3 %collective-permute-done.41.refs_2_ = bf16[32,2048]{1,0:T(8,128)(2,1)S(1)} collective-permute-done((bf16[32,2048]{1,0:T(8,128)(2,1)S(1)}, bf16[32,2048]{1,0:T(8,128)(2,1)S(1)}, u32[]{:S(2)}, u32[]{:S(2)}) %collective-permute-start.41) | collective-permute-done | bytes 131104 | tf_op jit(solution)/shard_map/ppermute | solution.py:50
  89.5 0.6 collective-permute-start.42
  90.1 2.2 %collective-permute-done.45.refs_2_ = bf16[32,2048]{1,0:T(8,128)(2,1)S(1)} collective-permute-done((bf16[32,2048]{1,0:T(8,128)(2,1)S(1)}, bf16[32,2048]{1,0:T(8,128)(2,1)S(1)}, u32[]{:S(2)}, u32[]{:S(2)}) %collective-permute-start.45) | collective-permute-done | bytes 131104 | tf_op jit(solution)/shard_map/ppermute | solution.py:50
  92.3 0.7 collective-permute-start.46
  93.0 4.3 %collective-permute-done.46.refs_3_ = bf16[32,2048]{1,0:T(8,128)(2,1)S(1)} collective-permute-done((bf16[32,2048]{1,0:T(8,128)(2,1)S(1)}, bf16[32,2048]{1,0:T(8,128)(2,1)S(1)}, u32[]{:S(2)}, u32[]{:S(2)}) %collective-permute-start.46) | collective-permute-done | bytes 131104 | tf_op jit(solution)/shard_map/ppermute | solution.py:50
  97.4 1.2 %collective-permute-start.47 = (bf16[32,2048]{1,0:T(8,128)(2,1)S(1)}, bf16[32,2048]{1,0:T(8,128)(2,1)S(1)}, u32[]{:S(2)}, u32[]{:S(2)}) collective-permute-start(bf16[32,2048]{1,0:T(8,128)(2,1)S(1)} %shard_map.76), channel_id=1, source_target_pairs={{0,8},{1,9},{2,10},{3,11},{4,12},{5,13},{6,14},{7,15},{8,0},{9,1},... | collective-permute-start | bytes 393224 | tf_op jit(solution)/shard_map/ppermute | solution.py:50
  99.1 5.8 %collective-permute-done.47.refs_3_ = bf16[32,2048]{1,0:T(8,128)(2,1)S(1)} collective-permute-done((bf16[32,2048]{1,0:T(8,128)(2,1)S(1)}, bf16[32,2048]{1,0:T(8,128)(2,1)S(1)}, u32[]{:S(2)}, u32[]{:S(2)}) %collective-permute-start.47) | collective-permute-done | bytes 131104 | tf_op jit(solution)/shard_map/ppermute | solution.py:50
  105.0 0.8 shard_map.77
  (75 shorter events, 9.4 us)
Async XLA Ops:
  1.2 9.4 %collective-permute-start = (bf16[32,2176]{1,0:T(8,128)(2,1)S(1)}, bf16[32,2176]{1,0:T(8,128)(2,1)S(1)}, u32[]{:S(2)}, u32[]{:S(2)}) collective-permute-start(bf16[32,2176]{1,0:T(8,128)(2,1)S(1)} %shard_map.56.refs_1_), channel_id=1, source_target_pairs={{0,4},{1,5},{2,6},{3,7},{4,0},{5,1},{6,2},{7,3},{8,12},{9,13},{10,... | collective-permute-start | bytes 417800 | tf_op jit(solution)/shard_map/ppermute | solution.py:50
  4.3 9.1 %collective-permute-start.1 = (bf16[32,2176]{1,0:T(8,128)(2,1)S(1)}, bf16[32,2176]{1,0:T(8,128)(2,1)S(1)}, u32[]{:S(2)}, u32[]{:S(2)}) collective-permute-start(bf16[32,2176]{1,0:T(8,128)(2,1)S(1)} %shard_map.56.refs_1_), channel_id=1, source_target_pairs={{0,8},{1,9},{2,10},{3,11},{4,12},{5,13},{6,14},{7,15},{8,0},{9,1},... | collective-permute-start | bytes 417800 | tf_op jit(solution)/shard_map/ppermute | solution.py:50
  10.7 10.9 %collective-permute-start.3 = (bf16[64,2176]{1,0:T(8,128)(2,1)S(1)}, bf16[64,2176]{1,0:T(8,128)(2,1)S(1)}, u32[]{:S(2)}, u32[]{:S(2)}) collective-permute-start(bf16[64,2176]{1,0:T(8,128)(2,1)S(1)} %shard_map.57.refs_0_.refs_1_), channel_id=1, source_target_pairs={{0,2},{1,3},{2,0},{3,1},{4,6},{5,7},{6,4},{7,5},{8,10},{9,11},{10,... | collective-permute-start | bytes 835592 | tf_op jit(solution)/shard_map/ppermute | solution.py:50
  13.4 8.2 %collective-permute-start.4 = (bf16[32,2176]{1,0:T(8,128)(2,1)S(1)}, bf16[32,2176]{1,0:T(8,128)(2,1)S(1)}, u32[]{:S(2)}, u32[]{:S(2)}) collective-permute-start(bf16[32,2176]{1,0:T(8,128)(2,1)S(1)} %shard_map.58.refs_1_), channel_id=1, source_target_pairs={{0,2},{1,3},{2,0},{3,1},{4,6},{5,7},{6,4},{7,5},{8,10},{9,11},{10,... | collective-permute-start | bytes 417800 | tf_op jit(solution)/shard_map/ppermute | solution.py:50
  15.0 6.6 %collective-permute-start.2 = (bf16[32,2176]{1,0:T(8,128)(2,1)S(1)}, bf16[32,2176]{1,0:T(8,128)(2,1)S(1)}, u32[]{:S(2)}, u32[]{:S(2)}) collective-permute-start(bf16[32,2176]{1,0:T(8,128)(2,1)S(1)} %shard_map.58.refs_1_), channel_id=1, source_target_pairs={{0,4},{1,5},{2,6},{3,7},{4,0},{5,1},{6,2},{7,3},{8,12},{9,13},{10,... | collective-permute-start | bytes 417800 | tf_op jit(solution)/shard_map/ppermute | solution.py:50
  15.4 7.8 %collective-permute-start.5 = (bf16[64,2176]{1,0:T(8,128)(2,1)S(1)}, bf16[64,2176]{1,0:T(8,128)(2,1)S(1)}, u32[]{:S(2)}, u32[]{:S(2)}) collective-permute-start(bf16[64,2176]{1,0:T(8,128)(2,1)S(1)} %shard_map.57.refs_0_.refs_1_), channel_id=1, source_target_pairs={{0,1},{1,0},{2,3},{3,2},{4,5},{5,4},{6,7},{7,6},{8,9},{9,8},{10,11... | collective-permute-start | bytes 835592 | tf_op jit(solution)/shard_map/ppermute | solution.py:50
  21.6 1.6 %collective-permute-start.6 = (bf16[64,2176]{1,0:T(8,128)(2,1)S(1)}, bf16[64,2176]{1,0:T(8,128)(2,1)S(1)}, u32[]{:S(2)}, u32[]{:S(2)}) collective-permute-start(bf16[64,2176]{1,0:T(8,128)(2,1)S(1)} %collective-permute-done.3.refs_2_), channel_id=1, source_target_pairs={{0,1},{1,0},{2,3},{3,2},{4,5},{5,4},{6,7},{7,6},{8,9},{9,8},{10,11... | collective-permute-start | bytes 835592 | tf_op jit(solution)/shard_map/ppermute | solution.py:50
  21.6 6.1 %collective-permute-start.9 = (bf16[32,2176]{1,0:T(8,128)(2,1)S(1)}, bf16[32,2176]{1,0:T(8,128)(2,1)S(1)}, u32[]{:S(2)}, u32[]{:S(2)}) collective-permute-start(bf16[32,2176]{1,0:T(8,128)(2,1)S(1)} %collective-permute-done.2.refs_0_.refs_2_), channel_id=1, source_target_pairs={{0,2},{1,3},{2,0},{3,1},{4,6},{5,7},{6,4},{7,5},{8,10},{9,11},{10,... | collective-permute-start | bytes 417800 | tf_op jit(solution)/shard_map/ppermute | solution.py:50
  25.8 1.9 %collective-permute-start.7 = (bf16[32,2048]{1,0:T(8,128)(2,1)S(1)}, bf16[32,2048]{1,0:T(8,128)(2,1)S(1)}, u32[]{:S(2)}, u32[]{:S(2)}) collective-permute-start(bf16[32,2048]{1,0:T(8,128)(2,1)S(1)} %get-tuple-element.56), channel_id=1, source_target_pairs={{0,1},{1,0},{2,3},{3,2},{4,5},{5,4},{6,7},{7,6},{8,9},{9,8},{10,11... | collective-permute-start | bytes 393224 | tf_op jit(solution)/shard_map/ppermute | solution.py:50
  26.0 3.3 %collective-permute-start.10 = (bf16[32,2176]{1,0:T(8,128)(2,1)S(1)}, bf16[32,2176]{1,0:T(8,128)(2,1)S(1)}, u32[]{:S(2)}, u32[]{:S(2)}) collective-permute-start(bf16[32,2176]{1,0:T(8,128)(2,1)S(1)} %shard_map.58.refs_1_), channel_id=1, source_target_pairs={{0,1},{1,0},{2,3},{3,2},{4,5},{5,4},{6,7},{7,6},{8,9},{9,8},{10,11... | collective-permute-start | bytes 417800 | tf_op jit(solution)/shard_map/ppermute | solution.py:50
  26.4 2.9 %collective-permute-start.12 = (bf16[32,2176]{1,0:T(8,128)(2,1)S(1)}, bf16[32,2176]{1,0:T(8,128)(2,1)S(1)}, u32[]{:S(2)}, u32[]{:S(2)}) collective-permute-start(bf16[32,2176]{1,0:T(8,128)(2,1)S(1)} %collective-permute-done.4.refs_3_), channel_id=1, source_target_pairs={{0,1},{1,0},{2,3},{3,2},{4,5},{5,4},{6,7},{7,6},{8,9},{9,8},{10,11... | collective-permute-start | bytes 417800 | tf_op jit(solution)/shard_map/ppermute | solution.py:50
  26.6 2.8 %collective-permute-start.11 = (bf16[32,2176]{1,0:T(8,128)(2,1)S(1)}, bf16[32,2176]{1,0:T(8,128)(2,1)S(1)}, u32[]{:S(2)}, u32[]{:S(2)}) collective-permute-start(bf16[32,2176]{1,0:T(8,128)(2,1)S(1)} %collective-permute-done.2.refs_0_.refs_2_), channel_id=1, source_target_pairs={{0,1},{1,0},{2,3},{3,2},{4,5},{5,4},{6,7},{7,6},{8,9},{9,8},{10,11... | collective-permute-start | bytes 417800 | tf_op jit(solution)/shard_map/ppermute | solution.py:50
  27.7 1.6 %collective-permute-start.13 = (bf16[32,2176]{1,0:T(8,128)(2,1)S(1)}, bf16[32,2176]{1,0:T(8,128)(2,1)S(1)}, u32[]{:S(2)}, u32[]{:S(2)}) collective-permute-start(bf16[32,2176]{1,0:T(8,128)(2,1)S(1)} %collective-permute-done.9.refs_4_), channel_id=1, source_target_pairs={{0,1},{1,0},{2,3},{3,2},{4,5},{5,4},{6,7},{7,6},{8,9},{9,8},{10,11... | collective-permute-start | bytes 417800 | tf_op jit(solution)/shard_map/ppermute | solution.py:50
  27.7 1.5 %collective-permute-start.8 = (bf16[32,2048]{1,0:T(8,128)(2,1)S(1)}, bf16[32,2048]{1,0:T(8,128)(2,1)S(1)}, u32[]{:S(2)}, u32[]{:S(2)}) collective-permute-start(bf16[32,2048]{1,0:T(8,128)(2,1)S(1)} %get-tuple-element.57), channel_id=1, source_target_pairs={{0,1},{1,0},{2,3},{3,2},{4,5},{5,4},{6,7},{7,6},{8,9},{9,8},{10,11... | collective-permute-start | bytes 393224 | tf_op jit(solution)/shard_map/ppermute | solution.py:50
  32.0 1.4 %collective-permute-start.14 = (bf16[32,2048]{1,0:T(8,128)(2,1)S(1)}, bf16[32,2048]{1,0:T(8,128)(2,1)S(1)}, u32[]{:S(2)}, u32[]{:S(2)}) collective-permute-start(bf16[32,2048]{1,0:T(8,128)(2,1)S(1)} %get-tuple-element.64), channel_id=1, source_target_pairs={{0,1},{1,0},{2,3},{3,2},{4,5},{5,4},{6,7},{7,6},{8,9},{9,8},{10,11... | collective-permute-start | bytes 393224 | tf_op jit(solution)/shard_map/ppermute | solution.py:50
  32.3 1.3 %collective-permute-start.15 = (bf16[32,2048]{1,0:T(8,128)(2,1)S(1)}, bf16[32,2048]{1,0:T(8,128)(2,1)S(1)}, u32[]{:S(2)}, u32[]{:S(2)}) collective-permute-start(bf16[32,2048]{1,0:T(8,128)(2,1)S(1)} %get-tuple-element.65), channel_id=1, source_target_pairs={{0,1},{1,0},{2,3},{3,2},{4,5},{5,4},{6,7},{7,6},{8,9},{9,8},{10,11... | collective-permute-start | bytes 393224 | tf_op jit(solution)/shard_map/ppermute | solution.py:50
  32.5 10.4 %collective-permute-start.20 = (bf16[64,2048]{1,0:T(8,128)(2,1)S(1)}, bf16[64,2048]{1,0:T(8,128)(2,1)S(1)}, u32[]{:S(2)}, u32[]{:S(2)}) collective-permute-start(bf16[64,2048]{1,0:T(8,128)(2,1)S(1)} %get-tuple-element.72), channel_id=1, source_target_pairs={{0,1},{1,0},{2,3},{3,2},{4,5},{5,4},{6,7},{7,6},{8,9},{9,8},{10,11... | collective-permute-start | bytes 786440 | tf_op jit(solution)/shard_map/ppermute | solution.py:50
  33.7 6.4 %collective-permute-start.17 = (bf16[32,2048]{1,0:T(8,128)(2,1)S(1)}, bf16[32,2048]{1,0:T(8,128)(2,1)S(1)}, u32[]{:S(2)}, u32[]{:S(2)}) collective-permute-start(bf16[32,2048]{1,0:T(8,128)(2,1)S(1)} %get-tuple-element.66.refs_0_), channel_id=1, source_target_pairs={{0,2},{1,3},{2,0},{3,1},{4,6},{5,7},{6,4},{7,5},{8,10},{9,11},{10,... | collective-permute-start | bytes 393224 | tf_op jit(solution)/shard_map/ppermute | solution.py:50
  35.3 7.6 %collective-permute-start.21 = (bf16[32,2048]{1,0:T(8,128)(2,1)S(1)}, bf16[32,2048]{1,0:T(8,128)(2,1)S(1)}, u32[]{:S(2)}, u32[]{:S(2)}) collective-permute-start(bf16[32,2048]{1,0:T(8,128)(2,1)S(1)} %get-tuple-element.67.refs_1_), channel_id=1, source_target_pairs={{0,2},{1,3},{2,0},{3,1},{4,6},{5,7},{6,4},{7,5},{8,10},{9,11},{10,... | collective-permute-start | bytes 393224 | tf_op jit(solution)/shard_map/ppermute | solution.py:50
  35.8 13.4 %collective-permute-start.16 = (bf16[64,2048]{1,0:T(8,128)(2,1)S(1)}, bf16[64,2048]{1,0:T(8,128)(2,1)S(1)}, u32[]{:S(2)}, u32[]{:S(2)}) collective-permute-start(bf16[64,2048]{1,0:T(8,128)(2,1)S(1)} %get-tuple-element.68), channel_id=1, source_target_pairs={{0,1},{1,0},{2,3},{3,2},{4,5},{5,4},{6,7},{7,6},{8,9},{9,8},{10,11... | collective-permute-start | bytes 786440 | tf_op jit(solution)/shard_map/ppermute | solution.py:50
  40.1 9.1 %collective-permute-start.18 = (bf16[64,2048]{1,0:T(8,128)(2,1)S(1)}, bf16[64,2048]{1,0:T(8,128)(2,1)S(1)}, u32[]{:S(2)}, u32[]{:S(2)}) collective-permute-start(bf16[64,2048]{1,0:T(8,128)(2,1)S(1)} %shard_map.60.refs_0_), channel_id=1, source_target_pairs={{0,2},{1,3},{2,0},{3,1},{4,6},{5,7},{6,4},{7,5},{8,10},{9,11},{10,... | collective-permute-start | bytes 786440 | tf_op jit(solution)/shard_map/ppermute | solution.py:50
  43.0 5.0 %collective-permute-start.22 = (bf16[32,2048]{1,0:T(8,128)(2,1)S(1)}, bf16[32,2048]{1,0:T(8,128)(2,1)S(1)}, u32[]{:S(2)}, u32[]{:S(2)}) collective-permute-start(bf16[32,2048]{1,0:T(8,128)(2,1)S(1)} %shard_map.65), channel_id=1, source_target_pairs={{0,4},{1,5},{2,6},{3,7},{4,0},{5,1},{6,2},{7,3},{8,12},{9,13},{10,... | collective-permute-start | bytes 393224 | tf_op jit(solution)/shard_map/ppermute | solution.py:50
  48.1 7.3 %collective-permute-start.23 = (bf16[32,2048]{1,0:T(8,128)(2,1)S(1)}, bf16[32,2048]{1,0:T(8,128)(2,1)S(1)}, u32[]{:S(2)}, u32[]{:S(2)}) collective-permute-start(bf16[32,2048]{1,0:T(8,128)(2,1)S(1)} %shard_map.66), channel_id=1, source_target_pairs={{0,8},{1,9},{2,10},{3,11},{4,12},{5,13},{6,14},{7,15},{8,0},{9,1},... | collective-permute-start | bytes 393224 | tf_op jit(solution)/shard_map/ppermute | solution.py:50
  49.4 6.7 %collective-permute-start.19 = (bf16[32,2048]{1,0:T(8,128)(2,1)S(1)}, bf16[32,2048]{1,0:T(8,128)(2,1)S(1)}, u32[]{:S(2)}, u32[]{:S(2)}) collective-permute-start(bf16[32,2048]{1,0:T(8,128)(2,1)S(1)} %get-tuple-element.71), channel_id=1, source_target_pairs={{0,4},{1,5},{2,6},{3,7},{4,0},{5,1},{6,2},{7,3},{8,12},{9,13},{10,... | collective-permute-start | bytes 393224 | tf_op jit(solution)/shard_map/ppermute | solution.py:50
  56.2 5.0 %collective-permute-start.24 = (bf16[32,2048]{1,0:T(8,128)(2,1)S(1)}, bf16[32,2048]{1,0:T(8,128)(2,1)S(1)}, u32[]{:S(2)}, u32[]{:S(2)}) collective-permute-start(bf16[32,2048]{1,0:T(8,128)(2,1)S(1)} %get-tuple-element.74.refs_1_), channel_id=1, source_target_pairs={{0,4},{1,5},{2,6},{3,7},{4,0},{5,1},{6,2},{7,3},{8,12},{9,13},{10,... | collective-permute-start | bytes 393224 | tf_op jit(solution)/shard_map/ppermute | solution.py:50
  57.4 7.4 %collective-permute-start.25 = (bf16[32,2048]{1,0:T(8,128)(2,1)S(1)}, bf16[32,2048]{1,0:T(8,128)(2,1)S(1)}, u32[]{:S(2)}, u32[]{:S(2)}) collective-permute-start(bf16[32,2048]{1,0:T(8,128)(2,1)S(1)} %get-tuple-element.74.refs_1_), channel_id=1, source_target_pairs={{0,8},{1,9},{2,10},{3,11},{4,12},{5,13},{6,14},{7,15},{8,0},{9,1},... | collective-permute-start | bytes 393224 | tf_op jit(solution)/shard_map/ppermute | solution.py:50
  61.3 9.9 %collective-permute-start.27 = (bf16[64,2048]{1,0:T(8,128)(2,1)S(1)}, bf16[64,2048]{1,0:T(8,128)(2,1)S(1)}, u32[]{:S(2)}, u32[]{:S(2)}) collective-permute-start(bf16[64,2048]{1,0:T(8,128)(2,1)S(1)} %shard_map.68.refs_0_.refs_1_), channel_id=1, source_target_pairs={{0,2},{1,3},{2,0},{3,1},{4,6},{5,7},{6,4},{7,5},{8,10},{9,11},{10,... | collective-permute-start | bytes 786440 | tf_op jit(solution)/shard_map/ppermute | solution.py:50
  64.8 5.0 %collective-permute-start.28 = (bf16[32,2048]{1,0:T(8,128)(2,1)S(1)}, bf16[32,2048]{1,0:T(8,128)(2,1)S(1)}, u32[]{:S(2)}, u32[]{:S(2)}) collective-permute-start(bf16[32,2048]{1,0:T(8,128)(2,1)S(1)} %shard_map.69.refs_1_), channel_id=1, source_target_pairs={{0,2},{1,3},{2,0},{3,1},{4,6},{5,7},{6,4},{7,5},{8,10},{9,11},{10,... | collective-permute-start | bytes 393224 | tf_op jit(solution)/shard_map/ppermute | solution.py:50
  66.2 5.0 %collective-permute-start.26 = (bf16[32,2048]{1,0:T(8,128)(2,1)S(1)}, bf16[32,2048]{1,0:T(8,128)(2,1)S(1)}, u32[]{:S(2)}, u32[]{:S(2)}) collective-permute-start(bf16[32,2048]{1,0:T(8,128)(2,1)S(1)} %shard_map.69.refs_1_), channel_id=1, source_target_pairs={{0,4},{1,5},{2,6},{3,7},{4,0},{5,1},{6,2},{7,3},{8,12},{9,13},{10,... | collective-permute-start | bytes 393224 | tf_op jit(solution)/shard_map/ppermute | solution.py:50
  66.9 5.0 %collective-permute-start.29 = (bf16[64,2048]{1,0:T(8,128)(2,1)S(1)}, bf16[64,2048]{1,0:T(8,128)(2,1)S(1)}, u32[]{:S(2)}, u32[]{:S(2)}) collective-permute-start(bf16[64,2048]{1,0:T(8,128)(2,1)S(1)} %shard_map.68.refs_0_.refs_1_), channel_id=1, source_target_pairs={{0,1},{1,0},{2,3},{3,2},{4,5},{5,4},{6,7},{7,6},{8,9},{9,8},{10,11... | collective-permute-start | bytes 786440 | tf_op jit(solution)/shard_map/ppermute | solution.py:50
  71.2 1.5 %collective-permute-start.30 = (bf16[64,2048]{1,0:T(8,128)(2,1)S(1)}, bf16[64,2048]{1,0:T(8,128)(2,1)S(1)}, u32[]{:S(2)}, u32[]{:S(2)}) collective-permute-start(bf16[64,2048]{1,0:T(8,128)(2,1)S(1)} %collective-permute-done.27.refs_2_), channel_id=1, source_target_pairs={{0,1},{1,0},{2,3},{3,2},{4,5},{5,4},{6,7},{7,6},{8,9},{9,8},{10,11... | collective-permute-start | bytes 786440 | tf_op jit(solution)/shard_map/ppermute | solution.py:50
  71.2 5.9 %collective-permute-start.33 = (bf16[32,2048]{1,0:T(8,128)(2,1)S(1)}, bf16[32,2048]{1,0:T(8,128)(2,1)S(1)}, u32[]{:S(2)}, u32[]{:S(2)}) collective-permute-start(bf16[32,2048]{1,0:T(8,128)(2,1)S(1)} %collective-permute-done.26.refs_0_.refs_2_), channel_id=1, source_target_pairs={{0,2},{1,3},{2,0},{3,1},{4,6},{5,7},{6,4},{7,5},{8,10},{9,11},{10,... | collective-permute-start | bytes 393224 | tf_op jit(solution)/shard_map/ppermute | solution.py:50
  75.4 1.8 %collective-permute-start.31 = (bf16[32,2048]{1,0:T(8,128)(2,1)S(1)}, bf16[32,2048]{1,0:T(8,128)(2,1)S(1)}, u32[]{:S(2)}, u32[]{:S(2)}) collective-permute-start(bf16[32,2048]{1,0:T(8,128)(2,1)S(1)} %get-tuple-element.80), channel_id=1, source_target_pairs={{0,1},{1,0},{2,3},{3,2},{4,5},{5,4},{6,7},{7,6},{8,9},{9,8},{10,11... | collective-permute-start | bytes 393224 | tf_op jit(solution)/shard_map/ppermute | solution.py:50
  75.6 3.0 %collective-permute-start.34 = (bf16[32,2048]{1,0:T(8,128)(2,1)S(1)}, bf16[32,2048]{1,0:T(8,128)(2,1)S(1)}, u32[]{:S(2)}, u32[]{:S(2)}) collective-permute-start(bf16[32,2048]{1,0:T(8,128)(2,1)S(1)} %shard_map.69.refs_1_), channel_id=1, source_target_pairs={{0,1},{1,0},{2,3},{3,2},{4,5},{5,4},{6,7},{7,6},{8,9},{9,8},{10,11... | collective-permute-start | bytes 393224 | tf_op jit(solution)/shard_map/ppermute | solution.py:50
  75.9 2.6 %collective-permute-start.36 = (bf16[32,2048]{1,0:T(8,128)(2,1)S(1)}, bf16[32,2048]{1,0:T(8,128)(2,1)S(1)}, u32[]{:S(2)}, u32[]{:S(2)}) collective-permute-start(bf16[32,2048]{1,0:T(8,128)(2,1)S(1)} %collective-permute-done.28.refs_3_), channel_id=1, source_target_pairs={{0,1},{1,0},{2,3},{3,2},{4,5},{5,4},{6,7},{7,6},{8,9},{9,8},{10,11... | collective-permute-start | bytes 393224 | tf_op jit(solution)/shard_map/ppermute | solution.py:50
  76.1 2.5 %collective-permute-start.35 = (bf16[32,2048]{1,0:T(8,128)(2,1)S(1)}, bf16[32,2048]{1,0:T(8,128)(2,1)S(1)}, u32[]{:S(2)}, u32[]{:S(2)}) collective-permute-start(bf16[32,2048]{1,0:T(8,128)(2,1)S(1)} %collective-permute-done.26.refs_0_.refs_2_), channel_id=1, source_target_pairs={{0,1},{1,0},{2,3},{3,2},{4,5},{5,4},{6,7},{7,6},{8,9},{9,8},{10,11... | collective-permute-start | bytes 393224 | tf_op jit(solution)/shard_map/ppermute | solution.py:50
  77.1 1.3 %collective-permute-start.32 = (bf16[32,2048]{1,0:T(8,128)(2,1)S(1)}, bf16[32,2048]{1,0:T(8,128)(2,1)S(1)}, u32[]{:S(2)}, u32[]{:S(2)}) collective-permute-start(bf16[32,2048]{1,0:T(8,128)(2,1)S(1)} %get-tuple-element.81), channel_id=1, source_target_pairs={{0,1},{1,0},{2,3},{3,2},{4,5},{5,4},{6,7},{7,6},{8,9},{9,8},{10,11... | collective-permute-start | bytes 393224 | tf_op jit(solution)/shard_map/ppermute | solution.py:50
  77.1 1.5 %collective-permute-start.37 = (bf16[32,2048]{1,0:T(8,128)(2,1)S(1)}, bf16[32,2048]{1,0:T(8,128)(2,1)S(1)}, u32[]{:S(2)}, u32[]{:S(2)}) collective-permute-start(bf16[32,2048]{1,0:T(8,128)(2,1)S(1)} %collective-permute-done.33.refs_4_), channel_id=1, source_target_pairs={{0,1},{1,0},{2,3},{3,2},{4,5},{5,4},{6,7},{7,6},{8,9},{9,8},{10,11... | collective-permute-start | bytes 393224 | tf_op jit(solution)/shard_map/ppermute | solution.py:50
  81.3 1.4 %collective-permute-start.38 = (bf16[32,2048]{1,0:T(8,128)(2,1)S(1)}, bf16[32,2048]{1,0:T(8,128)(2,1)S(1)}, u32[]{:S(2)}, u32[]{:S(2)}) collective-permute-start(bf16[32,2048]{1,0:T(8,128)(2,1)S(1)} %get-tuple-element.87), channel_id=1, source_target_pairs={{0,1},{1,0},{2,3},{3,2},{4,5},{5,4},{6,7},{7,6},{8,9},{9,8},{10,11... | collective-permute-start | bytes 393224 | tf_op jit(solution)/shard_map/ppermute | solution.py:50
  81.7 1.3 %collective-permute-start.39 = (bf16[32,2048]{1,0:T(8,128)(2,1)S(1)}, bf16[32,2048]{1,0:T(8,128)(2,1)S(1)}, u32[]{:S(2)}, u32[]{:S(2)}) collective-permute-start(bf16[32,2048]{1,0:T(8,128)(2,1)S(1)} %get-tuple-element.88), channel_id=1, source_target_pairs={{0,1},{1,0},{2,3},{3,2},{4,5},{5,4},{6,7},{7,6},{8,9},{9,8},{10,11... | collective-permute-start | bytes 393224 | tf_op jit(solution)/shard_map/ppermute | solution.py:50
  81.9 8.3 %collective-permute-start.44 = (bf16[64,2048]{1,0:T(8,128)(2,1)S(1)}, bf16[64,2048]{1,0:T(8,128)(2,1)S(1)}, u32[]{:S(2)}, u32[]{:S(2)}) collective-permute-start(bf16[64,2048]{1,0:T(8,128)(2,1)S(1)} %get-tuple-element.96), channel_id=1, source_target_pairs={{0,1},{1,0},{2,3},{3,2},{4,5},{5,4},{6,7},{7,6},{8,9},{9,8},{10,11... | collective-permute-start | bytes 786440 | tf_op jit(solution)/shard_map/ppermute | solution.py:50
  83.1 6.4 %collective-permute-start.41 = (bf16[32,2048]{1,0:T(8,128)(2,1)S(1)}, bf16[32,2048]{1,0:T(8,128)(2,1)S(1)}, u32[]{:S(2)}, u32[]{:S(2)}) collective-permute-start(bf16[32,2048]{1,0:T(8,128)(2,1)S(1)} %get-tuple-element.89.refs_0_), channel_id=1, source_target_pairs={{0,2},{1,3},{2,0},{3,1},{4,6},{5,7},{6,4},{7,5},{8,10},{9,11},{10,... | collective-permute-start | bytes 393224 | tf_op jit(solution)/shard_map/ppermute | solution.py:50
  83.8 8.5 %collective-permute-start.45 = (bf16[32,2048]{1,0:T(8,128)(2,1)S(1)}, bf16[32,2048]{1,0:T(8,128)(2,1)S(1)}, u32[]{:S(2)}, u32[]{:S(2)}) collective-permute-start(bf16[32,2048]{1,0:T(8,128)(2,1)S(1)} %get-tuple-element.90.refs_1_), channel_id=1, source_target_pairs={{0,2},{1,3},{2,0},{3,1},{4,6},{5,7},{6,4},{7,5},{8,10},{9,11},{10,... | collective-permute-start | bytes 393224 | tf_op jit(solution)/shard_map/ppermute | solution.py:50
  85.2 13.5 %collective-permute-start.40 = (bf16[64,2048]{1,0:T(8,128)(2,1)S(1)}, bf16[64,2048]{1,0:T(8,128)(2,1)S(1)}, u32[]{:S(2)}, u32[]{:S(2)}) collective-permute-start(bf16[64,2048]{1,0:T(8,128)(2,1)S(1)} %get-tuple-element.91), channel_id=1, source_target_pairs={{0,1},{1,0},{2,3},{3,2},{4,5},{5,4},{6,7},{7,6},{8,9},{9,8},{10,11... | collective-permute-start | bytes 786440 | tf_op jit(solution)/shard_map/ppermute | solution.py:50
  89.5 9.2 %collective-permute-start.42 = (bf16[64,2048]{1,0:T(8,128)(2,1)S(1)}, bf16[64,2048]{1,0:T(8,128)(2,1)S(1)}, u32[]{:S(2)}, u32[]{:S(2)}) collective-permute-start(bf16[64,2048]{1,0:T(8,128)(2,1)S(1)} %shard_map.71.refs_0_), channel_id=1, source_target_pairs={{0,2},{1,3},{2,0},{3,1},{4,6},{5,7},{6,4},{7,5},{8,10},{9,11},{10,... | collective-permute-start | bytes 786440 | tf_op jit(solution)/shard_map/ppermute | solution.py:50
  92.3 5.0 %collective-permute-start.46 = (bf16[32,2048]{1,0:T(8,128)(2,1)S(1)}, bf16[32,2048]{1,0:T(8,128)(2,1)S(1)}, u32[]{:S(2)}, u32[]{:S(2)}) collective-permute-start(bf16[32,2048]{1,0:T(8,128)(2,1)S(1)} %shard_map.75), channel_id=1, source_target_pairs={{0,4},{1,5},{2,6},{3,7},{4,0},{5,1},{6,2},{7,3},{8,12},{9,13},{10,... | collective-permute-start | bytes 393224 | tf_op jit(solution)/shard_map/ppermute | solution.py:50
  97.4 7.4 %collective-permute-start.47 = (bf16[32,2048]{1,0:T(8,128)(2,1)S(1)}, bf16[32,2048]{1,0:T(8,128)(2,1)S(1)}, u32[]{:S(2)}, u32[]{:S(2)}) collective-permute-start(bf16[32,2048]{1,0:T(8,128)(2,1)S(1)} %shard_map.76), channel_id=1, source_target_pairs={{0,8},{1,9},{2,10},{3,11},{4,12},{5,13},{6,14},{7,15},{8,0},{9,1},... | collective-permute-start | bytes 393224 | tf_op jit(solution)/shard_map/ppermute | solution.py:50
  98.7 6.3 %collective-permute-start.43 = (bf16[32,2048]{1,0:T(8,128)(2,1)S(1)}, bf16[32,2048]{1,0:T(8,128)(2,1)S(1)}, u32[]{:S(2)}, u32[]{:S(2)}) collective-permute-start(bf16[32,2048]{1,0:T(8,128)(2,1)S(1)} %get-tuple-element.94), channel_id=1, source_target_pairs={{0,4},{1,5},{2,6},{3,7},{4,0},{5,1},{6,2},{7,3},{8,12},{9,13},{10,... | collective-permute-start | bytes 393224 | tf_op jit(solution)/shard_map/ppermute | solution.py:50
  (2 other events, 13.4 us)

commit v12 on v11

--- a/solution.py
+++ b/solution.py
@@ -90,7 +90,7 @@
     rows = pieces[0].shape[0]
     for k, piece in enumerate(pieces):
         span = slice((first + k) * rows, (first + k + 1) * rows)
-        part = beside[k][...] if len(beside) == count else beside[0][span]
+        part = beside[k][...] if beside[0].shape[0] == rows else beside[0][span]
         total = mine[span] + near[span].astype(f32) + part.astype(f32)
         piece[...] = total.astype(piece.dtype)
 
@@ -98,7 +98,7 @@
 def cross_kernel(mine, near, beside, *refs):
     *arrived, out = refs
     rows = out.shape[0]
-    total = mine[:rows] + near[:rows].astype(f32) + beside[...].astype(f32)
+    total = mine[:rows] + near[:rows].astype(f32) + beside[:rows].astype(f32)
     for piece in arrived:
         total = total + piece[...].astype(f32)
     out[...] = total.astype(out.dtype)
@@ -120,22 +120,22 @@
     return mine_near, arrived_near, leaving
 
 
-def cross_rows(mine, near, beside):
-    far, count = lax.axis_size("expert") // 4, len(beside)
-    shape = beside[0].shape
+def cross_rows(mine, near, beside, count):
+    far = lax.axis_size("expert") // 4
+    shape = (mine.shape[0] // count, mine.shape[1])
     arrived = []
     if count > 1:
         hops = call(
             functools.partial(apart_kernel, 1, count - 1),
             [(shape, bf16)] * (count - 1),
-            [VMEM] * (count + 1),
+            [VMEM] * 3,
             mine,
             near,
-            *beside[1:],
+            beside,
         )
         arrived = [swap(piece, 4, k, far, True) for k, piece in enumerate(hops, 1)]
     (crossing,) = call(
-        cross_kernel, [(shape, bf16)], [VMEM] * (3 + len(arrived)), mine, near, beside[0], *arrived
+        cross_kernel, [(shape, bf16)], [VMEM] * (3 + len(arrived)), mine, near, beside, *arrived
     )
     return swap(crossing, 4, count, far, True)
 
@@ -349,10 +349,10 @@
     mine1, near1, leaving1 = leave_pair(outs, 1, ())
     second_beside[-1] = held(second_beside[-1], outs[0])
     outs, second_columns = worked(second, second_beside, routed[1], tuple(leaving1))
-    mine2, near2, leaving2 = leave_pair(outs, half, ())
+    mine2, near2, leaving2 = leave_pair(outs, 1, ())
     back2 = [swap(piece, 2, 1, 2, True) for piece in leaving2]
     back1 = [swap(held(piece, back2[0]), 2, 1, 2, True) for piece in leaving1]
-    crossed_back = cross_rows(mine2, near2, back2)
+    crossed_back = cross_rows(mine2, near2, back2[0], half)
     pieces = call(
         functools.partial(apart_kernel, 0, half),
         [(rows.shape[:1] + mine1.shape[1:], bf16 if k else f32) for k in range(half)],

time: 106 us -> 109 us (1.028)
  starting transfers between devices: 34.7 us -> 37.9 us
    ppermute x48 -> x46, starting transfers between devices: 34.7 us -> 37.9 us  [swap(): lax.ppermute(value, 'expert', [(i, partner(i)) for i in range(count)])]
    ppermute x48 -> x46, waiting for transfers between devices: 50 us -> 49.6 us  [swap(): lax.ppermute(value, 'expert', [(i, partner(i)) for i in range(count)])]
  transfers between devices with their start and end apart: 48 -> 46, of which waited for: 26 -> 22; matrix products, arithmetic and copies ran while one was open for 0% -> 0% of each run, Pallas kernels for 13% -> 12%
where the time goes in v12:
time: 109 us
  waiting for transfers between devices  49.6 us (46%)
  starting transfers between devices  37.9 us (35%)
  Pallas kernels  20.8 us (19%)
    ppermute x46, waiting for transfers between devices, swap(): lax.ppermute(value, 'expert', [(i, partner(i)) for i in range(count)])  49.6 us
    ppermute x46, starting transfers between devices, swap(): lax.ppermute(value, 'expert', [(i, partner(i)) for i in range(count)])  37.9 us
    pallas_call x23, Pallas kernels, call(): pl.pallas_call(lambda *refs: kernel(*refs[len(after):]), out_shape=shapes...  20.8 us
  transfers between devices with their start and end apart: 46, of which 22 were waited for; matrix products, arithmetic and copies ran while one was open for 0% of the time, Pallas kernels for 12%

profile of v12, /device:TPU:0, one launch (start us, length us, event | category | flops | bytes accessed | tf_op | source)
XLA Modules:
  0.0 108.5 jit_solution(2088862156461337392)
XLA Ops:
  0.0 1.2 %shard_map.56.refs_1_ = bf16[32,2176]{1,0:T(8,128)(2,1)S(1)} custom-call(bf16[32,2048]{1,0:T(8,128)(2,1)} %bitcast.2, s32[2,2,8,16]{3,2,1,0:T(8,128)} %bitcast.4, f32[2,2048]{1,0:T(2,128)} %refs_2_.5), custom_call_target="tpu_custom_call" | custom-call | tf_op jit(solution)/shard_map/pallas_call | solution.py:28
  1.2 3.1 %collective-permute-start = (bf16[32,2176]{1,0:T(8,128)(2,1)S(1)}, bf16[32,2176]{1,0:T(8,128)(2,1)S(1)}, u32[]{:S(2)}, u32[]{:S(2)}) collective-permute-start(bf16[32,2176]{1,0:T(8,128)(2,1)S(1)} %shard_map.56.refs_1_), channel_id=1, source_target_pairs={{0,4},{1,5},{2,6},{3,7},{4,0},{5,1},{6,2},{7,3},{8,12},{9,13},{10,... | collective-permute-start | bytes 417800 | tf_op jit(solution)/shard_map/ppermute | solution.py:50
  4.3 2.6 %collective-permute-start.1 = (bf16[32,2176]{1,0:T(8,128)(2,1)S(1)}, bf16[32,2176]{1,0:T(8,128)(2,1)S(1)}, u32[]{:S(2)}, u32[]{:S(2)}) collective-permute-start(bf16[32,2176]{1,0:T(8,128)(2,1)S(1)} %shard_map.56.refs_1_), channel_id=1, source_target_pairs={{0,8},{1,9},{2,10},{3,11},{4,12},{5,13},{6,14},{7,15},{8,0},{9,1},... | collective-permute-start | bytes 417800 | tf_op jit(solution)/shard_map/ppermute | solution.py:50
  6.9 3.7 %shard_map.55 = (bf16[2048,1536]{1,0:T(8,128)(2,1)S(1)}, bf16[768,2048]{1,0:T(8,128)(2,1)S(1)}, f32[8,128]{1,0:T(8,128)S(1)}) custom-call(bf16[2,1,2048,1536]{3,2,1,0:T(8,128)(2,1)} %refs_1_.3, bf16[2,1,768,2048]{3,2,1,0:T(8,128)(2,1)} %refs_2_.4), custom_call_target="tpu_custom_call" | custom-call | tf_op jit(solution)/shard_map/pallas_call | solution.py:28
  10.7 1.6 %collective-permute-start.3 = (bf16[64,2176]{1,0:T(8,128)(2,1)S(1)}, bf16[64,2176]{1,0:T(8,128)(2,1)S(1)}, u32[]{:S(2)}, u32[]{:S(2)}) collective-permute-start(bf16[64,2176]{1,0:T(8,128)(2,1)S(1)} %shard_map.57.refs_0_.refs_1_), channel_id=1, source_target_pairs={{0,2},{1,3},{2,0},{3,1},{4,6},{5,7},{6,4},{7,5},{8,10},{9,11},{10,... | collective-permute-start | bytes 835592 | tf_op jit(solution)/shard_map/ppermute | solution.py:50
  12.3 1.1 %collective-permute-done.1.refs_1_ = bf16[32,2176]{1,0:T(8,128)(2,1)S(1)} collective-permute-done((bf16[32,2176]{1,0:T(8,128)(2,1)S(1)}, bf16[32,2176]{1,0:T(8,128)(2,1)S(1)}, u32[]{:S(2)}, u32[]{:S(2)}) %collective-permute-start.1) | collective-permute-done | bytes 139296 | tf_op jit(solution)/shard_map/ppermute | solution.py:50
  13.4 1.6 %collective-permute-start.4 = (bf16[32,2176]{1,0:T(8,128)(2,1)S(1)}, bf16[32,2176]{1,0:T(8,128)(2,1)S(1)}, u32[]{:S(2)}, u32[]{:S(2)}) collective-permute-start(bf16[32,2176]{1,0:T(8,128)(2,1)S(1)} %shard_map.58.refs_1_), channel_id=1, source_target_pairs={{0,2},{1,3},{2,0},{3,1},{4,6},{5,7},{6,4},{7,5},{8,10},{9,11},{10,... | collective-permute-start | bytes 417800 | tf_op jit(solution)/shard_map/ppermute | solution.py:50
  15.0 0.4 collective-permute-start.2
  15.4 6.2 %collective-permute-done.4.refs_3_ = bf16[32,2176]{1,0:T(8,128)(2,1)S(1)} collective-permute-done((bf16[32,2176]{1,0:T(8,128)(2,1)S(1)}, bf16[32,2176]{1,0:T(8,128)(2,1)S(1)}, u32[]{:S(2)}, u32[]{:S(2)}) %collective-permute-start.4) | collective-permute-done | bytes 139296 | tf_op jit(solution)/shard_map/ppermute | solution.py:50
  21.6 1.6 %collective-permute-start.9 = (bf16[32,2176]{1,0:T(8,128)(2,1)S(1)}, bf16[32,2176]{1,0:T(8,128)(2,1)S(1)}, u32[]{:S(2)}, u32[]{:S(2)}) collective-permute-start(bf16[32,2176]{1,0:T(8,128)(2,1)S(1)} %collective-permute-done.2.refs_0_.refs_2_), channel_id=1, source_target_pairs={{0,2},{1,3},{2,0},{3,1},{4,6},{5,7},{6,4},{7,5},{8,10},{9,11},{10,... | collective-permute-start | bytes 417800 | tf_op jit(solution)/shard_map/ppermute | solution.py:50
  23.2 2.6 %shard_map.59 = (f32[64,2048]{1,0:T(8,128)S(1)}, f32[64,2048]{1,0:T(8,128)S(1)}, bf16[64,2048]{1,0:T(8,128)(2,1)S(1)}, bf16[32,2048]{1,0:T(8,128)(2,1)S(1)}, bf1...) custom-call(bf16[32,2176]{1,0:T(8,128)(2,1)S(1)} %collective-permute-done.2.refs_0_.refs_2_, ...), custom_call_target="tpu_custom_call" | custom-call | tf_op jit(solution)/shard_map/pallas_call | solution.py:28
  26.9 0.8 collective-permute-done.9.refs_4_
  27.7 0.5 collective-permute-start.8
  28.2 1.0 collective-permute-done.8.refs_2_
  29.3 2.6 %shard_map.61 = (f32[64,2048]{1,0:T(8,128)S(1)}, f32[64,2048]{1,0:T(8,128)S(1)}, bf16[64,2048]{1,0:T(8,128)(2,1)S(1)}, bf16[32,2048]{1,0:T(8,128)(2,1)S(1)}, bf1...) custom-call(bf16[64,2048]{1,0:T(8,128)(2,1)S(1)} %shard_map.60.refs_0_, bf16[32,2176]{1,0:T(8,128)(2,1)S(1)} %shard_map.58.refs_1_, ...), custom_call_target="tpu_custom_call" | custom-call | tf_op jit(solution)/shard_map/pallas_call | solution.py:28
  32.5 0.8 collective-permute-done.14.refs_1_
  33.7 1.6 %collective-permute-start.17 = (bf16[64,2048]{1,0:T(8,128)(2,1)S(1)}, bf16[64,2048]{1,0:T(8,128)(2,1)S(1)}, u32[]{:S(2)}, u32[]{:S(2)}) collective-permute-start(bf16[64,2048]{1,0:T(8,128)(2,1)S(1)} %shard_map.63.refs_0_), channel_id=1, source_target_pairs={{0,2},{1,3},{2,0},{3,1},{4,6},{5,7},{6,4},{7,5},{8,10},{9,11},{10,... | collective-permute-start | bytes 786440 | tf_op jit(solution)/shard_map/ppermute | solution.py:50
  35.3 0.5 collective-permute-start.16
  35.8 6.4 %collective-permute-done.17.refs_2_ = bf16[64,2048]{1,0:T(8,128)(2,1)S(1)} collective-permute-done((bf16[64,2048]{1,0:T(8,128)(2,1)S(1)}, bf16[64,2048]{1,0:T(8,128)(2,1)S(1)}, u32[]{:S(2)}, u32[]{:S(2)}) %collective-permute-start.17) | collective-permute-done | bytes 262176 | tf_op jit(solution)/shard_map/ppermute | solution.py:50
  42.2 1.5 %collective-permute-start.18 = (bf16[64,2048]{1,0:T(8,128)(2,1)S(1)}, bf16[64,2048]{1,0:T(8,128)(2,1)S(1)}, u32[]{:S(2)}, u32[]{:S(2)}) collective-permute-start(bf16[64,2048]{1,0:T(8,128)(2,1)S(1)} %shard_map.60.refs_0_), channel_id=1, source_target_pairs={{0,2},{1,3},{2,0},{3,1},{4,6},{5,7},{6,4},{7,5},{8,10},{9,11},{10,... | collective-permute-start | bytes 786440 | tf_op jit(solution)/shard_map/ppermute | solution.py:50
  43.8 0.5 collective-permute-start.21
  44.3 4.5 %collective-permute-done.21.refs_3_ = bf16[32,2048]{1,0:T(8,128)(2,1)S(1)} collective-permute-done((bf16[32,2048]{1,0:T(8,128)(2,1)S(1)}, bf16[32,2048]{1,0:T(8,128)(2,1)S(1)}, u32[]{:S(2)}, u32[]{:S(2)}) %collective-permute-start.21) | collective-permute-done | bytes 131104 | tf_op jit(solution)/shard_map/ppermute | solution.py:50
  48.9 1.1 %collective-permute-start.22 = (bf16[32,2048]{1,0:T(8,128)(2,1)S(1)}, bf16[32,2048]{1,0:T(8,128)(2,1)S(1)}, u32[]{:S(2)}, u32[]{:S(2)}) collective-permute-start(bf16[32,2048]{1,0:T(8,128)(2,1)S(1)} %shard_map.66), channel_id=1, source_target_pairs={{0,8},{1,9},{2,10},{3,11},{4,12},{5,13},{6,14},{7,15},{8,0},{9,1},... | collective-permute-start | bytes 393224 | tf_op jit(solution)/shard_map/ppermute | solution.py:50
  50.1 2.1 %collective-permute-start.19 = (bf16[32,2048]{1,0:T(8,128)(2,1)S(1)}, bf16[32,2048]{1,0:T(8,128)(2,1)S(1)}, u32[]{:S(2)}, u32[]{:S(2)}) collective-permute-start(bf16[32,2048]{1,0:T(8,128)(2,1)S(1)} %get-tuple-element.65), channel_id=1, source_target_pairs={{0,4},{1,5},{2,6},{3,7},{4,0},{5,1},{6,2},{7,3},{8,12},{9,13},{10,... | collective-permute-start | bytes 393224 | tf_op jit(solution)/shard_map/ppermute | solution.py:50
  52.2 3.7 %shard_map.62 = (bf16[2048,1536]{1,0:T(8,128)(2,1)S(1)}, bf16[768,2048]{1,0:T(8,128)(2,1)S(1)}, f32[8,128]{1,0:T(8,128)S(1)}) custom-call(f32[64,2048]{1,0:T(8,128)S(1)} %get-tuple-element.57.refs_0_, bf16[2,1,2048,1536]{3,2,1,0:T(8,128)(2,1)} %refs_1_.3, bf16[2,1,768,2048]{3,2,1,0:T(8,128)(2,1)} %refs_2_.4), custom_call_target="tpu_custom_call" | custom-call | tf_op jit(solution)/shard_map/pallas_call | solution.py:28
  56.8 0.6 collective-permute-start.23
  57.5 2.5 %collective-permute-start.24 = (bf16[32,2048]{1,0:T(8,128)(2,1)S(1)}, bf16[32,2048]{1,0:T(8,128)(2,1)S(1)}, u32[]{:S(2)}, u32[]{:S(2)}) collective-permute-start(bf16[32,2048]{1,0:T(8,128)(2,1)S(1)} %get-tuple-element.68.refs_1_), channel_id=1, source_target_pairs={{0,8},{1,9},{2,10},{3,11},{4,12},{5,13},{6,14},{7,15},{8,0},{9,1},... | collective-permute-start | bytes 393224 | tf_op jit(solution)/shard_map/ppermute | solution.py:50
  60.0 3.2 %collective-permute-done.23.refs_2_ = bf16[32,2048]{1,0:T(8,128)(2,1)S(1)} collective-permute-done((bf16[32,2048]{1,0:T(8,128)(2,1)S(1)}, bf16[32,2048]{1,0:T(8,128)(2,1)S(1)}, u32[]{:S(2)}, u32[]{:S(2)}) %collective-permute-start.23) | collective-permute-done | bytes 131104 | tf_op jit(solution)/shard_map/ppermute | solution.py:50
  63.2 2.4 %collective-permute-start.26 = (bf16[64,2048]{1,0:T(8,128)(2,1)S(1)}, bf16[64,2048]{1,0:T(8,128)(2,1)S(1)}, u32[]{:S(2)}, u32[]{:S(2)}) collective-permute-start(bf16[64,2048]{1,0:T(8,128)(2,1)S(1)} %shard_map.68.refs_0_.refs_1_), channel_id=1, source_target_pairs={{0,2},{1,3},{2,0},{3,1},{4,6},{5,7},{6,4},{7,5},{8,10},{9,11},{10,... | collective-permute-start | bytes 786440 | tf_op jit(solution)/shard_map/ppermute | solution.py:50
  65.6 1.3 %collective-permute-start.27 = (bf16[32,2048]{1,0:T(8,128)(2,1)S(1)}, bf16[32,2048]{1,0:T(8,128)(2,1)S(1)}, u32[]{:S(2)}, u32[]{:S(2)}) collective-permute-start(bf16[32,2048]{1,0:T(8,128)(2,1)S(1)} %shard_map.69.refs_1_), channel_id=1, source_target_pairs={{0,2},{1,3},{2,0},{3,1},{4,6},{5,7},{6,4},{7,5},{8,10},{9,11},{10,... | collective-permute-start | bytes 393224 | tf_op jit(solution)/shard_map/ppermute | solution.py:50
  67.2 5.9 %collective-permute-done.27.refs_3_ = bf16[32,2048]{1,0:T(8,128)(2,1)S(1)} collective-permute-done((bf16[32,2048]{1,0:T(8,128)(2,1)S(1)}, bf16[32,2048]{1,0:T(8,128)(2,1)S(1)}, u32[]{:S(2)}, u32[]{:S(2)}) %collective-permute-start.27) | collective-permute-done | bytes 131104 | tf_op jit(solution)/shard_map/ppermute | solution.py:50
  73.1 1.8 %collective-permute-start.32 = (bf16[32,2048]{1,0:T(8,128)(2,1)S(1)}, bf16[32,2048]{1,0:T(8,128)(2,1)S(1)}, u32[]{:S(2)}, u32[]{:S(2)}) collective-permute-start(bf16[32,2048]{1,0:T(8,128)(2,1)S(1)} %collective-permute-done.25.refs_0_.refs_2_), channel_id=1, source_target_pairs={{0,2},{1,3},{2,0},{3,1},{4,6},{5,7},{6,4},{7,5},{8,10},{9,11},{10,... | collective-permute-start | bytes 393224 | tf_op jit(solution)/shard_map/ppermute | solution.py:50
  74.9 2.6 %shard_map.70 = (f32[64,2048]{1,0:T(8,128)S(1)}, f32[64,2048]{1,0:T(8,128)S(1)}, bf16[64,2048]{1,0:T(8,128)(2,1)S(1)}, bf16[32,2048]{1,0:T(8,128)(2,1)S(1)}, bf16[32,2048]{1,0:T(8,128)(2,1)S(1)}) custom-call(bf16[32,2048]{1,0:T(8,128)(2,1)S(1)} %collective-permute-done.25.refs_0_.refs_2_, bf16[64,2048]{1,0:T(8,128)(2,1)S(1)} %shard_map.68.refs_0_.refs_1_, ...), custom_call_target="tpu_custom_call" | custom-call | tf_op jit(solution)/shard_map/pallas_call | solution.py:28
  78.6 0.4 collective-permute-done.32.refs_4_
  79.0 0.5 collective-permute-start.36
  79.5 0.8 collective-permute-done.31.refs_2_
  80.5 2.6 %shard_map.72 = (f32[64,2048]{1,0:T(8,128)S(1)}, f32[64,2048]{1,0:T(8,128)S(1)}, bf16[64,2048]{1,0:T(8,128)(2,1)S(1)}, bf16[32,2048]{1,0:T(8,128)(2,1)S(1)}, bf16[32,2048]{1,0:T(8,128)(2,1)S(1)}) custom-call(bf16[64,2048]{1,0:T(8,128)(2,1)S(1)} %shard_map.71.refs_0_, bf16[32,2048]{1,0:T(8,128)(2,1)S(1)} %shard_map.69.refs_1_, ...), custom_call_target="tpu_custom_call" | custom-call | tf_op jit(solution)/shard_map/pallas_call | solution.py:28
  83.1 0.4 collective-permute-start.37
  83.7 0.8 collective-permute-done.37.refs_1_
  84.9 1.8 %collective-permute-start.40 = (bf16[64,2048]{1,0:T(8,128)(2,1)S(1)}, bf16[64,2048]{1,0:T(8,128)(2,1)S(1)}, u32[]{:S(2)}, u32[]{:S(2)}) collective-permute-start(bf16[64,2048]{1,0:T(8,128)(2,1)S(1)} %shard_map.73.refs_0_), channel_id=1, source_target_pairs={{0,2},{1,3},{2,0},{3,1},{4,6},{5,7},{6,4},{7,5},{8,10},{9,11},{10,... | collective-permute-start | bytes 786440 | tf_op jit(solution)/shard_map/ppermute | solution.py:50
  86.7 0.5 collective-permute-start.39
  87.2 6.1 %collective-permute-done.40.refs_2_ = bf16[64,2048]{1,0:T(8,128)(2,1)S(1)} collective-permute-done((bf16[64,2048]{1,0:T(8,128)(2,1)S(1)}, bf16[64,2048]{1,0:T(8,128)(2,1)S(1)}, u32[]{:S(2)}, u32[]{:S(2)}) %collective-permute-start.40) | collective-permute-done | bytes 262176 | tf_op jit(solution)/shard_map/ppermute | solution.py:50
  93.4 1.7 %collective-permute-start.41 = (bf16[64,2048]{1,0:T(8,128)(2,1)S(1)}, bf16[64,2048]{1,0:T(8,128)(2,1)S(1)}, u32[]{:S(2)}, u32[]{:S(2)}) collective-permute-start(bf16[64,2048]{1,0:T(8,128)(2,1)S(1)} %shard_map.71.refs_0_), channel_id=1, source_target_pairs={{0,2},{1,3},{2,0},{3,1},{4,6},{5,7},{6,4},{7,5},{8,10},{9,11},{10,... | collective-permute-start | bytes 786440 | tf_op jit(solution)/shard_map/ppermute | solution.py:50
  95.3 5.0 %collective-permute-done.44.refs_3_ = bf16[32,2048]{1,0:T(8,128)(2,1)S(1)} collective-permute-done((bf16[32,2048]{1,0:T(8,128)(2,1)S(1)}, bf16[32,2048]{1,0:T(8,128)(2,1)S(1)}, u32[]{:S(2)}, u32[]{:S(2)}) %collective-permute-start.44) | collective-permute-done | bytes 131104 | tf_op jit(solution)/shard_map/ppermute | solution.py:50
  100.3 0.4 collective-permute-start.45
  101.1 1.8 %collective-permute-start.42 = (bf16[32,2048]{1,0:T(8,128)(2,1)S(1)}, bf16[32,2048]{1,0:T(8,128)(2,1)S(1)}, u32[]{:S(2)}, u32[]{:S(2)}) collective-permute-start(bf16[32,2048]{1,0:T(8,128)(2,1)S(1)} %get-tuple-element.86), channel_id=1, source_target_pairs={{0,4},{1,5},{2,6},{3,7},{4,0},{5,1},{6,2},{7,3},{8,12},{9,13},{10,... | collective-permute-start | bytes 393224 | tf_op jit(solution)/shard_map/ppermute | solution.py:50
  102.9 4.7 %collective-permute-done.45.refs_3_ = bf16[32,2048]{1,0:T(8,128)(2,1)S(1)} collective-permute-done((bf16[32,2048]{1,0:T(8,128)(2,1)S(1)}, bf16[32,2048]{1,0:T(8,128)(2,1)S(1)}, u32[]{:S(2)}, u32[]{:S(2)}) %collective-permute-start.45) | collective-permute-done | bytes 131104 | tf_op jit(solution)/shard_map/ppermute | solution.py:50
  107.8 0.8 shard_map.77
  (71 shorter events, 6.1 us)
Async XLA Ops:
  1.2 9.4 %collective-permute-start = (bf16[32,2176]{1,0:T(8,128)(2,1)S(1)}, bf16[32,2176]{1,0:T(8,128)(2,1)S(1)}, u32[]{:S(2)}, u32[]{:S(2)}) collective-permute-start(bf16[32,2176]{1,0:T(8,128)(2,1)S(1)} %shard_map.56.refs_1_), channel_id=1, source_target_pairs={{0,4},{1,5},{2,6},{3,7},{4,0},{5,1},{6,2},{7,3},{8,12},{9,13},{10,... | collective-permute-start | bytes 417800 | tf_op jit(solution)/shard_map/ppermute | solution.py:50
  4.3 9.1 %collective-permute-start.1 = (bf16[32,2176]{1,0:T(8,128)(2,1)S(1)}, bf16[32,2176]{1,0:T(8,128)(2,1)S(1)}, u32[]{:S(2)}, u32[]{:S(2)}) collective-permute-start(bf16[32,2176]{1,0:T(8,128)(2,1)S(1)} %shard_map.56.refs_1_), channel_id=1, source_target_pairs={{0,8},{1,9},{2,10},{3,11},{4,12},{5,13},{6,14},{7,15},{8,0},{9,1},... | collective-permute-start | bytes 417800 | tf_op jit(solution)/shard_map/ppermute | solution.py:50
  10.7 10.9 %collective-permute-start.3 = (bf16[64,2176]{1,0:T(8,128)(2,1)S(1)}, bf16[64,2176]{1,0:T(8,128)(2,1)S(1)}, u32[]{:S(2)}, u32[]{:S(2)}) collective-permute-start(bf16[64,2176]{1,0:T(8,128)(2,1)S(1)} %shard_map.57.refs_0_.refs_1_), channel_id=1, source_target_pairs={{0,2},{1,3},{2,0},{3,1},{4,6},{5,7},{6,4},{7,5},{8,10},{9,11},{10,... | collective-permute-start | bytes 835592 | tf_op jit(solution)/shard_map/ppermute | solution.py:50
  13.4 8.2 %collective-permute-start.4 = (bf16[32,2176]{1,0:T(8,128)(2,1)S(1)}, bf16[32,2176]{1,0:T(8,128)(2,1)S(1)}, u32[]{:S(2)}, u32[]{:S(2)}) collective-permute-start(bf16[32,2176]{1,0:T(8,128)(2,1)S(1)} %shard_map.58.refs_1_), channel_id=1, source_target_pairs={{0,2},{1,3},{2,0},{3,1},{4,6},{5,7},{6,4},{7,5},{8,10},{9,11},{10,... | collective-permute-start | bytes 417800 | tf_op jit(solution)/shard_map/ppermute | solution.py:50
  15.0 6.6 %collective-permute-start.2 = (bf16[32,2176]{1,0:T(8,128)(2,1)S(1)}, bf16[32,2176]{1,0:T(8,128)(2,1)S(1)}, u32[]{:S(2)}, u32[]{:S(2)}) collective-permute-start(bf16[32,2176]{1,0:T(8,128)(2,1)S(1)} %shard_map.58.refs_1_), channel_id=1, source_target_pairs={{0,4},{1,5},{2,6},{3,7},{4,0},{5,1},{6,2},{7,3},{8,12},{9,13},{10,... | collective-permute-start | bytes 417800 | tf_op jit(solution)/shard_map/ppermute | solution.py:50
  15.4 7.8 %collective-permute-start.5 = (bf16[64,2176]{1,0:T(8,128)(2,1)S(1)}, bf16[64,2176]{1,0:T(8,128)(2,1)S(1)}, u32[]{:S(2)}, u32[]{:S(2)}) collective-permute-start(bf16[64,2176]{1,0:T(8,128)(2,1)S(1)} %shard_map.57.refs_0_.refs_1_), channel_id=1, source_target_pairs={{0,1},{1,0},{2,3},{3,2},{4,5},{5,4},{6,7},{7,6},{8,9},{9,8},{10,11... | collective-permute-start | bytes 835592 | tf_op jit(solution)/shard_map/ppermute | solution.py:50
  21.6 1.6 %collective-permute-start.6 = (bf16[64,2176]{1,0:T(8,128)(2,1)S(1)}, bf16[64,2176]{1,0:T(8,128)(2,1)S(1)}, u32[]{:S(2)}, u32[]{:S(2)}) collective-permute-start(bf16[64,2176]{1,0:T(8,128)(2,1)S(1)} %collective-permute-done.3.refs_2_), channel_id=1, source_target_pairs={{0,1},{1,0},{2,3},{3,2},{4,5},{5,4},{6,7},{7,6},{8,9},{9,8},{10,11... | collective-permute-start | bytes 835592 | tf_op jit(solution)/shard_map/ppermute | solution.py:50
  21.6 6.1 %collective-permute-start.9 = (bf16[32,2176]{1,0:T(8,128)(2,1)S(1)}, bf16[32,2176]{1,0:T(8,128)(2,1)S(1)}, u32[]{:S(2)}, u32[]{:S(2)}) collective-permute-start(bf16[32,2176]{1,0:T(8,128)(2,1)S(1)} %collective-permute-done.2.refs_0_.refs_2_), channel_id=1, source_target_pairs={{0,2},{1,3},{2,0},{3,1},{4,6},{5,7},{6,4},{7,5},{8,10},{9,11},{10,... | collective-permute-start | bytes 417800 | tf_op jit(solution)/shard_map/ppermute | solution.py:50
  25.8 1.9 %collective-permute-start.7 = (bf16[32,2048]{1,0:T(8,128)(2,1)S(1)}, bf16[32,2048]{1,0:T(8,128)(2,1)S(1)}, u32[]{:S(2)}, u32[]{:S(2)}) collective-permute-start(bf16[32,2048]{1,0:T(8,128)(2,1)S(1)} %get-tuple-element.52), channel_id=1, source_target_pairs={{0,1},{1,0},{2,3},{3,2},{4,5},{5,4},{6,7},{7,6},{8,9},{9,8},{10,11... | collective-permute-start | bytes 393224 | tf_op jit(solution)/shard_map/ppermute | solution.py:50
  26.0 3.3 %collective-permute-start.10 = (bf16[32,2176]{1,0:T(8,128)(2,1)S(1)}, bf16[32,2176]{1,0:T(8,128)(2,1)S(1)}, u32[]{:S(2)}, u32[]{:S(2)}) collective-permute-start(bf16[32,2176]{1,0:T(8,128)(2,1)S(1)} %shard_map.58.refs_1_), channel_id=1, source_target_pairs={{0,1},{1,0},{2,3},{3,2},{4,5},{5,4},{6,7},{7,6},{8,9},{9,8},{10,11... | collective-permute-start | bytes 417800 | tf_op jit(solution)/shard_map/ppermute | solution.py:50
  26.4 2.9 %collective-permute-start.12 = (bf16[32,2176]{1,0:T(8,128)(2,1)S(1)}, bf16[32,2176]{1,0:T(8,128)(2,1)S(1)}, u32[]{:S(2)}, u32[]{:S(2)}) collective-permute-start(bf16[32,2176]{1,0:T(8,128)(2,1)S(1)} %collective-permute-done.4.refs_3_), channel_id=1, source_target_pairs={{0,1},{1,0},{2,3},{3,2},{4,5},{5,4},{6,7},{7,6},{8,9},{9,8},{10,11... | collective-permute-start | bytes 417800 | tf_op jit(solution)/shard_map/ppermute | solution.py:50
  26.6 2.8 %collective-permute-start.11 = (bf16[32,2176]{1,0:T(8,128)(2,1)S(1)}, bf16[32,2176]{1,0:T(8,128)(2,1)S(1)}, u32[]{:S(2)}, u32[]{:S(2)}) collective-permute-start(bf16[32,2176]{1,0:T(8,128)(2,1)S(1)} %collective-permute-done.2.refs_0_.refs_2_), channel_id=1, source_target_pairs={{0,1},{1,0},{2,3},{3,2},{4,5},{5,4},{6,7},{7,6},{8,9},{9,8},{10,11... | collective-permute-start | bytes 417800 | tf_op jit(solution)/shard_map/ppermute | solution.py:50
  27.7 1.6 %collective-permute-start.13 = (bf16[32,2176]{1,0:T(8,128)(2,1)S(1)}, bf16[32,2176]{1,0:T(8,128)(2,1)S(1)}, u32[]{:S(2)}, u32[]{:S(2)}) collective-permute-start(bf16[32,2176]{1,0:T(8,128)(2,1)S(1)} %collective-permute-done.9.refs_4_), channel_id=1, source_target_pairs={{0,1},{1,0},{2,3},{3,2},{4,5},{5,4},{6,7},{7,6},{8,9},{9,8},{10,11... | collective-permute-start | bytes 417800 | tf_op jit(solution)/shard_map/ppermute | solution.py:50
  27.7 1.5 %collective-permute-start.8 = (bf16[32,2048]{1,0:T(8,128)(2,1)S(1)}, bf16[32,2048]{1,0:T(8,128)(2,1)S(1)}, u32[]{:S(2)}, u32[]{:S(2)}) collective-permute-start(bf16[32,2048]{1,0:T(8,128)(2,1)S(1)} %get-tuple-element.53), channel_id=1, source_target_pairs={{0,1},{1,0},{2,3},{3,2},{4,5},{5,4},{6,7},{7,6},{8,9},{9,8},{10,11... | collective-permute-start | bytes 393224 | tf_op jit(solution)/shard_map/ppermute | solution.py:50
  32.0 1.4 %collective-permute-start.14 = (bf16[32,2048]{1,0:T(8,128)(2,1)S(1)}, bf16[32,2048]{1,0:T(8,128)(2,1)S(1)}, u32[]{:S(2)}, u32[]{:S(2)}) collective-permute-start(bf16[32,2048]{1,0:T(8,128)(2,1)S(1)} %get-tuple-element.60), channel_id=1, source_target_pairs={{0,1},{1,0},{2,3},{3,2},{4,5},{5,4},{6,7},{7,6},{8,9},{9,8},{10,11... | collective-permute-start | bytes 393224 | tf_op jit(solution)/shard_map/ppermute | solution.py:50
  32.3 1.3 %collective-permute-start.15 = (bf16[32,2048]{1,0:T(8,128)(2,1)S(1)}, bf16[32,2048]{1,0:T(8,128)(2,1)S(1)}, u32[]{:S(2)}, u32[]{:S(2)}) collective-permute-start(bf16[32,2048]{1,0:T(8,128)(2,1)S(1)} %get-tuple-element.61), channel_id=1, source_target_pairs={{0,1},{1,0},{2,3},{3,2},{4,5},{5,4},{6,7},{7,6},{8,9},{9,8},{10,11... | collective-permute-start | bytes 393224 | tf_op jit(solution)/shard_map/ppermute | solution.py:50
  33.7 8.5 %collective-permute-start.17 = (bf16[64,2048]{1,0:T(8,128)(2,1)S(1)}, bf16[64,2048]{1,0:T(8,128)(2,1)S(1)}, u32[]{:S(2)}, u32[]{:S(2)}) collective-permute-start(bf16[64,2048]{1,0:T(8,128)(2,1)S(1)} %shard_map.63.refs_0_), channel_id=1, source_target_pairs={{0,2},{1,3},{2,0},{3,1},{4,6},{5,7},{6,4},{7,5},{8,10},{9,11},{10,... | collective-permute-start | bytes 786440 | tf_op jit(solution)/shard_map/ppermute | solution.py:50
  35.3 8.4 %collective-permute-start.20 = (bf16[64,2048]{1,0:T(8,128)(2,1)S(1)}, bf16[64,2048]{1,0:T(8,128)(2,1)S(1)}, u32[]{:S(2)}, u32[]{:S(2)}) collective-permute-start(bf16[64,2048]{1,0:T(8,128)(2,1)S(1)} %get-tuple-element.66), channel_id=1, source_target_pairs={{0,1},{1,0},{2,3},{3,2},{4,5},{5,4},{6,7},{7,6},{8,9},{9,8},{10,11... | collective-permute-start | bytes 786440 | tf_op jit(solution)/shard_map/ppermute | solution.py:50
  35.3 14.7 %collective-permute-start.16 = (bf16[64,2048]{1,0:T(8,128)(2,1)S(1)}, bf16[64,2048]{1,0:T(8,128)(2,1)S(1)}, u32[]{:S(2)}, u32[]{:S(2)}) collective-permute-start(bf16[64,2048]{1,0:T(8,128)(2,1)S(1)} %get-tuple-element.62), channel_id=1, source_target_pairs={{0,1},{1,0},{2,3},{3,2},{4,5},{5,4},{6,7},{7,6},{8,9},{9,8},{10,11... | collective-permute-start | bytes 786440 | tf_op jit(solution)/shard_map/ppermute | solution.py:50
  42.2 7.8 %collective-permute-start.18 = (bf16[64,2048]{1,0:T(8,128)(2,1)S(1)}, bf16[64,2048]{1,0:T(8,128)(2,1)S(1)}, u32[]{:S(2)}, u32[]{:S(2)}) collective-permute-start(bf16[64,2048]{1,0:T(8,128)(2,1)S(1)} %shard_map.60.refs_0_), channel_id=1, source_target_pairs={{0,2},{1,3},{2,0},{3,1},{4,6},{5,7},{6,4},{7,5},{8,10},{9,11},{10,... | collective-permute-start | bytes 786440 | tf_op jit(solution)/shard_map/ppermute | solution.py:50
  43.8 5.0 %collective-permute-start.21 = (bf16[32,2048]{1,0:T(8,128)(2,1)S(1)}, bf16[32,2048]{1,0:T(8,128)(2,1)S(1)}, u32[]{:S(2)}, u32[]{:S(2)}) collective-permute-start(bf16[32,2048]{1,0:T(8,128)(2,1)S(1)} %shard_map.65), channel_id=1, source_target_pairs={{0,4},{1,5},{2,6},{3,7},{4,0},{5,1},{6,2},{7,3},{8,12},{9,13},{10,... | collective-permute-start | bytes 393224 | tf_op jit(solution)/shard_map/ppermute | solution.py:50
  48.9 7.4 %collective-permute-start.22 = (bf16[32,2048]{1,0:T(8,128)(2,1)S(1)}, bf16[32,2048]{1,0:T(8,128)(2,1)S(1)}, u32[]{:S(2)}, u32[]{:S(2)}) collective-permute-start(bf16[32,2048]{1,0:T(8,128)(2,1)S(1)} %shard_map.66), channel_id=1, source_target_pairs={{0,8},{1,9},{2,10},{3,11},{4,12},{5,13},{6,14},{7,15},{8,0},{9,1},... | collective-permute-start | bytes 393224 | tf_op jit(solution)/shard_map/ppermute | solution.py:50
  50.1 6.5 %copy-start = (bf16[2,16,2048]{2,1,0:T(8,128)(2,1)S(1)}, bf16[2,16,2048]{2,1,0:T(8,128)(2,1)}, u32[]{:S(2)}) copy-start(bf16[2,16,2048]{2,1,0:T(8,128)(2,1)} %param.5) | copy-start | bytes 393220
  50.1 6.5 %copy-start.1 = (f32[2,2048]{1,0:T(2,128)S(1)}, f32[2,2048]{1,0:T(2,128)}, u32[]{:S(2)}) copy-start(f32[2,2048]{1,0:T(2,128)} %refs_2_.5) | copy-start | bytes 49156
  50.1 6.5 %collective-permute-start.19 = (bf16[32,2048]{1,0:T(8,128)(2,1)S(1)}, bf16[32,2048]{1,0:T(8,128)(2,1)S(1)}, u32[]{:S(2)}, u32[]{:S(2)}) collective-permute-start(bf16[32,2048]{1,0:T(8,128)(2,1)S(1)} %get-tuple-element.65), channel_id=1, source_target_pairs={{0,4},{1,5},{2,6},{3,7},{4,0},{5,1},{6,2},{7,3},{8,12},{9,13},{10,... | collective-permute-start | bytes 393224 | tf_op jit(solution)/shard_map/ppermute | solution.py:50
  56.8 6.3 %collective-permute-start.23 = (bf16[32,2048]{1,0:T(8,128)(2,1)S(1)}, bf16[32,2048]{1,0:T(8,128)(2,1)S(1)}, u32[]{:S(2)}, u32[]{:S(2)}) collective-permute-start(bf16[32,2048]{1,0:T(8,128)(2,1)S(1)} %get-tuple-element.68.refs_1_), channel_id=1, source_target_pairs={{0,4},{1,5},{2,6},{3,7},{4,0},{5,1},{6,2},{7,3},{8,12},{9,13},{10,... | collective-permute-start | bytes 393224 | tf_op jit(solution)/shard_map/ppermute | solution.py:50
  57.5 8.2 %collective-permute-start.24 = (bf16[32,2048]{1,0:T(8,128)(2,1)S(1)}, bf16[32,2048]{1,0:T(8,128)(2,1)S(1)}, u32[]{:S(2)}, u32[]{:S(2)}) collective-permute-start(bf16[32,2048]{1,0:T(8,128)(2,1)S(1)} %get-tuple-element.68.refs_1_), channel_id=1, source_target_pairs={{0,8},{1,9},{2,10},{3,11},{4,12},{5,13},{6,14},{7,15},{8,0},{9,1},... | collective-permute-start | bytes 393224 | tf_op jit(solution)/shard_map/ppermute | solution.py:50
  63.2 9.9 %collective-permute-start.26 = (bf16[64,2048]{1,0:T(8,128)(2,1)S(1)}, bf16[64,2048]{1,0:T(8,128)(2,1)S(1)}, u32[]{:S(2)}, u32[]{:S(2)}) collective-permute-start(bf16[64,2048]{1,0:T(8,128)(2,1)S(1)} %shard_map.68.refs_0_.refs_1_), channel_id=1, source_target_pairs={{0,2},{1,3},{2,0},{3,1},{4,6},{5,7},{6,4},{7,5},{8,10},{9,11},{10,... | collective-permute-start | bytes 786440 | tf_op jit(solution)/shard_map/ppermute | solution.py:50
  65.6 7.4 %collective-permute-start.27 = (bf16[32,2048]{1,0:T(8,128)(2,1)S(1)}, bf16[32,2048]{1,0:T(8,128)(2,1)S(1)}, u32[]{:S(2)}, u32[]{:S(2)}) collective-permute-start(bf16[32,2048]{1,0:T(8,128)(2,1)S(1)} %shard_map.69.refs_1_), channel_id=1, source_target_pairs={{0,2},{1,3},{2,0},{3,1},{4,6},{5,7},{6,4},{7,5},{8,10},{9,11},{10,... | collective-permute-start | bytes 393224 | tf_op jit(solution)/shard_map/ppermute | solution.py:50
  67.0 6.1 %collective-permute-start.25 = (bf16[32,2048]{1,0:T(8,128)(2,1)S(1)}, bf16[32,2048]{1,0:T(8,128)(2,1)S(1)}, u32[]{:S(2)}, u32[]{:S(2)}) collective-permute-start(bf16[32,2048]{1,0:T(8,128)(2,1)S(1)} %shard_map.69.refs_1_), channel_id=1, source_target_pairs={{0,4},{1,5},{2,6},{3,7},{4,0},{5,1},{6,2},{7,3},{8,12},{9,13},{10,... | collective-permute-start | bytes 393224 | tf_op jit(solution)/shard_map/ppermute | solution.py:50
  67.2 7.7 %collective-permute-start.28 = (bf16[64,2048]{1,0:T(8,128)(2,1)S(1)}, bf16[64,2048]{1,0:T(8,128)(2,1)S(1)}, u32[]{:S(2)}, u32[]{:S(2)}) collective-permute-start(bf16[64,2048]{1,0:T(8,128)(2,1)S(1)} %shard_map.68.refs_0_.refs_1_), channel_id=1, source_target_pairs={{0,1},{1,0},{2,3},{3,2},{4,5},{5,4},{6,7},{7,6},{8,9},{9,8},{10,11... | collective-permute-start | bytes 786440 | tf_op jit(solution)/shard_map/ppermute | solution.py:50
  73.1 1.8 %collective-permute-start.29 = (bf16[64,2048]{1,0:T(8,128)(2,1)S(1)}, bf16[64,2048]{1,0:T(8,128)(2,1)S(1)}, u32[]{:S(2)}, u32[]{:S(2)}) collective-permute-start(bf16[64,2048]{1,0:T(8,128)(2,1)S(1)} %collective-permute-done.26.refs_2_), channel_id=1, source_target_pairs={{0,1},{1,0},{2,3},{3,2},{4,5},{5,4},{6,7},{7,6},{8,9},{9,8},{10,11... | collective-permute-start | bytes 786440 | tf_op jit(solution)/shard_map/ppermute | solution.py:50
  73.1 5.9 %collective-permute-start.32 = (bf16[32,2048]{1,0:T(8,128)(2,1)S(1)}, bf16[32,2048]{1,0:T(8,128)(2,1)S(1)}, u32[]{:S(2)}, u32[]{:S(2)}) collective-permute-start(bf16[32,2048]{1,0:T(8,128)(2,1)S(1)} %collective-permute-done.25.refs_0_.refs_2_), channel_id=1, source_target_pairs={{0,2},{1,3},{2,0},{3,1},{4,6},{5,7},{6,4},{7,5},{8,10},{9,11},{10,... | collective-permute-start | bytes 393224 | tf_op jit(solution)/shard_map/ppermute | solution.py:50
  77.5 1.5 %collective-permute-start.30 = (bf16[32,2048]{1,0:T(8,128)(2,1)S(1)}, bf16[32,2048]{1,0:T(8,128)(2,1)S(1)}, u32[]{:S(2)}, u32[]{:S(2)}) collective-permute-start(bf16[32,2048]{1,0:T(8,128)(2,1)S(1)} %get-tuple-element.74), channel_id=1, source_target_pairs={{0,1},{1,0},{2,3},{3,2},{4,5},{5,4},{6,7},{7,6},{8,9},{9,8},{10,11... | collective-permute-start | bytes 393224 | tf_op jit(solution)/shard_map/ppermute | solution.py:50
  77.7 2.7 %collective-permute-start.33 = (bf16[32,2048]{1,0:T(8,128)(2,1)S(1)}, bf16[32,2048]{1,0:T(8,128)(2,1)S(1)}, u32[]{:S(2)}, u32[]{:S(2)}) collective-permute-start(bf16[32,2048]{1,0:T(8,128)(2,1)S(1)} %shard_map.69.refs_1_), channel_id=1, source_target_pairs={{0,1},{1,0},{2,3},{3,2},{4,5},{5,4},{6,7},{7,6},{8,9},{9,8},{10,11... | collective-permute-start | bytes 393224 | tf_op jit(solution)/shard_map/ppermute | solution.py:50
  78.1 2.3 %collective-permute-start.35 = (bf16[32,2048]{1,0:T(8,128)(2,1)S(1)}, bf16[32,2048]{1,0:T(8,128)(2,1)S(1)}, u32[]{:S(2)}, u32[]{:S(2)}) collective-permute-start(bf16[32,2048]{1,0:T(8,128)(2,1)S(1)} %collective-permute-done.27.refs_3_), channel_id=1, source_target_pairs={{0,1},{1,0},{2,3},{3,2},{4,5},{5,4},{6,7},{7,6},{8,9},{9,8},{10,11... | collective-permute-start | bytes 393224 | tf_op jit(solution)/shard_map/ppermute | solution.py:50
  78.2 2.2 %collective-permute-start.34 = (bf16[32,2048]{1,0:T(8,128)(2,1)S(1)}, bf16[32,2048]{1,0:T(8,128)(2,1)S(1)}, u32[]{:S(2)}, u32[]{:S(2)}) collective-permute-start(bf16[32,2048]{1,0:T(8,128)(2,1)S(1)} %collective-permute-done.25.refs_0_.refs_2_), channel_id=1, source_target_pairs={{0,1},{1,0},{2,3},{3,2},{4,5},{5,4},{6,7},{7,6},{8,9},{9,8},{10,11... | collective-permute-start | bytes 393224 | tf_op jit(solution)/shard_map/ppermute | solution.py:50
  79.0 1.3 %collective-permute-start.31 = (bf16[32,2048]{1,0:T(8,128)(2,1)S(1)}, bf16[32,2048]{1,0:T(8,128)(2,1)S(1)}, u32[]{:S(2)}, u32[]{:S(2)}) collective-permute-start(bf16[32,2048]{1,0:T(8,128)(2,1)S(1)} %get-tuple-element.75), channel_id=1, source_target_pairs={{0,1},{1,0},{2,3},{3,2},{4,5},{5,4},{6,7},{7,6},{8,9},{9,8},{10,11... | collective-permute-start | bytes 393224 | tf_op jit(solution)/shard_map/ppermute | solution.py:50
  79.0 1.5 %collective-permute-start.36 = (bf16[32,2048]{1,0:T(8,128)(2,1)S(1)}, bf16[32,2048]{1,0:T(8,128)(2,1)S(1)}, u32[]{:S(2)}, u32[]{:S(2)}) collective-permute-start(bf16[32,2048]{1,0:T(8,128)(2,1)S(1)} %collective-permute-done.32.refs_4_), channel_id=1, source_target_pairs={{0,1},{1,0},{2,3},{3,2},{4,5},{5,4},{6,7},{7,6},{8,9},{9,8},{10,11... | collective-permute-start | bytes 393224 | tf_op jit(solution)/shard_map/ppermute | solution.py:50
  83.1 1.4 %collective-permute-start.37 = (bf16[32,2048]{1,0:T(8,128)(2,1)S(1)}, bf16[32,2048]{1,0:T(8,128)(2,1)S(1)}, u32[]{:S(2)}, u32[]{:S(2)}) collective-permute-start(bf16[32,2048]{1,0:T(8,128)(2,1)S(1)} %get-tuple-element.81), channel_id=1, source_target_pairs={{0,1},{1,0},{2,3},{3,2},{4,5},{5,4},{6,7},{7,6},{8,9},{9,8},{10,11... | collective-permute-start | bytes 393224 | tf_op jit(solution)/shard_map/ppermute | solution.py:50
  83.5 1.3 %collective-permute-start.38 = (bf16[32,2048]{1,0:T(8,128)(2,1)S(1)}, bf16[32,2048]{1,0:T(8,128)(2,1)S(1)}, u32[]{:S(2)}, u32[]{:S(2)}) collective-permute-start(bf16[32,2048]{1,0:T(8,128)(2,1)S(1)} %get-tuple-element.82), channel_id=1, source_target_pairs={{0,1},{1,0},{2,3},{3,2},{4,5},{5,4},{6,7},{7,6},{8,9},{9,8},{10,11... | collective-permute-start | bytes 393224 | tf_op jit(solution)/shard_map/ppermute | solution.py:50
  84.9 8.5 %collective-permute-start.40 = (bf16[64,2048]{1,0:T(8,128)(2,1)S(1)}, bf16[64,2048]{1,0:T(8,128)(2,1)S(1)}, u32[]{:S(2)}, u32[]{:S(2)}) collective-permute-start(bf16[64,2048]{1,0:T(8,128)(2,1)S(1)} %shard_map.73.refs_0_), channel_id=1, source_target_pairs={{0,2},{1,3},{2,0},{3,1},{4,6},{5,7},{6,4},{7,5},{8,10},{9,11},{10,... | collective-permute-start | bytes 786440 | tf_op jit(solution)/shard_map/ppermute | solution.py:50
  86.7 8.4 %collective-permute-start.43 = (bf16[64,2048]{1,0:T(8,128)(2,1)S(1)}, bf16[64,2048]{1,0:T(8,128)(2,1)S(1)}, u32[]{:S(2)}, u32[]{:S(2)}) collective-permute-start(bf16[64,2048]{1,0:T(8,128)(2,1)S(1)} %get-tuple-element.88), channel_id=1, source_target_pairs={{0,1},{1,0},{2,3},{3,2},{4,5},{5,4},{6,7},{7,6},{8,9},{9,8},{10,11... | collective-permute-start | bytes 786440 | tf_op jit(solution)/shard_map/ppermute | solution.py:50
  86.7 13.9 %collective-permute-start.39 = (bf16[64,2048]{1,0:T(8,128)(2,1)S(1)}, bf16[64,2048]{1,0:T(8,128)(2,1)S(1)}, u32[]{:S(2)}, u32[]{:S(2)}) collective-permute-start(bf16[64,2048]{1,0:T(8,128)(2,1)S(1)} %get-tuple-element.83), channel_id=1, source_target_pairs={{0,1},{1,0},{2,3},{3,2},{4,5},{5,4},{6,7},{7,6},{8,9},{9,8},{10,11... | collective-permute-start | bytes 786440 | tf_op jit(solution)/shard_map/ppermute | solution.py:50
  93.4 7.6 %collective-permute-start.41 = (bf16[64,2048]{1,0:T(8,128)(2,1)S(1)}, bf16[64,2048]{1,0:T(8,128)(2,1)S(1)}, u32[]{:S(2)}, u32[]{:S(2)}) collective-permute-start(bf16[64,2048]{1,0:T(8,128)(2,1)S(1)} %shard_map.71.refs_0_), channel_id=1, source_target_pairs={{0,2},{1,3},{2,0},{3,1},{4,6},{5,7},{6,4},{7,5},{8,10},{9,11},{10,... | collective-permute-start | bytes 786440 | tf_op jit(solution)/shard_map/ppermute | solution.py:50
  95.2 5.0 %collective-permute-start.44 = (bf16[32,2048]{1,0:T(8,128)(2,1)S(1)}, bf16[32,2048]{1,0:T(8,128)(2,1)S(1)}, u32[]{:S(2)}, u32[]{:S(2)}) collective-permute-start(bf16[32,2048]{1,0:T(8,128)(2,1)S(1)} %shard_map.75), channel_id=1, source_target_pairs={{0,4},{1,5},{2,6},{3,7},{4,0},{5,1},{6,2},{7,3},{8,12},{9,13},{10,... | collective-permute-start | bytes 393224 | tf_op jit(solution)/shard_map/ppermute | solution.py:50
  100.3 7.2 %collective-permute-start.45 = (bf16[32,2048]{1,0:T(8,128)(2,1)S(1)}, bf16[32,2048]{1,0:T(8,128)(2,1)S(1)}, u32[]{:S(2)}, u32[]{:S(2)}) collective-permute-start(bf16[32,2048]{1,0:T(8,128)(2,1)S(1)} %shard_map.76), channel_id=1, source_target_pairs={{0,8},{1,9},{2,10},{3,11},{4,12},{5,13},{6,14},{7,15},{8,0},{9,1},... | collective-permute-start | bytes 393224 | tf_op jit(solution)/shard_map/ppermute | solution.py:50
  101.1 6.7 %collective-permute-start.42 = (bf16[32,2048]{1,0:T(8,128)(2,1)S(1)}, bf16[32,2048]{1,0:T(8,128)(2,1)S(1)}, u32[]{:S(2)}, u32[]{:S(2)}) collective-permute-start(bf16[32,2048]{1,0:T(8,128)(2,1)S(1)} %get-tuple-element.86), channel_id=1, source_target_pairs={{0,4},{1,5},{2,6},{3,7},{4,0},{5,1},{6,2},{7,3},{8,12},{9,13},{10,... | collective-permute-start | bytes 393224 | tf_op jit(solution)/shard_map/ppermute | solution.py:50

commit v13 on v11

--- a/solution.py
+++ b/solution.py
@@ -123,7 +123,7 @@
 def cross_rows(mine, near, beside):
     far, count = lax.axis_size("expert") // 4, len(beside)
     shape = beside[0].shape
-    arrived = []
+    hops, arrived = [], []
     if count > 1:
         hops = call(
             functools.partial(apart_kernel, 1, count - 1),
@@ -137,7 +137,7 @@
     (crossing,) = call(
         cross_kernel, [(shape, bf16)], [VMEM] * (3 + len(arrived)), mine, near, beside[0], *arrived
     )
-    return swap(crossing, 4, count, far, True)
+    return swap(crossing, 4, count, far, True), tuple(hops)
 
 
 def normed_rows(widened, gain_row):
@@ -346,13 +346,13 @@
 
     first_beside = held(first_beside, (second[-1], second_beside[0]))
     outs, first_columns = worked([first], [first_beside], routed[0], (second[-1],))
-    mine1, near1, leaving1 = leave_pair(outs, 1, ())
+    mine1, near1, leaving1 = leave_pair(outs, half, ())
     second_beside[-1] = held(second_beside[-1], outs[0])
     outs, second_columns = worked(second, second_beside, routed[1], tuple(leaving1))
     mine2, near2, leaving2 = leave_pair(outs, half, ())
     back2 = [swap(piece, 2, 1, 2, True) for piece in leaving2]
-    back1 = [swap(held(piece, back2[0]), 2, 1, 2, True) for piece in leaving1]
-    crossed_back = cross_rows(mine2, near2, back2)
+    crossed_back, hops = cross_rows(mine2, near2, back2)
+    back1 = [swap(held(piece, (back2[0], *hops)), 2, 1, 2, True) for piece in leaving1]
     pieces = call(
         functools.partial(apart_kernel, 0, half),
         [(rows.shape[:1] + mine1.shape[1:], bf16 if k else f32) for k in range(half)],

time: 106 us -> 105 us (level)
    ppermute x48 -> x50, waiting for transfers between devices: 50 us -> 49.2 us  [swap(): lax.ppermute(value, 'expert', [(i, partner(i)) for i in range(count)])]
    ppermute x48 -> x50, starting transfers between devices: 34.7 us -> 34.4 us  [swap(): lax.ppermute(value, 'expert', [(i, partner(i)) for i in range(count)])]
  transfers between devices with their start and end apart: 48 -> 50, of which waited for: 26 -> 26; matrix products, arithmetic and copies ran while one was open for 0% -> 0% of each run, Pallas kernels for 13% -> 13%
where the time goes in v13:
time: 105 us
  waiting for transfers between devices  49.2 us (47%)
  starting transfers between devices  34.4 us (33%)
  Pallas kernels  20.8 us (20%)
    ppermute x50, waiting for transfers between devices, swap(): lax.ppermute(value, 'expert', [(i, partner(i)) for i in range(count)])  49.2 us
    ppermute x50, starting transfers between devices, swap(): lax.ppermute(value, 'expert', [(i, partner(i)) for i in range(count)])  34.4 us
    pallas_call x23, Pallas kernels, call(): pl.pallas_call(lambda *refs: kernel(*refs[len(after):]), out_shape=shapes...  20.8 us
  transfers between devices with their start and end apart: 50, of which 26 were waited for; matrix products, arithmetic and copies ran while one was open for 0% of the time, Pallas kernels for 13%

profile of v13, /device:TPU:0, one launch (start us, length us, event | category | flops | bytes accessed | tf_op | source)
XLA Modules:
  0.0 104.7 jit_solution(10868873768707582193)
XLA Ops:
  0.0 1.2 %shard_map.56.refs_1_ = bf16[32,2176]{1,0:T(8,128)(2,1)S(1)} custom-call(bf16[32,2048]{1,0:T(8,128)(2,1)} %bitcast.2, s32[2,2,8,16]{3,2,1,0:T(8,128)} %bitcast.4, f32[2,2048]{1,0:T(2,128)} %refs_2_.5), custom_call_target="tpu_custom_call" | custom-call | tf_op jit(solution)/shard_map/pallas_call | solution.py:28
  1.2 3.1 %collective-permute-start = (bf16[32,2176]{1,0:T(8,128)(2,1)S(1)}, bf16[32,2176]{1,0:T(8,128)(2,1)S(1)}, u32[]{:S(2)}, u32[]{:S(2)}) collective-permute-start(bf16[32,2176]{1,0:T(8,128)(2,1)S(1)} %shard_map.56.refs_1_), channel_id=1, source_target_pairs={{0,4},{1,5},{2,6},{3,7},{4,0},{5,1},{6,2},{7,3},{8,12},{9,13},{10,... | collective-permute-start | bytes 417800 | tf_op jit(solution)/shard_map/ppermute | solution.py:50
  4.3 2.6 %collective-permute-start.1 = (bf16[32,2176]{1,0:T(8,128)(2,1)S(1)}, bf16[32,2176]{1,0:T(8,128)(2,1)S(1)}, u32[]{:S(2)}, u32[]{:S(2)}) collective-permute-start(bf16[32,2176]{1,0:T(8,128)(2,1)S(1)} %shard_map.56.refs_1_), channel_id=1, source_target_pairs={{0,8},{1,9},{2,10},{3,11},{4,12},{5,13},{6,14},{7,15},{8,0},{9,1},... | collective-permute-start | bytes 417800 | tf_op jit(solution)/shard_map/ppermute | solution.py:50
  6.9 3.7 %shard_map.55 = (bf16[2048,1536]{1,0:T(8,128)(2,1)S(1)}, bf16[768,2048]{1,0:T(8,128)(2,1)S(1)}, f32[8,128]{1,0:T(8,128)S(1)}) custom-call(bf16[2,1,2048,1536]{3,2,1,0:T(8,128)(2,1)} %refs_1_.3, bf16[2,1,768,2048]{3,2,1,0:T(8,128)(2,1)} %refs_2_.4), custom_call_target="tpu_custom_call" | custom-call | tf_op jit(solution)/shard_map/pallas_call | solution.py:28
  10.7 1.6 %collective-permute-start.3 = (bf16[64,2176]{1,0:T(8,128)(2,1)S(1)}, bf16[64,2176]{1,0:T(8,128)(2,1)S(1)}, u32[]{:S(2)}, u32[]{:S(2)}) collective-permute-start(bf16[64,2176]{1,0:T(8,128)(2,1)S(1)} %shard_map.57.refs_0_.refs_1_), channel_id=1, source_target_pairs={{0,2},{1,3},{2,0},{3,1},{4,6},{5,7},{6,4},{7,5},{8,10},{9,11},{10,... | collective-permute-start | bytes 835592 | tf_op jit(solution)/shard_map/ppermute | solution.py:50
  12.3 1.1 %collective-permute-done.1.refs_1_ = bf16[32,2176]{1,0:T(8,128)(2,1)S(1)} collective-permute-done((bf16[32,2176]{1,0:T(8,128)(2,1)S(1)}, bf16[32,2176]{1,0:T(8,128)(2,1)S(1)}, u32[]{:S(2)}, u32[]{:S(2)}) %collective-permute-start.1) | collective-permute-done | bytes 139296 | tf_op jit(solution)/shard_map/ppermute | solution.py:50
  13.4 1.6 %collective-permute-start.4 = (bf16[32,2176]{1,0:T(8,128)(2,1)S(1)}, bf16[32,2176]{1,0:T(8,128)(2,1)S(1)}, u32[]{:S(2)}, u32[]{:S(2)}) collective-permute-start(bf16[32,2176]{1,0:T(8,128)(2,1)S(1)} %shard_map.58.refs_2_), channel_id=1, source_target_pairs={{0,2},{1,3},{2,0},{3,1},{4,6},{5,7},{6,4},{7,5},{8,10},{9,11},{10,... | collective-permute-start | bytes 417800 | tf_op jit(solution)/shard_map/ppermute | solution.py:50
  15.4 6.2 %collective-permute-done.4.refs_4_ = bf16[32,2176]{1,0:T(8,128)(2,1)S(1)} collective-permute-done((bf16[32,2176]{1,0:T(8,128)(2,1)S(1)}, bf16[32,2176]{1,0:T(8,128)(2,1)S(1)}, u32[]{:S(2)}, u32[]{:S(2)}) %collective-permute-start.4) | collective-permute-done | bytes 139296 | tf_op jit(solution)/shard_map/ppermute | solution.py:50
  21.6 1.6 %collective-permute-start.9 = (bf16[32,2176]{1,0:T(8,128)(2,1)S(1)}, bf16[32,2176]{1,0:T(8,128)(2,1)S(1)}, u32[]{:S(2)}, u32[]{:S(2)}) collective-permute-start(bf16[32,2176]{1,0:T(8,128)(2,1)S(1)} %collective-permute-done.2.refs_0_.refs_3_), channel_id=1, source_target_pairs={{0,2},{1,3},{2,0},{3,1},{4,6},{5,7},{6,4},{7,5},{8,10},{9,11},{10,... | collective-permute-start | bytes 417800 | tf_op jit(solution)/shard_map/ppermute | solution.py:50
  23.2 2.6 %shard_map.59 = (f32[64,2048]{1,0:T(8,128)S(1)}, f32[64,2048]{1,0:T(8,128)S(1)}, bf16[64,2048]{1,0:T(8,128)(2,1)S(1)}, bf16[32,2048]{1,0:T(8,128)(2,1)S(1)}, bf1...) custom-call(bf16[32,2176]{1,0:T(8,128)(2,1)S(1)} %collective-permute-done.2.refs_0_.refs_3_, ...), custom_call_target="tpu_custom_call" | custom-call | tf_op jit(solution)/shard_map/pallas_call | solution.py:28
  26.9 0.8 collective-permute-done.9.refs_5_
  28.2 1.0 collective-permute-done.8.refs_2_
  29.3 2.6 %shard_map.61 = (f32[64,2048]{1,0:T(8,128)S(1)}, f32[64,2048]{1,0:T(8,128)S(1)}, bf16[64,2048]{1,0:T(8,128)(2,1)S(1)}, bf16[32,2048]{1,0:T(8,128)(2,1)S(1)}, bf1...) custom-call(bf16[32,2048]{1,0:T(8,128)(2,1)S(1)} %get-tuple-element.78.refs_0_, ...), custom_call_target="tpu_custom_call" | custom-call | tf_op jit(solution)/shard_map/pallas_call | solution.py:28
  32.9 0.5 collective-permute-done.14.refs_1_
  33.7 1.6 %collective-permute-start.19 = (bf16[32,2048]{1,0:T(8,128)(2,1)S(1)}, bf16[32,2048]{1,0:T(8,128)(2,1)S(1)}, u32[]{:S(2)}, u32[]{:S(2)}) collective-permute-start(bf16[32,2048]{1,0:T(8,128)(2,1)S(1)} %get-tuple-element.75.refs_1_), channel_id=1, source_target_pairs={{0,2},{1,3},{2,0},{3,1},{4,6},{5,7},{6,4},{7,5},{8,10},{9,11},{10,... | collective-permute-start | bytes 393224 | tf_op jit(solution)/shard_map/ppermute | solution.py:50
  35.8 4.3 %collective-permute-done.19.refs_2_ = bf16[32,2048]{1,0:T(8,128)(2,1)S(1)} collective-permute-done((bf16[32,2048]{1,0:T(8,128)(2,1)S(1)}, bf16[32,2048]{1,0:T(8,128)(2,1)S(1)}, u32[]{:S(2)}, u32[]{:S(2)}) %collective-permute-start.19) | collective-permute-done | bytes 131104 | tf_op jit(solution)/shard_map/ppermute | solution.py:50
  40.2 0.5 collective-permute-start.23
  40.7 1.5 %collective-permute-done.17.refs_2_ = bf16[32,2048]{1,0:T(8,128)(2,1)S(1)} collective-permute-done((bf16[32,2048]{1,0:T(8,128)(2,1)S(1)}, bf16[32,2048]{1,0:T(8,128)(2,1)S(1)}, u32[]{:S(2)}, u32[]{:S(2)}) %collective-permute-start.17) | collective-permute-done | bytes 131104 | tf_op jit(solution)/shard_map/ppermute | solution.py:50
  42.2 1.5 %collective-permute-start.20 = (bf16[32,2048]{1,0:T(8,128)(2,1)S(1)}, bf16[32,2048]{1,0:T(8,128)(2,1)S(1)}, u32[]{:S(2)}, u32[]{:S(2)}) collective-permute-start(bf16[32,2048]{1,0:T(8,128)(2,1)S(1)} %get-tuple-element.78.refs_0_), channel_id=1, source_target_pairs={{0,2},{1,3},{2,0},{3,1},{4,6},{5,7},{6,4},{7,5},{8,10},{9,11},{10,... | collective-permute-start | bytes 393224 | tf_op jit(solution)/shard_map/ppermute | solution.py:50
  44.2 1.0 collective-permute-done.23.refs_3_
  45.3 1.1 %collective-permute-start.24 = (bf16[32,2048]{1,0:T(8,128)(2,1)S(1)}, bf16[32,2048]{1,0:T(8,128)(2,1)S(1)}, u32[]{:S(2)}, u32[]{:S(2)}) collective-permute-start(bf16[32,2048]{1,0:T(8,128)(2,1)S(1)} %shard_map.66), channel_id=1, source_target_pairs={{0,8},{1,9},{2,10},{3,11},{4,12},{5,13},{6,14},{7,15},{8,0},{9,1},... | collective-permute-start | bytes 393224 | tf_op jit(solution)/shard_map/ppermute | solution.py:50
  46.4 2.0 %collective-permute-done.20.refs_4_ = bf16[32,2048]{1,0:T(8,128)(2,1)S(1)} collective-permute-done((bf16[32,2048]{1,0:T(8,128)(2,1)S(1)}, bf16[32,2048]{1,0:T(8,128)(2,1)S(1)}, u32[]{:S(2)}, u32[]{:S(2)}) %collective-permute-start.20) | collective-permute-done | bytes 131104 | tf_op jit(solution)/shard_map/ppermute | solution.py:50
  48.4 1.4 %collective-permute-done.21.refs_5_ = bf16[32,2048]{1,0:T(8,128)(2,1)S(1)} collective-permute-done((bf16[32,2048]{1,0:T(8,128)(2,1)S(1)}, bf16[32,2048]{1,0:T(8,128)(2,1)S(1)}, u32[]{:S(2)}, u32[]{:S(2)}) %collective-permute-start.21) | collective-permute-done | bytes 131104 | tf_op jit(solution)/shard_map/ppermute | solution.py:50
  49.9 0.5 collective-permute-start.22
  50.4 3.7 %shard_map.62 = (bf16[2048,1536]{1,0:T(8,128)(2,1)S(1)}, bf16[768,2048]{1,0:T(8,128)(2,1)S(1)}, f32[8,128]{1,0:T(8,128)S(1)}) custom-call(f32[64,2048]{1,0:T(8,128)S(1)} %get-tuple-element.69.refs_0_, bf16[2,1,2048,1536]{3,2,1,0:T(8,128)(2,1)} %refs_1_.3, bf16[2,1,768,2048]{3,2,1,0:T(8,128)(2,1)} %refs_2_.4), custom_call_target="tpu_custom_call" | custom-call | tf_op jit(solution)/shard_map/pallas_call | solution.py:28
  54.2 0.9 collective-permute-done.22.refs_4_
  55.3 0.7 collective-permute-start.25
  56.1 2.2 %collective-permute-start.26 = (bf16[32,2048]{1,0:T(8,128)(2,1)S(1)}, bf16[32,2048]{1,0:T(8,128)(2,1)S(1)}, u32[]{:S(2)}, u32[]{:S(2)}) collective-permute-start(bf16[32,2048]{1,0:T(8,128)(2,1)S(1)} %get-tuple-element.83.refs_1_), channel_id=1, source_target_pairs={{0,8},{1,9},{2,10},{3,11},{4,12},{5,13},{6,14},{7,15},{8,0},{9,1},... | collective-permute-start | bytes 393224 | tf_op jit(solution)/shard_map/ppermute | solution.py:50
  58.3 3.9 %collective-permute-done.25.refs_2_ = bf16[32,2048]{1,0:T(8,128)(2,1)S(1)} collective-permute-done((bf16[32,2048]{1,0:T(8,128)(2,1)S(1)}, bf16[32,2048]{1,0:T(8,128)(2,1)S(1)}, u32[]{:S(2)}, u32[]{:S(2)}) %collective-permute-start.25) | collective-permute-done | bytes 131104 | tf_op jit(solution)/shard_map/ppermute | solution.py:50
  62.2 1.6 %collective-permute-start.28 = (bf16[64,2048]{1,0:T(8,128)(2,1)S(1)}, bf16[64,2048]{1,0:T(8,128)(2,1)S(1)}, u32[]{:S(2)}, u32[]{:S(2)}) collective-permute-start(bf16[64,2048]{1,0:T(8,128)(2,1)S(1)} %shard_map.68.refs_0_.refs_1_), channel_id=1, source_target_pairs={{0,2},{1,3},{2,0},{3,1},{4,6},{5,7},{6,4},{7,5},{8,10},{9,11},{10,... | collective-permute-start | bytes 786440 | tf_op jit(solution)/shard_map/ppermute | solution.py:50
  63.8 1.3 %collective-permute-start.29 = (bf16[32,2048]{1,0:T(8,128)(2,1)S(1)}, bf16[32,2048]{1,0:T(8,128)(2,1)S(1)}, u32[]{:S(2)}, u32[]{:S(2)}) collective-permute-start(bf16[32,2048]{1,0:T(8,128)(2,1)S(1)} %shard_map.69.refs_2_), channel_id=1, source_target_pairs={{0,2},{1,3},{2,0},{3,1},{4,6},{5,7},{6,4},{7,5},{8,10},{9,11},{10,... | collective-permute-start | bytes 393224 | tf_op jit(solution)/shard_map/ppermute | solution.py:50
  65.4 5.4 %collective-permute-done.29.refs_4_ = bf16[32,2048]{1,0:T(8,128)(2,1)S(1)} collective-permute-done((bf16[32,2048]{1,0:T(8,128)(2,1)S(1)}, bf16[32,2048]{1,0:T(8,128)(2,1)S(1)}, u32[]{:S(2)}, u32[]{:S(2)}) %collective-permute-start.29) | collective-permute-done | bytes 131104 | tf_op jit(solution)/shard_map/ppermute | solution.py:50
  70.9 1.6 %collective-permute-start.34 = (bf16[32,2048]{1,0:T(8,128)(2,1)S(1)}, bf16[32,2048]{1,0:T(8,128)(2,1)S(1)}, u32[]{:S(2)}, u32[]{:S(2)}) collective-permute-start(bf16[32,2048]{1,0:T(8,128)(2,1)S(1)} %collective-permute-done.27.refs_0_.refs_3_), channel_id=1, source_target_pairs={{0,2},{1,3},{2,0},{3,1},{4,6},{5,7},{6,4},{7,5},{8,10},{9,11},{10,... | collective-permute-start | bytes 393224 | tf_op jit(solution)/shard_map/ppermute | solution.py:50
  72.5 2.6 %shard_map.70 = (f32[64,2048]{1,0:T(8,128)S(1)}, f32[64,2048]{1,0:T(8,128)S(1)}, bf16[64,2048]{1,0:T(8,128)(2,1)S(1)}, bf16[32,2048]{1,0:T(8,128)(2,1)S(1)}, bf16[32,2048]{1,0:T(8,128)(2,1)S(1)}) custom-call(bf16[32,2048]{1,0:T(8,128)(2,1)S(1)} %collective-permute-done.27.refs_0_.refs_3_, bf16[64,2048]{1,0:T(8,128)(2,1)S(1)} %shard_map.68.refs_0_.refs_1_, ...), custom_call_target="tpu_custom_call" | custom-call | tf_op jit(solution)/shard_map/pallas_call | solution.py:28
  76.2 0.6 collective-permute-done.34.refs_5_
  77.3 0.8 collective-permute-done.33.refs_2_
  78.3 2.6 %shard_map.72 = (f32[64,2048]{1,0:T(8,128)S(1)}, f32[64,2048]{1,0:T(8,128)S(1)}, bf16[64,2048]{1,0:T(8,128)(2,1)S(1)}, bf16[32,2048]{1,0:T(8,128)(2,1)S(1)}, bf16[32,2048]{1,0:T(8,128)(2,1)S(1)}) custom-call(bf16[32,2048]{1,0:T(8,128)(2,1)S(1)} %get-tuple-element.105.refs_0_, bf16[32,2048]{1,0:T(8,128)(2,1)S(1)} %get-tuple-element.106.refs_1_, ...), custom_call_target="tpu_custom_call" | custom-call | tf_op jit(solution)/shard_map/pallas_call | solution.py:28
  81.8 0.5 collective-permute-done.39.refs_1_
  82.7 1.6 %collective-permute-start.44 = (bf16[32,2048]{1,0:T(8,128)(2,1)S(1)}, bf16[32,2048]{1,0:T(8,128)(2,1)S(1)}, u32[]{:S(2)}, u32[]{:S(2)}) collective-permute-start(bf16[32,2048]{1,0:T(8,128)(2,1)S(1)} %get-tuple-element.101.refs_1_), channel_id=1, source_target_pairs={{0,2},{1,3},{2,0},{3,1},{4,6},{5,7},{6,4},{7,5},{8,10},{9,11},{10,... | collective-permute-start | bytes 393224 | tf_op jit(solution)/shard_map/ppermute | solution.py:50
  84.8 4.3 %collective-permute-done.44.refs_2_ = bf16[32,2048]{1,0:T(8,128)(2,1)S(1)} collective-permute-done((bf16[32,2048]{1,0:T(8,128)(2,1)S(1)}, bf16[32,2048]{1,0:T(8,128)(2,1)S(1)}, u32[]{:S(2)}, u32[]{:S(2)}) %collective-permute-start.44) | collective-permute-done | bytes 131104 | tf_op jit(solution)/shard_map/ppermute | solution.py:50
  89.3 1.9 %collective-permute-done.42.refs_2_ = bf16[32,2048]{1,0:T(8,128)(2,1)S(1)} collective-permute-done((bf16[32,2048]{1,0:T(8,128)(2,1)S(1)}, bf16[32,2048]{1,0:T(8,128)(2,1)S(1)}, u32[]{:S(2)}, u32[]{:S(2)}) %collective-permute-start.42) | collective-permute-done | bytes 131104 | tf_op jit(solution)/shard_map/ppermute | solution.py:50
  91.2 1.5 %collective-permute-start.45 = (bf16[32,2048]{1,0:T(8,128)(2,1)S(1)}, bf16[32,2048]{1,0:T(8,128)(2,1)S(1)}, u32[]{:S(2)}, u32[]{:S(2)}) collective-permute-start(bf16[32,2048]{1,0:T(8,128)(2,1)S(1)} %get-tuple-element.105.refs_0_), channel_id=1, source_target_pairs={{0,2},{1,3},{2,0},{3,1},{4,6},{5,7},{6,4},{7,5},{8,10},{9,11},{10,... | collective-permute-start | bytes 393224 | tf_op jit(solution)/shard_map/ppermute | solution.py:50
  93.2 1.0 collective-permute-done.48.refs_3_
  94.5 2.9 %collective-permute-done.45.refs_4_ = bf16[32,2048]{1,0:T(8,128)(2,1)S(1)} collective-permute-done((bf16[32,2048]{1,0:T(8,128)(2,1)S(1)}, bf16[32,2048]{1,0:T(8,128)(2,1)S(1)}, u32[]{:S(2)}, u32[]{:S(2)}) %collective-permute-start.45) | collective-permute-done | bytes 131104 | tf_op jit(solution)/shard_map/ppermute | solution.py:50
  97.4 1.4 %collective-permute-done.46.refs_5_ = bf16[32,2048]{1,0:T(8,128)(2,1)S(1)} collective-permute-done((bf16[32,2048]{1,0:T(8,128)(2,1)S(1)}, bf16[32,2048]{1,0:T(8,128)(2,1)S(1)}, u32[]{:S(2)}, u32[]{:S(2)}) %collective-permute-start.46) | collective-permute-done | bytes 131104 | tf_op jit(solution)/shard_map/ppermute | solution.py:50
  98.9 2.2 %collective-permute-done.49.refs_3_ = bf16[32,2048]{1,0:T(8,128)(2,1)S(1)} collective-permute-done((bf16[32,2048]{1,0:T(8,128)(2,1)S(1)}, bf16[32,2048]{1,0:T(8,128)(2,1)S(1)}, u32[]{:S(2)}, u32[]{:S(2)}) %collective-permute-start.49) | collective-permute-done | bytes 131104 | tf_op jit(solution)/shard_map/ppermute | solution.py:50
  101.2 2.7 %collective-permute-done.47.refs_2_ = bf16[32,2048]{1,0:T(8,128)(2,1)S(1)} collective-permute-done((bf16[32,2048]{1,0:T(8,128)(2,1)S(1)}, bf16[32,2048]{1,0:T(8,128)(2,1)S(1)}, u32[]{:S(2)}, u32[]{:S(2)}) %collective-permute-start.47) | collective-permute-done | bytes 131104 | tf_op jit(solution)/shard_map/ppermute | solution.py:50
  103.9 0.8 shard_map.77
  (79 shorter events, 9.8 us)
Async XLA Ops:
  1.2 9.4 %collective-permute-start = (bf16[32,2176]{1,0:T(8,128)(2,1)S(1)}, bf16[32,2176]{1,0:T(8,128)(2,1)S(1)}, u32[]{:S(2)}, u32[]{:S(2)}) collective-permute-start(bf16[32,2176]{1,0:T(8,128)(2,1)S(1)} %shard_map.56.refs_1_), channel_id=1, source_target_pairs={{0,4},{1,5},{2,6},{3,7},{4,0},{5,1},{6,2},{7,3},{8,12},{9,13},{10,... | collective-permute-start | bytes 417800 | tf_op jit(solution)/shard_map/ppermute | solution.py:50
  4.3 9.1 %collective-permute-start.1 = (bf16[32,2176]{1,0:T(8,128)(2,1)S(1)}, bf16[32,2176]{1,0:T(8,128)(2,1)S(1)}, u32[]{:S(2)}, u32[]{:S(2)}) collective-permute-start(bf16[32,2176]{1,0:T(8,128)(2,1)S(1)} %shard_map.56.refs_1_), channel_id=1, source_target_pairs={{0,8},{1,9},{2,10},{3,11},{4,12},{5,13},{6,14},{7,15},{8,0},{9,1},... | collective-permute-start | bytes 417800 | tf_op jit(solution)/shard_map/ppermute | solution.py:50
  10.7 10.9 %collective-permute-start.3 = (bf16[64,2176]{1,0:T(8,128)(2,1)S(1)}, bf16[64,2176]{1,0:T(8,128)(2,1)S(1)}, u32[]{:S(2)}, u32[]{:S(2)}) collective-permute-start(bf16[64,2176]{1,0:T(8,128)(2,1)S(1)} %shard_map.57.refs_0_.refs_1_), channel_id=1, source_target_pairs={{0,2},{1,3},{2,0},{3,1},{4,6},{5,7},{6,4},{7,5},{8,10},{9,11},{10,... | collective-permute-start | bytes 835592 | tf_op jit(solution)/shard_map/ppermute | solution.py:50
  13.4 8.2 %collective-permute-start.4 = (bf16[32,2176]{1,0:T(8,128)(2,1)S(1)}, bf16[32,2176]{1,0:T(8,128)(2,1)S(1)}, u32[]{:S(2)}, u32[]{:S(2)}) collective-permute-start(bf16[32,2176]{1,0:T(8,128)(2,1)S(1)} %shard_map.58.refs_2_), channel_id=1, source_target_pairs={{0,2},{1,3},{2,0},{3,1},{4,6},{5,7},{6,4},{7,5},{8,10},{9,11},{10,... | collective-permute-start | bytes 417800 | tf_op jit(solution)/shard_map/ppermute | solution.py:50
  15.0 6.6 %collective-permute-start.2 = (bf16[32,2176]{1,0:T(8,128)(2,1)S(1)}, bf16[32,2176]{1,0:T(8,128)(2,1)S(1)}, u32[]{:S(2)}, u32[]{:S(2)}) collective-permute-start(bf16[32,2176]{1,0:T(8,128)(2,1)S(1)} %shard_map.58.refs_2_), channel_id=1, source_target_pairs={{0,4},{1,5},{2,6},{3,7},{4,0},{5,1},{6,2},{7,3},{8,12},{9,13},{10,... | collective-permute-start | bytes 417800 | tf_op jit(solution)/shard_map/ppermute | solution.py:50
  15.4 7.8 %collective-permute-start.5 = (bf16[64,2176]{1,0:T(8,128)(2,1)S(1)}, bf16[64,2176]{1,0:T(8,128)(2,1)S(1)}, u32[]{:S(2)}, u32[]{:S(2)}) collective-permute-start(bf16[64,2176]{1,0:T(8,128)(2,1)S(1)} %shard_map.57.refs_0_.refs_1_), channel_id=1, source_target_pairs={{0,1},{1,0},{2,3},{3,2},{4,5},{5,4},{6,7},{7,6},{8,9},{9,8},{10,11... | collective-permute-start | bytes 835592 | tf_op jit(solution)/shard_map/ppermute | solution.py:50
  21.6 1.6 %collective-permute-start.6 = (bf16[64,2176]{1,0:T(8,128)(2,1)S(1)}, bf16[64,2176]{1,0:T(8,128)(2,1)S(1)}, u32[]{:S(2)}, u32[]{:S(2)}) collective-permute-start(bf16[64,2176]{1,0:T(8,128)(2,1)S(1)} %collective-permute-done.3.refs_2_), channel_id=1, source_target_pairs={{0,1},{1,0},{2,3},{3,2},{4,5},{5,4},{6,7},{7,6},{8,9},{9,8},{10,11... | collective-permute-start | bytes 835592 | tf_op jit(solution)/shard_map/ppermute | solution.py:50
  21.6 6.1 %collective-permute-start.9 = (bf16[32,2176]{1,0:T(8,128)(2,1)S(1)}, bf16[32,2176]{1,0:T(8,128)(2,1)S(1)}, u32[]{:S(2)}, u32[]{:S(2)}) collective-permute-start(bf16[32,2176]{1,0:T(8,128)(2,1)S(1)} %collective-permute-done.2.refs_0_.refs_3_), channel_id=1, source_target_pairs={{0,2},{1,3},{2,0},{3,1},{4,6},{5,7},{6,4},{7,5},{8,10},{9,11},{10,... | collective-permute-start | bytes 417800 | tf_op jit(solution)/shard_map/ppermute | solution.py:50
  25.8 1.9 %collective-permute-start.7 = (bf16[32,2048]{1,0:T(8,128)(2,1)S(1)}, bf16[32,2048]{1,0:T(8,128)(2,1)S(1)}, u32[]{:S(2)}, u32[]{:S(2)}) collective-permute-start(bf16[32,2048]{1,0:T(8,128)(2,1)S(1)} %get-tuple-element.62), channel_id=1, source_target_pairs={{0,1},{1,0},{2,3},{3,2},{4,5},{5,4},{6,7},{7,6},{8,9},{9,8},{10,11... | collective-permute-start | bytes 393224 | tf_op jit(solution)/shard_map/ppermute | solution.py:50
  26.0 3.3 %collective-permute-start.10 = (bf16[32,2176]{1,0:T(8,128)(2,1)S(1)}, bf16[32,2176]{1,0:T(8,128)(2,1)S(1)}, u32[]{:S(2)}, u32[]{:S(2)}) collective-permute-start(bf16[32,2176]{1,0:T(8,128)(2,1)S(1)} %shard_map.58.refs_2_), channel_id=1, source_target_pairs={{0,1},{1,0},{2,3},{3,2},{4,5},{5,4},{6,7},{7,6},{8,9},{9,8},{10,11... | collective-permute-start | bytes 417800 | tf_op jit(solution)/shard_map/ppermute | solution.py:50
  26.4 2.9 %collective-permute-start.12 = (bf16[32,2176]{1,0:T(8,128)(2,1)S(1)}, bf16[32,2176]{1,0:T(8,128)(2,1)S(1)}, u32[]{:S(2)}, u32[]{:S(2)}) collective-permute-start(bf16[32,2176]{1,0:T(8,128)(2,1)S(1)} %collective-permute-done.4.refs_4_), channel_id=1, source_target_pairs={{0,1},{1,0},{2,3},{3,2},{4,5},{5,4},{6,7},{7,6},{8,9},{9,8},{10,11... | collective-permute-start | bytes 417800 | tf_op jit(solution)/shard_map/ppermute | solution.py:50
  26.6 2.8 %collective-permute-start.11 = (bf16[32,2176]{1,0:T(8,128)(2,1)S(1)}, bf16[32,2176]{1,0:T(8,128)(2,1)S(1)}, u32[]{:S(2)}, u32[]{:S(2)}) collective-permute-start(bf16[32,2176]{1,0:T(8,128)(2,1)S(1)} %collective-permute-done.2.refs_0_.refs_3_), channel_id=1, source_target_pairs={{0,1},{1,0},{2,3},{3,2},{4,5},{5,4},{6,7},{7,6},{8,9},{9,8},{10,11... | collective-permute-start | bytes 417800 | tf_op jit(solution)/shard_map/ppermute | solution.py:50
  27.7 1.6 %collective-permute-start.13 = (bf16[32,2176]{1,0:T(8,128)(2,1)S(1)}, bf16[32,2176]{1,0:T(8,128)(2,1)S(1)}, u32[]{:S(2)}, u32[]{:S(2)}) collective-permute-start(bf16[32,2176]{1,0:T(8,128)(2,1)S(1)} %collective-permute-done.9.refs_5_), channel_id=1, source_target_pairs={{0,1},{1,0},{2,3},{3,2},{4,5},{5,4},{6,7},{7,6},{8,9},{9,8},{10,11... | collective-permute-start | bytes 417800 | tf_op jit(solution)/shard_map/ppermute | solution.py:50
  27.7 1.5 %collective-permute-start.8 = (bf16[32,2048]{1,0:T(8,128)(2,1)S(1)}, bf16[32,2048]{1,0:T(8,128)(2,1)S(1)}, u32[]{:S(2)}, u32[]{:S(2)}) collective-permute-start(bf16[32,2048]{1,0:T(8,128)(2,1)S(1)} %get-tuple-element.63), channel_id=1, source_target_pairs={{0,1},{1,0},{2,3},{3,2},{4,5},{5,4},{6,7},{7,6},{8,9},{9,8},{10,11... | collective-permute-start | bytes 393224 | tf_op jit(solution)/shard_map/ppermute | solution.py:50
  32.0 1.4 %collective-permute-start.14 = (bf16[32,2048]{1,0:T(8,128)(2,1)S(1)}, bf16[32,2048]{1,0:T(8,128)(2,1)S(1)}, u32[]{:S(2)}, u32[]{:S(2)}) collective-permute-start(bf16[32,2048]{1,0:T(8,128)(2,1)S(1)} %get-tuple-element.72), channel_id=1, source_target_pairs={{0,1},{1,0},{2,3},{3,2},{4,5},{5,4},{6,7},{7,6},{8,9},{9,8},{10,11... | collective-permute-start | bytes 393224 | tf_op jit(solution)/shard_map/ppermute | solution.py:50
  32.3 1.3 %collective-permute-start.15 = (bf16[32,2048]{1,0:T(8,128)(2,1)S(1)}, bf16[32,2048]{1,0:T(8,128)(2,1)S(1)}, u32[]{:S(2)}, u32[]{:S(2)}) collective-permute-start(bf16[32,2048]{1,0:T(8,128)(2,1)S(1)} %get-tuple-element.73), channel_id=1, source_target_pairs={{0,1},{1,0},{2,3},{3,2},{4,5},{5,4},{6,7},{7,6},{8,9},{9,8},{10,11... | collective-permute-start | bytes 393224 | tf_op jit(solution)/shard_map/ppermute | solution.py:50
  32.5 7.6 %collective-permute-start.18 = (bf16[64,2048]{1,0:T(8,128)(2,1)S(1)}, bf16[64,2048]{1,0:T(8,128)(2,1)S(1)}, u32[]{:S(2)}, u32[]{:S(2)}) collective-permute-start(bf16[64,2048]{1,0:T(8,128)(2,1)S(1)} %get-tuple-element.77), channel_id=1, source_target_pairs={{0,1},{1,0},{2,3},{3,2},{4,5},{5,4},{6,7},{7,6},{8,9},{9,8},{10,11... | collective-permute-start | bytes 786440 | tf_op jit(solution)/shard_map/ppermute | solution.py:50
  33.7 6.4 %collective-permute-start.19 = (bf16[32,2048]{1,0:T(8,128)(2,1)S(1)}, bf16[32,2048]{1,0:T(8,128)(2,1)S(1)}, u32[]{:S(2)}, u32[]{:S(2)}) collective-permute-start(bf16[32,2048]{1,0:T(8,128)(2,1)S(1)} %get-tuple-element.75.refs_1_), channel_id=1, source_target_pairs={{0,2},{1,3},{2,0},{3,1},{4,6},{5,7},{6,4},{7,5},{8,10},{9,11},{10,... | collective-permute-start | bytes 393224 | tf_op jit(solution)/shard_map/ppermute | solution.py:50
  35.3 6.9 %collective-permute-start.17 = (bf16[32,2048]{1,0:T(8,128)(2,1)S(1)}, bf16[32,2048]{1,0:T(8,128)(2,1)S(1)}, u32[]{:S(2)}, u32[]{:S(2)}) collective-permute-start(bf16[32,2048]{1,0:T(8,128)(2,1)S(1)} %get-tuple-element.74.refs_0_), channel_id=1, source_target_pairs={{0,2},{1,3},{2,0},{3,1},{4,6},{5,7},{6,4},{7,5},{8,10},{9,11},{10,... | collective-permute-start | bytes 393224 | tf_op jit(solution)/shard_map/ppermute | solution.py:50
  35.8 10.6 %collective-permute-start.16 = (bf16[64,2048]{1,0:T(8,128)(2,1)S(1)}, bf16[64,2048]{1,0:T(8,128)(2,1)S(1)}, u32[]{:S(2)}, u32[]{:S(2)}) collective-permute-start(bf16[64,2048]{1,0:T(8,128)(2,1)S(1)} %get-tuple-element.76), channel_id=1, source_target_pairs={{0,1},{1,0},{2,3},{3,2},{4,5},{5,4},{6,7},{7,6},{8,9},{9,8},{10,11... | collective-permute-start | bytes 786440 | tf_op jit(solution)/shard_map/ppermute | solution.py:50
  40.2 5.0 %collective-permute-start.23 = (bf16[32,2048]{1,0:T(8,128)(2,1)S(1)}, bf16[32,2048]{1,0:T(8,128)(2,1)S(1)}, u32[]{:S(2)}, u32[]{:S(2)}) collective-permute-start(bf16[32,2048]{1,0:T(8,128)(2,1)S(1)} %shard_map.64), channel_id=1, source_target_pairs={{0,4},{1,5},{2,6},{3,7},{4,0},{5,1},{6,2},{7,3},{8,12},{9,13},{10,... | collective-permute-start | bytes 393224 | tf_op jit(solution)/shard_map/ppermute | solution.py:50
  42.2 6.2 %collective-permute-start.20 = (bf16[32,2048]{1,0:T(8,128)(2,1)S(1)}, bf16[32,2048]{1,0:T(8,128)(2,1)S(1)}, u32[]{:S(2)}, u32[]{:S(2)}) collective-permute-start(bf16[32,2048]{1,0:T(8,128)(2,1)S(1)} %get-tuple-element.78.refs_0_), channel_id=1, source_target_pairs={{0,2},{1,3},{2,0},{3,1},{4,6},{5,7},{6,4},{7,5},{8,10},{9,11},{10,... | collective-permute-start | bytes 393224 | tf_op jit(solution)/shard_map/ppermute | solution.py:50
  43.7 6.1 %collective-permute-start.21 = (bf16[32,2048]{1,0:T(8,128)(2,1)S(1)}, bf16[32,2048]{1,0:T(8,128)(2,1)S(1)}, u32[]{:S(2)}, u32[]{:S(2)}) collective-permute-start(bf16[32,2048]{1,0:T(8,128)(2,1)S(1)} %get-tuple-element.79.refs_1_), channel_id=1, source_target_pairs={{0,2},{1,3},{2,0},{3,1},{4,6},{5,7},{6,4},{7,5},{8,10},{9,11},{10,... | collective-permute-start | bytes 393224 | tf_op jit(solution)/shard_map/ppermute | solution.py:50
  45.3 8.9 %collective-permute-start.24 = (bf16[32,2048]{1,0:T(8,128)(2,1)S(1)}, bf16[32,2048]{1,0:T(8,128)(2,1)S(1)}, u32[]{:S(2)}, u32[]{:S(2)}) collective-permute-start(bf16[32,2048]{1,0:T(8,128)(2,1)S(1)} %shard_map.66), channel_id=1, source_target_pairs={{0,8},{1,9},{2,10},{3,11},{4,12},{5,13},{6,14},{7,15},{8,0},{9,1},... | collective-permute-start | bytes 393224 | tf_op jit(solution)/shard_map/ppermute | solution.py:50
  49.9 5.2 %collective-permute-start.22 = (bf16[32,2048]{1,0:T(8,128)(2,1)S(1)}, bf16[32,2048]{1,0:T(8,128)(2,1)S(1)}, u32[]{:S(2)}, u32[]{:S(2)}) collective-permute-start(bf16[32,2048]{1,0:T(8,128)(2,1)S(1)} %get-tuple-element.81), channel_id=1, source_target_pairs={{0,4},{1,5},{2,6},{3,7},{4,0},{5,1},{6,2},{7,3},{8,12},{9,13},{10,... | collective-permute-start | bytes 393224 | tf_op jit(solution)/shard_map/ppermute | solution.py:50
  55.3 6.9 %collective-permute-start.25 = (bf16[32,2048]{1,0:T(8,128)(2,1)S(1)}, bf16[32,2048]{1,0:T(8,128)(2,1)S(1)}, u32[]{:S(2)}, u32[]{:S(2)}) collective-permute-start(bf16[32,2048]{1,0:T(8,128)(2,1)S(1)} %get-tuple-element.83.refs_1_), channel_id=1, source_target_pairs={{0,4},{1,5},{2,6},{3,7},{4,0},{5,1},{6,2},{7,3},{8,12},{9,13},{10,... | collective-permute-start | bytes 393224 | tf_op jit(solution)/shard_map/ppermute | solution.py:50
  56.1 7.7 %collective-permute-start.26 = (bf16[32,2048]{1,0:T(8,128)(2,1)S(1)}, bf16[32,2048]{1,0:T(8,128)(2,1)S(1)}, u32[]{:S(2)}, u32[]{:S(2)}) collective-permute-start(bf16[32,2048]{1,0:T(8,128)(2,1)S(1)} %get-tuple-element.83.refs_1_), channel_id=1, source_target_pairs={{0,8},{1,9},{2,10},{3,11},{4,12},{5,13},{6,14},{7,15},{8,0},{9,1},... | collective-permute-start | bytes 393224 | tf_op jit(solution)/shard_map/ppermute | solution.py:50
  62.2 8.7 %collective-permute-start.28 = (bf16[64,2048]{1,0:T(8,128)(2,1)S(1)}, bf16[64,2048]{1,0:T(8,128)(2,1)S(1)}, u32[]{:S(2)}, u32[]{:S(2)}) collective-permute-start(bf16[64,2048]{1,0:T(8,128)(2,1)S(1)} %shard_map.68.refs_0_.refs_1_), channel_id=1, source_target_pairs={{0,2},{1,3},{2,0},{3,1},{4,6},{5,7},{6,4},{7,5},{8,10},{9,11},{10,... | collective-permute-start | bytes 786440 | tf_op jit(solution)/shard_map/ppermute | solution.py:50
  63.8 7.0 %collective-permute-start.29 = (bf16[32,2048]{1,0:T(8,128)(2,1)S(1)}, bf16[32,2048]{1,0:T(8,128)(2,1)S(1)}, u32[]{:S(2)}, u32[]{:S(2)}) collective-permute-start(bf16[32,2048]{1,0:T(8,128)(2,1)S(1)} %shard_map.69.refs_2_), channel_id=1, source_target_pairs={{0,2},{1,3},{2,0},{3,1},{4,6},{5,7},{6,4},{7,5},{8,10},{9,11},{10,... | collective-permute-start | bytes 393224 | tf_op jit(solution)/shard_map/ppermute | solution.py:50
  65.1 5.8 %collective-permute-start.27 = (bf16[32,2048]{1,0:T(8,128)(2,1)S(1)}, bf16[32,2048]{1,0:T(8,128)(2,1)S(1)}, u32[]{:S(2)}, u32[]{:S(2)}) collective-permute-start(bf16[32,2048]{1,0:T(8,128)(2,1)S(1)} %shard_map.69.refs_2_), channel_id=1, source_target_pairs={{0,4},{1,5},{2,6},{3,7},{4,0},{5,1},{6,2},{7,3},{8,12},{9,13},{10,... | collective-permute-start | bytes 393224 | tf_op jit(solution)/shard_map/ppermute | solution.py:50
  65.4 7.0 %collective-permute-start.30 = (bf16[64,2048]{1,0:T(8,128)(2,1)S(1)}, bf16[64,2048]{1,0:T(8,128)(2,1)S(1)}, u32[]{:S(2)}, u32[]{:S(2)}) collective-permute-start(bf16[64,2048]{1,0:T(8,128)(2,1)S(1)} %shard_map.68.refs_0_.refs_1_), channel_id=1, source_target_pairs={{0,1},{1,0},{2,3},{3,2},{4,5},{5,4},{6,7},{7,6},{8,9},{9,8},{10,11... | collective-permute-start | bytes 786440 | tf_op jit(solution)/shard_map/ppermute | solution.py:50
  70.9 1.6 %collective-permute-start.31 = (bf16[64,2048]{1,0:T(8,128)(2,1)S(1)}, bf16[64,2048]{1,0:T(8,128)(2,1)S(1)}, u32[]{:S(2)}, u32[]{:S(2)}) collective-permute-start(bf16[64,2048]{1,0:T(8,128)(2,1)S(1)} %collective-permute-done.28.refs_2_), channel_id=1, source_target_pairs={{0,1},{1,0},{2,3},{3,2},{4,5},{5,4},{6,7},{7,6},{8,9},{9,8},{10,11... | collective-permute-start | bytes 786440 | tf_op jit(solution)/shard_map/ppermute | solution.py:50
  70.9 5.9 %collective-permute-start.34 = (bf16[32,2048]{1,0:T(8,128)(2,1)S(1)}, bf16[32,2048]{1,0:T(8,128)(2,1)S(1)}, u32[]{:S(2)}, u32[]{:S(2)}) collective-permute-start(bf16[32,2048]{1,0:T(8,128)(2,1)S(1)} %collective-permute-done.27.refs_0_.refs_3_), channel_id=1, source_target_pairs={{0,2},{1,3},{2,0},{3,1},{4,6},{5,7},{6,4},{7,5},{8,10},{9,11},{10,... | collective-permute-start | bytes 393224 | tf_op jit(solution)/shard_map/ppermute | solution.py:50
  75.1 1.7 %collective-permute-start.32 = (bf16[32,2048]{1,0:T(8,128)(2,1)S(1)}, bf16[32,2048]{1,0:T(8,128)(2,1)S(1)}, u32[]{:S(2)}, u32[]{:S(2)}) collective-permute-start(bf16[32,2048]{1,0:T(8,128)(2,1)S(1)} %get-tuple-element.89), channel_id=1, source_target_pairs={{0,1},{1,0},{2,3},{3,2},{4,5},{5,4},{6,7},{7,6},{8,9},{9,8},{10,11... | collective-permute-start | bytes 393224 | tf_op jit(solution)/shard_map/ppermute | solution.py:50
  75.3 2.9 %collective-permute-start.35 = (bf16[32,2048]{1,0:T(8,128)(2,1)S(1)}, bf16[32,2048]{1,0:T(8,128)(2,1)S(1)}, u32[]{:S(2)}, u32[]{:S(2)}) collective-permute-start(bf16[32,2048]{1,0:T(8,128)(2,1)S(1)} %shard_map.69.refs_2_), channel_id=1, source_target_pairs={{0,1},{1,0},{2,3},{3,2},{4,5},{5,4},{6,7},{7,6},{8,9},{9,8},{10,11... | collective-permute-start | bytes 393224 | tf_op jit(solution)/shard_map/ppermute | solution.py:50
  75.7 2.5 %collective-permute-start.37 = (bf16[32,2048]{1,0:T(8,128)(2,1)S(1)}, bf16[32,2048]{1,0:T(8,128)(2,1)S(1)}, u32[]{:S(2)}, u32[]{:S(2)}) collective-permute-start(bf16[32,2048]{1,0:T(8,128)(2,1)S(1)} %collective-permute-done.29.refs_4_), channel_id=1, source_target_pairs={{0,1},{1,0},{2,3},{3,2},{4,5},{5,4},{6,7},{7,6},{8,9},{9,8},{10,11... | collective-permute-start | bytes 393224 | tf_op jit(solution)/shard_map/ppermute | solution.py:50
  75.8 2.4 %collective-permute-start.36 = (bf16[32,2048]{1,0:T(8,128)(2,1)S(1)}, bf16[32,2048]{1,0:T(8,128)(2,1)S(1)}, u32[]{:S(2)}, u32[]{:S(2)}) collective-permute-start(bf16[32,2048]{1,0:T(8,128)(2,1)S(1)} %collective-permute-done.27.refs_0_.refs_3_), channel_id=1, source_target_pairs={{0,1},{1,0},{2,3},{3,2},{4,5},{5,4},{6,7},{7,6},{8,9},{9,8},{10,11... | collective-permute-start | bytes 393224 | tf_op jit(solution)/shard_map/ppermute | solution.py:50
  76.8 1.5 %collective-permute-start.38 = (bf16[32,2048]{1,0:T(8,128)(2,1)S(1)}, bf16[32,2048]{1,0:T(8,128)(2,1)S(1)}, u32[]{:S(2)}, u32[]{:S(2)}) collective-permute-start(bf16[32,2048]{1,0:T(8,128)(2,1)S(1)} %collective-permute-done.34.refs_5_), channel_id=1, source_target_pairs={{0,1},{1,0},{2,3},{3,2},{4,5},{5,4},{6,7},{7,6},{8,9},{9,8},{10,11... | collective-permute-start | bytes 393224 | tf_op jit(solution)/shard_map/ppermute | solution.py:50
  80.9 1.4 %collective-permute-start.39 = (bf16[32,2048]{1,0:T(8,128)(2,1)S(1)}, bf16[32,2048]{1,0:T(8,128)(2,1)S(1)}, u32[]{:S(2)}, u32[]{:S(2)}) collective-permute-start(bf16[32,2048]{1,0:T(8,128)(2,1)S(1)} %get-tuple-element.98), channel_id=1, source_target_pairs={{0,1},{1,0},{2,3},{3,2},{4,5},{5,4},{6,7},{7,6},{8,9},{9,8},{10,11... | collective-permute-start | bytes 393224 | tf_op jit(solution)/shard_map/ppermute | solution.py:50
  81.5 3.3 %collective-permute-start.43 = (bf16[64,2048]{1,0:T(8,128)(2,1)S(1)}, bf16[64,2048]{1,0:T(8,128)(2,1)S(1)}, u32[]{:S(2)}, u32[]{:S(2)}) collective-permute-start(bf16[64,2048]{1,0:T(8,128)(2,1)S(1)} %get-tuple-element.104), channel_id=1, source_target_pairs={{0,1},{1,0},{2,3},{3,2},{4,5},{5,4},{6,7},{7,6},{8,9},{9,8},{10,11... | collective-permute-start | bytes 786440 | tf_op jit(solution)/shard_map/ppermute | solution.py:50
  82.7 6.4 %collective-permute-start.44 = (bf16[32,2048]{1,0:T(8,128)(2,1)S(1)}, bf16[32,2048]{1,0:T(8,128)(2,1)S(1)}, u32[]{:S(2)}, u32[]{:S(2)}) collective-permute-start(bf16[32,2048]{1,0:T(8,128)(2,1)S(1)} %get-tuple-element.101.refs_1_), channel_id=1, source_target_pairs={{0,2},{1,3},{2,0},{3,1},{4,6},{5,7},{6,4},{7,5},{8,10},{9,11},{10,... | collective-permute-start | bytes 393224 | tf_op jit(solution)/shard_map/ppermute | solution.py:50
  84.3 6.9 %collective-permute-start.42 = (bf16[32,2048]{1,0:T(8,128)(2,1)S(1)}, bf16[32,2048]{1,0:T(8,128)(2,1)S(1)}, u32[]{:S(2)}, u32[]{:S(2)}) collective-permute-start(bf16[32,2048]{1,0:T(8,128)(2,1)S(1)} %get-tuple-element.100.refs_0_), channel_id=1, source_target_pairs={{0,2},{1,3},{2,0},{3,1},{4,6},{5,7},{6,4},{7,5},{8,10},{9,11},{10,... | collective-permute-start | bytes 393224 | tf_op jit(solution)/shard_map/ppermute | solution.py:50
  84.8 9.7 %collective-permute-start.41 = (bf16[64,2048]{1,0:T(8,128)(2,1)S(1)}, bf16[64,2048]{1,0:T(8,128)(2,1)S(1)}, u32[]{:S(2)}, u32[]{:S(2)}) collective-permute-start(bf16[64,2048]{1,0:T(8,128)(2,1)S(1)} %get-tuple-element.102), channel_id=1, source_target_pairs={{0,1},{1,0},{2,3},{3,2},{4,5},{5,4},{6,7},{7,6},{8,9},{9,8},{10,11... | collective-permute-start | bytes 786440 | tf_op jit(solution)/shard_map/ppermute | solution.py:50
  89.2 5.0 %collective-permute-start.48 = (bf16[32,2048]{1,0:T(8,128)(2,1)S(1)}, bf16[32,2048]{1,0:T(8,128)(2,1)S(1)}, u32[]{:S(2)}, u32[]{:S(2)}) collective-permute-start(bf16[32,2048]{1,0:T(8,128)(2,1)S(1)} %shard_map.74), channel_id=1, source_target_pairs={{0,4},{1,5},{2,6},{3,7},{4,0},{5,1},{6,2},{7,3},{8,12},{9,13},{10,... | collective-permute-start | bytes 393224 | tf_op jit(solution)/shard_map/ppermute | solution.py:50
  91.2 6.2 %collective-permute-start.45 = (bf16[32,2048]{1,0:T(8,128)(2,1)S(1)}, bf16[32,2048]{1,0:T(8,128)(2,1)S(1)}, u32[]{:S(2)}, u32[]{:S(2)}) collective-permute-start(bf16[32,2048]{1,0:T(8,128)(2,1)S(1)} %get-tuple-element.105.refs_0_), channel_id=1, source_target_pairs={{0,2},{1,3},{2,0},{3,1},{4,6},{5,7},{6,4},{7,5},{8,10},{9,11},{10,... | collective-permute-start | bytes 393224 | tf_op jit(solution)/shard_map/ppermute | solution.py:50
  92.7 6.1 %collective-permute-start.46 = (bf16[32,2048]{1,0:T(8,128)(2,1)S(1)}, bf16[32,2048]{1,0:T(8,128)(2,1)S(1)}, u32[]{:S(2)}, u32[]{:S(2)}) collective-permute-start(bf16[32,2048]{1,0:T(8,128)(2,1)S(1)} %get-tuple-element.106.refs_1_), channel_id=1, source_target_pairs={{0,2},{1,3},{2,0},{3,1},{4,6},{5,7},{6,4},{7,5},{8,10},{9,11},{10,... | collective-permute-start | bytes 393224 | tf_op jit(solution)/shard_map/ppermute | solution.py:50
  94.3 6.9 %collective-permute-start.49 = (bf16[32,2048]{1,0:T(8,128)(2,1)S(1)}, bf16[32,2048]{1,0:T(8,128)(2,1)S(1)}, u32[]{:S(2)}, u32[]{:S(2)}) collective-permute-start(bf16[32,2048]{1,0:T(8,128)(2,1)S(1)} %shard_map.76), channel_id=1, source_target_pairs={{0,8},{1,9},{2,10},{3,11},{4,12},{5,13},{6,14},{7,15},{8,0},{9,1},... | collective-permute-start | bytes 393224 | tf_op jit(solution)/shard_map/ppermute | solution.py:50
  98.9 5.0 %collective-permute-start.47 = (bf16[32,2048]{1,0:T(8,128)(2,1)S(1)}, bf16[32,2048]{1,0:T(8,128)(2,1)S(1)}, u32[]{:S(2)}, u32[]{:S(2)}) collective-permute-start(bf16[32,2048]{1,0:T(8,128)(2,1)S(1)} %get-tuple-element.108), channel_id=1, source_target_pairs={{0,4},{1,5},{2,6},{3,7},{4,0},{5,1},{6,2},{7,3},{8,12},{9,13},{10,... | collective-permute-start | bytes 393224 | tf_op jit(solution)/shard_map/ppermute | solution.py:50
  (4 other events, 13.2 us)

commit v14 on v13

--- a/solution.py
+++ b/solution.py
@@ -352,7 +352,7 @@
     mine2, near2, leaving2 = leave_pair(outs, half, ())
     back2 = [swap(piece, 2, 1, 2, True) for piece in leaving2]
     crossed_back, hops = cross_rows(mine2, near2, back2)
-    back1 = [swap(held(piece, (back2[0], *hops)), 2, 1, 2, True) for piece in leaving1]
+    back1 = [swap(held(piece, hops), 2, 1, 2, True) for piece in leaving1]
     pieces = call(
         functools.partial(apart_kernel, 0, half),
         [(rows.shape[:1] + mine1.shape[1:], bf16 if k else f32) for k in range(half)],

time: 105 us -> 101 us (0.962)
  waiting for transfers between devices: 49.2 us -> 41 us
  starting transfers between devices: 34.4 us -> 38.6 us
    ppermute x50, waiting for transfers between devices: 49.2 us -> 41 us  [swap(): lax.ppermute(value, 'expert', [(i, partner(i)) for i in range(count)])]
    ppermute x50, starting transfers between devices: 34.4 us -> 38.6 us  [swap(): lax.ppermute(value, 'expert', [(i, partner(i)) for i in range(count)])]
where the time goes in v14:
time: 101 us
  waiting for transfers between devices  41 us (41%)
  starting transfers between devices  38.6 us (38%)
  Pallas kernels  20.8 us (21%)
    ppermute x50, waiting for transfers between devices, swap(): lax.ppermute(value, 'expert', [(i, partner(i)) for i in range(count)])  41 us
    ppermute x50, starting transfers between devices, swap(): lax.ppermute(value, 'expert', [(i, partner(i)) for i in range(count)])  38.6 us
    pallas_call x23, Pallas kernels, call(): pl.pallas_call(lambda *refs: kernel(*refs[len(after):]), out_shape=shapes...  20.8 us
  transfers between devices with their start and end apart: 50, of which 26 were waited for; matrix products, arithmetic and copies ran while one was open for 0% of the time, Pallas kernels for 13%

profile of v14, /device:TPU:0, one launch (start us, length us, event | category | flops | bytes accessed | tf_op | source)
XLA Modules:
  0.0 100.7 jit_solution(12515579730962879188)
XLA Ops:
  0.0 1.2 %shard_map.56.refs_1_ = bf16[32,2176]{1,0:T(8,128)(2,1)S(1)} custom-call(bf16[32,2048]{1,0:T(8,128)(2,1)} %bitcast.2, s32[2,2,8,16]{3,2,1,0:T(8,128)} %bitcast.4, f32[2,2048]{1,0:T(2,128)} %refs_2_.5), custom_call_target="tpu_custom_call" | custom-call | tf_op jit(solution)/shard_map/pallas_call | solution.py:28
  1.2 3.1 %collective-permute-start = (bf16[32,2176]{1,0:T(8,128)(2,1)S(1)}, bf16[32,2176]{1,0:T(8,128)(2,1)S(1)}, u32[]{:S(2)}, u32[]{:S(2)}) collective-permute-start(bf16[32,2176]{1,0:T(8,128)(2,1)S(1)} %shard_map.56.refs_1_), channel_id=1, source_target_pairs={{0,4},{1,5},{2,6},{3,7},{4,0},{5,1},{6,2},{7,3},{8,12},{9,13},{10,... | collective-permute-start | bytes 417800 | tf_op jit(solution)/shard_map/ppermute | solution.py:50
  4.3 2.6 %collective-permute-start.1 = (bf16[32,2176]{1,0:T(8,128)(2,1)S(1)}, bf16[32,2176]{1,0:T(8,128)(2,1)S(1)}, u32[]{:S(2)}, u32[]{:S(2)}) collective-permute-start(bf16[32,2176]{1,0:T(8,128)(2,1)S(1)} %shard_map.56.refs_1_), channel_id=1, source_target_pairs={{0,8},{1,9},{2,10},{3,11},{4,12},{5,13},{6,14},{7,15},{8,0},{9,1},... | collective-permute-start | bytes 417800 | tf_op jit(solution)/shard_map/ppermute | solution.py:50
  6.9 3.7 %shard_map.55 = (bf16[2048,1536]{1,0:T(8,128)(2,1)S(1)}, bf16[768,2048]{1,0:T(8,128)(2,1)S(1)}, f32[8,128]{1,0:T(8,128)S(1)}) custom-call(bf16[2,1,2048,1536]{3,2,1,0:T(8,128)(2,1)} %refs_1_.3, bf16[2,1,768,2048]{3,2,1,0:T(8,128)(2,1)} %refs_2_.4), custom_call_target="tpu_custom_call" | custom-call | tf_op jit(solution)/shard_map/pallas_call | solution.py:28
  10.7 1.6 %collective-permute-start.3 = (bf16[64,2176]{1,0:T(8,128)(2,1)S(1)}, bf16[64,2176]{1,0:T(8,128)(2,1)S(1)}, u32[]{:S(2)}, u32[]{:S(2)}) collective-permute-start(bf16[64,2176]{1,0:T(8,128)(2,1)S(1)} %shard_map.57.refs_0_.refs_1_), channel_id=1, source_target_pairs={{0,2},{1,3},{2,0},{3,1},{4,6},{5,7},{6,4},{7,5},{8,10},{9,11},{10,... | collective-permute-start | bytes 835592 | tf_op jit(solution)/shard_map/ppermute | solution.py:50
  12.3 1.1 %collective-permute-done.1.refs_1_ = bf16[32,2176]{1,0:T(8,128)(2,1)S(1)} collective-permute-done((bf16[32,2176]{1,0:T(8,128)(2,1)S(1)}, bf16[32,2176]{1,0:T(8,128)(2,1)S(1)}, u32[]{:S(2)}, u32[]{:S(2)}) %collective-permute-start.1) | collective-permute-done | bytes 139296 | tf_op jit(solution)/shard_map/ppermute | solution.py:50
  13.4 1.6 %collective-permute-start.4 = (bf16[32,2176]{1,0:T(8,128)(2,1)S(1)}, bf16[32,2176]{1,0:T(8,128)(2,1)S(1)}, u32[]{:S(2)}, u32[]{:S(2)}) collective-permute-start(bf16[32,2176]{1,0:T(8,128)(2,1)S(1)} %shard_map.58.refs_2_), channel_id=1, source_target_pairs={{0,2},{1,3},{2,0},{3,1},{4,6},{5,7},{6,4},{7,5},{8,10},{9,11},{10,... | collective-permute-start | bytes 417800 | tf_op jit(solution)/shard_map/ppermute | solution.py:50
  15.4 6.2 %collective-permute-done.4.refs_4_ = bf16[32,2176]{1,0:T(8,128)(2,1)S(1)} collective-permute-done((bf16[32,2176]{1,0:T(8,128)(2,1)S(1)}, bf16[32,2176]{1,0:T(8,128)(2,1)S(1)}, u32[]{:S(2)}, u32[]{:S(2)}) %collective-permute-start.4) | collective-permute-done | bytes 139296 | tf_op jit(solution)/shard_map/ppermute | solution.py:50
  21.6 1.6 %collective-permute-start.9 = (bf16[32,2176]{1,0:T(8,128)(2,1)S(1)}, bf16[32,2176]{1,0:T(8,128)(2,1)S(1)}, u32[]{:S(2)}, u32[]{:S(2)}) collective-permute-start(bf16[32,2176]{1,0:T(8,128)(2,1)S(1)} %collective-permute-done.2.refs_0_.refs_3_), channel_id=1, source_target_pairs={{0,2},{1,3},{2,0},{3,1},{4,6},{5,7},{6,4},{7,5},{8,10},{9,11},{10,... | collective-permute-start | bytes 417800 | tf_op jit(solution)/shard_map/ppermute | solution.py:50
  23.2 2.6 %shard_map.59 = (f32[64,2048]{1,0:T(8,128)S(1)}, f32[64,2048]{1,0:T(8,128)S(1)}, bf16[64,2048]{1,0:T(8,128)(2,1)S(1)}, bf16[32,2048]{1,0:T(8,128)(2,1)S(1)}, bf1...) custom-call(bf16[32,2176]{1,0:T(8,128)(2,1)S(1)} %collective-permute-done.2.refs_0_.refs_3_, ...), custom_call_target="tpu_custom_call" | custom-call | tf_op jit(solution)/shard_map/pallas_call | solution.py:28
  26.9 0.8 collective-permute-done.9.refs_5_
  28.2 1.0 %collective-permute-done.8.refs_2_ = bf16[32,2048]{1,0:T(8,128)(2,1)S(1)} collective-permute-done((bf16[32,2048]{1,0:T(8,128)(2,1)S(1)}, bf16[32,2048]{1,0:T(8,128)(2,1)S(1)}, u32[]{:S(2)}, u32[]{:S(2)}) %collective-permute-start.8) | collective-permute-done | bytes 131104 | tf_op jit(solution)/shard_map/ppermute | solution.py:50
  29.3 2.6 %shard_map.61 = (f32[64,2048]{1,0:T(8,128)S(1)}, f32[64,2048]{1,0:T(8,128)S(1)}, bf16[64,2048]{1,0:T(8,128)(2,1)S(1)}, bf16[32,2048]{1,0:T(8,128)(2,1)S(1)}, bf1...) custom-call(bf16[32,2048]{1,0:T(8,128)(2,1)S(1)} %get-tuple-element.78.refs_0_, ...), custom_call_target="tpu_custom_call" | custom-call | tf_op jit(solution)/shard_map/pallas_call | solution.py:28
  32.9 0.5 collective-permute-done.14.refs_1_
  33.7 1.6 %collective-permute-start.18 = (bf16[32,2048]{1,0:T(8,128)(2,1)S(1)}, bf16[32,2048]{1,0:T(8,128)(2,1)S(1)}, u32[]{:S(2)}, u32[]{:S(2)}) collective-permute-start(bf16[32,2048]{1,0:T(8,128)(2,1)S(1)} %get-tuple-element.75.refs_1_), channel_id=1, source_target_pairs={{0,2},{1,3},{2,0},{3,1},{4,6},{5,7},{6,4},{7,5},{8,10},{9,11},{10,... | collective-permute-start | bytes 393224 | tf_op jit(solution)/shard_map/ppermute | solution.py:50
  35.8 4.3 %collective-permute-done.18.refs_2_ = bf16[32,2048]{1,0:T(8,128)(2,1)S(1)} collective-permute-done((bf16[32,2048]{1,0:T(8,128)(2,1)S(1)}, bf16[32,2048]{1,0:T(8,128)(2,1)S(1)}, u32[]{:S(2)}, u32[]{:S(2)}) %collective-permute-start.18) | collective-permute-done | bytes 131104 | tf_op jit(solution)/shard_map/ppermute | solution.py:50
  40.2 0.5 collective-permute-start.23
  40.7 1.5 %collective-permute-start.19 = (bf16[32,2048]{1,0:T(8,128)(2,1)S(1)}, bf16[32,2048]{1,0:T(8,128)(2,1)S(1)}, u32[]{:S(2)}, u32[]{:S(2)}) collective-permute-start(bf16[32,2048]{1,0:T(8,128)(2,1)S(1)} %get-tuple-element.78.refs_0_), channel_id=1, source_target_pairs={{0,2},{1,3},{2,0},{3,1},{4,6},{5,7},{6,4},{7,5},{8,10},{9,11},{10,... | collective-permute-start | bytes 393224 | tf_op jit(solution)/shard_map/ppermute | solution.py:50
  42.7 2.5 %collective-permute-done.23.refs_3_ = bf16[32,2048]{1,0:T(8,128)(2,1)S(1)} collective-permute-done((bf16[32,2048]{1,0:T(8,128)(2,1)S(1)}, bf16[32,2048]{1,0:T(8,128)(2,1)S(1)}, u32[]{:S(2)}, u32[]{:S(2)}) %collective-permute-start.23) | collective-permute-done | bytes 131104 | tf_op jit(solution)/shard_map/ppermute | solution.py:50
  45.3 1.1 %collective-permute-start.24 = (bf16[32,2048]{1,0:T(8,128)(2,1)S(1)}, bf16[32,2048]{1,0:T(8,128)(2,1)S(1)}, u32[]{:S(2)}, u32[]{:S(2)}) collective-permute-start(bf16[32,2048]{1,0:T(8,128)(2,1)S(1)} %shard_map.66), channel_id=1, source_target_pairs={{0,8},{1,9},{2,10},{3,11},{4,12},{5,13},{6,14},{7,15},{8,0},{9,1},... | collective-permute-start | bytes 393224 | tf_op jit(solution)/shard_map/ppermute | solution.py:50
  46.4 1.4 %collective-permute-done.20.refs_5_ = bf16[32,2048]{1,0:T(8,128)(2,1)S(1)} collective-permute-done((bf16[32,2048]{1,0:T(8,128)(2,1)S(1)}, bf16[32,2048]{1,0:T(8,128)(2,1)S(1)}, u32[]{:S(2)}, u32[]{:S(2)}) %collective-permute-start.20) | collective-permute-done | bytes 131104 | tf_op jit(solution)/shard_map/ppermute | solution.py:50
  48.0 1.1 %collective-permute-start.21 = (bf16[32,2048]{1,0:T(8,128)(2,1)S(1)}, bf16[32,2048]{1,0:T(8,128)(2,1)S(1)}, u32[]{:S(2)}, u32[]{:S(2)}) collective-permute-start(bf16[32,2048]{1,0:T(8,128)(2,1)S(1)} %get-tuple-element.81), channel_id=1, source_target_pairs={{0,4},{1,5},{2,6},{3,7},{4,0},{5,1},{6,2},{7,3},{8,12},{9,13},{10,... | collective-permute-start | bytes 393224 | tf_op jit(solution)/shard_map/ppermute | solution.py:50
  49.0 3.7 %shard_map.62 = (bf16[2048,1536]{1,0:T(8,128)(2,1)S(1)}, bf16[768,2048]{1,0:T(8,128)(2,1)S(1)}, f32[8,128]{1,0:T(8,128)S(1)}) custom-call(f32[64,2048]{1,0:T(8,128)S(1)} %get-tuple-element.69.refs_0_, bf16[2,1,2048,1536]{3,2,1,0:T(8,128)(2,1)} %refs_1_.3, bf16[2,1,768,2048]{3,2,1,0:T(8,128)(2,1)} %refs_2_.4), custom_call_target="tpu_custom_call" | custom-call | tf_op jit(solution)/shard_map/pallas_call | solution.py:28
  52.8 0.7 collective-permute-done.21.refs_4_
  53.7 0.6 collective-permute-start.25
  54.3 2.8 %collective-permute-start.26 = (bf16[32,2048]{1,0:T(8,128)(2,1)S(1)}, bf16[32,2048]{1,0:T(8,128)(2,1)S(1)}, u32[]{:S(2)}, u32[]{:S(2)}) collective-permute-start(bf16[32,2048]{1,0:T(8,128)(2,1)S(1)} %get-tuple-element.83.refs_1_), channel_id=1, source_target_pairs={{0,8},{1,9},{2,10},{3,11},{4,12},{5,13},{6,14},{7,15},{8,0},{9,1},... | collective-permute-start | bytes 393224 | tf_op jit(solution)/shard_map/ppermute | solution.py:50
  57.1 2.7 %collective-permute-done.25.refs_2_ = bf16[32,2048]{1,0:T(8,128)(2,1)S(1)} collective-permute-done((bf16[32,2048]{1,0:T(8,128)(2,1)S(1)}, bf16[32,2048]{1,0:T(8,128)(2,1)S(1)}, u32[]{:S(2)}, u32[]{:S(2)}) %collective-permute-start.25) | collective-permute-done | bytes 131104 | tf_op jit(solution)/shard_map/ppermute | solution.py:50
  59.9 1.6 %collective-permute-start.28 = (bf16[64,2048]{1,0:T(8,128)(2,1)S(1)}, bf16[64,2048]{1,0:T(8,128)(2,1)S(1)}, u32[]{:S(2)}, u32[]{:S(2)}) collective-permute-start(bf16[64,2048]{1,0:T(8,128)(2,1)S(1)} %shard_map.68.refs_0_.refs_1_), channel_id=1, source_target_pairs={{0,2},{1,3},{2,0},{3,1},{4,6},{5,7},{6,4},{7,5},{8,10},{9,11},{10,... | collective-permute-start | bytes 786440 | tf_op jit(solution)/shard_map/ppermute | solution.py:50
  61.6 1.7 %collective-permute-start.29 = (bf16[32,2048]{1,0:T(8,128)(2,1)S(1)}, bf16[32,2048]{1,0:T(8,128)(2,1)S(1)}, u32[]{:S(2)}, u32[]{:S(2)}) collective-permute-start(bf16[32,2048]{1,0:T(8,128)(2,1)S(1)} %shard_map.69.refs_2_), channel_id=1, source_target_pairs={{0,2},{1,3},{2,0},{3,1},{4,6},{5,7},{6,4},{7,5},{8,10},{9,11},{10,... | collective-permute-start | bytes 393224 | tf_op jit(solution)/shard_map/ppermute | solution.py:50
  63.4 4.7 %collective-permute-done.29.refs_4_ = bf16[32,2048]{1,0:T(8,128)(2,1)S(1)} collective-permute-done((bf16[32,2048]{1,0:T(8,128)(2,1)S(1)}, bf16[32,2048]{1,0:T(8,128)(2,1)S(1)}, u32[]{:S(2)}, u32[]{:S(2)}) %collective-permute-start.29) | collective-permute-done | bytes 131104 | tf_op jit(solution)/shard_map/ppermute | solution.py:50
  68.2 1.5 %collective-permute-start.34 = (bf16[32,2048]{1,0:T(8,128)(2,1)S(1)}, bf16[32,2048]{1,0:T(8,128)(2,1)S(1)}, u32[]{:S(2)}, u32[]{:S(2)}) collective-permute-start(bf16[32,2048]{1,0:T(8,128)(2,1)S(1)} %collective-permute-done.27.refs_0_.refs_3_), channel_id=1, source_target_pairs={{0,2},{1,3},{2,0},{3,1},{4,6},{5,7},{6,4},{7,5},{8,10},{9,11},{10,... | collective-permute-start | bytes 393224 | tf_op jit(solution)/shard_map/ppermute | solution.py:50
  69.8 2.6 %shard_map.70 = (f32[64,2048]{1,0:T(8,128)S(1)}, f32[64,2048]{1,0:T(8,128)S(1)}, bf16[64,2048]{1,0:T(8,128)(2,1)S(1)}, bf16[32,2048]{1,0:T(8,128)(2,1)S(1)}, bf16[32,2048]{1,0:T(8,128)(2,1)S(1)}) custom-call(bf16[32,2048]{1,0:T(8,128)(2,1)S(1)} %collective-permute-done.27.refs_0_.refs_3_, bf16[64,2048]{1,0:T(8,128)(2,1)S(1)} %shard_map.68.refs_0_.refs_1_, ...), custom_call_target="tpu_custom_call" | custom-call | tf_op jit(solution)/shard_map/pallas_call | solution.py:28
  73.5 0.7 collective-permute-done.34.refs_5_
  74.6 0.8 collective-permute-done.33.refs_2_
  75.7 2.6 %shard_map.72 = (f32[64,2048]{1,0:T(8,128)S(1)}, f32[64,2048]{1,0:T(8,128)S(1)}, bf16[64,2048]{1,0:T(8,128)(2,1)S(1)}, bf16[32,2048]{1,0:T(8,128)(2,1)S(1)}, bf16[32,2048]{1,0:T(8,128)(2,1)S(1)}) custom-call(bf16[32,2048]{1,0:T(8,128)(2,1)S(1)} %get-tuple-element.105.refs_0_, bf16[32,2048]{1,0:T(8,128)(2,1)S(1)} %get-tuple-element.106.refs_1_, ...), custom_call_target="tpu_custom_call" | custom-call | tf_op jit(solution)/shard_map/pallas_call | solution.py:28
  79.2 0.5 collective-permute-done.39.refs_1_
  80.1 1.5 %collective-permute-start.43 = (bf16[32,2048]{1,0:T(8,128)(2,1)S(1)}, bf16[32,2048]{1,0:T(8,128)(2,1)S(1)}, u32[]{:S(2)}, u32[]{:S(2)}) collective-permute-start(bf16[32,2048]{1,0:T(8,128)(2,1)S(1)} %get-tuple-element.101.refs_1_), channel_id=1, source_target_pairs={{0,2},{1,3},{2,0},{3,1},{4,6},{5,7},{6,4},{7,5},{8,10},{9,11},{10,... | collective-permute-start | bytes 393224 | tf_op jit(solution)/shard_map/ppermute | solution.py:50
  81.5 0.6 collective-permute-start.47
  82.2 4.3 %collective-permute-done.43.refs_2_ = bf16[32,2048]{1,0:T(8,128)(2,1)S(1)} collective-permute-done((bf16[32,2048]{1,0:T(8,128)(2,1)S(1)}, bf16[32,2048]{1,0:T(8,128)(2,1)S(1)}, u32[]{:S(2)}, u32[]{:S(2)}) %collective-permute-start.43) | collective-permute-done | bytes 131104 | tf_op jit(solution)/shard_map/ppermute | solution.py:50
  86.7 1.3 %collective-permute-start.44 = (bf16[32,2048]{1,0:T(8,128)(2,1)S(1)}, bf16[32,2048]{1,0:T(8,128)(2,1)S(1)}, u32[]{:S(2)}, u32[]{:S(2)}) collective-permute-start(bf16[32,2048]{1,0:T(8,128)(2,1)S(1)} %get-tuple-element.105.refs_0_), channel_id=1, source_target_pairs={{0,2},{1,3},{2,0},{3,1},{4,6},{5,7},{6,4},{7,5},{8,10},{9,11},{10,... | collective-permute-start | bytes 393224 | tf_op jit(solution)/shard_map/ppermute | solution.py:50
  88.1 0.7 collective-permute-start.45
  89.1 2.4 %collective-permute-done.48.refs_3_ = bf16[32,2048]{1,0:T(8,128)(2,1)S(1)} collective-permute-done((bf16[32,2048]{1,0:T(8,128)(2,1)S(1)}, bf16[32,2048]{1,0:T(8,128)(2,1)S(1)}, u32[]{:S(2)}, u32[]{:S(2)}) %collective-permute-start.48) | collective-permute-done | bytes 131104 | tf_op jit(solution)/shard_map/ppermute | solution.py:50
  91.6 2.0 %collective-permute-start.49 = (bf16[32,2048]{1,0:T(8,128)(2,1)S(1)}, bf16[32,2048]{1,0:T(8,128)(2,1)S(1)}, u32[]{:S(2)}, u32[]{:S(2)}) collective-permute-start(bf16[32,2048]{1,0:T(8,128)(2,1)S(1)} %shard_map.76), channel_id=1, source_target_pairs={{0,8},{1,9},{2,10},{3,11},{4,12},{5,13},{6,14},{7,15},{8,0},{9,1},... | collective-permute-start | bytes 393224 | tf_op jit(solution)/shard_map/ppermute | solution.py:50
  93.6 0.5 collective-permute-done.45.refs_5_
  94.2 1.2 %collective-permute-start.46 = (bf16[32,2048]{1,0:T(8,128)(2,1)S(1)}, bf16[32,2048]{1,0:T(8,128)(2,1)S(1)}, u32[]{:S(2)}, u32[]{:S(2)}) collective-permute-start(bf16[32,2048]{1,0:T(8,128)(2,1)S(1)} %get-tuple-element.108), channel_id=1, source_target_pairs={{0,4},{1,5},{2,6},{3,7},{4,0},{5,1},{6,2},{7,3},{8,12},{9,13},{10,... | collective-permute-start | bytes 393224 | tf_op jit(solution)/shard_map/ppermute | solution.py:50
  95.5 3.4 %collective-permute-done.49.refs_3_ = bf16[32,2048]{1,0:T(8,128)(2,1)S(1)} collective-permute-done((bf16[32,2048]{1,0:T(8,128)(2,1)S(1)}, bf16[32,2048]{1,0:T(8,128)(2,1)S(1)}, u32[]{:S(2)}, u32[]{:S(2)}) %collective-permute-start.49) | collective-permute-done | bytes 131104 | tf_op jit(solution)/shard_map/ppermute | solution.py:50
  98.9 1.0 %collective-permute-done.46.refs_2_ = bf16[32,2048]{1,0:T(8,128)(2,1)S(1)} collective-permute-done((bf16[32,2048]{1,0:T(8,128)(2,1)S(1)}, bf16[32,2048]{1,0:T(8,128)(2,1)S(1)}, u32[]{:S(2)}, u32[]{:S(2)}) %collective-permute-start.46) | collective-permute-done | bytes 131104 | tf_op jit(solution)/shard_map/ppermute | solution.py:50
  99.9 0.8 shard_map.77
  (79 shorter events, 9.1 us)
Async XLA Ops:
  1.2 9.4 %collective-permute-start = (bf16[32,2176]{1,0:T(8,128)(2,1)S(1)}, bf16[32,2176]{1,0:T(8,128)(2,1)S(1)}, u32[]{:S(2)}, u32[]{:S(2)}) collective-permute-start(bf16[32,2176]{1,0:T(8,128)(2,1)S(1)} %shard_map.56.refs_1_), channel_id=1, source_target_pairs={{0,4},{1,5},{2,6},{3,7},{4,0},{5,1},{6,2},{7,3},{8,12},{9,13},{10,... | collective-permute-start | bytes 417800 | tf_op jit(solution)/shard_map/ppermute | solution.py:50
  4.3 9.1 %collective-permute-start.1 = (bf16[32,2176]{1,0:T(8,128)(2,1)S(1)}, bf16[32,2176]{1,0:T(8,128)(2,1)S(1)}, u32[]{:S(2)}, u32[]{:S(2)}) collective-permute-start(bf16[32,2176]{1,0:T(8,128)(2,1)S(1)} %shard_map.56.refs_1_), channel_id=1, source_target_pairs={{0,8},{1,9},{2,10},{3,11},{4,12},{5,13},{6,14},{7,15},{8,0},{9,1},... | collective-permute-start | bytes 417800 | tf_op jit(solution)/shard_map/ppermute | solution.py:50
  10.7 10.9 %collective-permute-start.3 = (bf16[64,2176]{1,0:T(8,128)(2,1)S(1)}, bf16[64,2176]{1,0:T(8,128)(2,1)S(1)}, u32[]{:S(2)}, u32[]{:S(2)}) collective-permute-start(bf16[64,2176]{1,0:T(8,128)(2,1)S(1)} %shard_map.57.refs_0_.refs_1_), channel_id=1, source_target_pairs={{0,2},{1,3},{2,0},{3,1},{4,6},{5,7},{6,4},{7,5},{8,10},{9,11},{10,... | collective-permute-start | bytes 835592 | tf_op jit(solution)/shard_map/ppermute | solution.py:50
  13.4 8.2 %collective-permute-start.4 = (bf16[32,2176]{1,0:T(8,128)(2,1)S(1)}, bf16[32,2176]{1,0:T(8,128)(2,1)S(1)}, u32[]{:S(2)}, u32[]{:S(2)}) collective-permute-start(bf16[32,2176]{1,0:T(8,128)(2,1)S(1)} %shard_map.58.refs_2_), channel_id=1, source_target_pairs={{0,2},{1,3},{2,0},{3,1},{4,6},{5,7},{6,4},{7,5},{8,10},{9,11},{10,... | collective-permute-start | bytes 417800 | tf_op jit(solution)/shard_map/ppermute | solution.py:50
  15.0 6.6 %collective-permute-start.2 = (bf16[32,2176]{1,0:T(8,128)(2,1)S(1)}, bf16[32,2176]{1,0:T(8,128)(2,1)S(1)}, u32[]{:S(2)}, u32[]{:S(2)}) collective-permute-start(bf16[32,2176]{1,0:T(8,128)(2,1)S(1)} %shard_map.58.refs_2_), channel_id=1, source_target_pairs={{0,4},{1,5},{2,6},{3,7},{4,0},{5,1},{6,2},{7,3},{8,12},{9,13},{10,... | collective-permute-start | bytes 417800 | tf_op jit(solution)/shard_map/ppermute | solution.py:50
  15.4 7.8 %collective-permute-start.5 = (bf16[64,2176]{1,0:T(8,128)(2,1)S(1)}, bf16[64,2176]{1,0:T(8,128)(2,1)S(1)}, u32[]{:S(2)}, u32[]{:S(2)}) collective-permute-start(bf16[64,2176]{1,0:T(8,128)(2,1)S(1)} %shard_map.57.refs_0_.refs_1_), channel_id=1, source_target_pairs={{0,1},{1,0},{2,3},{3,2},{4,5},{5,4},{6,7},{7,6},{8,9},{9,8},{10,11... | collective-permute-start | bytes 835592 | tf_op jit(solution)/shard_map/ppermute | solution.py:50
  21.6 1.6 %collective-permute-start.6 = (bf16[64,2176]{1,0:T(8,128)(2,1)S(1)}, bf16[64,2176]{1,0:T(8,128)(2,1)S(1)}, u32[]{:S(2)}, u32[]{:S(2)}) collective-permute-start(bf16[64,2176]{1,0:T(8,128)(2,1)S(1)} %collective-permute-done.3.refs_2_), channel_id=1, source_target_pairs={{0,1},{1,0},{2,3},{3,2},{4,5},{5,4},{6,7},{7,6},{8,9},{9,8},{10,11... | collective-permute-start | bytes 835592 | tf_op jit(solution)/shard_map/ppermute | solution.py:50
  21.6 6.1 %collective-permute-start.9 = (bf16[32,2176]{1,0:T(8,128)(2,1)S(1)}, bf16[32,2176]{1,0:T(8,128)(2,1)S(1)}, u32[]{:S(2)}, u32[]{:S(2)}) collective-permute-start(bf16[32,2176]{1,0:T(8,128)(2,1)S(1)} %collective-permute-done.2.refs_0_.refs_3_), channel_id=1, source_target_pairs={{0,2},{1,3},{2,0},{3,1},{4,6},{5,7},{6,4},{7,5},{8,10},{9,11},{10,... | collective-permute-start | bytes 417800 | tf_op jit(solution)/shard_map/ppermute | solution.py:50
  25.8 1.9 %collective-permute-start.7 = (bf16[32,2048]{1,0:T(8,128)(2,1)S(1)}, bf16[32,2048]{1,0:T(8,128)(2,1)S(1)}, u32[]{:S(2)}, u32[]{:S(2)}) collective-permute-start(bf16[32,2048]{1,0:T(8,128)(2,1)S(1)} %get-tuple-element.62), channel_id=1, source_target_pairs={{0,1},{1,0},{2,3},{3,2},{4,5},{5,4},{6,7},{7,6},{8,9},{9,8},{10,11... | collective-permute-start | bytes 393224 | tf_op jit(solution)/shard_map/ppermute | solution.py:50
  26.0 3.3 %collective-permute-start.10 = (bf16[32,2176]{1,0:T(8,128)(2,1)S(1)}, bf16[32,2176]{1,0:T(8,128)(2,1)S(1)}, u32[]{:S(2)}, u32[]{:S(2)}) collective-permute-start(bf16[32,2176]{1,0:T(8,128)(2,1)S(1)} %shard_map.58.refs_2_), channel_id=1, source_target_pairs={{0,1},{1,0},{2,3},{3,2},{4,5},{5,4},{6,7},{7,6},{8,9},{9,8},{10,11... | collective-permute-start | bytes 417800 | tf_op jit(solution)/shard_map/ppermute | solution.py:50
  26.4 2.9 %collective-permute-start.12 = (bf16[32,2176]{1,0:T(8,128)(2,1)S(1)}, bf16[32,2176]{1,0:T(8,128)(2,1)S(1)}, u32[]{:S(2)}, u32[]{:S(2)}) collective-permute-start(bf16[32,2176]{1,0:T(8,128)(2,1)S(1)} %collective-permute-done.4.refs_4_), channel_id=1, source_target_pairs={{0,1},{1,0},{2,3},{3,2},{4,5},{5,4},{6,7},{7,6},{8,9},{9,8},{10,11... | collective-permute-start | bytes 417800 | tf_op jit(solution)/shard_map/ppermute | solution.py:50
  26.6 2.8 %collective-permute-start.11 = (bf16[32,2176]{1,0:T(8,128)(2,1)S(1)}, bf16[32,2176]{1,0:T(8,128)(2,1)S(1)}, u32[]{:S(2)}, u32[]{:S(2)}) collective-permute-start(bf16[32,2176]{1,0:T(8,128)(2,1)S(1)} %collective-permute-done.2.refs_0_.refs_3_), channel_id=1, source_target_pairs={{0,1},{1,0},{2,3},{3,2},{4,5},{5,4},{6,7},{7,6},{8,9},{9,8},{10,11... | collective-permute-start | bytes 417800 | tf_op jit(solution)/shard_map/ppermute | solution.py:50
  27.7 1.6 %collective-permute-start.13 = (bf16[32,2176]{1,0:T(8,128)(2,1)S(1)}, bf16[32,2176]{1,0:T(8,128)(2,1)S(1)}, u32[]{:S(2)}, u32[]{:S(2)}) collective-permute-start(bf16[32,2176]{1,0:T(8,128)(2,1)S(1)} %collective-permute-done.9.refs_5_), channel_id=1, source_target_pairs={{0,1},{1,0},{2,3},{3,2},{4,5},{5,4},{6,7},{7,6},{8,9},{9,8},{10,11... | collective-permute-start | bytes 417800 | tf_op jit(solution)/shard_map/ppermute | solution.py:50
  27.7 1.5 %collective-permute-start.8 = (bf16[32,2048]{1,0:T(8,128)(2,1)S(1)}, bf16[32,2048]{1,0:T(8,128)(2,1)S(1)}, u32[]{:S(2)}, u32[]{:S(2)}) collective-permute-start(bf16[32,2048]{1,0:T(8,128)(2,1)S(1)} %get-tuple-element.63), channel_id=1, source_target_pairs={{0,1},{1,0},{2,3},{3,2},{4,5},{5,4},{6,7},{7,6},{8,9},{9,8},{10,11... | collective-permute-start | bytes 393224 | tf_op jit(solution)/shard_map/ppermute | solution.py:50
  32.0 1.4 %collective-permute-start.14 = (bf16[32,2048]{1,0:T(8,128)(2,1)S(1)}, bf16[32,2048]{1,0:T(8,128)(2,1)S(1)}, u32[]{:S(2)}, u32[]{:S(2)}) collective-permute-start(bf16[32,2048]{1,0:T(8,128)(2,1)S(1)} %get-tuple-element.72), channel_id=1, source_target_pairs={{0,1},{1,0},{2,3},{3,2},{4,5},{5,4},{6,7},{7,6},{8,9},{9,8},{10,11... | collective-permute-start | bytes 393224 | tf_op jit(solution)/shard_map/ppermute | solution.py:50
  32.3 1.3 %collective-permute-start.15 = (bf16[32,2048]{1,0:T(8,128)(2,1)S(1)}, bf16[32,2048]{1,0:T(8,128)(2,1)S(1)}, u32[]{:S(2)}, u32[]{:S(2)}) collective-permute-start(bf16[32,2048]{1,0:T(8,128)(2,1)S(1)} %get-tuple-element.73), channel_id=1, source_target_pairs={{0,1},{1,0},{2,3},{3,2},{4,5},{5,4},{6,7},{7,6},{8,9},{9,8},{10,11... | collective-permute-start | bytes 393224 | tf_op jit(solution)/shard_map/ppermute | solution.py:50
  32.5 7.6 %collective-permute-start.17 = (bf16[64,2048]{1,0:T(8,128)(2,1)S(1)}, bf16[64,2048]{1,0:T(8,128)(2,1)S(1)}, u32[]{:S(2)}, u32[]{:S(2)}) collective-permute-start(bf16[64,2048]{1,0:T(8,128)(2,1)S(1)} %get-tuple-element.77), channel_id=1, source_target_pairs={{0,1},{1,0},{2,3},{3,2},{4,5},{5,4},{6,7},{7,6},{8,9},{9,8},{10,11... | collective-permute-start | bytes 786440 | tf_op jit(solution)/shard_map/ppermute | solution.py:50
  33.7 6.4 %collective-permute-start.18 = (bf16[32,2048]{1,0:T(8,128)(2,1)S(1)}, bf16[32,2048]{1,0:T(8,128)(2,1)S(1)}, u32[]{:S(2)}, u32[]{:S(2)}) collective-permute-start(bf16[32,2048]{1,0:T(8,128)(2,1)S(1)} %get-tuple-element.75.refs_1_), channel_id=1, source_target_pairs={{0,2},{1,3},{2,0},{3,1},{4,6},{5,7},{6,4},{7,5},{8,10},{9,11},{10,... | collective-permute-start | bytes 393224 | tf_op jit(solution)/shard_map/ppermute | solution.py:50
  35.3 11.1 %collective-permute-start.16 = (bf16[64,2048]{1,0:T(8,128)(2,1)S(1)}, bf16[64,2048]{1,0:T(8,128)(2,1)S(1)}, u32[]{:S(2)}, u32[]{:S(2)}) collective-permute-start(bf16[64,2048]{1,0:T(8,128)(2,1)S(1)} %get-tuple-element.76), channel_id=1, source_target_pairs={{0,1},{1,0},{2,3},{3,2},{4,5},{5,4},{6,7},{7,6},{8,9},{9,8},{10,11... | collective-permute-start | bytes 786440 | tf_op jit(solution)/shard_map/ppermute | solution.py:50
  35.3 7.4 %collective-permute-start.22 = (bf16[32,2048]{1,0:T(8,128)(2,1)S(1)}, bf16[32,2048]{1,0:T(8,128)(2,1)S(1)}, u32[]{:S(2)}, u32[]{:S(2)}) collective-permute-start(bf16[32,2048]{1,0:T(8,128)(2,1)S(1)} %get-tuple-element.74.refs_0_), channel_id=1, source_target_pairs={{0,2},{1,3},{2,0},{3,1},{4,6},{5,7},{6,4},{7,5},{8,10},{9,11},{10,... | collective-permute-start | bytes 393224 | tf_op jit(solution)/shard_map/ppermute | solution.py:50
  40.2 5.0 %collective-permute-start.23 = (bf16[32,2048]{1,0:T(8,128)(2,1)S(1)}, bf16[32,2048]{1,0:T(8,128)(2,1)S(1)}, u32[]{:S(2)}, u32[]{:S(2)}) collective-permute-start(bf16[32,2048]{1,0:T(8,128)(2,1)S(1)} %shard_map.64), channel_id=1, source_target_pairs={{0,4},{1,5},{2,6},{3,7},{4,0},{5,1},{6,2},{7,3},{8,12},{9,13},{10,... | collective-permute-start | bytes 393224 | tf_op jit(solution)/shard_map/ppermute | solution.py:50
  40.7 5.7 %collective-permute-start.19 = (bf16[32,2048]{1,0:T(8,128)(2,1)S(1)}, bf16[32,2048]{1,0:T(8,128)(2,1)S(1)}, u32[]{:S(2)}, u32[]{:S(2)}) collective-permute-start(bf16[32,2048]{1,0:T(8,128)(2,1)S(1)} %get-tuple-element.78.refs_0_), channel_id=1, source_target_pairs={{0,2},{1,3},{2,0},{3,1},{4,6},{5,7},{6,4},{7,5},{8,10},{9,11},{10,... | collective-permute-start | bytes 393224 | tf_op jit(solution)/shard_map/ppermute | solution.py:50
  42.2 5.6 %collective-permute-start.20 = (bf16[32,2048]{1,0:T(8,128)(2,1)S(1)}, bf16[32,2048]{1,0:T(8,128)(2,1)S(1)}, u32[]{:S(2)}, u32[]{:S(2)}) collective-permute-start(bf16[32,2048]{1,0:T(8,128)(2,1)S(1)} %get-tuple-element.79.refs_1_), channel_id=1, source_target_pairs={{0,2},{1,3},{2,0},{3,1},{4,6},{5,7},{6,4},{7,5},{8,10},{9,11},{10,... | collective-permute-start | bytes 393224 | tf_op jit(solution)/shard_map/ppermute | solution.py:50
  45.3 7.5 %collective-permute-start.24 = (bf16[32,2048]{1,0:T(8,128)(2,1)S(1)}, bf16[32,2048]{1,0:T(8,128)(2,1)S(1)}, u32[]{:S(2)}, u32[]{:S(2)}) collective-permute-start(bf16[32,2048]{1,0:T(8,128)(2,1)S(1)} %shard_map.66), channel_id=1, source_target_pairs={{0,8},{1,9},{2,10},{3,11},{4,12},{5,13},{6,14},{7,15},{8,0},{9,1},... | collective-permute-start | bytes 393224 | tf_op jit(solution)/shard_map/ppermute | solution.py:50
  48.0 5.6 %collective-permute-start.21 = (bf16[32,2048]{1,0:T(8,128)(2,1)S(1)}, bf16[32,2048]{1,0:T(8,128)(2,1)S(1)}, u32[]{:S(2)}, u32[]{:S(2)}) collective-permute-start(bf16[32,2048]{1,0:T(8,128)(2,1)S(1)} %get-tuple-element.81), channel_id=1, source_target_pairs={{0,4},{1,5},{2,6},{3,7},{4,0},{5,1},{6,2},{7,3},{8,12},{9,13},{10,... | collective-permute-start | bytes 393224 | tf_op jit(solution)/shard_map/ppermute | solution.py:50
  53.7 6.1 %collective-permute-start.25 = (bf16[32,2048]{1,0:T(8,128)(2,1)S(1)}, bf16[32,2048]{1,0:T(8,128)(2,1)S(1)}, u32[]{:S(2)}, u32[]{:S(2)}) collective-permute-start(bf16[32,2048]{1,0:T(8,128)(2,1)S(1)} %get-tuple-element.83.refs_1_), channel_id=1, source_target_pairs={{0,4},{1,5},{2,6},{3,7},{4,0},{5,1},{6,2},{7,3},{8,12},{9,13},{10,... | collective-permute-start | bytes 393224 | tf_op jit(solution)/shard_map/ppermute | solution.py:50
  54.3 7.3 %collective-permute-start.26 = (bf16[32,2048]{1,0:T(8,128)(2,1)S(1)}, bf16[32,2048]{1,0:T(8,128)(2,1)S(1)}, u32[]{:S(2)}, u32[]{:S(2)}) collective-permute-start(bf16[32,2048]{1,0:T(8,128)(2,1)S(1)} %get-tuple-element.83.refs_1_), channel_id=1, source_target_pairs={{0,8},{1,9},{2,10},{3,11},{4,12},{5,13},{6,14},{7,15},{8,0},{9,1},... | collective-permute-start | bytes 393224 | tf_op jit(solution)/shard_map/ppermute | solution.py:50
  59.9 8.4 %collective-permute-start.28 = (bf16[64,2048]{1,0:T(8,128)(2,1)S(1)}, bf16[64,2048]{1,0:T(8,128)(2,1)S(1)}, u32[]{:S(2)}, u32[]{:S(2)}) collective-permute-start(bf16[64,2048]{1,0:T(8,128)(2,1)S(1)} %shard_map.68.refs_0_.refs_1_), channel_id=1, source_target_pairs={{0,2},{1,3},{2,0},{3,1},{4,6},{5,7},{6,4},{7,5},{8,10},{9,11},{10,... | collective-permute-start | bytes 786440 | tf_op jit(solution)/shard_map/ppermute | solution.py:50
  61.6 6.5 %collective-permute-start.29 = (bf16[32,2048]{1,0:T(8,128)(2,1)S(1)}, bf16[32,2048]{1,0:T(8,128)(2,1)S(1)}, u32[]{:S(2)}, u32[]{:S(2)}) collective-permute-start(bf16[32,2048]{1,0:T(8,128)(2,1)S(1)} %shard_map.69.refs_2_), channel_id=1, source_target_pairs={{0,2},{1,3},{2,0},{3,1},{4,6},{5,7},{6,4},{7,5},{8,10},{9,11},{10,... | collective-permute-start | bytes 393224 | tf_op jit(solution)/shard_map/ppermute | solution.py:50
  63.2 5.0 %collective-permute-start.27 = (bf16[32,2048]{1,0:T(8,128)(2,1)S(1)}, bf16[32,2048]{1,0:T(8,128)(2,1)S(1)}, u32[]{:S(2)}, u32[]{:S(2)}) collective-permute-start(bf16[32,2048]{1,0:T(8,128)(2,1)S(1)} %shard_map.69.refs_2_), channel_id=1, source_target_pairs={{0,4},{1,5},{2,6},{3,7},{4,0},{5,1},{6,2},{7,3},{8,12},{9,13},{10,... | collective-permute-start | bytes 393224 | tf_op jit(solution)/shard_map/ppermute | solution.py:50
  63.4 6.3 %collective-permute-start.30 = (bf16[64,2048]{1,0:T(8,128)(2,1)S(1)}, bf16[64,2048]{1,0:T(8,128)(2,1)S(1)}, u32[]{:S(2)}, u32[]{:S(2)}) collective-permute-start(bf16[64,2048]{1,0:T(8,128)(2,1)S(1)} %shard_map.68.refs_0_.refs_1_), channel_id=1, source_target_pairs={{0,1},{1,0},{2,3},{3,2},{4,5},{5,4},{6,7},{7,6},{8,9},{9,8},{10,11... | collective-permute-start | bytes 786440 | tf_op jit(solution)/shard_map/ppermute | solution.py:50
  68.2 1.5 %collective-permute-start.31 = (bf16[64,2048]{1,0:T(8,128)(2,1)S(1)}, bf16[64,2048]{1,0:T(8,128)(2,1)S(1)}, u32[]{:S(2)}, u32[]{:S(2)}) collective-permute-start(bf16[64,2048]{1,0:T(8,128)(2,1)S(1)} %collective-permute-done.28.refs_2_), channel_id=1, source_target_pairs={{0,1},{1,0},{2,3},{3,2},{4,5},{5,4},{6,7},{7,6},{8,9},{9,8},{10,11... | collective-permute-start | bytes 786440 | tf_op jit(solution)/shard_map/ppermute | solution.py:50
  68.2 5.9 %collective-permute-start.34 = (bf16[32,2048]{1,0:T(8,128)(2,1)S(1)}, bf16[32,2048]{1,0:T(8,128)(2,1)S(1)}, u32[]{:S(2)}, u32[]{:S(2)}) collective-permute-start(bf16[32,2048]{1,0:T(8,128)(2,1)S(1)} %collective-permute-done.27.refs_0_.refs_3_), channel_id=1, source_target_pairs={{0,2},{1,3},{2,0},{3,1},{4,6},{5,7},{6,4},{7,5},{8,10},{9,11},{10,... | collective-permute-start | bytes 393224 | tf_op jit(solution)/shard_map/ppermute | solution.py:50
  72.4 1.8 %collective-permute-start.32 = (bf16[32,2048]{1,0:T(8,128)(2,1)S(1)}, bf16[32,2048]{1,0:T(8,128)(2,1)S(1)}, u32[]{:S(2)}, u32[]{:S(2)}) collective-permute-start(bf16[32,2048]{1,0:T(8,128)(2,1)S(1)} %get-tuple-element.89), channel_id=1, source_target_pairs={{0,1},{1,0},{2,3},{3,2},{4,5},{5,4},{6,7},{7,6},{8,9},{9,8},{10,11... | collective-permute-start | bytes 393224 | tf_op jit(solution)/shard_map/ppermute | solution.py:50
  72.6 3.0 %collective-permute-start.35 = (bf16[32,2048]{1,0:T(8,128)(2,1)S(1)}, bf16[32,2048]{1,0:T(8,128)(2,1)S(1)}, u32[]{:S(2)}, u32[]{:S(2)}) collective-permute-start(bf16[32,2048]{1,0:T(8,128)(2,1)S(1)} %shard_map.69.refs_2_), channel_id=1, source_target_pairs={{0,1},{1,0},{2,3},{3,2},{4,5},{5,4},{6,7},{7,6},{8,9},{9,8},{10,11... | collective-permute-start | bytes 393224 | tf_op jit(solution)/shard_map/ppermute | solution.py:50
  73.0 2.6 %collective-permute-start.37 = (bf16[32,2048]{1,0:T(8,128)(2,1)S(1)}, bf16[32,2048]{1,0:T(8,128)(2,1)S(1)}, u32[]{:S(2)}, u32[]{:S(2)}) collective-permute-start(bf16[32,2048]{1,0:T(8,128)(2,1)S(1)} %collective-permute-done.29.refs_4_), channel_id=1, source_target_pairs={{0,1},{1,0},{2,3},{3,2},{4,5},{5,4},{6,7},{7,6},{8,9},{9,8},{10,11... | collective-permute-start | bytes 393224 | tf_op jit(solution)/shard_map/ppermute | solution.py:50
  73.1 2.5 %collective-permute-start.36 = (bf16[32,2048]{1,0:T(8,128)(2,1)S(1)}, bf16[32,2048]{1,0:T(8,128)(2,1)S(1)}, u32[]{:S(2)}, u32[]{:S(2)}) collective-permute-start(bf16[32,2048]{1,0:T(8,128)(2,1)S(1)} %collective-permute-done.27.refs_0_.refs_3_), channel_id=1, source_target_pairs={{0,1},{1,0},{2,3},{3,2},{4,5},{5,4},{6,7},{7,6},{8,9},{9,8},{10,11... | collective-permute-start | bytes 393224 | tf_op jit(solution)/shard_map/ppermute | solution.py:50
  74.1 1.5 %collective-permute-start.38 = (bf16[32,2048]{1,0:T(8,128)(2,1)S(1)}, bf16[32,2048]{1,0:T(8,128)(2,1)S(1)}, u32[]{:S(2)}, u32[]{:S(2)}) collective-permute-start(bf16[32,2048]{1,0:T(8,128)(2,1)S(1)} %collective-permute-done.34.refs_5_), channel_id=1, source_target_pairs={{0,1},{1,0},{2,3},{3,2},{4,5},{5,4},{6,7},{7,6},{8,9},{9,8},{10,11... | collective-permute-start | bytes 393224 | tf_op jit(solution)/shard_map/ppermute | solution.py:50
  78.3 1.4 %collective-permute-start.39 = (bf16[32,2048]{1,0:T(8,128)(2,1)S(1)}, bf16[32,2048]{1,0:T(8,128)(2,1)S(1)}, u32[]{:S(2)}, u32[]{:S(2)}) collective-permute-start(bf16[32,2048]{1,0:T(8,128)(2,1)S(1)} %get-tuple-element.98), channel_id=1, source_target_pairs={{0,1},{1,0},{2,3},{3,2},{4,5},{5,4},{6,7},{7,6},{8,9},{9,8},{10,11... | collective-permute-start | bytes 393224 | tf_op jit(solution)/shard_map/ppermute | solution.py:50
  78.9 3.3 %collective-permute-start.42 = (bf16[64,2048]{1,0:T(8,128)(2,1)S(1)}, bf16[64,2048]{1,0:T(8,128)(2,1)S(1)}, u32[]{:S(2)}, u32[]{:S(2)}) collective-permute-start(bf16[64,2048]{1,0:T(8,128)(2,1)S(1)} %get-tuple-element.104), channel_id=1, source_target_pairs={{0,1},{1,0},{2,3},{3,2},{4,5},{5,4},{6,7},{7,6},{8,9},{9,8},{10,11... | collective-permute-start | bytes 786440 | tf_op jit(solution)/shard_map/ppermute | solution.py:50
  80.1 6.4 %collective-permute-start.43 = (bf16[32,2048]{1,0:T(8,128)(2,1)S(1)}, bf16[32,2048]{1,0:T(8,128)(2,1)S(1)}, u32[]{:S(2)}, u32[]{:S(2)}) collective-permute-start(bf16[32,2048]{1,0:T(8,128)(2,1)S(1)} %get-tuple-element.101.refs_1_), channel_id=1, source_target_pairs={{0,2},{1,3},{2,0},{3,1},{4,6},{5,7},{6,4},{7,5},{8,10},{9,11},{10,... | collective-permute-start | bytes 393224 | tf_op jit(solution)/shard_map/ppermute | solution.py:50
  81.5 12.1 %collective-permute-start.41 = (bf16[64,2048]{1,0:T(8,128)(2,1)S(1)}, bf16[64,2048]{1,0:T(8,128)(2,1)S(1)}, u32[]{:S(2)}, u32[]{:S(2)}) collective-permute-start(bf16[64,2048]{1,0:T(8,128)(2,1)S(1)} %get-tuple-element.102), channel_id=1, source_target_pairs={{0,1},{1,0},{2,3},{3,2},{4,5},{5,4},{6,7},{7,6},{8,9},{9,8},{10,11... | collective-permute-start | bytes 786440 | tf_op jit(solution)/shard_map/ppermute | solution.py:50
  81.5 7.6 %collective-permute-start.47 = (bf16[32,2048]{1,0:T(8,128)(2,1)S(1)}, bf16[32,2048]{1,0:T(8,128)(2,1)S(1)}, u32[]{:S(2)}, u32[]{:S(2)}) collective-permute-start(bf16[32,2048]{1,0:T(8,128)(2,1)S(1)} %get-tuple-element.100.refs_0_), channel_id=1, source_target_pairs={{0,2},{1,3},{2,0},{3,1},{4,6},{5,7},{6,4},{7,5},{8,10},{9,11},{10,... | collective-permute-start | bytes 393224 | tf_op jit(solution)/shard_map/ppermute | solution.py:50
  86.5 5.0 %collective-permute-start.48 = (bf16[32,2048]{1,0:T(8,128)(2,1)S(1)}, bf16[32,2048]{1,0:T(8,128)(2,1)S(1)}, u32[]{:S(2)}, u32[]{:S(2)}) collective-permute-start(bf16[32,2048]{1,0:T(8,128)(2,1)S(1)} %shard_map.74), channel_id=1, source_target_pairs={{0,4},{1,5},{2,6},{3,7},{4,0},{5,1},{6,2},{7,3},{8,12},{9,13},{10,... | collective-permute-start | bytes 393224 | tf_op jit(solution)/shard_map/ppermute | solution.py:50
  86.7 6.9 %collective-permute-start.44 = (bf16[32,2048]{1,0:T(8,128)(2,1)S(1)}, bf16[32,2048]{1,0:T(8,128)(2,1)S(1)}, u32[]{:S(2)}, u32[]{:S(2)}) collective-permute-start(bf16[32,2048]{1,0:T(8,128)(2,1)S(1)} %get-tuple-element.105.refs_0_), channel_id=1, source_target_pairs={{0,2},{1,3},{2,0},{3,1},{4,6},{5,7},{6,4},{7,5},{8,10},{9,11},{10,... | collective-permute-start | bytes 393224 | tf_op jit(solution)/shard_map/ppermute | solution.py:50
  88.1 6.1 %collective-permute-start.45 = (bf16[32,2048]{1,0:T(8,128)(2,1)S(1)}, bf16[32,2048]{1,0:T(8,128)(2,1)S(1)}, u32[]{:S(2)}, u32[]{:S(2)}) collective-permute-start(bf16[32,2048]{1,0:T(8,128)(2,1)S(1)} %get-tuple-element.106.refs_1_), channel_id=1, source_target_pairs={{0,2},{1,3},{2,0},{3,1},{4,6},{5,7},{6,4},{7,5},{8,10},{9,11},{10,... | collective-permute-start | bytes 393224 | tf_op jit(solution)/shard_map/ppermute | solution.py:50
  91.6 7.3 %collective-permute-start.49 = (bf16[32,2048]{1,0:T(8,128)(2,1)S(1)}, bf16[32,2048]{1,0:T(8,128)(2,1)S(1)}, u32[]{:S(2)}, u32[]{:S(2)}) collective-permute-start(bf16[32,2048]{1,0:T(8,128)(2,1)S(1)} %shard_map.76), channel_id=1, source_target_pairs={{0,8},{1,9},{2,10},{3,11},{4,12},{5,13},{6,14},{7,15},{8,0},{9,1},... | collective-permute-start | bytes 393224 | tf_op jit(solution)/shard_map/ppermute | solution.py:50
  94.2 5.7 %collective-permute-start.46 = (bf16[32,2048]{1,0:T(8,128)(2,1)S(1)}, bf16[32,2048]{1,0:T(8,128)(2,1)S(1)}, u32[]{:S(2)}, u32[]{:S(2)}) collective-permute-start(bf16[32,2048]{1,0:T(8,128)(2,1)S(1)} %get-tuple-element.108), channel_id=1, source_target_pairs={{0,4},{1,5},{2,6},{3,7},{4,0},{5,1},{6,2},{7,3},{8,12},{9,13},{10,... | collective-permute-start | bytes 393224 | tf_op jit(solution)/shard_map/ppermute | solution.py:50
  (4 other events, 13.8 us)

commit v15 on v14

--- a/solution.py
+++ b/solution.py
@@ -331,13 +331,13 @@
     routed = routed or [None, None]
     half = far // 2
     sent = [rows] + [swap(rows, 4, k, far) for k in range(1, half)]
-    first = join_rows(sent, loaded, 0)
+    first = join_rows(sent, (), 0)
     first_beside = swap(first, 2, 1, 2)
     crossed = join_rows([swap(rows, 4, half, far)], (first,), WAIT)
     second = [crossed] + [swap(crossed, 4, k, far) for k in range(1, half)]
     second_beside = [swap(crossed, 2, 1, 2)]
     for piece in second[1:]:
-        second_beside.append(swap(held(piece, (second_beside[0], first_beside)), 2, 1, 2))
+        second_beside.append(swap(held(piece, (second_beside[0], first_beside, *loaded)), 2, 1, 2))
 
     def worked(near, beside, routed, after):
         parts = near + beside

time: 101 us -> 103 us (1.020)
  starting transfers between devices: 38.6 us -> 44.1 us
  waiting for transfers between devices: 41 us -> 36.9 us
    ppermute x50, starting transfers between devices: 38.6 us -> 44.1 us  [swap(): lax.ppermute(value, 'expert', [(i, partner(i)) for i in range(count)])]
    ppermute x50, waiting for transfers between devices: 41 us -> 36.9 us  [swap(): lax.ppermute(value, 'expert', [(i, partner(i)) for i in range(count)])]
  transfers between devices with their start and end apart: 50 -> 50, of which waited for: 26 -> 23; matrix products, arithmetic and copies ran while one was open for 0% -> 0% of each run, Pallas kernels for 13% -> 14%
where the time goes in v15:
time: 103 us
  starting transfers between devices  44.1 us (43%)
  waiting for transfers between devices  36.9 us (36%)
  Pallas kernels  21.4 us (21%)
    ppermute x50, starting transfers between devices, swap(): lax.ppermute(value, 'expert', [(i, partner(i)) for i in range(count)])  44.1 us
    ppermute x50, waiting for transfers between devices, swap(): lax.ppermute(value, 'expert', [(i, partner(i)) for i in range(count)])  36.9 us
    pallas_call x23, Pallas kernels, call(): pl.pallas_call(lambda *refs: kernel(*refs[len(after):]), out_shape=shapes...  21.4 us
  transfers between devices with their start and end apart: 50, of which 23 were waited for; matrix products, arithmetic and copies ran while one was open for 0% of the time, Pallas kernels for 14%

profile of v15, /device:TPU:0, one launch (start us, length us, event | category | flops | bytes accessed | tf_op | source)
XLA Modules:
  0.0 102.7 jit_solution(3365234247780793112)
XLA Ops:
  0.0 1.2 %shard_map.55.refs_0_ = bf16[32,2176]{1,0:T(8,128)(2,1)S(1)} custom-call(bf16[32,2048]{1,0:T(8,128)(2,1)} %bitcast.2, s32[2,2,8,16]{3,2,1,0:T(8,128)} %bitcast.4, f32[2,2048]{1,0:T(2,128)} %refs_2_.5), custom_call_target="tpu_custom_call" | custom-call | tf_op jit(solution)/shard_map/pallas_call | solution.py:28
  1.2 3.1 %collective-permute-start = (bf16[32,2176]{1,0:T(8,128)(2,1)S(1)}, bf16[32,2176]{1,0:T(8,128)(2,1)S(1)}, u32[]{:S(2)}, u32[]{:S(2)}) collective-permute-start(bf16[32,2176]{1,0:T(8,128)(2,1)S(1)} %shard_map.55.refs_0_), channel_id=1, source_target_pairs={{0,4},{1,5},{2,6},{3,7},{4,0},{5,1},{6,2},{7,3},{8,12},{9,13},{10,... | collective-permute-start | bytes 417800 | tf_op jit(solution)/shard_map/ppermute | solution.py:50
  4.3 2.6 %collective-permute-start.1 = (bf16[32,2176]{1,0:T(8,128)(2,1)S(1)}, bf16[32,2176]{1,0:T(8,128)(2,1)S(1)}, u32[]{:S(2)}, u32[]{:S(2)}) collective-permute-start(bf16[32,2176]{1,0:T(8,128)(2,1)S(1)} %shard_map.55.refs_0_), channel_id=1, source_target_pairs={{0,8},{1,9},{2,10},{3,11},{4,12},{5,13},{6,14},{7,15},{8,0},{9,1},... | collective-permute-start | bytes 417800 | tf_op jit(solution)/shard_map/ppermute | solution.py:50
  6.9 3.3 %collective-permute-done.refs_1_ = bf16[32,2176]{1,0:T(8,128)(2,1)S(1)} collective-permute-done((bf16[32,2176]{1,0:T(8,128)(2,1)S(1)}, bf16[32,2176]{1,0:T(8,128)(2,1)S(1)}, u32[]{:S(2)}, u32[]{:S(2)}) %collective-permute-start) | collective-permute-done | bytes 139296 | tf_op jit(solution)/shard_map/ppermute | solution.py:50
  10.2 1.9 %collective-permute-start.3 = (bf16[64,2176]{1,0:T(8,128)(2,1)S(1)}, bf16[64,2176]{1,0:T(8,128)(2,1)S(1)}, u32[]{:S(2)}, u32[]{:S(2)}) collective-permute-start(bf16[64,2176]{1,0:T(8,128)(2,1)S(1)} %shard_map.56.refs_0_.refs_1_), channel_id=1, source_target_pairs={{0,2},{1,3},{2,0},{3,1},{4,6},{5,7},{6,4},{7,5},{8,10},{9,11},{10,... | collective-permute-start | bytes 835592 | tf_op jit(solution)/shard_map/ppermute | solution.py:50
  12.1 1.3 %collective-permute-done.1.refs_1_ = bf16[32,2176]{1,0:T(8,128)(2,1)S(1)} collective-permute-done((bf16[32,2176]{1,0:T(8,128)(2,1)S(1)}, bf16[32,2176]{1,0:T(8,128)(2,1)S(1)}, u32[]{:S(2)}, u32[]{:S(2)}) %collective-permute-start.1) | collective-permute-done | bytes 139296 | tf_op jit(solution)/shard_map/ppermute | solution.py:50
  13.4 1.6 %collective-permute-start.4 = (bf16[32,2176]{1,0:T(8,128)(2,1)S(1)}, bf16[32,2176]{1,0:T(8,128)(2,1)S(1)}, u32[]{:S(2)}, u32[]{:S(2)}) collective-permute-start(bf16[32,2176]{1,0:T(8,128)(2,1)S(1)} %shard_map.57.refs_2_), channel_id=1, source_target_pairs={{0,2},{1,3},{2,0},{3,1},{4,6},{5,7},{6,4},{7,5},{8,10},{9,11},{10,... | collective-permute-start | bytes 417800 | tf_op jit(solution)/shard_map/ppermute | solution.py:50
  15.4 3.5 %collective-permute-done.4.refs_4_ = bf16[32,2176]{1,0:T(8,128)(2,1)S(1)} collective-permute-done((bf16[32,2176]{1,0:T(8,128)(2,1)S(1)}, bf16[32,2176]{1,0:T(8,128)(2,1)S(1)}, u32[]{:S(2)}, u32[]{:S(2)}) %collective-permute-start.4) | collective-permute-done | bytes 139296 | tf_op jit(solution)/shard_map/ppermute | solution.py:50
  18.9 1.1 %collective-permute-done.2.refs_0_.refs_3_ = bf16[32,2176]{1,0:T(8,128)(2,1)S(1)} collective-permute-done((bf16[32,2176]{1,0:T(8,128)(2,1)S(1)}, bf16[32,2176]{1,0:T(8,128)(2,1)S(1)}, u32[]{:S(2)}, u32[]{:S(2)}) %collective-permute-start.2) | collective-permute-done | bytes 139296 | tf_op jit(solution)/shard_map/ppermute | solution.py:50
  20.0 0.5 collective-permute-start.9
  20.5 4.3 %shard_map.58 = (bf16[2048,1536]{1,0:T(8,128)(2,1)S(1)}, bf16[768,2048]{1,0:T(8,128)(2,1)S(1)}, f32[8,128]{1,0:T(8,128)}) custom-call(bf16[2,1,2048,1536]{3,2,1,0:T(8,128)(2,1)} %refs_1_.3, bf16[2,1,768,2048]{3,2,1,0:T(8,128)(2,1)} %refs_2_.4), custom_call_target="tpu_custom_call" | custom-call | tf_op jit(solution)/shard_map/pallas_call | solution.py:28
  24.9 2.6 %shard_map.59 = (f32[64,2048]{1,0:T(8,128)S(1)}, f32[64,2048]{1,0:T(8,128)S(1)}, bf16[64,2048]{1,0:T(8,128)(2,1)S(1)}, bf16[32,2048]{1,0:T(8,128)(2,1)S(1)}, bf1...) custom-call(bf16[32,2176]{1,0:T(8,128)(2,1)S(1)} %collective-permute-done.2.refs_0_.refs_3_, ...), custom_call_target="tpu_custom_call" | custom-call | tf_op jit(solution)/shard_map/pallas_call | solution.py:28
  29.2 1.1 %collective-permute-done.8.refs_2_ = bf16[32,2048]{1,0:T(8,128)(2,1)S(1)} collective-permute-done((bf16[32,2048]{1,0:T(8,128)(2,1)S(1)}, bf16[32,2048]{1,0:T(8,128)(2,1)S(1)}, u32[]{:S(2)}, u32[]{:S(2)}) %collective-permute-start.8) | collective-permute-done | bytes 131104 | tf_op jit(solution)/shard_map/ppermute | solution.py:50
  30.4 2.6 %shard_map.61 = (f32[64,2048]{1,0:T(8,128)S(1)}, f32[64,2048]{1,0:T(8,128)S(1)}, bf16[64,2048]{1,0:T(8,128)(2,1)S(1)}, bf16[32,2048]{1,0:T(8,128)(2,1)S(1)}, bf1...) custom-call(bf16[32,2048]{1,0:T(8,128)(2,1)S(1)} %get-tuple-element.76.refs_0_, ...), custom_call_target="tpu_custom_call" | custom-call | tf_op jit(solution)/shard_map/pallas_call | solution.py:28
  33.8 0.6 collective-permute-done.14.refs_1_
  34.7 1.6 %collective-permute-start.18 = (bf16[32,2048]{1,0:T(8,128)(2,1)S(1)}, bf16[32,2048]{1,0:T(8,128)(2,1)S(1)}, u32[]{:S(2)}, u32[]{:S(2)}) collective-permute-start(bf16[32,2048]{1,0:T(8,128)(2,1)S(1)} %get-tuple-element.73.refs_1_), channel_id=1, source_target_pairs={{0,2},{1,3},{2,0},{3,1},{4,6},{5,7},{6,4},{7,5},{8,10},{9,11},{10,... | collective-permute-start | bytes 393224 | tf_op jit(solution)/shard_map/ppermute | solution.py:50
  36.3 0.5 collective-permute-start.22
  36.8 4.3 %collective-permute-done.18.refs_2_ = bf16[32,2048]{1,0:T(8,128)(2,1)S(1)} collective-permute-done((bf16[32,2048]{1,0:T(8,128)(2,1)S(1)}, bf16[32,2048]{1,0:T(8,128)(2,1)S(1)}, u32[]{:S(2)}, u32[]{:S(2)}) %collective-permute-start.18) | collective-permute-done | bytes 131104 | tf_op jit(solution)/shard_map/ppermute | solution.py:50
  41.2 1.4 %collective-permute-start.23 = (bf16[32,2048]{1,0:T(8,128)(2,1)S(1)}, bf16[32,2048]{1,0:T(8,128)(2,1)S(1)}, u32[]{:S(2)}, u32[]{:S(2)}) collective-permute-start(bf16[32,2048]{1,0:T(8,128)(2,1)S(1)} %shard_map.64), channel_id=1, source_target_pairs={{0,4},{1,5},{2,6},{3,7},{4,0},{5,1},{6,2},{7,3},{8,12},{9,13},{10,... | collective-permute-start | bytes 393224 | tf_op jit(solution)/shard_map/ppermute | solution.py:50
  42.6 0.6 collective-permute-start.19
  43.2 1.4 %collective-permute-start.20 = (bf16[32,2048]{1,0:T(8,128)(2,1)S(1)}, bf16[32,2048]{1,0:T(8,128)(2,1)S(1)}, u32[]{:S(2)}, u32[]{:S(2)}) collective-permute-start(bf16[32,2048]{1,0:T(8,128)(2,1)S(1)} %get-tuple-element.77.refs_1_), channel_id=1, source_target_pairs={{0,2},{1,3},{2,0},{3,1},{4,6},{5,7},{6,4},{7,5},{8,10},{9,11},{10,... | collective-permute-start | bytes 393224 | tf_op jit(solution)/shard_map/ppermute | solution.py:50
  44.6 1.6 %collective-permute-done.23.refs_3_ = bf16[32,2048]{1,0:T(8,128)(2,1)S(1)} collective-permute-done((bf16[32,2048]{1,0:T(8,128)(2,1)S(1)}, bf16[32,2048]{1,0:T(8,128)(2,1)S(1)}, u32[]{:S(2)}, u32[]{:S(2)}) %collective-permute-start.23) | collective-permute-done | bytes 131104 | tf_op jit(solution)/shard_map/ppermute | solution.py:50
  46.3 3.7 %collective-permute-start.24 = (bf16[32,2048]{1,0:T(8,128)(2,1)S(1)}, bf16[32,2048]{1,0:T(8,128)(2,1)S(1)}, u32[]{:S(2)}, u32[]{:S(2)}) collective-permute-start(bf16[32,2048]{1,0:T(8,128)(2,1)S(1)} %shard_map.66), channel_id=1, source_target_pairs={{0,8},{1,9},{2,10},{3,11},{4,12},{5,13},{6,14},{7,15},{8,0},{9,1},... | collective-permute-start | bytes 393224 | tf_op jit(solution)/shard_map/ppermute | solution.py:50
  50.1 2.1 %collective-permute-start.21 = (bf16[32,2048]{1,0:T(8,128)(2,1)S(1)}, bf16[32,2048]{1,0:T(8,128)(2,1)S(1)}, u32[]{:S(2)}, u32[]{:S(2)}) collective-permute-start(bf16[32,2048]{1,0:T(8,128)(2,1)S(1)} %get-tuple-element.79), channel_id=1, source_target_pairs={{0,4},{1,5},{2,6},{3,7},{4,0},{5,1},{6,2},{7,3},{8,12},{9,13},{10,... | collective-permute-start | bytes 393224 | tf_op jit(solution)/shard_map/ppermute | solution.py:50
  52.2 3.7 %shard_map.62 = (bf16[2048,1536]{1,0:T(8,128)(2,1)S(1)}, bf16[768,2048]{1,0:T(8,128)(2,1)S(1)}, f32[8,128]{1,0:T(8,128)S(1)}) custom-call(f32[64,2048]{1,0:T(8,128)S(1)} %get-tuple-element.67.refs_0_, bf16[2,1,2048,1536]{3,2,1,0:T(8,128)(2,1)} %refs_1_.3, bf16[2,1,768,2048]{3,2,1,0:T(8,128)(2,1)} %refs_2_.4), custom_call_target="tpu_custom_call" | custom-call | tf_op jit(solution)/shard_map/pallas_call | solution.py:28
  56.2 1.7 %collective-permute-start.25 = (bf16[32,2048]{1,0:T(8,128)(2,1)S(1)}, bf16[32,2048]{1,0:T(8,128)(2,1)S(1)}, u32[]{:S(2)}, u32[]{:S(2)}) collective-permute-start(bf16[32,2048]{1,0:T(8,128)(2,1)S(1)} %get-tuple-element.81.refs_0_), channel_id=1, source_target_pairs={{0,4},{1,5},{2,6},{3,7},{4,0},{5,1},{6,2},{7,3},{8,12},{9,13},{10,... | collective-permute-start | bytes 393224 | tf_op jit(solution)/shard_map/ppermute | solution.py:50
  57.9 2.7 %collective-permute-start.26 = (bf16[32,2048]{1,0:T(8,128)(2,1)S(1)}, bf16[32,2048]{1,0:T(8,128)(2,1)S(1)}, u32[]{:S(2)}, u32[]{:S(2)}) collective-permute-start(bf16[32,2048]{1,0:T(8,128)(2,1)S(1)} %get-tuple-element.81.refs_0_), channel_id=1, source_target_pairs={{0,8},{1,9},{2,10},{3,11},{4,12},{5,13},{6,14},{7,15},{8,0},{9,1},... | collective-permute-start | bytes 393224 | tf_op jit(solution)/shard_map/ppermute | solution.py:50
  60.5 0.7 collective-permute-done.25.refs_1_
  61.2 0.6 collective-permute-start.28
  61.8 3.3 %collective-permute-done.26.refs_1_ = bf16[32,2048]{1,0:T(8,128)(2,1)S(1)} collective-permute-done((bf16[32,2048]{1,0:T(8,128)(2,1)S(1)}, bf16[32,2048]{1,0:T(8,128)(2,1)S(1)}, u32[]{:S(2)}, u32[]{:S(2)}) %collective-permute-start.26) | collective-permute-done | bytes 131104 | tf_op jit(solution)/shard_map/ppermute | solution.py:50
  65.2 0.9 collective-permute-start.27
  66.2 4.0 %collective-permute-done.29.refs_4_ = bf16[32,2048]{1,0:T(8,128)(2,1)S(1)} collective-permute-done((bf16[32,2048]{1,0:T(8,128)(2,1)S(1)}, bf16[32,2048]{1,0:T(8,128)(2,1)S(1)}, u32[]{:S(2)}, u32[]{:S(2)}) %collective-permute-start.29) | collective-permute-done | bytes 131104 | tf_op jit(solution)/shard_map/ppermute | solution.py:50
  70.3 1.9 %collective-permute-start.34 = (bf16[32,2048]{1,0:T(8,128)(2,1)S(1)}, bf16[32,2048]{1,0:T(8,128)(2,1)S(1)}, u32[]{:S(2)}, u32[]{:S(2)}) collective-permute-start(bf16[32,2048]{1,0:T(8,128)(2,1)S(1)} %collective-permute-done.27.refs_0_.refs_3_), channel_id=1, source_target_pairs={{0,2},{1,3},{2,0},{3,1},{4,6},{5,7},{6,4},{7,5},{8,10},{9,11},{10,... | collective-permute-start | bytes 393224 | tf_op jit(solution)/shard_map/ppermute | solution.py:50
  72.2 2.6 %shard_map.70 = (f32[64,2048]{1,0:T(8,128)S(1)}, f32[64,2048]{1,0:T(8,128)S(1)}, bf16[64,2048]{1,0:T(8,128)(2,1)S(1)}, bf16[32,2048]{1,0:T(8,128)(2,1)S(1)}, bf16[32,2048]{1,0:T(8,128)(2,1)S(1)}) custom-call(bf16[32,2048]{1,0:T(8,128)(2,1)S(1)} %collective-permute-done.27.refs_0_.refs_3_, bf16[64,2048]{1,0:T(8,128)(2,1)S(1)} %shard_map.68.refs_0_.refs_1_, ...), custom_call_target="tpu_custom_call" | custom-call | tf_op jit(solution)/shard_map/pallas_call | solution.py:28
  76.4 0.5 collective-permute-start.38
  76.9 0.8 collective-permute-done.33.refs_2_
  77.9 2.6 %shard_map.72 = (f32[64,2048]{1,0:T(8,128)S(1)}, f32[64,2048]{1,0:T(8,128)S(1)}, bf16[64,2048]{1,0:T(8,128)(2,1)S(1)}, bf16[32,2048]{1,0:T(8,128)(2,1)S(1)}, bf16[32,2048]{1,0:T(8,128)(2,1)S(1)}) custom-call(bf16[32,2048]{1,0:T(8,128)(2,1)S(1)} %get-tuple-element.103.refs_0_, bf16[32,2048]{1,0:T(8,128)(2,1)S(1)} %get-tuple-element.104.refs_1_, ...), custom_call_target="tpu_custom_call" | custom-call | tf_op jit(solution)/shard_map/pallas_call | solution.py:28
  81.4 0.5 collective-permute-done.39.refs_1_
  82.3 1.8 %collective-permute-start.43 = (bf16[32,2048]{1,0:T(8,128)(2,1)S(1)}, bf16[32,2048]{1,0:T(8,128)(2,1)S(1)}, u32[]{:S(2)}, u32[]{:S(2)}) collective-permute-start(bf16[32,2048]{1,0:T(8,128)(2,1)S(1)} %get-tuple-element.99.refs_1_), channel_id=1, source_target_pairs={{0,2},{1,3},{2,0},{3,1},{4,6},{5,7},{6,4},{7,5},{8,10},{9,11},{10,... | collective-permute-start | bytes 393224 | tf_op jit(solution)/shard_map/ppermute | solution.py:50
  84.4 4.3 %collective-permute-done.43.refs_2_ = bf16[32,2048]{1,0:T(8,128)(2,1)S(1)} collective-permute-done((bf16[32,2048]{1,0:T(8,128)(2,1)S(1)}, bf16[32,2048]{1,0:T(8,128)(2,1)S(1)}, u32[]{:S(2)}, u32[]{:S(2)}) %collective-permute-start.43) | collective-permute-done | bytes 131104 | tf_op jit(solution)/shard_map/ppermute | solution.py:50
  88.7 0.8 collective-permute-start.48
  89.5 1.6 %collective-permute-start.44 = (bf16[32,2048]{1,0:T(8,128)(2,1)S(1)}, bf16[32,2048]{1,0:T(8,128)(2,1)S(1)}, u32[]{:S(2)}, u32[]{:S(2)}) collective-permute-start(bf16[32,2048]{1,0:T(8,128)(2,1)S(1)} %get-tuple-element.103.refs_0_), channel_id=1, source_target_pairs={{0,2},{1,3},{2,0},{3,1},{4,6},{5,7},{6,4},{7,5},{8,10},{9,11},{10,... | collective-permute-start | bytes 393224 | tf_op jit(solution)/shard_map/ppermute | solution.py:50
  91.5 2.2 %collective-permute-done.48.refs_3_ = bf16[32,2048]{1,0:T(8,128)(2,1)S(1)} collective-permute-done((bf16[32,2048]{1,0:T(8,128)(2,1)S(1)}, bf16[32,2048]{1,0:T(8,128)(2,1)S(1)}, u32[]{:S(2)}, u32[]{:S(2)}) %collective-permute-start.48) | collective-permute-done | bytes 131104 | tf_op jit(solution)/shard_map/ppermute | solution.py:50
  93.8 2.9 %collective-permute-start.49 = (bf16[32,2048]{1,0:T(8,128)(2,1)S(1)}, bf16[32,2048]{1,0:T(8,128)(2,1)S(1)}, u32[]{:S(2)}, u32[]{:S(2)}) collective-permute-start(bf16[32,2048]{1,0:T(8,128)(2,1)S(1)} %shard_map.76), channel_id=1, source_target_pairs={{0,8},{1,9},{2,10},{3,11},{4,12},{5,13},{6,14},{7,15},{8,0},{9,1},... | collective-permute-start | bytes 393224 | tf_op jit(solution)/shard_map/ppermute | solution.py:50
  96.8 2.1 %collective-permute-start.46 = (bf16[32,2048]{1,0:T(8,128)(2,1)S(1)}, bf16[32,2048]{1,0:T(8,128)(2,1)S(1)}, u32[]{:S(2)}, u32[]{:S(2)}) collective-permute-start(bf16[32,2048]{1,0:T(8,128)(2,1)S(1)} %get-tuple-element.106), channel_id=1, source_target_pairs={{0,4},{1,5},{2,6},{3,7},{4,0},{5,1},{6,2},{7,3},{8,12},{9,13},{10,... | collective-permute-start | bytes 393224 | tf_op jit(solution)/shard_map/ppermute | solution.py:50
  98.9 0.9 collective-permute-done.49.refs_3_
  99.9 2.0 %collective-permute-done.46.refs_2_ = bf16[32,2048]{1,0:T(8,128)(2,1)S(1)} collective-permute-done((bf16[32,2048]{1,0:T(8,128)(2,1)S(1)}, bf16[32,2048]{1,0:T(8,128)(2,1)S(1)}, u32[]{:S(2)}, u32[]{:S(2)}) %collective-permute-start.46) | collective-permute-done | bytes 131104 | tf_op jit(solution)/shard_map/ppermute | solution.py:50
  101.9 0.8 shard_map.77
  (79 shorter events, 7.8 us)
Async XLA Ops:
  1.2 9.0 %collective-permute-start = (bf16[32,2176]{1,0:T(8,128)(2,1)S(1)}, bf16[32,2176]{1,0:T(8,128)(2,1)S(1)}, u32[]{:S(2)}, u32[]{:S(2)}) collective-permute-start(bf16[32,2176]{1,0:T(8,128)(2,1)S(1)} %shard_map.55.refs_0_), channel_id=1, source_target_pairs={{0,4},{1,5},{2,6},{3,7},{4,0},{5,1},{6,2},{7,3},{8,12},{9,13},{10,... | collective-permute-start | bytes 417800 | tf_op jit(solution)/shard_map/ppermute | solution.py:50
  4.3 9.1 %collective-permute-start.1 = (bf16[32,2176]{1,0:T(8,128)(2,1)S(1)}, bf16[32,2176]{1,0:T(8,128)(2,1)S(1)}, u32[]{:S(2)}, u32[]{:S(2)}) collective-permute-start(bf16[32,2176]{1,0:T(8,128)(2,1)S(1)} %shard_map.55.refs_0_), channel_id=1, source_target_pairs={{0,8},{1,9},{2,10},{3,11},{4,12},{5,13},{6,14},{7,15},{8,0},{9,1},... | collective-permute-start | bytes 417800 | tf_op jit(solution)/shard_map/ppermute | solution.py:50
  10.2 9.8 %collective-permute-start.3 = (bf16[64,2176]{1,0:T(8,128)(2,1)S(1)}, bf16[64,2176]{1,0:T(8,128)(2,1)S(1)}, u32[]{:S(2)}, u32[]{:S(2)}) collective-permute-start(bf16[64,2176]{1,0:T(8,128)(2,1)S(1)} %shard_map.56.refs_0_.refs_1_), channel_id=1, source_target_pairs={{0,2},{1,3},{2,0},{3,1},{4,6},{5,7},{6,4},{7,5},{8,10},{9,11},{10,... | collective-permute-start | bytes 835592 | tf_op jit(solution)/shard_map/ppermute | solution.py:50
  13.4 5.5 %collective-permute-start.4 = (bf16[32,2176]{1,0:T(8,128)(2,1)S(1)}, bf16[32,2176]{1,0:T(8,128)(2,1)S(1)}, u32[]{:S(2)}, u32[]{:S(2)}) collective-permute-start(bf16[32,2176]{1,0:T(8,128)(2,1)S(1)} %shard_map.57.refs_2_), channel_id=1, source_target_pairs={{0,2},{1,3},{2,0},{3,1},{4,6},{5,7},{6,4},{7,5},{8,10},{9,11},{10,... | collective-permute-start | bytes 417800 | tf_op jit(solution)/shard_map/ppermute | solution.py:50
  15.0 5.1 %collective-permute-start.2 = (bf16[32,2176]{1,0:T(8,128)(2,1)S(1)}, bf16[32,2176]{1,0:T(8,128)(2,1)S(1)}, u32[]{:S(2)}, u32[]{:S(2)}) collective-permute-start(bf16[32,2176]{1,0:T(8,128)(2,1)S(1)} %shard_map.57.refs_2_), channel_id=1, source_target_pairs={{0,4},{1,5},{2,6},{3,7},{4,0},{5,1},{6,2},{7,3},{8,12},{9,13},{10,... | collective-permute-start | bytes 417800 | tf_op jit(solution)/shard_map/ppermute | solution.py:50
  15.4 9.5 %collective-permute-start.5 = (bf16[64,2176]{1,0:T(8,128)(2,1)S(1)}, bf16[64,2176]{1,0:T(8,128)(2,1)S(1)}, u32[]{:S(2)}, u32[]{:S(2)}) collective-permute-start(bf16[64,2176]{1,0:T(8,128)(2,1)S(1)} %shard_map.56.refs_0_.refs_1_), channel_id=1, source_target_pairs={{0,1},{1,0},{2,3},{3,2},{4,5},{5,4},{6,7},{7,6},{8,9},{9,8},{10,11... | collective-permute-start | bytes 835592 | tf_op jit(solution)/shard_map/ppermute | solution.py:50
  20.0 4.9 %collective-permute-start.6 = (bf16[64,2176]{1,0:T(8,128)(2,1)S(1)}, bf16[64,2176]{1,0:T(8,128)(2,1)S(1)}, u32[]{:S(2)}, u32[]{:S(2)}) collective-permute-start(bf16[64,2176]{1,0:T(8,128)(2,1)S(1)} %collective-permute-done.3.refs_2_), channel_id=1, source_target_pairs={{0,1},{1,0},{2,3},{3,2},{4,5},{5,4},{6,7},{7,6},{8,9},{9,8},{10,11... | collective-permute-start | bytes 835592 | tf_op jit(solution)/shard_map/ppermute | solution.py:50
  20.0 8.6 %collective-permute-start.9 = (bf16[32,2176]{1,0:T(8,128)(2,1)S(1)}, bf16[32,2176]{1,0:T(8,128)(2,1)S(1)}, u32[]{:S(2)}, u32[]{:S(2)}) collective-permute-start(bf16[32,2176]{1,0:T(8,128)(2,1)S(1)} %collective-permute-done.2.refs_0_.refs_3_), channel_id=1, source_target_pairs={{0,2},{1,3},{2,0},{3,1},{4,6},{5,7},{6,4},{7,5},{8,10},{9,11},{10,... | collective-permute-start | bytes 417800 | tf_op jit(solution)/shard_map/ppermute | solution.py:50
  27.5 1.4 %collective-permute-start.7 = (bf16[32,2048]{1,0:T(8,128)(2,1)S(1)}, bf16[32,2048]{1,0:T(8,128)(2,1)S(1)}, u32[]{:S(2)}, u32[]{:S(2)}) collective-permute-start(bf16[32,2048]{1,0:T(8,128)(2,1)S(1)} %get-tuple-element.60), channel_id=1, source_target_pairs={{0,1},{1,0},{2,3},{3,2},{4,5},{5,4},{6,7},{7,6},{8,9},{9,8},{10,11... | collective-permute-start | bytes 393224 | tf_op jit(solution)/shard_map/ppermute | solution.py:50
  27.8 2.5 %collective-permute-start.10 = (bf16[32,2176]{1,0:T(8,128)(2,1)S(1)}, bf16[32,2176]{1,0:T(8,128)(2,1)S(1)}, u32[]{:S(2)}, u32[]{:S(2)}) collective-permute-start(bf16[32,2176]{1,0:T(8,128)(2,1)S(1)} %shard_map.57.refs_2_), channel_id=1, source_target_pairs={{0,1},{1,0},{2,3},{3,2},{4,5},{5,4},{6,7},{7,6},{8,9},{9,8},{10,11... | collective-permute-start | bytes 417800 | tf_op jit(solution)/shard_map/ppermute | solution.py:50
  28.1 2.3 %collective-permute-start.12 = (bf16[32,2176]{1,0:T(8,128)(2,1)S(1)}, bf16[32,2176]{1,0:T(8,128)(2,1)S(1)}, u32[]{:S(2)}, u32[]{:S(2)}) collective-permute-start(bf16[32,2176]{1,0:T(8,128)(2,1)S(1)} %collective-permute-done.4.refs_4_), channel_id=1, source_target_pairs={{0,1},{1,0},{2,3},{3,2},{4,5},{5,4},{6,7},{7,6},{8,9},{9,8},{10,11... | collective-permute-start | bytes 417800 | tf_op jit(solution)/shard_map/ppermute | solution.py:50
  28.3 2.0 %collective-permute-start.11 = (bf16[32,2176]{1,0:T(8,128)(2,1)S(1)}, bf16[32,2176]{1,0:T(8,128)(2,1)S(1)}, u32[]{:S(2)}, u32[]{:S(2)}) collective-permute-start(bf16[32,2176]{1,0:T(8,128)(2,1)S(1)} %collective-permute-done.2.refs_0_.refs_3_), channel_id=1, source_target_pairs={{0,1},{1,0},{2,3},{3,2},{4,5},{5,4},{6,7},{7,6},{8,9},{9,8},{10,11... | collective-permute-start | bytes 417800 | tf_op jit(solution)/shard_map/ppermute | solution.py:50
  28.6 1.8 %collective-permute-start.13 = (bf16[32,2176]{1,0:T(8,128)(2,1)S(1)}, bf16[32,2176]{1,0:T(8,128)(2,1)S(1)}, u32[]{:S(2)}, u32[]{:S(2)}) collective-permute-start(bf16[32,2176]{1,0:T(8,128)(2,1)S(1)} %collective-permute-done.9.refs_5_), channel_id=1, source_target_pairs={{0,1},{1,0},{2,3},{3,2},{4,5},{5,4},{6,7},{7,6},{8,9},{9,8},{10,11... | collective-permute-start | bytes 417800 | tf_op jit(solution)/shard_map/ppermute | solution.py:50
  28.9 1.3 %collective-permute-start.8 = (bf16[32,2048]{1,0:T(8,128)(2,1)S(1)}, bf16[32,2048]{1,0:T(8,128)(2,1)S(1)}, u32[]{:S(2)}, u32[]{:S(2)}) collective-permute-start(bf16[32,2048]{1,0:T(8,128)(2,1)S(1)} %get-tuple-element.61), channel_id=1, source_target_pairs={{0,1},{1,0},{2,3},{3,2},{4,5},{5,4},{6,7},{7,6},{8,9},{9,8},{10,11... | collective-permute-start | bytes 393224 | tf_op jit(solution)/shard_map/ppermute | solution.py:50
  33.0 1.4 %collective-permute-start.14 = (bf16[32,2048]{1,0:T(8,128)(2,1)S(1)}, bf16[32,2048]{1,0:T(8,128)(2,1)S(1)}, u32[]{:S(2)}, u32[]{:S(2)}) collective-permute-start(bf16[32,2048]{1,0:T(8,128)(2,1)S(1)} %get-tuple-element.70), channel_id=1, source_target_pairs={{0,1},{1,0},{2,3},{3,2},{4,5},{5,4},{6,7},{7,6},{8,9},{9,8},{10,11... | collective-permute-start | bytes 393224 | tf_op jit(solution)/shard_map/ppermute | solution.py:50
  33.3 1.3 %collective-permute-start.15 = (bf16[32,2048]{1,0:T(8,128)(2,1)S(1)}, bf16[32,2048]{1,0:T(8,128)(2,1)S(1)}, u32[]{:S(2)}, u32[]{:S(2)}) collective-permute-start(bf16[32,2048]{1,0:T(8,128)(2,1)S(1)} %get-tuple-element.71), channel_id=1, source_target_pairs={{0,1},{1,0},{2,3},{3,2},{4,5},{5,4},{6,7},{7,6},{8,9},{9,8},{10,11... | collective-permute-start | bytes 393224 | tf_op jit(solution)/shard_map/ppermute | solution.py:50
  33.6 7.5 %collective-permute-start.17 = (bf16[64,2048]{1,0:T(8,128)(2,1)S(1)}, bf16[64,2048]{1,0:T(8,128)(2,1)S(1)}, u32[]{:S(2)}, u32[]{:S(2)}) collective-permute-start(bf16[64,2048]{1,0:T(8,128)(2,1)S(1)} %get-tuple-element.75), channel_id=1, source_target_pairs={{0,1},{1,0},{2,3},{3,2},{4,5},{5,4},{6,7},{7,6},{8,9},{9,8},{10,11... | collective-permute-start | bytes 786440 | tf_op jit(solution)/shard_map/ppermute | solution.py:50
  34.7 6.4 %collective-permute-start.18 = (bf16[32,2048]{1,0:T(8,128)(2,1)S(1)}, bf16[32,2048]{1,0:T(8,128)(2,1)S(1)}, u32[]{:S(2)}, u32[]{:S(2)}) collective-permute-start(bf16[32,2048]{1,0:T(8,128)(2,1)S(1)} %get-tuple-element.73.refs_1_), channel_id=1, source_target_pairs={{0,2},{1,3},{2,0},{3,1},{4,6},{5,7},{6,4},{7,5},{8,10},{9,11},{10,... | collective-permute-start | bytes 393224 | tf_op jit(solution)/shard_map/ppermute | solution.py:50
  36.3 13.7 %collective-permute-start.16 = (bf16[64,2048]{1,0:T(8,128)(2,1)S(1)}, bf16[64,2048]{1,0:T(8,128)(2,1)S(1)}, u32[]{:S(2)}, u32[]{:S(2)}) collective-permute-start(bf16[64,2048]{1,0:T(8,128)(2,1)S(1)} %get-tuple-element.74), channel_id=1, source_target_pairs={{0,1},{1,0},{2,3},{3,2},{4,5},{5,4},{6,7},{7,6},{8,9},{9,8},{10,11... | collective-permute-start | bytes 786440 | tf_op jit(solution)/shard_map/ppermute | solution.py:50
  36.3 8.3 %collective-permute-start.22 = (bf16[32,2048]{1,0:T(8,128)(2,1)S(1)}, bf16[32,2048]{1,0:T(8,128)(2,1)S(1)}, u32[]{:S(2)}, u32[]{:S(2)}) collective-permute-start(bf16[32,2048]{1,0:T(8,128)(2,1)S(1)} %get-tuple-element.72.refs_0_), channel_id=1, source_target_pairs={{0,2},{1,3},{2,0},{3,1},{4,6},{5,7},{6,4},{7,5},{8,10},{9,11},{10,... | collective-permute-start | bytes 393224 | tf_op jit(solution)/shard_map/ppermute | solution.py:50
  41.2 5.0 %collective-permute-start.23 = (bf16[32,2048]{1,0:T(8,128)(2,1)S(1)}, bf16[32,2048]{1,0:T(8,128)(2,1)S(1)}, u32[]{:S(2)}, u32[]{:S(2)}) collective-permute-start(bf16[32,2048]{1,0:T(8,128)(2,1)S(1)} %shard_map.64), channel_id=1, source_target_pairs={{0,4},{1,5},{2,6},{3,7},{4,0},{5,1},{6,2},{7,3},{8,12},{9,13},{10,... | collective-permute-start | bytes 393224 | tf_op jit(solution)/shard_map/ppermute | solution.py:50
  42.6 7.4 %collective-permute-start.19 = (bf16[32,2048]{1,0:T(8,128)(2,1)S(1)}, bf16[32,2048]{1,0:T(8,128)(2,1)S(1)}, u32[]{:S(2)}, u32[]{:S(2)}) collective-permute-start(bf16[32,2048]{1,0:T(8,128)(2,1)S(1)} %get-tuple-element.76.refs_0_), channel_id=1, source_target_pairs={{0,2},{1,3},{2,0},{3,1},{4,6},{5,7},{6,4},{7,5},{8,10},{9,11},{10,... | collective-permute-start | bytes 393224 | tf_op jit(solution)/shard_map/ppermute | solution.py:50
  43.2 6.8 %collective-permute-start.20 = (bf16[32,2048]{1,0:T(8,128)(2,1)S(1)}, bf16[32,2048]{1,0:T(8,128)(2,1)S(1)}, u32[]{:S(2)}, u32[]{:S(2)}) collective-permute-start(bf16[32,2048]{1,0:T(8,128)(2,1)S(1)} %get-tuple-element.77.refs_1_), channel_id=1, source_target_pairs={{0,2},{1,3},{2,0},{3,1},{4,6},{5,7},{6,4},{7,5},{8,10},{9,11},{10,... | collective-permute-start | bytes 393224 | tf_op jit(solution)/shard_map/ppermute | solution.py:50
  46.3 9.7 %collective-permute-start.24 = (bf16[32,2048]{1,0:T(8,128)(2,1)S(1)}, bf16[32,2048]{1,0:T(8,128)(2,1)S(1)}, u32[]{:S(2)}, u32[]{:S(2)}) collective-permute-start(bf16[32,2048]{1,0:T(8,128)(2,1)S(1)} %shard_map.66), channel_id=1, source_target_pairs={{0,8},{1,9},{2,10},{3,11},{4,12},{5,13},{6,14},{7,15},{8,0},{9,1},... | collective-permute-start | bytes 393224 | tf_op jit(solution)/shard_map/ppermute | solution.py:50
  50.1 5.9 %collective-permute-start.21 = (bf16[32,2048]{1,0:T(8,128)(2,1)S(1)}, bf16[32,2048]{1,0:T(8,128)(2,1)S(1)}, u32[]{:S(2)}, u32[]{:S(2)}) collective-permute-start(bf16[32,2048]{1,0:T(8,128)(2,1)S(1)} %get-tuple-element.79), channel_id=1, source_target_pairs={{0,4},{1,5},{2,6},{3,7},{4,0},{5,1},{6,2},{7,3},{8,12},{9,13},{10,... | collective-permute-start | bytes 393224 | tf_op jit(solution)/shard_map/ppermute | solution.py:50
  56.2 5.0 %collective-permute-start.25 = (bf16[32,2048]{1,0:T(8,128)(2,1)S(1)}, bf16[32,2048]{1,0:T(8,128)(2,1)S(1)}, u32[]{:S(2)}, u32[]{:S(2)}) collective-permute-start(bf16[32,2048]{1,0:T(8,128)(2,1)S(1)} %get-tuple-element.81.refs_0_), channel_id=1, source_target_pairs={{0,4},{1,5},{2,6},{3,7},{4,0},{5,1},{6,2},{7,3},{8,12},{9,13},{10,... | collective-permute-start | bytes 393224 | tf_op jit(solution)/shard_map/ppermute | solution.py:50
  57.9 7.3 %collective-permute-start.26 = (bf16[32,2048]{1,0:T(8,128)(2,1)S(1)}, bf16[32,2048]{1,0:T(8,128)(2,1)S(1)}, u32[]{:S(2)}, u32[]{:S(2)}) collective-permute-start(bf16[32,2048]{1,0:T(8,128)(2,1)S(1)} %get-tuple-element.81.refs_0_), channel_id=1, source_target_pairs={{0,8},{1,9},{2,10},{3,11},{4,12},{5,13},{6,14},{7,15},{8,0},{9,1},... | collective-permute-start | bytes 393224 | tf_op jit(solution)/shard_map/ppermute | solution.py:50
  61.2 9.0 %collective-permute-start.28 = (bf16[64,2048]{1,0:T(8,128)(2,1)S(1)}, bf16[64,2048]{1,0:T(8,128)(2,1)S(1)}, u32[]{:S(2)}, u32[]{:S(2)}) collective-permute-start(bf16[64,2048]{1,0:T(8,128)(2,1)S(1)} %shard_map.68.refs_0_.refs_1_), channel_id=1, source_target_pairs={{0,2},{1,3},{2,0},{3,1},{4,6},{5,7},{6,4},{7,5},{8,10},{9,11},{10,... | collective-permute-start | bytes 786440 | tf_op jit(solution)/shard_map/ppermute | solution.py:50
  65.1 5.0 %collective-permute-start.29 = (bf16[32,2048]{1,0:T(8,128)(2,1)S(1)}, bf16[32,2048]{1,0:T(8,128)(2,1)S(1)}, u32[]{:S(2)}, u32[]{:S(2)}) collective-permute-start(bf16[32,2048]{1,0:T(8,128)(2,1)S(1)} %shard_map.69.refs_2_), channel_id=1, source_target_pairs={{0,2},{1,3},{2,0},{3,1},{4,6},{5,7},{6,4},{7,5},{8,10},{9,11},{10,... | collective-permute-start | bytes 393224 | tf_op jit(solution)/shard_map/ppermute | solution.py:50
  65.2 5.0 %collective-permute-start.27 = (bf16[32,2048]{1,0:T(8,128)(2,1)S(1)}, bf16[32,2048]{1,0:T(8,128)(2,1)S(1)}, u32[]{:S(2)}, u32[]{:S(2)}) collective-permute-start(bf16[32,2048]{1,0:T(8,128)(2,1)S(1)} %shard_map.69.refs_2_), channel_id=1, source_target_pairs={{0,4},{1,5},{2,6},{3,7},{4,0},{5,1},{6,2},{7,3},{8,12},{9,13},{10,... | collective-permute-start | bytes 393224 | tf_op jit(solution)/shard_map/ppermute | solution.py:50
  66.2 6.0 %collective-permute-start.30 = (bf16[64,2048]{1,0:T(8,128)(2,1)S(1)}, bf16[64,2048]{1,0:T(8,128)(2,1)S(1)}, u32[]{:S(2)}, u32[]{:S(2)}) collective-permute-start(bf16[64,2048]{1,0:T(8,128)(2,1)S(1)} %shard_map.68.refs_0_.refs_1_), channel_id=1, source_target_pairs={{0,1},{1,0},{2,3},{3,2},{4,5},{5,4},{6,7},{7,6},{8,9},{9,8},{10,11... | collective-permute-start | bytes 786440 | tf_op jit(solution)/shard_map/ppermute | solution.py:50
  70.3 2.0 %collective-permute-start.31 = (bf16[64,2048]{1,0:T(8,128)(2,1)S(1)}, bf16[64,2048]{1,0:T(8,128)(2,1)S(1)}, u32[]{:S(2)}, u32[]{:S(2)}) collective-permute-start(bf16[64,2048]{1,0:T(8,128)(2,1)S(1)} %collective-permute-done.28.refs_2_), channel_id=1, source_target_pairs={{0,1},{1,0},{2,3},{3,2},{4,5},{5,4},{6,7},{7,6},{8,9},{9,8},{10,11... | collective-permute-start | bytes 786440 | tf_op jit(solution)/shard_map/ppermute | solution.py:50
  70.3 6.1 %collective-permute-start.34 = (bf16[32,2048]{1,0:T(8,128)(2,1)S(1)}, bf16[32,2048]{1,0:T(8,128)(2,1)S(1)}, u32[]{:S(2)}, u32[]{:S(2)}) collective-permute-start(bf16[32,2048]{1,0:T(8,128)(2,1)S(1)} %collective-permute-done.27.refs_0_.refs_3_), channel_id=1, source_target_pairs={{0,2},{1,3},{2,0},{3,1},{4,6},{5,7},{6,4},{7,5},{8,10},{9,11},{10,... | collective-permute-start | bytes 393224 | tf_op jit(solution)/shard_map/ppermute | solution.py:50
  74.8 1.5 %collective-permute-start.32 = (bf16[32,2048]{1,0:T(8,128)(2,1)S(1)}, bf16[32,2048]{1,0:T(8,128)(2,1)S(1)}, u32[]{:S(2)}, u32[]{:S(2)}) collective-permute-start(bf16[32,2048]{1,0:T(8,128)(2,1)S(1)} %get-tuple-element.87), channel_id=1, source_target_pairs={{0,1},{1,0},{2,3},{3,2},{4,5},{5,4},{6,7},{7,6},{8,9},{9,8},{10,11... | collective-permute-start | bytes 393224 | tf_op jit(solution)/shard_map/ppermute | solution.py:50
  75.1 2.6 %collective-permute-start.35 = (bf16[32,2048]{1,0:T(8,128)(2,1)S(1)}, bf16[32,2048]{1,0:T(8,128)(2,1)S(1)}, u32[]{:S(2)}, u32[]{:S(2)}) collective-permute-start(bf16[32,2048]{1,0:T(8,128)(2,1)S(1)} %shard_map.69.refs_2_), channel_id=1, source_target_pairs={{0,1},{1,0},{2,3},{3,2},{4,5},{5,4},{6,7},{7,6},{8,9},{9,8},{10,11... | collective-permute-start | bytes 393224 | tf_op jit(solution)/shard_map/ppermute | solution.py:50
  75.4 2.4 %collective-permute-start.37 = (bf16[32,2048]{1,0:T(8,128)(2,1)S(1)}, bf16[32,2048]{1,0:T(8,128)(2,1)S(1)}, u32[]{:S(2)}, u32[]{:S(2)}) collective-permute-start(bf16[32,2048]{1,0:T(8,128)(2,1)S(1)} %collective-permute-done.29.refs_4_), channel_id=1, source_target_pairs={{0,1},{1,0},{2,3},{3,2},{4,5},{5,4},{6,7},{7,6},{8,9},{9,8},{10,11... | collective-permute-start | bytes 393224 | tf_op jit(solution)/shard_map/ppermute | solution.py:50
  75.6 2.2 %collective-permute-start.36 = (bf16[32,2048]{1,0:T(8,128)(2,1)S(1)}, bf16[32,2048]{1,0:T(8,128)(2,1)S(1)}, u32[]{:S(2)}, u32[]{:S(2)}) collective-permute-start(bf16[32,2048]{1,0:T(8,128)(2,1)S(1)} %collective-permute-done.27.refs_0_.refs_3_), channel_id=1, source_target_pairs={{0,1},{1,0},{2,3},{3,2},{4,5},{5,4},{6,7},{7,6},{8,9},{9,8},{10,11... | collective-permute-start | bytes 393224 | tf_op jit(solution)/shard_map/ppermute | solution.py:50
  76.4 1.5 %collective-permute-start.38 = (bf16[32,2048]{1,0:T(8,128)(2,1)S(1)}, bf16[32,2048]{1,0:T(8,128)(2,1)S(1)}, u32[]{:S(2)}, u32[]{:S(2)}) collective-permute-start(bf16[32,2048]{1,0:T(8,128)(2,1)S(1)} %collective-permute-done.34.refs_5_), channel_id=1, source_target_pairs={{0,1},{1,0},{2,3},{3,2},{4,5},{5,4},{6,7},{7,6},{8,9},{9,8},{10,11... | collective-permute-start | bytes 393224 | tf_op jit(solution)/shard_map/ppermute | solution.py:50
  80.5 1.4 %collective-permute-start.39 = (bf16[32,2048]{1,0:T(8,128)(2,1)S(1)}, bf16[32,2048]{1,0:T(8,128)(2,1)S(1)}, u32[]{:S(2)}, u32[]{:S(2)}) collective-permute-start(bf16[32,2048]{1,0:T(8,128)(2,1)S(1)} %get-tuple-element.96), channel_id=1, source_target_pairs={{0,1},{1,0},{2,3},{3,2},{4,5},{5,4},{6,7},{7,6},{8,9},{9,8},{10,11... | collective-permute-start | bytes 393224 | tf_op jit(solution)/shard_map/ppermute | solution.py:50
  81.1 3.3 %collective-permute-start.42 = (bf16[64,2048]{1,0:T(8,128)(2,1)S(1)}, bf16[64,2048]{1,0:T(8,128)(2,1)S(1)}, u32[]{:S(2)}, u32[]{:S(2)}) collective-permute-start(bf16[64,2048]{1,0:T(8,128)(2,1)S(1)} %get-tuple-element.102), channel_id=1, source_target_pairs={{0,1},{1,0},{2,3},{3,2},{4,5},{5,4},{6,7},{7,6},{8,9},{9,8},{10,11... | collective-permute-start | bytes 786440 | tf_op jit(solution)/shard_map/ppermute | solution.py:50
  82.3 6.4 %collective-permute-start.43 = (bf16[32,2048]{1,0:T(8,128)(2,1)S(1)}, bf16[32,2048]{1,0:T(8,128)(2,1)S(1)}, u32[]{:S(2)}, u32[]{:S(2)}) collective-permute-start(bf16[32,2048]{1,0:T(8,128)(2,1)S(1)} %get-tuple-element.99.refs_1_), channel_id=1, source_target_pairs={{0,2},{1,3},{2,0},{3,1},{4,6},{5,7},{6,4},{7,5},{8,10},{9,11},{10,... | collective-permute-start | bytes 393224 | tf_op jit(solution)/shard_map/ppermute | solution.py:50
  84.1 12.6 %collective-permute-start.41 = (bf16[64,2048]{1,0:T(8,128)(2,1)S(1)}, bf16[64,2048]{1,0:T(8,128)(2,1)S(1)}, u32[]{:S(2)}, u32[]{:S(2)}) collective-permute-start(bf16[64,2048]{1,0:T(8,128)(2,1)S(1)} %get-tuple-element.100), channel_id=1, source_target_pairs={{0,1},{1,0},{2,3},{3,2},{4,5},{5,4},{6,7},{7,6},{8,9},{9,8},{10,11... | collective-permute-start | bytes 786440 | tf_op jit(solution)/shard_map/ppermute | solution.py:50
  84.1 7.4 %collective-permute-start.47 = (bf16[32,2048]{1,0:T(8,128)(2,1)S(1)}, bf16[32,2048]{1,0:T(8,128)(2,1)S(1)}, u32[]{:S(2)}, u32[]{:S(2)}) collective-permute-start(bf16[32,2048]{1,0:T(8,128)(2,1)S(1)} %get-tuple-element.98.refs_0_), channel_id=1, source_target_pairs={{0,2},{1,3},{2,0},{3,1},{4,6},{5,7},{6,4},{7,5},{8,10},{9,11},{10,... | collective-permute-start | bytes 393224 | tf_op jit(solution)/shard_map/ppermute | solution.py:50
  88.7 5.0 %collective-permute-start.48 = (bf16[32,2048]{1,0:T(8,128)(2,1)S(1)}, bf16[32,2048]{1,0:T(8,128)(2,1)S(1)}, u32[]{:S(2)}, u32[]{:S(2)}) collective-permute-start(bf16[32,2048]{1,0:T(8,128)(2,1)S(1)} %shard_map.74), channel_id=1, source_target_pairs={{0,4},{1,5},{2,6},{3,7},{4,0},{5,1},{6,2},{7,3},{8,12},{9,13},{10,... | collective-permute-start | bytes 393224 | tf_op jit(solution)/shard_map/ppermute | solution.py:50
  89.5 7.2 %collective-permute-start.44 = (bf16[32,2048]{1,0:T(8,128)(2,1)S(1)}, bf16[32,2048]{1,0:T(8,128)(2,1)S(1)}, u32[]{:S(2)}, u32[]{:S(2)}) collective-permute-start(bf16[32,2048]{1,0:T(8,128)(2,1)S(1)} %get-tuple-element.103.refs_0_), channel_id=1, source_target_pairs={{0,2},{1,3},{2,0},{3,1},{4,6},{5,7},{6,4},{7,5},{8,10},{9,11},{10,... | collective-permute-start | bytes 393224 | tf_op jit(solution)/shard_map/ppermute | solution.py:50
  91.1 5.7 %collective-permute-start.45 = (bf16[32,2048]{1,0:T(8,128)(2,1)S(1)}, bf16[32,2048]{1,0:T(8,128)(2,1)S(1)}, u32[]{:S(2)}, u32[]{:S(2)}) collective-permute-start(bf16[32,2048]{1,0:T(8,128)(2,1)S(1)} %get-tuple-element.104.refs_1_), channel_id=1, source_target_pairs={{0,2},{1,3},{2,0},{3,1},{4,6},{5,7},{6,4},{7,5},{8,10},{9,11},{10,... | collective-permute-start | bytes 393224 | tf_op jit(solution)/shard_map/ppermute | solution.py:50
  93.8 6.0 %collective-permute-start.49 = (bf16[32,2048]{1,0:T(8,128)(2,1)S(1)}, bf16[32,2048]{1,0:T(8,128)(2,1)S(1)}, u32[]{:S(2)}, u32[]{:S(2)}) collective-permute-start(bf16[32,2048]{1,0:T(8,128)(2,1)S(1)} %shard_map.76), channel_id=1, source_target_pairs={{0,8},{1,9},{2,10},{3,11},{4,12},{5,13},{6,14},{7,15},{8,0},{9,1},... | collective-permute-start | bytes 393224 | tf_op jit(solution)/shard_map/ppermute | solution.py:50
  96.8 5.0 %collective-permute-start.46 = (bf16[32,2048]{1,0:T(8,128)(2,1)S(1)}, bf16[32,2048]{1,0:T(8,128)(2,1)S(1)}, u32[]{:S(2)}, u32[]{:S(2)}) collective-permute-start(bf16[32,2048]{1,0:T(8,128)(2,1)S(1)} %get-tuple-element.106), channel_id=1, source_target_pairs={{0,4},{1,5},{2,6},{3,7},{4,0},{5,1},{6,2},{7,3},{8,12},{9,13},{10,... | collective-permute-start | bytes 393224 | tf_op jit(solution)/shard_map/ppermute | solution.py:50
  (4 other events, 14.5 us)

commit v16 on v14

--- a/solution.py
+++ b/solution.py
@@ -104,11 +104,27 @@
     out[...] = total.astype(out.dtype)
 
 
-def leave_pair(found, count, after):
+def part_kernel(k):
+    def kernel(mine, part, total):
+        rows = part.shape[0]
+        summed = mine[k * rows : (k + 1) * rows] + part[...].astype(f32)
+        total[...] = summed.astype(total.dtype)
+
+    return kernel
+
+
+def leave_pair(found, count, after, apart=False):
     mine_near, mine_beside, other_near, *other_beside = found
     arrived_beside = [swap(half, 1, 1, 2, True) for half in other_beside]
     arrived_near = swap(other_near, 1, 1, 2, True)
     rows, width = mine_beside.shape
+    if count == len(other_beside) and apart:
+        shape = (rows // count, width)
+        leaving = [
+            call(part_kernel(k), [(shape, bf16)], [VMEM] * 2, mine_beside, part, after=after)[0]
+            for k, part in enumerate(arrived_beside)
+        ]
+        return mine_near, arrived_near, leaving
     leaving = call(
         functools.partial(sum_kernel, len(other_beside)),
         [((rows // count, width), bf16)] * count,
@@ -349,7 +365,7 @@
     mine1, near1, leaving1 = leave_pair(outs, half, ())
     second_beside[-1] = held(second_beside[-1], outs[0])
     outs, second_columns = worked(second, second_beside, routed[1], tuple(leaving1))
-    mine2, near2, leaving2 = leave_pair(outs, half, ())
+    mine2, near2, leaving2 = leave_pair(outs, half, (), True)
     back2 = [swap(piece, 2, 1, 2, True) for piece in leaving2]
     crossed_back, hops = cross_rows(mine2, near2, back2)
     back1 = [swap(held(piece, hops), 2, 1, 2, True) for piece in leaving1]

time: 101 us -> 100 us (0.990)
  starting transfers between devices: 38.6 us -> 36.8 us
  waiting for transfers between devices: 41 us -> 42.4 us
    ppermute x50, starting transfers between devices: 38.6 us -> 36.8 us  [swap(): lax.ppermute(value, 'expert', [(i, partner(i)) for i in range(count)])]
    ppermute x50, waiting for transfers between devices: 41 us -> 42.4 us  [swap(): lax.ppermute(value, 'expert', [(i, partner(i)) for i in range(count)])]
    pallas_call x23 -> x25, Pallas kernels: 20.8 us -> 20.8 us  [call(): pl.pallas_call(lambda *refs: kernel(*refs[len(after):]), out_shape=shapes...]
where the time goes in v16:
time: 100 us
  waiting for transfers between devices  42.4 us (42%)
  starting transfers between devices  36.8 us (37%)
  Pallas kernels  20.8 us (21%)
    ppermute x50, waiting for transfers between devices, swap(): lax.ppermute(value, 'expert', [(i, partner(i)) for i in range(count)])  42.4 us
    ppermute x50, starting transfers between devices, swap(): lax.ppermute(value, 'expert', [(i, partner(i)) for i in range(count)])  36.8 us
    pallas_call x25, Pallas kernels, call(): pl.pallas_call(lambda *refs: kernel(*refs[len(after):]), out_shape=shapes...  20.8 us
  transfers between devices with their start and end apart: 50, of which 26 were waited for; matrix products, arithmetic and copies ran while one was open for 0% of the time, Pallas kernels for 13%

profile of v16, /device:TPU:0, one launch (start us, length us, event | category | flops | bytes accessed | tf_op | source)
XLA Modules:
  0.0 100.3 jit_solution(9882904489047807831)
XLA Ops:
  0.0 1.2 %shard_map.56.refs_1_ = bf16[32,2176]{1,0:T(8,128)(2,1)S(1)} custom-call(bf16[32,2048]{1,0:T(8,128)(2,1)} %bitcast.2, s32[2,2,8,16]{3,2,1,0:T(8,128)} %bitcast.4, f32[2,2048]{1,0:T(2,128)} %refs_2_.5), custom_call_target="tpu_custom_call" | custom-call | tf_op jit(solution)/shard_map/pallas_call | solution.py:28
  1.2 3.1 %collective-permute-start = (bf16[32,2176]{1,0:T(8,128)(2,1)S(1)}, bf16[32,2176]{1,0:T(8,128)(2,1)S(1)}, u32[]{:S(2)}, u32[]{:S(2)}) collective-permute-start(bf16[32,2176]{1,0:T(8,128)(2,1)S(1)} %shard_map.56.refs_1_), channel_id=1, source_target_pairs={{0,4},{1,5},{2,6},{3,7},{4,0},{5,1},{6,2},{7,3},{8,12},{9,13},{10,... | collective-permute-start | bytes 417800 | tf_op jit(solution)/shard_map/ppermute | solution.py:50
  4.3 2.6 %collective-permute-start.1 = (bf16[32,2176]{1,0:T(8,128)(2,1)S(1)}, bf16[32,2176]{1,0:T(8,128)(2,1)S(1)}, u32[]{:S(2)}, u32[]{:S(2)}) collective-permute-start(bf16[32,2176]{1,0:T(8,128)(2,1)S(1)} %shard_map.56.refs_1_), channel_id=1, source_target_pairs={{0,8},{1,9},{2,10},{3,11},{4,12},{5,13},{6,14},{7,15},{8,0},{9,1},... | collective-permute-start | bytes 417800 | tf_op jit(solution)/shard_map/ppermute | solution.py:50
  6.9 3.7 %shard_map.55 = (bf16[2048,1536]{1,0:T(8,128)(2,1)S(1)}, bf16[768,2048]{1,0:T(8,128)(2,1)S(1)}, f32[8,128]{1,0:T(8,128)S(1)}) custom-call(bf16[2,1,2048,1536]{3,2,1,0:T(8,128)(2,1)} %refs_1_.3, bf16[2,1,768,2048]{3,2,1,0:T(8,128)(2,1)} %refs_2_.4), custom_call_target="tpu_custom_call" | custom-call | tf_op jit(solution)/shard_map/pallas_call | solution.py:28
  10.7 1.6 %collective-permute-start.3 = (bf16[64,2176]{1,0:T(8,128)(2,1)S(1)}, bf16[64,2176]{1,0:T(8,128)(2,1)S(1)}, u32[]{:S(2)}, u32[]{:S(2)}) collective-permute-start(bf16[64,2176]{1,0:T(8,128)(2,1)S(1)} %shard_map.57.refs_0_.refs_1_), channel_id=1, source_target_pairs={{0,2},{1,3},{2,0},{3,1},{4,6},{5,7},{6,4},{7,5},{8,10},{9,11},{10,... | collective-permute-start | bytes 835592 | tf_op jit(solution)/shard_map/ppermute | solution.py:50
  12.3 1.1 %collective-permute-done.1.refs_1_ = bf16[32,2176]{1,0:T(8,128)(2,1)S(1)} collective-permute-done((bf16[32,2176]{1,0:T(8,128)(2,1)S(1)}, bf16[32,2176]{1,0:T(8,128)(2,1)S(1)}, u32[]{:S(2)}, u32[]{:S(2)}) %collective-permute-start.1) | collective-permute-done | bytes 139296 | tf_op jit(solution)/shard_map/ppermute | solution.py:50
  13.4 1.6 %collective-permute-start.4 = (bf16[32,2176]{1,0:T(8,128)(2,1)S(1)}, bf16[32,2176]{1,0:T(8,128)(2,1)S(1)}, u32[]{:S(2)}, u32[]{:S(2)}) collective-permute-start(bf16[32,2176]{1,0:T(8,128)(2,1)S(1)} %shard_map.58.refs_2_), channel_id=1, source_target_pairs={{0,2},{1,3},{2,0},{3,1},{4,6},{5,7},{6,4},{7,5},{8,10},{9,11},{10,... | collective-permute-start | bytes 417800 | tf_op jit(solution)/shard_map/ppermute | solution.py:50
  15.4 6.2 %collective-permute-done.4.refs_4_ = bf16[32,2176]{1,0:T(8,128)(2,1)S(1)} collective-permute-done((bf16[32,2176]{1,0:T(8,128)(2,1)S(1)}, bf16[32,2176]{1,0:T(8,128)(2,1)S(1)}, u32[]{:S(2)}, u32[]{:S(2)}) %collective-permute-start.4) | collective-permute-done | bytes 139296 | tf_op jit(solution)/shard_map/ppermute | solution.py:50
  21.6 1.6 %collective-permute-start.9 = (bf16[32,2176]{1,0:T(8,128)(2,1)S(1)}, bf16[32,2176]{1,0:T(8,128)(2,1)S(1)}, u32[]{:S(2)}, u32[]{:S(2)}) collective-permute-start(bf16[32,2176]{1,0:T(8,128)(2,1)S(1)} %collective-permute-done.2.refs_0_.refs_3_), channel_id=1, source_target_pairs={{0,2},{1,3},{2,0},{3,1},{4,6},{5,7},{6,4},{7,5},{8,10},{9,11},{10,... | collective-permute-start | bytes 417800 | tf_op jit(solution)/shard_map/ppermute | solution.py:50
  23.2 2.6 %shard_map.59 = (f32[64,2048]{1,0:T(8,128)S(1)}, f32[64,2048]{1,0:T(8,128)S(1)}, bf16[64,2048]{1,0:T(8,128)(2,1)S(1)}, bf16[32,2048]{1,0:T(8,128)(2,1)S(1)}, bf1...) custom-call(bf16[32,2176]{1,0:T(8,128)(2,1)S(1)} %collective-permute-done.2.refs_0_.refs_3_, ...), custom_call_target="tpu_custom_call" | custom-call | tf_op jit(solution)/shard_map/pallas_call | solution.py:28
  26.9 0.8 collective-permute-done.9.refs_5_
  28.2 1.0 %collective-permute-done.8.refs_2_ = bf16[32,2048]{1,0:T(8,128)(2,1)S(1)} collective-permute-done((bf16[32,2048]{1,0:T(8,128)(2,1)S(1)}, bf16[32,2048]{1,0:T(8,128)(2,1)S(1)}, u32[]{:S(2)}, u32[]{:S(2)}) %collective-permute-start.8) | collective-permute-done | bytes 131104 | tf_op jit(solution)/shard_map/ppermute | solution.py:50
  29.3 2.6 %shard_map.61 = (f32[64,2048]{1,0:T(8,128)S(1)}, f32[64,2048]{1,0:T(8,128)S(1)}, bf16[64,2048]{1,0:T(8,128)(2,1)S(1)}, bf16[32,2048]{1,0:T(8,128)(2,1)S(1)}, bf1...) custom-call(bf16[32,2048]{1,0:T(8,128)(2,1)S(1)} %get-tuple-element.72.refs_0_, ...), custom_call_target="tpu_custom_call" | custom-call | tf_op jit(solution)/shard_map/pallas_call | solution.py:28
  32.9 0.5 collective-permute-done.15.refs_1_
  33.4 1.6 %collective-permute-start.18 = (bf16[32,2048]{1,0:T(8,128)(2,1)S(1)}, bf16[32,2048]{1,0:T(8,128)(2,1)S(1)}, u32[]{:S(2)}, u32[]{:S(2)}) collective-permute-start(bf16[32,2048]{1,0:T(8,128)(2,1)S(1)} %shard_map.64.refs_1_), channel_id=1, source_target_pairs={{0,2},{1,3},{2,0},{3,1},{4,6},{5,7},{6,4},{7,5},{8,10},{9,11},{10,... | collective-permute-start | bytes 393224 | tf_op jit(solution)/shard_map/ppermute | solution.py:50
  35.1 0.6 collective-permute-start.22
  35.7 4.1 %collective-permute-done.18.refs_2_ = bf16[32,2048]{1,0:T(8,128)(2,1)S(1)} collective-permute-done((bf16[32,2048]{1,0:T(8,128)(2,1)S(1)}, bf16[32,2048]{1,0:T(8,128)(2,1)S(1)}, u32[]{:S(2)}, u32[]{:S(2)}) %collective-permute-start.18) | collective-permute-done | bytes 131104 | tf_op jit(solution)/shard_map/ppermute | solution.py:50
  40.4 1.5 %collective-permute-start.19 = (bf16[32,2048]{1,0:T(8,128)(2,1)S(1)}, bf16[32,2048]{1,0:T(8,128)(2,1)S(1)}, u32[]{:S(2)}, u32[]{:S(2)}) collective-permute-start(bf16[32,2048]{1,0:T(8,128)(2,1)S(1)} %get-tuple-element.72.refs_0_), channel_id=1, source_target_pairs={{0,2},{1,3},{2,0},{3,1},{4,6},{5,7},{6,4},{7,5},{8,10},{9,11},{10,... | collective-permute-start | bytes 393224 | tf_op jit(solution)/shard_map/ppermute | solution.py:50
  42.4 2.5 %collective-permute-done.23.refs_3_ = bf16[32,2048]{1,0:T(8,128)(2,1)S(1)} collective-permute-done((bf16[32,2048]{1,0:T(8,128)(2,1)S(1)}, bf16[32,2048]{1,0:T(8,128)(2,1)S(1)}, u32[]{:S(2)}, u32[]{:S(2)}) %collective-permute-start.23) | collective-permute-done | bytes 131104 | tf_op jit(solution)/shard_map/ppermute | solution.py:50
  44.9 1.1 %collective-permute-start.24 = (bf16[32,2048]{1,0:T(8,128)(2,1)S(1)}, bf16[32,2048]{1,0:T(8,128)(2,1)S(1)}, u32[]{:S(2)}, u32[]{:S(2)}) collective-permute-start(bf16[32,2048]{1,0:T(8,128)(2,1)S(1)} %shard_map.67), channel_id=1, source_target_pairs={{0,8},{1,9},{2,10},{3,11},{4,12},{5,13},{6,14},{7,15},{8,0},{9,1},... | collective-permute-start | bytes 393224 | tf_op jit(solution)/shard_map/ppermute | solution.py:50
  46.2 1.4 %collective-permute-done.20.refs_5_ = bf16[32,2048]{1,0:T(8,128)(2,1)S(1)} collective-permute-done((bf16[32,2048]{1,0:T(8,128)(2,1)S(1)}, bf16[32,2048]{1,0:T(8,128)(2,1)S(1)}, u32[]{:S(2)}, u32[]{:S(2)}) %collective-permute-start.20) | collective-permute-done | bytes 131104 | tf_op jit(solution)/shard_map/ppermute | solution.py:50
  47.7 1.2 %collective-permute-start.21 = (bf16[32,2048]{1,0:T(8,128)(2,1)S(1)}, bf16[32,2048]{1,0:T(8,128)(2,1)S(1)}, u32[]{:S(2)}, u32[]{:S(2)}) collective-permute-start(bf16[32,2048]{1,0:T(8,128)(2,1)S(1)} %get-tuple-element.75), channel_id=1, source_target_pairs={{0,4},{1,5},{2,6},{3,7},{4,0},{5,1},{6,2},{7,3},{8,12},{9,13},{10,... | collective-permute-start | bytes 393224 | tf_op jit(solution)/shard_map/ppermute | solution.py:50
  48.9 3.7 %shard_map.62 = (bf16[2048,1536]{1,0:T(8,128)(2,1)S(1)}, bf16[768,2048]{1,0:T(8,128)(2,1)S(1)}, f32[8,128]{1,0:T(8,128)S(1)}) custom-call(f32[64,2048]{1,0:T(8,128)S(1)} %get-tuple-element.65.refs_0_, bf16[2,1,2048,1536]{3,2,1,0:T(8,128)(2,1)} %refs_1_.3, bf16[2,1,768,2048]{3,2,1,0:T(8,128)(2,1)} %refs_2_.4), custom_call_target="tpu_custom_call" | custom-call | tf_op jit(solution)/shard_map/pallas_call | solution.py:28
  52.7 0.6 collective-permute-done.21.refs_4_
  53.5 0.7 collective-permute-start.25
  54.2 2.5 %collective-permute-start.26 = (bf16[32,2048]{1,0:T(8,128)(2,1)S(1)}, bf16[32,2048]{1,0:T(8,128)(2,1)S(1)}, u32[]{:S(2)}, u32[]{:S(2)}) collective-permute-start(bf16[32,2048]{1,0:T(8,128)(2,1)S(1)} %get-tuple-element.77.refs_1_), channel_id=1, source_target_pairs={{0,8},{1,9},{2,10},{3,11},{4,12},{5,13},{6,14},{7,15},{8,0},{9,1},... | collective-permute-start | bytes 393224 | tf_op jit(solution)/shard_map/ppermute | solution.py:50
  56.6 2.0 %collective-permute-done.25.refs_2_ = bf16[32,2048]{1,0:T(8,128)(2,1)S(1)} collective-permute-done((bf16[32,2048]{1,0:T(8,128)(2,1)S(1)}, bf16[32,2048]{1,0:T(8,128)(2,1)S(1)}, u32[]{:S(2)}, u32[]{:S(2)}) %collective-permute-start.25) | collective-permute-done | bytes 131104 | tf_op jit(solution)/shard_map/ppermute | solution.py:50
  58.6 1.6 %collective-permute-start.28 = (bf16[64,2048]{1,0:T(8,128)(2,1)S(1)}, bf16[64,2048]{1,0:T(8,128)(2,1)S(1)}, u32[]{:S(2)}, u32[]{:S(2)}) collective-permute-start(bf16[64,2048]{1,0:T(8,128)(2,1)S(1)} %shard_map.69.refs_0_.refs_1_), channel_id=1, source_target_pairs={{0,2},{1,3},{2,0},{3,1},{4,6},{5,7},{6,4},{7,5},{8,10},{9,11},{10,... | collective-permute-start | bytes 786440 | tf_op jit(solution)/shard_map/ppermute | solution.py:50
  60.2 1.2 %collective-permute-done.26.refs_1_ = bf16[32,2048]{1,0:T(8,128)(2,1)S(1)} collective-permute-done((bf16[32,2048]{1,0:T(8,128)(2,1)S(1)}, bf16[32,2048]{1,0:T(8,128)(2,1)S(1)}, u32[]{:S(2)}, u32[]{:S(2)}) %collective-permute-start.26) | collective-permute-done | bytes 131104 | tf_op jit(solution)/shard_map/ppermute | solution.py:50
  61.5 1.7 %collective-permute-start.29 = (bf16[32,2048]{1,0:T(8,128)(2,1)S(1)}, bf16[32,2048]{1,0:T(8,128)(2,1)S(1)}, u32[]{:S(2)}, u32[]{:S(2)}) collective-permute-start(bf16[32,2048]{1,0:T(8,128)(2,1)S(1)} %shard_map.70.refs_2_), channel_id=1, source_target_pairs={{0,2},{1,3},{2,0},{3,1},{4,6},{5,7},{6,4},{7,5},{8,10},{9,11},{10,... | collective-permute-start | bytes 393224 | tf_op jit(solution)/shard_map/ppermute | solution.py:50
  63.3 3.2 %collective-permute-done.29.refs_4_ = bf16[32,2048]{1,0:T(8,128)(2,1)S(1)} collective-permute-done((bf16[32,2048]{1,0:T(8,128)(2,1)S(1)}, bf16[32,2048]{1,0:T(8,128)(2,1)S(1)}, u32[]{:S(2)}, u32[]{:S(2)}) %collective-permute-start.29) | collective-permute-done | bytes 131104 | tf_op jit(solution)/shard_map/ppermute | solution.py:50
  66.5 1.6 %collective-permute-done.27.refs_0_.refs_3_ = bf16[32,2048]{1,0:T(8,128)(2,1)S(1)} collective-permute-done((bf16[32,2048]{1,0:T(8,128)(2,1)S(1)}, bf16[32,2048]{1,0:T(8,128)(2,1)S(1)}, u32[]{:S(2)}, u32[]{:S(2)}) %collective-permute-start.27) | collective-permute-done | bytes 131104 | tf_op jit(solution)/shard_map/ppermute | solution.py:50
  68.5 1.1 %collective-permute-done.31.refs_4_ = bf16[64,2048]{1,0:T(8,128)(2,1)S(1)} collective-permute-done((bf16[64,2048]{1,0:T(8,128)(2,1)S(1)}, bf16[64,2048]{1,0:T(8,128)(2,1)S(1)}, u32[]{:S(2)}, u32[]{:S(2)}) %collective-permute-start.31) | collective-permute-done | bytes 262176 | tf_op jit(solution)/shard_map/ppermute | solution.py:50
  69.7 2.6 %shard_map.71 = (f32[64,2048]{1,0:T(8,128)S(1)}, f32[64,2048]{1,0:T(8,128)S(1)}, bf16[64,2048]{1,0:T(8,128)(2,1)S(1)}, bf16[32,2048]{1,0:T(8,128)(2,1)S(1)}, bf16[32,2048]{1,0:T(8,128)(2,1)S(1)}) custom-call(bf16[32,2048]{1,0:T(8,128)(2,1)S(1)} %collective-permute-done.27.refs_0_.refs_3_, bf16[64,2048]{1,0:T(8,128)(2,1)S(1)} %shard_map.69.refs_0_.refs_1_, ...), custom_call_target="tpu_custom_call" | custom-call | tf_op jit(solution)/shard_map/pallas_call | solution.py:28
  73.4 0.7 collective-permute-done.34.refs_5_
  74.6 0.8 collective-permute-done.33.refs_2_
  75.6 2.6 %shard_map.73 = (f32[64,2048]{1,0:T(8,128)S(1)}, f32[64,2048]{1,0:T(8,128)S(1)}, bf16[64,2048]{1,0:T(8,128)(2,1)S(1)}, bf16[32,2048]{1,0:T(8,128)(2,1)S(1)}, bf16[32,2048]{1,0:T(8,128)(2,1)S(1)}) custom-call(bf16[32,2048]{1,0:T(8,128)(2,1)S(1)} %get-tuple-element.97.refs_0_, bf16[32,2048]{1,0:T(8,128)(2,1)S(1)} %get-tuple-element.98.refs_1_, ...), custom_call_target="tpu_custom_call" | custom-call | tf_op jit(solution)/shard_map/pallas_call | solution.py:28
  80.3 1.5 %collective-permute-start.47 = (bf16[32,2048]{1,0:T(8,128)(2,1)S(1)}, bf16[32,2048]{1,0:T(8,128)(2,1)S(1)}, u32[]{:S(2)}, u32[]{:S(2)}) collective-permute-start(bf16[32,2048]{1,0:T(8,128)(2,1)S(1)} %shard_map.74.refs_0_), channel_id=1, source_target_pairs={{0,2},{1,3},{2,0},{3,1},{4,6},{5,7},{6,4},{7,5},{8,10},{9,11},{10,... | collective-permute-start | bytes 393224 | tf_op jit(solution)/shard_map/ppermute | solution.py:50
  81.9 4.1 %collective-permute-done.43.refs_2_ = bf16[32,2048]{1,0:T(8,128)(2,1)S(1)} collective-permute-done((bf16[32,2048]{1,0:T(8,128)(2,1)S(1)}, bf16[32,2048]{1,0:T(8,128)(2,1)S(1)}, u32[]{:S(2)}, u32[]{:S(2)}) %collective-permute-start.43) | collective-permute-done | bytes 131104 | tf_op jit(solution)/shard_map/ppermute | solution.py:50
  86.3 0.8 collective-permute-start.44
  87.1 1.3 %collective-permute-start.45 = (bf16[32,2048]{1,0:T(8,128)(2,1)S(1)}, bf16[32,2048]{1,0:T(8,128)(2,1)S(1)}, u32[]{:S(2)}, u32[]{:S(2)}) collective-permute-start(bf16[32,2048]{1,0:T(8,128)(2,1)S(1)} %get-tuple-element.98.refs_1_), channel_id=1, source_target_pairs={{0,2},{1,3},{2,0},{3,1},{4,6},{5,7},{6,4},{7,5},{8,10},{9,11},{10,... | collective-permute-start | bytes 393224 | tf_op jit(solution)/shard_map/ppermute | solution.py:50
  88.7 2.4 %collective-permute-done.48.refs_3_ = bf16[32,2048]{1,0:T(8,128)(2,1)S(1)} collective-permute-done((bf16[32,2048]{1,0:T(8,128)(2,1)S(1)}, bf16[32,2048]{1,0:T(8,128)(2,1)S(1)}, u32[]{:S(2)}, u32[]{:S(2)}) %collective-permute-start.48) | collective-permute-done | bytes 131104 | tf_op jit(solution)/shard_map/ppermute | solution.py:50
  91.2 1.3 %collective-permute-start.49 = (bf16[32,2048]{1,0:T(8,128)(2,1)S(1)}, bf16[32,2048]{1,0:T(8,128)(2,1)S(1)}, u32[]{:S(2)}, u32[]{:S(2)}) collective-permute-start(bf16[32,2048]{1,0:T(8,128)(2,1)S(1)} %shard_map.78), channel_id=1, source_target_pairs={{0,8},{1,9},{2,10},{3,11},{4,12},{5,13},{6,14},{7,15},{8,0},{9,1},... | collective-permute-start | bytes 393224 | tf_op jit(solution)/shard_map/ppermute | solution.py:50
  92.5 1.4 %collective-permute-done.45.refs_5_ = bf16[32,2048]{1,0:T(8,128)(2,1)S(1)} collective-permute-done((bf16[32,2048]{1,0:T(8,128)(2,1)S(1)}, bf16[32,2048]{1,0:T(8,128)(2,1)S(1)}, u32[]{:S(2)}, u32[]{:S(2)}) %collective-permute-start.45) | collective-permute-done | bytes 131104 | tf_op jit(solution)/shard_map/ppermute | solution.py:50
  93.9 1.2 %collective-permute-start.46 = (bf16[32,2048]{1,0:T(8,128)(2,1)S(1)}, bf16[32,2048]{1,0:T(8,128)(2,1)S(1)}, u32[]{:S(2)}, u32[]{:S(2)}) collective-permute-start(bf16[32,2048]{1,0:T(8,128)(2,1)S(1)} %get-tuple-element.100), channel_id=1, source_target_pairs={{0,4},{1,5},{2,6},{3,7},{4,0},{5,1},{6,2},{7,3},{8,12},{9,13},{10,... | collective-permute-start | bytes 393224 | tf_op jit(solution)/shard_map/ppermute | solution.py:50
  95.2 3.0 %collective-permute-done.49.refs_3_ = bf16[32,2048]{1,0:T(8,128)(2,1)S(1)} collective-permute-done((bf16[32,2048]{1,0:T(8,128)(2,1)S(1)}, bf16[32,2048]{1,0:T(8,128)(2,1)S(1)}, u32[]{:S(2)}, u32[]{:S(2)}) %collective-permute-start.49) | collective-permute-done | bytes 131104 | tf_op jit(solution)/shard_map/ppermute | solution.py:50
  98.2 1.3 %collective-permute-done.46.refs_2_ = bf16[32,2048]{1,0:T(8,128)(2,1)S(1)} collective-permute-done((bf16[32,2048]{1,0:T(8,128)(2,1)S(1)}, bf16[32,2048]{1,0:T(8,128)(2,1)S(1)}, u32[]{:S(2)}, u32[]{:S(2)}) %collective-permute-start.46) | collective-permute-done | bytes 131104 | tf_op jit(solution)/shard_map/ppermute | solution.py:50
  99.5 0.8 shard_map.79
  (81 shorter events, 10.0 us)
Async XLA Ops:
  1.2 9.4 %collective-permute-start = (bf16[32,2176]{1,0:T(8,128)(2,1)S(1)}, bf16[32,2176]{1,0:T(8,128)(2,1)S(1)}, u32[]{:S(2)}, u32[]{:S(2)}) collective-permute-start(bf16[32,2176]{1,0:T(8,128)(2,1)S(1)} %shard_map.56.refs_1_), channel_id=1, source_target_pairs={{0,4},{1,5},{2,6},{3,7},{4,0},{5,1},{6,2},{7,3},{8,12},{9,13},{10,... | collective-permute-start | bytes 417800 | tf_op jit(solution)/shard_map/ppermute | solution.py:50
  4.3 9.1 %collective-permute-start.1 = (bf16[32,2176]{1,0:T(8,128)(2,1)S(1)}, bf16[32,2176]{1,0:T(8,128)(2,1)S(1)}, u32[]{:S(2)}, u32[]{:S(2)}) collective-permute-start(bf16[32,2176]{1,0:T(8,128)(2,1)S(1)} %shard_map.56.refs_1_), channel_id=1, source_target_pairs={{0,8},{1,9},{2,10},{3,11},{4,12},{5,13},{6,14},{7,15},{8,0},{9,1},... | collective-permute-start | bytes 417800 | tf_op jit(solution)/shard_map/ppermute | solution.py:50
  10.7 10.9 %collective-permute-start.3 = (bf16[64,2176]{1,0:T(8,128)(2,1)S(1)}, bf16[64,2176]{1,0:T(8,128)(2,1)S(1)}, u32[]{:S(2)}, u32[]{:S(2)}) collective-permute-start(bf16[64,2176]{1,0:T(8,128)(2,1)S(1)} %shard_map.57.refs_0_.refs_1_), channel_id=1, source_target_pairs={{0,2},{1,3},{2,0},{3,1},{4,6},{5,7},{6,4},{7,5},{8,10},{9,11},{10,... | collective-permute-start | bytes 835592 | tf_op jit(solution)/shard_map/ppermute | solution.py:50
  13.4 8.2 %collective-permute-start.4 = (bf16[32,2176]{1,0:T(8,128)(2,1)S(1)}, bf16[32,2176]{1,0:T(8,128)(2,1)S(1)}, u32[]{:S(2)}, u32[]{:S(2)}) collective-permute-start(bf16[32,2176]{1,0:T(8,128)(2,1)S(1)} %shard_map.58.refs_2_), channel_id=1, source_target_pairs={{0,2},{1,3},{2,0},{3,1},{4,6},{5,7},{6,4},{7,5},{8,10},{9,11},{10,... | collective-permute-start | bytes 417800 | tf_op jit(solution)/shard_map/ppermute | solution.py:50
  15.0 6.6 %collective-permute-start.2 = (bf16[32,2176]{1,0:T(8,128)(2,1)S(1)}, bf16[32,2176]{1,0:T(8,128)(2,1)S(1)}, u32[]{:S(2)}, u32[]{:S(2)}) collective-permute-start(bf16[32,2176]{1,0:T(8,128)(2,1)S(1)} %shard_map.58.refs_2_), channel_id=1, source_target_pairs={{0,4},{1,5},{2,6},{3,7},{4,0},{5,1},{6,2},{7,3},{8,12},{9,13},{10,... | collective-permute-start | bytes 417800 | tf_op jit(solution)/shard_map/ppermute | solution.py:50
  15.4 7.8 %collective-permute-start.5 = (bf16[64,2176]{1,0:T(8,128)(2,1)S(1)}, bf16[64,2176]{1,0:T(8,128)(2,1)S(1)}, u32[]{:S(2)}, u32[]{:S(2)}) collective-permute-start(bf16[64,2176]{1,0:T(8,128)(2,1)S(1)} %shard_map.57.refs_0_.refs_1_), channel_id=1, source_target_pairs={{0,1},{1,0},{2,3},{3,2},{4,5},{5,4},{6,7},{7,6},{8,9},{9,8},{10,11... | collective-permute-start | bytes 835592 | tf_op jit(solution)/shard_map/ppermute | solution.py:50
  21.6 1.6 %collective-permute-start.6 = (bf16[64,2176]{1,0:T(8,128)(2,1)S(1)}, bf16[64,2176]{1,0:T(8,128)(2,1)S(1)}, u32[]{:S(2)}, u32[]{:S(2)}) collective-permute-start(bf16[64,2176]{1,0:T(8,128)(2,1)S(1)} %collective-permute-done.3.refs_2_), channel_id=1, source_target_pairs={{0,1},{1,0},{2,3},{3,2},{4,5},{5,4},{6,7},{7,6},{8,9},{9,8},{10,11... | collective-permute-start | bytes 835592 | tf_op jit(solution)/shard_map/ppermute | solution.py:50
  21.6 6.1 %collective-permute-start.9 = (bf16[32,2176]{1,0:T(8,128)(2,1)S(1)}, bf16[32,2176]{1,0:T(8,128)(2,1)S(1)}, u32[]{:S(2)}, u32[]{:S(2)}) collective-permute-start(bf16[32,2176]{1,0:T(8,128)(2,1)S(1)} %collective-permute-done.2.refs_0_.refs_3_), channel_id=1, source_target_pairs={{0,2},{1,3},{2,0},{3,1},{4,6},{5,7},{6,4},{7,5},{8,10},{9,11},{10,... | collective-permute-start | bytes 417800 | tf_op jit(solution)/shard_map/ppermute | solution.py:50
  25.8 1.9 %collective-permute-start.7 = (bf16[32,2048]{1,0:T(8,128)(2,1)S(1)}, bf16[32,2048]{1,0:T(8,128)(2,1)S(1)}, u32[]{:S(2)}, u32[]{:S(2)}) collective-permute-start(bf16[32,2048]{1,0:T(8,128)(2,1)S(1)} %get-tuple-element.58), channel_id=1, source_target_pairs={{0,1},{1,0},{2,3},{3,2},{4,5},{5,4},{6,7},{7,6},{8,9},{9,8},{10,11... | collective-permute-start | bytes 393224 | tf_op jit(solution)/shard_map/ppermute | solution.py:50
  26.0 3.3 %collective-permute-start.10 = (bf16[32,2176]{1,0:T(8,128)(2,1)S(1)}, bf16[32,2176]{1,0:T(8,128)(2,1)S(1)}, u32[]{:S(2)}, u32[]{:S(2)}) collective-permute-start(bf16[32,2176]{1,0:T(8,128)(2,1)S(1)} %shard_map.58.refs_2_), channel_id=1, source_target_pairs={{0,1},{1,0},{2,3},{3,2},{4,5},{5,4},{6,7},{7,6},{8,9},{9,8},{10,11... | collective-permute-start | bytes 417800 | tf_op jit(solution)/shard_map/ppermute | solution.py:50
  26.4 2.9 %collective-permute-start.12 = (bf16[32,2176]{1,0:T(8,128)(2,1)S(1)}, bf16[32,2176]{1,0:T(8,128)(2,1)S(1)}, u32[]{:S(2)}, u32[]{:S(2)}) collective-permute-start(bf16[32,2176]{1,0:T(8,128)(2,1)S(1)} %collective-permute-done.4.refs_4_), channel_id=1, source_target_pairs={{0,1},{1,0},{2,3},{3,2},{4,5},{5,4},{6,7},{7,6},{8,9},{9,8},{10,11... | collective-permute-start | bytes 417800 | tf_op jit(solution)/shard_map/ppermute | solution.py:50
  26.6 2.8 %collective-permute-start.11 = (bf16[32,2176]{1,0:T(8,128)(2,1)S(1)}, bf16[32,2176]{1,0:T(8,128)(2,1)S(1)}, u32[]{:S(2)}, u32[]{:S(2)}) collective-permute-start(bf16[32,2176]{1,0:T(8,128)(2,1)S(1)} %collective-permute-done.2.refs_0_.refs_3_), channel_id=1, source_target_pairs={{0,1},{1,0},{2,3},{3,2},{4,5},{5,4},{6,7},{7,6},{8,9},{9,8},{10,11... | collective-permute-start | bytes 417800 | tf_op jit(solution)/shard_map/ppermute | solution.py:50
  27.7 1.6 %collective-permute-start.13 = (bf16[32,2176]{1,0:T(8,128)(2,1)S(1)}, bf16[32,2176]{1,0:T(8,128)(2,1)S(1)}, u32[]{:S(2)}, u32[]{:S(2)}) collective-permute-start(bf16[32,2176]{1,0:T(8,128)(2,1)S(1)} %collective-permute-done.9.refs_5_), channel_id=1, source_target_pairs={{0,1},{1,0},{2,3},{3,2},{4,5},{5,4},{6,7},{7,6},{8,9},{9,8},{10,11... | collective-permute-start | bytes 417800 | tf_op jit(solution)/shard_map/ppermute | solution.py:50
  27.7 1.5 %collective-permute-start.8 = (bf16[32,2048]{1,0:T(8,128)(2,1)S(1)}, bf16[32,2048]{1,0:T(8,128)(2,1)S(1)}, u32[]{:S(2)}, u32[]{:S(2)}) collective-permute-start(bf16[32,2048]{1,0:T(8,128)(2,1)S(1)} %get-tuple-element.59), channel_id=1, source_target_pairs={{0,1},{1,0},{2,3},{3,2},{4,5},{5,4},{6,7},{7,6},{8,9},{9,8},{10,11... | collective-permute-start | bytes 393224 | tf_op jit(solution)/shard_map/ppermute | solution.py:50
  32.0 1.4 %collective-permute-start.15 = (bf16[32,2048]{1,0:T(8,128)(2,1)S(1)}, bf16[32,2048]{1,0:T(8,128)(2,1)S(1)}, u32[]{:S(2)}, u32[]{:S(2)}) collective-permute-start(bf16[32,2048]{1,0:T(8,128)(2,1)S(1)} %get-tuple-element.69), channel_id=1, source_target_pairs={{0,1},{1,0},{2,3},{3,2},{4,5},{5,4},{6,7},{7,6},{8,9},{9,8},{10,11... | collective-permute-start | bytes 393224 | tf_op jit(solution)/shard_map/ppermute | solution.py:50
  32.3 7.5 %collective-permute-start.17 = (bf16[64,2048]{1,0:T(8,128)(2,1)S(1)}, bf16[64,2048]{1,0:T(8,128)(2,1)S(1)}, u32[]{:S(2)}, u32[]{:S(2)}) collective-permute-start(bf16[64,2048]{1,0:T(8,128)(2,1)S(1)} %get-tuple-element.71), channel_id=1, source_target_pairs={{0,1},{1,0},{2,3},{3,2},{4,5},{5,4},{6,7},{7,6},{8,9},{9,8},{10,11... | collective-permute-start | bytes 786440 | tf_op jit(solution)/shard_map/ppermute | solution.py:50
  32.5 2.5 %collective-permute-start.14 = (bf16[32,2048]{1,0:T(8,128)(2,1)S(1)}, bf16[32,2048]{1,0:T(8,128)(2,1)S(1)}, u32[]{:S(2)}, u32[]{:S(2)}) collective-permute-start(bf16[32,2048]{1,0:T(8,128)(2,1)S(1)} %get-tuple-element.68), channel_id=1, source_target_pairs={{0,1},{1,0},{2,3},{3,2},{4,5},{5,4},{6,7},{7,6},{8,9},{9,8},{10,11... | collective-permute-start | bytes 393224 | tf_op jit(solution)/shard_map/ppermute | solution.py:50
  33.4 6.4 %collective-permute-start.18 = (bf16[32,2048]{1,0:T(8,128)(2,1)S(1)}, bf16[32,2048]{1,0:T(8,128)(2,1)S(1)}, u32[]{:S(2)}, u32[]{:S(2)}) collective-permute-start(bf16[32,2048]{1,0:T(8,128)(2,1)S(1)} %shard_map.64.refs_1_), channel_id=1, source_target_pairs={{0,2},{1,3},{2,0},{3,1},{4,6},{5,7},{6,4},{7,5},{8,10},{9,11},{10,... | collective-permute-start | bytes 393224 | tf_op jit(solution)/shard_map/ppermute | solution.py:50
  35.0 11.1 %collective-permute-start.16 = (bf16[64,2048]{1,0:T(8,128)(2,1)S(1)}, bf16[64,2048]{1,0:T(8,128)(2,1)S(1)}, u32[]{:S(2)}, u32[]{:S(2)}) collective-permute-start(bf16[64,2048]{1,0:T(8,128)(2,1)S(1)} %get-tuple-element.70), channel_id=1, source_target_pairs={{0,1},{1,0},{2,3},{3,2},{4,5},{5,4},{6,7},{7,6},{8,9},{9,8},{10,11... | collective-permute-start | bytes 786440 | tf_op jit(solution)/shard_map/ppermute | solution.py:50
  35.1 7.3 %collective-permute-start.22 = (bf16[32,2048]{1,0:T(8,128)(2,1)S(1)}, bf16[32,2048]{1,0:T(8,128)(2,1)S(1)}, u32[]{:S(2)}, u32[]{:S(2)}) collective-permute-start(bf16[32,2048]{1,0:T(8,128)(2,1)S(1)} %shard_map.63.refs_0_), channel_id=1, source_target_pairs={{0,2},{1,3},{2,0},{3,1},{4,6},{5,7},{6,4},{7,5},{8,10},{9,11},{10,... | collective-permute-start | bytes 393224 | tf_op jit(solution)/shard_map/ppermute | solution.py:50
  39.8 5.0 %collective-permute-start.23 = (bf16[32,2048]{1,0:T(8,128)(2,1)S(1)}, bf16[32,2048]{1,0:T(8,128)(2,1)S(1)}, u32[]{:S(2)}, u32[]{:S(2)}) collective-permute-start(bf16[32,2048]{1,0:T(8,128)(2,1)S(1)} %shard_map.65), channel_id=1, source_target_pairs={{0,4},{1,5},{2,6},{3,7},{4,0},{5,1},{6,2},{7,3},{8,12},{9,13},{10,... | collective-permute-start | bytes 393224 | tf_op jit(solution)/shard_map/ppermute | solution.py:50
  40.4 5.9 %collective-permute-start.19 = (bf16[32,2048]{1,0:T(8,128)(2,1)S(1)}, bf16[32,2048]{1,0:T(8,128)(2,1)S(1)}, u32[]{:S(2)}, u32[]{:S(2)}) collective-permute-start(bf16[32,2048]{1,0:T(8,128)(2,1)S(1)} %get-tuple-element.72.refs_0_), channel_id=1, source_target_pairs={{0,2},{1,3},{2,0},{3,1},{4,6},{5,7},{6,4},{7,5},{8,10},{9,11},{10,... | collective-permute-start | bytes 393224 | tf_op jit(solution)/shard_map/ppermute | solution.py:50
  41.9 5.7 %collective-permute-start.20 = (bf16[32,2048]{1,0:T(8,128)(2,1)S(1)}, bf16[32,2048]{1,0:T(8,128)(2,1)S(1)}, u32[]{:S(2)}, u32[]{:S(2)}) collective-permute-start(bf16[32,2048]{1,0:T(8,128)(2,1)S(1)} %get-tuple-element.73.refs_1_), channel_id=1, source_target_pairs={{0,2},{1,3},{2,0},{3,1},{4,6},{5,7},{6,4},{7,5},{8,10},{9,11},{10,... | collective-permute-start | bytes 393224 | tf_op jit(solution)/shard_map/ppermute | solution.py:50
  44.9 7.8 %collective-permute-start.24 = (bf16[32,2048]{1,0:T(8,128)(2,1)S(1)}, bf16[32,2048]{1,0:T(8,128)(2,1)S(1)}, u32[]{:S(2)}, u32[]{:S(2)}) collective-permute-start(bf16[32,2048]{1,0:T(8,128)(2,1)S(1)} %shard_map.67), channel_id=1, source_target_pairs={{0,8},{1,9},{2,10},{3,11},{4,12},{5,13},{6,14},{7,15},{8,0},{9,1},... | collective-permute-start | bytes 393224 | tf_op jit(solution)/shard_map/ppermute | solution.py:50
  47.7 5.6 %collective-permute-start.21 = (bf16[32,2048]{1,0:T(8,128)(2,1)S(1)}, bf16[32,2048]{1,0:T(8,128)(2,1)S(1)}, u32[]{:S(2)}, u32[]{:S(2)}) collective-permute-start(bf16[32,2048]{1,0:T(8,128)(2,1)S(1)} %get-tuple-element.75), channel_id=1, source_target_pairs={{0,4},{1,5},{2,6},{3,7},{4,0},{5,1},{6,2},{7,3},{8,12},{9,13},{10,... | collective-permute-start | bytes 393224 | tf_op jit(solution)/shard_map/ppermute | solution.py:50
  53.5 5.1 %collective-permute-start.25 = (bf16[32,2048]{1,0:T(8,128)(2,1)S(1)}, bf16[32,2048]{1,0:T(8,128)(2,1)S(1)}, u32[]{:S(2)}, u32[]{:S(2)}) collective-permute-start(bf16[32,2048]{1,0:T(8,128)(2,1)S(1)} %get-tuple-element.77.refs_1_), channel_id=1, source_target_pairs={{0,4},{1,5},{2,6},{3,7},{4,0},{5,1},{6,2},{7,3},{8,12},{9,13},{10,... | collective-permute-start | bytes 393224 | tf_op jit(solution)/shard_map/ppermute | solution.py:50
  54.2 7.3 %collective-permute-start.26 = (bf16[32,2048]{1,0:T(8,128)(2,1)S(1)}, bf16[32,2048]{1,0:T(8,128)(2,1)S(1)}, u32[]{:S(2)}, u32[]{:S(2)}) collective-permute-start(bf16[32,2048]{1,0:T(8,128)(2,1)S(1)} %get-tuple-element.77.refs_1_), channel_id=1, source_target_pairs={{0,8},{1,9},{2,10},{3,11},{4,12},{5,13},{6,14},{7,15},{8,0},{9,1},... | collective-permute-start | bytes 393224 | tf_op jit(solution)/shard_map/ppermute | solution.py:50
  58.6 9.5 %collective-permute-start.28 = (bf16[64,2048]{1,0:T(8,128)(2,1)S(1)}, bf16[64,2048]{1,0:T(8,128)(2,1)S(1)}, u32[]{:S(2)}, u32[]{:S(2)}) collective-permute-start(bf16[64,2048]{1,0:T(8,128)(2,1)S(1)} %shard_map.69.refs_0_.refs_1_), channel_id=1, source_target_pairs={{0,2},{1,3},{2,0},{3,1},{4,6},{5,7},{6,4},{7,5},{8,10},{9,11},{10,... | collective-permute-start | bytes 786440 | tf_op jit(solution)/shard_map/ppermute | solution.py:50
  61.5 5.0 %collective-permute-start.29 = (bf16[32,2048]{1,0:T(8,128)(2,1)S(1)}, bf16[32,2048]{1,0:T(8,128)(2,1)S(1)}, u32[]{:S(2)}, u32[]{:S(2)}) collective-permute-start(bf16[32,2048]{1,0:T(8,128)(2,1)S(1)} %shard_map.70.refs_2_), channel_id=1, source_target_pairs={{0,2},{1,3},{2,0},{3,1},{4,6},{5,7},{6,4},{7,5},{8,10},{9,11},{10,... | collective-permute-start | bytes 393224 | tf_op jit(solution)/shard_map/ppermute | solution.py:50
  63.2 5.0 %collective-permute-start.27 = (bf16[32,2048]{1,0:T(8,128)(2,1)S(1)}, bf16[32,2048]{1,0:T(8,128)(2,1)S(1)}, u32[]{:S(2)}, u32[]{:S(2)}) collective-permute-start(bf16[32,2048]{1,0:T(8,128)(2,1)S(1)} %shard_map.70.refs_2_), channel_id=1, source_target_pairs={{0,4},{1,5},{2,6},{3,7},{4,0},{5,1},{6,2},{7,3},{8,12},{9,13},{10,... | collective-permute-start | bytes 393224 | tf_op jit(solution)/shard_map/ppermute | solution.py:50
  63.3 5.2 %collective-permute-start.30 = (bf16[64,2048]{1,0:T(8,128)(2,1)S(1)}, bf16[64,2048]{1,0:T(8,128)(2,1)S(1)}, u32[]{:S(2)}, u32[]{:S(2)}) collective-permute-start(bf16[64,2048]{1,0:T(8,128)(2,1)S(1)} %shard_map.69.refs_0_.refs_1_), channel_id=1, source_target_pairs={{0,1},{1,0},{2,3},{3,2},{4,5},{5,4},{6,7},{7,6},{8,9},{9,8},{10,11... | collective-permute-start | bytes 786440 | tf_op jit(solution)/shard_map/ppermute | solution.py:50
  68.1 1.5 %collective-permute-start.31 = (bf16[64,2048]{1,0:T(8,128)(2,1)S(1)}, bf16[64,2048]{1,0:T(8,128)(2,1)S(1)}, u32[]{:S(2)}, u32[]{:S(2)}) collective-permute-start(bf16[64,2048]{1,0:T(8,128)(2,1)S(1)} %collective-permute-done.28.refs_2_), channel_id=1, source_target_pairs={{0,1},{1,0},{2,3},{3,2},{4,5},{5,4},{6,7},{7,6},{8,9},{9,8},{10,11... | collective-permute-start | bytes 786440 | tf_op jit(solution)/shard_map/ppermute | solution.py:50
  68.1 5.9 %collective-permute-start.34 = (bf16[32,2048]{1,0:T(8,128)(2,1)S(1)}, bf16[32,2048]{1,0:T(8,128)(2,1)S(1)}, u32[]{:S(2)}, u32[]{:S(2)}) collective-permute-start(bf16[32,2048]{1,0:T(8,128)(2,1)S(1)} %collective-permute-done.27.refs_0_.refs_3_), channel_id=1, source_target_pairs={{0,2},{1,3},{2,0},{3,1},{4,6},{5,7},{6,4},{7,5},{8,10},{9,11},{10,... | collective-permute-start | bytes 393224 | tf_op jit(solution)/shard_map/ppermute | solution.py:50
  72.3 1.8 %collective-permute-start.32 = (bf16[32,2048]{1,0:T(8,128)(2,1)S(1)}, bf16[32,2048]{1,0:T(8,128)(2,1)S(1)}, u32[]{:S(2)}, u32[]{:S(2)}) collective-permute-start(bf16[32,2048]{1,0:T(8,128)(2,1)S(1)} %get-tuple-element.83), channel_id=1, source_target_pairs={{0,1},{1,0},{2,3},{3,2},{4,5},{5,4},{6,7},{7,6},{8,9},{9,8},{10,11... | collective-permute-start | bytes 393224 | tf_op jit(solution)/shard_map/ppermute | solution.py:50
  72.5 3.0 %collective-permute-start.35 = (bf16[32,2048]{1,0:T(8,128)(2,1)S(1)}, bf16[32,2048]{1,0:T(8,128)(2,1)S(1)}, u32[]{:S(2)}, u32[]{:S(2)}) collective-permute-start(bf16[32,2048]{1,0:T(8,128)(2,1)S(1)} %shard_map.70.refs_2_), channel_id=1, source_target_pairs={{0,1},{1,0},{2,3},{3,2},{4,5},{5,4},{6,7},{7,6},{8,9},{9,8},{10,11... | collective-permute-start | bytes 393224 | tf_op jit(solution)/shard_map/ppermute | solution.py:50
  72.9 2.6 %collective-permute-start.37 = (bf16[32,2048]{1,0:T(8,128)(2,1)S(1)}, bf16[32,2048]{1,0:T(8,128)(2,1)S(1)}, u32[]{:S(2)}, u32[]{:S(2)}) collective-permute-start(bf16[32,2048]{1,0:T(8,128)(2,1)S(1)} %collective-permute-done.29.refs_4_), channel_id=1, source_target_pairs={{0,1},{1,0},{2,3},{3,2},{4,5},{5,4},{6,7},{7,6},{8,9},{9,8},{10,11... | collective-permute-start | bytes 393224 | tf_op jit(solution)/shard_map/ppermute | solution.py:50
  73.0 2.5 %collective-permute-start.36 = (bf16[32,2048]{1,0:T(8,128)(2,1)S(1)}, bf16[32,2048]{1,0:T(8,128)(2,1)S(1)}, u32[]{:S(2)}, u32[]{:S(2)}) collective-permute-start(bf16[32,2048]{1,0:T(8,128)(2,1)S(1)} %collective-permute-done.27.refs_0_.refs_3_), channel_id=1, source_target_pairs={{0,1},{1,0},{2,3},{3,2},{4,5},{5,4},{6,7},{7,6},{8,9},{9,8},{10,11... | collective-permute-start | bytes 393224 | tf_op jit(solution)/shard_map/ppermute | solution.py:50
  74.1 1.5 %collective-permute-start.38 = (bf16[32,2048]{1,0:T(8,128)(2,1)S(1)}, bf16[32,2048]{1,0:T(8,128)(2,1)S(1)}, u32[]{:S(2)}, u32[]{:S(2)}) collective-permute-start(bf16[32,2048]{1,0:T(8,128)(2,1)S(1)} %collective-permute-done.34.refs_5_), channel_id=1, source_target_pairs={{0,1},{1,0},{2,3},{3,2},{4,5},{5,4},{6,7},{7,6},{8,9},{9,8},{10,11... | collective-permute-start | bytes 393224 | tf_op jit(solution)/shard_map/ppermute | solution.py:50
  78.6 3.3 %collective-permute-start.42 = (bf16[64,2048]{1,0:T(8,128)(2,1)S(1)}, bf16[64,2048]{1,0:T(8,128)(2,1)S(1)}, u32[]{:S(2)}, u32[]{:S(2)}) collective-permute-start(bf16[64,2048]{1,0:T(8,128)(2,1)S(1)} %get-tuple-element.96), channel_id=1, source_target_pairs={{0,1},{1,0},{2,3},{3,2},{4,5},{5,4},{6,7},{7,6},{8,9},{9,8},{10,11... | collective-permute-start | bytes 786440 | tf_op jit(solution)/shard_map/ppermute | solution.py:50
  78.8 1.5 %collective-permute-start.39 = (bf16[32,2048]{1,0:T(8,128)(2,1)S(1)}, bf16[32,2048]{1,0:T(8,128)(2,1)S(1)}, u32[]{:S(2)}, u32[]{:S(2)}) collective-permute-start(bf16[32,2048]{1,0:T(8,128)(2,1)S(1)} %get-tuple-element.92), channel_id=1, source_target_pairs={{0,1},{1,0},{2,3},{3,2},{4,5},{5,4},{6,7},{7,6},{8,9},{9,8},{10,11... | collective-permute-start | bytes 393224 | tf_op jit(solution)/shard_map/ppermute | solution.py:50
  79.6 6.4 %collective-permute-start.43 = (bf16[32,2048]{1,0:T(8,128)(2,1)S(1)}, bf16[32,2048]{1,0:T(8,128)(2,1)S(1)}, u32[]{:S(2)}, u32[]{:S(2)}) collective-permute-start(bf16[32,2048]{1,0:T(8,128)(2,1)S(1)} %shard_map.75.refs_1_), channel_id=1, source_target_pairs={{0,2},{1,3},{2,0},{3,1},{4,6},{5,7},{6,4},{7,5},{8,10},{9,11},{10,... | collective-permute-start | bytes 393224 | tf_op jit(solution)/shard_map/ppermute | solution.py:50
  80.1 12.4 %collective-permute-start.41 = (bf16[64,2048]{1,0:T(8,128)(2,1)S(1)}, bf16[64,2048]{1,0:T(8,128)(2,1)S(1)}, u32[]{:S(2)}, u32[]{:S(2)}) collective-permute-start(bf16[64,2048]{1,0:T(8,128)(2,1)S(1)} %get-tuple-element.94), channel_id=1, source_target_pairs={{0,1},{1,0},{2,3},{3,2},{4,5},{5,4},{6,7},{7,6},{8,9},{9,8},{10,11... | collective-permute-start | bytes 786440 | tf_op jit(solution)/shard_map/ppermute | solution.py:50
  80.3 8.3 %collective-permute-start.47 = (bf16[32,2048]{1,0:T(8,128)(2,1)S(1)}, bf16[32,2048]{1,0:T(8,128)(2,1)S(1)}, u32[]{:S(2)}, u32[]{:S(2)}) collective-permute-start(bf16[32,2048]{1,0:T(8,128)(2,1)S(1)} %shard_map.74.refs_0_), channel_id=1, source_target_pairs={{0,2},{1,3},{2,0},{3,1},{4,6},{5,7},{6,4},{7,5},{8,10},{9,11},{10,... | collective-permute-start | bytes 393224 | tf_op jit(solution)/shard_map/ppermute | solution.py:50
  86.1 5.0 %collective-permute-start.48 = (bf16[32,2048]{1,0:T(8,128)(2,1)S(1)}, bf16[32,2048]{1,0:T(8,128)(2,1)S(1)}, u32[]{:S(2)}, u32[]{:S(2)}) collective-permute-start(bf16[32,2048]{1,0:T(8,128)(2,1)S(1)} %shard_map.76), channel_id=1, source_target_pairs={{0,4},{1,5},{2,6},{3,7},{4,0},{5,1},{6,2},{7,3},{8,12},{9,13},{10,... | collective-permute-start | bytes 393224 | tf_op jit(solution)/shard_map/ppermute | solution.py:50
  86.3 6.2 %collective-permute-start.44 = (bf16[32,2048]{1,0:T(8,128)(2,1)S(1)}, bf16[32,2048]{1,0:T(8,128)(2,1)S(1)}, u32[]{:S(2)}, u32[]{:S(2)}) collective-permute-start(bf16[32,2048]{1,0:T(8,128)(2,1)S(1)} %get-tuple-element.97.refs_0_), channel_id=1, source_target_pairs={{0,2},{1,3},{2,0},{3,1},{4,6},{5,7},{6,4},{7,5},{8,10},{9,11},{10,... | collective-permute-start | bytes 393224 | tf_op jit(solution)/shard_map/ppermute | solution.py:50
  87.1 6.8 %collective-permute-start.45 = (bf16[32,2048]{1,0:T(8,128)(2,1)S(1)}, bf16[32,2048]{1,0:T(8,128)(2,1)S(1)}, u32[]{:S(2)}, u32[]{:S(2)}) collective-permute-start(bf16[32,2048]{1,0:T(8,128)(2,1)S(1)} %get-tuple-element.98.refs_1_), channel_id=1, source_target_pairs={{0,2},{1,3},{2,0},{3,1},{4,6},{5,7},{6,4},{7,5},{8,10},{9,11},{10,... | collective-permute-start | bytes 393224 | tf_op jit(solution)/shard_map/ppermute | solution.py:50
  91.2 7.0 %collective-permute-start.49 = (bf16[32,2048]{1,0:T(8,128)(2,1)S(1)}, bf16[32,2048]{1,0:T(8,128)(2,1)S(1)}, u32[]{:S(2)}, u32[]{:S(2)}) collective-permute-start(bf16[32,2048]{1,0:T(8,128)(2,1)S(1)} %shard_map.78), channel_id=1, source_target_pairs={{0,8},{1,9},{2,10},{3,11},{4,12},{5,13},{6,14},{7,15},{8,0},{9,1},... | collective-permute-start | bytes 393224 | tf_op jit(solution)/shard_map/ppermute | solution.py:50
  93.9 5.6 %collective-permute-start.46 = (bf16[32,2048]{1,0:T(8,128)(2,1)S(1)}, bf16[32,2048]{1,0:T(8,128)(2,1)S(1)}, u32[]{:S(2)}, u32[]{:S(2)}) collective-permute-start(bf16[32,2048]{1,0:T(8,128)(2,1)S(1)} %get-tuple-element.100), channel_id=1, source_target_pairs={{0,4},{1,5},{2,6},{3,7},{4,0},{5,1},{6,2},{7,3},{8,12},{9,13},{10,... | collective-permute-start | bytes 393224 | tf_op jit(solution)/shard_map/ppermute | solution.py:50
  (4 other events, 14.0 us)
